TPU v7x, 32 devices: a whole 2x2x4 slice. The times are simulated.
32 devices in a mesh: expert: 16 (over z, x, core), half: 2 (over y).
Axes of the slice: x: 2, y: 2, z: 4, core: 2. Of those that a mesh axis runs over, the one named last changes fastest.
Arguments:
- tokens: bfloat16 [512, 4096], P('expert'), may hold values from -6 to 6
- target: bfloat16 [512, 4096], P('expert', 'half'), may hold values from -3 to 3
- routes: int32 [512, 8], P('expert'), may hold values from 0 to 15, all different within a row; in each aligned block of 32 rows (0 to 31, 32 to 63, ...) at most 32 rows name the same one
- route_scores: float32 [512, 8], P('expert'), may hold values from 0.1 to 1
- in_codes: bfloat16 [16, 2, 4096, 1536], P('expert', None, None, 'half'), may hold values from 0 to 255, as said below
- in_low: float32 [16, 2, 32, 1536], P('expert', None, None, 'half'), may hold values from -0.0390625 to -0.015625
- in_high: float32 [16, 2, 32, 1536], P('expert', None, None, 'half'), may hold values from 0.015625 to 0.0390625
- down_codes: bfloat16 [16, 1536, 4096], P('expert', None, 'half'), may hold values from 0 to 255, as said below
- down_low: float32 [16, 12, 4096], P('expert', None, 'half'), may hold values from -0.063788794 to -0.02551552
- down_high: float32 [16, 12, 4096], P('expert', None, 'half'), may hold values from 0.02551552 to 0.063788794
Outputs:
- grad_tokens: bfloat16 [512, 4096], P('expert', 'half')
- in_range_grad: float32 [16, 4, 32, 1536], P('expert', None, None, 'half')
- down_range_grad: float32 [16, 2, 12, 4096], P('expert', None, None, 'half')
Inputs may be any that keep to these rules, and one draw needn't show every extreme that they name: `routes`: each row names 8 different experts. In each aligned block of 32 rows (the tokens of one index of expert) no expert is named by more than 32 rows, a bound that some block reaches. `in_codes`: whole numbers. `down_codes`: whole numbers.
All inputs are finite; a program needn't handle non-finite values.
Results may differ from a plain program's by a relative error of at most 0.013.
Values may be sent and summed in bfloat16 or wider, within the bound.
No kernel may reach another device: no remote copies, remote signals or barrier semaphores. Data moves between devices by JAX's collectives and lax.ppermute only.
A program may use at most 128 MiB of HBM per device.

v0:
```python
import jax
import jax.numpy as jnp
from jax import lax
from jax.sharding import PartitionSpec as P


def route_tables(route_block, experts, capacity):
    flat_ids = route_block.reshape(-1)
    pair_count = flat_ids.shape[0]
    onehot = (flat_ids[:, None] == jnp.arange(experts, dtype=jnp.int32)[None, :]).astype(jnp.int32)
    before = jnp.cumsum(onehot, axis=0) - onehot
    slot_rank = jnp.sum(before * onehot, axis=1)
    dest_slot = flat_ids * capacity + slot_rank
    matches = dest_slot[None, :] == jnp.arange(experts * capacity, dtype=jnp.int32)[:, None]
    is_valid = jnp.any(matches, axis=1)
    source = jnp.sum(
        jnp.where(matches, jnp.arange(pair_count, dtype=jnp.int32)[None, :], 0), axis=1
    )
    return (dest_slot, source, is_valid)


def dequant(code_vals, low_edge, high_edge):
    groups = low_edge.shape[0]
    scaled = code_vals.astype(jnp.float32).reshape(groups, -1, code_vals.shape[-1]) / 255.0
    weight = low_edge[:, None, :] + (high_edge - low_edge)[:, None, :] * scaled
    return weight.reshape(code_vals.shape).astype(jnp.bfloat16)


def range_grads(grad_weight, code_vals, groups):
    shaped = grad_weight.reshape(groups, -1, grad_weight.shape[-1])
    scaled = code_vals.astype(jnp.float32).reshape(groups, -1, code_vals.shape[-1]) / 255.0
    low_grad = jnp.sum(shaped * (1.0 - scaled), axis=1)
    high_grad = jnp.sum(shaped * scaled, axis=1)
    return (low_grad, high_grad)


def contract_rows(left, right):
    return lax.dot_general(
        left, right, (((0,), (0,)), ((), ())), preferred_element_type=jnp.float32
    )


def contract_cols(left, right):
    return lax.dot_general(
        left, right, (((1,), (1,)), ((), ())), preferred_element_type=jnp.float32
    )


def local(
    tokens, target, routes, route_scores, in_codes, in_low, in_high, down_codes, down_low, down_high
):
    experts = lax.axis_size("expert")
    tok_count = tokens.shape[0]
    top_count = routes.shape[1]
    quarter = target.shape[1]
    capacity = min(tok_count, 2 * tok_count * top_count // experts)
    dest_slot, source, is_valid = route_tables(routes, experts, capacity)
    weights = route_scores / jnp.sum(route_scores, axis=1, keepdims=True)
    token_of = source // top_count
    w_gate = dequant(in_codes[0, 0], in_low[0, 0], in_high[0, 0])
    w_up = dequant(in_codes[0, 1], in_low[0, 1], in_high[0, 1])
    w_down = dequant(down_codes[0], down_low[0], down_high[0])
    send_rows = jnp.where(is_valid[:, None], tokens[token_of], jnp.zeros((), tokens.dtype))
    expert_rows = lax.all_to_all(
        send_rows.reshape(experts, capacity, -1), "expert", split_axis=0, concat_axis=0, tiled=True
    )
    expert_rows = expert_rows.reshape(experts * capacity, -1)
    gate_pre = jnp.dot(expert_rows, w_gate, preferred_element_type=jnp.float32)
    up_pre = jnp.dot(expert_rows, w_up, preferred_element_type=jnp.float32)
    sigmoid_gate = jax.nn.sigmoid(gate_pre)
    gate_act = gate_pre * sigmoid_gate
    hidden = (gate_act * up_pre).astype(jnp.bfloat16)
    hidden_all = lax.all_gather(hidden, "half", axis=1, tiled=True)
    out_rows = jnp.dot(hidden_all, w_down, preferred_element_type=jnp.float32).astype(jnp.bfloat16)
    returned = lax.all_to_all(
        out_rows.reshape(experts, capacity, quarter),
        "expert",
        split_axis=0,
        concat_axis=0,
        tiled=True,
    )
    picked = returned.reshape(experts * capacity, quarter)[dest_slot].astype(jnp.float32)
    picked = picked.reshape(tok_count, top_count, quarter)
    mixed_out = jnp.sum(weights[:, :, None] * picked, axis=1)
    recon_error = mixed_out - target.astype(jnp.float32)
    grad_list = (
        (weights[:, :, None] * recon_error[:, None, :])
        .astype(jnp.bfloat16)
        .reshape(tok_count * top_count, quarter)
    )
    grad_send = jnp.where(is_valid[:, None], grad_list[source], jnp.zeros((), grad_list.dtype))
    error_grads = lax.all_to_all(
        grad_send.reshape(experts, capacity, quarter),
        "expert",
        split_axis=0,
        concat_axis=0,
        tiled=True,
    )
    error_grads = error_grads.reshape(experts * capacity, quarter)
    partial_hidden = contract_cols(error_grads, w_down)
    grad_hidden = lax.psum_scatter(partial_hidden, "half", scatter_dimension=1, tiled=True)
    grad_gate = (
        grad_hidden * up_pre * sigmoid_gate * (1.0 + gate_pre * (1.0 - sigmoid_gate))
    ).astype(jnp.bfloat16)
    grad_up = (grad_hidden * gate_act).astype(jnp.bfloat16)
    groups_width = in_low.shape[2]
    gate_low, gate_high = range_grads(
        contract_rows(expert_rows, grad_gate), in_codes[0, 0], groups_width
    )
    up_low, up_high = range_grads(contract_rows(expert_rows, grad_up), in_codes[0, 1], groups_width)
    down_lowg, down_highg = range_grads(
        contract_rows(hidden_all, error_grads), down_codes[0], down_low.shape[1]
    )
    in_grad = jnp.stack([gate_low, gate_high, up_low, up_high])[None]
    down_grad = jnp.stack([down_lowg, down_highg])[None]
    row_part = (contract_cols(grad_gate, w_gate) + contract_cols(grad_up, w_up)).astype(
        jnp.bfloat16
    )
    grad_rows = (
        lax.psum_scatter(row_part, "half", scatter_dimension=1, tiled=True)
        .astype(jnp.float32)
        .astype(jnp.bfloat16)
    )
    grad_back = lax.all_to_all(
        grad_rows.reshape(experts, capacity, quarter),
        "expert",
        split_axis=0,
        concat_axis=0,
        tiled=True,
    )
    grad_back = grad_back.reshape(experts * capacity, quarter)
    grad_picked = grad_back[dest_slot].astype(jnp.float32)
    grad_tokens = jnp.sum(grad_picked.reshape(tok_count, top_count, quarter), axis=1).astype(
        jnp.bfloat16
    )
    return (grad_tokens, in_grad, down_grad)


def solution(mesh):
    placed = (
        P("expert", None),
        P("expert", "half"),
        P("expert", None),
        P("expert", None),
        P("expert", None, None, "half"),
        P("expert", None, None, "half"),
        P("expert", None, None, "half"),
        P("expert", None, "half"),
        P("expert", None, "half"),
        P("expert", None, "half"),
    )
    return jax.shard_map(
        local,
        mesh=mesh,
        in_specs=placed,
        out_specs=(
            P("expert", "half"),
            P("expert", None, None, "half"),
            P("expert", None, None, "half"),
        ),
        check_vma=False,
    )
```

profile of v0, /device:TPU:0, one launch (start us, length us, event | category | flops | bytes accessed | tf_op | source)
XLA Modules:
  0.0 480.2 jit_solution(6586231892480214913)
XLA Ops:
  7.2 0.8 copy.24
  8.0 0.1 eq.39
  8.1 0.1 reshape.295
  8.2 0.6 reduce-window.6
  8.8 0.2 slice_reduce_fusion
  9.0 0.1 fusion.19
  9.1 0.2 select_reduce_fusion
  9.3 0.2 fusion.13
  9.5 0.1 broadcast_in_dim.42
  9.5 4.4 gather_fusion
  13.9 4.5 broadcast_select_fusion
  18.4 7.5 %all-to-all-start = ((bf16[16,32,4096]{2,1,0:T(8,128)(2,1)}), bf16[16,32,4096]{2,1,0:T(8,128)(2,1)}, u32[]{:S(2)}, u32[]{:S(2)}) async-start(bf16[16,32,4096]{2,1,0:T(8,128)(2,1)} %broadcast_select_fusion), calls=%async_computation | async-start | bytes 8388608 | tf_op jit(solution)/shard_map/all_to_all | solution.py:64
  25.9 0.2 all-gather.2.cloned.1.call-start
  26.3 6.0 %slice_convert_fusion = (f32[1,1,4096,768]{3,2,1,0:T(8,128)S(1)}, f32[1,1,4096,768]{3,2,1,0:T(8,128)S(1)}) fusion(bf16[1,2,4096,768]{3,2,1,0:T(8,128)(2,1)} %param.14), kind=kLoop, calls=%fused_computation.23 | loop fusion | flops 6291456 | bytes 37748736 | tf_op jit(solution)/shard_map/convert_element_type | solution.py:24
  32.4 4.5 copy-done.2
  36.8 3.7 copy-done.3
  40.6 8.0 %add_convert_fusion.1 = (bf16[32,128,768]{2,1,0:T(8,128)(2,1)}, bf16[32,128,768]{2,1,0:T(8,128)(2,1)}) fusion(f32[32,128,768]{2,1,0:T(8,128)S(1)} %bitcast.146, f32[32,768]{1,0:T(8,128)S(1)} %get-tuple-element.16, f32[32,768]{1,0:T(8,128)S(1)} %get-tuple-element.18, f32[32,128,768]{2,1,0:T(8,128)S(1)} %bitcast.148, f32[32,768]{1,0:T(8,128)S(1)} %get-tuple-element.17, ...), kind=kLoop, calls=%fused_computation.20 | loop fusion | flops 18874368 | bytes 38141952 | tf_op jit(solution)/shard_map/convert_element_type | solution.py:26
  48.5 55.1 %all-to-all-done = bf16[16,32,4096]{2,1,0:T(8,128)(2,1)} async-done(((bf16[16,32,4096]{2,1,0:T(8,128)(2,1)}), bf16[16,32,4096]{2,1,0:T(8,128)(2,1)}, u32[]{:S(2)}, u32[]{:S(2)}) %all-to-all-start) | async-done | bytes 4194336 | tf_op jit(solution)/shard_map/all_to_all | solution.py:64
  103.6 7.2 %fusion.21 = f32[512,768]{1,0:T(8,128)S(1)} fusion(bf16[512,4096]{1,0:T(8,128)(2,1)} %bitcast.4, bf16[4096,768]{1,0:T(8,128)(2,1)} %bitcast.153), kind=kOutput, calls=%fused_computation.79 | convolution fusion | flops 3221225472 | bytes 12058624 | tf_op jit(solution)/shard_map/dot_general | solution.py:68
  110.8 7.6 %multiply_convert_fusion.2 = (bf16[512,768]{1,0:T(8,128)(2,1)}, f32[512,768]{1,0:T(8,128)}) fusion(f32[512,768]{1,0:T(8,128)S(1)} %fusion.21, bf16[512,4096]{1,0:T(8,128)(2,1)} %bitcast.4, bf16[4096,768]{1,0:T(8,128)(2,1)S(1)} %bitcast.152), kind=kOutput, calls=%fused_computation.34 | convolution fusion | flops 3223584768 | bytes 14417920 | tf_op jit(solution)/shard_map/dot_general | solution.py:69
  118.5 0.0 all-gather.2.cloned.1.call-update
  118.5 0.1 fusion.14
  118.6 7.8 %fusion.5 = bf16[1536,2048]{1,0:T(8,128)(2,1)} fusion(f32[12,2048]{1,0:T(8,128)S(1)} %fusion.14, f32[12,2048]{1,0:T(8,128)S(1)} %bitcast.166, bf16[1,1536,2048]{2,1,0:T(8,128)(2,1)} %param.17), kind=kLoop, calls=%fused_computation.12 | loop fusion | flops 12582912 | bytes 12779520 | tf_op jit(solution)/shard_map/convert_element_type | solution.py:26
  126.4 34.4 %all-gather.2.cloned.1.call-done = bf16[512,1536]{1,0:T(8,128)(2,1)} async-done(((bf16[512,768]{1,0:T(8,128)(2,1)}), bf16[512,1536]{1,0:T(8,128)(2,1)}) %all-gather.2.cloned.1.call-update) | async-done | bytes 1572880 | tf_op jit(solution)/shard_map/all_gather | solution.py:73
  160.8 8.0 %convolution_convert_fusion = bf16[512,2048]{1,0:T(8,128)(2,1)} fusion(bf16[512,1536]{1,0:T(8,128)(2,1)} %all-gather.2.cloned.1.call-done, bf16[1536,2048]{1,0:T(8,128)(2,1)} %fusion.5), kind=kOutput, calls=%fused_computation.26 | convolution fusion | flops 3222274048 | bytes 9961472 | tf_op jit(solution)/shard_map/dot_general | solution.py:74
  168.8 5.8 %all-to-all-start.1 = ((bf16[16,32,2048]{2,1,0:T(8,128)(2,1)}), bf16[16,32,2048]{2,1,0:T(8,128)(2,1)S(1)}, u32[]{:S(2)}, u32[]{:S(2)}) async-start(bf16[16,32,2048]{2,1,0:T(8,128)(2,1)} %bitcast.161), calls=%async_computation.1 | async-start | bytes 4194304 | tf_op jit(solution)/shard_map/all_to_all | solution.py:75
  174.7 0.1 copy.29
  174.8 0.1 mul.184
  174.9 0.1 copy.27
  175.0 0.1 mul.165
  175.1 40.7 %all-to-all-done.1 = bf16[16,32,2048]{2,1,0:T(8,128)(2,1)S(1)} async-done(((bf16[16,32,2048]{2,1,0:T(8,128)(2,1)}), bf16[16,32,2048]{2,1,0:T(8,128)(2,1)S(1)}, u32[]{:S(2)}, u32[]{:S(2)}) %all-to-all-start.1) | async-done | bytes 2097184 | tf_op jit(solution)/shard_map/all_to_all | solution.py:75
  215.7 1.4 gather_fusion.1
  217.1 1.0 fusion.6
  218.1 0.9 convert_subtract_fusion
  219.0 0.2 fusion.7
  219.2 2.5 gather_fusion.2
  221.7 1.6 broadcast_select_fusion.1
  223.3 11.2 %all-to-all-start.2 = ((bf16[16,32,2048]{2,1,0:T(8,128)(2,1)}), bf16[16,32,2048]{2,1,0:T(8,128)(2,1)S(1)}, u32[]{:S(2)}, u32[]{:S(2)}) async-start(bf16[16,32,2048]{2,1,0:T(8,128)(2,1)} %broadcast_select_fusion.1), calls=%async_computation.2 | async-start | bytes 4194304 | tf_op jit(solution)/shard_map/all_to_all | solution.py:92
  234.5 0.0 reduce-scatter.3.cloned.1.call-start
  234.5 2.6 copy.31
  237.2 38.4 %all-to-all-done.2 = bf16[16,32,2048]{2,1,0:T(8,128)(2,1)S(1)} async-done(((bf16[16,32,2048]{2,1,0:T(8,128)(2,1)}), bf16[16,32,2048]{2,1,0:T(8,128)(2,1)S(1)}, u32[]{:S(2)}, u32[]{:S(2)}) %all-to-all-start.2) | async-done | bytes 2097184 | tf_op jit(solution)/shard_map/all_to_all | solution.py:92
  275.6 10.8 %multiply_reduce_fusion.1 = (f32[12,2048]{1,0:T(8,128)}, f32[12,2048]{1,0:T(8,128)}, f32[12,128,2048]{2,1,0:T(8,128)}) fusion(bf16[12,128,2048]{2,1,0:T(8,128)(2,1)} %bitcast.154, bf16[12,128,512]{2,1,0:T(8,128)(2,1)} %bitcast.165, bf16[512,2048,1]{1,0,2:T(8,128)(2,1)S(1)} %bitcast.162), kind=kOutput, calls=%fused_computation.14 | convolution fusion | flops 3243196416 | bytes 22740992 | tf_op jit(solution)/shard_map/dot_general | solution.py:38
  286.4 9.3 %add_convert_fusion = bf16[12,128,2048]{2,1,0:T(8,128)(2,1)} fusion(f32[12,128,2048]{2,1,0:T(8,128)} %get-tuple-element.9, f32[12,2048]{1,0:T(8,128)S(1)} %fusion.14, f32[12,2048]{1,0:T(8,128)S(1)} %bitcast.167), kind=kLoop, calls=%fused_computation.19 | loop fusion | flops 9437184 | bytes 19070976 | tf_op jit(solution)/shard_map/convert_element_type | solution.py:26
  295.7 7.9 %fusion.22 = f32[512,1536]{1,0:T(8,128)} fusion(bf16[512,2048]{1,0:T(8,128)(2,1)S(1)} %bitcast.163, bf16[1536,2048]{1,0:T(8,128)(2,1)} %bitcast.157), kind=kOutput, calls=%fused_computation.80 | convolution fusion | flops 3221225472 | bytes 11534336 | tf_op jit(solution)/shard_map/dot_general | solution.py:44
  303.6 0.0 reduce-scatter.3.cloned.1.call-update
  303.6 0.3 reduce-scatter.5.cloned.1.call-start
  304.0 12.0 %fusion.1 = (bf16[4096,768]{1,0:T(8,128)(2,1)}, bf16[4096,768]{1,0:T(8,128)(2,1)}) fusion(f32[32,768]{1,0:T(8,128)S(1)} %get-tuple-element.16, f32[32,768]{1,0:T(8,128)S(1)} %copy-done.13, bf16[1,2,4096,768]{3,2,1,0:T(8,128)(2,1)} %param.14, f32[32,768]{1,0:T(8,128)S(1)} %copy-done.11, f32[32,768]{1,0:T(8,128)} %copy-done.14), kind=kLoop, calls=%fused_computation.6 | loop fusion | flops 25165824 | bytes 25559040 | tf_op jit(solution)/shard_map/convert_element_type | solution.py:26
  316.0 36.7 %reduce-scatter.3.cloned.1.call-done = f32[512,768]{1,0:T(8,128)} async-done(((f32[512,1536]{1,0:T(8,128)}), f32[512,768]{1,0:T(8,128)}) %reduce-scatter.3.cloned.1.call-update) | async-done | bytes 1572880 | tf_op jit(solution)/shard_map/reduce_scatter | solution.py:101
  352.7 2.3 multiply_convert_fusion
  355.1 0.9 copy-done.5
  356.0 5.7 %fusion.23 = f32[512,4096]{1,0:T(8,128)} fusion(bf16[512,768]{1,0:T(8,128)(2,1)S(1)} %get-tuple-element.15, bf16[4096,768]{1,0:T(8,128)(2,1)S(1)} %copy-done.5), kind=kOutput, calls=%fused_computation.81 | convolution fusion | flops 3221225472 | bytes 15466496 | tf_op jit(solution)/shard_map/dot_general | solution.py:44
  361.7 7.4 %add_convert_fusion.3 = bf16[512,4096]{1,0:T(8,128)(2,1)} fusion(f32[512,4096]{1,0:T(8,128)} %fusion.23, bf16[512,768]{1,0:T(8,128)(2,1)S(1)} %get-tuple-element.14, bf16[4096,768]{1,0:T(8,128)(2,1)S(1)} %bitcast.156), kind=kOutput, calls=%fused_computation.22 | convolution fusion | flops 3225419776 | bytes 19660800 | tf_op jit(solution)/shard_map/dot_general | solution.py:44
  369.1 54.5 %reduce-scatter.5.cloned.1.call-done = bf16[512,2048]{1,0:T(8,128)(2,1)} async-done(((bf16[512,4096]{1,0:T(8,128)(2,1)}), bf16[512,2048]{1,0:T(8,128)(2,1)}) %reduce-scatter.5.cloned.1.call-update) | async-done | bytes 2097168 | tf_op jit(solution)/shard_map/reduce_scatter | solution.py:120
  423.6 5.7 %all-to-all-start.3 = ((bf16[16,32,2048]{2,1,0:T(8,128)(2,1)}), bf16[16,32,2048]{2,1,0:T(8,128)(2,1)S(1)}, u32[]{:S(2)}, u32[]{:S(2)}) async-start(bf16[16,32,2048]{2,1,0:T(8,128)(2,1)} %bitcast.160), calls=%async_computation.5 | async-start | bytes 4194304 | tf_op jit(solution)/shard_map/all_to_all | solution.py:124
  429.4 6.5 %copy.30 = bf16[4096,512]{1,0:T(8,128)(2,1)} copy(bf16[4096,512]{0,1:T(8,128)(2,1)} %bitcast.36) | data formatting | bytes 8388608 | tf_op jit(solution)/shard_map/dot_general | solution.py:38
  435.8 0.1 stack.29
  435.9 0.1 stack.30
  436.0 0.9 maximum_bitcast_fusion.1
  436.9 9.9 %multiply_reduce_fusion.5 = (f32[32,768]{1,0:T(8,128)S(1)}, f32[32,768]{1,0:T(8,128)S(1)}) fusion(f32[32,128,768]{2,1,0:T(8,128)} %bitcast.149, bf16[32,128,512]{2,1,0:T(8,128)(2,1)} %bitcast.158, bf16[512,768]{1,0:T(8,128)(2,1)S(1)} %copy-done.18), kind=kOutput, calls=%fused_computation.18 | convolution fusion | flops 3240050688 | bytes 17760256 | tf_op jit(solution)/shard_map/dot_general | solution.py:38
  446.8 7.7 %multiply_reduce_fusion.3 = (f32[32,768]{1,0:T(8,128)S(1)}, f32[32,768]{1,0:T(8,128)S(1)}) fusion(f32[32,128,768]{2,1,0:T(8,128)} %bitcast.147, bf16[32,128,512]{2,1,0:T(8,128)(2,1)S(1)} %bitcast.159, bf16[512,768]{1,0:T(8,128)(2,1)S(1)} %copy-done.16), kind=kOutput, calls=%fused_computation.16 | convolution fusion | flops 3240050688 | bytes 17760256 | tf_op jit(solution)/shard_map/dot_general | solution.py:38
  454.5 0.8 maximum_bitcast_fusion
  455.3 15.2 %all-to-all-done.3 = bf16[16,32,2048]{2,1,0:T(8,128)(2,1)S(1)} async-done(((bf16[16,32,2048]{2,1,0:T(8,128)(2,1)}), bf16[16,32,2048]{2,1,0:T(8,128)(2,1)S(1)}, u32[]{:S(2)}, u32[]{:S(2)}) %all-to-all-start.3) | async-done | bytes 2097184 | tf_op jit(solution)/shard_map/all_to_all | solution.py:124
  470.5 1.4 gather_fusion.3
  471.8 1.4 bitcast_reduce_fusion
  (72 shorter events, 0.3 us)
Async XLA Ops:
  7.2 2.4 copy-start
  18.4 7.8 %copy-start.19 = (f32[1,2,32,768]{3,2,1,0:T(8,128)S(1)}, f32[1,2,32,768]{3,2,1,0:T(8,128)}, u32[]{:S(2)}) copy-start(f32[1,2,32,768]{3,2,1,0:T(8,128)} %param.15) | copy-start | bytes 589828
  18.4 7.8 %copy-start.21 = (f32[1,2,32,768]{3,2,1,0:T(8,128)S(1)}, f32[1,2,32,768]{3,2,1,0:T(8,128)}, u32[]{:S(2)}) copy-start(f32[1,2,32,768]{3,2,1,0:T(8,128)} %param.16) | copy-start | bytes 589828
  18.4 85.2 %all-to-all-start = ((bf16[16,32,4096]{2,1,0:T(8,128)(2,1)}), bf16[16,32,4096]{2,1,0:T(8,128)(2,1)}, u32[]{:S(2)}, u32[]{:S(2)}) async-start(bf16[16,32,4096]{2,1,0:T(8,128)(2,1)} %broadcast_select_fusion), calls=%async_computation | async-start | bytes 8388608 | tf_op jit(solution)/shard_map/all_to_all | solution.py:64
  25.9 134.9 %all-gather.2.cloned.1.call-start = ((), (), s32[]{:S(2)}) async-start(), calls=%async_computation.6 | async-start | bytes 2359296 | tf_op jit(solution)/shard_map/all_gather | solution.py:73
  26.2 6.1 %copy-start.12 = (f32[32,768]{1,0:T(8,128)}, f32[32,768]{1,0:T(8,128)S(1)}, u32[]{:S(2)}) copy-start(f32[32,768]{1,0:T(8,128)S(1)} %get-tuple-element.18) | copy-start | bytes 294916
  26.2 6.1 %copy-start.14 = (f32[32,768]{1,0:T(8,128)}, f32[32,768]{1,0:T(8,128)S(1)}, u32[]{:S(2)}) copy-start(f32[32,768]{1,0:T(8,128)S(1)} %get-tuple-element.19) | copy-start | bytes 294916
  26.3 6.1 %copy-start.10 = (f32[32,768]{1,0:T(8,128)}, f32[32,768]{1,0:T(8,128)S(1)}, u32[]{:S(2)}) copy-start(f32[32,768]{1,0:T(8,128)S(1)} %get-tuple-element.17) | copy-start | bytes 294916
  32.3 4.5 copy-start.2
  32.3 8.2 %copy-start.3 = (f32[1,1,4096,768]{3,2,1,0:T(8,128)}, f32[1,1,4096,768]{3,2,1,0:T(8,128)S(1)}, u32[]{:S(2)}) copy-start(f32[1,1,4096,768]{3,2,1,0:T(8,128)S(1)} %get-tuple-element.13) | copy-start | bytes 37748740
  103.6 7.2 %copy-start.4 = (bf16[32,128,768]{2,1,0:T(8,128)(2,1)S(1)}, bf16[32,128,768]{2,1,0:T(8,128)(2,1)}, u32[]{:S(2)}) copy-start(bf16[32,128,768]{2,1,0:T(8,128)(2,1)} %get-tuple-element.24) | copy-start | bytes 18874372
  110.8 7.7 %copy-start.7 = (f32[512,768]{1,0:T(8,128)}, f32[512,768]{1,0:T(8,128)S(1)}, u32[]{:S(2)}) copy-start(f32[512,768]{1,0:T(8,128)S(1)} %fusion.21) | copy-start | bytes 4718596
  110.8 7.7 %copy-start.20 = (f32[1,12,2048]{2,0,1:T(1,128)S(1)}, f32[1,12,2048]{2,0,1:T(1,128)}, u32[]{:S(2)}) copy-start(f32[1,12,2048]{2,0,1:T(1,128)} %param.18) | copy-start | bytes 294916
  110.8 7.7 %copy-start.24 = (f32[1,12,2048]{2,0,1:T(1,128)S(1)}, f32[1,12,2048]{2,0,1:T(1,128)}, u32[]{:S(2)}) copy-start(f32[1,12,2048]{2,0,1:T(1,128)} %param.19) | copy-start | bytes 294916
  126.4 48.2 %copy-start.25 = (s32[32,8]{0,1:T(8,128)S(1)}, s32[32,8]{0,1:T(8,128)}, u32[]{:S(2)}) copy-start(s32[32,8]{0,1:T(8,128)} %param.12) | copy-start | bytes 3076
  126.4 48.4 %copy-start.26 = (f32[32,8]{0,1:T(8,128)S(1)}, f32[32,8]{0,1:T(8,128)}, u32[]{:S(2)}) copy-start(f32[32,8]{0,1:T(8,128)} %param.13) | copy-start | bytes 3076
  168.8 46.9 %all-to-all-start.1 = ((bf16[16,32,2048]{2,1,0:T(8,128)(2,1)}), bf16[16,32,2048]{2,1,0:T(8,128)(2,1)S(1)}, u32[]{:S(2)}, u32[]{:S(2)}) async-start(bf16[16,32,2048]{2,1,0:T(8,128)(2,1)} %bitcast.161), calls=%async_computation.1 | async-start | bytes 4194304 | tf_op jit(solution)/shard_map/all_to_all | solution.py:75
  223.3 52.3 %all-to-all-start.2 = ((bf16[16,32,2048]{2,1,0:T(8,128)(2,1)}), bf16[16,32,2048]{2,1,0:T(8,128)(2,1)S(1)}, u32[]{:S(2)}, u32[]{:S(2)}) async-start(bf16[16,32,2048]{2,1,0:T(8,128)(2,1)} %broadcast_select_fusion.1), calls=%async_computation.2 | async-start | bytes 4194304 | tf_op jit(solution)/shard_map/all_to_all | solution.py:92
  234.5 118.2 %reduce-scatter.3.cloned.1.call-start = ((), (), s32[]{:S(2)}) async-start(), calls=%async_computation.7 | async-start | bytes 4718592 | tf_op jit(solution)/shard_map/reduce_scatter | solution.py:101
  295.7 8.2 %copy-start.11 = (f32[32,768]{1,0:T(8,128)S(1)}, f32[32,768]{1,0:T(8,128)}, u32[]{:S(2)}) copy-start(f32[32,768]{1,0:T(8,128)} %copy-done.10) | copy-start | bytes 294916
  295.7 8.2 %copy-start.13 = (f32[32,768]{1,0:T(8,128)S(1)}, f32[32,768]{1,0:T(8,128)}, u32[]{:S(2)}) copy-start(f32[32,768]{1,0:T(8,128)} %copy-done.12) | copy-start | bytes 294916
  303.6 49.1 %copy-start.8 = (f32[512,768]{1,0:T(8,128)S(1)}, f32[512,768]{1,0:T(8,128)}, u32[]{:S(2)}) copy-start(f32[512,768]{1,0:T(8,128)} %copy-done.7) | copy-start | bytes 4718596
  303.6 49.1 %copy-start.9 = (f32[512,768]{1,0:T(8,128)S(1)}, f32[512,768]{1,0:T(8,128)}, u32[]{:S(2)}) copy-start(f32[512,768]{1,0:T(8,128)} %get-tuple-element.23) | copy-start | bytes 4718596
  303.6 119.9 %reduce-scatter.5.cloned.1.call-start = ((), (), s32[]{:S(2)}) async-start(), calls=%async_computation.8 | async-start | bytes 6291456 | tf_op jit(solution)/shard_map/reduce_scatter | solution.py:120
  352.7 3.3 copy-start.5
  352.7 9.0 %slice-start = ((s8[6291456]{0:T(1024)(128)(4,1)}), s8[4194304]{0:T(1024)(128)(4,1)S(1)}, s32[]{:S(2)}) async-start(s8[6291456]{0:T(1024)(128)(4,1)} %bitcast.155), calls=%async_computation.9 | async-start | bytes 8388608
  355.0 6.6 %copy-start.17 = (bf16[512,768]{1,0:T(8,128)(2,1)}, bf16[512,768]{1,0:T(8,128)(2,1)S(1)}, u32[]{:S(2)}) copy-start(bf16[512,768]{1,0:T(8,128)(2,1)S(1)} %get-tuple-element.15) | copy-start | bytes 2359300
  355.1 6.6 %copy-start.15 = (bf16[512,768]{1,0:T(8,128)(2,1)}, bf16[512,768]{1,0:T(8,128)(2,1)S(1)}, u32[]{:S(2)}) copy-start(bf16[512,768]{1,0:T(8,128)(2,1)S(1)} %get-tuple-element.14) | copy-start | bytes 2359300
  356.0 5.7 %slice-start.1 = ((s8[6291456]{0:T(1024)(128)(4,1)}), s8[2097152]{0:T(1024)(128)(4,1)S(1)}, s32[]{:S(2)}) async-start(s8[6291456]{0:T(1024)(128)(4,1)} %bitcast.155), calls=%async_computation.10 | async-start | bytes 4194304
  423.6 12.3 %copy-start.23 = (f32[12,2048]{1,0:T(8,128)S(1)}, f32[12,2048]{1,0:T(8,128)}, u32[]{:S(2)}) copy-start(f32[12,2048]{1,0:T(8,128)} %get-tuple-element.3) | copy-start | bytes 294916
  423.6 12.3 %copy-start.22 = (f32[12,2048]{1,0:T(8,128)S(1)}, f32[12,2048]{1,0:T(8,128)}, u32[]{:S(2)}) copy-start(f32[12,2048]{1,0:T(8,128)} %get-tuple-element.4) | copy-start | bytes 294916
  423.6 13.3 %copy-start.18 = (bf16[512,768]{1,0:T(8,128)(2,1)S(1)}, bf16[512,768]{1,0:T(8,128)(2,1)}, u32[]{:S(2)}) copy-start(bf16[512,768]{1,0:T(8,128)(2,1)} %copy-done.17) | copy-start | bytes 2359300
  423.6 46.9 %all-to-all-start.3 = ((bf16[16,32,2048]{2,1,0:T(8,128)(2,1)}), bf16[16,32,2048]{2,1,0:T(8,128)(2,1)S(1)}, u32[]{:S(2)}, u32[]{:S(2)}) async-start(bf16[16,32,2048]{2,1,0:T(8,128)(2,1)} %bitcast.160), calls=%async_computation.5 | async-start | bytes 4194304 | tf_op jit(solution)/shard_map/all_to_all | solution.py:124
  436.9 9.9 %copy-start.6 = (bf16[4096,512]{1,0:T(8,128)(2,1)S(1)}, bf16[4096,512]{1,0:T(8,128)(2,1)}, u32[]{:S(2)}) copy-start(bf16[4096,512]{1,0:T(8,128)(2,1)} %copy.30) | copy-start | bytes 12582916
  436.9 10.0 %copy-start.16 = (bf16[512,768]{1,0:T(8,128)(2,1)S(1)}, bf16[512,768]{1,0:T(8,128)(2,1)}, u32[]{:S(2)}) copy-start(bf16[512,768]{1,0:T(8,128)(2,1)} %copy-done.15) | copy-start | bytes 2359300
  446.8 26.4 %copy-start.1 = (bf16[32,4096]{1,0:T(8,128)(2,1)S(1)}, bf16[32,4096]{1,0:T(8,128)(2,1)}, u32[]{:S(2)}) copy-start(bf16[32,4096]{1,0:T(8,128)(2,1)} %param.10) | copy-start | bytes 786436
Sparse Core Ops, SparseCore 0:
  118.6 42.1 all-gather.1
  303.7 48.9 reduce-scatter.2
  369.2 54.3 reduce-scatter.4
where the time goes:
time: 489 us; the launch traced here: 480 us
  waiting for transfers between devices  275 us (56%)
  matrix products  72.2 us (15%)
  other arithmetic  57.8 us (12%)
  starting transfers between devices  30.9 us (6%)
  local copies, waits for them, and re-layouts  29.6 us (6%)
  between operations  14.7 us (3%)
    all_to_all x1, waiting for transfers between devices, local(): lax.all_to_all(send_rows.reshape(experts, capacity, -1), 'expert', split_...  55.1 us
    reduce_scatter x1, waiting for transfers between devices, local(): lax.psum_scatter(row_part, 'half', scatter_dimension=1, tiled=True)  54.5 us
    all_to_all x1, waiting for transfers between devices, local(): lax.all_to_all(out_rows.reshape(experts, capacity, quarter), 'expert', sp...  40.7 us
    all_to_all x1, waiting for transfers between devices, local(): lax.all_to_all(grad_send.reshape(experts, capacity, quarter), 'expert', s...  38.4 us
    convert_element_type x4, other arithmetic, dequant(): return weight.reshape(code_vals.shape).astype(jnp.bfloat16)  37.1 us
    reduce_scatter x1, waiting for transfers between devices, local(): lax.psum_scatter(partial_hidden, 'half', scatter_dimension=1, tiled=True)  36.7 us
    all_gather x1, waiting for transfers between devices, local(): hidden_all = lax.all_gather(hidden, 'half', axis=1, tiled=True)  34.4 us
    dot_general x3, matrix products, contract_rows(): lax.dot_general(left, right, (((0,), (0,)), ((), ())), preferred_element_...  28.4 us
  transfers between devices with their start and end apart: 7, of which 7 were waited for; matrix products, arithmetic and copies ran while one was open for 13% of the time, Pallas kernels for 0%

commit v1 on v0

v1 whole, which is shorter than its diff:
```python
import functools

import jax
import jax.numpy as jnp
from jax import lax
from jax.experimental import pallas as pl
from jax.experimental.pallas import tpu as pltpu
from jax.sharding import PartitionSpec as P

CHUNKS = 2
BF16 = jnp.bfloat16
F32 = jnp.float32
MIB = 1 << 20


def swap(array, axis, distance):
    size = lax.axis_size(axis)
    return lax.ppermute(array, axis, [(i, i ^ distance) for i in range(size)])


def far_distances():
    experts = lax.axis_size("expert")
    distances = []
    distance = experts // 2
    while distance > 1:
        distances.append(distance)
        distance //= 2
    return distances


def gather_rows(block):
    for distance in far_distances():
        block = jnp.concatenate([block, swap(block, "expert", distance)], axis=0)
    return block, swap(block, "expert", 1)


def scatter_rows(first, second):
    total, arrived = first, second
    for distance in reversed(far_distances()):
        half = total.shape[0] // 2
        leave = (total[half:].astype(F32) + arrived[half:].astype(F32)).astype(BF16)
        sent = swap(leave, "expert", distance)
        total = total[:half].astype(F32) + arrived[:half].astype(F32)
        arrived = sent
    return total.astype(F32) + arrived.astype(F32)


def dot(left, right):
    return jnp.dot(left, right, preferred_element_type=F32)


def dot_cols(left, right):
    return lax.dot_general(left, right, (((1,), (1,)), ((), ())), preferred_element_type=F32)


def dot_rows(left, right):
    return lax.dot_general(left, right, (((0,), (0,)), ((), ())), preferred_element_type=F32)


def cost(flops, bytes_accessed):
    return pl.CostEstimate(flops=int(flops), bytes_accessed=int(bytes_accessed), transcendentals=0)


def params(mib):
    return pltpu.CompilerParams(vmem_limit_bytes=mib * MIB)


def moved(step, blocks, place):
    return ((step // blocks) ^ place[1]) * blocks + step % blocks


def call(kernel, grid, ins, outs, place, scratch=(), mib=32, flops=0):
    total = sum(a.size * a.dtype.itemsize for a, _, _ in ins)
    for shape, kind, _, _ in outs:
        count = 1
        for extent in shape:
            count *= extent
        total += count * jnp.dtype(kind).itemsize
    spec = pltpu.PrefetchScalarGridSpec(
        num_scalar_prefetch=1,
        grid=grid,
        in_specs=[pl.BlockSpec(block, index) for _, block, index in ins],
        out_specs=[pl.BlockSpec(block, index) for _, _, block, index in outs],
        scratch_shapes=list(scratch),
    )
    return pl.pallas_call(
        kernel,
        grid_spec=spec,
        out_shape=[jax.ShapeDtypeStruct(shape, kind) for shape, kind, _, _ in outs],
        compiler_params=params(mib),
        cost_estimate=cost(flops, total),
    )(place, *[a for a, _, _ in ins])


def whole2(*_):
    return (0, 0)


def whole3(*_):
    return (0, 0, 0)


def whole4(*_):
    return (0, 0, 0, 0)


def dequant_in(place, codes, low, high, halves):
    _, _, width, hidden = codes.shape
    groups = low.shape[2]
    size = width // groups
    per = max(1, 512 // size)
    rows = per * size
    blocks = width // halves // rows

    def kernel(place_ref, code_ref, low_ref, high_ref, out_ref):
        base = moved(pl.program_id(0), blocks, place_ref) * per
        for k in range(2):
            for g in range(per):
                bottom = low_ref[0, k, pl.ds(base + g, 1), :]
                scale = (high_ref[0, k, pl.ds(base + g, 1), :] - bottom) * (1.0 / 255.0)
                vals = code_ref[0, k, g * size : (g + 1) * size, :].astype(F32)
                out_ref[g * size : (g + 1) * size, k * hidden : (k + 1) * hidden] = (
                    bottom + scale * vals
                ).astype(BF16)

    return call(
        kernel,
        (width // rows,),
        [
            (codes, (1, 2, rows, hidden), lambda i, p: (0, 0, moved(i, blocks, p), 0)),
            (low, low.shape, whole4),
            (high, high.shape, whole4),
        ],
        [((width, 2 * hidden), BF16, (rows, 2 * hidden), lambda i, p: (i, 0))],
        place,
    )[0]


def hidden_rows(total_groups, size, halves):
    per = total_groups // halves
    while per > 3:
        per = next(f for f in range(2, per + 1) if per % f == 0) and per // next(
            f for f in range(2, per + 1) if per % f == 0
        )
    return per, per * size


def dequant_down(place, codes, low, high, halves):
    _, height, quarter = codes.shape
    groups = low.shape[1]
    size = height // groups
    per, rows = hidden_rows(groups, size, halves)
    blocks = height // halves // rows

    def kernel(place_ref, code_ref, low_ref, high_ref, out_ref):
        base = moved(pl.program_id(0), blocks, place_ref) * per
        for g in range(per):
            bottom = low_ref[0, pl.ds(base + g, 1), :]
            scale = (high_ref[0, pl.ds(base + g, 1), :] - bottom) * (1.0 / 255.0)
            vals = code_ref[0, g * size : (g + 1) * size, :].astype(F32)
            out_ref[g * size : (g + 1) * size, :] = (bottom + scale * vals).astype(BF16)

    return call(
        kernel,
        (height // rows,),
        [
            (codes, (1, rows, quarter), lambda i, p: (0, moved(i, blocks, p), 0)),
            (low, low.shape, whole3),
            (high, high.shape, whole3),
        ],
        [((height, quarter), BF16, (rows, quarter), lambda i, p: (i, 0))],
        place,
    )[0]


def forward_in(place, x_own, x_other, w_in):
    rows = x_own.shape[0]
    width, both = w_in.shape
    hidden = both // 2
    depth = min(512, width)
    steps = width // depth

    def kernel(place_ref, own_ref, other_ref, w_ref, hidden_ref, slope_ref, act_ref, acc_ref):
        step = pl.program_id(0)
        x = jnp.concatenate([own_ref[...], other_ref[...]], axis=0)
        part = dot(x, w_ref[...])

        @pl.when(step == 0)
        def _():
            acc_ref[...] = part

        @pl.when(step > 0)
        def _():
            acc_ref[...] += part

        @pl.when(step == steps - 1)
        def _():
            gate = acc_ref[:, :hidden]
            up = acc_ref[:, hidden:]
            sig = 1.0 / (1.0 + jnp.exp(-gate))
            act = gate * sig
            hidden_ref[...] = (act * up).astype(BF16)
            slope_ref[...] = up * sig * (1.0 + gate * (1.0 - sig))
            act_ref[...] = act

    shape = (2 * rows, hidden)
    return call(
        kernel,
        (steps,),
        [
            (x_own, (rows, depth), lambda i, p: (0, i)),
            (x_other, (rows, depth), lambda i, p: (0, i)),
            (w_in, (depth, both), lambda i, p: (i, 0)),
        ],
        [(shape, BF16, shape, whole2), (shape, F32, shape, whole2), (shape, F32, shape, whole2)],
        place,
        scratch=[pltpu.VMEM((2 * rows, both), F32)],
        flops=4 * rows * width * both,
    )


def route_weight(extra, place_ref, experts):
    lane = lax.broadcasted_iota(jnp.int32, extra.shape, 1)
    me = place_ref[0]
    named = (lane == me) | (lane == me + experts) | (lane == me + 2 * experts)
    return jnp.sum(jnp.where(named, extra.astype(F32), 0.0), axis=1, keepdims=True)


def forward_down(place, hidden, w_down, x_own, x_other, extra):
    experts = lax.axis_size("expert")
    rows = x_own.shape[0]
    own = hidden[0].shape[1]
    height, quarter = w_down.shape
    cols = min(512, quarter)
    at = (x_own.shape[1] - extra) // extra

    def kernel(place_ref, *refs):
        *hidden_refs, w_ref, own_ref, other_ref, out_own_ref, out_other_ref = refs
        total = dot(hidden_refs[0][...], w_ref[:own, :])
        for d in range(1, len(hidden_refs)):
            total += dot(hidden_refs[d][...], w_ref[d * own : (d + 1) * own, :])
        out_own_ref[...] = (
            route_weight(own_ref[...], place_ref, experts) * total[:rows]
        ).astype(BF16)
        out_other_ref[...] = (
            route_weight(other_ref[...], place_ref, experts) * total[rows:]
        ).astype(BF16)

    return call(
        kernel,
        (quarter // cols,),
        [(part, part.shape, whole2) for part in hidden]
        + [
            (w_down, (height, cols), lambda i, p: (0, i)),
            (x_own, (rows, extra), lambda i, p: (0, at)),
            (x_other, (rows, extra), lambda i, p: (0, at)),
        ],
        [((rows, quarter), BF16, (rows, cols), lambda i, p: (0, i))] * 2,
        place,
        flops=4 * rows * height * quarter,
    )


def backward_down(place, err_own, err_other, x_own, x_other, w_down, extra, halves):
    experts = lax.axis_size("expert")
    rows, quarter = err_own.shape
    height = w_down.shape[0]
    own = height // halves
    cuts = 2 if own % 256 == 0 else 1
    size = own // cuts
    at = (x_own.shape[1] - extra) // extra

    def kernel(place_ref, err_own_ref, err_other_ref, own_ref, other_ref, w_ref, grad_ref, *outs):
        step = pl.program_id(0)

        @pl.when(step == 0)
        def _():
            weight = route_weight(own_ref[...], place_ref, experts)
            grad_ref[:rows, :] = (weight * err_own_ref[...].astype(F32)).astype(BF16)
            weight = route_weight(other_ref[...], place_ref, experts)
            grad_ref[rows:, :] = (weight * err_other_ref[...].astype(F32)).astype(BF16)

        part = dot_cols(grad_ref[...], w_ref[...])
        for d in range(halves):
            for c in range(cuts):

                @pl.when(step == d * cuts + c)
                def _():
                    outs[d][:, c * size : (c + 1) * size] = part.astype(outs[d].dtype)

    shape = (2 * rows, own)
    return call(
        kernel,
        (halves * cuts,),
        [
            (err_own, (rows, quarter), whole2),
            (err_other, (rows, quarter), whole2),
            (x_own, (rows, extra), lambda i, p: (0, at)),
            (x_other, (rows, extra), lambda i, p: (0, at)),
            (w_down, (size, quarter), lambda i, p: (i, 0)),
        ],
        [((2 * rows, quarter), BF16, (2 * rows, quarter), whole2), (shape, F32, shape, whole2)]
        + [(shape, BF16, shape, whole2)] * (halves - 1),
        place,
        flops=4 * rows * height * quarter,
    )


def backward_hidden(place, grad_own, arrived, slope, act, w_in, d, quarter):
    both_rows, hidden = slope.shape
    rows = both_rows // 2
    size = min(512, quarter)
    steps = quarter // size
    count = len(arrived)

    def kernel(place_ref, grad_own_ref, *refs):
        arrived_refs = refs[:count]
        slope_ref, act_ref, w_ref, grad_ref, out_own_ref, out_other_ref = refs[count:]

        @pl.when(pl.program_id(0) == 0)
        def _():
            grad_hidden = grad_own_ref[...]
            for ref in arrived_refs:
                grad_hidden += ref[...].astype(F32)
            grad_ref[:, :hidden] = (grad_hidden * slope_ref[...]).astype(BF16)
            grad_ref[:, hidden:] = (grad_hidden * act_ref[...]).astype(BF16)

        part = dot_cols(grad_ref[...], w_ref[...]).astype(BF16)
        out_own_ref[...] = part[:rows]
        out_other_ref[...] = part[rows:]

    shape = (both_rows, hidden)
    return call(
        kernel,
        (steps,),
        [(part, shape, whole2) for part in [grad_own, *arrived, slope, act]]
        + [(w_in, (size, 2 * hidden), lambda i, p: (d * steps + i, 0))],
        [((both_rows, 2 * hidden), BF16, (both_rows, 2 * hidden), whole2)]
        + [((rows, quarter), BF16, (rows, size), lambda i, p: (0, i))] * 2,
        place,
        flops=4 * both_rows * hidden * quarter,
    )


def row_part(place, grad_in, w_in, d, quarter):
    both_rows, both = grad_in.shape
    rows = both_rows // 2
    size = min(512, quarter)
    steps = quarter // size

    def kernel(place_ref, grad_ref, w_ref, out_own_ref, out_other_ref):
        part = dot_cols(grad_ref[...], w_ref[...]).astype(BF16)
        out_own_ref[...] = part[:rows]
        out_other_ref[...] = part[rows:]

    return call(
        kernel,
        (steps,),
        [
            (grad_in, grad_in.shape, whole2),
            (w_in, (size, both), lambda i, p: (d * steps + i, 0)),
        ],
        [((rows, quarter), BF16, (rows, size), lambda i, p: (0, i))] * 2,
        place,
        flops=2 * both_rows * both * quarter,
    )


def ends(grad, codes):
    upper = jnp.sum(grad * codes.astype(F32), axis=0, keepdims=True) * (1.0 / 255.0)
    return jnp.sum(grad, axis=0, keepdims=True) - upper, upper


def ranges_down(place, hidden, grads, codes, groups, halves):
    _, height, quarter = codes.shape
    size = height // groups
    per, rows = hidden_rows(groups, size, halves)
    blocks = height // halves // rows
    flat = [part for parts in hidden for part in parts]
    chunks = len(grads)

    def kernel(place_ref, *refs):
        hidden_refs = refs[: len(flat)]
        grad_refs = refs[len(flat) : len(flat) + chunks]
        code_ref, out_ref = refs[len(flat) + chunks :]
        step = pl.program_id(0)
        base = moved(step, blocks, place_ref) * per
        for d in range(halves):

            @pl.when(step // blocks == d)
            def _():
                for g in range(per):
                    cut = slice(g * size, (g + 1) * size)
                    grad = dot_rows(hidden_refs[d][:, cut], grad_refs[0][...])
                    for c in range(1, chunks):
                        grad += dot_rows(hidden_refs[c * halves + d][:, cut], grad_refs[c][...])
                    low, high = ends(grad, code_ref[0, cut, :])
                    out_ref[0, pl.ds(base + g, 1), :] = low
                    out_ref[1, pl.ds(base + g, 1), :] = high

    shape = (2, groups, quarter)
    return call(
        kernel,
        (height // rows,),
        [(part, (part.shape[0], rows), lambda i, p: (0, i % blocks)) for part in flat]
        + [(grad, grad.shape, whole2) for grad in grads]
        + [(codes, (1, rows, quarter), lambda i, p: (0, moved(i, blocks, p), 0))],
        [(shape, F32, shape, whole3)],
        place,
        flops=2 * sum(g.shape[0] for g in grads) * height * quarter,
    )[0]


def ranges_in(place, x, grads, codes, groups, halves):
    _, _, width, hidden = codes.shape
    size = width // groups
    per = 2
    rows = per * size
    blocks = width // halves // rows
    chunks = len(grads)

    def kernel(place_ref, *refs):
        x_refs = refs[: 2 * chunks]
        grad_refs = refs[2 * chunks : 3 * chunks]
        code_ref, out_ref = refs[3 * chunks :]
        base = moved(pl.program_id(0), blocks, place_ref) * per
        grad = None
        for c in range(chunks):
            left = jnp.concatenate([x_refs[2 * c][...], x_refs[2 * c + 1][...]], axis=0)
            part = dot_rows(left, grad_refs[c][...])
            grad = part if grad is None else grad + part
        for k in range(2):
            for g in range(per):
                cut = slice(g * size, (g + 1) * size)
                low, high = ends(
                    grad[cut, k * hidden : (k + 1) * hidden], code_ref[0, k, cut, :]
                )
                out_ref[2 * k, pl.ds(base + g, 1), :] = low
                out_ref[2 * k + 1, pl.ds(base + g, 1), :] = high

    shape = (4, groups, hidden)
    flat = [part for pair in x for part in pair]
    return call(
        kernel,
        (width // rows,),
        [(part, (part.shape[0], rows), lambda i, p: (0, i)) for part in flat]
        + [(grad, grad.shape, whole2) for grad in grads]
        + [(codes, (1, 2, rows, hidden), lambda i, p: (0, 0, moved(i, blocks, p), 0))],
        [(shape, F32, shape, whole3)],
        place,
        flops=2 * sum(g.size for g in grads) * width,
    )[0]


def local(
    tokens, target, routes, route_scores, in_codes, in_low, in_high, down_codes, down_low, down_high
):
    experts = lax.axis_size("expert")
    halves = lax.axis_size("half")
    me = lax.axis_index("expert")
    my_half = lax.axis_index("half")
    place = jnp.stack([me, my_half]).astype(jnp.int32)
    rows = tokens.shape[0] // CHUNKS
    quarter = target.shape[1]
    parts = range(halves)
    chunks = range(CHUNKS)

    weights = route_scores / jnp.sum(route_scores, axis=1, keepdims=True)
    names = routes[:, :, None] == jnp.arange(experts, dtype=jnp.int32)[None, None, :]
    table = jnp.sum(jnp.where(names, weights[:, :, None], 0.0), axis=1)
    top = lax.reduce_precision(table, 8, 7)
    middle = lax.reduce_precision(table - top, 8, 7)
    bottom = table - top - middle
    extra = -(-3 * experts // 128) * 128
    terms = jnp.concatenate([top, middle, bottom], axis=1)
    terms = jnp.pad(terms, ((0, 0), (0, extra - terms.shape[1]))).astype(BF16)

    mine = [
        lax.dynamic_slice_in_dim(tokens, (my_half ^ d) * quarter, quarter, 1) for d in parts
    ]
    mine = jnp.concatenate(mine + [terms], axis=1)
    x = [gather_rows(mine[c * rows : (c + 1) * rows]) for c in chunks]
    w_in = dequant_in(place, in_codes, in_low, in_high, halves)
    w_down = dequant_down(place, down_codes, down_low, down_high, halves)

    hidden, slope, act = [], [], []
    for c in chunks:
        own, chunk_slope, chunk_act = forward_in(place, *x[c], w_in)
        hidden.append([own] + [swap(own, "half", d) for d in parts if d])
        slope.append(chunk_slope)
        act.append(chunk_act)

    errors = []
    for c in chunks:
        out_own, out_other = forward_down(place, hidden[c], w_down, *x[c], extra)
        mixed = scatter_rows(out_own, swap(out_other, "expert", 1))
        wanted = target[c * rows : (c + 1) * rows].astype(F32)
        errors.append(gather_rows((mixed - wanted).astype(BF16)))

    grads, grad_own, arrived = [], [], []
    for c in chunks:
        grad, own, *others = backward_down(place, *errors[c], *x[c], w_down, extra, halves)
        grads.append(grad)
        grad_own.append(own)
        arrived.append([swap(other, "half", d + 1) for d, other in enumerate(others)])

    grad_in, grad_tokens = [], []
    for c in chunks:
        total = None
        for d in reversed(parts):
            if d == halves - 1:
                both, own, other = backward_hidden(
                    place, grad_own[c], arrived[c], slope[c], act[c], w_in, d, quarter
                )
                grad_in.append(both)
            else:
                own, other = row_part(place, grad_in[c], w_in, d, quarter)
            summed = own.astype(F32) + swap(other, "expert", 1).astype(F32)
            if d:
                summed = swap(summed.astype(BF16), "half", d)
            total = summed if total is None else total.astype(F32) + summed.astype(F32)
        grad_tokens.append(total)
    grad_tokens = [scatter_sum(total) for total in grad_tokens]

    down_grad = ranges_down(place, hidden, grads, down_codes, down_low.shape[1], halves)
    in_grad = ranges_in(place, x, grad_in, in_codes, in_low.shape[2], halves)
    return (
        jnp.concatenate(grad_tokens, axis=0).astype(BF16),
        in_grad[None],
        down_grad[None],
    )


def scatter_sum(total):
    for distance in reversed(far_distances()):
        half = total.shape[0] // 2
        arrived = swap(total[half:].astype(BF16), "expert", distance)
        total = total[:half].astype(F32) + arrived.astype(F32)
    return total


def solution(mesh):
    placed = (
        P("expert", None),
        P("expert", "half"),
        P("expert", None),
        P("expert", None),
        P("expert", None, None, "half"),
        P("expert", None, None, "half"),
        P("expert", None, None, "half"),
        P("expert", None, "half"),
        P("expert", None, "half"),
        P("expert", None, "half"),
    )
    return jax.shard_map(
        local,
        mesh=mesh,
        in_specs=placed,
        out_specs=(
            P("expert", "half"),
            P("expert", None, None, "half"),
            P("expert", None, None, "half"),
        ),
        check_vma=False,
    )
```

time: 489 us -> 246 us (0.50); the launches traced: 480 us -> 244 us
  waiting for transfers between devices: 275 us -> 79.2 us
  Pallas kernels: 0 us -> 80.1 us
  matrix products: 72.2 us -> 0 us
  other arithmetic: 57.8 us -> 7.8 us
  starting transfers between devices: 30.9 us -> 53.4 us
  between operations: 14.7 us -> 1.35 us
  local copies, waits for them, and re-layouts: 29.6 us -> 22.6 us
    all_to_all x4 -> x0, waiting for transfers between devices: 149 us -> none  [the longest x1 55.1 us: local(): lax.all_to_all(send_rows.reshape(experts, capacity, -1), 'expert', split_...]
    reduce_scatter x2 -> x0, waiting for transfers between devices: 91.2 us -> none  [the longest x1 54.5 us: local(): lax.psum_scatter(row_part, 'half', scatter_dimension=1, tiled=True)]
    pallas_call x0 -> x14, Pallas kernels: none -> 80.1 us  [call(): pl.pallas_call(kernel, grid_spec=spec, out_shape=[jax.ShapeDtypeStruct(sh...]
    ppermute x0 -> x40, waiting for transfers between devices: none -> 79.2 us  [swap(): return lax.ppermute(array, axis, [(i, i ^ distance) for i in range(size)])]
    dot_general x9 -> x0, matrix products: 72.2 us -> none  [the longest x3 28.4 us: contract_rows(): lax.dot_general(left, right, (((0,), (0,)), ((), ())), preferred_element_...]
    ppermute x0 -> x40, starting transfers between devices: none -> 53.4 us  [swap(): return lax.ppermute(array, axis, [(i, i ^ distance) for i in range(size)])]
    convert_element_type x8 -> x9, other arithmetic: 45.6 us -> 2.75 us  [the longest x2 2.34 us: local(): summed = swap(summed.astype(BF16), 'half', d)]
    all_gather x1 -> x0, waiting for transfers between devices: 34.4 us -> none  [local(): hidden_all = lax.all_gather(hidden, 'half', axis=1, tiled=True)]
  transfers between devices with their start and end apart: 7 -> 40, of which waited for: 7 -> 23; matrix products, arithmetic and copies ran while one was open for 13% -> 2% of each run, Pallas kernels for 0% -> 33%
where the time goes in v1:
time: 246 us; the launch traced here: 244 us
  Pallas kernels  80.1 us (33%)
  waiting for transfers between devices  79.2 us (32%)
  starting transfers between devices  53.4 us (22%)
  local copies, waits for them, and re-layouts  22.6 us (9%)
  other arithmetic  7.8 us (3%)
    pallas_call x14, Pallas kernels, call(): pl.pallas_call(kernel, grid_spec=spec, out_shape=[jax.ShapeDtypeStruct(sh...  80.1 us
    ppermute x40, waiting for transfers between devices, swap(): return lax.ppermute(array, axis, [(i, i ^ distance) for i in range(size)])  79.2 us
    ppermute x40, starting transfers between devices, swap(): return lax.ppermute(array, axis, [(i, i ^ distance) for i in range(size)])  53.4 us
    unnamed x87, local copies, waits for them, and re-layouts  21.4 us
  transfers between devices with their start and end apart: 40, of which 23 were waited for; matrix products, arithmetic and copies ran while one was open for 2% of the time, Pallas kernels for 33%

profile of v1, /device:TPU:0, one launch (start us, length us, event | category | flops | bytes accessed | tf_op | source)
XLA Modules:
  0.0 244.5 jit_solution(14827876846941009905)
XLA Ops:
  4.0 4.1 %collective-permute-start = (bf16[16,4224]{1,0:T(8,128)(2,1)S(1)}, bf16[16,4224]{1,0:T(8,128)(2,1)S(1)}, u32[]{:S(2)}, u32[]{:S(2)}) collective-permute-start(bf16[16,4224]{1,0:T(8,128)(2,1)S(1)} %get-tuple-element.72), channel_id=1, source_target_pairs={{0,16},{2,18},{4,20},{6,22},{8,24},{10,26},{12,28},{14,30},{16,0},... | collective-permute-start | bytes 405512 | tf_op jit(solution)/shard_map/ppermute | solution.py:18
  8.2 10.1 %collective-permute-done = bf16[16,4224]{1,0:T(8,128)(2,1)S(1)} collective-permute-done((bf16[16,4224]{1,0:T(8,128)(2,1)S(1)}, bf16[16,4224]{1,0:T(8,128)(2,1)S(1)}, u32[]{:S(2)}, u32[]{:S(2)}) %collective-permute-start) | collective-permute-done | bytes 135200 | tf_op jit(solution)/shard_map/ppermute | solution.py:18
  18.5 2.1 collective-permute-done.20
  21.2 6.6 %collective-permute-done.1 = bf16[32,4224]{1,0:T(8,128)(2,1)S(1)} collective-permute-done((bf16[32,4224]{1,0:T(8,128)(2,1)S(1)}, bf16[32,4224]{1,0:T(8,128)(2,1)S(1)}, u32[]{:S(2)}, u32[]{:S(2)}) %collective-permute-start.1) | collective-permute-done | bytes 270368 | tf_op jit(solution)/shard_map/ppermute | solution.py:18
  27.9 1.9 collective-permute-start.2
  29.8 2.2 collective-permute-done.21
  32.1 1.6 collective-permute-start.22
  33.7 9.5 %collective-permute-done.2 = bf16[64,4224]{1,0:T(8,128)(2,1)S(1)} collective-permute-done((bf16[64,4224]{1,0:T(8,128)(2,1)S(1)}, bf16[64,4224]{1,0:T(8,128)(2,1)S(1)}, u32[]{:S(2)}, u32[]{:S(2)}) %collective-permute-start.2) | collective-permute-done | bytes 540704 | tf_op jit(solution)/shard_map/ppermute | solution.py:18
  43.4 7.2 %collective-permute-done.22 = bf16[64,4224]{1,0:T(8,128)(2,1)S(1)} collective-permute-done((bf16[64,4224]{1,0:T(8,128)(2,1)S(1)}, bf16[64,4224]{1,0:T(8,128)(2,1)S(1)}, u32[]{:S(2)}, u32[]{:S(2)}) %collective-permute-start.22) | collective-permute-done | bytes 540704 | tf_op jit(solution)/shard_map/ppermute | solution.py:18
  51.7 8.7 %shard_map.121.w_ref.refs_3_ = bf16[4096,1536]{1,0:T(8,128)(2,1)S(1)} custom-call(s32[2]{0:T(128)S(1)} %pad_add_fusion.place_ref, bf16[1,2,4096,768]{3,2,1,0:T(8,128)(2,1)} %refs_6_.2, f32[1,2,32,768]{3,2,1,0:T(8,128)S(1)} %copy-done.30, f32[1,2,32,768]{3,2,1,0:T(8,128)S(1)} %copy-done.31), custom_call_target="tpu_custom_call" | custom-call | bytes 25559040 | tf_op jit(solution)/shard_map/pallas_call | solution.py:86
  60.5 7.4 %shard_map.122 = (bf16[256,768]{1,0:T(8,128)(2,1)S(1)}, f32[256,768]{1,0:T(8,128)S(1)}, f32[256,768]{1,0:T(8,128)S(1)}) custom-call(s32[2]{0:T(128)S(1)} %pad_add_fusion.place_ref, bf16[128,4224]{1,0:T(8,128)(2,1)S(1)} %pad_maximum_fusion.own_ref.refs_3_.refs_0_, bf16[128,4224]{1,0:T(8,128)(2,1)S(1)} %collective-permute-done.3.other_ref.refs_4_.refs_1_, ...), custom_call_target="tpu_custom_call" | custom-call | flops 3221225472 | bytes 16711680 | tf_op jit(solution)/shard_map/pallas_call | solution.py:86
  67.9 1.3 collective-permute-start.4
  69.3 2.8 %copy-done.4 = bf16[1,1536,2048]{2,1,0:T(8,128)(2,1)S(1)} copy-done((bf16[1,1536,2048]{2,1,0:T(8,128)(2,1)S(1)}, bf16[1,1536,2048]{2,1,0:T(8,128)(2,1)}, u32[]{:S(2)}) %copy-start.4) | copy-done | bytes 6291480
  72.1 2.1 shard_map.123.refs_2_.w_ref
  74.3 2.6 %copy-done = bf16[1536,2048]{1,0:T(8,128)(2,1)} copy-done((bf16[1536,2048]{1,0:T(8,128)(2,1)}, bf16[1536,2048]{1,0:T(8,128)(2,1)S(1)}, u32[]{:S(2)}) %copy-start) | copy-done | bytes 6291480
  76.9 8.6 %shard_map.128 = (bf16[256,768]{1,0:T(8,128)(2,1)S(1)}, f32[256,768]{1,0:T(8,128)S(1)}, f32[256,768]{1,0:T(8,128)S(1)}) custom-call(s32[2]{0:T(128)S(1)} %pad_add_fusion.place_ref, bf16[128,4224]{1,0:T(8,128)(2,1)S(1)} %pad_maximum_fusion.1.own_ref.refs_3_.refs_2_, bf16[128,4224]{1,0:T(8,128)(2,1)} %collective-permute-done.23.other_ref.refs_4_.refs_3_, ...), custom_call_target="tpu_custom_call" | custom-call | flops 3221225472 | bytes 16711680 | tf_op jit(solution)/shard_map/pallas_call | solution.py:86
  90.6 4.1 %shard_map.124 = (bf16[128,2048]{1,0:T(8,128)(2,1)S(1)}, bf16[128,2048]{1,0:T(8,128)(2,1)}) custom-call(s32[2]{0:T(128)S(1)} %pad_add_fusion.place_ref, bf16[256,768]{1,0:T(8,128)(2,1)S(1)} %copy-done.19, bf16[256,768]{1,0:T(8,128)(2,1)S(1)} %copy-done.22, bf16[1536,2048]{1,0:T(8,128)(2,1)S(1)} %copy-done.1, ...), custom_call_target="tpu_custom_call" | custom-call | flops 1610612736 | bytes 10289152 | tf_op jit(solution)/shard_map/pallas_call | solution.py:86
  94.7 3.8 %collective-permute-done.24.refs_1_.refs_3_ = bf16[256,768]{1,0:T(8,128)(2,1)S(1)} collective-permute-done((bf16[256,768]{1,0:T(8,128)(2,1)S(1)}, bf16[256,768]{1,0:T(8,128)(2,1)S(1)}, u32[]{:S(2)}, u32[]{:S(2)}) %collective-permute-start.24) | collective-permute-done | bytes 393248 | tf_op jit(solution)/shard_map/ppermute | solution.py:18
  101.3 4.5 %shard_map.129 = (bf16[128,2048]{1,0:T(8,128)(2,1)S(1)}, bf16[128,2048]{1,0:T(8,128)(2,1)S(1)}) custom-call(s32[2]{0:T(128)S(1)} %pad_add_fusion.place_ref, bf16[256,768]{1,0:T(8,128)(2,1)S(1)} %copy-done.25, bf16[256,768]{1,0:T(8,128)(2,1)S(1)} %copy-done.28, bf16[1536,2048]{1,0:T(8,128)(2,1)S(1)} %copy-done.2, ...), custom_call_target="tpu_custom_call" | custom-call | flops 1610612736 | bytes 10289152 | tf_op jit(solution)/shard_map/pallas_call | solution.py:86
  106.0 1.6 collective-permute-start.6
  107.8 1.6 collective-permute-start.26
  109.4 5.7 %collective-permute-done.6 = bf16[64,2048]{1,0:T(8,128)(2,1)S(1)} collective-permute-done((bf16[64,2048]{1,0:T(8,128)(2,1)S(1)}, bf16[64,2048]{1,0:T(8,128)(2,1)S(1)}, u32[]{:S(2)}, u32[]{:S(2)}) %collective-permute-start.6) | collective-permute-done | bytes 262176 | tf_op jit(solution)/shard_map/ppermute | solution.py:18
  115.2 1.0 collective-permute-start.7
  116.2 4.1 %collective-permute-done.26 = bf16[64,2048]{1,0:T(8,128)(2,1)S(1)} collective-permute-done((bf16[64,2048]{1,0:T(8,128)(2,1)S(1)}, bf16[64,2048]{1,0:T(8,128)(2,1)S(1)}, u32[]{:S(2)}, u32[]{:S(2)}) %collective-permute-start.26) | collective-permute-done | bytes 262176 | tf_op jit(solution)/shard_map/ppermute | solution.py:18
  120.4 1.0 collective-permute-start.27
  121.4 4.3 %collective-permute-start.8 = (bf16[16,2048]{1,0:T(8,128)(2,1)S(1)}, bf16[16,2048]{1,0:T(8,128)(2,1)S(1)}, u32[]{:S(2)}, u32[]{:S(2)}) collective-permute-start(bf16[16,2048]{1,0:T(8,128)(2,1)S(1)} %fusion.8), channel_id=1, source_target_pairs={{0,16},{2,18},{4,20},{6,22},{8,24},{10,26},{12,28},{14,30},{16,0},... | collective-permute-start | bytes 196616 | tf_op jit(solution)/shard_map/ppermute | solution.py:18
  125.7 4.0 %collective-permute-start.28 = (bf16[16,2048]{1,0:T(8,128)(2,1)S(1)}, bf16[16,2048]{1,0:T(8,128)(2,1)S(1)}, u32[]{:S(2)}, u32[]{:S(2)}) collective-permute-start(bf16[16,2048]{1,0:T(8,128)(2,1)S(1)} %fusion.3), channel_id=1, source_target_pairs={{0,16},{2,18},{4,20},{6,22},{8,24},{10,26},{12,28},{14,30},{16,0},... | collective-permute-start | bytes 196616 | tf_op jit(solution)/shard_map/ppermute | solution.py:18
  129.7 2.4 collective-permute-done.28
  132.2 2.8 %collective-permute-start.29 = (bf16[16,2048]{1,0:T(8,128)(2,1)S(1)}, bf16[16,2048]{1,0:T(8,128)(2,1)S(1)}, u32[]{:S(2)}, u32[]{:S(2)}) collective-permute-start(bf16[16,2048]{1,0:T(8,128)(2,1)S(1)} %get-tuple-element.77), channel_id=1, source_target_pairs={{0,16},{2,18},{4,20},{6,22},{8,24},{10,26},{12,28},{14,30},{16,0},... | collective-permute-start | bytes 196616 | tf_op jit(solution)/shard_map/ppermute | solution.py:18
  135.2 3.0 %collective-permute-done.29 = bf16[16,2048]{1,0:T(8,128)(2,1)S(1)} collective-permute-done((bf16[16,2048]{1,0:T(8,128)(2,1)S(1)}, bf16[16,2048]{1,0:T(8,128)(2,1)S(1)}, u32[]{:S(2)}, u32[]{:S(2)}) %collective-permute-start.29) | collective-permute-done | bytes 65568 | tf_op jit(solution)/shard_map/ppermute | solution.py:18
  138.2 3.7 %collective-permute-start.30 = (bf16[32,2048]{1,0:T(8,128)(2,1)S(1)}, bf16[32,2048]{1,0:T(8,128)(2,1)S(1)}, u32[]{:S(2)}, u32[]{:S(2)}) collective-permute-start(bf16[32,2048]{1,0:T(8,128)(2,1)S(1)} %pad_maximum_fusion.12), channel_id=1, source_target_pairs={{0,8},{2,10},{4,12},{6,14},{8,0},{10,2},{12,4},{14,6},{16,24},{18,... | collective-permute-start | bytes 393224 | tf_op jit(solution)/shard_map/ppermute | solution.py:18
  142.0 2.5 %collective-permute-start.10 = (bf16[32,2048]{1,0:T(8,128)(2,1)S(1)}, bf16[32,2048]{1,0:T(8,128)(2,1)S(1)}, u32[]{:S(2)}, u32[]{:S(2)}) collective-permute-start(bf16[32,2048]{1,0:T(8,128)(2,1)S(1)} %pad_maximum_fusion.11), channel_id=1, source_target_pairs={{0,8},{2,10},{4,12},{6,14},{8,0},{10,2},{12,4},{14,6},{16,24},{18,... | collective-permute-start | bytes 393224 | tf_op jit(solution)/shard_map/ppermute | solution.py:18
  144.9 1.6 collective-permute-start.31
  147.5 1.6 collective-permute-start.11
  149.0 2.4 collective-permute-done.31
  151.5 2.7 %collective-permute-done.11 = bf16[64,2048]{1,0:T(8,128)(2,1)S(1)} collective-permute-done((bf16[64,2048]{1,0:T(8,128)(2,1)S(1)}, bf16[64,2048]{1,0:T(8,128)(2,1)S(1)}, u32[]{:S(2)}, u32[]{:S(2)}) %collective-permute-start.11) | collective-permute-done | bytes 262176 | tf_op jit(solution)/shard_map/ppermute | solution.py:18
  154.4 4.7 %shard_map.130 = (bf16[256,2048]{1,0:T(8,128)(2,1)S(1)}, f32[256,768]{1,0:T(8,128)S(1)}, bf16[256,768]{1,0:T(8,128)(2,1)S(1)}) custom-call(s32[2]{0:T(128)S(1)} %pad_add_fusion.place_ref, bf16[128,2048]{1,0:T(8,128)(2,1)S(1)} %pad_maximum_fusion.5.err_own_ref, bf16[128,2048]{1,0:T(8,128)(2,1)S(1)} %collective-permute-done.32.err_other_ref, ...), custom_call_target="tpu_custom_call" | custom-call | flops 1610612736 | bytes 11730944 | tf_op jit(solution)/shard_map/pallas_call | solution.py:86
  159.0 1.0 copy-done.32
  160.8 2.8 %copy-done.3 = bf16[1536,2048]{1,0:T(8,128)(2,1)S(1)} copy-done((bf16[1536,2048]{1,0:T(8,128)(2,1)S(1)}, bf16[1536,2048]{1,0:T(8,128)(2,1)}, u32[]{:S(2)}) %copy-start.3) | copy-done | bytes 6291480
  163.6 3.9 %shard_map.125 = (bf16[256,2048]{1,0:T(8,128)(2,1)S(1)}, f32[256,768]{1,0:T(8,128)S(1)}, bf16[256,768]{1,0:T(8,128)(2,1)S(1)}) custom-call(s32[2]{0:T(128)S(1)} %pad_add_fusion.place_ref, bf16[128,2048]{1,0:T(8,128)(2,1)S(1)} %pad_maximum_fusion.4.err_own_ref, bf16[128,2048]{1,0:T(8,128)(2,1)S(1)} %collective-permute-done.12.err_other_ref, ...), custom_call_target="tpu_custom_call" | custom-call | flops 1610612736 | bytes 11730944 | tf_op jit(solution)/shard_map/pallas_call | solution.py:86
  167.5 1.3 collective-permute-start.13
  168.8 3.1 %collective-permute-done.33.refs_0_ = bf16[256,768]{1,0:T(8,128)(2,1)S(1)} collective-permute-done((bf16[256,768]{1,0:T(8,128)(2,1)S(1)}, bf16[256,768]{1,0:T(8,128)(2,1)S(1)}, u32[]{:S(2)}, u32[]{:S(2)}) %collective-permute-start.33) | collective-permute-done | bytes 393248 | tf_op jit(solution)/shard_map/ppermute | solution.py:18
  172.0 3.9 %shard_map.131 = (bf16[256,1536]{1,0:T(8,128)(2,1)S(1)}, bf16[128,2048]{1,0:T(8,128)(2,1)S(1)}, bf16[128,2048]{1,0:T(8,128)(2,1)}) custom-call(s32[2]{0:T(128)S(1)} %pad_add_fusion.place_ref, f32[256,768]{1,0:T(8,128)S(1)} %get-tuple-element.44.grad_own_ref, bf16[256,768]{1,0:T(8,128)(2,1)S(1)} %collective-permute-done.33.refs_0_, ...), custom_call_target="tpu_custom_call" | custom-call | flops 1610612736 | bytes 17170432 | tf_op jit(solution)/shard_map/pallas_call | solution.py:86
  176.0 3.2 %copy-done.5 = bf16[1,1536,2048]{2,1,0:T(8,128)(2,1)S(1)} copy-done((bf16[1,1536,2048]{2,1,0:T(8,128)(2,1)S(1)}, bf16[1,1536,2048]{2,1,0:T(8,128)(2,1)}, u32[]{:S(2)}) %copy-start.5) | copy-done | bytes 6291480
  179.2 6.5 %shard_map.134 = f32[2,12,2048]{2,1,0:T(8,128)S(1)} custom-call(s32[2]{0:T(128)S(1)} %pad_add_fusion.place_ref, bf16[256,768]{1,0:T(8,128)(2,1)S(1)} %copy-done.20, bf16[256,768]{1,0:T(8,128)(2,1)S(1)} %copy-done.23, bf16[256,768]{1,0:T(8,128)(2,1)S(1)} %copy-done.26, bf16[256,768]{1,0:T(8,128)(2,1)S(1)} %copy-done.29, ...), custom_call_target="tpu_custom_call" | custom-call | flops 3221225472 | bytes 10158080 | tf_op jit(solution)/shard_map/pallas_call | solution.py:86
  186.6 3.7 %shard_map.132 = (bf16[128,2048]{1,0:T(8,128)(2,1)S(1)}, bf16[128,2048]{1,0:T(8,128)(2,1)}) custom-call(s32[2]{0:T(128)S(1)} %pad_add_fusion.place_ref, bf16[256,1536]{1,0:T(8,128)(2,1)S(1)} %get-tuple-element.50.grad_ref.refs_5_, bf16[4096,1536]{1,0:T(8,128)(2,1)S(1)} %shard_map.121.w_ref.refs_3_), custom_call_target="tpu_custom_call" | custom-call | flops 1610612736 | bytes 14417920 | tf_op jit(solution)/shard_map/pallas_call | solution.py:86
  190.5 3.4 %shard_map.126 = (bf16[256,1536]{1,0:T(8,128)(2,1)S(1)}, bf16[128,2048]{1,0:T(8,128)(2,1)S(1)}, bf16[128,2048]{1,0:T(8,128)(2,1)S(1)}) custom-call(s32[2]{0:T(128)S(1)} %pad_add_fusion.place_ref, f32[256,768]{1,0:T(8,128)S(1)} %get-tuple-element.32.grad_own_ref, bf16[256,768]{1,0:T(8,128)(2,1)S(1)} %collective-permute-done.13.refs_0_, ...), custom_call_target="tpu_custom_call" | custom-call | flops 1610612736 | bytes 17170432 | tf_op jit(solution)/shard_map/pallas_call | solution.py:86
  194.4 3.1 %shard_map.127 = (bf16[128,2048]{1,0:T(8,128)(2,1)S(1)}, bf16[128,2048]{1,0:T(8,128)(2,1)S(1)}) custom-call(s32[2]{0:T(128)S(1)} %pad_add_fusion.place_ref, bf16[256,1536]{1,0:T(8,128)(2,1)S(1)} %get-tuple-element.38.grad_ref.refs_4_, bf16[4096,1536]{1,0:T(8,128)(2,1)S(1)} %shard_map.121.w_ref.refs_3_), custom_call_target="tpu_custom_call" | custom-call | flops 1610612736 | bytes 14417920 | tf_op jit(solution)/shard_map/pallas_call | solution.py:86
  197.6 1.2 add_convert_fusion
  199.7 1.2 add_convert_fusion.1
  200.8 1.3 collective-permute-start.15
  202.2 15.4 %shard_map.133 = f32[4,32,768]{2,1,0:T(8,128)} custom-call(s32[2]{0:T(128)S(1)} %pad_add_fusion.place_ref, bf16[128,4224]{1,0:T(8,128)(2,1)S(1)} %pad_maximum_fusion.own_ref.refs_3_.refs_0_, bf16[128,4224]{1,0:T(8,128)(2,1)S(1)} %collective-permute-done.3.other_ref.refs_4_.refs_1_, bf16[128,4224]{1,0:T(8,128)(2,1)S(1)} %pad_maximum_fusion.1.own_ref.refs_3_.refs_2_, ...), custom_call_target="tpu_custom_call" | custom-call | flops 6442450944 | bytes 18874368 | tf_op jit(solution)/shard_map/pallas_call | solution.py:86
  217.6 1.2 add_add_fusion
  218.9 1.6 collective-permute-start.37
  220.5 3.9 %collective-permute-done.15 = bf16[128,2048]{1,0:T(8,128)(2,1)S(1)} collective-permute-done((bf16[128,2048]{1,0:T(8,128)(2,1)S(1)}, bf16[128,2048]{1,0:T(8,128)(2,1)S(1)}, u32[]{:S(2)}, u32[]{:S(2)}) %collective-permute-start.15) | collective-permute-done | bytes 524320 | tf_op jit(solution)/shard_map/ppermute | solution.py:18
  224.6 1.5 collective-permute-start.17
  227.2 2.1 collective-permute-start.38
  229.3 3.4 %collective-permute-done.17 = bf16[64,2048]{1,0:T(8,128)(2,1)S(1)} collective-permute-done((bf16[64,2048]{1,0:T(8,128)(2,1)S(1)}, bf16[64,2048]{1,0:T(8,128)(2,1)S(1)}, u32[]{:S(2)}, u32[]{:S(2)}) %collective-permute-start.17) | collective-permute-done | bytes 262176 | tf_op jit(solution)/shard_map/ppermute | solution.py:18
  232.8 2.1 collective-permute-start.18
  234.9 2.5 %collective-permute-start.39 = (bf16[16,2048]{1,0:T(8,128)(2,1)S(1)}, bf16[16,2048]{1,0:T(8,128)(2,1)S(1)}, u32[]{:S(2)}, u32[]{:S(2)}) collective-permute-start(bf16[16,2048]{1,0:T(8,128)(2,1)S(1)} %slice.266), channel_id=1, source_target_pairs={{0,16},{2,18},{4,20},{6,22},{8,24},{10,26},{12,28},{14,30},{16,0},... | collective-permute-start | bytes 196616 | tf_op jit(solution)/shard_map/ppermute | solution.py:18
  237.4 1.1 collective-permute-done.18
  238.6 2.1 collective-permute-start.19
  240.6 1.6 collective-permute-done.39
  242.3 1.5 collective-permute-done.19
  (167 shorter events, 21.5 us)
Async XLA Ops:
  4.0 14.3 %collective-permute-start = (bf16[16,4224]{1,0:T(8,128)(2,1)S(1)}, bf16[16,4224]{1,0:T(8,128)(2,1)S(1)}, u32[]{:S(2)}, u32[]{:S(2)}) collective-permute-start(bf16[16,4224]{1,0:T(8,128)(2,1)S(1)} %get-tuple-element.72), channel_id=1, source_target_pairs={{0,16},{2,18},{4,20},{6,22},{8,24},{10,26},{12,28},{14,30},{16,0},... | collective-permute-start | bytes 405512 | tf_op jit(solution)/shard_map/ppermute | solution.py:18
  8.1 12.4 %collective-permute-start.20 = (bf16[16,4224]{1,0:T(8,128)(2,1)S(1)}, bf16[16,4224]{1,0:T(8,128)(2,1)S(1)}, u32[]{:S(2)}, u32[]{:S(2)}) collective-permute-start(bf16[16,4224]{1,0:T(8,128)(2,1)S(1)} %get-tuple-element.73), channel_id=1, source_target_pairs={{0,16},{2,18},{4,20},{6,22},{8,24},{10,26},{12,28},{14,30},{16,0},... | collective-permute-start | bytes 405512 | tf_op jit(solution)/shard_map/ppermute | solution.py:18
  18.4 9.5 %collective-permute-start.1 = (bf16[32,4224]{1,0:T(8,128)(2,1)S(1)}, bf16[32,4224]{1,0:T(8,128)(2,1)S(1)}, u32[]{:S(2)}, u32[]{:S(2)}) collective-permute-start(bf16[32,4224]{1,0:T(8,128)(2,1)S(1)} %pad_maximum_fusion.7), channel_id=1, source_target_pairs={{0,8},{2,10},{4,12},{6,14},{8,0},{10,2},{12,4},{14,6},{16,24},{18,... | collective-permute-start | bytes 811016 | tf_op jit(solution)/shard_map/ppermute | solution.py:18
  20.5 11.5 %collective-permute-start.21 = (bf16[32,4224]{1,0:T(8,128)(2,1)S(1)}, bf16[32,4224]{1,0:T(8,128)(2,1)S(1)}, u32[]{:S(2)}, u32[]{:S(2)}) collective-permute-start(bf16[32,4224]{1,0:T(8,128)(2,1)S(1)} %pad_maximum_fusion.8), channel_id=1, source_target_pairs={{0,8},{2,10},{4,12},{6,14},{8,0},{10,2},{12,4},{14,6},{16,24},{18,... | collective-permute-start | bytes 811016 | tf_op jit(solution)/shard_map/ppermute | solution.py:18
  27.9 15.3 %collective-permute-start.2 = (bf16[64,4224]{1,0:T(8,128)(2,1)S(1)}, bf16[64,4224]{1,0:T(8,128)(2,1)S(1)}, u32[]{:S(2)}, u32[]{:S(2)}) collective-permute-start(bf16[64,4224]{1,0:T(8,128)(2,1)S(1)} %pad_maximum_fusion.2), channel_id=1, source_target_pairs={{0,4},{2,6},{4,0},{6,2},{8,12},{10,14},{12,8},{14,10},{16,20},{18,... | collective-permute-start | bytes 1622024 | tf_op jit(solution)/shard_map/ppermute | solution.py:18
  32.1 18.5 %collective-permute-start.22 = (bf16[64,4224]{1,0:T(8,128)(2,1)S(1)}, bf16[64,4224]{1,0:T(8,128)(2,1)S(1)}, u32[]{:S(2)}, u32[]{:S(2)}) collective-permute-start(bf16[64,4224]{1,0:T(8,128)(2,1)S(1)} %pad_maximum_fusion.3), channel_id=1, source_target_pairs={{0,4},{2,6},{4,0},{6,2},{8,12},{10,14},{12,8},{14,10},{16,20},{18,... | collective-permute-start | bytes 1622024 | tf_op jit(solution)/shard_map/ppermute | solution.py:18
  43.3 7.5 %copy-start.30 = (f32[1,2,32,768]{3,2,1,0:T(8,128)S(1)}, f32[1,2,32,768]{3,2,1,0:T(8,128)}, u32[]{:S(2)}) copy-start(f32[1,2,32,768]{3,2,1,0:T(8,128)} %low_ref.2) | copy-start | bytes 589828
  43.3 17.2 %collective-permute-start.3 = (bf16[128,4224]{1,0:T(8,128)(2,1)S(1)}, bf16[128,4224]{1,0:T(8,128)(2,1)S(1)}, u32[]{:S(2)}, u32[]{:S(2)}) collective-permute-start(bf16[128,4224]{1,0:T(8,128)(2,1)S(1)} %pad_maximum_fusion.own_ref.refs_3_.refs_0_), channel_id=1, source_target_pairs={{0,2},{2,0},{4,6},{6,4},{8,10},{10,8},{12,14},{14,12},{16,18},{18,... | collective-permute-start | bytes 3244040 | tf_op jit(solution)/shard_map/ppermute | solution.py:18
  50.6 26.2 %collective-permute-start.23 = (bf16[128,4224]{1,0:T(8,128)(2,1)S(1)}, bf16[128,4224]{1,0:T(8,128)(2,1)}, u32[]{:S(2)}, u32[]{:S(2)}) collective-permute-start(bf16[128,4224]{1,0:T(8,128)(2,1)S(1)} %pad_maximum_fusion.1.own_ref.refs_3_.refs_2_), channel_id=1, source_target_pairs={{0,2},{2,0},{4,6},{6,4},{8,10},{10,8},{12,14},{14,12},{16,18},{18,... | collective-permute-start | bytes 3244040 | tf_op jit(solution)/shard_map/ppermute | solution.py:18
  60.4 8.8 %copy-start.35 = (f32[1,12,2048]{2,0,1:T(1,128)S(1)}, f32[1,12,2048]{2,0,1:T(1,128)}, u32[]{:S(2)}) copy-start(f32[1,12,2048]{2,0,1:T(1,128)} %param.18) | copy-start | bytes 294916
  60.4 8.8 %copy-start.36 = (f32[1,12,2048]{2,0,1:T(1,128)S(1)}, f32[1,12,2048]{2,0,1:T(1,128)}, u32[]{:S(2)}) copy-start(f32[1,12,2048]{2,0,1:T(1,128)} %param.19) | copy-start | bytes 294916
  67.8 6.4 %copy-start.6 = (f32[256,768]{1,0:T(8,128)}, f32[256,768]{1,0:T(8,128)S(1)}, u32[]{:S(2)}) copy-start(f32[256,768]{1,0:T(8,128)S(1)} %get-tuple-element.34.refs_1_) | copy-start | bytes 2359300
  67.8 6.4 %copy-start.8 = (f32[256,768]{1,0:T(8,128)}, f32[256,768]{1,0:T(8,128)S(1)}, u32[]{:S(2)}) copy-start(f32[256,768]{1,0:T(8,128)S(1)} %get-tuple-element.35.refs_2_) | copy-start | bytes 2359300
  67.8 6.4 %copy-start.18 = (bf16[256,768]{1,0:T(8,128)(2,1)}, bf16[256,768]{1,0:T(8,128)(2,1)S(1)}, u32[]{:S(2)}) copy-start(bf16[256,768]{1,0:T(8,128)(2,1)S(1)} %get-tuple-element.29.refs_0_) | copy-start | bytes 1179652
  67.9 21.0 %collective-permute-start.4 = (bf16[256,768]{1,0:T(8,128)(2,1)S(1)}, bf16[256,768]{1,0:T(8,128)(2,1)S(1)}, u32[]{:S(2)}, u32[]{:S(2)}) collective-permute-start(bf16[256,768]{1,0:T(8,128)(2,1)S(1)} %get-tuple-element.29.refs_0_), channel_id=1, source_target_pairs={{0,1},{1,0},{2,3},{3,2},{4,5},{5,4},{6,7},{7,6},{8,9},{9,8},{10,11... | collective-permute-start | bytes 1179656 | tf_op jit(solution)/shard_map/ppermute | solution.py:18
  76.9 12.7 %copy-start.1 = (bf16[1536,2048]{1,0:T(8,128)(2,1)S(1)}, bf16[1536,2048]{1,0:T(8,128)(2,1)}, u32[]{:S(2)}) copy-start(bf16[1536,2048]{1,0:T(8,128)(2,1)} %copy-done) | copy-start | bytes 18874372
  76.9 12.7 %copy-start.19 = (bf16[256,768]{1,0:T(8,128)(2,1)S(1)}, bf16[256,768]{1,0:T(8,128)(2,1)}, u32[]{:S(2)}) copy-start(bf16[256,768]{1,0:T(8,128)(2,1)} %copy-done.18) | copy-start | bytes 1179652
  87.3 11.2 %collective-permute-start.24 = (bf16[256,768]{1,0:T(8,128)(2,1)S(1)}, bf16[256,768]{1,0:T(8,128)(2,1)S(1)}, u32[]{:S(2)}, u32[]{:S(2)}) collective-permute-start(bf16[256,768]{1,0:T(8,128)(2,1)S(1)} %get-tuple-element.41.refs_0_.refs_2_), channel_id=1, source_target_pairs={{0,1},{1,0},{2,3},{3,2},{4,5},{5,4},{6,7},{7,6},{8,9},{9,8},{10,11... | collective-permute-start | bytes 1179656 | tf_op jit(solution)/shard_map/ppermute | solution.py:18
  90.6 8.7 %copy-start.2 = (bf16[1536,2048]{1,0:T(8,128)(2,1)S(1)}, bf16[1536,2048]{1,0:T(8,128)(2,1)}, u32[]{:S(2)}) copy-start(bf16[1536,2048]{1,0:T(8,128)(2,1)} %copy-done) | copy-start | bytes 18874372
  94.7 11.1 %collective-permute-start.5 = (bf16[128,2048]{1,0:T(8,128)(2,1)}, bf16[128,2048]{1,0:T(8,128)(2,1)S(1)}, u32[]{:S(2)}, u32[]{:S(2)}) collective-permute-start(bf16[128,2048]{1,0:T(8,128)(2,1)} %get-tuple-element.31), channel_id=1, source_target_pairs={{0,2},{2,0},{4,6},{6,4},{8,10},{10,8},{12,14},{14,12},{16,18},{18,... | collective-permute-start | bytes 1572872 | tf_op jit(solution)/shard_map/ppermute | solution.py:18
  101.3 53.1 %slice-start = ((s8[6291456]{0:T(1024)(128)(4,1)}), s8[4194304]{0:T(1024)(128)(4,1)S(1)}, s32[]{:S(2)}) async-start(s8[6291456]{0:T(1024)(128)(4,1)} %bitcast.4), calls=%async_computation | async-start | bytes 8388608
  105.7 2.0 collective-permute-start.25
  105.8 48.5 %slice-start.1 = ((s8[6291456]{0:T(1024)(128)(4,1)}), s8[2097152]{0:T(1024)(128)(4,1)S(1)}, s32[]{:S(2)}) async-start(s8[6291456]{0:T(1024)(128)(4,1)} %bitcast.4), calls=%async_computation.1 | async-start | bytes 4194304
  106.0 9.2 %collective-permute-start.6 = (bf16[64,2048]{1,0:T(8,128)(2,1)S(1)}, bf16[64,2048]{1,0:T(8,128)(2,1)S(1)}, u32[]{:S(2)}, u32[]{:S(2)}) collective-permute-start(bf16[64,2048]{1,0:T(8,128)(2,1)S(1)} %get-tuple-element.64), channel_id=1, source_target_pairs={{0,4},{2,6},{4,0},{6,2},{8,12},{10,14},{12,8},{14,10},{16,20},{18,... | collective-permute-start | bytes 786440 | tf_op jit(solution)/shard_map/ppermute | solution.py:18
  107.8 12.5 %collective-permute-start.26 = (bf16[64,2048]{1,0:T(8,128)(2,1)S(1)}, bf16[64,2048]{1,0:T(8,128)(2,1)S(1)}, u32[]{:S(2)}, u32[]{:S(2)}) collective-permute-start(bf16[64,2048]{1,0:T(8,128)(2,1)S(1)} %get-tuple-element.66), channel_id=1, source_target_pairs={{0,4},{2,6},{4,0},{6,2},{8,12},{10,14},{12,8},{14,10},{16,20},{18,... | collective-permute-start | bytes 786440 | tf_op jit(solution)/shard_map/ppermute | solution.py:18
  115.2 16.9 %copy-start.34 = (bf16[32,2048]{1,0:T(8,128)(2,1)S(1)}, bf16[32,2048]{1,0:T(8,128)(2,1)}, u32[]{:S(2)}) copy-start(bf16[32,2048]{1,0:T(8,128)(2,1)} %param.11) | copy-start | bytes 393220
  115.2 6.2 %collective-permute-start.7 = (bf16[32,2048]{1,0:T(8,128)(2,1)S(1)}, bf16[32,2048]{1,0:T(8,128)(2,1)S(1)}, u32[]{:S(2)}, u32[]{:S(2)}) collective-permute-start(bf16[32,2048]{1,0:T(8,128)(2,1)S(1)} %get-tuple-element.68), channel_id=1, source_target_pairs={{0,8},{2,10},{4,12},{6,14},{8,0},{10,2},{12,4},{14,6},{16,24},{18,... | collective-permute-start | bytes 393224 | tf_op jit(solution)/shard_map/ppermute | solution.py:18
  120.4 5.3 %collective-permute-start.27 = (bf16[32,2048]{1,0:T(8,128)(2,1)S(1)}, bf16[32,2048]{1,0:T(8,128)(2,1)S(1)}, u32[]{:S(2)}, u32[]{:S(2)}) collective-permute-start(bf16[32,2048]{1,0:T(8,128)(2,1)S(1)} %get-tuple-element.70), channel_id=1, source_target_pairs={{0,8},{2,10},{4,12},{6,14},{8,0},{10,2},{12,4},{14,6},{16,24},{18,... | collective-permute-start | bytes 393224 | tf_op jit(solution)/shard_map/ppermute | solution.py:18
  121.4 8.3 %collective-permute-start.8 = (bf16[16,2048]{1,0:T(8,128)(2,1)S(1)}, bf16[16,2048]{1,0:T(8,128)(2,1)S(1)}, u32[]{:S(2)}, u32[]{:S(2)}) collective-permute-start(bf16[16,2048]{1,0:T(8,128)(2,1)S(1)} %fusion.8), channel_id=1, source_target_pairs={{0,16},{2,18},{4,20},{6,22},{8,24},{10,26},{12,28},{14,30},{16,0},... | collective-permute-start | bytes 196616 | tf_op jit(solution)/shard_map/ppermute | solution.py:18
  125.7 6.4 %collective-permute-start.28 = (bf16[16,2048]{1,0:T(8,128)(2,1)S(1)}, bf16[16,2048]{1,0:T(8,128)(2,1)S(1)}, u32[]{:S(2)}, u32[]{:S(2)}) collective-permute-start(bf16[16,2048]{1,0:T(8,128)(2,1)S(1)} %fusion.3), channel_id=1, source_target_pairs={{0,16},{2,18},{4,20},{6,22},{8,24},{10,26},{12,28},{14,30},{16,0},... | collective-permute-start | bytes 196616 | tf_op jit(solution)/shard_map/ppermute | solution.py:18
  132.2 6.0 %collective-permute-start.29 = (bf16[16,2048]{1,0:T(8,128)(2,1)S(1)}, bf16[16,2048]{1,0:T(8,128)(2,1)S(1)}, u32[]{:S(2)}, u32[]{:S(2)}) collective-permute-start(bf16[16,2048]{1,0:T(8,128)(2,1)S(1)} %get-tuple-element.77), channel_id=1, source_target_pairs={{0,16},{2,18},{4,20},{6,22},{8,24},{10,26},{12,28},{14,30},{16,0},... | collective-permute-start | bytes 196616 | tf_op jit(solution)/shard_map/ppermute | solution.py:18
  135.0 7.0 %collective-permute-start.9 = (bf16[16,2048]{1,0:T(8,128)(2,1)S(1)}, bf16[16,2048]{1,0:T(8,128)(2,1)S(1)}, u32[]{:S(2)}, u32[]{:S(2)}) collective-permute-start(bf16[16,2048]{1,0:T(8,128)(2,1)S(1)} %get-tuple-element.76), channel_id=1, source_target_pairs={{0,16},{2,18},{4,20},{6,22},{8,24},{10,26},{12,28},{14,30},{16,0},... | collective-permute-start | bytes 196616 | tf_op jit(solution)/shard_map/ppermute | solution.py:18
  138.2 6.7 %collective-permute-start.30 = (bf16[32,2048]{1,0:T(8,128)(2,1)S(1)}, bf16[32,2048]{1,0:T(8,128)(2,1)S(1)}, u32[]{:S(2)}, u32[]{:S(2)}) collective-permute-start(bf16[32,2048]{1,0:T(8,128)(2,1)S(1)} %pad_maximum_fusion.12), channel_id=1, source_target_pairs={{0,8},{2,10},{4,12},{6,14},{8,0},{10,2},{12,4},{14,6},{16,24},{18,... | collective-permute-start | bytes 393224 | tf_op jit(solution)/shard_map/ppermute | solution.py:18
  142.0 5.4 %collective-permute-start.10 = (bf16[32,2048]{1,0:T(8,128)(2,1)S(1)}, bf16[32,2048]{1,0:T(8,128)(2,1)S(1)}, u32[]{:S(2)}, u32[]{:S(2)}) collective-permute-start(bf16[32,2048]{1,0:T(8,128)(2,1)S(1)} %pad_maximum_fusion.11), channel_id=1, source_target_pairs={{0,8},{2,10},{4,12},{6,14},{8,0},{10,2},{12,4},{14,6},{16,24},{18,... | collective-permute-start | bytes 393224 | tf_op jit(solution)/shard_map/ppermute | solution.py:18
  144.9 6.4 %collective-permute-start.31 = (bf16[64,2048]{1,0:T(8,128)(2,1)S(1)}, bf16[64,2048]{1,0:T(8,128)(2,1)S(1)}, u32[]{:S(2)}, u32[]{:S(2)}) collective-permute-start(bf16[64,2048]{1,0:T(8,128)(2,1)S(1)} %pad_maximum_fusion.10), channel_id=1, source_target_pairs={{0,4},{2,6},{4,0},{6,2},{8,12},{10,14},{12,8},{14,10},{16,20},{18,... | collective-permute-start | bytes 786440 | tf_op jit(solution)/shard_map/ppermute | solution.py:18
  147.5 6.7 %collective-permute-start.11 = (bf16[64,2048]{1,0:T(8,128)(2,1)S(1)}, bf16[64,2048]{1,0:T(8,128)(2,1)S(1)}, u32[]{:S(2)}, u32[]{:S(2)}) collective-permute-start(bf16[64,2048]{1,0:T(8,128)(2,1)S(1)} %pad_maximum_fusion.9), channel_id=1, source_target_pairs={{0,4},{2,6},{4,0},{6,2},{8,12},{10,14},{12,8},{14,10},{16,20},{18,... | collective-permute-start | bytes 786440 | tf_op jit(solution)/shard_map/ppermute | solution.py:18
  151.4 2.9 %collective-permute-start.32 = (bf16[128,2048]{1,0:T(8,128)(2,1)S(1)}, bf16[128,2048]{1,0:T(8,128)(2,1)S(1)}, u32[]{:S(2)}, u32[]{:S(2)}) collective-permute-start(bf16[128,2048]{1,0:T(8,128)(2,1)S(1)} %pad_maximum_fusion.5.err_own_ref), channel_id=1, source_target_pairs={{0,2},{2,0},{4,6},{6,4},{8,10},{10,8},{12,14},{14,12},{16,18},{18,... | collective-permute-start | bytes 1572872 | tf_op jit(solution)/shard_map/ppermute | solution.py:18
  154.2 6.6 %collective-permute-start.12 = (bf16[128,2048]{1,0:T(8,128)(2,1)S(1)}, bf16[128,2048]{1,0:T(8,128)(2,1)S(1)}, u32[]{:S(2)}, u32[]{:S(2)}) collective-permute-start(bf16[128,2048]{1,0:T(8,128)(2,1)S(1)} %pad_maximum_fusion.4.err_own_ref), channel_id=1, source_target_pairs={{0,2},{2,0},{4,6},{6,4},{8,10},{10,8},{12,14},{14,12},{16,18},{18,... | collective-permute-start | bytes 1572872 | tf_op jit(solution)/shard_map/ppermute | solution.py:18
  160.0 11.9 %collective-permute-start.33 = (bf16[256,768]{1,0:T(8,128)(2,1)S(1)}, bf16[256,768]{1,0:T(8,128)(2,1)S(1)}, u32[]{:S(2)}, u32[]{:S(2)}) collective-permute-start(bf16[256,768]{1,0:T(8,128)(2,1)S(1)} %get-tuple-element.45), channel_id=1, source_target_pairs={{0,1},{1,0},{2,3},{3,2},{4,5},{5,4},{6,7},{7,6},{8,9},{9,8},{10,11... | collective-permute-start | bytes 1179656 | tf_op jit(solution)/shard_map/ppermute | solution.py:18
  163.6 8.3 %copy-start.11 = (f32[256,768]{1,0:T(8,128)S(1)}, f32[256,768]{1,0:T(8,128)}, u32[]{:S(2)}) copy-start(f32[256,768]{1,0:T(8,128)} %copy-done.10) | copy-start | bytes 2359300
  163.6 8.3 %copy-start.13 = (f32[256,768]{1,0:T(8,128)S(1)}, f32[256,768]{1,0:T(8,128)}, u32[]{:S(2)}) copy-start(f32[256,768]{1,0:T(8,128)} %copy-done.12) | copy-start | bytes 2359300
  167.5 22.9 %collective-permute-start.13 = (bf16[256,768]{1,0:T(8,128)(2,1)S(1)}, bf16[256,768]{1,0:T(8,128)(2,1)S(1)}, u32[]{:S(2)}, u32[]{:S(2)}) collective-permute-start(bf16[256,768]{1,0:T(8,128)(2,1)S(1)} %get-tuple-element.33), channel_id=1, source_target_pairs={{0,1},{1,0},{2,3},{3,2},{4,5},{5,4},{6,7},{7,6},{8,9},{9,8},{10,11... | collective-permute-start | bytes 1179656 | tf_op jit(solution)/shard_map/ppermute | solution.py:18
  172.0 4.0 %copy-start.20 = (bf16[256,768]{1,0:T(8,128)(2,1)S(1)}, bf16[256,768]{1,0:T(8,128)(2,1)}, u32[]{:S(2)}) copy-start(bf16[256,768]{1,0:T(8,128)(2,1)} %copy-done.18) | copy-start | bytes 1179652
  172.0 4.0 %copy-start.23 = (bf16[256,768]{1,0:T(8,128)(2,1)S(1)}, bf16[256,768]{1,0:T(8,128)(2,1)}, u32[]{:S(2)}) copy-start(bf16[256,768]{1,0:T(8,128)(2,1)} %copy-done.21) | copy-start | bytes 1179652
  172.0 4.0 %copy-start.26 = (bf16[256,768]{1,0:T(8,128)(2,1)S(1)}, bf16[256,768]{1,0:T(8,128)(2,1)}, u32[]{:S(2)}) copy-start(bf16[256,768]{1,0:T(8,128)(2,1)} %copy-done.24) | copy-start | bytes 1179652
  172.0 4.0 %copy-start.29 = (bf16[256,768]{1,0:T(8,128)(2,1)S(1)}, bf16[256,768]{1,0:T(8,128)(2,1)}, u32[]{:S(2)}) copy-start(bf16[256,768]{1,0:T(8,128)(2,1)} %copy-done.27) | copy-start | bytes 1179652
  172.0 4.0 %copy-start.33 = (bf16[256,2048]{1,0:T(8,128)(2,1)S(1)}, bf16[256,2048]{1,0:T(8,128)(2,1)}, u32[]{:S(2)}) copy-start(bf16[256,2048]{1,0:T(8,128)(2,1)} %copy-done.32) | copy-start | bytes 3145732
  175.9 9.8 %copy-start.16 = (bf16[128,2048]{1,0:T(8,128)(2,1)}, bf16[128,2048]{1,0:T(8,128)(2,1)S(1)}, u32[]{:S(2)}) copy-start(bf16[128,2048]{1,0:T(8,128)(2,1)S(1)} %get-tuple-element.48) | copy-start | bytes 1572868
  175.9 10.7 %copy-start.14 = (bf16[256,1536]{1,0:T(8,128)(2,1)}, bf16[256,1536]{1,0:T(8,128)(2,1)S(1)}, u32[]{:S(2)}) copy-start(bf16[256,1536]{1,0:T(8,128)(2,1)S(1)} %get-tuple-element.50.grad_ref.refs_5_) | copy-start | bytes 2359300
  175.9 21.7 %collective-permute-start.34 = (bf16[128,2048]{1,0:T(8,128)(2,1)}, bf16[128,2048]{1,0:T(8,128)(2,1)}, u32[]{:S(2)}, u32[]{:S(2)}) collective-permute-start(bf16[128,2048]{1,0:T(8,128)(2,1)} %get-tuple-element.49), channel_id=1, source_target_pairs={{0,2},{2,0},{4,6},{6,4},{8,10},{10,8},{12,14},{14,12},{16,18},{18,... | collective-permute-start | bytes 1572872 | tf_op jit(solution)/shard_map/ppermute | solution.py:18
  190.4 27.3 %collective-permute-start.36 = (bf16[128,2048]{1,0:T(8,128)(2,1)}, bf16[128,2048]{1,0:T(8,128)(2,1)}, u32[]{:S(2)}, u32[]{:S(2)}) collective-permute-start(bf16[128,2048]{1,0:T(8,128)(2,1)} %get-tuple-element.52), channel_id=1, source_target_pairs={{0,2},{2,0},{4,6},{6,4},{8,10},{10,8},{12,14},{14,12},{16,18},{18,... | collective-permute-start | bytes 1572872 | tf_op jit(solution)/shard_map/ppermute | solution.py:18
  190.4 11.7 %slice-start.2 = ((s8[12582912]{0:T(1024)(128)(4,1)}), s8[4194304]{0:T(1024)(128)(4,1)S(1)}, s32[]{:S(2)}) async-start(s8[12582912]{0:T(1024)(128)(4,1)} %bitcast.6), calls=%async_computation.2 | async-start | bytes 8388608
  190.4 11.7 %slice-start.3 = ((s8[12582912]{0:T(1024)(128)(4,1)}), s8[4194304]{0:T(1024)(128)(4,1)S(1)}, s32[]{:S(2)}) async-start(s8[12582912]{0:T(1024)(128)(4,1)} %bitcast.6), calls=%async_computation.3 | async-start | bytes 8388608
  193.9 5.7 %collective-permute-start.14 = (bf16[128,2048]{1,0:T(8,128)(2,1)S(1)}, bf16[128,2048]{1,0:T(8,128)(2,1)}, u32[]{:S(2)}, u32[]{:S(2)}) collective-permute-start(bf16[128,2048]{1,0:T(8,128)(2,1)S(1)} %get-tuple-element.37), channel_id=1, source_target_pairs={{0,2},{2,0},{4,6},{6,4},{8,10},{10,8},{12,14},{14,12},{16,18},{18,... | collective-permute-start | bytes 1572872 | tf_op jit(solution)/shard_map/ppermute | solution.py:18
  194.4 7.7 %slice-start.4 = ((s8[12582912]{0:T(1024)(128)(4,1)}), s8[4194304]{0:T(1024)(128)(4,1)S(1)}, s32[]{:S(2)}) async-start(s8[12582912]{0:T(1024)(128)(4,1)} %bitcast.6), calls=%async_computation.4 | async-start | bytes 8388608
  197.5 23.0 %collective-permute-start.16 = (bf16[128,2048]{1,0:T(8,128)(2,1)S(1)}, bf16[128,2048]{1,0:T(8,128)(2,1)S(1)}, u32[]{:S(2)}, u32[]{:S(2)}) collective-permute-start(bf16[128,2048]{1,0:T(8,128)(2,1)S(1)} %get-tuple-element.40), channel_id=1, source_target_pairs={{0,2},{2,0},{4,6},{6,4},{8,10},{10,8},{12,14},{14,12},{16,18},{18,... | collective-permute-start | bytes 1572872 | tf_op jit(solution)/shard_map/ppermute | solution.py:18
  198.8 18.8 %collective-permute-start.35 = (bf16[128,2048]{1,0:T(8,128)(2,1)S(1)}, bf16[128,2048]{1,0:T(8,128)(2,1)S(1)}, u32[]{:S(2)}, u32[]{:S(2)}) collective-permute-start(bf16[128,2048]{1,0:T(8,128)(2,1)S(1)} %add_convert_fusion), channel_id=1, source_target_pairs={{0,1},{1,0},{2,3},{3,2},{4,5},{5,4},{6,7},{7,6},{8,9},{9,8},{10,11... | collective-permute-start | bytes 1572872 | tf_op jit(solution)/shard_map/ppermute | solution.py:18
  200.8 23.6 %collective-permute-start.15 = (bf16[128,2048]{1,0:T(8,128)(2,1)S(1)}, bf16[128,2048]{1,0:T(8,128)(2,1)S(1)}, u32[]{:S(2)}, u32[]{:S(2)}) collective-permute-start(bf16[128,2048]{1,0:T(8,128)(2,1)S(1)} %add_convert_fusion.1), channel_id=1, source_target_pairs={{0,1},{1,0},{2,3},{3,2},{4,5},{5,4},{6,7},{7,6},{8,9},{9,8},{10,11... | collective-permute-start | bytes 1572872 | tf_op jit(solution)/shard_map/ppermute | solution.py:18
  218.9 8.2 %collective-permute-start.37 = (bf16[64,2048]{1,0:T(8,128)(2,1)S(1)}, bf16[64,2048]{1,0:T(8,128)(2,1)S(1)}, u32[]{:S(2)}, u32[]{:S(2)}) collective-permute-start(bf16[64,2048]{1,0:T(8,128)(2,1)S(1)} %slice.262), channel_id=1, source_target_pairs={{0,4},{2,6},{4,0},{6,2},{8,12},{10,14},{12,8},{14,10},{16,20},{18,... | collective-permute-start | bytes 786440 | tf_op jit(solution)/shard_map/ppermute | solution.py:18
  224.6 8.1 %collective-permute-start.17 = (bf16[64,2048]{1,0:T(8,128)(2,1)S(1)}, bf16[64,2048]{1,0:T(8,128)(2,1)S(1)}, u32[]{:S(2)}, u32[]{:S(2)}) collective-permute-start(bf16[64,2048]{1,0:T(8,128)(2,1)S(1)} %slice.263), channel_id=1, source_target_pairs={{0,4},{2,6},{4,0},{6,2},{8,12},{10,14},{12,8},{14,10},{16,20},{18,... | collective-permute-start | bytes 786440 | tf_op jit(solution)/shard_map/ppermute | solution.py:18
  227.2 7.7 %collective-permute-start.38 = (bf16[32,2048]{1,0:T(8,128)(2,1)S(1)}, bf16[32,2048]{1,0:T(8,128)(2,1)S(1)}, u32[]{:S(2)}, u32[]{:S(2)}) collective-permute-start(bf16[32,2048]{1,0:T(8,128)(2,1)S(1)} %slice.264), channel_id=1, source_target_pairs={{0,8},{2,10},{4,12},{6,14},{8,0},{10,2},{12,4},{14,6},{16,24},{18,... | collective-permute-start | bytes 393224 | tf_op jit(solution)/shard_map/ppermute | solution.py:18
  232.8 5.7 %collective-permute-start.18 = (bf16[32,2048]{1,0:T(8,128)(2,1)S(1)}, bf16[32,2048]{1,0:T(8,128)(2,1)S(1)}, u32[]{:S(2)}, u32[]{:S(2)}) collective-permute-start(bf16[32,2048]{1,0:T(8,128)(2,1)S(1)} %slice.265), channel_id=1, source_target_pairs={{0,8},{2,10},{4,12},{6,14},{8,0},{10,2},{12,4},{14,6},{16,24},{18,... | collective-permute-start | bytes 393224 | tf_op jit(solution)/shard_map/ppermute | solution.py:18
  234.9 7.3 %collective-permute-start.39 = (bf16[16,2048]{1,0:T(8,128)(2,1)S(1)}, bf16[16,2048]{1,0:T(8,128)(2,1)S(1)}, u32[]{:S(2)}, u32[]{:S(2)}) collective-permute-start(bf16[16,2048]{1,0:T(8,128)(2,1)S(1)} %slice.266), channel_id=1, source_target_pairs={{0,16},{2,18},{4,20},{6,22},{8,24},{10,26},{12,28},{14,30},{16,0},... | collective-permute-start | bytes 196616 | tf_op jit(solution)/shard_map/ppermute | solution.py:18
  238.6 5.2 %collective-permute-start.19 = (bf16[16,2048]{1,0:T(8,128)(2,1)S(1)}, bf16[16,2048]{1,0:T(8,128)(2,1)S(1)}, u32[]{:S(2)}, u32[]{:S(2)}) collective-permute-start(bf16[16,2048]{1,0:T(8,128)(2,1)S(1)} %slice.267), channel_id=1, source_target_pairs={{0,16},{2,18},{4,20},{6,22},{8,24},{10,26},{12,28},{14,30},{16,0},... | collective-permute-start | bytes 196616 | tf_op jit(solution)/shard_map/ppermute | solution.py:18
  (18 other events, 34.6 us)

commit v2 on v1

--- a/solution.py
+++ b/solution.py
@@ -7,7 +7,6 @@
 from jax.experimental.pallas import tpu as pltpu
 from jax.sharding import PartitionSpec as P
 
-CHUNKS = 2
 BF16 = jnp.bfloat16
 F32 = jnp.float32
 MIB = 1 << 20
@@ -16,33 +15,59 @@
 def swap(array, axis, distance):
     size = lax.axis_size(axis)
     return lax.ppermute(array, axis, [(i, i ^ distance) for i in range(size)])
+
+
+def tie(array, *others):
+    return lax.optimization_barrier((array, *others))[0]
 
 
 def far_distances():
     experts = lax.axis_size("expert")
     distances = []
     distance = experts // 2
-    while distance > 1:
+    while distance > 4:
         distances.append(distance)
         distance //= 2
     return distances
 
 
-def gather_rows(block):
+def join(parts):
+    return parts[0] if len(parts) == 1 else jnp.concatenate(parts, axis=0)
+
+
+def gather_far(block):
+    parts = [block]
     for distance in far_distances():
-        block = jnp.concatenate([block, swap(block, "expert", distance)], axis=0)
-    return block, swap(block, "expert", 1)
-
-
-def scatter_rows(first, second):
-    total, arrived = first, second
+        parts.append(swap(join(parts), "expert", distance))
+    return parts
+
+
+def pick(part, cut):
+    if isinstance(part, list):
+        return part[0] if cut.start else part[1]
+    return part[cut]
+
+
+def add(parts):
+    total = parts[0].astype(F32)
+    for part in parts[1:]:
+        total = total + part.astype(F32)
+    return total
+
+
+def scatter_rows(near, across):
+    rows = near[0].shape[0] // 2
+    totals = []
+    for cut in (slice(rows, 2 * rows), slice(0, rows)):
+        sent = swap(add([pick(part, cut) for part in across]).astype(BF16), "expert", 2)
+        totals.append([pick(part, cut) for part in near] + [sent])
+    sent = swap(add(totals[0]).astype(BF16), "expert", 4)
+    terms = totals[1] + [sent]
     for distance in reversed(far_distances()):
-        half = total.shape[0] // 2
-        leave = (total[half:].astype(F32) + arrived[half:].astype(F32)).astype(BF16)
-        sent = swap(leave, "expert", distance)
-        total = total[:half].astype(F32) + arrived[:half].astype(F32)
-        arrived = sent
-    return total.astype(F32) + arrived.astype(F32)
+        half = terms[0].shape[0] // 2
+        sent = swap(add([part[half:] for part in terms]).astype(BF16), "expert", distance)
+        terms = [part[:half] for part in terms] + [sent]
+    return add(terms)
 
 
 def dot(left, right):
@@ -69,7 +94,7 @@
     return ((step // blocks) ^ place[1]) * blocks + step % blocks
 
 
-def call(kernel, grid, ins, outs, place, scratch=(), mib=32, flops=0):
+def call(kernel, grid, ins, outs, place, scratch=(), mib=44, flops=0, reuse=None):
     total = sum(a.size * a.dtype.itemsize for a, _, _ in ins)
     for shape, kind, _, _ in outs:
         count = 1
@@ -79,7 +104,8 @@
     spec = pltpu.PrefetchScalarGridSpec(
         num_scalar_prefetch=1,
         grid=grid,
-        in_specs=[pl.BlockSpec(block, index) for _, block, index in ins],
+        in_specs=[pl.BlockSpec(block, index) for _, block, index in ins]
+        + ([] if reuse is None else [pl.BlockSpec(memory_space=pl.ANY)]),
         out_specs=[pl.BlockSpec(block, index) for _, _, block, index in outs],
         scratch_shapes=list(scratch),
     )
@@ -89,7 +115,8 @@
         out_shape=[jax.ShapeDtypeStruct(shape, kind) for shape, kind, _, _ in outs],
         compiler_params=params(mib),
         cost_estimate=cost(flops, total),
-    )(place, *[a for a, _, _ in ins])
+        input_output_aliases={} if reuse is None else {1 + len(ins): 0},
+    )(place, *[a for a, _, _ in ins], *([] if reuse is None else [reuse]))
 
 
 def whole2(*_):
@@ -133,6 +160,7 @@
         ],
         [((width, 2 * hidden), BF16, (rows, 2 * hidden), lambda i, p: (i, 0))],
         place,
+        mib=56,
     )[0]
 
 
@@ -170,6 +198,7 @@
         ],
         [((height, quarter), BF16, (rows, quarter), lambda i, p: (i, 0))],
         place,
+        mib=56,
     )[0]
 
 
@@ -411,44 +440,91 @@
     )[0]
 
 
-def ranges_in(place, x, grads, codes, groups, halves):
+def ranges_in(place, x, grads, codes, groups, halves, d, found):
     _, _, width, hidden = codes.shape
     size = width // groups
     per = 2
     rows = per * size
     blocks = width // halves // rows
+    held = groups // halves
     chunks = len(grads)
 
     def kernel(place_ref, *refs):
         x_refs = refs[: 2 * chunks]
         grad_refs = refs[2 * chunks : 3 * chunks]
-        code_ref, out_ref = refs[3 * chunks :]
-        base = moved(pl.program_id(0), blocks, place_ref) * per
-        grad = None
-        for c in range(chunks):
-            left = jnp.concatenate([x_refs[2 * c][...], x_refs[2 * c + 1][...]], axis=0)
-            part = dot_rows(left, grad_refs[c][...])
-            grad = part if grad is None else grad + part
+        code_ref, out_ref = refs[3 * chunks], refs[-1]
+        base = pl.program_id(0) * per
+        left = [
+            jnp.concatenate([x_refs[2 * c][...], x_refs[2 * c + 1][...]], axis=0)
+            for c in range(chunks)
+        ]
         for k in range(2):
+            cols = slice(k * hidden, (k + 1) * hidden)
+            grad = dot_rows(left[0], grad_refs[0][:, cols])
+            for c in range(1, chunks):
+                grad += dot_rows(left[c], grad_refs[c][:, cols])
             for g in range(per):
                 cut = slice(g * size, (g + 1) * size)
-                low, high = ends(
-                    grad[cut, k * hidden : (k + 1) * hidden], code_ref[0, k, cut, :]
-                )
+                low, high = ends(grad[cut], code_ref[0, k, cut, :])
                 out_ref[2 * k, pl.ds(base + g, 1), :] = low
                 out_ref[2 * k + 1, pl.ds(base + g, 1), :] = high
 
     shape = (4, groups, hidden)
     flat = [part for pair in x for part in pair]
-    return call(
-        kernel,
-        (width // rows,),
-        [(part, (part.shape[0], rows), lambda i, p: (0, i)) for part in flat]
+    ins = (
+        [(part, (part.shape[0], rows), lambda i, p: (0, d * blocks + i)) for part in flat]
         + [(grad, grad.shape, whole2) for grad in grads]
-        + [(codes, (1, 2, rows, hidden), lambda i, p: (0, 0, moved(i, blocks, p), 0))],
-        [(shape, F32, shape, whole3)],
-        place,
-        flops=2 * sum(g.size for g in grads) * width,
+        + [
+            (
+                codes,
+                (1, 2, rows, hidden),
+                lambda i, p: (0, 0, (p[1] ^ d) * blocks + i, 0),
+            )
+        ]
+    )
+    return call(
+        kernel,
+        (blocks,),
+        ins,
+        [(shape, F32, (4, held, hidden), lambda i, p: (0, p[1] ^ d, 0))],
+        place,
+        flops=2 * sum(g.size for g in grads) * (width // halves),
+        reuse=found,
+    )[0]
+
+
+def prepare(place, tokens, routes, route_scores, extra):
+    experts = lax.axis_size("expert")
+    halves = lax.axis_size("half")
+    rows, width = tokens.shape
+    quarter = width // halves
+    top_count = routes.shape[1]
+
+    def kernel(place_ref, token_ref, route_ref, score_ref, out_ref):
+        for d in range(halves):
+            start = pl.multiple_of((place_ref[1] ^ d) * quarter, 128)
+            out_ref[:, d * quarter : (d + 1) * quarter] = token_ref[:, pl.ds(start, quarter)]
+        scores = score_ref[...]
+        weights = scores / jnp.sum(scores, axis=1, keepdims=True)
+        names = route_ref[...]
+        lane = lax.broadcasted_iota(jnp.int32, (rows, extra), 1)
+        third = jnp.where(lane < experts, 0, jnp.where(lane < 2 * experts, 1, 2))
+        expert = lane - third * experts
+        table = jnp.zeros((rows, extra), F32)
+        for k in range(top_count):
+            table += jnp.where(expert == names[:, k : k + 1], weights[:, k : k + 1], 0.0)
+        top = table.astype(BF16).astype(F32)
+        middle = (table - top).astype(BF16).astype(F32)
+        bottom = table - top - middle
+        terms = jnp.where(third == 0, top, jnp.where(third == 1, middle, bottom))
+        out_ref[:, width:] = terms.astype(BF16)
+
+    return call(
+        kernel,
+        (1,),
+        [(a, a.shape, whole2) for a in (tokens, routes, route_scores)],
+        [((rows, width + extra), BF16, (rows, width + extra), whole2)],
+        place,
     )[0]
 
 
@@ -457,86 +533,97 @@
 ):
     experts = lax.axis_size("expert")
     halves = lax.axis_size("half")
-    me = lax.axis_index("expert")
-    my_half = lax.axis_index("half")
-    place = jnp.stack([me, my_half]).astype(jnp.int32)
-    rows = tokens.shape[0] // CHUNKS
+    place = jnp.stack([lax.axis_index("expert"), lax.axis_index("half")]).astype(jnp.int32)
     quarter = target.shape[1]
     parts = range(halves)
-    chunks = range(CHUNKS)
-
-    weights = route_scores / jnp.sum(route_scores, axis=1, keepdims=True)
-    names = routes[:, :, None] == jnp.arange(experts, dtype=jnp.int32)[None, None, :]
-    table = jnp.sum(jnp.where(names, weights[:, :, None], 0.0), axis=1)
-    top = lax.reduce_precision(table, 8, 7)
-    middle = lax.reduce_precision(table - top, 8, 7)
-    bottom = table - top - middle
+    chunks = (0, 1)
     extra = -(-3 * experts // 128) * 128
-    terms = jnp.concatenate([top, middle, bottom], axis=1)
-    terms = jnp.pad(terms, ((0, 0), (0, extra - terms.shape[1]))).astype(BF16)
-
-    mine = [
-        lax.dynamic_slice_in_dim(tokens, (my_half ^ d) * quarter, quarter, 1) for d in parts
-    ]
-    mine = jnp.concatenate(mine + [terms], axis=1)
-    x = [gather_rows(mine[c * rows : (c + 1) * rows]) for c in chunks]
+
+    mine = prepare(place, tokens, routes, route_scores, extra)
+    near_own = swap(mine, "expert", 4)
+    across = [swap(mine, "expert", 2)]
+    far = join(gather_far(mine)[1:])
     w_in = dequant_in(place, in_codes, in_low, in_high, halves)
     w_down = dequant_down(place, down_codes, down_low, down_high, halves)
+    far = tie(far, w_in, w_down)
+    near_far = swap(far, "expert", 4)
+    first = jnp.concatenate([mine, far, near_own, near_far], axis=0)
+    across += [swap(part, "expert", 2) for part in (far, near_own, near_far)]
+    x = [(first, swap(first, "expert", 1))]
 
     hidden, slope, act = [], [], []
     for c in chunks:
+        if c == 1:
+            across[3] = tie(across[3], hidden[0][0])
+            second = jnp.concatenate(across, axis=0)
+            x.append((second, swap(second, "expert", 1)))
         own, chunk_slope, chunk_act = forward_in(place, *x[c], w_in)
         hidden.append([own] + [swap(own, "half", d) for d in parts if d])
         slope.append(chunk_slope)
         act.append(chunk_act)
 
-    errors = []
+    sums = []
     for c in chunks:
+        if c == 1:
+            hidden[1][1:] = [tie(part, sums[0][0]) for part in hidden[1][1:]]
         out_own, out_other = forward_down(place, hidden[c], w_down, *x[c], extra)
-        mixed = scatter_rows(out_own, swap(out_other, "expert", 1))
-        wanted = target[c * rows : (c + 1) * rows].astype(F32)
-        errors.append(gather_rows((mixed - wanted).astype(BF16)))
-
+        sums.append([out_own, swap(out_other, "expert", 1)])
+    mixed = scatter_rows(sums[0], sums[1])
+    error = (mixed - target.astype(F32)).astype(BF16)
+
+    kept = join(gather_far(error))
+    near = swap(kept, "expert", 4)
+    across = [swap(kept, "expert", 2), swap(near, "expert", 2)]
+    first = jnp.concatenate([kept, near], axis=0)
+    errors = [(first, swap(first, "expert", 1))]
     grads, grad_own, arrived = [], [], []
     for c in chunks:
+        if c == 1:
+            across[1] = tie(across[1], grads[0])
+            second = jnp.concatenate(across, axis=0)
+            errors.append((second, swap(second, "expert", 1)))
         grad, own, *others = backward_down(place, *errors[c], *x[c], w_down, extra, halves)
         grads.append(grad)
         grad_own.append(own)
         arrived.append([swap(other, "half", d + 1) for d, other in enumerate(others)])
 
-    grad_in, grad_tokens = [], []
+    grad_in, sums = [], [[], []]
+    last = halves - 1
+
+    def spread(c, d, own, other):
+        rows = own.shape[0] // 2
+        cuts = [slice(rows, 2 * rows), slice(0, rows)] if c else [slice(0, 2 * rows)]
+        pieces = [add([own[cut], other[cut]]).astype(BF16) for cut in cuts]
+        if c:
+            pieces = [tie(piece, sums[0][-1]) for piece in pieces] if d == last else pieces
+        sent = [swap(piece, "half", d) for piece in pieces]
+        sums[c].append(sent if c else sent[0])
+        return pieces
+
     for c in chunks:
-        total = None
-        for d in reversed(parts):
-            if d == halves - 1:
-                both, own, other = backward_hidden(
-                    place, grad_own[c], arrived[c], slope[c], act[c], w_in, d, quarter
-                )
-                grad_in.append(both)
+        if c == 1:
+            arrived[1] = [tie(part, *pieces) for part in arrived[1]]
+        both, own, other = backward_hidden(
+            place, grad_own[c], arrived[c], slope[c], act[c], w_in, last, quarter
+        )
+        grad_in.append(both)
+        pieces = spread(c, last, own, swap(other, "expert", 1))
+    for d in range(last - 1, -1, -1):
+        for c in chunks:
+            own, other = row_part(place, grad_in[c], w_in, d, quarter)
+            other = swap(other, "expert", 1)
+            if d:
+                spread(c, d, own, other)
             else:
-                own, other = row_part(place, grad_in[c], w_in, d, quarter)
-            summed = own.astype(F32) + swap(other, "expert", 1).astype(F32)
-            if d:
-                summed = swap(summed.astype(BF16), "half", d)
-            total = summed if total is None else total.astype(F32) + summed.astype(F32)
-        grad_tokens.append(total)
-    grad_tokens = [scatter_sum(total) for total in grad_tokens]
-
+                sums[c] += [own, other]
+    grad_tokens = scatter_rows(*sums)
+
+    grads = [tie(grad, *grad_in) for grad in grads]
     down_grad = ranges_down(place, hidden, grads, down_codes, down_low.shape[1], halves)
-    in_grad = ranges_in(place, x, grad_in, in_codes, in_low.shape[2], halves)
-    return (
-        jnp.concatenate(grad_tokens, axis=0).astype(BF16),
-        in_grad[None],
-        down_grad[None],
-    )
-
-
-def scatter_sum(total):
-    for distance in reversed(far_distances()):
-        half = total.shape[0] // 2
-        arrived = swap(total[half:].astype(BF16), "expert", distance)
-        total = total[:half].astype(F32) + arrived.astype(F32)
-    return total
+    in_grad = None
+    for d in parts:
+        in_grad = ranges_in(place, x, grad_in, in_codes, in_low.shape[2], halves, d, in_grad)
+    return (grad_tokens.astype(BF16), in_grad[None], down_grad[None])
 
 
 def solution(mesh):

time: 246 us -> 240 us (0.976)
  Pallas kernels: 80.1 us -> 111 us
  starting transfers between devices: 53.4 us -> 31.2 us
  local copies, waits for them, and re-layouts: 22.6 us -> 6.67 us
  waiting for transfers between devices: 79.2 us -> 86.9 us
  other arithmetic: 7.8 us -> 2.09 us
    pallas_call x14 -> x16, Pallas kernels: 80.1 us -> 111 us  [call(): pl.pallas_call(kernel, grid_spec=spec, out_shape=[jax.ShapeDtypeStruct(sh...]
    ppermute x40 -> x36, starting transfers between devices: 53.4 us -> 31.2 us  [swap(): return lax.ppermute(array, axis, [(i, i ^ distance) for i in range(size)])]
    unnamed x87 -> x45, local copies, waits for them, and re-layouts: 21.4 us -> 6.63 us
    ppermute x40 -> x36, waiting for transfers between devices: 79.2 us -> 86.9 us  [swap(): return lax.ppermute(array, axis, [(i, i ^ distance) for i in range(size)])]
  transfers between devices with their start and end apart: 40 -> 36, of which waited for: 23 -> 18; matrix products, arithmetic and copies ran while one was open for 2% -> 2% of each run, Pallas kernels for 33% -> 42%
where the time goes in v2:
time: 240 us; the launch traced here: 239 us
  Pallas kernels  111 us (46%)
  waiting for transfers between devices  86.9 us (36%)
  starting transfers between devices  31.2 us (13%)
  local copies, waits for them, and re-layouts  6.67 us (3%)
    pallas_call x16, Pallas kernels, call(): pl.pallas_call(kernel, grid_spec=spec, out_shape=[jax.ShapeDtypeStruct(sh...  111 us
    ppermute x36, waiting for transfers between devices, swap(): return lax.ppermute(array, axis, [(i, i ^ distance) for i in range(size)])  86.9 us
    ppermute x36, starting transfers between devices, swap(): return lax.ppermute(array, axis, [(i, i ^ distance) for i in range(size)])  31.2 us
    unnamed x45, local copies, waits for them, and re-layouts  6.63 us
  transfers between devices with their start and end apart: 36, of which 18 were waited for; matrix products, arithmetic and copies ran while one was open for 2% of the time, Pallas kernels for 42%

profile of v2, /device:TPU:0, one launch (start us, length us, event | category | flops | bytes accessed | tf_op | source)
XLA Modules:
  0.0 239.0 jit_solution(13800441864344313264)
XLA Ops:
  0.6 0.8 copy.14.route_ref
  1.4 0.8 copy.15.score_ref
  2.2 0.9 copy-done.6
  3.2 0.8 shard_map.121
  3.9 4.1 %collective-permute-start = (bf16[32,4224]{1,0:T(8,128)(2,1)S(1)}, bf16[32,4224]{1,0:T(8,128)(2,1)S(1)}, u32[]{:S(2)}, u32[]{:S(2)}) collective-permute-start(bf16[32,4224]{1,0:T(8,128)(2,1)S(1)} %shard_map.121), channel_id=1, source_target_pairs={{0,16},{2,18},{4,20},{6,22},{8,24},{10,26},{12,28},{14,30},{16,0},... | collective-permute-start | bytes 811016 | tf_op jit(solution)/shard_map/ppermute | solution.py:17
  8.0 1.6 collective-permute-start.1
  9.6 1.5 collective-permute-start.6
  11.1 1.6 copy.16.low_ref
  12.7 1.6 copy.17.high_ref
  14.3 7.1 %shard_map.123.refs_2_.w_ref = bf16[1536,2048]{1,0:T(8,128)(2,1)} custom-call(s32[2]{0:T(128)} %copy-done.7, bf16[1,1536,2048]{2,1,0:T(8,128)(2,1)} %refs_6_.5, f32[1,12,2048]{2,1,0:T(8,128)} %copy.16.low_ref, f32[1,12,2048]{2,1,0:T(8,128)} %copy.17.high_ref), custom_call_target="tpu_custom_call" | custom-call | bytes 12779520 | tf_op jit(solution)/shard_map/pallas_call | solution.py:112
  21.4 13.2 %shard_map.122.w_ref.refs_3_ = bf16[4096,1536]{1,0:T(8,128)(2,1)} custom-call(s32[2]{0:T(128)} %copy-done.7, bf16[1,2,4096,768]{3,2,1,0:T(8,128)(2,1)} %refs_6_.4, f32[1,2,32,768]{3,2,1,0:T(8,128)} %low_ref.2, f32[1,2,32,768]{3,2,1,0:T(8,128)} %high_ref.2), custom_call_target="tpu_custom_call" | custom-call | bytes 25559040 | tf_op jit(solution)/shard_map/pallas_call | solution.py:112
  34.6 0.6 collective-permute-start.7
  35.1 0.4 collective-permute-start.2
  35.6 1.5 collective-permute-start.8
  37.1 5.1 %collective-permute-done.2 = bf16[32,4224]{1,0:T(8,128)(2,1)S(1)} collective-permute-done((bf16[32,4224]{1,0:T(8,128)(2,1)S(1)}, bf16[32,4224]{1,0:T(8,128)(2,1)S(1)}, u32[]{:S(2)}, u32[]{:S(2)}) %collective-permute-start.2) | collective-permute-done | bytes 270368 | tf_op jit(solution)/shard_map/ppermute | solution.py:17
  42.4 1.6 collective-permute-start.9
  44.0 5.8 %collective-permute-done.8 = bf16[32,4224]{1,0:T(8,128)(2,1)S(1)} collective-permute-done((bf16[32,4224]{1,0:T(8,128)(2,1)S(1)}, bf16[32,4224]{1,0:T(8,128)(2,1)S(1)}, u32[]{:S(2)}, u32[]{:S(2)}) %collective-permute-start.8) | collective-permute-done | bytes 270368 | tf_op jit(solution)/shard_map/ppermute | solution.py:17
  49.9 11.2 %shard_map.124 = (bf16[256,768]{1,0:T(8,128)(2,1)S(1)}, f32[256,768]{1,0:T(8,128)S(1)}, f32[256,768]{1,0:T(8,128)S(1)}) custom-call(s32[2]{0:T(128)S(1)} %copy-done.8, bf16[128,4224]{1,0:T(8,128)(2,1)S(1)} %pad_maximum_fusion.own_ref.refs_3_.refs_0_, bf16[128,4224]{1,0:T(8,128)(2,1)S(1)} %collective-permute-done.3.other_ref.refs_4_.refs_1_, ...), custom_call_target="tpu_custom_call" | custom-call | flops 3221225472 | bytes 16711680 | tf_op jit(solution)/shard_map/pallas_call | solution.py:112
  61.2 1.6 collective-permute-start.4
  62.7 1.1 collective-permute-done.10.other_ref.refs_4_.refs_3_
  63.9 10.8 %shard_map.126 = (bf16[256,768]{1,0:T(8,128)(2,1)S(1)}, f32[256,768]{1,0:T(8,128)S(1)}, f32[256,768]{1,0:T(8,128)S(1)}) custom-call(s32[2]{0:T(128)S(1)} %copy-done.8, bf16[128,4224]{1,0:T(8,128)(2,1)S(1)} %constant_dynamic-update-slice_fusion.own_ref.refs_3_.refs_2_, bf16[128,4224]{1,0:T(8,128)(2,1)S(1)} %collective-permute-done.10.other_ref.refs_4_.refs_3_, ...), custom_call_target="tpu_custom_call" | custom-call | flops 3221225472 | bytes 16711680 | tf_op jit(solution)/shard_map/pallas_call | solution.py:112
  74.7 1.6 collective-permute-start.11
  76.3 3.5 %shard_map.125 = (bf16[128,2048]{1,0:T(8,128)(2,1)S(1)}, bf16[128,2048]{1,0:T(8,128)(2,1)S(1)}) custom-call(s32[2]{0:T(128)S(1)} %copy-done.8, bf16[256,768]{1,0:T(8,128)(2,1)S(1)} %get-tuple-element.39.refs_0_, bf16[256,768]{1,0:T(8,128)(2,1)S(1)} %collective-permute-done.4.refs_1_, bf16[1536,2048]{1,0:T(8,128)(2,1)S(1)} %bitcast.5, ...), custom_call_target="tpu_custom_call" | custom-call | flops 1610612736 | bytes 10289152 | tf_op jit(solution)/shard_map/pallas_call | solution.py:112
  79.8 6.1 %collective-permute-done.11.refs_1_.refs_3_ = bf16[256,768]{1,0:T(8,128)(2,1)S(1)} collective-permute-done((bf16[256,768]{1,0:T(8,128)(2,1)S(1)}, bf16[256,768]{1,0:T(8,128)(2,1)S(1)}, u32[]{:S(2)}, u32[]{:S(2)}) %collective-permute-start.11) | collective-permute-done | bytes 393248 | tf_op jit(solution)/shard_map/ppermute | solution.py:17
  85.9 3.5 %shard_map.127 = (bf16[128,2048]{1,0:T(8,128)(2,1)S(1)}, bf16[128,2048]{1,0:T(8,128)(2,1)S(1)}) custom-call(s32[2]{0:T(128)S(1)} %copy-done.8, bf16[256,768]{1,0:T(8,128)(2,1)S(1)} %get-tuple-element.43.refs_0_.refs_2_, bf16[256,768]{1,0:T(8,128)(2,1)S(1)} %collective-permute-done.11.refs_1_.refs_3_, bf16[1536,2048]{1,0:T(8,128)(2,1)S(1)} %bitcast.5, ...), custom_call_target="tpu_custom_call" | custom-call | flops 1610612736 | bytes 10289152 | tf_op jit(solution)/shard_map/pallas_call | solution.py:112
  89.5 0.5 collective-permute-start.5
  90.0 1.4 collective-permute-done.12
  91.6 2.0 collective-permute-start.13
  93.7 7.1 %collective-permute-done.14 = bf16[64,2048]{1,0:T(8,128)(2,1)S(1)} collective-permute-done((bf16[64,2048]{1,0:T(8,128)(2,1)S(1)}, bf16[64,2048]{1,0:T(8,128)(2,1)S(1)}, u32[]{:S(2)}, u32[]{:S(2)}) %collective-permute-start.14) | collective-permute-done | bytes 262176 | tf_op jit(solution)/shard_map/ppermute | solution.py:17
  100.9 0.5 collective-permute-start.15
  101.4 4.2 %collective-permute-done.13 = bf16[64,2048]{1,0:T(8,128)(2,1)S(1)} collective-permute-done((bf16[64,2048]{1,0:T(8,128)(2,1)S(1)}, bf16[64,2048]{1,0:T(8,128)(2,1)S(1)}, u32[]{:S(2)}, u32[]{:S(2)}) %collective-permute-start.13) | collective-permute-done | bytes 262176 | tf_op jit(solution)/shard_map/ppermute | solution.py:17
  105.6 2.1 collective-permute-done.15
  107.7 0.4 collective-permute-start.16
  108.1 9.4 %collective-permute-done.16 = bf16[32,2048]{1,0:T(8,128)(2,1)S(1)} collective-permute-done((bf16[32,2048]{1,0:T(8,128)(2,1)S(1)}, bf16[32,2048]{1,0:T(8,128)(2,1)S(1)}, u32[]{:S(2)}, u32[]{:S(2)}) %collective-permute-start.16) | collective-permute-done | bytes 131104 | tf_op jit(solution)/shard_map/ppermute | solution.py:17
  117.8 6.0 %collective-permute-done.17 = bf16[32,2048]{1,0:T(8,128)(2,1)S(1)} collective-permute-done((bf16[32,2048]{1,0:T(8,128)(2,1)S(1)}, bf16[32,2048]{1,0:T(8,128)(2,1)S(1)}, u32[]{:S(2)}, u32[]{:S(2)}) %collective-permute-start.17) | collective-permute-done | bytes 131104 | tf_op jit(solution)/shard_map/ppermute | solution.py:17
  123.8 6.4 %collective-permute-done.18 = bf16[64,2048]{1,0:T(8,128)(2,1)S(1)} collective-permute-done((bf16[64,2048]{1,0:T(8,128)(2,1)S(1)}, bf16[64,2048]{1,0:T(8,128)(2,1)S(1)}, u32[]{:S(2)}, u32[]{:S(2)}) %collective-permute-start.18) | collective-permute-done | bytes 262176 | tf_op jit(solution)/shard_map/ppermute | solution.py:17
  130.4 2.0 collective-permute-start.25
  132.4 6.1 %shard_map.128 = (bf16[256,2048]{1,0:T(8,128)(2,1)S(1)}, f32[256,768]{1,0:T(8,128)S(1)}, bf16[256,768]{1,0:T(8,128)(2,1)S(1)}) custom-call(s32[2]{0:T(128)S(1)} %copy-done.8, bf16[128,2048]{1,0:T(8,128)(2,1)S(1)} %pad_maximum_fusion.1.err_own_ref, bf16[128,2048]{1,0:T(8,128)(2,1)S(1)} %collective-permute-done.19.err_other_ref, ...), custom_call_target="tpu_custom_call" | custom-call | flops 1610612736 | bytes 11730944 | tf_op jit(solution)/shard_map/pallas_call | solution.py:112
  138.5 1.6 collective-permute-start.20
  140.1 4.5 %collective-permute-done.25 = bf16[64,2048]{1,0:T(8,128)(2,1)S(1)} collective-permute-done((bf16[64,2048]{1,0:T(8,128)(2,1)S(1)}, bf16[64,2048]{1,0:T(8,128)(2,1)S(1)}, u32[]{:S(2)}, u32[]{:S(2)}) %collective-permute-start.25) | collective-permute-done | bytes 262176 | tf_op jit(solution)/shard_map/ppermute | solution.py:17
  144.7 4.8 %collective-permute-done.20.refs_0_ = bf16[256,768]{1,0:T(8,128)(2,1)S(1)} collective-permute-done((bf16[256,768]{1,0:T(8,128)(2,1)S(1)}, bf16[256,768]{1,0:T(8,128)(2,1)S(1)}, u32[]{:S(2)}, u32[]{:S(2)}) %collective-permute-start.20) | collective-permute-done | bytes 393248 | tf_op jit(solution)/shard_map/ppermute | solution.py:17
  149.5 5.6 %shard_map.129 = (bf16[256,1536]{1,0:T(8,128)(2,1)S(1)}, bf16[128,2048]{1,0:T(8,128)(2,1)S(1)}, bf16[128,2048]{1,0:T(8,128)(2,1)S(1)}) custom-call(s32[2]{0:T(128)S(1)} %copy-done.8, f32[256,768]{1,0:T(8,128)S(1)} %get-tuple-element.47.grad_own_ref, bf16[256,768]{1,0:T(8,128)(2,1)S(1)} %collective-permute-done.20.refs_0_, f32[256,768]{1,0:T(8,128)S(1)} %copy-done.1, ...), custom_call_target="tpu_custom_call" | custom-call | flops 1610612736 | bytes 17170432 | tf_op jit(solution)/shard_map/pallas_call | solution.py:112
  155.2 6.1 %shard_map.131 = (bf16[256,2048]{1,0:T(8,128)(2,1)S(1)}, f32[256,768]{1,0:T(8,128)S(1)}, bf16[256,768]{1,0:T(8,128)(2,1)S(1)}) custom-call(s32[2]{0:T(128)S(1)} %copy-done.8, bf16[128,2048]{1,0:T(8,128)(2,1)S(1)} %constant_dynamic-update-slice_fusion.4.err_own_ref, bf16[128,2048]{1,0:T(8,128)(2,1)S(1)} %collective-permute-done.26.err_other_ref, ...), custom_call_target="tpu_custom_call" | custom-call | flops 1610612736 | bytes 11730944 | tf_op jit(solution)/shard_map/pallas_call | solution.py:112
  161.3 1.6 collective-permute-start.27
  163.0 9.8 %collective-permute-done.27.refs_0_ = bf16[256,768]{1,0:T(8,128)(2,1)S(1)} collective-permute-done((bf16[256,768]{1,0:T(8,128)(2,1)S(1)}, bf16[256,768]{1,0:T(8,128)(2,1)S(1)}, u32[]{:S(2)}, u32[]{:S(2)}) %collective-permute-start.27) | collective-permute-done | bytes 393248 | tf_op jit(solution)/shard_map/ppermute | solution.py:17
  172.9 5.6 %shard_map.132 = (bf16[256,1536]{1,0:T(8,128)(2,1)S(1)}, bf16[128,2048]{1,0:T(8,128)(2,1)S(1)}, bf16[128,2048]{1,0:T(8,128)(2,1)S(1)}) custom-call(s32[2]{0:T(128)S(1)} %copy-done.8, f32[256,768]{1,0:T(8,128)S(1)} %get-tuple-element.58.grad_own_ref, bf16[256,768]{1,0:T(8,128)(2,1)S(1)} %collective-permute-done.27.refs_0_, ...), custom_call_target="tpu_custom_call" | custom-call | flops 1610612736 | bytes 17170432 | tf_op jit(solution)/shard_map/pallas_call | solution.py:112
  178.5 1.6 collective-permute-start.22
  180.1 5.4 %shard_map.133 = (bf16[128,2048]{1,0:T(8,128)(2,1)S(1)}, bf16[128,2048]{1,0:T(8,128)(2,1)S(1)}) custom-call(s32[2]{0:T(128)S(1)} %copy-done.8, bf16[256,1536]{1,0:T(8,128)(2,1)S(1)} %get-tuple-element.66.grad_ref.refs_5_, bf16[4096,1536]{1,0:T(8,128)(2,1)} %shard_map.122.w_ref.refs_3_), custom_call_target="tpu_custom_call" | custom-call | flops 1610612736 | bytes 14417920 | tf_op jit(solution)/shard_map/pallas_call | solution.py:112
  185.5 0.2 collective-permute-start.30
  185.9 7.0 %collective-permute-done.22 = bf16[128,2048]{1,0:T(8,128)(2,1)S(1)} collective-permute-done((bf16[128,2048]{1,0:T(8,128)(2,1)S(1)}, bf16[128,2048]{1,0:T(8,128)(2,1)S(1)}, u32[]{:S(2)}, u32[]{:S(2)}) %collective-permute-start.22) | collective-permute-done | bytes 524320 | tf_op jit(solution)/shard_map/ppermute | solution.py:17
  192.9 1.5 collective-permute-start.32
  194.4 0.5 collective-permute-start.29
  194.9 5.4 %shard_map.130 = (bf16[128,2048]{1,0:T(8,128)(2,1)S(1)}, bf16[128,2048]{1,0:T(8,128)(2,1)S(1)}) custom-call(s32[2]{0:T(128)S(1)} %copy-done.8, bf16[256,1536]{1,0:T(8,128)(2,1)S(1)} %get-tuple-element.53.grad_ref.refs_4_, bf16[4096,1536]{1,0:T(8,128)(2,1)} %shard_map.122.w_ref.refs_3_), custom_call_target="tpu_custom_call" | custom-call | flops 1610612736 | bytes 14417920 | tf_op jit(solution)/shard_map/pallas_call | solution.py:112
  200.4 1.7 collective-permute-done.32
  202.1 4.3 %collective-permute-done.29 = bf16[64,2048]{1,0:T(8,128)(2,1)S(1)} collective-permute-done((bf16[64,2048]{1,0:T(8,128)(2,1)S(1)}, bf16[64,2048]{1,0:T(8,128)(2,1)S(1)}, u32[]{:S(2)}, u32[]{:S(2)}) %collective-permute-start.29) | collective-permute-done | bytes 262176 | tf_op jit(solution)/shard_map/ppermute | solution.py:17
  206.4 0.2 add_convert_fusion.4
  206.6 0.3 collective-permute-start.33
  206.9 10.0 %shard_map.134.refs_7_ = f32[4,32,768]{2,1,0:T(8,128)} custom-call(s32[2]{0:T(128)S(1)} %copy-done.8, bf16[128,4224]{1,0:T(8,128)(2,1)S(1)} %pad_maximum_fusion.own_ref.refs_3_.refs_0_, bf16[128,4224]{1,0:T(8,128)(2,1)S(1)} %collective-permute-done.3.other_ref.refs_4_.refs_1_, ...), custom_call_target="tpu_custom_call" | custom-call | flops 3221225472 | bytes 18874368 | tf_op jit(solution)/shard_map/pallas_call | solution.py:112
  217.0 1.8 collective-permute-start.31
  219.0 10.4 %shard_map.135 = f32[4,32,768]{2,1,0:T(8,128)} custom-call(s32[2]{0:T(128)S(1)} %copy-done.8, bf16[128,4224]{1,0:T(8,128)(2,1)S(1)} %pad_maximum_fusion.own_ref.refs_3_.refs_0_, bf16[128,4224]{1,0:T(8,128)(2,1)S(1)} %collective-permute-done.3.other_ref.refs_4_.refs_1_, ...), custom_call_target="tpu_custom_call", output_to_operand_aliasing={{}: (8, {})} | custom-call | flops 3221225472 | bytes 18874368 | tf_op jit(solution)/shard_map/pallas_call | solution.py:112
  229.5 1.3 collective-permute-start.35
  230.9 6.6 %shard_map.136 = f32[2,12,2048]{2,1,0:T(8,128)S(1)} custom-call(s32[2]{0:T(128)S(1)} %copy-done.8, bf16[256,768]{1,0:T(8,128)(2,1)S(1)} %get-tuple-element.39.refs_0_, bf16[256,768]{1,0:T(8,128)(2,1)S(1)} %collective-permute-done.4.refs_1_, bf16[256,768]{1,0:T(8,128)(2,1)S(1)} %copy-done.3, bf16[256,768]{1,0:T(8,128)(2,1)S(1)} %copy-done.5, ...), custom_call_target="tpu_custom_call" | custom-call | flops 3221225472 | bytes 10158080 | tf_op jit(solution)/shard_map/pallas_call | solution.py:112
  237.4 0.8 copy.18
  238.2 0.8 add_convert_fusion.9
  (87 shorter events, 2.3 us)
Async XLA Ops:
  2.2 0.9 copy-start.6
  3.2 11.1 %copy-start.7 = (s32[2]{0:T(128)}, s32[2]{0:T(128)S(1)}, u32[]{:S(2)}) copy-start(s32[2]{0:T(128)S(1)} %pad_add_fusion.place_ref) | copy-start | bytes 28
  3.9 30.6 %collective-permute-start = (bf16[32,4224]{1,0:T(8,128)(2,1)S(1)}, bf16[32,4224]{1,0:T(8,128)(2,1)S(1)}, u32[]{:S(2)}, u32[]{:S(2)}) collective-permute-start(bf16[32,4224]{1,0:T(8,128)(2,1)S(1)} %shard_map.121), channel_id=1, source_target_pairs={{0,16},{2,18},{4,20},{6,22},{8,24},{10,26},{12,28},{14,30},{16,0},... | collective-permute-start | bytes 811016 | tf_op jit(solution)/shard_map/ppermute | solution.py:17
  8.0 27.5 %collective-permute-start.1 = (bf16[32,4224]{1,0:T(8,128)(2,1)S(1)}, bf16[32,4224]{1,0:T(8,128)(2,1)S(1)}, u32[]{:S(2)}, u32[]{:S(2)}) collective-permute-start(bf16[32,4224]{1,0:T(8,128)(2,1)S(1)} %shard_map.121), channel_id=1, source_target_pairs={{0,8},{2,10},{4,12},{6,14},{8,0},{10,2},{12,4},{14,6},{16,24},{18,... | collective-permute-start | bytes 811016 | tf_op jit(solution)/shard_map/ppermute | solution.py:17
  9.6 27.4 %collective-permute-start.6 = (bf16[32,4224]{1,0:T(8,128)(2,1)S(1)}, bf16[32,4224]{1,0:T(8,128)(2,1)S(1)}, u32[]{:S(2)}, u32[]{:S(2)}) collective-permute-start(bf16[32,4224]{1,0:T(8,128)(2,1)S(1)} %shard_map.121), channel_id=1, source_target_pairs={{0,4},{2,6},{4,0},{6,2},{8,12},{10,14},{12,8},{14,10},{16,20},{18,... | collective-permute-start | bytes 811016 | tf_op jit(solution)/shard_map/ppermute | solution.py:17
  34.6 9.4 %collective-permute-start.7 = (bf16[32,4224]{1,0:T(8,128)(2,1)S(1)}, bf16[32,4224]{1,0:T(8,128)(2,1)S(1)}, u32[]{:S(2)}, u32[]{:S(2)}) collective-permute-start(bf16[32,4224]{1,0:T(8,128)(2,1)S(1)} %collective-permute-done), channel_id=1, source_target_pairs={{0,4},{2,6},{4,0},{6,2},{8,12},{10,14},{12,8},{14,10},{16,20},{18,... | collective-permute-start | bytes 811016 | tf_op jit(solution)/shard_map/ppermute | solution.py:17
  35.1 7.1 %collective-permute-start.2 = (bf16[32,4224]{1,0:T(8,128)(2,1)S(1)}, bf16[32,4224]{1,0:T(8,128)(2,1)S(1)}, u32[]{:S(2)}, u32[]{:S(2)}) collective-permute-start(bf16[32,4224]{1,0:T(8,128)(2,1)S(1)} %collective-permute-done), channel_id=1, source_target_pairs={{0,8},{2,10},{4,12},{6,14},{8,0},{10,2},{12,4},{14,6},{16,24},{18,... | collective-permute-start | bytes 811016 | tf_op jit(solution)/shard_map/ppermute | solution.py:17
  35.6 14.2 %collective-permute-start.8 = (bf16[32,4224]{1,0:T(8,128)(2,1)S(1)}, bf16[32,4224]{1,0:T(8,128)(2,1)S(1)}, u32[]{:S(2)}, u32[]{:S(2)}) collective-permute-start(bf16[32,4224]{1,0:T(8,128)(2,1)S(1)} %collective-permute-done.1), channel_id=1, source_target_pairs={{0,4},{2,6},{4,0},{6,2},{8,12},{10,14},{12,8},{14,10},{16,20},{18,... | collective-permute-start | bytes 811016 | tf_op jit(solution)/shard_map/ppermute | solution.py:17
  37.1 12.7 %copy-start.8 = (s32[2]{0:T(128)S(1)}, s32[2]{0:T(128)}, u32[]{:S(2)}) copy-start(s32[2]{0:T(128)} %copy-done.7) | copy-start | bytes 28
  42.3 7.5 %collective-permute-start.3 = (bf16[128,4224]{1,0:T(8,128)(2,1)S(1)}, bf16[128,4224]{1,0:T(8,128)(2,1)S(1)}, u32[]{:S(2)}, u32[]{:S(2)}) collective-permute-start(bf16[128,4224]{1,0:T(8,128)(2,1)S(1)} %pad_maximum_fusion.own_ref.refs_3_.refs_0_), channel_id=1, source_target_pairs={{0,2},{2,0},{4,6},{6,4},{8,10},{10,8},{12,14},{14,12},{16,18},{18,... | collective-permute-start | bytes 3244040 | tf_op jit(solution)/shard_map/ppermute | solution.py:17
  42.4 18.6 %collective-permute-start.9 = (bf16[32,4224]{1,0:T(8,128)(2,1)S(1)}, bf16[32,4224]{1,0:T(8,128)(2,1)S(1)}, u32[]{:S(2)}, u32[]{:S(2)}) collective-permute-start(bf16[32,4224]{1,0:T(8,128)(2,1)S(1)} %collective-permute-done.2), channel_id=1, source_target_pairs={{0,4},{2,6},{4,0},{6,2},{8,12},{10,14},{12,8},{14,10},{16,20},{18,... | collective-permute-start | bytes 811016 | tf_op jit(solution)/shard_map/ppermute | solution.py:17
  49.8 26.5 %slice-start = ((s8[6291456]{0:T(1024)(128)(4,1)}), s8[4194304]{0:T(1024)(128)(4,1)S(1)}, s32[]{:S(2)}) async-start(s8[6291456]{0:T(1024)(128)(4,1)} %bitcast.4), calls=%async_computation | async-start | bytes 8388608
  61.0 13.7 %copy-start = (f32[256,768]{1,0:T(8,128)}, f32[256,768]{1,0:T(8,128)S(1)}, u32[]{:S(2)}) copy-start(f32[256,768]{1,0:T(8,128)S(1)} %get-tuple-element.49.refs_1_) | copy-start | bytes 2359300
  61.0 15.3 %slice-start.1 = ((s8[6291456]{0:T(1024)(128)(4,1)}), s8[2097152]{0:T(1024)(128)(4,1)S(1)}, s32[]{:S(2)}) async-start(s8[6291456]{0:T(1024)(128)(4,1)} %bitcast.4), calls=%async_computation.1 | async-start | bytes 4194304
  61.1 2.8 %collective-permute-start.10 = (bf16[128,4224]{1,0:T(8,128)(2,1)S(1)}, bf16[128,4224]{1,0:T(8,128)(2,1)S(1)}, u32[]{:S(2)}, u32[]{:S(2)}) collective-permute-start(bf16[128,4224]{1,0:T(8,128)(2,1)S(1)} %constant_dynamic-update-slice_fusion.own_ref.refs_3_.refs_2_), channel_id=1, source_target_pairs={{0,2},{2,0},{4,6},{6,4},{8,10},{10,8},{12,14},{14,12},{16,18},{18,... | collective-permute-start | bytes 3244040 | tf_op jit(solution)/shard_map/ppermute | solution.py:17
  61.2 15.1 %collective-permute-start.4 = (bf16[256,768]{1,0:T(8,128)(2,1)S(1)}, bf16[256,768]{1,0:T(8,128)(2,1)S(1)}, u32[]{:S(2)}, u32[]{:S(2)}) collective-permute-start(bf16[256,768]{1,0:T(8,128)(2,1)S(1)} %get-tuple-element.39.refs_0_), channel_id=1, source_target_pairs={{0,1},{1,0},{2,3},{3,2},{4,5},{5,4},{6,7},{7,6},{8,9},{9,8},{10,11... | collective-permute-start | bytes 1179656 | tf_op jit(solution)/shard_map/ppermute | solution.py:17
  74.7 11.2 %copy-start.2 = (bf16[256,768]{1,0:T(8,128)(2,1)}, bf16[256,768]{1,0:T(8,128)(2,1)S(1)}, u32[]{:S(2)}) copy-start(bf16[256,768]{1,0:T(8,128)(2,1)S(1)} %get-tuple-element.43.refs_0_.refs_2_) | copy-start | bytes 1179652
  74.7 11.2 %collective-permute-start.11 = (bf16[256,768]{1,0:T(8,128)(2,1)S(1)}, bf16[256,768]{1,0:T(8,128)(2,1)S(1)}, u32[]{:S(2)}, u32[]{:S(2)}) collective-permute-start(bf16[256,768]{1,0:T(8,128)(2,1)S(1)} %get-tuple-element.43.refs_0_.refs_2_), channel_id=1, source_target_pairs={{0,1},{1,0},{2,3},{3,2},{4,5},{5,4},{6,7},{7,6},{8,9},{9,8},{10,11... | collective-permute-start | bytes 1179656 | tf_op jit(solution)/shard_map/ppermute | solution.py:17
  85.9 3.5 %copy-start.4 = (bf16[256,768]{1,0:T(8,128)(2,1)}, bf16[256,768]{1,0:T(8,128)(2,1)S(1)}, u32[]{:S(2)}) copy-start(bf16[256,768]{1,0:T(8,128)(2,1)S(1)} %collective-permute-done.11.refs_1_.refs_3_) | copy-start | bytes 1179652
  89.4 2.0 collective-permute-start.12
  89.5 4.1 %collective-permute-start.5 = (bf16[128,2048]{1,0:T(8,128)(2,1)S(1)}, bf16[128,2048]{1,0:T(8,128)(2,1)S(1)}, u32[]{:S(2)}, u32[]{:S(2)}) collective-permute-start(bf16[128,2048]{1,0:T(8,128)(2,1)S(1)} %get-tuple-element.41), channel_id=1, source_target_pairs={{0,2},{2,0},{4,6},{6,4},{8,10},{10,8},{12,14},{14,12},{16,18},{18,... | collective-permute-start | bytes 1572872 | tf_op jit(solution)/shard_map/ppermute | solution.py:17
  91.6 26.0 %copy-start.13 = (bf16[32,2048]{1,0:T(8,128)(2,1)S(1)}, bf16[32,2048]{1,0:T(8,128)(2,1)}, u32[]{:S(2)}) copy-start(bf16[32,2048]{1,0:T(8,128)(2,1)} %param.11) | copy-start | bytes 393220
  91.6 9.2 %collective-permute-start.14 = (bf16[64,2048]{1,0:T(8,128)(2,1)S(1)}, bf16[64,2048]{1,0:T(8,128)(2,1)S(1)}, u32[]{:S(2)}, u32[]{:S(2)}) collective-permute-start(bf16[64,2048]{1,0:T(8,128)(2,1)S(1)} %get-tuple-element.81), channel_id=1, source_target_pairs={{0,4},{2,6},{4,0},{6,2},{8,12},{10,14},{12,8},{14,10},{16,20},{18,... | collective-permute-start | bytes 786440 | tf_op jit(solution)/shard_map/ppermute | solution.py:17
  91.6 14.0 %collective-permute-start.13 = (bf16[64,2048]{1,0:T(8,128)(2,1)S(1)}, bf16[64,2048]{1,0:T(8,128)(2,1)S(1)}, u32[]{:S(2)}, u32[]{:S(2)}) collective-permute-start(bf16[64,2048]{1,0:T(8,128)(2,1)S(1)} %get-tuple-element.80), channel_id=1, source_target_pairs={{0,4},{2,6},{4,0},{6,2},{8,12},{10,14},{12,8},{14,10},{16,20},{18,... | collective-permute-start | bytes 786440 | tf_op jit(solution)/shard_map/ppermute | solution.py:17
  100.9 6.8 %collective-permute-start.15 = (bf16[64,2048]{1,0:T(8,128)(2,1)S(1)}, bf16[64,2048]{1,0:T(8,128)(2,1)S(1)}, u32[]{:S(2)}, u32[]{:S(2)}) collective-permute-start(bf16[64,2048]{1,0:T(8,128)(2,1)S(1)} %add_convert_fusion.6), channel_id=1, source_target_pairs={{0,8},{2,10},{4,12},{6,14},{8,0},{10,2},{12,4},{14,6},{16,24},{18,... | collective-permute-start | bytes 786440 | tf_op jit(solution)/shard_map/ppermute | solution.py:17
  107.7 9.8 %collective-permute-start.16 = (bf16[32,2048]{1,0:T(8,128)(2,1)S(1)}, bf16[32,2048]{1,0:T(8,128)(2,1)S(1)}, u32[]{:S(2)}, u32[]{:S(2)}) collective-permute-start(bf16[32,2048]{1,0:T(8,128)(2,1)S(1)} %add_convert_fusion.11), channel_id=1, source_target_pairs={{0,16},{2,18},{4,20},{6,22},{8,24},{10,26},{12,28},{14,30},{16,0},... | collective-permute-start | bytes 393224 | tf_op jit(solution)/shard_map/ppermute | solution.py:17
  117.7 6.0 %collective-permute-start.17 = (bf16[32,2048]{1,0:T(8,128)(2,1)S(1)}, bf16[32,2048]{1,0:T(8,128)(2,1)S(1)}, u32[]{:S(2)}, u32[]{:S(2)}) collective-permute-start(bf16[32,2048]{1,0:T(8,128)(2,1)S(1)} %subtract_convert_fusion), channel_id=1, source_target_pairs={{0,16},{2,18},{4,20},{6,22},{8,24},{10,26},{12,28},{14,30},{16,0},... | collective-permute-start | bytes 393224 | tf_op jit(solution)/shard_map/ppermute | solution.py:17
  123.7 6.4 %collective-permute-start.18 = (bf16[64,2048]{1,0:T(8,128)(2,1)S(1)}, bf16[64,2048]{1,0:T(8,128)(2,1)S(1)}, u32[]{:S(2)}, u32[]{:S(2)}) collective-permute-start(bf16[64,2048]{1,0:T(8,128)(2,1)S(1)} %pad_maximum_fusion.2), channel_id=1, source_target_pairs={{0,8},{2,10},{4,12},{6,14},{8,0},{10,2},{12,4},{14,6},{16,24},{18,... | collective-permute-start | bytes 786440 | tf_op jit(solution)/shard_map/ppermute | solution.py:17
  130.2 2.2 collective-permute-start.19
  130.3 9.8 %collective-permute-start.24 = (bf16[64,2048]{1,0:T(8,128)(2,1)S(1)}, bf16[64,2048]{1,0:T(8,128)(2,1)S(1)}, u32[]{:S(2)}, u32[]{:S(2)}) collective-permute-start(bf16[64,2048]{1,0:T(8,128)(2,1)S(1)} %pad_maximum_fusion.2), channel_id=1, source_target_pairs={{0,4},{2,6},{4,0},{6,2},{8,12},{10,14},{12,8},{14,10},{16,20},{18,... | collective-permute-start | bytes 786440 | tf_op jit(solution)/shard_map/ppermute | solution.py:17
  130.4 14.3 %collective-permute-start.25 = (bf16[64,2048]{1,0:T(8,128)(2,1)S(1)}, bf16[64,2048]{1,0:T(8,128)(2,1)S(1)}, u32[]{:S(2)}, u32[]{:S(2)}) collective-permute-start(bf16[64,2048]{1,0:T(8,128)(2,1)S(1)} %collective-permute-done.18), channel_id=1, source_target_pairs={{0,4},{2,6},{4,0},{6,2},{8,12},{10,14},{12,8},{14,10},{16,20},{18,... | collective-permute-start | bytes 786440 | tf_op jit(solution)/shard_map/ppermute | solution.py:17
  138.5 16.6 %copy-start.9 = (bf16[256,2048]{1,0:T(8,128)(2,1)}, bf16[256,2048]{1,0:T(8,128)(2,1)S(1)}, u32[]{:S(2)}) copy-start(bf16[256,2048]{1,0:T(8,128)(2,1)S(1)} %get-tuple-element.70.refs_4_) | copy-start | bytes 3145732
  138.5 11.0 %copy-start.1 = (f32[256,768]{1,0:T(8,128)S(1)}, f32[256,768]{1,0:T(8,128)}, u32[]{:S(2)}) copy-start(f32[256,768]{1,0:T(8,128)} %copy-done) | copy-start | bytes 2359300
  138.5 11.0 %collective-permute-start.20 = (bf16[256,768]{1,0:T(8,128)(2,1)S(1)}, bf16[256,768]{1,0:T(8,128)(2,1)S(1)}, u32[]{:S(2)}, u32[]{:S(2)}) collective-permute-start(bf16[256,768]{1,0:T(8,128)(2,1)S(1)} %get-tuple-element.48), channel_id=1, source_target_pairs={{0,1},{1,0},{2,3},{3,2},{4,5},{5,4},{6,7},{7,6},{8,9},{9,8},{10,11... | collective-permute-start | bytes 1179656 | tf_op jit(solution)/shard_map/ppermute | solution.py:17
  144.7 10.5 %collective-permute-start.26 = (bf16[128,2048]{1,0:T(8,128)(2,1)S(1)}, bf16[128,2048]{1,0:T(8,128)(2,1)S(1)}, u32[]{:S(2)}, u32[]{:S(2)}) collective-permute-start(bf16[128,2048]{1,0:T(8,128)(2,1)S(1)} %constant_dynamic-update-slice_fusion.4.err_own_ref), channel_id=1, source_target_pairs={{0,2},{2,0},{4,6},{6,4},{8,10},{10,8},{12,14},{14,12},{16,18},{18,... | collective-permute-start | bytes 1572872 | tf_op jit(solution)/shard_map/ppermute | solution.py:17
  155.1 7.8 %collective-permute-start.21 = (bf16[128,2048]{1,0:T(8,128)(2,1)S(1)}, bf16[128,2048]{1,0:T(8,128)(2,1)S(1)}, u32[]{:S(2)}, u32[]{:S(2)}) collective-permute-start(bf16[128,2048]{1,0:T(8,128)(2,1)S(1)} %get-tuple-element.52), channel_id=1, source_target_pairs={{0,2},{2,0},{4,6},{6,4},{8,10},{10,8},{12,14},{14,12},{16,18},{18,... | collective-permute-start | bytes 1572872 | tf_op jit(solution)/shard_map/ppermute | solution.py:17
  161.3 17.2 %copy-start.11 = (bf16[256,2048]{1,0:T(8,128)(2,1)}, bf16[256,2048]{1,0:T(8,128)(2,1)S(1)}, u32[]{:S(2)}) copy-start(bf16[256,2048]{1,0:T(8,128)(2,1)S(1)} %get-tuple-element.72.refs_5_) | copy-start | bytes 3145732
  161.3 11.6 %collective-permute-start.27 = (bf16[256,768]{1,0:T(8,128)(2,1)S(1)}, bf16[256,768]{1,0:T(8,128)(2,1)S(1)}, u32[]{:S(2)}, u32[]{:S(2)}) collective-permute-start(bf16[256,768]{1,0:T(8,128)(2,1)S(1)} %get-tuple-element.59), channel_id=1, source_target_pairs={{0,1},{1,0},{2,3},{3,2},{4,5},{5,4},{6,7},{7,6},{8,9},{9,8},{10,11... | collective-permute-start | bytes 1179656 | tf_op jit(solution)/shard_map/ppermute | solution.py:17
  178.5 7.3 %collective-permute-start.28 = (bf16[128,2048]{1,0:T(8,128)(2,1)S(1)}, bf16[128,2048]{1,0:T(8,128)(2,1)S(1)}, u32[]{:S(2)}, u32[]{:S(2)}) collective-permute-start(bf16[128,2048]{1,0:T(8,128)(2,1)S(1)} %get-tuple-element.64), channel_id=1, source_target_pairs={{0,2},{2,0},{4,6},{6,4},{8,10},{10,8},{12,14},{14,12},{16,18},{18,... | collective-permute-start | bytes 1572872 | tf_op jit(solution)/shard_map/ppermute | solution.py:17
  178.5 14.3 %collective-permute-start.22 = (bf16[128,2048]{1,0:T(8,128)(2,1)S(1)}, bf16[128,2048]{1,0:T(8,128)(2,1)S(1)}, u32[]{:S(2)}, u32[]{:S(2)}) collective-permute-start(bf16[128,2048]{1,0:T(8,128)(2,1)S(1)} %add_convert_fusion), channel_id=1, source_target_pairs={{0,1},{1,0},{2,3},{3,2},{4,5},{5,4},{6,7},{7,6},{8,9},{9,8},{10,11... | collective-permute-start | bytes 1572872 | tf_op jit(solution)/shard_map/ppermute | solution.py:17
  185.5 14.9 %collective-permute-start.30 = (bf16[128,2048]{1,0:T(8,128)(2,1)S(1)}, bf16[128,2048]{1,0:T(8,128)(2,1)S(1)}, u32[]{:S(2)}, u32[]{:S(2)}) collective-permute-start(bf16[128,2048]{1,0:T(8,128)(2,1)S(1)} %get-tuple-element.68), channel_id=1, source_target_pairs={{0,2},{2,0},{4,6},{6,4},{8,10},{10,8},{12,14},{14,12},{16,18},{18,... | collective-permute-start | bytes 1572872 | tf_op jit(solution)/shard_map/ppermute | solution.py:17
  192.9 9.2 %collective-permute-start.32 = (bf16[64,2048]{1,0:T(8,128)(2,1)S(1)}, bf16[64,2048]{1,0:T(8,128)(2,1)S(1)}, u32[]{:S(2)}, u32[]{:S(2)}) collective-permute-start(bf16[64,2048]{1,0:T(8,128)(2,1)S(1)} %get-tuple-element.69), channel_id=1, source_target_pairs={{0,1},{1,0},{2,3},{3,2},{4,5},{5,4},{6,7},{7,6},{8,9},{9,8},{10,11... | collective-permute-start | bytes 786440 | tf_op jit(solution)/shard_map/ppermute | solution.py:17
  194.4 12.0 %collective-permute-start.29 = (bf16[64,2048]{1,0:T(8,128)(2,1)S(1)}, bf16[64,2048]{1,0:T(8,128)(2,1)S(1)}, u32[]{:S(2)}, u32[]{:S(2)}) collective-permute-start(bf16[64,2048]{1,0:T(8,128)(2,1)S(1)} %get-tuple-element.65), channel_id=1, source_target_pairs={{0,1},{1,0},{2,3},{3,2},{4,5},{5,4},{6,7},{7,6},{8,9},{9,8},{10,11... | collective-permute-start | bytes 786440 | tf_op jit(solution)/shard_map/ppermute | solution.py:17
  200.3 18.5 %collective-permute-start.23 = (bf16[128,2048]{1,0:T(8,128)(2,1)S(1)}, bf16[128,2048]{1,0:T(8,128)(2,1)S(1)}, u32[]{:S(2)}, u32[]{:S(2)}) collective-permute-start(bf16[128,2048]{1,0:T(8,128)(2,1)S(1)} %get-tuple-element.55), channel_id=1, source_target_pairs={{0,2},{2,0},{4,6},{6,4},{8,10},{10,8},{12,14},{14,12},{16,18},{18,... | collective-permute-start | bytes 1572872 | tf_op jit(solution)/shard_map/ppermute | solution.py:17
  206.6 12.1 %collective-permute-start.33 = (bf16[64,2048]{1,0:T(8,128)(2,1)S(1)}, bf16[64,2048]{1,0:T(8,128)(2,1)S(1)}, u32[]{:S(2)}, u32[]{:S(2)}) collective-permute-start(bf16[64,2048]{1,0:T(8,128)(2,1)S(1)} %get-tuple-element.77), channel_id=1, source_target_pairs={{0,4},{2,6},{4,0},{6,2},{8,12},{10,14},{12,8},{14,10},{16,20},{18,... | collective-permute-start | bytes 786440 | tf_op jit(solution)/shard_map/ppermute | solution.py:17
  217.0 12.4 %collective-permute-start.31 = (bf16[64,2048]{1,0:T(8,128)(2,1)S(1)}, bf16[64,2048]{1,0:T(8,128)(2,1)S(1)}, u32[]{:S(2)}, u32[]{:S(2)}) collective-permute-start(bf16[64,2048]{1,0:T(8,128)(2,1)S(1)} %get-tuple-element.76), channel_id=1, source_target_pairs={{0,4},{2,6},{4,0},{6,2},{8,12},{10,14},{12,8},{14,10},{16,20},{18,... | collective-permute-start | bytes 786440 | tf_op jit(solution)/shard_map/ppermute | solution.py:17
  218.8 12.1 %slice-start.2 = ((s8[6291456]{0:T(1024)(128)(4,1)}), s8[4194304]{0:T(1024)(128)(4,1)S(1)}, s32[]{:S(2)}) async-start(s8[6291456]{0:T(1024)(128)(4,1)} %bitcast.6), calls=%async_computation.2 | async-start | bytes 8388608
  218.9 11.9 %slice-start.3 = ((s8[6291456]{0:T(1024)(128)(4,1)}), s8[2097152]{0:T(1024)(128)(4,1)S(1)}, s32[]{:S(2)}) async-start(s8[6291456]{0:T(1024)(128)(4,1)} %bitcast.6), calls=%async_computation.3 | async-start | bytes 4194304
  218.9 11.9 %copy-start.3 = (bf16[256,768]{1,0:T(8,128)(2,1)S(1)}, bf16[256,768]{1,0:T(8,128)(2,1)}, u32[]{:S(2)}) copy-start(bf16[256,768]{1,0:T(8,128)(2,1)} %copy-done.2) | copy-start | bytes 1179652
  218.9 11.9 %copy-start.5 = (bf16[256,768]{1,0:T(8,128)(2,1)S(1)}, bf16[256,768]{1,0:T(8,128)(2,1)}, u32[]{:S(2)}) copy-start(bf16[256,768]{1,0:T(8,128)(2,1)} %copy-done.4) | copy-start | bytes 1179652
  218.9 11.9 %copy-start.10 = (bf16[256,2048]{1,0:T(8,128)(2,1)S(1)}, bf16[256,2048]{1,0:T(8,128)(2,1)}, u32[]{:S(2)}) copy-start(bf16[256,2048]{1,0:T(8,128)(2,1)} %copy-done.9) | copy-start | bytes 3145732
  218.9 11.9 %copy-start.12 = (bf16[256,2048]{1,0:T(8,128)(2,1)S(1)}, bf16[256,2048]{1,0:T(8,128)(2,1)}, u32[]{:S(2)}) copy-start(bf16[256,2048]{1,0:T(8,128)(2,1)} %copy-done.11) | copy-start | bytes 3145732
  219.0 10.4 %collective-permute-start.34 = (bf16[64,2048]{1,0:T(8,128)(2,1)S(1)}, bf16[64,2048]{1,0:T(8,128)(2,1)S(1)}, u32[]{:S(2)}, u32[]{:S(2)}) collective-permute-start(bf16[64,2048]{1,0:T(8,128)(2,1)S(1)} %add_convert_fusion.1), channel_id=1, source_target_pairs={{0,8},{2,10},{4,12},{6,14},{8,0},{10,2},{12,4},{14,6},{16,24},{18,... | collective-permute-start | bytes 786440 | tf_op jit(solution)/shard_map/ppermute | solution.py:17
  229.5 8.8 %collective-permute-start.35 = (bf16[32,2048]{1,0:T(8,128)(2,1)S(1)}, bf16[32,2048]{1,0:T(8,128)(2,1)S(1)}, u32[]{:S(2)}, u32[]{:S(2)}) collective-permute-start(bf16[32,2048]{1,0:T(8,128)(2,1)S(1)} %add_convert_fusion.10), channel_id=1, source_target_pairs={{0,16},{2,18},{4,20},{6,22},{8,24},{10,26},{12,28},{14,30},{16,0},... | collective-permute-start | bytes 393224 | tf_op jit(solution)/shard_map/ppermute | solution.py:17

commit v3 on v2

v3 whole, which is shorter than its diff:
```python
import functools

import jax
import jax.numpy as jnp
from jax import lax
from jax.experimental import pallas as pl
from jax.experimental.pallas import tpu as pltpu
from jax.sharding import PartitionSpec as P

BF16 = jnp.bfloat16
F32 = jnp.float32
MIB = 1 << 20


def swap(array, axis, distance):
    size = lax.axis_size(axis)
    return lax.ppermute(array, axis, [(i, i ^ distance) for i in range(size)])


def tie(array, *others):
    return lax.optimization_barrier((array, *others))[0]


def far_distances():
    experts = lax.axis_size("expert")
    distances = []
    distance = experts // 2
    while distance > 4:
        distances.append(distance)
        distance //= 2
    return distances


def join(parts):
    return parts[0] if len(parts) == 1 else jnp.concatenate(parts, axis=0)


def gather_far(block):
    parts = [block]
    for distance in far_distances():
        parts.append(swap(join(parts), "expert", distance))
    return parts


def pick(part, cut):
    if isinstance(part, list):
        return part[0] if cut.start else part[1]
    return part[cut]


def add(parts):
    total = parts[0].astype(F32)
    for part in parts[1:]:
        total = total + part.astype(F32)
    return total


def scatter_rows(near, across):
    rows = near[0].shape[0] // 2
    totals = []
    for cut in (slice(rows, 2 * rows), slice(0, rows)):
        sent = swap(add([pick(part, cut) for part in across]).astype(BF16), "expert", 2)
        totals.append([pick(part, cut) for part in near] + [sent])
    sent = swap(add(totals[0]).astype(BF16), "expert", 4)
    terms = totals[1] + [sent]
    for distance in reversed(far_distances()):
        half = terms[0].shape[0] // 2
        sent = swap(add([part[half:] for part in terms]).astype(BF16), "expert", distance)
        terms = [part[:half] for part in terms] + [sent]
    return add(terms)


def dot(left, right):
    return jnp.dot(left, right, preferred_element_type=F32)


def dot_cols(left, right):
    return lax.dot_general(left, right, (((1,), (1,)), ((), ())), preferred_element_type=F32)


def dot_rows(left, right):
    return lax.dot_general(left, right, (((0,), (0,)), ((), ())), preferred_element_type=F32)


def cost(flops, bytes_accessed):
    return pl.CostEstimate(flops=int(flops), bytes_accessed=int(bytes_accessed), transcendentals=0)


def moved(step, blocks, place):
    return ((step // blocks) ^ place[1]) * blocks + step % blocks


def call(kernel, grid, ins, outs, place, scratch=(), mib=16, flops=0, reuse=None):
    total = sum(a.size * a.dtype.itemsize for a, _, _ in ins)
    for shape, kind, _, _ in outs:
        count = 1
        for extent in shape:
            count *= extent
        total += count * jnp.dtype(kind).itemsize

    def spec(block, index):
        if isinstance(block, tuple):
            return pl.BlockSpec(block, index)
        return pl.BlockSpec(memory_space=block)

    in_specs = [spec(block, index) for _, block, index in ins]
    arrays = [a for a, _, _ in ins]
    if reuse is not None:
        in_specs.append(pl.BlockSpec(memory_space=pl.ANY))
        arrays.append(reuse)
    return pl.pallas_call(
        kernel,
        grid_spec=pltpu.PrefetchScalarGridSpec(
            num_scalar_prefetch=1,
            grid=grid,
            in_specs=in_specs,
            out_specs=[spec(block, index) for _, _, block, index in outs],
            scratch_shapes=list(scratch),
        ),
        out_shape=[jax.ShapeDtypeStruct(shape, kind) for shape, kind, _, _ in outs],
        compiler_params=pltpu.CompilerParams(vmem_limit_bytes=mib * MIB),
        cost_estimate=cost(flops, total),
        input_output_aliases={} if reuse is None else {1 + len(ins): 0},
    )(place, *arrays)


def resident(kernel, ins, outs, place, mib=16, flops=0, scratch=()):
    return call(
        kernel,
        (),
        [(a, pltpu.VMEM, None) for a in ins],
        [(shape, kind, pltpu.VMEM, None) for shape, kind in outs],
        place,
        mib=mib,
        flops=flops,
        scratch=scratch,
    )


def step_of(extent):
    return 256 if extent % 256 == 0 else 128


def tiles(extent, body):
    size = step_of(extent)

    def step(i, carry):
        body(pl.multiple_of(i * size, size))
        return carry

    lax.fori_loop(0, extent // size, step, 0)


def whole2(*_):
    return (0, 0)


def whole3(*_):
    return (0, 0, 0)


def whole4(*_):
    return (0, 0, 0, 0)


def dequant(place, codes, low, high, halves):
    count, height, cols = codes.shape
    groups = low.shape[1]
    size = height // groups
    held = groups // halves

    def kernel(place_ref, code_ref, low_ref, high_ref, out_ref):
        def block(i, carry):
            base = moved(i, held, place_ref)
            source = pl.multiple_of(base * size, size)
            to = pl.multiple_of(i * size, size)
            for k in range(count):
                bottom = low_ref[k, pl.ds(base, 1), :]
                scale = (high_ref[k, pl.ds(base, 1), :] - bottom) * (1.0 / 255.0)
                vals = code_ref[k, pl.ds(source, size), :].astype(F32)
                out_ref[pl.ds(to, size), k * cols : (k + 1) * cols] = (
                    bottom + scale * vals
                ).astype(BF16)
            return carry

        lax.fori_loop(0, groups, block, 0)

    return resident(
        kernel, [codes, low, high], [((height, count * cols), BF16)], place
    )[0]


def hidden_rows(total_groups, size, halves):
    per = total_groups // halves
    while per > 3:
        per = next(f for f in range(2, per + 1) if per % f == 0) and per // next(
            f for f in range(2, per + 1) if per % f == 0
        )
    return per, per * size


def forward_in(place, x_own, x_other, w_in):
    rows = x_own.shape[0]
    width, both = w_in.shape
    hidden = both // 2
    size = step_of(hidden)

    def kernel(place_ref, own_ref, other_ref, w_ref, hidden_ref, slope_ref, act_ref):
        x = jnp.concatenate([own_ref[:, :width], other_ref[:, :width]], axis=0)

        def body(start):
            gate = dot(x, w_ref[:, pl.ds(start, size)])
            up = dot(x, w_ref[:, pl.ds(pl.multiple_of(hidden + start, size), size)])
            sig = 1.0 / (1.0 + jnp.exp(-gate))
            act = gate * sig
            hidden_ref[:, pl.ds(start, size)] = (act * up).astype(BF16)
            slope_ref[:, pl.ds(start, size)] = up * sig * (1.0 + gate * (1.0 - sig))
            act_ref[:, pl.ds(start, size)] = act

        tiles(hidden, body)

    shape = (2 * rows, hidden)
    return resident(
        kernel,
        [x_own, x_other, w_in],
        [(shape, BF16), (shape, F32), (shape, F32)],
        place,
        flops=4 * rows * width * both,
    )


def route_weight(extra, place_ref, experts):
    lane = lax.broadcasted_iota(jnp.int32, extra.shape, 1)
    me = place_ref[0]
    named = (lane == me) | (lane == me + experts) | (lane == me + 2 * experts)
    return jnp.sum(jnp.where(named, extra.astype(F32), 0.0), axis=1, keepdims=True)


def forward_down(place, hidden, w_down, x_own, x_other, extra):
    experts = lax.axis_size("expert")
    rows = x_own.shape[0]
    height, quarter = w_down.shape
    width = x_own.shape[1] - extra
    size = step_of(quarter)

    def kernel(place_ref, *refs):
        *hidden_refs, w_ref, own_ref, other_ref, out_own_ref, out_other_ref = refs
        left = jnp.concatenate([ref[...] for ref in hidden_refs], axis=1)
        own = route_weight(own_ref[:, width:], place_ref, experts)
        other = route_weight(other_ref[:, width:], place_ref, experts)

        def body(start):
            total = dot(left, w_ref[:, pl.ds(start, size)])
            out_own_ref[:, pl.ds(start, size)] = (own * total[:rows]).astype(BF16)
            out_other_ref[:, pl.ds(start, size)] = (other * total[rows:]).astype(BF16)

        tiles(quarter, body)

    return resident(
        kernel,
        [*hidden, w_down, x_own, x_other],
        [((rows, quarter), BF16)] * 2,
        place,
        flops=4 * rows * height * quarter,
    )


def backward_down(place, err_own, err_other, x_own, x_other, w_down, extra, halves):
    experts = lax.axis_size("expert")
    rows, quarter = err_own.shape
    height = w_down.shape[0]
    own = height // halves
    width = x_own.shape[1] - extra
    size = step_of(own)

    def kernel(place_ref, err_own_ref, err_other_ref, own_ref, other_ref, w_ref, grad_ref, *outs):
        weight = route_weight(own_ref[:, width:], place_ref, experts)
        grad_ref[:rows, :] = (weight * err_own_ref[...].astype(F32)).astype(BF16)
        weight = route_weight(other_ref[:, width:], place_ref, experts)
        grad_ref[rows:, :] = (weight * err_other_ref[...].astype(F32)).astype(BF16)
        for d in range(halves):

            def body(start):
                at = pl.multiple_of(d * own + start, size)
                part = dot_cols(grad_ref[...], w_ref[pl.ds(at, size), :])
                outs[d][:, pl.ds(start, size)] = part.astype(outs[d].dtype)

            tiles(own, body)

    shape = (2 * rows, own)
    return resident(
        kernel,
        [err_own, err_other, x_own, x_other, w_down],
        [((2 * rows, quarter), BF16), (shape, F32)] + [(shape, BF16)] * (halves - 1),
        place,
        flops=4 * rows * height * quarter,
    )


def backward_hidden(place, grad_own, arrived, slope, act, w_in, d, quarter):
    both_rows, hidden = slope.shape
    rows = both_rows // 2
    size = step_of(quarter)
    count = len(arrived)

    def kernel(place_ref, grad_own_ref, *refs):
        arrived_refs = refs[:count]
        slope_ref, act_ref, w_ref, grad_ref, out_own_ref, out_other_ref = refs[count:]
        grad_hidden = grad_own_ref[...]
        for ref in arrived_refs:
            grad_hidden += ref[...].astype(F32)
        grad_ref[:, :hidden] = (grad_hidden * slope_ref[...]).astype(BF16)
        grad_ref[:, hidden:] = (grad_hidden * act_ref[...]).astype(BF16)

        def body(start):
            at = pl.multiple_of(d * quarter + start, size)
            part = dot_cols(grad_ref[...], w_ref[pl.ds(at, size), :]).astype(BF16)
            out_own_ref[:, pl.ds(start, size)] = part[:rows]
            out_other_ref[:, pl.ds(start, size)] = part[rows:]

        tiles(quarter, body)

    return resident(
        kernel,
        [grad_own, *arrived, slope, act, w_in],
        [((both_rows, 2 * hidden), BF16)] + [((rows, quarter), BF16)] * 2,
        place,
        flops=4 * both_rows * hidden * quarter,
    )


def row_part(place, grad_in, w_in, d, quarter):
    both_rows, both = grad_in.shape
    rows = both_rows // 2
    size = step_of(quarter)

    def kernel(place_ref, grad_ref, w_ref, out_own_ref, out_other_ref):
        def body(start):
            at = pl.multiple_of(d * quarter + start, size)
            part = dot_cols(grad_ref[...], w_ref[pl.ds(at, size), :]).astype(BF16)
            out_own_ref[:, pl.ds(start, size)] = part[:rows]
            out_other_ref[:, pl.ds(start, size)] = part[rows:]

        tiles(quarter, body)

    return resident(
        kernel,
        [grad_in, w_in],
        [((rows, quarter), BF16)] * 2,
        place,
        flops=2 * both_rows * both * quarter,
    )


def ends(grad, codes):
    upper = jnp.sum(grad * codes.astype(F32), axis=0, keepdims=True) * (1.0 / 255.0)
    return jnp.sum(grad, axis=0, keepdims=True) - upper, upper


def range_tile(left, right, size, step, codes, store):
    turned = left.T
    for start in range(0, right.shape[1], step):
        cols = slice(start, start + step)
        grad = dot(turned, right[:, cols])
        for g in range(turned.shape[0] // size):
            cut = slice(g * size, (g + 1) * size)
            low, high = ends(grad[cut], codes(cut, cols))
            store(g, cols, low, high)


def ranges_down(place, hidden, grads, codes, groups, halves):
    _, height, quarter = codes.shape
    size = height // groups
    per, rows = hidden_rows(groups, size, halves)
    blocks = height // halves // rows
    flat = [part for parts in hidden for part in parts]
    chunks = len(grads)
    tokens = grads[0].shape[0]

    def kernel(place_ref, *refs):
        hidden_refs = refs[: len(flat)]
        grad_refs = refs[len(flat) : len(flat) + chunks]
        code_ref, out_ref, right_ref = refs[len(flat) + chunks :]
        step = pl.program_id(0)
        base = moved(step, blocks, place_ref) * per

        @pl.when(step == 0)
        def _():
            for c in range(chunks):
                right_ref[c * tokens : (c + 1) * tokens, :] = grad_refs[c][...]

        def store(g, cols, low, high):
            out_ref[0, pl.ds(base + g, 1), cols] = low
            out_ref[1, pl.ds(base + g, 1), cols] = high

        for d in range(halves):

            @pl.when(step // blocks == d)
            def _():
                left = [hidden_refs[c * halves + d][...] for c in range(chunks)]
                range_tile(
                    jnp.concatenate(left, axis=0),
                    right_ref,
                    size,
                    step_of(quarter),
                    lambda cut, cols: code_ref[0, cut, cols],
                    store,
                )

    shape = (2, groups, quarter)
    return call(
        kernel,
        (height // rows,),
        [(part, (part.shape[0], rows), lambda i, p: (0, i % blocks)) for part in flat]
        + [(grad, pltpu.VMEM, None) for grad in grads]
        + [(codes, (1, rows, quarter), lambda i, p: (0, moved(i, blocks, p), 0))],
        [(shape, F32, shape, whole3)],
        place,
        scratch=[pltpu.VMEM((chunks * tokens, quarter), BF16)],
        mib=20,
        flops=2 * sum(g.shape[0] for g in grads) * height * quarter,
    )[0]


def ranges_in(place, x, grads, codes, groups, halves, d, found):
    _, _, width, hidden = codes.shape
    size = width // groups
    held = groups // halves
    per = next(p for p in (4, 2, 1) if held % p == 0)
    rows = per * size
    blocks = held // per
    chunks = len(grads)
    tokens, both = grads[0].shape

    def kernel(place_ref, *refs):
        x_refs = refs[: 2 * chunks]
        grad_refs = refs[2 * chunks : 3 * chunks]
        code_ref, out_ref, right_ref = refs[3 * chunks], refs[-2], refs[-1]
        step = pl.program_id(0)
        base = step * per

        @pl.when(step == 0)
        def _():
            for c in range(chunks):
                right_ref[c * tokens : (c + 1) * tokens, :] = grad_refs[c][...]

        def split(cols):
            k = cols.start // hidden
            return k, slice(cols.start - k * hidden, cols.stop - k * hidden)

        def codes_at(cut, cols):
            k, cols = split(cols)
            return code_ref[0, k, cut, cols]

        def store(g, cols, low, high):
            k, cols = split(cols)
            out_ref[2 * k, pl.ds(base + g, 1), cols] = low
            out_ref[2 * k + 1, pl.ds(base + g, 1), cols] = high

        left = jnp.concatenate([ref[...] for ref in x_refs], axis=0)
        wide = 256 if hidden % 256 == 0 else hidden
        range_tile(left, right_ref, size, wide, codes_at, store)

    shape = (4, groups, hidden)
    flat = [part for pair in x for part in pair]
    return call(
        kernel,
        (blocks,),
        [(part, (part.shape[0], rows), lambda i, p: (0, d * blocks + i)) for part in flat]
        + [(grad, pltpu.VMEM, None) for grad in grads]
        + [
            (
                codes,
                (1, 2, rows, hidden),
                lambda i, p: (0, 0, (p[1] ^ d) * blocks + i, 0),
            )
        ],
        [(shape, F32, (4, held, hidden), lambda i, p: (0, p[1] ^ d, 0))],
        place,
        scratch=[pltpu.VMEM((chunks * tokens, both), BF16)],
        mib=20,
        flops=2 * sum(g.size for g in grads) * (width // halves),
        reuse=found,
    )[0]


def prepare(place, tokens, routes, route_scores, extra):
    experts = lax.axis_size("expert")
    halves = lax.axis_size("half")
    rows, width = tokens.shape
    quarter = width // halves
    top_count = routes.shape[1]

    def kernel(place_ref, token_ref, route_ref, score_ref, out_ref):
        for d in range(halves):
            start = pl.multiple_of((place_ref[1] ^ d) * quarter, 128)
            out_ref[:, d * quarter : (d + 1) * quarter] = token_ref[:, pl.ds(start, quarter)]
        scores = score_ref[...]
        weights = scores / jnp.sum(scores, axis=1, keepdims=True)
        names = route_ref[...]
        lane = lax.broadcasted_iota(jnp.int32, (rows, extra), 1)
        third = jnp.where(lane < experts, 0, jnp.where(lane < 2 * experts, 1, 2))
        expert = lane - third * experts
        table = jnp.zeros((rows, extra), F32)
        for k in range(top_count):
            table += jnp.where(expert == names[:, k : k + 1], weights[:, k : k + 1], 0.0)
        top = table.astype(BF16).astype(F32)
        middle = (table - top).astype(BF16).astype(F32)
        bottom = table - top - middle
        terms = jnp.where(third == 0, top, jnp.where(third == 1, middle, bottom))
        out_ref[:, width:] = terms.astype(BF16)

    return call(
        kernel,
        (1,),
        [(a, a.shape, whole2) for a in (tokens, routes, route_scores)],
        [((rows, width + extra), BF16, (rows, width + extra), whole2)],
        place,
    )[0]


def local(
    tokens, target, routes, route_scores, in_codes, in_low, in_high, down_codes, down_low, down_high
):
    experts = lax.axis_size("expert")
    halves = lax.axis_size("half")
    place = jnp.stack([lax.axis_index("expert"), lax.axis_index("half")]).astype(jnp.int32)
    quarter = target.shape[1]
    parts = range(halves)
    chunks = (0, 1)
    extra = -(-3 * experts // 128) * 128

    mine = prepare(place, tokens, routes, route_scores, extra)
    near_own = swap(mine, "expert", 4)
    across = [swap(mine, "expert", 2)]
    far = join(gather_far(mine)[1:])
    w_in = dequant(place, in_codes[0], in_low[0], in_high[0], halves)
    far = tie(far, w_in)
    near_far = swap(far, "expert", 4)
    w_down = dequant(place, down_codes, tie(down_low, w_in), down_high, halves)
    near_far = tie(near_far, w_down)
    first = jnp.concatenate([mine, far, near_own, near_far], axis=0)
    across += [swap(part, "expert", 2) for part in (far, near_own, near_far)]
    x = [(first, swap(first, "expert", 1))]

    hidden, slope, act = [], [], []
    for c in chunks:
        if c == 1:
            across[3] = tie(across[3], hidden[0][0])
            second = jnp.concatenate(across, axis=0)
            x.append((second, swap(second, "expert", 1)))
        own, chunk_slope, chunk_act = forward_in(place, *x[c], w_in)
        hidden.append([own] + [swap(own, "half", d) for d in parts if d])
        slope.append(chunk_slope)
        act.append(chunk_act)

    sums = []
    for c in chunks:
        if c == 1:
            hidden[1][1:] = [tie(part, sums[0][0]) for part in hidden[1][1:]]
        out_own, out_other = forward_down(place, hidden[c], w_down, *x[c], extra)
        sums.append([out_own, swap(out_other, "expert", 1)])
    mixed = scatter_rows(sums[0], sums[1])
    error = (mixed - target.astype(F32)).astype(BF16)

    kept = join(gather_far(error))
    near = swap(kept, "expert", 4)
    across = [swap(kept, "expert", 2), swap(near, "expert", 2)]
    first = jnp.concatenate([kept, near], axis=0)
    errors = [(first, swap(first, "expert", 1))]
    grads, grad_own, arrived = [], [], []
    for c in chunks:
        if c == 1:
            across[1] = tie(across[1], grads[0])
            second = jnp.concatenate(across, axis=0)
            errors.append((second, swap(second, "expert", 1)))
        grad, own, *others = backward_down(place, *errors[c], *x[c], w_down, extra, halves)
        grads.append(grad)
        grad_own.append(own)
        arrived.append([swap(other, "half", d + 1) for d, other in enumerate(others)])

    grad_in, sums = [], [[], []]
    last = halves - 1

    def spread(c, d, own, other):
        rows = own.shape[0] // 2
        cuts = [slice(rows, 2 * rows), slice(0, rows)] if c else [slice(0, 2 * rows)]
        pieces = [add([own[cut], other[cut]]).astype(BF16) for cut in cuts]
        if c:
            pieces = [tie(piece, sums[0][-1]) for piece in pieces] if d == last else pieces
        sent = [swap(piece, "half", d) for piece in pieces]
        sums[c].append(sent if c else sent[0])
        return pieces

    arrived[0] = [tie(part, grads[1]) for part in arrived[0]]
    for c in chunks:
        if c == 1:
            arrived[1] = [tie(part, *pieces) for part in arrived[1]]
        both, own, other = backward_hidden(
            place, grad_own[c], arrived[c], slope[c], act[c], w_in, last, quarter
        )
        grad_in.append(both)
        pieces = spread(c, last, own, swap(other, "expert", 1))
    for d in range(last - 1, -1, -1):
        for c in chunks:
            own, other = row_part(place, grad_in[c], w_in, d, quarter)
            other = swap(other, "expert", 1)
            if d:
                spread(c, d, own, other)
            else:
                sums[c] += [own, other]
    grad_tokens = scatter_rows(*sums)

    grads = [tie(grad, *grad_in) for grad in grads]
    down_grad = ranges_down(place, hidden, grads, down_codes, down_low.shape[1], halves)
    in_grad = None
    for d in parts:
        in_grad = ranges_in(place, x, grad_in, in_codes, in_low.shape[2], halves, d, in_grad)
    return (grad_tokens.astype(BF16), in_grad[None], down_grad[None])


def solution(mesh):
    placed = (
        P("expert", None),
        P("expert", "half"),
        P("expert", None),
        P("expert", None),
        P("expert", None, None, "half"),
        P("expert", None, None, "half"),
        P("expert", None, None, "half"),
        P("expert", None, "half"),
        P("expert", None, "half"),
        P("expert", None, "half"),
    )
    return jax.shard_map(
        local,
        mesh=mesh,
        in_specs=placed,
        out_specs=(
            P("expert", "half"),
            P("expert", None, None, "half"),
            P("expert", None, None, "half"),
        ),
        check_vma=False,
    )
```

time: 240 us -> 208 us (0.87)
  Pallas kernels: 111 us -> 66.1 us
  waiting for transfers between devices: 86.9 us -> 95.8 us
  local copies, waits for them, and re-layouts: 6.67 us -> 11.9 us
    pallas_call x16, Pallas kernels: 111 us -> 66.1 us  [call(): pl.pallas_call(kernel, grid_spec=pltpu.PrefetchScalarGridSpec(num_scalar_...]
    ppermute x36, waiting for transfers between devices: 86.9 us -> 95.8 us  [swap(): return lax.ppermute(array, axis, [(i, i ^ distance) for i in range(size)])]
    unnamed x45 -> x40, local copies, waits for them, and re-layouts: 6.63 us -> 11.8 us
  transfers between devices with their start and end apart: 36 -> 36, of which waited for: 18 -> 22; matrix products, arithmetic and copies ran while one was open for 2% -> 1% of each run, Pallas kernels for 42% -> 26%
where the time goes in v3:
time: 208 us
  waiting for transfers between devices  95.8 us (46%)
  Pallas kernels  66.1 us (32%)
  starting transfers between devices  31.2 us (15%)
  local copies, waits for them, and re-layouts  11.9 us (6%)
  other arithmetic  2.09 us (1%)
    ppermute x36, waiting for transfers between devices, swap(): return lax.ppermute(array, axis, [(i, i ^ distance) for i in range(size)])  95.8 us
    pallas_call x16, Pallas kernels, call(): pl.pallas_call(kernel, grid_spec=pltpu.PrefetchScalarGridSpec(num_scalar_...  66.1 us
    ppermute x36, starting transfers between devices, swap(): return lax.ppermute(array, axis, [(i, i ^ distance) for i in range(size)])  31.2 us
    unnamed x40, local copies, waits for them, and re-layouts  11.8 us
  transfers between devices with their start and end apart: 36, of which 22 were waited for; matrix products, arithmetic and copies ran while one was open for 1% of the time, Pallas kernels for 26%

profile of v3, /device:TPU:0, one launch (start us, length us, event | category | flops | bytes accessed | tf_op | source)
XLA Modules:
  0.0 208.1 jit_solution(12123139172414083213)
XLA Ops:
  0.6 0.8 copy.14.route_ref
  1.4 0.8 copy.15.score_ref
  2.2 0.9 copy-done.6
  3.2 0.8 shard_map.121
  3.9 4.1 %collective-permute-start = (bf16[32,4224]{1,0:T(8,128)(2,1)S(1)}, bf16[32,4224]{1,0:T(8,128)(2,1)S(1)}, u32[]{:S(2)}, u32[]{:S(2)}) collective-permute-start(bf16[32,4224]{1,0:T(8,128)(2,1)S(1)} %shard_map.121), channel_id=1, source_target_pairs={{0,16},{2,18},{4,20},{6,22},{8,24},{10,26},{12,28},{14,30},{16,0},... | collective-permute-start | bytes 811016 | tf_op jit(solution)/shard_map/ppermute | solution.py:17
  8.0 1.6 collective-permute-start.1
  9.6 1.5 collective-permute-start.6
  11.1 0.9 copy.17.high_ref
  12.1 4.6 %copy-done = bf16[1,2,4096,768]{3,2,1,0:T(8,128)(2,1)S(1)} copy-done((bf16[1,2,4096,768]{3,2,1,0:T(8,128)(2,1)S(1)}, bf16[1,2,4096,768]{3,2,1,0:T(8,128)(2,1)}, u32[]{:S(2)}) %copy-start) | copy-done | bytes 12582936
  16.6 0.9 copy-done.7
  17.6 0.9 copy-done.8
  18.5 4.0 %shard_map.122.w_ref.refs_3_ = bf16[4096,1536]{1,0:T(8,128)(2,1)S(1)} custom-call(s32[2]{0:T(128)S(1)} %pad_add_fusion.place_ref, bf16[2,4096,768]{2,1,0:T(8,128)(2,1)S(1)} %bitcast.7, f32[2,32,768]{2,1,0:T(8,128)S(1)} %bitcast.11, f32[2,32,768]{2,1,0:T(8,128)S(1)} %bitcast.12), custom_call_target="tpu_custom_call" | custom-call | bytes 25559040 | tf_op jit(solution)/shard_map/pallas_call | solution.py:111
  22.5 2.3 %shard_map.123.refs_2_.w_ref = bf16[1536,2048]{1,0:T(8,128)(2,1)S(1)} custom-call(s32[2]{0:T(128)S(1)} %pad_add_fusion.place_ref, bf16[1,1536,2048]{2,1,0:T(8,128)(2,1)S(1)} %copy-done.1, f32[1,12,2048]{2,1,0:T(8,128)S(1)} %copy.16.low_ref, f32[1,12,2048]{2,1,0:T(8,128)S(1)} %copy.17.high_ref), custom_call_target="tpu_custom_call" | custom-call | bytes 12779520 | tf_op jit(solution)/shard_map/pallas_call | solution.py:111
  24.8 0.6 collective-permute-start.7
  25.9 1.5 collective-permute-start.8
  27.4 5.1 %collective-permute-done.2 = bf16[32,4224]{1,0:T(8,128)(2,1)S(1)} collective-permute-done((bf16[32,4224]{1,0:T(8,128)(2,1)S(1)}, bf16[32,4224]{1,0:T(8,128)(2,1)S(1)}, u32[]{:S(2)}, u32[]{:S(2)}) %collective-permute-start.2) | collective-permute-done | bytes 270368 | tf_op jit(solution)/shard_map/ppermute | solution.py:17
  32.5 1.5 collective-permute-start.9
  34.3 5.8 %collective-permute-done.8 = bf16[32,4224]{1,0:T(8,128)(2,1)S(1)} collective-permute-done((bf16[32,4224]{1,0:T(8,128)(2,1)S(1)}, bf16[32,4224]{1,0:T(8,128)(2,1)S(1)}, u32[]{:S(2)}, u32[]{:S(2)}) %collective-permute-start.8) | collective-permute-done | bytes 270368 | tf_op jit(solution)/shard_map/ppermute | solution.py:17
  40.1 4.7 %shard_map.124 = (bf16[256,768]{1,0:T(8,128)(2,1)S(1)}, f32[256,768]{1,0:T(8,128)S(1)}, f32[256,768]{1,0:T(8,128)S(1)}) custom-call(s32[2]{0:T(128)S(1)} %pad_add_fusion.place_ref, bf16[128,4224]{1,0:T(8,128)(2,1)S(1)} %pad_maximum_fusion.own_ref.refs_3_.refs_0_, bf16[128,4224]{1,0:T(8,128)(2,1)S(1)} %collective-permute-done.3.other_ref.refs_4_.refs_1_, ...), custom_call_target="tpu_custom_call" | custom-call | flops 3221225472 | bytes 16711680 | tf_op jit(solution)/shard_map/pallas_call | solution.py:111
  45.0 1.6 collective-permute-start.4
  46.6 1.1 collective-permute-done.10.other_ref.refs_4_.refs_3_
  47.7 4.7 %shard_map.126 = (bf16[256,768]{1,0:T(8,128)(2,1)S(1)}, f32[256,768]{1,0:T(8,128)S(1)}, f32[256,768]{1,0:T(8,128)S(1)}) custom-call(s32[2]{0:T(128)S(1)} %pad_add_fusion.place_ref, bf16[128,4224]{1,0:T(8,128)(2,1)S(1)} %constant_dynamic-update-slice_fusion.own_ref.refs_3_.refs_2_, bf16[128,4224]{1,0:T(8,128)(2,1)S(1)} %collective-permute-done.10.other_ref.refs_4_.refs_3_, ...), custom_call_target="tpu_custom_call" | custom-call | flops 3221225472 | bytes 16711680 | tf_op jit(solution)/shard_map/pallas_call | solution.py:111
  52.4 1.6 collective-permute-start.11
  54.0 3.0 %collective-permute-done.4.refs_1_ = bf16[256,768]{1,0:T(8,128)(2,1)S(1)} collective-permute-done((bf16[256,768]{1,0:T(8,128)(2,1)S(1)}, bf16[256,768]{1,0:T(8,128)(2,1)S(1)}, u32[]{:S(2)}, u32[]{:S(2)}) %collective-permute-start.4) | collective-permute-done | bytes 393248 | tf_op jit(solution)/shard_map/ppermute | solution.py:17
  57.0 3.8 %shard_map.125 = (bf16[128,2048]{1,0:T(8,128)(2,1)S(1)}, bf16[128,2048]{1,0:T(8,128)(2,1)S(1)}) custom-call(s32[2]{0:T(128)S(1)} %pad_add_fusion.place_ref, bf16[256,768]{1,0:T(8,128)(2,1)S(1)} %get-tuple-element.44.refs_0_, bf16[256,768]{1,0:T(8,128)(2,1)S(1)} %collective-permute-done.4.refs_1_, bf16[1536,2048]{1,0:T(8,128)(2,1)S(1)} %shard_map.123.refs_2_.w_ref, ...), custom_call_target="tpu_custom_call" | custom-call | flops 1610612736 | bytes 10289152 | tf_op jit(solution)/shard_map/pallas_call | solution.py:111
  60.7 4.2 %collective-permute-done.11.refs_1_.refs_3_ = bf16[256,768]{1,0:T(8,128)(2,1)S(1)} collective-permute-done((bf16[256,768]{1,0:T(8,128)(2,1)S(1)}, bf16[256,768]{1,0:T(8,128)(2,1)S(1)}, u32[]{:S(2)}, u32[]{:S(2)}) %collective-permute-start.11) | collective-permute-done | bytes 393248 | tf_op jit(solution)/shard_map/ppermute | solution.py:17
  64.9 3.8 %shard_map.127 = (bf16[128,2048]{1,0:T(8,128)(2,1)S(1)}, bf16[128,2048]{1,0:T(8,128)(2,1)S(1)}) custom-call(s32[2]{0:T(128)S(1)} %pad_add_fusion.place_ref, bf16[256,768]{1,0:T(8,128)(2,1)S(1)} %get-tuple-element.48.refs_0_.refs_2_, bf16[256,768]{1,0:T(8,128)(2,1)S(1)} %collective-permute-done.11.refs_1_.refs_3_, ...), custom_call_target="tpu_custom_call" | custom-call | flops 1610612736 | bytes 10289152 | tf_op jit(solution)/shard_map/pallas_call | solution.py:111
  69.3 1.4 collective-permute-done.12
  70.8 0.6 collective-permute-start.14
  71.4 1.5 collective-permute-start.13
  72.9 7.1 %collective-permute-done.14 = bf16[64,2048]{1,0:T(8,128)(2,1)S(1)} collective-permute-done((bf16[64,2048]{1,0:T(8,128)(2,1)S(1)}, bf16[64,2048]{1,0:T(8,128)(2,1)S(1)}, u32[]{:S(2)}, u32[]{:S(2)}) %collective-permute-start.14) | collective-permute-done | bytes 262176 | tf_op jit(solution)/shard_map/ppermute | solution.py:17
  80.1 0.5 collective-permute-start.15
  80.7 4.2 %collective-permute-done.13 = bf16[64,2048]{1,0:T(8,128)(2,1)S(1)} collective-permute-done((bf16[64,2048]{1,0:T(8,128)(2,1)S(1)}, bf16[64,2048]{1,0:T(8,128)(2,1)S(1)}, u32[]{:S(2)}, u32[]{:S(2)}) %collective-permute-start.13) | collective-permute-done | bytes 262176 | tf_op jit(solution)/shard_map/ppermute | solution.py:17
  84.9 2.1 collective-permute-done.15
  87.4 9.5 %collective-permute-done.16 = bf16[32,2048]{1,0:T(8,128)(2,1)S(1)} collective-permute-done((bf16[32,2048]{1,0:T(8,128)(2,1)S(1)}, bf16[32,2048]{1,0:T(8,128)(2,1)S(1)}, u32[]{:S(2)}, u32[]{:S(2)}) %collective-permute-start.16) | collective-permute-done | bytes 131104 | tf_op jit(solution)/shard_map/ppermute | solution.py:17
  97.0 6.0 %collective-permute-done.17 = bf16[32,2048]{1,0:T(8,128)(2,1)S(1)} collective-permute-done((bf16[32,2048]{1,0:T(8,128)(2,1)S(1)}, bf16[32,2048]{1,0:T(8,128)(2,1)S(1)}, u32[]{:S(2)}, u32[]{:S(2)}) %collective-permute-start.17) | collective-permute-done | bytes 131104 | tf_op jit(solution)/shard_map/ppermute | solution.py:17
  103.1 6.4 %collective-permute-done.18 = bf16[64,2048]{1,0:T(8,128)(2,1)S(1)} collective-permute-done((bf16[64,2048]{1,0:T(8,128)(2,1)S(1)}, bf16[64,2048]{1,0:T(8,128)(2,1)S(1)}, u32[]{:S(2)}, u32[]{:S(2)}) %collective-permute-start.18) | collective-permute-done | bytes 262176 | tf_op jit(solution)/shard_map/ppermute | solution.py:17
  109.6 0.6 collective-permute-start.21
  110.1 1.5 collective-permute-start.22
  111.7 7.1 %collective-permute-done.21 = bf16[64,2048]{1,0:T(8,128)(2,1)S(1)} collective-permute-done((bf16[64,2048]{1,0:T(8,128)(2,1)S(1)}, bf16[64,2048]{1,0:T(8,128)(2,1)S(1)}, u32[]{:S(2)}, u32[]{:S(2)}) %collective-permute-start.21) | collective-permute-done | bytes 262176 | tf_op jit(solution)/shard_map/ppermute | solution.py:17
  118.8 3.6 %shard_map.128 = (bf16[256,2048]{1,0:T(8,128)(2,1)S(1)}, f32[256,768]{1,0:T(8,128)S(1)}, bf16[256,768]{1,0:T(8,128)(2,1)S(1)}) custom-call(s32[2]{0:T(128)S(1)} %pad_add_fusion.place_ref, bf16[128,2048]{1,0:T(8,128)(2,1)S(1)} %pad_maximum_fusion.1.err_own_ref, bf16[128,2048]{1,0:T(8,128)(2,1)S(1)} %collective-permute-done.19.err_other_ref, ...), custom_call_target="tpu_custom_call" | custom-call | flops 1610612736 | bytes 11730944 | tf_op jit(solution)/shard_map/pallas_call | solution.py:111
  122.4 1.0 copy-done.9
  124.0 1.6 collective-permute-start.20
  125.9 3.6 %shard_map.129 = (bf16[256,2048]{1,0:T(8,128)(2,1)S(1)}, f32[256,768]{1,0:T(8,128)S(1)}, bf16[256,768]{1,0:T(8,128)(2,1)S(1)}) custom-call(s32[2]{0:T(128)S(1)} %pad_add_fusion.place_ref, bf16[128,2048]{1,0:T(8,128)(2,1)S(1)} %constant_dynamic-update-slice_fusion.4.err_own_ref, bf16[128,2048]{1,0:T(8,128)(2,1)S(1)} %collective-permute-done.23.err_other_ref, ...), custom_call_target="tpu_custom_call" | custom-call | flops 1610612736 | bytes 11730944 | tf_op jit(solution)/shard_map/pallas_call | solution.py:111
  129.6 6.0 %collective-permute-done.20.refs_0_ = bf16[256,768]{1,0:T(8,128)(2,1)S(1)} collective-permute-done((bf16[256,768]{1,0:T(8,128)(2,1)S(1)}, bf16[256,768]{1,0:T(8,128)(2,1)S(1)}, u32[]{:S(2)}, u32[]{:S(2)}) %collective-permute-start.20) | collective-permute-done | bytes 393248 | tf_op jit(solution)/shard_map/ppermute | solution.py:17
  135.6 4.0 %shard_map.130 = (bf16[256,1536]{1,0:T(8,128)(2,1)S(1)}, bf16[128,2048]{1,0:T(8,128)(2,1)S(1)}, bf16[128,2048]{1,0:T(8,128)(2,1)S(1)}) custom-call(s32[2]{0:T(128)S(1)} %pad_add_fusion.place_ref, f32[256,768]{1,0:T(8,128)S(1)} %get-tuple-element.52.grad_own_ref, bf16[256,768]{1,0:T(8,128)(2,1)S(1)} %collective-permute-done.20.refs_0_, ...), custom_call_target="tpu_custom_call" | custom-call | flops 1610612736 | bytes 17170432 | tf_op jit(solution)/shard_map/pallas_call | solution.py:111
  139.6 1.6 collective-permute-start.27
  141.6 9.5 %collective-permute-done.27.refs_0_ = bf16[256,768]{1,0:T(8,128)(2,1)S(1)} collective-permute-done((bf16[256,768]{1,0:T(8,128)(2,1)S(1)}, bf16[256,768]{1,0:T(8,128)(2,1)S(1)}, u32[]{:S(2)}, u32[]{:S(2)}) %collective-permute-start.27) | collective-permute-done | bytes 393248 | tf_op jit(solution)/shard_map/ppermute | solution.py:17
  151.1 4.0 %shard_map.132 = (bf16[256,1536]{1,0:T(8,128)(2,1)S(1)}, bf16[128,2048]{1,0:T(8,128)(2,1)S(1)}, bf16[128,2048]{1,0:T(8,128)(2,1)S(1)}) custom-call(s32[2]{0:T(128)S(1)} %pad_add_fusion.place_ref, f32[256,768]{1,0:T(8,128)S(1)} %get-tuple-element.65.grad_own_ref, bf16[256,768]{1,0:T(8,128)(2,1)S(1)} %collective-permute-done.27.refs_0_, ...), custom_call_target="tpu_custom_call" | custom-call | flops 1610612736 | bytes 17170432 | tf_op jit(solution)/shard_map/pallas_call | solution.py:111
  155.2 1.6 collective-permute-start.25
  156.8 3.8 %shard_map.133 = (bf16[128,2048]{1,0:T(8,128)(2,1)S(1)}, bf16[128,2048]{1,0:T(8,128)(2,1)S(1)}) custom-call(s32[2]{0:T(128)S(1)} %pad_add_fusion.place_ref, bf16[256,1536]{1,0:T(8,128)(2,1)S(1)} %get-tuple-element.73.grad_ref.refs_5_, bf16[4096,1536]{1,0:T(8,128)(2,1)S(1)} %shard_map.122.w_ref.refs_3_), custom_call_target="tpu_custom_call" | custom-call | flops 1610612736 | bytes 14417920 | tf_op jit(solution)/shard_map/pallas_call | solution.py:111
  160.9 8.6 %collective-permute-done.25 = bf16[128,2048]{1,0:T(8,128)(2,1)S(1)} collective-permute-done((bf16[128,2048]{1,0:T(8,128)(2,1)S(1)}, bf16[128,2048]{1,0:T(8,128)(2,1)S(1)}, u32[]{:S(2)}, u32[]{:S(2)}) %collective-permute-start.25) | collective-permute-done | bytes 524320 | tf_op jit(solution)/shard_map/ppermute | solution.py:17
  169.5 1.5 collective-permute-start.29
  171.6 3.8 %shard_map.131 = (bf16[128,2048]{1,0:T(8,128)(2,1)S(1)}, bf16[128,2048]{1,0:T(8,128)(2,1)S(1)}) custom-call(s32[2]{0:T(128)S(1)} %pad_add_fusion.place_ref, bf16[256,1536]{1,0:T(8,128)(2,1)S(1)} %get-tuple-element.62.grad_ref.refs_4_, bf16[4096,1536]{1,0:T(8,128)(2,1)S(1)} %shard_map.122.w_ref.refs_3_), custom_call_target="tpu_custom_call" | custom-call | flops 1610612736 | bytes 14417920 | tf_op jit(solution)/shard_map/pallas_call | solution.py:111
  175.4 3.3 %collective-permute-done.29 = bf16[64,2048]{1,0:T(8,128)(2,1)S(1)} collective-permute-done((bf16[64,2048]{1,0:T(8,128)(2,1)S(1)}, bf16[64,2048]{1,0:T(8,128)(2,1)S(1)}, u32[]{:S(2)}, u32[]{:S(2)}) %collective-permute-start.29) | collective-permute-done | bytes 262176 | tf_op jit(solution)/shard_map/ppermute | solution.py:17
  178.7 4.3 %collective-permute-done.32 = bf16[64,2048]{1,0:T(8,128)(2,1)S(1)} collective-permute-done((bf16[64,2048]{1,0:T(8,128)(2,1)S(1)}, bf16[64,2048]{1,0:T(8,128)(2,1)S(1)}, u32[]{:S(2)}, u32[]{:S(2)}) %collective-permute-start.32) | collective-permute-done | bytes 262176 | tf_op jit(solution)/shard_map/ppermute | solution.py:17
  183.3 0.6 collective-permute-start.33
  183.8 6.8 %shard_map.134.refs_7_ = f32[4,32,768]{2,1,0:T(8,128)} custom-call(s32[2]{0:T(128)S(1)} %pad_add_fusion.place_ref, bf16[128,4224]{1,0:T(8,128)(2,1)S(1)} %pad_maximum_fusion.own_ref.refs_3_.refs_0_, bf16[128,4224]{1,0:T(8,128)(2,1)S(1)} %collective-permute-done.3.other_ref.refs_4_.refs_1_, ...), custom_call_target="tpu_custom_call" | custom-call | flops 3221225472 | bytes 18874368 | tf_op jit(solution)/shard_map/pallas_call | solution.py:111
  190.7 1.5 collective-permute-start.31
  192.4 7.0 %shard_map.135 = f32[4,32,768]{2,1,0:T(8,128)} custom-call(s32[2]{0:T(128)S(1)} %pad_add_fusion.place_ref, bf16[128,4224]{1,0:T(8,128)(2,1)S(1)} %pad_maximum_fusion.own_ref.refs_3_.refs_0_, bf16[128,4224]{1,0:T(8,128)(2,1)S(1)} %collective-permute-done.3.other_ref.refs_4_.refs_1_, ...), custom_call_target="tpu_custom_call", output_to_operand_aliasing={{}: (8, {})} | custom-call | flops 3221225472 | bytes 18874368 | tf_op jit(solution)/shard_map/pallas_call | solution.py:111
  199.5 1.3 collective-permute-start.35
  200.9 5.6 %shard_map.136 = f32[2,12,2048]{2,1,0:T(8,128)S(1)} custom-call(s32[2]{0:T(128)S(1)} %pad_add_fusion.place_ref, bf16[256,768]{1,0:T(8,128)(2,1)S(1)} %get-tuple-element.44.refs_0_, bf16[256,768]{1,0:T(8,128)(2,1)S(1)} %collective-permute-done.4.refs_1_, bf16[256,768]{1,0:T(8,128)(2,1)S(1)} %copy-done.3, bf16[256,768]{1,0:T(8,128)(2,1)S(1)} %copy-done.5, ...), custom_call_target="tpu_custom_call" | custom-call | flops 3221225472 | bytes 10158080 | tf_op jit(solution)/shard_map/pallas_call | solution.py:111
  206.5 0.8 copy.18
  207.3 0.8 add_convert_fusion.9
  (82 shorter events, 5.6 us)
Async XLA Ops:
  2.2 0.9 copy-start.6
  3.9 20.9 %collective-permute-start = (bf16[32,4224]{1,0:T(8,128)(2,1)S(1)}, bf16[32,4224]{1,0:T(8,128)(2,1)S(1)}, u32[]{:S(2)}, u32[]{:S(2)}) collective-permute-start(bf16[32,4224]{1,0:T(8,128)(2,1)S(1)} %shard_map.121), channel_id=1, source_target_pairs={{0,16},{2,18},{4,20},{6,22},{8,24},{10,26},{12,28},{14,30},{16,0},... | collective-permute-start | bytes 811016 | tf_op jit(solution)/shard_map/ppermute | solution.py:17
  8.0 17.8 %collective-permute-start.1 = (bf16[32,4224]{1,0:T(8,128)(2,1)S(1)}, bf16[32,4224]{1,0:T(8,128)(2,1)S(1)}, u32[]{:S(2)}, u32[]{:S(2)}) collective-permute-start(bf16[32,4224]{1,0:T(8,128)(2,1)S(1)} %shard_map.121), channel_id=1, source_target_pairs={{0,8},{2,10},{4,12},{6,14},{8,0},{10,2},{12,4},{14,6},{16,24},{18,... | collective-permute-start | bytes 811016 | tf_op jit(solution)/shard_map/ppermute | solution.py:17
  9.6 17.8 %collective-permute-start.6 = (bf16[32,4224]{1,0:T(8,128)(2,1)S(1)}, bf16[32,4224]{1,0:T(8,128)(2,1)S(1)}, u32[]{:S(2)}, u32[]{:S(2)}) collective-permute-start(bf16[32,4224]{1,0:T(8,128)(2,1)S(1)} %shard_map.121), channel_id=1, source_target_pairs={{0,4},{2,6},{4,0},{6,2},{8,12},{10,14},{12,8},{14,10},{16,20},{18,... | collective-permute-start | bytes 811016 | tf_op jit(solution)/shard_map/ppermute | solution.py:17
  12.0 4.6 %copy-start = (bf16[1,2,4096,768]{3,2,1,0:T(8,128)(2,1)S(1)}, bf16[1,2,4096,768]{3,2,1,0:T(8,128)(2,1)}, u32[]{:S(2)}) copy-start(bf16[1,2,4096,768]{3,2,1,0:T(8,128)(2,1)} %refs_6_.4) | copy-start | bytes 37748740
  16.6 0.9 copy-start.7
  17.5 0.9 copy-start.8
  18.5 4.0 %copy-start.12 = (f32[1,12,2048]{2,0,1:T(1,128)S(1)}, f32[1,12,2048]{2,0,1:T(1,128)}, u32[]{:S(2)}) copy-start(f32[1,12,2048]{2,0,1:T(1,128)} %param.18) | copy-start | bytes 294916
  18.5 4.1 %copy-start.1 = (bf16[1,1536,2048]{2,1,0:T(8,128)(2,1)S(1)}, bf16[1,1536,2048]{2,1,0:T(8,128)(2,1)}, u32[]{:S(2)}) copy-start(bf16[1,1536,2048]{2,1,0:T(8,128)(2,1)} %refs_6_.5) | copy-start | bytes 18874372
  24.8 9.5 %collective-permute-start.7 = (bf16[32,4224]{1,0:T(8,128)(2,1)S(1)}, bf16[32,4224]{1,0:T(8,128)(2,1)S(1)}, u32[]{:S(2)}, u32[]{:S(2)}) collective-permute-start(bf16[32,4224]{1,0:T(8,128)(2,1)S(1)} %collective-permute-done), channel_id=1, source_target_pairs={{0,4},{2,6},{4,0},{6,2},{8,12},{10,14},{12,8},{14,10},{16,20},{18,... | collective-permute-start | bytes 811016 | tf_op jit(solution)/shard_map/ppermute | solution.py:17
  25.4 7.1 %collective-permute-start.2 = (bf16[32,4224]{1,0:T(8,128)(2,1)S(1)}, bf16[32,4224]{1,0:T(8,128)(2,1)S(1)}, u32[]{:S(2)}, u32[]{:S(2)}) collective-permute-start(bf16[32,4224]{1,0:T(8,128)(2,1)S(1)} %collective-permute-done), channel_id=1, source_target_pairs={{0,8},{2,10},{4,12},{6,14},{8,0},{10,2},{12,4},{14,6},{16,24},{18,... | collective-permute-start | bytes 811016 | tf_op jit(solution)/shard_map/ppermute | solution.py:17
  25.9 14.2 %collective-permute-start.8 = (bf16[32,4224]{1,0:T(8,128)(2,1)S(1)}, bf16[32,4224]{1,0:T(8,128)(2,1)S(1)}, u32[]{:S(2)}, u32[]{:S(2)}) collective-permute-start(bf16[32,4224]{1,0:T(8,128)(2,1)S(1)} %collective-permute-done.1), channel_id=1, source_target_pairs={{0,4},{2,6},{4,0},{6,2},{8,12},{10,14},{12,8},{14,10},{16,20},{18,... | collective-permute-start | bytes 811016 | tf_op jit(solution)/shard_map/ppermute | solution.py:17
  32.5 12.3 %collective-permute-start.9 = (bf16[32,4224]{1,0:T(8,128)(2,1)S(1)}, bf16[32,4224]{1,0:T(8,128)(2,1)S(1)}, u32[]{:S(2)}, u32[]{:S(2)}) collective-permute-start(bf16[32,4224]{1,0:T(8,128)(2,1)S(1)} %collective-permute-done.2), channel_id=1, source_target_pairs={{0,4},{2,6},{4,0},{6,2},{8,12},{10,14},{12,8},{14,10},{16,20},{18,... | collective-permute-start | bytes 811016 | tf_op jit(solution)/shard_map/ppermute | solution.py:17
  34.1 6.0 %collective-permute-start.3 = (bf16[128,4224]{1,0:T(8,128)(2,1)S(1)}, bf16[128,4224]{1,0:T(8,128)(2,1)S(1)}, u32[]{:S(2)}, u32[]{:S(2)}) collective-permute-start(bf16[128,4224]{1,0:T(8,128)(2,1)S(1)} %pad_maximum_fusion.own_ref.refs_3_.refs_0_), channel_id=1, source_target_pairs={{0,2},{2,0},{4,6},{6,4},{8,10},{10,8},{12,14},{14,12},{16,18},{18,... | collective-permute-start | bytes 3244040 | tf_op jit(solution)/shard_map/ppermute | solution.py:17
  44.9 2.8 %collective-permute-start.10 = (bf16[128,4224]{1,0:T(8,128)(2,1)S(1)}, bf16[128,4224]{1,0:T(8,128)(2,1)S(1)}, u32[]{:S(2)}, u32[]{:S(2)}) collective-permute-start(bf16[128,4224]{1,0:T(8,128)(2,1)S(1)} %constant_dynamic-update-slice_fusion.own_ref.refs_3_.refs_2_), channel_id=1, source_target_pairs={{0,2},{2,0},{4,6},{6,4},{8,10},{10,8},{12,14},{14,12},{16,18},{18,... | collective-permute-start | bytes 3244040 | tf_op jit(solution)/shard_map/ppermute | solution.py:17
  45.0 12.0 %collective-permute-start.4 = (bf16[256,768]{1,0:T(8,128)(2,1)S(1)}, bf16[256,768]{1,0:T(8,128)(2,1)S(1)}, u32[]{:S(2)}, u32[]{:S(2)}) collective-permute-start(bf16[256,768]{1,0:T(8,128)(2,1)S(1)} %get-tuple-element.44.refs_0_), channel_id=1, source_target_pairs={{0,1},{1,0},{2,3},{3,2},{4,5},{5,4},{6,7},{7,6},{8,9},{9,8},{10,11... | collective-permute-start | bytes 1179656 | tf_op jit(solution)/shard_map/ppermute | solution.py:17
  52.4 12.6 %copy-start.2 = (bf16[256,768]{1,0:T(8,128)(2,1)}, bf16[256,768]{1,0:T(8,128)(2,1)S(1)}, u32[]{:S(2)}) copy-start(bf16[256,768]{1,0:T(8,128)(2,1)S(1)} %get-tuple-element.48.refs_0_.refs_2_) | copy-start | bytes 1179652
  52.4 12.5 %collective-permute-start.11 = (bf16[256,768]{1,0:T(8,128)(2,1)S(1)}, bf16[256,768]{1,0:T(8,128)(2,1)S(1)}, u32[]{:S(2)}, u32[]{:S(2)}) collective-permute-start(bf16[256,768]{1,0:T(8,128)(2,1)S(1)} %get-tuple-element.48.refs_0_.refs_2_), channel_id=1, source_target_pairs={{0,1},{1,0},{2,3},{3,2},{4,5},{5,4},{6,7},{7,6},{8,9},{9,8},{10,11... | collective-permute-start | bytes 1179656 | tf_op jit(solution)/shard_map/ppermute | solution.py:17
  64.9 3.8 %copy-start.4 = (bf16[256,768]{1,0:T(8,128)(2,1)}, bf16[256,768]{1,0:T(8,128)(2,1)S(1)}, u32[]{:S(2)}) copy-start(bf16[256,768]{1,0:T(8,128)(2,1)S(1)} %collective-permute-done.11.refs_1_.refs_3_) | copy-start | bytes 1179652
  68.7 2.0 collective-permute-start.12
  68.8 4.1 %collective-permute-start.5 = (bf16[128,2048]{1,0:T(8,128)(2,1)S(1)}, bf16[128,2048]{1,0:T(8,128)(2,1)S(1)}, u32[]{:S(2)}, u32[]{:S(2)}) collective-permute-start(bf16[128,2048]{1,0:T(8,128)(2,1)S(1)} %get-tuple-element.46), channel_id=1, source_target_pairs={{0,2},{2,0},{4,6},{6,4},{8,10},{10,8},{12,14},{14,12},{16,18},{18,... | collective-permute-start | bytes 1572872 | tf_op jit(solution)/shard_map/ppermute | solution.py:17
  70.8 26.0 %copy-start.11 = (bf16[32,2048]{1,0:T(8,128)(2,1)S(1)}, bf16[32,2048]{1,0:T(8,128)(2,1)}, u32[]{:S(2)}) copy-start(bf16[32,2048]{1,0:T(8,128)(2,1)} %param.11) | copy-start | bytes 393220
  70.8 9.2 %collective-permute-start.14 = (bf16[64,2048]{1,0:T(8,128)(2,1)S(1)}, bf16[64,2048]{1,0:T(8,128)(2,1)S(1)}, u32[]{:S(2)}, u32[]{:S(2)}) collective-permute-start(bf16[64,2048]{1,0:T(8,128)(2,1)S(1)} %get-tuple-element.87), channel_id=1, source_target_pairs={{0,4},{2,6},{4,0},{6,2},{8,12},{10,14},{12,8},{14,10},{16,20},{18,... | collective-permute-start | bytes 786440 | tf_op jit(solution)/shard_map/ppermute | solution.py:17
  71.4 13.4 %collective-permute-start.13 = (bf16[64,2048]{1,0:T(8,128)(2,1)S(1)}, bf16[64,2048]{1,0:T(8,128)(2,1)S(1)}, u32[]{:S(2)}, u32[]{:S(2)}) collective-permute-start(bf16[64,2048]{1,0:T(8,128)(2,1)S(1)} %get-tuple-element.86), channel_id=1, source_target_pairs={{0,4},{2,6},{4,0},{6,2},{8,12},{10,14},{12,8},{14,10},{16,20},{18,... | collective-permute-start | bytes 786440 | tf_op jit(solution)/shard_map/ppermute | solution.py:17
  80.1 6.8 %collective-permute-start.15 = (bf16[64,2048]{1,0:T(8,128)(2,1)S(1)}, bf16[64,2048]{1,0:T(8,128)(2,1)S(1)}, u32[]{:S(2)}, u32[]{:S(2)}) collective-permute-start(bf16[64,2048]{1,0:T(8,128)(2,1)S(1)} %add_convert_fusion.6), channel_id=1, source_target_pairs={{0,8},{2,10},{4,12},{6,14},{8,0},{10,2},{12,4},{14,6},{16,24},{18,... | collective-permute-start | bytes 786440 | tf_op jit(solution)/shard_map/ppermute | solution.py:17
  87.0 9.9 %collective-permute-start.16 = (bf16[32,2048]{1,0:T(8,128)(2,1)S(1)}, bf16[32,2048]{1,0:T(8,128)(2,1)S(1)}, u32[]{:S(2)}, u32[]{:S(2)}) collective-permute-start(bf16[32,2048]{1,0:T(8,128)(2,1)S(1)} %add_convert_fusion.11), channel_id=1, source_target_pairs={{0,16},{2,18},{4,20},{6,22},{8,24},{10,26},{12,28},{14,30},{16,0},... | collective-permute-start | bytes 393224 | tf_op jit(solution)/shard_map/ppermute | solution.py:17
  97.0 6.0 %collective-permute-start.17 = (bf16[32,2048]{1,0:T(8,128)(2,1)S(1)}, bf16[32,2048]{1,0:T(8,128)(2,1)S(1)}, u32[]{:S(2)}, u32[]{:S(2)}) collective-permute-start(bf16[32,2048]{1,0:T(8,128)(2,1)S(1)} %subtract_convert_fusion), channel_id=1, source_target_pairs={{0,16},{2,18},{4,20},{6,22},{8,24},{10,26},{12,28},{14,30},{16,0},... | collective-permute-start | bytes 393224 | tf_op jit(solution)/shard_map/ppermute | solution.py:17
  103.0 6.4 %collective-permute-start.18 = (bf16[64,2048]{1,0:T(8,128)(2,1)S(1)}, bf16[64,2048]{1,0:T(8,128)(2,1)S(1)}, u32[]{:S(2)}, u32[]{:S(2)}) collective-permute-start(bf16[64,2048]{1,0:T(8,128)(2,1)S(1)} %pad_maximum_fusion.2), channel_id=1, source_target_pairs={{0,8},{2,10},{4,12},{6,14},{8,0},{10,2},{12,4},{14,6},{16,24},{18,... | collective-permute-start | bytes 786440 | tf_op jit(solution)/shard_map/ppermute | solution.py:17
  109.5 9.3 %collective-permute-start.19 = (bf16[128,2048]{1,0:T(8,128)(2,1)S(1)}, bf16[128,2048]{1,0:T(8,128)(2,1)S(1)}, u32[]{:S(2)}, u32[]{:S(2)}) collective-permute-start(bf16[128,2048]{1,0:T(8,128)(2,1)S(1)} %pad_maximum_fusion.1.err_own_ref), channel_id=1, source_target_pairs={{0,2},{2,0},{4,6},{6,4},{8,10},{10,8},{12,14},{14,12},{16,18},{18,... | collective-permute-start | bytes 1572872 | tf_op jit(solution)/shard_map/ppermute | solution.py:17
  109.6 9.2 %collective-permute-start.21 = (bf16[64,2048]{1,0:T(8,128)(2,1)S(1)}, bf16[64,2048]{1,0:T(8,128)(2,1)S(1)}, u32[]{:S(2)}, u32[]{:S(2)}) collective-permute-start(bf16[64,2048]{1,0:T(8,128)(2,1)S(1)} %pad_maximum_fusion.2), channel_id=1, source_target_pairs={{0,4},{2,6},{4,0},{6,2},{8,12},{10,14},{12,8},{14,10},{16,20},{18,... | collective-permute-start | bytes 786440 | tf_op jit(solution)/shard_map/ppermute | solution.py:17
  110.1 13.8 %collective-permute-start.22 = (bf16[64,2048]{1,0:T(8,128)(2,1)S(1)}, bf16[64,2048]{1,0:T(8,128)(2,1)S(1)}, u32[]{:S(2)}, u32[]{:S(2)}) collective-permute-start(bf16[64,2048]{1,0:T(8,128)(2,1)S(1)} %collective-permute-done.18), channel_id=1, source_target_pairs={{0,4},{2,6},{4,0},{6,2},{8,12},{10,14},{12,8},{14,10},{16,20},{18,... | collective-permute-start | bytes 786440 | tf_op jit(solution)/shard_map/ppermute | solution.py:17
  122.4 1.0 copy-start.9
  123.9 2.0 collective-permute-start.23
  124.0 11.5 %collective-permute-start.20 = (bf16[256,768]{1,0:T(8,128)(2,1)S(1)}, bf16[256,768]{1,0:T(8,128)(2,1)S(1)}, u32[]{:S(2)}, u32[]{:S(2)}) collective-permute-start(bf16[256,768]{1,0:T(8,128)(2,1)S(1)} %get-tuple-element.53), channel_id=1, source_target_pairs={{0,1},{1,0},{2,3},{3,2},{4,5},{5,4},{6,7},{7,6},{8,9},{9,8},{10,11... | collective-permute-start | bytes 1179656 | tf_op jit(solution)/shard_map/ppermute | solution.py:17
  139.5 2.0 collective-permute-start.24
  139.6 11.5 %collective-permute-start.27 = (bf16[256,768]{1,0:T(8,128)(2,1)S(1)}, bf16[256,768]{1,0:T(8,128)(2,1)S(1)}, u32[]{:S(2)}, u32[]{:S(2)}) collective-permute-start(bf16[256,768]{1,0:T(8,128)(2,1)S(1)} %get-tuple-element.66), channel_id=1, source_target_pairs={{0,1},{1,0},{2,3},{3,2},{4,5},{5,4},{6,7},{7,6},{8,9},{9,8},{10,11... | collective-permute-start | bytes 1179656 | tf_op jit(solution)/shard_map/ppermute | solution.py:17
  155.1 5.7 %collective-permute-start.28 = (bf16[128,2048]{1,0:T(8,128)(2,1)S(1)}, bf16[128,2048]{1,0:T(8,128)(2,1)S(1)}, u32[]{:S(2)}, u32[]{:S(2)}) collective-permute-start(bf16[128,2048]{1,0:T(8,128)(2,1)S(1)} %get-tuple-element.71), channel_id=1, source_target_pairs={{0,2},{2,0},{4,6},{6,4},{8,10},{10,8},{12,14},{14,12},{16,18},{18,... | collective-permute-start | bytes 1572872 | tf_op jit(solution)/shard_map/ppermute | solution.py:17
  155.2 14.3 %collective-permute-start.25 = (bf16[128,2048]{1,0:T(8,128)(2,1)S(1)}, bf16[128,2048]{1,0:T(8,128)(2,1)S(1)}, u32[]{:S(2)}, u32[]{:S(2)}) collective-permute-start(bf16[128,2048]{1,0:T(8,128)(2,1)S(1)} %add_convert_fusion), channel_id=1, source_target_pairs={{0,1},{1,0},{2,3},{3,2},{4,5},{5,4},{6,7},{7,6},{8,9},{9,8},{10,11... | collective-permute-start | bytes 1572872 | tf_op jit(solution)/shard_map/ppermute | solution.py:17
  156.8 27.1 %slice-start = ((s8[12582912]{0:T(1024)(128)(4,1)}), s8[4194304]{0:T(1024)(128)(4,1)S(1)}, s32[]{:S(2)}) async-start(s8[12582912]{0:T(1024)(128)(4,1)} %bitcast.8), calls=%async_computation | async-start | bytes 8388608
  156.8 27.1 %slice-start.1 = ((s8[12582912]{0:T(1024)(128)(4,1)}), s8[4194304]{0:T(1024)(128)(4,1)S(1)}, s32[]{:S(2)}) async-start(s8[12582912]{0:T(1024)(128)(4,1)} %bitcast.8), calls=%async_computation.1 | async-start | bytes 8388608
  160.6 14.9 %collective-permute-start.30 = (bf16[128,2048]{1,0:T(8,128)(2,1)S(1)}, bf16[128,2048]{1,0:T(8,128)(2,1)S(1)}, u32[]{:S(2)}, u32[]{:S(2)}) collective-permute-start(bf16[128,2048]{1,0:T(8,128)(2,1)S(1)} %get-tuple-element.75), channel_id=1, source_target_pairs={{0,2},{2,0},{4,6},{6,4},{8,10},{10,8},{12,14},{14,12},{16,18},{18,... | collective-permute-start | bytes 1572872 | tf_op jit(solution)/shard_map/ppermute | solution.py:17
  169.5 9.2 %collective-permute-start.29 = (bf16[64,2048]{1,0:T(8,128)(2,1)S(1)}, bf16[64,2048]{1,0:T(8,128)(2,1)S(1)}, u32[]{:S(2)}, u32[]{:S(2)}) collective-permute-start(bf16[64,2048]{1,0:T(8,128)(2,1)S(1)} %get-tuple-element.72), channel_id=1, source_target_pairs={{0,1},{1,0},{2,3},{3,2},{4,5},{5,4},{6,7},{7,6},{8,9},{9,8},{10,11... | collective-permute-start | bytes 786440 | tf_op jit(solution)/shard_map/ppermute | solution.py:17
  171.0 12.0 %collective-permute-start.32 = (bf16[64,2048]{1,0:T(8,128)(2,1)S(1)}, bf16[64,2048]{1,0:T(8,128)(2,1)S(1)}, u32[]{:S(2)}, u32[]{:S(2)}) collective-permute-start(bf16[64,2048]{1,0:T(8,128)(2,1)S(1)} %get-tuple-element.76), channel_id=1, source_target_pairs={{0,1},{1,0},{2,3},{3,2},{4,5},{5,4},{6,7},{7,6},{8,9},{9,8},{10,11... | collective-permute-start | bytes 786440 | tf_op jit(solution)/shard_map/ppermute | solution.py:17
  171.5 12.3 %slice-start.2 = ((s8[12582912]{0:T(1024)(128)(4,1)}), s8[4194304]{0:T(1024)(128)(4,1)S(1)}, s32[]{:S(2)}) async-start(s8[12582912]{0:T(1024)(128)(4,1)} %bitcast.8), calls=%async_computation.2 | async-start | bytes 8388608
  175.3 16.8 %collective-permute-start.26 = (bf16[128,2048]{1,0:T(8,128)(2,1)S(1)}, bf16[128,2048]{1,0:T(8,128)(2,1)S(1)}, u32[]{:S(2)}, u32[]{:S(2)}) collective-permute-start(bf16[128,2048]{1,0:T(8,128)(2,1)S(1)} %get-tuple-element.64), channel_id=1, source_target_pairs={{0,2},{2,0},{4,6},{6,4},{8,10},{10,8},{12,14},{14,12},{16,18},{18,... | collective-permute-start | bytes 1572872 | tf_op jit(solution)/shard_map/ppermute | solution.py:17
  183.3 8.9 %collective-permute-start.33 = (bf16[64,2048]{1,0:T(8,128)(2,1)S(1)}, bf16[64,2048]{1,0:T(8,128)(2,1)S(1)}, u32[]{:S(2)}, u32[]{:S(2)}) collective-permute-start(bf16[64,2048]{1,0:T(8,128)(2,1)S(1)} %get-tuple-element.83), channel_id=1, source_target_pairs={{0,4},{2,6},{4,0},{6,2},{8,12},{10,14},{12,8},{14,10},{16,20},{18,... | collective-permute-start | bytes 786440 | tf_op jit(solution)/shard_map/ppermute | solution.py:17
  190.7 8.8 %collective-permute-start.31 = (bf16[64,2048]{1,0:T(8,128)(2,1)S(1)}, bf16[64,2048]{1,0:T(8,128)(2,1)S(1)}, u32[]{:S(2)}, u32[]{:S(2)}) collective-permute-start(bf16[64,2048]{1,0:T(8,128)(2,1)S(1)} %get-tuple-element.82), channel_id=1, source_target_pairs={{0,4},{2,6},{4,0},{6,2},{8,12},{10,14},{12,8},{14,10},{16,20},{18,... | collective-permute-start | bytes 786440 | tf_op jit(solution)/shard_map/ppermute | solution.py:17
  192.3 8.5 %copy-start.3 = (bf16[256,768]{1,0:T(8,128)(2,1)S(1)}, bf16[256,768]{1,0:T(8,128)(2,1)}, u32[]{:S(2)}) copy-start(bf16[256,768]{1,0:T(8,128)(2,1)} %copy-done.2) | copy-start | bytes 1179652
  192.3 8.5 %copy-start.5 = (bf16[256,768]{1,0:T(8,128)(2,1)S(1)}, bf16[256,768]{1,0:T(8,128)(2,1)}, u32[]{:S(2)}) copy-start(bf16[256,768]{1,0:T(8,128)(2,1)} %copy-done.4) | copy-start | bytes 1179652
  192.3 8.5 %copy-start.10 = (bf16[256,2048]{1,0:T(8,128)(2,1)S(1)}, bf16[256,2048]{1,0:T(8,128)(2,1)}, u32[]{:S(2)}) copy-start(bf16[256,2048]{1,0:T(8,128)(2,1)} %copy-done.9) | copy-start | bytes 3145732
  192.3 7.1 %collective-permute-start.34 = (bf16[64,2048]{1,0:T(8,128)(2,1)S(1)}, bf16[64,2048]{1,0:T(8,128)(2,1)S(1)}, u32[]{:S(2)}, u32[]{:S(2)}) collective-permute-start(bf16[64,2048]{1,0:T(8,128)(2,1)S(1)} %add_convert_fusion.1), channel_id=1, source_target_pairs={{0,8},{2,10},{4,12},{6,14},{8,0},{10,2},{12,4},{14,6},{16,24},{18,... | collective-permute-start | bytes 786440 | tf_op jit(solution)/shard_map/ppermute | solution.py:17
  199.5 7.8 %collective-permute-start.35 = (bf16[32,2048]{1,0:T(8,128)(2,1)S(1)}, bf16[32,2048]{1,0:T(8,128)(2,1)S(1)}, u32[]{:S(2)}, u32[]{:S(2)}) collective-permute-start(bf16[32,2048]{1,0:T(8,128)(2,1)S(1)} %add_convert_fusion.10), channel_id=1, source_target_pairs={{0,16},{2,18},{4,20},{6,22},{8,24},{10,26},{12,28},{14,30},{16,0},... | collective-permute-start | bytes 393224 | tf_op jit(solution)/shard_map/ppermute | solution.py:17

commit v4 on v3

--- a/solution.py
+++ b/solution.py
@@ -42,12 +42,6 @@
     return parts
 
 
-def pick(part, cut):
-    if isinstance(part, list):
-        return part[0] if cut.start else part[1]
-    return part[cut]
-
-
 def add(parts):
     total = parts[0].astype(F32)
     for part in parts[1:]:
@@ -55,19 +49,20 @@
     return total
 
 
-def scatter_rows(near, across):
-    rows = near[0].shape[0] // 2
-    totals = []
-    for cut in (slice(rows, 2 * rows), slice(0, rows)):
-        sent = swap(add([pick(part, cut) for part in across]).astype(BF16), "expert", 2)
-        totals.append([pick(part, cut) for part in near] + [sent])
-    sent = swap(add(totals[0]).astype(BF16), "expert", 4)
-    terms = totals[1] + [sent]
+def scatter_far(terms):
     for distance in reversed(far_distances()):
         half = terms[0].shape[0] // 2
         sent = swap(add([part[half:] for part in terms]).astype(BF16), "expert", distance)
         terms = [part[:half] for part in terms] + [sent]
     return add(terms)
+
+
+def scatter_rows(near, across):
+    rows = near[0].shape[0] // 2
+    upper = swap(add([part[rows:] for part in across]).astype(BF16), "expert", 2)
+    sent = swap(add([part[rows:] for part in near] + [upper]).astype(BF16), "expert", 4)
+    lower = tie(add([part[:rows] for part in across]).astype(BF16), upper)
+    return scatter_far([part[:rows] for part in near] + [swap(lower, "expert", 2), sent])
 
 
 def dot(left, right):
@@ -163,7 +158,19 @@
     return (0, 0, 0, 0)
 
 
-def dequant(place, codes, low, high, halves):
+def pack(place, parts):
+    rows = sum(part.shape[0] for part in parts)
+
+    def kernel(place_ref, *refs):
+        start = 0
+        for ref in refs[:-1]:
+            refs[-1][start : start + ref.shape[0], :] = ref[...]
+            start += ref.shape[0]
+
+    return resident(kernel, parts, [((rows, parts[0].shape[1]), parts[0].dtype)], place)[0]
+
+
+def dequant(place, codes, low, high, halves=1):
     count, height, cols = codes.shape
     groups = low.shape[1]
     size = height // groups
@@ -171,7 +178,7 @@
 
     def kernel(place_ref, code_ref, low_ref, high_ref, out_ref):
         def block(i, carry):
-            base = moved(i, held, place_ref)
+            base = moved(i, held, place_ref) if halves > 1 else i
             source = pl.multiple_of(base * size, size)
             to = pl.multiple_of(i * size, size)
             for k in range(count):
@@ -206,7 +213,7 @@
     size = step_of(hidden)
 
     def kernel(place_ref, own_ref, other_ref, w_ref, hidden_ref, slope_ref, act_ref):
-        x = jnp.concatenate([own_ref[:, :width], other_ref[:, :width]], axis=0)
+        x = jnp.concatenate([own_ref[...], other_ref[...]], axis=0)
 
         def body(start):
             gate = dot(x, w_ref[:, pl.ds(start, size)])
@@ -236,18 +243,18 @@
     return jnp.sum(jnp.where(named, extra.astype(F32), 0.0), axis=1, keepdims=True)
 
 
-def forward_down(place, hidden, w_down, x_own, x_other, extra):
+def forward_down(place, hidden, w_down, terms, c):
     experts = lax.axis_size("expert")
-    rows = x_own.shape[0]
+    rows = hidden[0].shape[0] // 2
     height, quarter = w_down.shape
-    width = x_own.shape[1] - extra
     size = step_of(quarter)
+    held = slice(c * rows, (c + 1) * rows)
 
     def kernel(place_ref, *refs):
         *hidden_refs, w_ref, own_ref, other_ref, out_own_ref, out_other_ref = refs
         left = jnp.concatenate([ref[...] for ref in hidden_refs], axis=1)
-        own = route_weight(own_ref[:, width:], place_ref, experts)
-        other = route_weight(other_ref[:, width:], place_ref, experts)
+        own = route_weight(own_ref[held, :], place_ref, experts)
+        other = route_weight(other_ref[held, :], place_ref, experts)
 
         def body(start):
             total = dot(left, w_ref[:, pl.ds(start, size)])
@@ -258,27 +265,27 @@
 
     return resident(
         kernel,
-        [*hidden, w_down, x_own, x_other],
+        [*hidden, w_down, *terms],
         [((rows, quarter), BF16)] * 2,
         place,
         flops=4 * rows * height * quarter,
     )
 
 
-def backward_down(place, err_own, err_other, x_own, x_other, w_down, extra, halves):
+def backward_down(place, err_own, err_other, w_down, terms, c, halves):
     experts = lax.axis_size("expert")
     rows, quarter = err_own.shape
     height = w_down.shape[0]
     own = height // halves
-    width = x_own.shape[1] - extra
     size = step_of(own)
+    held = slice(c * rows, (c + 1) * rows)
 
     def kernel(place_ref, err_own_ref, err_other_ref, own_ref, other_ref, w_ref, grad_ref, *outs):
-        weight = route_weight(own_ref[:, width:], place_ref, experts)
+        weight = route_weight(own_ref[held, :], place_ref, experts)
         grad_ref[:rows, :] = (weight * err_own_ref[...].astype(F32)).astype(BF16)
-        weight = route_weight(other_ref[:, width:], place_ref, experts)
+        weight = route_weight(other_ref[held, :], place_ref, experts)
         grad_ref[rows:, :] = (weight * err_other_ref[...].astype(F32)).astype(BF16)
-        for d in range(halves):
+        for d in reversed(range(halves)):
 
             def body(start):
                 at = pl.multiple_of(d * own + start, size)
@@ -290,66 +297,46 @@
     shape = (2 * rows, own)
     return resident(
         kernel,
-        [err_own, err_other, x_own, x_other, w_down],
+        [err_own, err_other, *terms, w_down],
         [((2 * rows, quarter), BF16), (shape, F32)] + [(shape, BF16)] * (halves - 1),
         place,
         flops=4 * rows * height * quarter,
     )
 
 
-def backward_hidden(place, grad_own, arrived, slope, act, w_in, d, quarter):
+def backward_hidden(place, grad_own, arrived, slope, act, w_in, halves):
     both_rows, hidden = slope.shape
     rows = both_rows // 2
+    quarter = w_in.shape[0] // halves
     size = step_of(quarter)
     count = len(arrived)
 
     def kernel(place_ref, grad_own_ref, *refs):
         arrived_refs = refs[:count]
-        slope_ref, act_ref, w_ref, grad_ref, out_own_ref, out_other_ref = refs[count:]
+        slope_ref, act_ref, w_ref, grad_ref, *outs = refs[count:]
         grad_hidden = grad_own_ref[...]
         for ref in arrived_refs:
             grad_hidden += ref[...].astype(F32)
         grad_ref[:, :hidden] = (grad_hidden * slope_ref[...]).astype(BF16)
         grad_ref[:, hidden:] = (grad_hidden * act_ref[...]).astype(BF16)
-
-        def body(start):
-            at = pl.multiple_of(d * quarter + start, size)
-            part = dot_cols(grad_ref[...], w_ref[pl.ds(at, size), :]).astype(BF16)
-            out_own_ref[:, pl.ds(start, size)] = part[:rows]
-            out_other_ref[:, pl.ds(start, size)] = part[rows:]
-
-        tiles(quarter, body)
-
-    return resident(
+        for d in range(halves):
+
+            def body(start):
+                at = pl.multiple_of((place_ref[1] ^ d) * quarter + start, size)
+                part = dot_cols(grad_ref[...], w_ref[pl.ds(at, size), :]).astype(BF16)
+                outs[2 * d][:, pl.ds(start, size)] = part[:rows]
+                outs[2 * d + 1][:, pl.ds(start, size)] = part[rows:]
+
+            tiles(quarter, body)
+
+    grad, *parts = resident(
         kernel,
         [grad_own, *arrived, slope, act, w_in],
-        [((both_rows, 2 * hidden), BF16)] + [((rows, quarter), BF16)] * 2,
+        [((both_rows, 2 * hidden), BF16)] + [((rows, quarter), BF16)] * (2 * halves),
         place,
-        flops=4 * both_rows * hidden * quarter,
-    )
-
-
-def row_part(place, grad_in, w_in, d, quarter):
-    both_rows, both = grad_in.shape
-    rows = both_rows // 2
-    size = step_of(quarter)
-
-    def kernel(place_ref, grad_ref, w_ref, out_own_ref, out_other_ref):
-        def body(start):
-            at = pl.multiple_of(d * quarter + start, size)
-            part = dot_cols(grad_ref[...], w_ref[pl.ds(at, size), :]).astype(BF16)
-            out_own_ref[:, pl.ds(start, size)] = part[:rows]
-            out_other_ref[:, pl.ds(start, size)] = part[rows:]
-
-        tiles(quarter, body)
-
-    return resident(
-        kernel,
-        [grad_in, w_in],
-        [((rows, quarter), BF16)] * 2,
-        place,
-        flops=2 * both_rows * both * quarter,
-    )
+        flops=4 * both_rows * hidden * quarter * halves,
+    )
+    return grad, parts
 
 
 def ends(grad, codes):
@@ -422,24 +409,25 @@
     )[0]
 
 
-def ranges_in(place, x, grads, codes, groups, halves, d, found):
+def ranges_in(place, x, grads, codes, groups, part, parts, found):
     _, _, width, hidden = codes.shape
     size = width // groups
-    held = groups // halves
+    held = groups // parts
     per = next(p for p in (4, 2, 1) if held % p == 0)
     rows = per * size
     blocks = held // per
+    flat = [array for pair in x for array in pair]
     chunks = len(grads)
     tokens, both = grads[0].shape
+    wide = 256 if hidden % 256 == 0 else hidden
 
     def kernel(place_ref, *refs):
-        x_refs = refs[: 2 * chunks]
-        grad_refs = refs[2 * chunks : 3 * chunks]
-        code_ref, out_ref, right_ref = refs[3 * chunks], refs[-2], refs[-1]
-        step = pl.program_id(0)
-        base = step * per
-
-        @pl.when(step == 0)
+        x_refs = refs[: len(flat)]
+        grad_refs = refs[len(flat) : len(flat) + chunks]
+        code_ref, out_ref, right_ref = refs[len(flat) + chunks], refs[-2], refs[-1]
+        base = pl.program_id(0) * per
+
+        @pl.when(pl.program_id(0) == 0)
         def _():
             for c in range(chunks):
                 right_ref[c * tokens : (c + 1) * tokens, :] = grad_refs[c][...]
@@ -458,43 +446,29 @@
             out_ref[2 * k + 1, pl.ds(base + g, 1), cols] = high
 
         left = jnp.concatenate([ref[...] for ref in x_refs], axis=0)
-        wide = 256 if hidden % 256 == 0 else hidden
         range_tile(left, right_ref, size, wide, codes_at, store)
 
     shape = (4, groups, hidden)
-    flat = [part for pair in x for part in pair]
     return call(
         kernel,
         (blocks,),
-        [(part, (part.shape[0], rows), lambda i, p: (0, d * blocks + i)) for part in flat]
+        [(a, (a.shape[0], rows), lambda i, p: (0, part * blocks + i)) for a in flat]
         + [(grad, pltpu.VMEM, None) for grad in grads]
-        + [
-            (
-                codes,
-                (1, 2, rows, hidden),
-                lambda i, p: (0, 0, (p[1] ^ d) * blocks + i, 0),
-            )
-        ],
-        [(shape, F32, (4, held, hidden), lambda i, p: (0, p[1] ^ d, 0))],
+        + [(codes, (1, 2, rows, hidden), lambda i, p: (0, 0, part * blocks + i, 0))],
+        [(shape, F32, (4, held, hidden), lambda i, p: (0, part, 0))],
         place,
         scratch=[pltpu.VMEM((chunks * tokens, both), BF16)],
         mib=20,
-        flops=2 * sum(g.size for g in grads) * (width // halves),
+        flops=2 * sum(grad.size for grad in grads) * (width // parts),
         reuse=found,
     )[0]
 
 
-def prepare(place, tokens, routes, route_scores, extra):
+def prepare(place, routes, route_scores, extra):
     experts = lax.axis_size("expert")
-    halves = lax.axis_size("half")
-    rows, width = tokens.shape
-    quarter = width // halves
-    top_count = routes.shape[1]
-
-    def kernel(place_ref, token_ref, route_ref, score_ref, out_ref):
-        for d in range(halves):
-            start = pl.multiple_of((place_ref[1] ^ d) * quarter, 128)
-            out_ref[:, d * quarter : (d + 1) * quarter] = token_ref[:, pl.ds(start, quarter)]
+    rows, top_count = routes.shape
+
+    def kernel(place_ref, route_ref, score_ref, out_ref):
         scores = score_ref[...]
         weights = scores / jnp.sum(scores, axis=1, keepdims=True)
         names = route_ref[...]
@@ -508,15 +482,9 @@
         middle = (table - top).astype(BF16).astype(F32)
         bottom = table - top - middle
         terms = jnp.where(third == 0, top, jnp.where(third == 1, middle, bottom))
-        out_ref[:, width:] = terms.astype(BF16)
-
-    return call(
-        kernel,
-        (1,),
-        [(a, a.shape, whole2) for a in (tokens, routes, route_scores)],
-        [((rows, width + extra), BF16, (rows, width + extra), whole2)],
-        place,
-    )[0]
+        out_ref[...] = terms.astype(BF16)
+
+    return resident(kernel, [routes, route_scores], [((rows, extra), BF16)], place)[0]
 
 
 def local(
@@ -528,94 +496,125 @@
     quarter = target.shape[1]
     parts = range(halves)
     chunks = (0, 1)
+
+    near_own = swap(tokens, "expert", 4)
+    across = [swap(tokens, "expert", 2)]
+    far = join(gather_far(tokens)[1:])
+    w_in = dequant(place, in_codes[0], in_low[0], in_high[0])
+    near_own = tie(near_own, w_in)
+    far = tie(far, w_in, across[0])
+    near_far = swap(far, "expert", 4)
+    across += [swap(near_own, "expert", 2), swap(far, "expert", 2)]
+    w_down = dequant(place, down_codes, tie(down_low, far), down_high, halves)
     extra = -(-3 * experts // 128) * 128
-
-    mine = prepare(place, tokens, routes, route_scores, extra)
-    near_own = swap(mine, "expert", 4)
-    across = [swap(mine, "expert", 2)]
-    far = join(gather_far(mine)[1:])
-    w_in = dequant(place, in_codes[0], in_low[0], in_high[0], halves)
-    far = tie(far, w_in)
-    near_far = swap(far, "expert", 4)
-    w_down = dequant(place, down_codes, tie(down_low, w_in), down_high, halves)
-    near_far = tie(near_far, w_down)
-    first = jnp.concatenate([mine, far, near_own, near_far], axis=0)
-    across += [swap(part, "expert", 2) for part in (far, near_own, near_far)]
-    x = [(first, swap(first, "expert", 1))]
+    terms = join(gather_far(prepare(place, tie(routes, w_in), route_scores, extra)))
+    near_far = tie(near_far, w_down, terms, across[1])
+    near_terms = swap(terms, "expert", 4)
+    across.append(swap(near_far, "expert", 2))
+    first = pack(place, [tokens, far, near_own, near_far])
+    x = [(first, tie(swap(first, "expert", 1), across[2]))]
 
     hidden, slope, act = [], [], []
     for c in chunks:
         if c == 1:
-            across[3] = tie(across[3], hidden[0][0])
-            second = jnp.concatenate(across, axis=0)
+            across[3] = tie(across[3], hidden[0][0], near_terms)
+            second = pack(place, [across[i] for i in (0, 2, 1, 3)])
             x.append((second, swap(second, "expert", 1)))
         own, chunk_slope, chunk_act = forward_in(place, *x[c], w_in)
         hidden.append([own] + [swap(own, "half", d) for d in parts if d])
         slope.append(chunk_slope)
         act.append(chunk_act)
+    terms = jnp.concatenate([terms, near_terms], axis=0)
+    terms = jnp.concatenate([terms, swap(terms, "expert", 2)], axis=0)
+    terms = (terms, swap(terms, "expert", 1))
 
     sums = []
     for c in chunks:
         if c == 1:
             hidden[1][1:] = [tie(part, sums[0][0]) for part in hidden[1][1:]]
-        out_own, out_other = forward_down(place, hidden[c], w_down, *x[c], extra)
+        out_own, out_other = forward_down(place, hidden[c], w_down, terms, c)
         sums.append([out_own, swap(out_other, "expert", 1)])
     mixed = scatter_rows(sums[0], sums[1])
     error = (mixed - target.astype(F32)).astype(BF16)
 
     kept = join(gather_far(error))
     near = swap(kept, "expert", 4)
-    across = [swap(kept, "expert", 2), swap(near, "expert", 2)]
-    first = jnp.concatenate([kept, near], axis=0)
+    across = [swap(kept, "expert", 2)]
+    near = tie(near, across[0])
+    across.append(swap(near, "expert", 2))
+    first = pack(place, [kept, near])
     errors = [(first, swap(first, "expert", 1))]
     grads, grad_own, arrived = [], [], []
     for c in chunks:
         if c == 1:
-            across[1] = tie(across[1], grads[0])
-            second = jnp.concatenate(across, axis=0)
+            second = pack(place, [across[0], tie(across[1], grads[0])])
             errors.append((second, swap(second, "expert", 1)))
-        grad, own, *others = backward_down(place, *errors[c], *x[c], w_down, extra, halves)
+        grad, own, *others = backward_down(place, *errors[c], w_down, terms, c, halves)
         grads.append(grad)
         grad_own.append(own)
         arrived.append([swap(other, "half", d + 1) for d, other in enumerate(others)])
 
-    grad_in, sums = [], [[], []]
-    last = halves - 1
-
-    def spread(c, d, own, other):
-        rows = own.shape[0] // 2
-        cuts = [slice(rows, 2 * rows), slice(0, rows)] if c else [slice(0, 2 * rows)]
-        pieces = [add([own[cut], other[cut]]).astype(BF16) for cut in cuts]
-        if c:
-            pieces = [tie(piece, sums[0][-1]) for piece in pieces] if d == last else pieces
-        sent = [swap(piece, "half", d) for piece in pieces]
-        sums[c].append(sent if c else sent[0])
-        return pieces
-
+    grad_in, kinds = [], []
     arrived[0] = [tie(part, grads[1]) for part in arrived[0]]
     for c in chunks:
         if c == 1:
-            arrived[1] = [tie(part, *pieces) for part in arrived[1]]
-        both, own, other = backward_hidden(
-            place, grad_own[c], arrived[c], slope[c], act[c], w_in, last, quarter
+            arrived[1] = [tie(part, grad_in[0]) for part in arrived[1]]
+        grad, found = backward_hidden(
+            place, grad_own[c], arrived[c], slope[c], act[c], w_in, halves
         )
-        grad_in.append(both)
-        pieces = spread(c, last, own, swap(other, "expert", 1))
-    for d in range(last - 1, -1, -1):
-        for c in chunks:
-            own, other = row_part(place, grad_in[c], w_in, d, quarter)
-            other = swap(other, "expert", 1)
-            if d:
-                spread(c, d, own, other)
-            else:
-                sums[c] += [own, other]
-    grad_tokens = scatter_rows(*sums)
+        grad_in.append(grad)
+        kinds.append(found)
+    kinds[0] = [tie(part, grad_in[1]) for part in kinds[0]]
+    lower, upper = slice(0, first.shape[0] // 2), slice(first.shape[0] // 2, first.shape[0])
+    keep, go = [
+        [[found[2 * d], swap(found[2 * d + 1], "expert", 1)] for d in parts] for found in kinds
+    ]
+    stay, leave = keep[0], go[0]
+    outer = [(d, keep[d]) for d in parts if d]
+    crossed = [
+        (
+            swap(add([part[upper] for part in go[d]]).astype(BF16), "half", d),
+            swap(add([part[lower] for part in go[d]]).astype(BF16), "expert", 2),
+        )
+        for d in parts
+        if d
+    ]
+    by_half = [pair[0] for pair in crossed]
+    across_upper = swap(
+        add([part[upper] for part in leave] + by_half).astype(BF16), "expert", 2
+    )
+    arrived_upper = [
+        swap(tie(add([part[upper] for part in keep]).astype(BF16), *by_half), "half", d)
+        for d, keep in outer
+    ]
+    near = swap(
+        add([part[upper] for part in stay] + arrived_upper + [across_upper]).astype(BF16),
+        "expert",
+        4,
+    )
+    across_lower = swap(
+        tie(add([part[lower] for part in leave]).astype(BF16), across_upper), "expert", 2
+    )
+    arrived_lower = [
+        swap(
+            tie(
+                add([part[lower] for part in keep] + [pair[1]]).astype(BF16), *arrived_upper
+            ),
+            "half",
+            d,
+        )
+        for (d, keep), pair in zip(outer, crossed)
+    ]
+    grad_tokens = scatter_far(
+        [part[lower] for part in stay] + arrived_lower + [across_lower, near]
+    )
 
     grads = [tie(grad, *grad_in) for grad in grads]
     down_grad = ranges_down(place, hidden, grads, down_codes, down_low.shape[1], halves)
     in_grad = None
-    for d in parts:
-        in_grad = ranges_in(place, x, grad_in, in_codes, in_low.shape[2], halves, d, in_grad)
+    pieces = 2
+    for part in range(pieces):
+        in_grad = ranges_in(place, x, grad_in, in_codes, in_low.shape[2], part, pieces, in_grad)
     return (grad_tokens.astype(BF16), in_grad[None], down_grad[None])
 
 

time: 208 us -> 192 us (0.923)
  waiting for transfers between devices: 95.8 us -> 70.4 us
  starting transfers between devices: 31.2 us -> 37.8 us
  local copies, waits for them, and re-layouts: 11.9 us -> 14.9 us
    ppermute x36 -> x41, waiting for transfers between devices: 95.8 us -> 70.4 us  [swap(): return lax.ppermute(array, axis, [(i, i ^ distance) for i in range(size)])]
    ppermute x36 -> x41, starting transfers between devices: 31.2 us -> 37.8 us  [swap(): return lax.ppermute(array, axis, [(i, i ^ distance) for i in range(size)])]
    unnamed x40 -> x37, local copies, waits for them, and re-layouts: 11.8 us -> 14.8 us
    pallas_call x16 -> x18, Pallas kernels: 66.1 us -> 66.1 us  [call(): pl.pallas_call(kernel, grid_spec=pltpu.PrefetchScalarGridSpec(num_scalar_...]
  transfers between devices with their start and end apart: 36 -> 41, of which waited for: 22 -> 23; matrix products, arithmetic and copies ran while one was open for 1% -> 1% of each run, Pallas kernels for 26% -> 27%
where the time goes in v4:
time: 192 us
  waiting for transfers between devices  70.4 us (37%)
  Pallas kernels  66.1 us (34%)
  starting transfers between devices  37.8 us (20%)
  local copies, waits for them, and re-layouts  14.9 us (8%)
  other arithmetic  1.96 us (1%)
    ppermute x41, waiting for transfers between devices, swap(): return lax.ppermute(array, axis, [(i, i ^ distance) for i in range(size)])  70.4 us
    pallas_call x18, Pallas kernels, call(): pl.pallas_call(kernel, grid_spec=pltpu.PrefetchScalarGridSpec(num_scalar_...  66.1 us
    ppermute x41, starting transfers between devices, swap(): return lax.ppermute(array, axis, [(i, i ^ distance) for i in range(size)])  37.8 us
    unnamed x37, local copies, waits for them, and re-layouts  14.8 us
  transfers between devices with their start and end apart: 41, of which 23 were waited for; matrix products, arithmetic and copies ran while one was open for 1% of the time, Pallas kernels for 27%

profile of v4, /device:TPU:0, one launch (start us, length us, event | category | flops | bytes accessed | tf_op | source)
XLA Modules:
  0.0 192.2 jit_solution(12634693687026729406)
XLA Ops:
  0.6 3.1 %collective-permute-start.2 = (bf16[32,4096]{1,0:T(8,128)(2,1)}, bf16[32,4096]{1,0:T(8,128)(2,1)S(1)}, u32[]{:S(2)}, u32[]{:S(2)}) collective-permute-start(bf16[32,4096]{1,0:T(8,128)(2,1)} %refs_0_.1), channel_id=1, source_target_pairs={{0,8},{2,10},{4,12},{6,14},{8,0},{10,2},{12,4},{14,6},{16,24},{18,... | collective-permute-start | bytes 786440 | tf_op jit(solution)/shard_map/ppermute | solution.py:17
  3.7 1.5 collective-permute-start.1
  5.2 2.6 %collective-permute-start = (bf16[32,4096]{1,0:T(8,128)(2,1)}, bf16[32,4096]{1,0:T(8,128)(2,1)S(1)}, u32[]{:S(2)}, u32[]{:S(2)}) collective-permute-start(bf16[32,4096]{1,0:T(8,128)(2,1)} %refs_0_.1), channel_id=1, source_target_pairs={{0,16},{2,18},{4,20},{6,22},{8,24},{10,26},{12,28},{14,30},{16,0},... | collective-permute-start | bytes 786440 | tf_op jit(solution)/shard_map/ppermute | solution.py:17
  7.9 4.6 %copy-done.2 = bf16[1,2,4096,768]{3,2,1,0:T(8,128)(2,1)S(1)} copy-done((bf16[1,2,4096,768]{3,2,1,0:T(8,128)(2,1)S(1)}, bf16[1,2,4096,768]{3,2,1,0:T(8,128)(2,1)}, u32[]{:S(2)}) %copy-start.2) | copy-done | bytes 12582936
  12.5 0.9 copy-done.5
  13.4 0.9 copy-done.6
  14.3 3.7 %shard_map.121.w_ref.refs_3_ = bf16[4096,1536]{1,0:T(8,128)(2,1)S(1)} custom-call(s32[2]{0:T(128)S(1)} %pad_add_fusion.place_ref, bf16[2,4096,768]{2,1,0:T(8,128)(2,1)S(1)} %bitcast.7, f32[2,32,768]{2,1,0:T(8,128)S(1)} %bitcast.13, f32[2,32,768]{2,1,0:T(8,128)S(1)} %bitcast.14), custom_call_target="tpu_custom_call" | custom-call | bytes 25559040 | tf_op jit(solution)/shard_map/pallas_call | solution.py:106
  18.1 4.6 %copy-done = bf16[4096,1536]{1,0:T(8,128)(2,1)} copy-done((bf16[4096,1536]{1,0:T(8,128)(2,1)}, bf16[4096,1536]{1,0:T(8,128)(2,1)S(1)}, u32[]{:S(2)}) %copy-start) | copy-done | bytes 12582936
  23.9 0.8 shard_map.123
  24.8 4.6 %collective-permute-done.4 = bf16[32,128]{1,0:T(8,128)(2,1)S(1)} collective-permute-done((bf16[32,128]{1,0:T(8,128)(2,1)S(1)}, bf16[32,128]{1,0:T(8,128)(2,1)S(1)}, u32[]{:S(2)}, u32[]{:S(2)}) %collective-permute-start.4) | collective-permute-done | bytes 8224 | tf_op jit(solution)/shard_map/ppermute | solution.py:17
  29.4 2.8 %copy-done.3 = bf16[1,1536,2048]{2,1,0:T(8,128)(2,1)S(1)} copy-done((bf16[1,1536,2048]{2,1,0:T(8,128)(2,1)S(1)}, bf16[1,1536,2048]{2,1,0:T(8,128)(2,1)}, u32[]{:S(2)}) %copy-start.3) | copy-done | bytes 6291480
  32.2 2.3 %shard_map.122.refs_2_.w_ref = bf16[1536,2048]{1,0:T(8,128)(2,1)S(1)} custom-call(s32[2]{0:T(128)S(1)} %pad_add_fusion.place_ref, bf16[1,1536,2048]{2,1,0:T(8,128)(2,1)S(1)} %copy-done.3, f32[1,12,2048]{2,1,0:T(8,128)S(1)} %copy.14.low_ref, f32[1,12,2048]{2,1,0:T(8,128)S(1)} %copy.15.high_ref), custom_call_target="tpu_custom_call" | custom-call | bytes 12779520 | tf_op jit(solution)/shard_map/pallas_call | solution.py:106
  34.5 0.6 shard_map.124.own_ref.refs_0_
  35.2 1.4 collective-permute-start.7
  36.6 1.6 collective-permute-start.9
  38.8 5.6 %collective-permute-done.7.refs_1_ = bf16[32,4096]{1,0:T(8,128)(2,1)S(1)} collective-permute-done((bf16[32,4096]{1,0:T(8,128)(2,1)S(1)}, bf16[32,4096]{1,0:T(8,128)(2,1)S(1)}, u32[]{:S(2)}, u32[]{:S(2)}) %collective-permute-start.7) | collective-permute-done | bytes 262176 | tf_op jit(solution)/shard_map/ppermute | solution.py:17
  44.4 4.7 %shard_map.125 = (bf16[256,768]{1,0:T(8,128)(2,1)S(1)}, f32[256,768]{1,0:T(8,128)S(1)}, f32[256,768]{1,0:T(8,128)S(1)}) custom-call(s32[2]{0:T(128)S(1)} %pad_add_fusion.place_ref, bf16[128,4096]{1,0:T(8,128)(2,1)S(1)} %shard_map.124.own_ref.refs_0_, bf16[128,4096]{1,0:T(8,128)(2,1)S(1)} %collective-permute-done.6.other_ref.refs_1_, ...), custom_call_target="tpu_custom_call" | custom-call | flops 3221225472 | bytes 16646144 | tf_op jit(solution)/shard_map/pallas_call | solution.py:106
  49.5 0.6 shard_map.127.own_ref.refs_2_
  50.2 1.6 collective-permute-start.8
  51.8 1.1 collective-permute-done.14.other_ref.refs_3_
  52.9 4.7 %shard_map.128 = (bf16[256,768]{1,0:T(8,128)(2,1)S(1)}, f32[256,768]{1,0:T(8,128)S(1)}, f32[256,768]{1,0:T(8,128)S(1)}) custom-call(s32[2]{0:T(128)S(1)} %pad_add_fusion.place_ref, bf16[128,4096]{1,0:T(8,128)(2,1)S(1)} %shard_map.127.own_ref.refs_2_, bf16[128,4096]{1,0:T(8,128)(2,1)S(1)} %collective-permute-done.14.other_ref.refs_3_, ...), custom_call_target="tpu_custom_call" | custom-call | flops 3221225472 | bytes 16646144 | tf_op jit(solution)/shard_map/pallas_call | solution.py:106
  57.6 1.6 collective-permute-start.15
  59.2 1.4 collective-permute-start.10
  60.6 2.5 %collective-permute-done.10 = bf16[128,128]{1,0:T(8,128)(2,1)S(1)} collective-permute-done((bf16[128,128]{1,0:T(8,128)(2,1)S(1)}, bf16[128,128]{1,0:T(8,128)(2,1)S(1)}, u32[]{:S(2)}, u32[]{:S(2)}) %collective-permute-start.10) | collective-permute-done | bytes 32800 | tf_op jit(solution)/shard_map/ppermute | solution.py:17
  63.1 1.2 collective-permute-done.11.refs_4_.other_ref
  64.4 3.8 %shard_map.126 = (bf16[128,2048]{1,0:T(8,128)(2,1)S(1)}, bf16[128,2048]{1,0:T(8,128)(2,1)S(1)}) custom-call(s32[2]{0:T(128)S(1)} %pad_add_fusion.place_ref, bf16[256,768]{1,0:T(8,128)(2,1)S(1)} %get-tuple-element.57.refs_0_, bf16[256,768]{1,0:T(8,128)(2,1)S(1)} %collective-permute-done.8.refs_1_, bf16[1536,2048]{1,0:T(8,128)(2,1)S(1)} %shard_map.122.refs_2_.w_ref, ...), custom_call_target="tpu_custom_call" | custom-call | flops 1610612736 | bytes 8257536 | tf_op jit(solution)/shard_map/pallas_call | solution.py:106
  68.1 2.1 %collective-permute-done.15.refs_1_.refs_3_ = bf16[256,768]{1,0:T(8,128)(2,1)S(1)} collective-permute-done((bf16[256,768]{1,0:T(8,128)(2,1)S(1)}, bf16[256,768]{1,0:T(8,128)(2,1)S(1)}, u32[]{:S(2)}, u32[]{:S(2)}) %collective-permute-start.15) | collective-permute-done | bytes 393248 | tf_op jit(solution)/shard_map/ppermute | solution.py:17
  70.2 3.8 %shard_map.129 = (bf16[128,2048]{1,0:T(8,128)(2,1)S(1)}, bf16[128,2048]{1,0:T(8,128)(2,1)S(1)}) custom-call(s32[2]{0:T(128)S(1)} %pad_add_fusion.place_ref, bf16[256,768]{1,0:T(8,128)(2,1)S(1)} %get-tuple-element.61.refs_0_.refs_2_, bf16[256,768]{1,0:T(8,128)(2,1)S(1)} %collective-permute-done.15.refs_1_.refs_3_, ...), custom_call_target="tpu_custom_call" | custom-call | flops 1610612736 | bytes 8257536 | tf_op jit(solution)/shard_map/pallas_call | solution.py:106
  74.5 1.4 collective-permute-done.16
  76.1 1.5 collective-permute-start.17
  77.5 7.0 %collective-permute-done.17 = bf16[64,2048]{1,0:T(8,128)(2,1)S(1)} collective-permute-done((bf16[64,2048]{1,0:T(8,128)(2,1)S(1)}, bf16[64,2048]{1,0:T(8,128)(2,1)S(1)}, u32[]{:S(2)}, u32[]{:S(2)}) %collective-permute-start.17) | collective-permute-done | bytes 262176 | tf_op jit(solution)/shard_map/ppermute | solution.py:17
  84.6 1.5 collective-permute-start.19
  86.1 1.5 collective-permute-start.18
  87.6 4.6 %collective-permute-done.19 = bf16[64,2048]{1,0:T(8,128)(2,1)S(1)} collective-permute-done((bf16[64,2048]{1,0:T(8,128)(2,1)S(1)}, bf16[64,2048]{1,0:T(8,128)(2,1)S(1)}, u32[]{:S(2)}, u32[]{:S(2)}) %collective-permute-start.19) | collective-permute-done | bytes 262176 | tf_op jit(solution)/shard_map/ppermute | solution.py:17
  92.2 1.2 collective-permute-done.18
  93.4 1.1 collective-permute-start.20
  94.5 6.3 %collective-permute-done.20 = bf16[32,2048]{1,0:T(8,128)(2,1)S(1)} collective-permute-done((bf16[32,2048]{1,0:T(8,128)(2,1)S(1)}, bf16[32,2048]{1,0:T(8,128)(2,1)S(1)}, u32[]{:S(2)}, u32[]{:S(2)}) %collective-permute-start.20) | collective-permute-done | bytes 131104 | tf_op jit(solution)/shard_map/ppermute | solution.py:17
  100.9 7.4 %collective-permute-done.21 = bf16[32,2048]{1,0:T(8,128)(2,1)S(1)} collective-permute-done((bf16[32,2048]{1,0:T(8,128)(2,1)S(1)}, bf16[32,2048]{1,0:T(8,128)(2,1)S(1)}, u32[]{:S(2)}, u32[]{:S(2)}) %collective-permute-start.21) | collective-permute-done | bytes 131104 | tf_op jit(solution)/shard_map/ppermute | solution.py:17
  108.3 2.0 %collective-permute-start.23 = (bf16[64,2048]{1,0:T(8,128)(2,1)S(1)}, bf16[64,2048]{1,0:T(8,128)(2,1)S(1)}, u32[]{:S(2)}, u32[]{:S(2)}) collective-permute-start(bf16[64,2048]{1,0:T(8,128)(2,1)S(1)} %pad_maximum_fusion.refs_0_), channel_id=1, source_target_pairs={{0,4},{2,6},{4,0},{6,2},{8,12},{10,14},{12,8},{14,10},{16,20},{18,... | collective-permute-start | bytes 786440 | tf_op jit(solution)/shard_map/ppermute | solution.py:17
  110.3 4.5 %collective-permute-done.23.refs_0_ = bf16[64,2048]{1,0:T(8,128)(2,1)S(1)} collective-permute-done((bf16[64,2048]{1,0:T(8,128)(2,1)S(1)}, bf16[64,2048]{1,0:T(8,128)(2,1)S(1)}, u32[]{:S(2)}, u32[]{:S(2)}) %collective-permute-start.23) | collective-permute-done | bytes 262176 | tf_op jit(solution)/shard_map/ppermute | solution.py:17
  114.8 1.9 collective-permute-done.22.refs_1_
  116.7 0.6 shard_map.130.err_own_ref
  117.5 1.7 collective-permute-done.24.err_other_ref
  119.2 3.6 %shard_map.131 = (bf16[256,2048]{1,0:T(8,128)(2,1)S(1)}, f32[256,768]{1,0:T(8,128)S(1)}, bf16[256,768]{1,0:T(8,128)(2,1)S(1)}) custom-call(s32[2]{0:T(128)S(1)} %pad_add_fusion.place_ref, bf16[128,2048]{1,0:T(8,128)(2,1)S(1)} %shard_map.130.err_own_ref, bf16[128,2048]{1,0:T(8,128)(2,1)S(1)} %collective-permute-done.24.err_other_ref, ...), custom_call_target="tpu_custom_call" | custom-call | flops 1610612736 | bytes 9699328 | tf_op jit(solution)/shard_map/pallas_call | solution.py:106
  122.8 3.2 %collective-permute-done.26.refs_1_ = bf16[64,2048]{1,0:T(8,128)(2,1)S(1)} collective-permute-done((bf16[64,2048]{1,0:T(8,128)(2,1)S(1)}, bf16[64,2048]{1,0:T(8,128)(2,1)S(1)}, u32[]{:S(2)}, u32[]{:S(2)}) %collective-permute-start.26) | collective-permute-done | bytes 262176 | tf_op jit(solution)/shard_map/ppermute | solution.py:17
  126.0 0.6 shard_map.132.err_own_ref
  126.7 1.6 collective-permute-start.25
  128.6 3.6 %shard_map.133 = (bf16[256,2048]{1,0:T(8,128)(2,1)S(1)}, f32[256,768]{1,0:T(8,128)S(1)}, bf16[256,768]{1,0:T(8,128)(2,1)S(1)}) custom-call(s32[2]{0:T(128)S(1)} %pad_add_fusion.place_ref, bf16[128,2048]{1,0:T(8,128)(2,1)S(1)} %shard_map.132.err_own_ref, bf16[128,2048]{1,0:T(8,128)(2,1)S(1)} %collective-permute-done.27.err_other_ref, ...), custom_call_target="tpu_custom_call" | custom-call | flops 1610612736 | bytes 9699328 | tf_op jit(solution)/shard_map/pallas_call | solution.py:106
  132.2 1.6 collective-permute-start.28
  133.8 4.9 %collective-permute-done.25.refs_0_ = bf16[256,768]{1,0:T(8,128)(2,1)S(1)} collective-permute-done((bf16[256,768]{1,0:T(8,128)(2,1)S(1)}, bf16[256,768]{1,0:T(8,128)(2,1)S(1)}, u32[]{:S(2)}, u32[]{:S(2)}) %collective-permute-start.25) | collective-permute-done | bytes 393248 | tf_op jit(solution)/shard_map/ppermute | solution.py:17
  138.7 7.2 %shard_map.134 = (bf16[256,1536]{1,0:T(8,128)(2,1)S(1)}, bf16[128,2048]{1,0:T(8,128)(2,1)S(1)}, bf16[128,2048]{1,0:T(8,128)(2,1)S(1)}, bf16[128,2048]{1,0:T(8,128)(2,1)S(1)}, bf16[128,2048]{1,0:T(8,128)(2,1)S(1)}) custom-call(s32[2]{0:T(128)S(1)} %pad_add_fusion.place_ref, f32[256,768]{1,0:T(8,128)S(1)} %get-tuple-element.67.grad_own_ref, ...), custom_call_target="tpu_custom_call" | custom-call | flops 3221225472 | bytes 18219008 | tf_op jit(solution)/shard_map/pallas_call | solution.py:106
  145.9 0.8 collective-permute-done.28.refs_0_
  146.7 7.2 %shard_map.135 = (bf16[256,1536]{1,0:T(8,128)(2,1)S(1)}, bf16[128,2048]{1,0:T(8,128)(2,1)S(1)}, bf16[128,2048]{1,0:T(8,128)(2,1)S(1)}, bf16[128,2048]{1,0:T(8,128)(2,1)S(1)}, bf16[128,2048]{1,0:T(8,128)(2,1)S(1)}) custom-call(s32[2]{0:T(128)S(1)} %pad_add_fusion.place_ref, f32[256,768]{1,0:T(8,128)S(1)} %get-tuple-element.76.grad_own_ref, ...), custom_call_target="tpu_custom_call" | custom-call | flops 3221225472 | bytes 18219008 | tf_op jit(solution)/shard_map/pallas_call | solution.py:106
  154.4 1.4 collective-permute-done.31
  156.8 1.5 collective-permute-start.33
  158.3 6.0 %collective-permute-done.32 = bf16[64,2048]{1,0:T(8,128)(2,1)S(1)} collective-permute-done((bf16[64,2048]{1,0:T(8,128)(2,1)S(1)}, bf16[64,2048]{1,0:T(8,128)(2,1)S(1)}, u32[]{:S(2)}, u32[]{:S(2)}) %collective-permute-start.32) | collective-permute-done | bytes 262176 | tf_op jit(solution)/shard_map/ppermute | solution.py:17
  165.0 1.5 collective-permute-start.34
  166.8 1.8 collective-permute-start.37
  168.6 6.3 %shard_map.136.refs_7_ = f32[4,32,768]{2,1,0:T(8,128)} custom-call(s32[2]{0:T(128)S(1)} %pad_add_fusion.place_ref, bf16[128,4096]{1,0:T(8,128)(2,1)S(1)} %shard_map.124.own_ref.refs_0_, bf16[128,4096]{1,0:T(8,128)(2,1)S(1)} %collective-permute-done.6.other_ref.refs_1_, bf16[128,4096]{1,0:T(8,128)(2,1)S(1)} %shard_map.127.own_ref.refs_2_, ...), custom_call_target="tpu_custom_call" | custom-call | flops 3221225472 | bytes 18743296 | tf_op jit(solution)/shard_map/pallas_call | solution.py:106
  175.9 6.5 %shard_map.137 = f32[4,32,768]{2,1,0:T(8,128)} custom-call(s32[2]{0:T(128)S(1)} %pad_add_fusion.place_ref, bf16[128,4096]{1,0:T(8,128)(2,1)S(1)} %shard_map.124.own_ref.refs_0_, bf16[128,4096]{1,0:T(8,128)(2,1)S(1)} %collective-permute-done.6.other_ref.refs_1_, bf16[128,4096]{1,0:T(8,128)(2,1)S(1)} %shard_map.127.own_ref.refs_2_, ...), custom_call_target="tpu_custom_call", output_to_operand_aliasing={{}: (8, {})} | custom-call | flops 3221225472 | bytes 18743296 | tf_op jit(solution)/shard_map/pallas_call | solution.py:106
  182.5 2.5 %collective-permute-start.40 = (bf16[32,2048]{1,0:T(8,128)(2,1)S(1)}, bf16[32,2048]{1,0:T(8,128)(2,1)S(1)}, u32[]{:S(2)}, u32[]{:S(2)}) collective-permute-start(bf16[32,2048]{1,0:T(8,128)(2,1)S(1)} %add_convert_fusion.11), channel_id=1, source_target_pairs={{0,16},{2,18},{4,20},{6,22},{8,24},{10,26},{12,28},{14,30},{16,0},... | collective-permute-start | bytes 393224 | tf_op jit(solution)/shard_map/ppermute | solution.py:17
  185.0 5.6 %shard_map.138 = f32[2,12,2048]{2,1,0:T(8,128)S(1)} custom-call(s32[2]{0:T(128)S(1)} %pad_add_fusion.place_ref, bf16[256,768]{1,0:T(8,128)(2,1)S(1)} %get-tuple-element.57.refs_0_, bf16[256,768]{1,0:T(8,128)(2,1)S(1)} %collective-permute-done.8.refs_1_, bf16[256,768]{1,0:T(8,128)(2,1)S(1)} %get-tuple-element.61.refs_0_.refs_2_, ...), custom_call_target="tpu_custom_call" | custom-call | flops 3221225472 | bytes 10158080 | tf_op jit(solution)/shard_map/pallas_call | solution.py:106
  190.6 0.8 copy.18
  191.5 0.8 add_convert_fusion.10
  (92 shorter events, 7.8 us)
Async XLA Ops:
  0.6 22.0 %collective-permute-start.2 = (bf16[32,4096]{1,0:T(8,128)(2,1)}, bf16[32,4096]{1,0:T(8,128)(2,1)S(1)}, u32[]{:S(2)}, u32[]{:S(2)}) collective-permute-start(bf16[32,4096]{1,0:T(8,128)(2,1)} %refs_0_.1), channel_id=1, source_target_pairs={{0,8},{2,10},{4,12},{6,14},{8,0},{10,2},{12,4},{14,6},{16,24},{18,... | collective-permute-start | bytes 786440 | tf_op jit(solution)/shard_map/ppermute | solution.py:17
  3.7 18.9 %collective-permute-start.1 = (bf16[32,4096]{1,0:T(8,128)(2,1)}, bf16[32,4096]{1,0:T(8,128)(2,1)S(1)}, u32[]{:S(2)}, u32[]{:S(2)}) collective-permute-start(bf16[32,4096]{1,0:T(8,128)(2,1)} %refs_0_.1), channel_id=1, source_target_pairs={{0,4},{2,6},{4,0},{6,2},{8,12},{10,14},{12,8},{14,10},{16,20},{18,... | collective-permute-start | bytes 786440 | tf_op jit(solution)/shard_map/ppermute | solution.py:17
  5.2 17.5 %collective-permute-start = (bf16[32,4096]{1,0:T(8,128)(2,1)}, bf16[32,4096]{1,0:T(8,128)(2,1)S(1)}, u32[]{:S(2)}, u32[]{:S(2)}) collective-permute-start(bf16[32,4096]{1,0:T(8,128)(2,1)} %refs_0_.1), channel_id=1, source_target_pairs={{0,16},{2,18},{4,20},{6,22},{8,24},{10,26},{12,28},{14,30},{16,0},... | collective-permute-start | bytes 786440 | tf_op jit(solution)/shard_map/ppermute | solution.py:17
  7.9 4.6 %copy-start.2 = (bf16[1,2,4096,768]{3,2,1,0:T(8,128)(2,1)S(1)}, bf16[1,2,4096,768]{3,2,1,0:T(8,128)(2,1)}, u32[]{:S(2)}) copy-start(bf16[1,2,4096,768]{3,2,1,0:T(8,128)(2,1)} %refs_6_.4) | copy-start | bytes 37748740
  12.5 0.9 copy-start.5
  13.4 0.9 copy-start.6
  14.3 9.4 %copy-start.10 = (f32[32,8]{0,1:T(8,128)S(1)}, f32[32,8]{0,1:T(8,128)}, u32[]{:S(2)}) copy-start(f32[32,8]{0,1:T(8,128)} %param.13) | copy-start | bytes 3076
  14.3 9.5 %copy-start.11 = (s32[32,8]{0,1:T(8,128)S(1)}, s32[32,8]{0,1:T(8,128)}, u32[]{:S(2)}) copy-start(s32[32,8]{0,1:T(8,128)} %param.12) | copy-start | bytes 3076
  14.3 10.4 %copy-start.8 = (f32[1,12,2048]{2,0,1:T(1,128)S(1)}, f32[1,12,2048]{2,0,1:T(1,128)}, u32[]{:S(2)}) copy-start(f32[1,12,2048]{2,0,1:T(1,128)} %param.19) | copy-start | bytes 294916
  14.3 15.1 %copy-start.9 = (f32[1,12,2048]{2,0,1:T(1,128)S(1)}, f32[1,12,2048]{2,0,1:T(1,128)}, u32[]{:S(2)}) copy-start(f32[1,12,2048]{2,0,1:T(1,128)} %param.18) | copy-start | bytes 294916
  14.3 20.2 %copy-start.4 = (bf16[32,4096]{1,0:T(8,128)(2,1)S(1)}, bf16[32,4096]{1,0:T(8,128)(2,1)}, u32[]{:S(2)}) copy-start(bf16[32,4096]{1,0:T(8,128)(2,1)} %refs_0_.1) | copy-start | bytes 786436
  18.1 4.6 %copy-start = (bf16[4096,1536]{1,0:T(8,128)(2,1)}, bf16[4096,1536]{1,0:T(8,128)(2,1)S(1)}, u32[]{:S(2)}) copy-start(bf16[4096,1536]{1,0:T(8,128)(2,1)S(1)} %shard_map.121.w_ref.refs_3_) | copy-start | bytes 37748740
  22.7 11.8 %collective-permute-start.3 = (bf16[32,4096]{1,0:T(8,128)(2,1)S(1)}, bf16[32,4096]{1,0:T(8,128)(2,1)S(1)}, u32[]{:S(2)}, u32[]{:S(2)}) collective-permute-start(bf16[32,4096]{1,0:T(8,128)(2,1)S(1)} %collective-permute-done.refs_1_), channel_id=1, source_target_pairs={{0,8},{2,10},{4,12},{6,14},{8,0},{10,2},{12,4},{14,6},{16,24},{18,... | collective-permute-start | bytes 786440 | tf_op jit(solution)/shard_map/ppermute | solution.py:17
  23.2 11.3 %collective-permute-start.5 = (bf16[32,4096]{1,0:T(8,128)(2,1)S(1)}, bf16[32,4096]{1,0:T(8,128)(2,1)S(1)}, u32[]{:S(2)}, u32[]{:S(2)}) collective-permute-start(bf16[32,4096]{1,0:T(8,128)(2,1)S(1)} %collective-permute-done.2.refs_2_), channel_id=1, source_target_pairs={{0,4},{2,6},{4,0},{6,2},{8,12},{10,14},{12,8},{14,10},{16,20},{18,... | collective-permute-start | bytes 786440 | tf_op jit(solution)/shard_map/ppermute | solution.py:17
  23.9 20.5 %copy-start.1 = (bf16[4096,1536]{1,0:T(8,128)(2,1)S(1)}, bf16[4096,1536]{1,0:T(8,128)(2,1)}, u32[]{:S(2)}) copy-start(bf16[4096,1536]{1,0:T(8,128)(2,1)} %copy-done) | copy-start | bytes 37748740
  24.6 4.7 %collective-permute-start.4 = (bf16[32,128]{1,0:T(8,128)(2,1)S(1)}, bf16[32,128]{1,0:T(8,128)(2,1)S(1)}, u32[]{:S(2)}, u32[]{:S(2)}) collective-permute-start(bf16[32,128]{1,0:T(8,128)(2,1)S(1)} %shard_map.123), channel_id=1, source_target_pairs={{0,16},{2,18},{4,20},{6,22},{8,24},{10,26},{12,28},{14,30},{16,0},... | collective-permute-start | bytes 24584 | tf_op jit(solution)/shard_map/ppermute | solution.py:17
  29.4 2.8 %copy-start.3 = (bf16[1,1536,2048]{2,1,0:T(8,128)(2,1)S(1)}, bf16[1,1536,2048]{2,1,0:T(8,128)(2,1)}, u32[]{:S(2)}) copy-start(bf16[1,1536,2048]{2,1,0:T(8,128)(2,1)} %refs_6_.5) | copy-start | bytes 18874372
  35.1 9.3 %collective-permute-start.6 = (bf16[128,4096]{1,0:T(8,128)(2,1)S(1)}, bf16[128,4096]{1,0:T(8,128)(2,1)S(1)}, u32[]{:S(2)}, u32[]{:S(2)}) collective-permute-start(bf16[128,4096]{1,0:T(8,128)(2,1)S(1)} %shard_map.124.own_ref.refs_0_), channel_id=1, source_target_pairs={{0,2},{2,0},{4,6},{6,4},{8,10},{10,8},{12,14},{14,12},{16,18},{18,... | collective-permute-start | bytes 3145736 | tf_op jit(solution)/shard_map/ppermute | solution.py:17
  35.2 9.2 %collective-permute-start.7 = (bf16[32,4096]{1,0:T(8,128)(2,1)S(1)}, bf16[32,4096]{1,0:T(8,128)(2,1)S(1)}, u32[]{:S(2)}, u32[]{:S(2)}) collective-permute-start(bf16[32,4096]{1,0:T(8,128)(2,1)S(1)} %collective-permute-done.refs_1_), channel_id=1, source_target_pairs={{0,4},{2,6},{4,0},{6,2},{8,12},{10,14},{12,8},{14,10},{16,20},{18,... | collective-permute-start | bytes 786440 | tf_op jit(solution)/shard_map/ppermute | solution.py:17
  36.6 12.4 %collective-permute-start.9 = (bf16[64,128]{1,0:T(8,128)(2,1)S(1)}, bf16[64,128]{1,0:T(8,128)(2,1)S(1)}, u32[]{:S(2)}, u32[]{:S(2)}) collective-permute-start(bf16[64,128]{1,0:T(8,128)(2,1)S(1)} %pad_maximum_fusion.3), channel_id=1, source_target_pairs={{0,8},{2,10},{4,12},{6,14},{8,0},{10,2},{12,4},{14,6},{16,24},{18,... | collective-permute-start | bytes 49160 | tf_op jit(solution)/shard_map/ppermute | solution.py:17
  38.2 11.3 %collective-permute-start.13 = (bf16[32,4096]{1,0:T(8,128)(2,1)S(1)}, bf16[32,4096]{1,0:T(8,128)(2,1)S(1)}, u32[]{:S(2)}, u32[]{:S(2)}) collective-permute-start(bf16[32,4096]{1,0:T(8,128)(2,1)S(1)} %collective-permute-done.3.refs_3_), channel_id=1, source_target_pairs={{0,4},{2,6},{4,0},{6,2},{8,12},{10,14},{12,8},{14,10},{16,20},{18,... | collective-permute-start | bytes 786440 | tf_op jit(solution)/shard_map/ppermute | solution.py:17
  50.1 2.7 %collective-permute-start.14 = (bf16[128,4096]{1,0:T(8,128)(2,1)S(1)}, bf16[128,4096]{1,0:T(8,128)(2,1)S(1)}, u32[]{:S(2)}, u32[]{:S(2)}) collective-permute-start(bf16[128,4096]{1,0:T(8,128)(2,1)S(1)} %shard_map.127.own_ref.refs_2_), channel_id=1, source_target_pairs={{0,2},{2,0},{4,6},{6,4},{8,10},{10,8},{12,14},{14,12},{16,18},{18,... | collective-permute-start | bytes 3145736 | tf_op jit(solution)/shard_map/ppermute | solution.py:17
  50.2 14.1 %collective-permute-start.8 = (bf16[256,768]{1,0:T(8,128)(2,1)S(1)}, bf16[256,768]{1,0:T(8,128)(2,1)S(1)}, u32[]{:S(2)}, u32[]{:S(2)}) collective-permute-start(bf16[256,768]{1,0:T(8,128)(2,1)S(1)} %get-tuple-element.57.refs_0_), channel_id=1, source_target_pairs={{0,1},{1,0},{2,3},{3,2},{4,5},{5,4},{6,7},{7,6},{8,9},{9,8},{10,11... | collective-permute-start | bytes 1179656 | tf_op jit(solution)/shard_map/ppermute | solution.py:17
  57.6 43.2 %copy-start.7 = (bf16[32,2048]{1,0:T(8,128)(2,1)S(1)}, bf16[32,2048]{1,0:T(8,128)(2,1)}, u32[]{:S(2)}) copy-start(bf16[32,2048]{1,0:T(8,128)(2,1)} %param.11) | copy-start | bytes 393220
  57.6 12.6 %collective-permute-start.15 = (bf16[256,768]{1,0:T(8,128)(2,1)S(1)}, bf16[256,768]{1,0:T(8,128)(2,1)S(1)}, u32[]{:S(2)}, u32[]{:S(2)}) collective-permute-start(bf16[256,768]{1,0:T(8,128)(2,1)S(1)} %get-tuple-element.61.refs_0_.refs_2_), channel_id=1, source_target_pairs={{0,1},{1,0},{2,3},{3,2},{4,5},{5,4},{6,7},{7,6},{8,9},{9,8},{10,11... | collective-permute-start | bytes 1179656 | tf_op jit(solution)/shard_map/ppermute | solution.py:17
  59.2 3.9 %collective-permute-start.10 = (bf16[128,128]{1,0:T(8,128)(2,1)S(1)}, bf16[128,128]{1,0:T(8,128)(2,1)S(1)}, u32[]{:S(2)}, u32[]{:S(2)}) collective-permute-start(bf16[128,128]{1,0:T(8,128)(2,1)S(1)} %pad_maximum_fusion.2), channel_id=1, source_target_pairs={{0,4},{2,6},{4,0},{6,2},{8,12},{10,14},{12,8},{14,10},{16,20},{18,... | collective-permute-start | bytes 98312 | tf_op jit(solution)/shard_map/ppermute | solution.py:17
  63.1 1.3 collective-permute-start.11
  74.0 2.0 %collective-permute-start.16 = (bf16[128,2048]{1,0:T(8,128)(2,1)S(1)}, bf16[128,2048]{1,0:T(8,128)(2,1)S(1)}, u32[]{:S(2)}, u32[]{:S(2)}) collective-permute-start(bf16[128,2048]{1,0:T(8,128)(2,1)S(1)} %get-tuple-element.64), channel_id=1, source_target_pairs={{0,2},{2,0},{4,6},{6,4},{8,10},{10,8},{12,14},{14,12},{16,18},{18,... | collective-permute-start | bytes 1572872 | tf_op jit(solution)/shard_map/ppermute | solution.py:17
  74.0 10.4 %collective-permute-start.12 = (bf16[128,2048]{1,0:T(8,128)(2,1)S(1)}, bf16[128,2048]{1,0:T(8,128)(2,1)S(1)}, u32[]{:S(2)}, u32[]{:S(2)}) collective-permute-start(bf16[128,2048]{1,0:T(8,128)(2,1)S(1)} %get-tuple-element.59), channel_id=1, source_target_pairs={{0,2},{2,0},{4,6},{6,4},{8,10},{10,8},{12,14},{14,12},{16,18},{18,... | collective-permute-start | bytes 1572872 | tf_op jit(solution)/shard_map/ppermute | solution.py:17
  76.1 8.4 %collective-permute-start.17 = (bf16[64,2048]{1,0:T(8,128)(2,1)S(1)}, bf16[64,2048]{1,0:T(8,128)(2,1)S(1)}, u32[]{:S(2)}, u32[]{:S(2)}) collective-permute-start(bf16[64,2048]{1,0:T(8,128)(2,1)S(1)} %get-tuple-element.109), channel_id=1, source_target_pairs={{0,4},{2,6},{4,0},{6,2},{8,12},{10,14},{12,8},{14,10},{16,20},{18,... | collective-permute-start | bytes 786440 | tf_op jit(solution)/shard_map/ppermute | solution.py:17
  84.6 7.6 %collective-permute-start.19 = (bf16[64,2048]{1,0:T(8,128)(2,1)S(1)}, bf16[64,2048]{1,0:T(8,128)(2,1)S(1)}, u32[]{:S(2)}, u32[]{:S(2)}) collective-permute-start(bf16[64,2048]{1,0:T(8,128)(2,1)S(1)} %add_convert_fusion.7), channel_id=1, source_target_pairs={{0,8},{2,10},{4,12},{6,14},{8,0},{10,2},{12,4},{14,6},{16,24},{18,... | collective-permute-start | bytes 786440 | tf_op jit(solution)/shard_map/ppermute | solution.py:17
  86.1 7.2 %collective-permute-start.18 = (bf16[64,2048]{1,0:T(8,128)(2,1)S(1)}, bf16[64,2048]{1,0:T(8,128)(2,1)S(1)}, u32[]{:S(2)}, u32[]{:S(2)}) collective-permute-start(bf16[64,2048]{1,0:T(8,128)(2,1)S(1)} %get-tuple-element.65), channel_id=1, source_target_pairs={{0,4},{2,6},{4,0},{6,2},{8,12},{10,14},{12,8},{14,10},{16,20},{18,... | collective-permute-start | bytes 786440 | tf_op jit(solution)/shard_map/ppermute | solution.py:17
  93.4 7.3 %collective-permute-start.20 = (bf16[32,2048]{1,0:T(8,128)(2,1)S(1)}, bf16[32,2048]{1,0:T(8,128)(2,1)S(1)}, u32[]{:S(2)}, u32[]{:S(2)}) collective-permute-start(bf16[32,2048]{1,0:T(8,128)(2,1)S(1)} %add_convert_fusion.12), channel_id=1, source_target_pairs={{0,16},{2,18},{4,20},{6,22},{8,24},{10,26},{12,28},{14,30},{16,0},... | collective-permute-start | bytes 393224 | tf_op jit(solution)/shard_map/ppermute | solution.py:17
  100.9 7.4 %collective-permute-start.21 = (bf16[32,2048]{1,0:T(8,128)(2,1)S(1)}, bf16[32,2048]{1,0:T(8,128)(2,1)S(1)}, u32[]{:S(2)}, u32[]{:S(2)}) collective-permute-start(bf16[32,2048]{1,0:T(8,128)(2,1)S(1)} %subtract_convert_fusion), channel_id=1, source_target_pairs={{0,16},{2,18},{4,20},{6,22},{8,24},{10,26},{12,28},{14,30},{16,0},... | collective-permute-start | bytes 393224 | tf_op jit(solution)/shard_map/ppermute | solution.py:17
  108.3 6.4 %collective-permute-start.23 = (bf16[64,2048]{1,0:T(8,128)(2,1)S(1)}, bf16[64,2048]{1,0:T(8,128)(2,1)S(1)}, u32[]{:S(2)}, u32[]{:S(2)}) collective-permute-start(bf16[64,2048]{1,0:T(8,128)(2,1)S(1)} %pad_maximum_fusion.refs_0_), channel_id=1, source_target_pairs={{0,4},{2,6},{4,0},{6,2},{8,12},{10,14},{12,8},{14,10},{16,20},{18,... | collective-permute-start | bytes 786440 | tf_op jit(solution)/shard_map/ppermute | solution.py:17
  110.3 6.4 %collective-permute-start.22 = (bf16[64,2048]{1,0:T(8,128)(2,1)S(1)}, bf16[64,2048]{1,0:T(8,128)(2,1)S(1)}, u32[]{:S(2)}, u32[]{:S(2)}) collective-permute-start(bf16[64,2048]{1,0:T(8,128)(2,1)S(1)} %pad_maximum_fusion.refs_0_), channel_id=1, source_target_pairs={{0,8},{2,10},{4,12},{6,14},{8,0},{10,2},{12,4},{14,6},{16,24},{18,... | collective-permute-start | bytes 786440 | tf_op jit(solution)/shard_map/ppermute | solution.py:17
  117.2 2.0 %collective-permute-start.24 = (bf16[128,2048]{1,0:T(8,128)(2,1)S(1)}, bf16[128,2048]{1,0:T(8,128)(2,1)S(1)}, u32[]{:S(2)}, u32[]{:S(2)}) collective-permute-start(bf16[128,2048]{1,0:T(8,128)(2,1)S(1)} %shard_map.130.err_own_ref), channel_id=1, source_target_pairs={{0,2},{2,0},{4,6},{6,4},{8,10},{10,8},{12,14},{14,12},{16,18},{18,... | collective-permute-start | bytes 1572872 | tf_op jit(solution)/shard_map/ppermute | solution.py:17
  117.3 8.7 %collective-permute-start.26 = (bf16[64,2048]{1,0:T(8,128)(2,1)S(1)}, bf16[64,2048]{1,0:T(8,128)(2,1)S(1)}, u32[]{:S(2)}, u32[]{:S(2)}) collective-permute-start(bf16[64,2048]{1,0:T(8,128)(2,1)S(1)} %collective-permute-done.22.refs_1_), channel_id=1, source_target_pairs={{0,4},{2,6},{4,0},{6,2},{8,12},{10,14},{12,8},{14,10},{16,20},{18,... | collective-permute-start | bytes 786440 | tf_op jit(solution)/shard_map/ppermute | solution.py:17
  126.6 2.0 %collective-permute-start.27 = (bf16[128,2048]{1,0:T(8,128)(2,1)S(1)}, bf16[128,2048]{1,0:T(8,128)(2,1)S(1)}, u32[]{:S(2)}, u32[]{:S(2)}) collective-permute-start(bf16[128,2048]{1,0:T(8,128)(2,1)S(1)} %shard_map.132.err_own_ref), channel_id=1, source_target_pairs={{0,2},{2,0},{4,6},{6,4},{8,10},{10,8},{12,14},{14,12},{16,18},{18,... | collective-permute-start | bytes 1572872 | tf_op jit(solution)/shard_map/ppermute | solution.py:17
  126.7 12.0 %collective-permute-start.25 = (bf16[256,768]{1,0:T(8,128)(2,1)S(1)}, bf16[256,768]{1,0:T(8,128)(2,1)S(1)}, u32[]{:S(2)}, u32[]{:S(2)}) collective-permute-start(bf16[256,768]{1,0:T(8,128)(2,1)S(1)} %get-tuple-element.68), channel_id=1, source_target_pairs={{0,1},{1,0},{2,3},{3,2},{4,5},{5,4},{6,7},{7,6},{8,9},{9,8},{10,11... | collective-permute-start | bytes 1179656 | tf_op jit(solution)/shard_map/ppermute | solution.py:17
  132.2 14.4 %collective-permute-start.28 = (bf16[256,768]{1,0:T(8,128)(2,1)S(1)}, bf16[256,768]{1,0:T(8,128)(2,1)S(1)}, u32[]{:S(2)}, u32[]{:S(2)}) collective-permute-start(bf16[256,768]{1,0:T(8,128)(2,1)S(1)} %get-tuple-element.77), channel_id=1, source_target_pairs={{0,1},{1,0},{2,3},{3,2},{4,5},{5,4},{6,7},{7,6},{8,9},{9,8},{10,11... | collective-permute-start | bytes 1179656 | tf_op jit(solution)/shard_map/ppermute | solution.py:17
  138.7 29.9 %slice-start = ((s8[12582912]{0:T(1024)(128)(4,1)}), s8[4194304]{0:T(1024)(128)(4,1)S(1)}, s32[]{:S(2)}) async-start(s8[12582912]{0:T(1024)(128)(4,1)} %bitcast.8), calls=%async_computation | async-start | bytes 8388608
  138.7 29.9 %slice-start.1 = ((s8[12582912]{0:T(1024)(128)(4,1)}), s8[4194304]{0:T(1024)(128)(4,1)S(1)}, s32[]{:S(2)}) async-start(s8[12582912]{0:T(1024)(128)(4,1)} %bitcast.8), calls=%async_computation.1 | async-start | bytes 8388608
  146.7 21.9 %slice-start.2 = ((s8[12582912]{0:T(1024)(128)(4,1)}), s8[4194304]{0:T(1024)(128)(4,1)S(1)}, s32[]{:S(2)}) async-start(s8[12582912]{0:T(1024)(128)(4,1)} %bitcast.8), calls=%async_computation.2 | async-start | bytes 8388608
  153.9 2.0 %collective-permute-start.31 = (bf16[128,2048]{1,0:T(8,128)(2,1)S(1)}, bf16[128,2048]{1,0:T(8,128)(2,1)S(1)}, u32[]{:S(2)}, u32[]{:S(2)}) collective-permute-start(bf16[128,2048]{1,0:T(8,128)(2,1)S(1)} %get-tuple-element.91), channel_id=1, source_target_pairs={{0,2},{2,0},{4,6},{6,4},{8,10},{10,8},{12,14},{14,12},{16,18},{18,... | collective-permute-start | bytes 1572872 | tf_op jit(solution)/shard_map/ppermute | solution.py:17
  153.9 4.4 %collective-permute-start.30 = (bf16[128,2048]{1,0:T(8,128)(2,1)S(1)}, bf16[128,2048]{1,0:T(8,128)(2,1)S(1)}, u32[]{:S(2)}, u32[]{:S(2)}) collective-permute-start(bf16[128,2048]{1,0:T(8,128)(2,1)S(1)} %get-tuple-element.89), channel_id=1, source_target_pairs={{0,2},{2,0},{4,6},{6,4},{8,10},{10,8},{12,14},{14,12},{16,18},{18,... | collective-permute-start | bytes 1572872 | tf_op jit(solution)/shard_map/ppermute | solution.py:17
  156.0 8.4 %collective-permute-start.32 = (bf16[64,2048]{1,0:T(8,128)(2,1)S(1)}, bf16[64,2048]{1,0:T(8,128)(2,1)S(1)}, u32[]{:S(2)}, u32[]{:S(2)}) collective-permute-start(bf16[64,2048]{1,0:T(8,128)(2,1)S(1)} %get-tuple-element.104), channel_id=1, source_target_pairs={{0,4},{2,6},{4,0},{6,2},{8,12},{10,14},{12,8},{14,10},{16,20},{18,... | collective-permute-start | bytes 786440 | tf_op jit(solution)/shard_map/ppermute | solution.py:17
  156.3 10.3 %collective-permute-start.36 = (bf16[128,2048]{1,0:T(8,128)(2,1)S(1)}, bf16[128,2048]{1,0:T(8,128)(2,1)S(1)}, u32[]{:S(2)}, u32[]{:S(2)}) collective-permute-start(bf16[128,2048]{1,0:T(8,128)(2,1)S(1)} %get-tuple-element.95), channel_id=1, source_target_pairs={{0,2},{2,0},{4,6},{6,4},{8,10},{10,8},{12,14},{14,12},{16,18},{18,... | collective-permute-start | bytes 1572872 | tf_op jit(solution)/shard_map/ppermute | solution.py:17
  156.3 19.4 %collective-permute-start.29 = (bf16[128,2048]{1,0:T(8,128)(2,1)S(1)}, bf16[128,2048]{1,0:T(8,128)(2,1)S(1)}, u32[]{:S(2)}, u32[]{:S(2)}) collective-permute-start(bf16[128,2048]{1,0:T(8,128)(2,1)S(1)} %get-tuple-element.85), channel_id=1, source_target_pairs={{0,2},{2,0},{4,6},{6,4},{8,10},{10,8},{12,14},{14,12},{16,18},{18,... | collective-permute-start | bytes 1572872 | tf_op jit(solution)/shard_map/ppermute | solution.py:17
  156.8 8.2 %collective-permute-start.33 = (bf16[64,2048]{1,0:T(8,128)(2,1)S(1)}, bf16[64,2048]{1,0:T(8,128)(2,1)S(1)}, u32[]{:S(2)}, u32[]{:S(2)}) collective-permute-start(bf16[64,2048]{1,0:T(8,128)(2,1)S(1)} %get-tuple-element.105), channel_id=1, source_target_pairs={{0,1},{1,0},{2,3},{3,2},{4,5},{5,4},{6,7},{7,6},{8,9},{9,8},{10,11... | collective-permute-start | bytes 786440 | tf_op jit(solution)/shard_map/ppermute | solution.py:17
  165.0 9.9 %collective-permute-start.34 = (bf16[64,2048]{1,0:T(8,128)(2,1)S(1)}, bf16[64,2048]{1,0:T(8,128)(2,1)S(1)}, u32[]{:S(2)}, u32[]{:S(2)}) collective-permute-start(bf16[64,2048]{1,0:T(8,128)(2,1)S(1)} %get-tuple-element.92), channel_id=1, source_target_pairs={{0,1},{1,0},{2,3},{3,2},{4,5},{5,4},{6,7},{7,6},{8,9},{9,8},{10,11... | collective-permute-start | bytes 786440 | tf_op jit(solution)/shard_map/ppermute | solution.py:17
  166.8 8.6 %collective-permute-start.37 = (bf16[64,2048]{1,0:T(8,128)(2,1)S(1)}, bf16[64,2048]{1,0:T(8,128)(2,1)S(1)}, u32[]{:S(2)}, u32[]{:S(2)}) collective-permute-start(bf16[64,2048]{1,0:T(8,128)(2,1)S(1)} %get-tuple-element.107), channel_id=1, source_target_pairs={{0,4},{2,6},{4,0},{6,2},{8,12},{10,14},{12,8},{14,10},{16,20},{18,... | collective-permute-start | bytes 786440 | tf_op jit(solution)/shard_map/ppermute | solution.py:17
  174.9 10.1 %slice-start.3 = ((s8[6291456]{0:T(1024)(128)(4,1)}), s8[4194304]{0:T(1024)(128)(4,1)S(1)}, s32[]{:S(2)}) async-start(s8[6291456]{0:T(1024)(128)(4,1)} %bitcast.10), calls=%async_computation.3 | async-start | bytes 8388608
  174.9 7.5 %collective-permute-start.35 = (bf16[64,2048]{1,0:T(8,128)(2,1)S(1)}, bf16[64,2048]{1,0:T(8,128)(2,1)S(1)}, u32[]{:S(2)}, u32[]{:S(2)}) collective-permute-start(bf16[64,2048]{1,0:T(8,128)(2,1)S(1)} %get-tuple-element.93), channel_id=1, source_target_pairs={{0,1},{1,0},{2,3},{3,2},{4,5},{5,4},{6,7},{7,6},{8,9},{9,8},{10,11... | collective-permute-start | bytes 786440 | tf_op jit(solution)/shard_map/ppermute | solution.py:17
  175.4 7.0 %collective-permute-start.38 = (bf16[64,2048]{1,0:T(8,128)(2,1)S(1)}, bf16[64,2048]{1,0:T(8,128)(2,1)S(1)}, u32[]{:S(2)}, u32[]{:S(2)}) collective-permute-start(bf16[64,2048]{1,0:T(8,128)(2,1)S(1)} %get-tuple-element.96), channel_id=1, source_target_pairs={{0,4},{2,6},{4,0},{6,2},{8,12},{10,14},{12,8},{14,10},{16,20},{18,... | collective-permute-start | bytes 786440 | tf_op jit(solution)/shard_map/ppermute | solution.py:17
  175.8 9.2 %slice-start.4 = ((s8[6291456]{0:T(1024)(128)(4,1)}), s8[2097152]{0:T(1024)(128)(4,1)S(1)}, s32[]{:S(2)}) async-start(s8[6291456]{0:T(1024)(128)(4,1)} %bitcast.10), calls=%async_computation.4 | async-start | bytes 4194304
  175.8 6.6 %collective-permute-start.39 = (bf16[64,2048]{1,0:T(8,128)(2,1)S(1)}, bf16[64,2048]{1,0:T(8,128)(2,1)S(1)}, u32[]{:S(2)}, u32[]{:S(2)}) collective-permute-start(bf16[64,2048]{1,0:T(8,128)(2,1)S(1)} %add_convert_fusion), channel_id=1, source_target_pairs={{0,8},{2,10},{4,12},{6,14},{8,0},{10,2},{12,4},{14,6},{16,24},{18,... | collective-permute-start | bytes 786440 | tf_op jit(solution)/shard_map/ppermute | solution.py:17
  182.5 9.0 %collective-permute-start.40 = (bf16[32,2048]{1,0:T(8,128)(2,1)S(1)}, bf16[32,2048]{1,0:T(8,128)(2,1)S(1)}, u32[]{:S(2)}, u32[]{:S(2)}) collective-permute-start(bf16[32,2048]{1,0:T(8,128)(2,1)S(1)} %add_convert_fusion.11), channel_id=1, source_target_pairs={{0,16},{2,18},{4,20},{6,22},{8,24},{10,26},{12,28},{14,30},{16,0},... | collective-permute-start | bytes 393224 | tf_op jit(solution)/shard_map/ppermute | solution.py:17

commit v5 on v4

--- a/solution.py
+++ b/solution.py
@@ -57,12 +57,18 @@
     return add(terms)
 
 
-def scatter_rows(near, across):
+def scatter_rows(near, across, cuts):
     rows = near[0].shape[0] // 2
-    upper = swap(add([part[rows:] for part in across]).astype(BF16), "expert", 2)
-    sent = swap(add([part[rows:] for part in near] + [upper]).astype(BF16), "expert", 4)
-    lower = tie(add([part[:rows] for part in across]).astype(BF16), upper)
-    return scatter_far([part[:rows] for part in near] + [swap(lower, "expert", 2), sent])
+    upper = [swap(add([part[rows:, cut] for part in across]).astype(BF16), "expert", 2) for cut in cuts]
+    sent = [
+        swap(add([part[rows:, cut] for part in near] + [part_of]).astype(BF16), "expert", 4)
+        for cut, part_of in zip(cuts, upper)
+    ]
+    lower = swap(tie(add([part[:rows] for part in across]).astype(BF16), *upper), "expert", 2)
+    return [
+        scatter_far([part[:rows, cut] for part in near] + [lower[:, cut], part_of])
+        for cut, part_of in zip(cuts, sent)
+    ]
 
 
 def dot(left, right):
@@ -133,17 +139,13 @@
 
 
 def step_of(extent):
-    return 256 if extent % 256 == 0 else 128
+    return next(size for size in (512, 256, 128) if extent % size == 0)
 
 
 def tiles(extent, body):
     size = step_of(extent)
-
-    def step(i, carry):
-        body(pl.multiple_of(i * size, size))
-        return carry
-
-    lax.fori_loop(0, extent // size, step, 0)
+    for start in range(0, extent, size):
+        body(start)
 
 
 def whole2(*_):
@@ -159,15 +161,22 @@
 
 
 def pack(place, parts):
-    rows = sum(part.shape[0] for part in parts)
+    rows = sum(line[0].shape[0] for line in parts)
+    cols = sum(part.shape[1] for part in parts[0])
 
     def kernel(place_ref, *refs):
-        start = 0
-        for ref in refs[:-1]:
-            refs[-1][start : start + ref.shape[0], :] = ref[...]
-            start += ref.shape[0]
-
-    return resident(kernel, parts, [((rows, parts[0].shape[1]), parts[0].dtype)], place)[0]
+        refs, out_ref = list(refs[:-1]), refs[-1]
+        row = 0
+        for line in parts:
+            col = 0
+            for part in line:
+                height, width = part.shape
+                out_ref[row : row + height, col : col + width] = refs.pop(0)[...]
+                col += width
+            row += line[0].shape[0]
+
+    flat = [part for line in parts for part in line]
+    return resident(kernel, flat, [((rows, cols), parts[0][0].dtype)], place)[0]
 
 
 def dequant(place, codes, low, high, halves=1):
@@ -217,7 +226,7 @@
 
         def body(start):
             gate = dot(x, w_ref[:, pl.ds(start, size)])
-            up = dot(x, w_ref[:, pl.ds(pl.multiple_of(hidden + start, size), size)])
+            up = dot(x, w_ref[:, pl.ds(hidden + start, size)])
             sig = 1.0 / (1.0 + jnp.exp(-gate))
             act = gate * sig
             hidden_ref[:, pl.ds(start, size)] = (act * up).astype(BF16)
@@ -288,7 +297,7 @@
         for d in reversed(range(halves)):
 
             def body(start):
-                at = pl.multiple_of(d * own + start, size)
+                at = d * own + start
                 part = dot_cols(grad_ref[...], w_ref[pl.ds(at, size), :])
                 outs[d][:, pl.ds(start, size)] = part.astype(outs[d].dtype)
 
@@ -389,7 +398,7 @@
                     jnp.concatenate(left, axis=0),
                     right_ref,
                     size,
-                    step_of(quarter),
+                    256,
                     lambda cut, cols: code_ref[0, cut, cols],
                     store,
                 )
@@ -497,28 +506,28 @@
     parts = range(halves)
     chunks = (0, 1)
 
+    far = join(gather_far(tokens)[1:])
     near_own = swap(tokens, "expert", 4)
     across = [swap(tokens, "expert", 2)]
-    far = join(gather_far(tokens)[1:])
     w_in = dequant(place, in_codes[0], in_low[0], in_high[0])
-    near_own = tie(near_own, w_in)
-    far = tie(far, w_in, across[0])
+    w_down = dequant(place, down_codes, tie(down_low, w_in), down_high, halves)
+    far = tie(far, w_in, w_down, across[0])
     near_far = swap(far, "expert", 4)
-    across += [swap(near_own, "expert", 2), swap(far, "expert", 2)]
-    w_down = dequant(place, down_codes, tie(down_low, far), down_high, halves)
+    middle = pack(place, [[far], [near_own]])
+    across.append(swap(middle, "expert", 2))
     extra = -(-3 * experts // 128) * 128
-    terms = join(gather_far(prepare(place, tie(routes, w_in), route_scores, extra)))
-    near_far = tie(near_far, w_down, terms, across[1])
+    terms = join(gather_far(prepare(place, tie(routes, far), route_scores, extra)))
+    near_far = tie(near_far, across[1], terms)
+    across.append(swap(near_far, "expert", 2))
+    first = pack(place, [[tokens], [middle], [near_far]])
+    x = [(first, swap(first, "expert", 1))]
     near_terms = swap(terms, "expert", 4)
-    across.append(swap(near_far, "expert", 2))
-    first = pack(place, [tokens, far, near_own, near_far])
-    x = [(first, tie(swap(first, "expert", 1), across[2]))]
 
     hidden, slope, act = [], [], []
     for c in chunks:
         if c == 1:
-            across[3] = tie(across[3], hidden[0][0], near_terms)
-            second = pack(place, [across[i] for i in (0, 2, 1, 3)])
+            across[2] = tie(across[2], hidden[0][0], near_terms)
+            second = pack(place, [[part] for part in across])
             x.append((second, swap(second, "expert", 1)))
         own, chunk_slope, chunk_act = forward_in(place, *x[c], w_in)
         hidden.append([own] + [swap(own, "half", d) for d in parts if d])
@@ -534,20 +543,25 @@
             hidden[1][1:] = [tie(part, sums[0][0]) for part in hidden[1][1:]]
         out_own, out_other = forward_down(place, hidden[c], w_down, terms, c)
         sums.append([out_own, swap(out_other, "expert", 1)])
-    mixed = scatter_rows(sums[0], sums[1])
-    error = (mixed - target.astype(F32)).astype(BF16)
-
-    kept = join(gather_far(error))
-    near = swap(kept, "expert", 4)
-    across = [swap(kept, "expert", 2)]
-    near = tie(near, across[0])
-    across.append(swap(near, "expert", 2))
-    first = pack(place, [kept, near])
+    middle = quarter // 2
+    cuts = [slice(0, middle), slice(middle, quarter)]
+    mixed = scatter_rows(sums[0], sums[1], cuts)
+    error = [
+        (mixed[f] - target[:, cuts[f]].astype(F32)).astype(BF16) for f in range(len(cuts))
+    ]
+
+    kept = [gather_far(part) for part in error]
+    near = [swap(join(part), "expert", 4) for part in kept]
+    kept = pack(place, [list(line) for line in zip(*kept)])
+    across = swap(kept, "expert", 2)
+    near = [tie(part, across) for part in near]
+    near_across = [swap(part, "expert", 2) for part in near]
+    first = pack(place, [[kept], near])
     errors = [(first, swap(first, "expert", 1))]
     grads, grad_own, arrived = [], [], []
     for c in chunks:
         if c == 1:
-            second = pack(place, [across[0], tie(across[1], grads[0])])
+            second = pack(place, [[across], [tie(part, grads[0]) for part in near_across]])
             errors.append((second, swap(second, "expert", 1)))
         grad, own, *others = backward_down(place, *errors[c], w_down, terms, c, halves)
         grads.append(grad)

time: 192 us -> 191 us (level)
  Pallas kernels: 66.1 us -> 54.4 us
  starting transfers between devices: 37.8 us -> 44.1 us
  local copies, waits for them, and re-layouts: 14.9 us -> 20.2 us
    pallas_call x18 -> x20, Pallas kernels: 66.1 us -> 54.4 us  [call(): pl.pallas_call(kernel, grid_spec=pltpu.PrefetchScalarGridSpec(num_scalar_...]
    ppermute x41 -> x46, starting transfers between devices: 37.8 us -> 44.1 us  [swap(): return lax.ppermute(array, axis, [(i, i ^ distance) for i in range(size)])]
    unnamed x37 -> x43, local copies, waits for them, and re-layouts: 14.8 us -> 20.1 us
    ppermute x41 -> x46, waiting for transfers between devices: 70.4 us -> 69 us  [swap(): return lax.ppermute(array, axis, [(i, i ^ distance) for i in range(size)])]
  transfers between devices with their start and end apart: 41 -> 46, of which waited for: 23 -> 26; matrix products, arithmetic and copies ran while one was open for 1% -> 2% of each run, Pallas kernels for 27% -> 23%
where the time goes in v5:
time: 191 us
  waiting for transfers between devices  69 us (36%)
  Pallas kernels  54.4 us (28%)
  starting transfers between devices  44.1 us (23%)
  local copies, waits for them, and re-layouts  20.2 us (11%)
  other arithmetic  2.01 us (1%)
    ppermute x46, waiting for transfers between devices, swap(): return lax.ppermute(array, axis, [(i, i ^ distance) for i in range(size)])  69 us
    pallas_call x20, Pallas kernels, call(): pl.pallas_call(kernel, grid_spec=pltpu.PrefetchScalarGridSpec(num_scalar_...  54.4 us
    ppermute x46, starting transfers between devices, swap(): return lax.ppermute(array, axis, [(i, i ^ distance) for i in range(size)])  44.1 us
    unnamed x43, local copies, waits for them, and re-layouts  20.1 us
  transfers between devices with their start and end apart: 46, of which 26 were waited for; matrix products, arithmetic and copies ran while one was open for 2% of the time, Pallas kernels for 23%

profile of v5, /device:TPU:0, one launch (start us, length us, event | category | flops | bytes accessed | tf_op | source)
XLA Modules:
  0.0 190.7 jit_solution(15269837951629422149)
XLA Ops:
  0.6 3.0 %collective-permute-start.1 = (bf16[32,4096]{1,0:T(8,128)(2,1)}, bf16[32,4096]{1,0:T(8,128)(2,1)S(1)}, u32[]{:S(2)}, u32[]{:S(2)}) collective-permute-start(bf16[32,4096]{1,0:T(8,128)(2,1)} %refs_0_.1), channel_id=1, source_target_pairs={{0,4},{2,6},{4,0},{6,2},{8,12},{10,14},{12,8},{14,10},{16,20},{18,... | collective-permute-start | bytes 786440 | tf_op jit(solution)/shard_map/ppermute | solution.py:17
  3.6 2.6 %collective-permute-start = (bf16[32,4096]{1,0:T(8,128)(2,1)}, bf16[32,4096]{1,0:T(8,128)(2,1)S(1)}, u32[]{:S(2)}, u32[]{:S(2)}) collective-permute-start(bf16[32,4096]{1,0:T(8,128)(2,1)} %refs_0_.1), channel_id=1, source_target_pairs={{0,16},{2,18},{4,20},{6,22},{8,24},{10,26},{12,28},{14,30},{16,0},... | collective-permute-start | bytes 786440 | tf_op jit(solution)/shard_map/ppermute | solution.py:17
  6.2 1.6 collective-permute-start.2
  7.8 0.9 copy.15.high_ref
  8.8 4.6 %copy-done.4 = bf16[1,2,4096,768]{3,2,1,0:T(8,128)(2,1)S(1)} copy-done((bf16[1,2,4096,768]{3,2,1,0:T(8,128)(2,1)S(1)}, bf16[1,2,4096,768]{3,2,1,0:T(8,128)(2,1)}, u32[]{:S(2)}) %copy-start.4) | copy-done | bytes 12582936
  13.4 0.9 copy-done.7
  14.3 0.9 copy-done.8
  15.2 3.7 %shard_map.121.w_ref.refs_3_ = bf16[4096,1536]{1,0:T(8,128)(2,1)S(1)} custom-call(s32[2]{0:T(128)S(1)} %pad_add_fusion.place_ref, bf16[2,4096,768]{2,1,0:T(8,128)(2,1)S(1)} %bitcast.9, f32[2,32,768]{2,1,0:T(8,128)S(1)} %bitcast.15, f32[2,32,768]{2,1,0:T(8,128)S(1)} %bitcast.16), custom_call_target="tpu_custom_call" | custom-call | bytes 25559040 | tf_op jit(solution)/shard_map/pallas_call | solution.py:112
  19.0 4.6 %copy-done = bf16[4096,1536]{1,0:T(8,128)(2,1)} copy-done((bf16[4096,1536]{1,0:T(8,128)(2,1)}, bf16[4096,1536]{1,0:T(8,128)(2,1)S(1)}, u32[]{:S(2)}) %copy-start) | copy-done | bytes 12582936
  23.7 2.3 %shard_map.122.refs_2_.w_ref = bf16[1536,2048]{1,0:T(8,128)(2,1)S(1)} custom-call(s32[2]{0:T(128)S(1)} %pad_add_fusion.place_ref, bf16[1,1536,2048]{2,1,0:T(8,128)(2,1)S(1)} %copy-done.5, f32[1,12,2048]{2,1,0:T(8,128)S(1)} %copy.14.low_ref, f32[1,12,2048]{2,1,0:T(8,128)S(1)} %copy.15.high_ref), custom_call_target="tpu_custom_call" | custom-call | bytes 12779520 | tf_op jit(solution)/shard_map/pallas_call | solution.py:112
  25.9 2.6 %copy-done.3 = bf16[1536,2048]{1,0:T(8,128)(2,1)} copy-done((bf16[1536,2048]{1,0:T(8,128)(2,1)}, bf16[1536,2048]{1,0:T(8,128)(2,1)S(1)}, u32[]{:S(2)}) %copy-start.3) | copy-done | bytes 6291480
  31.2 4.6 %collective-permute-done.5 = bf16[32,128]{1,0:T(8,128)(2,1)S(1)} collective-permute-done((bf16[32,128]{1,0:T(8,128)(2,1)S(1)}, bf16[32,128]{1,0:T(8,128)(2,1)S(1)}, u32[]{:S(2)}, u32[]{:S(2)}) %collective-permute-start.5) | collective-permute-done | bytes 8224 | tf_op jit(solution)/shard_map/ppermute | solution.py:17
  35.8 1.0 collective-permute-done.3.refs_2_
  36.8 5.2 %collective-permute-done.4.refs_1_ = bf16[64,4096]{1,0:T(8,128)(2,1)S(1)} collective-permute-done((bf16[64,4096]{1,0:T(8,128)(2,1)S(1)}, bf16[64,4096]{1,0:T(8,128)(2,1)S(1)}, u32[]{:S(2)}, u32[]{:S(2)}) %collective-permute-start.4) | collective-permute-done | bytes 524320 | tf_op jit(solution)/shard_map/ppermute | solution.py:17
  43.7 1.6 collective-permute-done.6.other_ref.refs_1_
  45.3 4.6 %copy-done.1 = bf16[4096,1536]{1,0:T(8,128)(2,1)S(1)} copy-done((bf16[4096,1536]{1,0:T(8,128)(2,1)S(1)}, bf16[4096,1536]{1,0:T(8,128)(2,1)}, u32[]{:S(2)}) %copy-start.1) | copy-done | bytes 12582936
  49.9 4.1 %shard_map.126 = (bf16[256,768]{1,0:T(8,128)(2,1)S(1)}, f32[256,768]{1,0:T(8,128)S(1)}, f32[256,768]{1,0:T(8,128)S(1)}) custom-call(s32[2]{0:T(128)S(1)} %pad_add_fusion.place_ref, bf16[128,4096]{1,0:T(8,128)(2,1)S(1)} %shard_map.125.own_ref.refs_0_, bf16[128,4096]{1,0:T(8,128)(2,1)S(1)} %collective-permute-done.6.other_ref.refs_1_, ...), custom_call_target="tpu_custom_call" | custom-call | flops 3221225472 | bytes 16646144 | tf_op jit(solution)/shard_map/pallas_call | solution.py:112
  54.8 1.5 collective-permute-start.7
  56.4 1.0 collective-permute-done.13.other_ref.refs_3_
  57.4 4.1 %shard_map.129 = (bf16[256,768]{1,0:T(8,128)(2,1)S(1)}, f32[256,768]{1,0:T(8,128)S(1)}, f32[256,768]{1,0:T(8,128)S(1)}) custom-call(s32[2]{0:T(128)S(1)} %pad_add_fusion.place_ref, bf16[128,4096]{1,0:T(8,128)(2,1)S(1)} %shard_map.128.own_ref.refs_2_, bf16[128,4096]{1,0:T(8,128)(2,1)S(1)} %collective-permute-done.13.other_ref.refs_3_, ...), custom_call_target="tpu_custom_call" | custom-call | flops 3221225472 | bytes 16646144 | tf_op jit(solution)/shard_map/pallas_call | solution.py:112
  61.5 1.6 collective-permute-start.14
  63.6 3.4 %collective-permute-done.9 = bf16[128,128]{1,0:T(8,128)(2,1)S(1)} collective-permute-done((bf16[128,128]{1,0:T(8,128)(2,1)S(1)}, bf16[128,128]{1,0:T(8,128)(2,1)S(1)}, u32[]{:S(2)}, u32[]{:S(2)}) %collective-permute-start.9) | collective-permute-done | bytes 32800 | tf_op jit(solution)/shard_map/ppermute | solution.py:17
  67.0 1.2 collective-permute-done.10.refs_4_.other_ref
  68.3 2.3 %shard_map.127 = (bf16[128,2048]{1,0:T(8,128)(2,1)S(1)}, bf16[128,2048]{1,0:T(8,128)(2,1)S(1)}) custom-call(s32[2]{0:T(128)S(1)} %pad_add_fusion.place_ref, bf16[256,768]{1,0:T(8,128)(2,1)S(1)} %get-tuple-element.55.refs_0_, bf16[256,768]{1,0:T(8,128)(2,1)S(1)} %collective-permute-done.7.refs_1_, bf16[1536,2048]{1,0:T(8,128)(2,1)S(1)} %bitcast.8, ...), custom_call_target="tpu_custom_call" | custom-call | flops 1610612736 | bytes 8257536 | tf_op jit(solution)/shard_map/pallas_call | solution.py:112
  70.6 4.1 %collective-permute-done.14.refs_1_.refs_3_ = bf16[256,768]{1,0:T(8,128)(2,1)S(1)} collective-permute-done((bf16[256,768]{1,0:T(8,128)(2,1)S(1)}, bf16[256,768]{1,0:T(8,128)(2,1)S(1)}, u32[]{:S(2)}, u32[]{:S(2)}) %collective-permute-start.14) | collective-permute-done | bytes 393248 | tf_op jit(solution)/shard_map/ppermute | solution.py:17
  74.7 2.3 %shard_map.130 = (bf16[128,2048]{1,0:T(8,128)(2,1)S(1)}, bf16[128,2048]{1,0:T(8,128)(2,1)S(1)}) custom-call(s32[2]{0:T(128)S(1)} %pad_add_fusion.place_ref, bf16[256,768]{1,0:T(8,128)(2,1)S(1)} %get-tuple-element.59.refs_0_.refs_2_, bf16[256,768]{1,0:T(8,128)(2,1)S(1)} %collective-permute-done.14.refs_1_.refs_3_, bf16[1536,2048]{1,0:T(8,128)(2,1)S(1)} %bitcast.8, ...), custom_call_target="tpu_custom_call" | custom-call | flops 1610612736 | bytes 8257536 | tf_op jit(solution)/shard_map/pallas_call | solution.py:112
  77.6 1.4 collective-permute-done.15
  79.7 1.5 collective-permute-start.16
  81.2 4.3 %collective-permute-done.17 = bf16[64,1024]{1,0:T(8,128)(2,1)S(1)} collective-permute-done((bf16[64,1024]{1,0:T(8,128)(2,1)S(1)}, bf16[64,1024]{1,0:T(8,128)(2,1)S(1)}, u32[]{:S(2)}, u32[]{:S(2)}) %collective-permute-start.17) | collective-permute-done | bytes 131104 | tf_op jit(solution)/shard_map/ppermute | solution.py:17
  85.5 2.0 %collective-permute-done.16 = bf16[64,1024]{1,0:T(8,128)(2,1)S(1)} collective-permute-done((bf16[64,1024]{1,0:T(8,128)(2,1)S(1)}, bf16[64,1024]{1,0:T(8,128)(2,1)S(1)}, u32[]{:S(2)}, u32[]{:S(2)}) %collective-permute-start.16) | collective-permute-done | bytes 131104 | tf_op jit(solution)/shard_map/ppermute | solution.py:17
  88.1 1.0 collective-permute-start.21
  89.1 1.1 collective-permute-start.19
  90.2 3.8 %collective-permute-done.21 = bf16[64,1024]{1,0:T(8,128)(2,1)S(1)} collective-permute-done((bf16[64,1024]{1,0:T(8,128)(2,1)S(1)}, bf16[64,1024]{1,0:T(8,128)(2,1)S(1)}, u32[]{:S(2)}, u32[]{:S(2)}) %collective-permute-start.21) | collective-permute-done | bytes 131104 | tf_op jit(solution)/shard_map/ppermute | solution.py:17
  94.0 1.4 collective-permute-done.19
  95.9 2.6 %collective-permute-start.20 = (bf16[32,1024]{1,0:T(8,128)(2,1)S(1)}, bf16[32,1024]{1,0:T(8,128)(2,1)S(1)}, u32[]{:S(2)}, u32[]{:S(2)}) collective-permute-start(bf16[32,1024]{1,0:T(8,128)(2,1)S(1)} %get-tuple-element.105), channel_id=1, source_target_pairs={{0,16},{2,18},{4,20},{6,22},{8,24},{10,26},{12,28},{14,30},{16,0},... | collective-permute-start | bytes 196616 | tf_op jit(solution)/shard_map/ppermute | solution.py:17
  98.5 3.6 %collective-permute-done.22 = bf16[32,1024]{1,0:T(8,128)(2,1)S(1)} collective-permute-done((bf16[32,1024]{1,0:T(8,128)(2,1)S(1)}, bf16[32,1024]{1,0:T(8,128)(2,1)S(1)}, u32[]{:S(2)}, u32[]{:S(2)}) %collective-permute-start.22) | collective-permute-done | bytes 65568 | tf_op jit(solution)/shard_map/ppermute | solution.py:17
  103.0 1.0 collective-permute-start.24
  104.0 2.0 %collective-permute-start.23 = (bf16[32,1024]{1,0:T(8,128)(2,1)S(1)}, bf16[32,1024]{1,0:T(8,128)(2,1)S(1)}, u32[]{:S(2)}, u32[]{:S(2)}) collective-permute-start(bf16[32,1024]{1,0:T(8,128)(2,1)S(1)} %get-tuple-element.103.refs_0_), channel_id=1, source_target_pairs={{0,16},{2,18},{4,20},{6,22},{8,24},{10,26},{12,28},{14,30},{16,0},... | collective-permute-start | bytes 196616 | tf_op jit(solution)/shard_map/ppermute | solution.py:17
  106.0 2.2 %collective-permute-done.24.refs_3_ = bf16[32,1024]{1,0:T(8,128)(2,1)S(1)} collective-permute-done((bf16[32,1024]{1,0:T(8,128)(2,1)S(1)}, bf16[32,1024]{1,0:T(8,128)(2,1)S(1)}, u32[]{:S(2)}, u32[]{:S(2)}) %collective-permute-start.24) | collective-permute-done | bytes 65568 | tf_op jit(solution)/shard_map/ppermute | solution.py:17
  108.2 0.9 collective-permute-done.23.refs_2_
  109.7 2.7 %collective-permute-start.26 = (bf16[64,2048]{1,0:T(8,128)(2,1)S(1)}, bf16[64,2048]{1,0:T(8,128)(2,1)S(1)}, u32[]{:S(2)}, u32[]{:S(2)}) collective-permute-start(bf16[64,2048]{1,0:T(8,128)(2,1)S(1)} %shard_map.131.refs_0_), channel_id=1, source_target_pairs={{0,4},{2,6},{4,0},{6,2},{8,12},{10,14},{12,8},{14,10},{16,20},{18,... | collective-permute-start | bytes 786440 | tf_op jit(solution)/shard_map/ppermute | solution.py:17
  112.5 2.1 %collective-permute-start.25 = (bf16[64,1024]{1,0:T(8,128)(2,1)S(1)}, bf16[64,1024]{1,0:T(8,128)(2,1)S(1)}, u32[]{:S(2)}, u32[]{:S(2)}) collective-permute-start(bf16[64,1024]{1,0:T(8,128)(2,1)S(1)} %pad_maximum_fusion), channel_id=1, source_target_pairs={{0,8},{2,10},{4,12},{6,14},{8,0},{10,2},{12,4},{14,6},{16,24},{18,... | collective-permute-start | bytes 393224 | tf_op jit(solution)/shard_map/ppermute | solution.py:17
  114.6 2.9 %collective-permute-done.27.refs_2_ = bf16[64,1024]{1,0:T(8,128)(2,1)S(1)} collective-permute-done((bf16[64,1024]{1,0:T(8,128)(2,1)S(1)}, bf16[64,1024]{1,0:T(8,128)(2,1)S(1)}, u32[]{:S(2)}, u32[]{:S(2)}) %collective-permute-start.27) | collective-permute-done | bytes 131104 | tf_op jit(solution)/shard_map/ppermute | solution.py:17
  117.4 1.4 collective-permute-done.25.refs_1_
  119.6 2.0 %collective-permute-start.31 = (bf16[64,1024]{1,0:T(8,128)(2,1)S(1)}, bf16[64,1024]{1,0:T(8,128)(2,1)S(1)}, u32[]{:S(2)}, u32[]{:S(2)}) collective-permute-start(bf16[64,1024]{1,0:T(8,128)(2,1)S(1)} %collective-permute-done.27.refs_2_), channel_id=1, source_target_pairs={{0,4},{2,6},{4,0},{6,2},{8,12},{10,14},{12,8},{14,10},{16,20},{18,... | collective-permute-start | bytes 393224 | tf_op jit(solution)/shard_map/ppermute | solution.py:17
  121.6 2.6 %shard_map.133 = (bf16[256,2048]{1,0:T(8,128)(2,1)S(1)}, f32[256,768]{1,0:T(8,128)S(1)}, bf16[256,768]{1,0:T(8,128)(2,1)S(1)}) custom-call(s32[2]{0:T(128)S(1)} %pad_add_fusion.place_ref, bf16[128,2048]{1,0:T(8,128)(2,1)S(1)} %shard_map.132.err_own_ref, bf16[128,2048]{1,0:T(8,128)(2,1)S(1)} %collective-permute-done.28.err_other_ref, ...), custom_call_target="tpu_custom_call" | custom-call | flops 1610612736 | bytes 9699328 | tf_op jit(solution)/shard_map/pallas_call | solution.py:112
  124.2 4.0 %collective-permute-done.31.refs_2_ = bf16[64,1024]{1,0:T(8,128)(2,1)S(1)} collective-permute-done((bf16[64,1024]{1,0:T(8,128)(2,1)S(1)}, bf16[64,1024]{1,0:T(8,128)(2,1)S(1)}, u32[]{:S(2)}, u32[]{:S(2)}) %collective-permute-start.31) | collective-permute-done | bytes 131104 | tf_op jit(solution)/shard_map/ppermute | solution.py:17
  128.9 1.6 collective-permute-start.29
  130.8 2.4 %shard_map.135 = (bf16[256,2048]{1,0:T(8,128)(2,1)S(1)}, f32[256,768]{1,0:T(8,128)S(1)}, bf16[256,768]{1,0:T(8,128)(2,1)S(1)}) custom-call(s32[2]{0:T(128)S(1)} %pad_add_fusion.place_ref, bf16[128,2048]{1,0:T(8,128)(2,1)S(1)} %shard_map.134.err_own_ref, bf16[128,2048]{1,0:T(8,128)(2,1)S(1)} %collective-permute-done.32.err_other_ref, ...), custom_call_target="tpu_custom_call" | custom-call | flops 1610612736 | bytes 9699328 | tf_op jit(solution)/shard_map/pallas_call | solution.py:112
  133.2 1.6 collective-permute-start.33
  134.8 6.0 %collective-permute-done.29.refs_0_ = bf16[256,768]{1,0:T(8,128)(2,1)S(1)} collective-permute-done((bf16[256,768]{1,0:T(8,128)(2,1)S(1)}, bf16[256,768]{1,0:T(8,128)(2,1)S(1)}, u32[]{:S(2)}, u32[]{:S(2)}) %collective-permute-start.29) | collective-permute-done | bytes 393248 | tf_op jit(solution)/shard_map/ppermute | solution.py:17
  140.9 4.0 %shard_map.136 = (bf16[256,1536]{1,0:T(8,128)(2,1)S(1)}, bf16[128,2048]{1,0:T(8,128)(2,1)S(1)}, bf16[128,2048]{1,0:T(8,128)(2,1)S(1)}, bf16[128,2048]{1,0:T(8,128)(2,1)S(1)}, bf16[128,2048]{1,0:T(8,128)(2,1)S(1)}) custom-call(s32[2]{0:T(128)S(1)} %pad_add_fusion.place_ref, f32[256,768]{1,0:T(8,128)S(1)} %get-tuple-element.66.grad_own_ref, ...), custom_call_target="tpu_custom_call" | custom-call | flops 3221225472 | bytes 18219008 | tf_op jit(solution)/shard_map/pallas_call | solution.py:112
  144.9 3.9 %collective-permute-done.33.refs_0_ = bf16[256,768]{1,0:T(8,128)(2,1)S(1)} collective-permute-done((bf16[256,768]{1,0:T(8,128)(2,1)S(1)}, bf16[256,768]{1,0:T(8,128)(2,1)S(1)}, u32[]{:S(2)}, u32[]{:S(2)}) %collective-permute-start.33) | collective-permute-done | bytes 393248 | tf_op jit(solution)/shard_map/ppermute | solution.py:17
  148.8 4.0 %shard_map.137 = (bf16[256,1536]{1,0:T(8,128)(2,1)S(1)}, bf16[128,2048]{1,0:T(8,128)(2,1)S(1)}, bf16[128,2048]{1,0:T(8,128)(2,1)S(1)}, bf16[128,2048]{1,0:T(8,128)(2,1)S(1)}, bf16[128,2048]{1,0:T(8,128)(2,1)S(1)}) custom-call(s32[2]{0:T(128)S(1)} %pad_add_fusion.place_ref, f32[256,768]{1,0:T(8,128)S(1)} %get-tuple-element.76.grad_own_ref, ...), custom_call_target="tpu_custom_call" | custom-call | flops 3221225472 | bytes 18219008 | tf_op jit(solution)/shard_map/pallas_call | solution.py:112
  153.4 1.4 collective-permute-done.36
  155.8 1.5 collective-permute-start.38
  157.3 6.0 %collective-permute-done.37 = bf16[64,2048]{1,0:T(8,128)(2,1)S(1)} collective-permute-done((bf16[64,2048]{1,0:T(8,128)(2,1)S(1)}, bf16[64,2048]{1,0:T(8,128)(2,1)S(1)}, u32[]{:S(2)}, u32[]{:S(2)}) %collective-permute-start.37) | collective-permute-done | bytes 262176 | tf_op jit(solution)/shard_map/ppermute | solution.py:17
  164.0 1.5 collective-permute-start.39
  165.7 1.8 collective-permute-start.42
  167.6 6.3 %shard_map.138.refs_7_ = f32[4,32,768]{2,1,0:T(8,128)} custom-call(s32[2]{0:T(128)S(1)} %pad_add_fusion.place_ref, bf16[128,4096]{1,0:T(8,128)(2,1)S(1)} %shard_map.125.own_ref.refs_0_, bf16[128,4096]{1,0:T(8,128)(2,1)S(1)} %collective-permute-done.6.other_ref.refs_1_, bf16[128,4096]{1,0:T(8,128)(2,1)S(1)} %shard_map.128.own_ref.refs_2_, ...), custom_call_target="tpu_custom_call" | custom-call | flops 3221225472 | bytes 18743296 | tf_op jit(solution)/shard_map/pallas_call | solution.py:112
  175.6 6.3 %shard_map.139 = f32[4,32,768]{2,1,0:T(8,128)} custom-call(s32[2]{0:T(128)S(1)} %pad_add_fusion.place_ref, bf16[128,4096]{1,0:T(8,128)(2,1)S(1)} %shard_map.125.own_ref.refs_0_, bf16[128,4096]{1,0:T(8,128)(2,1)S(1)} %collective-permute-done.6.other_ref.refs_1_, bf16[128,4096]{1,0:T(8,128)(2,1)S(1)} %shard_map.128.own_ref.refs_2_, ...), custom_call_target="tpu_custom_call", output_to_operand_aliasing={{}: (8, {})} | custom-call | flops 3221225472 | bytes 18743296 | tf_op jit(solution)/shard_map/pallas_call | solution.py:112
  182.0 1.5 collective-permute-start.45
  183.5 5.6 %shard_map.140 = f32[2,12,2048]{2,1,0:T(8,128)S(1)} custom-call(s32[2]{0:T(128)S(1)} %pad_add_fusion.place_ref, bf16[256,768]{1,0:T(8,128)(2,1)S(1)} %get-tuple-element.55.refs_0_, bf16[256,768]{1,0:T(8,128)(2,1)S(1)} %collective-permute-done.7.refs_1_, bf16[256,768]{1,0:T(8,128)(2,1)S(1)} %get-tuple-element.59.refs_0_.refs_2_, ...), custom_call_target="tpu_custom_call" | custom-call | flops 3221225472 | bytes 10158080 | tf_op jit(solution)/shard_map/pallas_call | solution.py:112
  189.1 0.8 copy.18
  (113 shorter events, 16.4 us)
Async XLA Ops:
  0.6 27.9 %collective-permute-start.1 = (bf16[32,4096]{1,0:T(8,128)(2,1)}, bf16[32,4096]{1,0:T(8,128)(2,1)S(1)}, u32[]{:S(2)}, u32[]{:S(2)}) collective-permute-start(bf16[32,4096]{1,0:T(8,128)(2,1)} %refs_0_.1), channel_id=1, source_target_pairs={{0,4},{2,6},{4,0},{6,2},{8,12},{10,14},{12,8},{14,10},{16,20},{18,... | collective-permute-start | bytes 786440 | tf_op jit(solution)/shard_map/ppermute | solution.py:17
  3.6 24.9 %collective-permute-start = (bf16[32,4096]{1,0:T(8,128)(2,1)}, bf16[32,4096]{1,0:T(8,128)(2,1)S(1)}, u32[]{:S(2)}, u32[]{:S(2)}) collective-permute-start(bf16[32,4096]{1,0:T(8,128)(2,1)} %refs_0_.1), channel_id=1, source_target_pairs={{0,16},{2,18},{4,20},{6,22},{8,24},{10,26},{12,28},{14,30},{16,0},... | collective-permute-start | bytes 786440 | tf_op jit(solution)/shard_map/ppermute | solution.py:17
  6.2 22.3 %collective-permute-start.2 = (bf16[32,4096]{1,0:T(8,128)(2,1)}, bf16[32,4096]{1,0:T(8,128)(2,1)S(1)}, u32[]{:S(2)}, u32[]{:S(2)}) collective-permute-start(bf16[32,4096]{1,0:T(8,128)(2,1)} %refs_0_.1), channel_id=1, source_target_pairs={{0,8},{2,10},{4,12},{6,14},{8,0},{10,2},{12,4},{14,6},{16,24},{18,... | collective-permute-start | bytes 786440 | tf_op jit(solution)/shard_map/ppermute | solution.py:17
  8.8 4.6 %copy-start.4 = (bf16[1,2,4096,768]{3,2,1,0:T(8,128)(2,1)S(1)}, bf16[1,2,4096,768]{3,2,1,0:T(8,128)(2,1)}, u32[]{:S(2)}) copy-start(bf16[1,2,4096,768]{3,2,1,0:T(8,128)(2,1)} %refs_6_.4) | copy-start | bytes 37748740
  15.2 8.4 %copy-start.10 = (f32[1,12,2048]{2,0,1:T(1,128)S(1)}, f32[1,12,2048]{2,0,1:T(1,128)}, u32[]{:S(2)}) copy-start(f32[1,12,2048]{2,0,1:T(1,128)} %param.18) | copy-start | bytes 294916
  15.2 8.4 %copy-start.5 = (bf16[1,1536,2048]{2,1,0:T(8,128)(2,1)S(1)}, bf16[1,1536,2048]{2,1,0:T(8,128)(2,1)}, u32[]{:S(2)}) copy-start(bf16[1,1536,2048]{2,1,0:T(8,128)(2,1)} %refs_6_.5) | copy-start | bytes 18874372
  19.0 4.6 %copy-start = (bf16[4096,1536]{1,0:T(8,128)(2,1)}, bf16[4096,1536]{1,0:T(8,128)(2,1)S(1)}, u32[]{:S(2)}) copy-start(bf16[4096,1536]{1,0:T(8,128)(2,1)S(1)} %shard_map.121.w_ref.refs_3_) | copy-start | bytes 37748740
  23.6 6.6 %copy-start.11 = (f32[32,8]{0,1:T(8,128)S(1)}, f32[32,8]{0,1:T(8,128)}, u32[]{:S(2)}) copy-start(f32[32,8]{0,1:T(8,128)} %param.13) | copy-start | bytes 3076
  23.6 6.6 %copy-start.12 = (s32[32,8]{0,1:T(8,128)S(1)}, s32[32,8]{0,1:T(8,128)}, u32[]{:S(2)}) copy-start(s32[32,8]{0,1:T(8,128)} %param.12) | copy-start | bytes 3076
  23.6 18.4 %copy-start.6 = (bf16[32,4096]{1,0:T(8,128)(2,1)S(1)}, bf16[32,4096]{1,0:T(8,128)(2,1)}, u32[]{:S(2)}) copy-start(bf16[32,4096]{1,0:T(8,128)(2,1)} %refs_0_.1) | copy-start | bytes 786436
  25.9 2.6 %copy-start.3 = (bf16[1536,2048]{1,0:T(8,128)(2,1)}, bf16[1536,2048]{1,0:T(8,128)(2,1)S(1)}, u32[]{:S(2)}) copy-start(bf16[1536,2048]{1,0:T(8,128)(2,1)S(1)} %shard_map.122.refs_2_.w_ref) | copy-start | bytes 18874372
  29.1 12.9 %collective-permute-start.4 = (bf16[64,4096]{1,0:T(8,128)(2,1)S(1)}, bf16[64,4096]{1,0:T(8,128)(2,1)S(1)}, u32[]{:S(2)}, u32[]{:S(2)}) collective-permute-start(bf16[64,4096]{1,0:T(8,128)(2,1)S(1)} %shard_map.123.refs_1_), channel_id=1, source_target_pairs={{0,4},{2,6},{4,0},{6,2},{8,12},{10,14},{12,8},{14,10},{16,20},{18,... | collective-permute-start | bytes 1572872 | tf_op jit(solution)/shard_map/ppermute | solution.py:17
  29.7 7.1 %collective-permute-start.3 = (bf16[32,4096]{1,0:T(8,128)(2,1)S(1)}, bf16[32,4096]{1,0:T(8,128)(2,1)S(1)}, u32[]{:S(2)}, u32[]{:S(2)}) collective-permute-start(bf16[32,4096]{1,0:T(8,128)(2,1)S(1)} %collective-permute-done.refs_0_), channel_id=1, source_target_pairs={{0,8},{2,10},{4,12},{6,14},{8,0},{10,2},{12,4},{14,6},{16,24},{18,... | collective-permute-start | bytes 786440 | tf_op jit(solution)/shard_map/ppermute | solution.py:17
  31.1 4.7 %collective-permute-start.5 = (bf16[32,128]{1,0:T(8,128)(2,1)S(1)}, bf16[32,128]{1,0:T(8,128)(2,1)S(1)}, u32[]{:S(2)}, u32[]{:S(2)}) collective-permute-start(bf16[32,128]{1,0:T(8,128)(2,1)S(1)} %shard_map.124), channel_id=1, source_target_pairs={{0,16},{2,18},{4,20},{6,22},{8,24},{10,26},{12,28},{14,30},{16,0},... | collective-permute-start | bytes 24584 | tf_op jit(solution)/shard_map/ppermute | solution.py:17
  42.6 2.7 %collective-permute-start.6 = (bf16[128,4096]{1,0:T(8,128)(2,1)S(1)}, bf16[128,4096]{1,0:T(8,128)(2,1)S(1)}, u32[]{:S(2)}, u32[]{:S(2)}) collective-permute-start(bf16[128,4096]{1,0:T(8,128)(2,1)S(1)} %shard_map.125.own_ref.refs_0_), channel_id=1, source_target_pairs={{0,2},{2,0},{4,6},{6,4},{8,10},{10,8},{12,14},{14,12},{16,18},{18,... | collective-permute-start | bytes 3145736 | tf_op jit(solution)/shard_map/ppermute | solution.py:17
  42.7 11.3 %collective-permute-start.8 = (bf16[64,128]{1,0:T(8,128)(2,1)S(1)}, bf16[64,128]{1,0:T(8,128)(2,1)S(1)}, u32[]{:S(2)}, u32[]{:S(2)}) collective-permute-start(bf16[64,128]{1,0:T(8,128)(2,1)S(1)} %pad_maximum_fusion.4), channel_id=1, source_target_pairs={{0,8},{2,10},{4,12},{6,14},{8,0},{10,2},{12,4},{14,6},{16,24},{18,... | collective-permute-start | bytes 49160 | tf_op jit(solution)/shard_map/ppermute | solution.py:17
  43.2 10.8 %collective-permute-start.12 = (bf16[32,4096]{1,0:T(8,128)(2,1)S(1)}, bf16[32,4096]{1,0:T(8,128)(2,1)S(1)}, u32[]{:S(2)}, u32[]{:S(2)}) collective-permute-start(bf16[32,4096]{1,0:T(8,128)(2,1)S(1)} %collective-permute-done.3.refs_2_), channel_id=1, source_target_pairs={{0,4},{2,6},{4,0},{6,2},{8,12},{10,14},{12,8},{14,10},{16,20},{18,... | collective-permute-start | bytes 786440 | tf_op jit(solution)/shard_map/ppermute | solution.py:17
  45.3 4.6 %copy-start.1 = (bf16[4096,1536]{1,0:T(8,128)(2,1)S(1)}, bf16[4096,1536]{1,0:T(8,128)(2,1)}, u32[]{:S(2)}) copy-start(bf16[4096,1536]{1,0:T(8,128)(2,1)} %copy-done) | copy-start | bytes 37748740
  49.9 7.5 %copy-start.2 = (bf16[4096,1536]{1,0:T(8,128)(2,1)S(1)}, bf16[4096,1536]{1,0:T(8,128)(2,1)}, u32[]{:S(2)}) copy-start(bf16[4096,1536]{1,0:T(8,128)(2,1)} %copy-done) | copy-start | bytes 37748740
  49.9 18.3 %slice-start = ((s8[6291456]{0:T(1024)(128)(4,1)}), s8[4194304]{0:T(1024)(128)(4,1)S(1)}, s32[]{:S(2)}) async-start(s8[6291456]{0:T(1024)(128)(4,1)} %bitcast.7), calls=%async_computation | async-start | bytes 8388608
  54.0 14.2 %slice-start.1 = ((s8[6291456]{0:T(1024)(128)(4,1)}), s8[2097152]{0:T(1024)(128)(4,1)S(1)}, s32[]{:S(2)}) async-start(s8[6291456]{0:T(1024)(128)(4,1)} %bitcast.7), calls=%async_computation.1 | async-start | bytes 4194304
  54.6 2.7 %collective-permute-start.13 = (bf16[128,4096]{1,0:T(8,128)(2,1)S(1)}, bf16[128,4096]{1,0:T(8,128)(2,1)S(1)}, u32[]{:S(2)}, u32[]{:S(2)}) collective-permute-start(bf16[128,4096]{1,0:T(8,128)(2,1)S(1)} %shard_map.128.own_ref.refs_2_), channel_id=1, source_target_pairs={{0,2},{2,0},{4,6},{6,4},{8,10},{10,8},{12,14},{14,12},{16,18},{18,... | collective-permute-start | bytes 3145736 | tf_op jit(solution)/shard_map/ppermute | solution.py:17
  54.8 13.4 %collective-permute-start.7 = (bf16[256,768]{1,0:T(8,128)(2,1)S(1)}, bf16[256,768]{1,0:T(8,128)(2,1)S(1)}, u32[]{:S(2)}, u32[]{:S(2)}) collective-permute-start(bf16[256,768]{1,0:T(8,128)(2,1)S(1)} %get-tuple-element.55.refs_0_), channel_id=1, source_target_pairs={{0,1},{1,0},{2,3},{3,2},{4,5},{5,4},{6,7},{7,6},{8,9},{9,8},{10,11... | collective-permute-start | bytes 1179656 | tf_op jit(solution)/shard_map/ppermute | solution.py:17
  61.5 41.4 %copy-start.9 = (bf16[32,2048]{1,0:T(8,128)(2,1)S(1)}, bf16[32,2048]{1,0:T(8,128)(2,1)}, u32[]{:S(2)}) copy-start(bf16[32,2048]{1,0:T(8,128)(2,1)} %param.11) | copy-start | bytes 393220
  61.5 13.2 %collective-permute-start.14 = (bf16[256,768]{1,0:T(8,128)(2,1)S(1)}, bf16[256,768]{1,0:T(8,128)(2,1)S(1)}, u32[]{:S(2)}, u32[]{:S(2)}) collective-permute-start(bf16[256,768]{1,0:T(8,128)(2,1)S(1)} %get-tuple-element.59.refs_0_.refs_2_), channel_id=1, source_target_pairs={{0,1},{1,0},{2,3},{3,2},{4,5},{5,4},{6,7},{7,6},{8,9},{9,8},{10,11... | collective-permute-start | bytes 1179656 | tf_op jit(solution)/shard_map/ppermute | solution.py:17
  63.1 3.9 %collective-permute-start.9 = (bf16[128,128]{1,0:T(8,128)(2,1)S(1)}, bf16[128,128]{1,0:T(8,128)(2,1)S(1)}, u32[]{:S(2)}, u32[]{:S(2)}) collective-permute-start(bf16[128,128]{1,0:T(8,128)(2,1)S(1)} %pad_maximum_fusion.3), channel_id=1, source_target_pairs={{0,4},{2,6},{4,0},{6,2},{8,12},{10,14},{12,8},{14,10},{16,20},{18,... | collective-permute-start | bytes 98312 | tf_op jit(solution)/shard_map/ppermute | solution.py:17
  67.0 1.3 collective-permute-start.10
  77.0 2.0 %collective-permute-start.15 = (bf16[128,2048]{1,0:T(8,128)(2,1)S(1)}, bf16[128,2048]{1,0:T(8,128)(2,1)S(1)}, u32[]{:S(2)}, u32[]{:S(2)}) collective-permute-start(bf16[128,2048]{1,0:T(8,128)(2,1)S(1)} %get-tuple-element.62), channel_id=1, source_target_pairs={{0,2},{2,0},{4,6},{6,4},{8,10},{10,8},{12,14},{14,12},{16,18},{18,... | collective-permute-start | bytes 1572872 | tf_op jit(solution)/shard_map/ppermute | solution.py:17
  77.1 10.9 %collective-permute-start.11 = (bf16[128,2048]{1,0:T(8,128)(2,1)S(1)}, bf16[128,2048]{1,0:T(8,128)(2,1)S(1)}, u32[]{:S(2)}, u32[]{:S(2)}) collective-permute-start(bf16[128,2048]{1,0:T(8,128)(2,1)S(1)} %get-tuple-element.57), channel_id=1, source_target_pairs={{0,2},{2,0},{4,6},{6,4},{8,10},{10,8},{12,14},{14,12},{16,18},{18,... | collective-permute-start | bytes 1572872 | tf_op jit(solution)/shard_map/ppermute | solution.py:17
  79.1 6.4 %collective-permute-start.17 = (bf16[64,1024]{1,0:T(8,128)(2,1)S(1)}, bf16[64,1024]{1,0:T(8,128)(2,1)S(1)}, u32[]{:S(2)}, u32[]{:S(2)}) collective-permute-start(bf16[64,1024]{1,0:T(8,128)(2,1)S(1)} %get-tuple-element.114), channel_id=1, source_target_pairs={{0,4},{2,6},{4,0},{6,2},{8,12},{10,14},{12,8},{14,10},{16,20},{18,... | collective-permute-start | bytes 393224 | tf_op jit(solution)/shard_map/ppermute | solution.py:17
  79.7 7.8 %collective-permute-start.16 = (bf16[64,1024]{1,0:T(8,128)(2,1)S(1)}, bf16[64,1024]{1,0:T(8,128)(2,1)S(1)}, u32[]{:S(2)}, u32[]{:S(2)}) collective-permute-start(bf16[64,1024]{1,0:T(8,128)(2,1)S(1)} %get-tuple-element.115), channel_id=1, source_target_pairs={{0,4},{2,6},{4,0},{6,2},{8,12},{10,14},{12,8},{14,10},{16,20},{18,... | collective-permute-start | bytes 393224 | tf_op jit(solution)/shard_map/ppermute | solution.py:17
  87.5 8.0 %collective-permute-start.18 = (bf16[64,2048]{1,0:T(8,128)(2,1)S(1)}, bf16[64,2048]{1,0:T(8,128)(2,1)S(1)}, u32[]{:S(2)}, u32[]{:S(2)}) collective-permute-start(bf16[64,2048]{1,0:T(8,128)(2,1)S(1)} %add_convert_fusion.7), channel_id=1, source_target_pairs={{0,4},{2,6},{4,0},{6,2},{8,12},{10,14},{12,8},{14,10},{16,20},{18,... | collective-permute-start | bytes 786440 | tf_op jit(solution)/shard_map/ppermute | solution.py:17
  88.1 5.9 %collective-permute-start.21 = (bf16[64,1024]{1,0:T(8,128)(2,1)S(1)}, bf16[64,1024]{1,0:T(8,128)(2,1)S(1)}, u32[]{:S(2)}, u32[]{:S(2)}) collective-permute-start(bf16[64,1024]{1,0:T(8,128)(2,1)S(1)} %get-tuple-element.112), channel_id=1, source_target_pairs={{0,8},{2,10},{4,12},{6,14},{8,0},{10,2},{12,4},{14,6},{16,24},{18,... | collective-permute-start | bytes 393224 | tf_op jit(solution)/shard_map/ppermute | solution.py:17
  89.1 6.3 %collective-permute-start.19 = (bf16[64,1024]{1,0:T(8,128)(2,1)S(1)}, bf16[64,1024]{1,0:T(8,128)(2,1)S(1)}, u32[]{:S(2)}, u32[]{:S(2)}) collective-permute-start(bf16[64,1024]{1,0:T(8,128)(2,1)S(1)} %get-tuple-element.113), channel_id=1, source_target_pairs={{0,8},{2,10},{4,12},{6,14},{8,0},{10,2},{12,4},{14,6},{16,24},{18,... | collective-permute-start | bytes 393224 | tf_op jit(solution)/shard_map/ppermute | solution.py:17
  95.5 6.6 %collective-permute-start.22 = (bf16[32,1024]{1,0:T(8,128)(2,1)S(1)}, bf16[32,1024]{1,0:T(8,128)(2,1)S(1)}, u32[]{:S(2)}, u32[]{:S(2)}) collective-permute-start(bf16[32,1024]{1,0:T(8,128)(2,1)S(1)} %get-tuple-element.104), channel_id=1, source_target_pairs={{0,16},{2,18},{4,20},{6,22},{8,24},{10,26},{12,28},{14,30},{16,0},... | collective-permute-start | bytes 196616 | tf_op jit(solution)/shard_map/ppermute | solution.py:17
  95.9 6.9 %collective-permute-start.20 = (bf16[32,1024]{1,0:T(8,128)(2,1)S(1)}, bf16[32,1024]{1,0:T(8,128)(2,1)S(1)}, u32[]{:S(2)}, u32[]{:S(2)}) collective-permute-start(bf16[32,1024]{1,0:T(8,128)(2,1)S(1)} %get-tuple-element.105), channel_id=1, source_target_pairs={{0,16},{2,18},{4,20},{6,22},{8,24},{10,26},{12,28},{14,30},{16,0},... | collective-permute-start | bytes 196616 | tf_op jit(solution)/shard_map/ppermute | solution.py:17
  103.0 5.2 %collective-permute-start.24 = (bf16[32,1024]{1,0:T(8,128)(2,1)S(1)}, bf16[32,1024]{1,0:T(8,128)(2,1)S(1)}, u32[]{:S(2)}, u32[]{:S(2)}) collective-permute-start(bf16[32,1024]{1,0:T(8,128)(2,1)S(1)} %get-tuple-element.102.refs_1_), channel_id=1, source_target_pairs={{0,16},{2,18},{4,20},{6,22},{8,24},{10,26},{12,28},{14,30},{16,0},... | collective-permute-start | bytes 196616 | tf_op jit(solution)/shard_map/ppermute | solution.py:17
  104.0 5.2 %collective-permute-start.23 = (bf16[32,1024]{1,0:T(8,128)(2,1)S(1)}, bf16[32,1024]{1,0:T(8,128)(2,1)S(1)}, u32[]{:S(2)}, u32[]{:S(2)}) collective-permute-start(bf16[32,1024]{1,0:T(8,128)(2,1)S(1)} %get-tuple-element.103.refs_0_), channel_id=1, source_target_pairs={{0,16},{2,18},{4,20},{6,22},{8,24},{10,26},{12,28},{14,30},{16,0},... | collective-permute-start | bytes 196616 | tf_op jit(solution)/shard_map/ppermute | solution.py:17
  109.7 7.7 %collective-permute-start.26 = (bf16[64,2048]{1,0:T(8,128)(2,1)S(1)}, bf16[64,2048]{1,0:T(8,128)(2,1)S(1)}, u32[]{:S(2)}, u32[]{:S(2)}) collective-permute-start(bf16[64,2048]{1,0:T(8,128)(2,1)S(1)} %shard_map.131.refs_0_), channel_id=1, source_target_pairs={{0,4},{2,6},{4,0},{6,2},{8,12},{10,14},{12,8},{14,10},{16,20},{18,... | collective-permute-start | bytes 786440 | tf_op jit(solution)/shard_map/ppermute | solution.py:17
  112.4 5.0 %collective-permute-start.27 = (bf16[64,1024]{1,0:T(8,128)(2,1)S(1)}, bf16[64,1024]{1,0:T(8,128)(2,1)S(1)}, u32[]{:S(2)}, u32[]{:S(2)}) collective-permute-start(bf16[64,1024]{1,0:T(8,128)(2,1)S(1)} %pad_maximum_fusion.1), channel_id=1, source_target_pairs={{0,8},{2,10},{4,12},{6,14},{8,0},{10,2},{12,4},{14,6},{16,24},{18,... | collective-permute-start | bytes 393224 | tf_op jit(solution)/shard_map/ppermute | solution.py:17
  112.5 6.3 %collective-permute-start.25 = (bf16[64,1024]{1,0:T(8,128)(2,1)S(1)}, bf16[64,1024]{1,0:T(8,128)(2,1)S(1)}, u32[]{:S(2)}, u32[]{:S(2)}) collective-permute-start(bf16[64,1024]{1,0:T(8,128)(2,1)S(1)} %pad_maximum_fusion), channel_id=1, source_target_pairs={{0,8},{2,10},{4,12},{6,14},{8,0},{10,2},{12,4},{14,6},{16,24},{18,... | collective-permute-start | bytes 393224 | tf_op jit(solution)/shard_map/ppermute | solution.py:17
  119.4 2.2 %collective-permute-start.28 = (bf16[128,2048]{1,0:T(8,128)(2,1)S(1)}, bf16[128,2048]{1,0:T(8,128)(2,1)S(1)}, u32[]{:S(2)}, u32[]{:S(2)}) collective-permute-start(bf16[128,2048]{1,0:T(8,128)(2,1)S(1)} %shard_map.132.err_own_ref), channel_id=1, source_target_pairs={{0,2},{2,0},{4,6},{6,4},{8,10},{10,8},{12,14},{14,12},{16,18},{18,... | collective-permute-start | bytes 1572872 | tf_op jit(solution)/shard_map/ppermute | solution.py:17
  119.5 8.7 %collective-permute-start.30 = (bf16[64,1024]{1,0:T(8,128)(2,1)S(1)}, bf16[64,1024]{1,0:T(8,128)(2,1)S(1)}, u32[]{:S(2)}, u32[]{:S(2)}) collective-permute-start(bf16[64,1024]{1,0:T(8,128)(2,1)S(1)} %collective-permute-done.25.refs_1_), channel_id=1, source_target_pairs={{0,4},{2,6},{4,0},{6,2},{8,12},{10,14},{12,8},{14,10},{16,20},{18,... | collective-permute-start | bytes 393224 | tf_op jit(solution)/shard_map/ppermute | solution.py:17
  119.6 8.6 %collective-permute-start.31 = (bf16[64,1024]{1,0:T(8,128)(2,1)S(1)}, bf16[64,1024]{1,0:T(8,128)(2,1)S(1)}, u32[]{:S(2)}, u32[]{:S(2)}) collective-permute-start(bf16[64,1024]{1,0:T(8,128)(2,1)S(1)} %collective-permute-done.27.refs_2_), channel_id=1, source_target_pairs={{0,4},{2,6},{4,0},{6,2},{8,12},{10,14},{12,8},{14,10},{16,20},{18,... | collective-permute-start | bytes 393224 | tf_op jit(solution)/shard_map/ppermute | solution.py:17
  128.8 2.0 %collective-permute-start.32 = (bf16[128,2048]{1,0:T(8,128)(2,1)S(1)}, bf16[128,2048]{1,0:T(8,128)(2,1)S(1)}, u32[]{:S(2)}, u32[]{:S(2)}) collective-permute-start(bf16[128,2048]{1,0:T(8,128)(2,1)S(1)} %shard_map.134.err_own_ref), channel_id=1, source_target_pairs={{0,2},{2,0},{4,6},{6,4},{8,10},{10,8},{12,14},{14,12},{16,18},{18,... | collective-permute-start | bytes 1572872 | tf_op jit(solution)/shard_map/ppermute | solution.py:17
  128.9 12.0 %collective-permute-start.29 = (bf16[256,768]{1,0:T(8,128)(2,1)S(1)}, bf16[256,768]{1,0:T(8,128)(2,1)S(1)}, u32[]{:S(2)}, u32[]{:S(2)}) collective-permute-start(bf16[256,768]{1,0:T(8,128)(2,1)S(1)} %get-tuple-element.67), channel_id=1, source_target_pairs={{0,1},{1,0},{2,3},{3,2},{4,5},{5,4},{6,7},{7,6},{8,9},{9,8},{10,11... | collective-permute-start | bytes 1179656 | tf_op jit(solution)/shard_map/ppermute | solution.py:17
  133.2 15.6 %collective-permute-start.33 = (bf16[256,768]{1,0:T(8,128)(2,1)S(1)}, bf16[256,768]{1,0:T(8,128)(2,1)S(1)}, u32[]{:S(2)}, u32[]{:S(2)}) collective-permute-start(bf16[256,768]{1,0:T(8,128)(2,1)S(1)} %get-tuple-element.77), channel_id=1, source_target_pairs={{0,1},{1,0},{2,3},{3,2},{4,5},{5,4},{6,7},{7,6},{8,9},{9,8},{10,11... | collective-permute-start | bytes 1179656 | tf_op jit(solution)/shard_map/ppermute | solution.py:17
  140.9 26.7 %slice-start.2 = ((s8[12582912]{0:T(1024)(128)(4,1)}), s8[4194304]{0:T(1024)(128)(4,1)S(1)}, s32[]{:S(2)}) async-start(s8[12582912]{0:T(1024)(128)(4,1)} %bitcast.10), calls=%async_computation.2 | async-start | bytes 8388608
  140.9 26.7 %slice-start.3 = ((s8[12582912]{0:T(1024)(128)(4,1)}), s8[4194304]{0:T(1024)(128)(4,1)S(1)}, s32[]{:S(2)}) async-start(s8[12582912]{0:T(1024)(128)(4,1)} %bitcast.10), calls=%async_computation.3 | async-start | bytes 8388608
  148.8 18.7 %slice-start.4 = ((s8[12582912]{0:T(1024)(128)(4,1)}), s8[4194304]{0:T(1024)(128)(4,1)S(1)}, s32[]{:S(2)}) async-start(s8[12582912]{0:T(1024)(128)(4,1)} %bitcast.10), calls=%async_computation.4 | async-start | bytes 8388608
  152.9 2.0 %collective-permute-start.36 = (bf16[128,2048]{1,0:T(8,128)(2,1)S(1)}, bf16[128,2048]{1,0:T(8,128)(2,1)S(1)}, u32[]{:S(2)}, u32[]{:S(2)}) collective-permute-start(bf16[128,2048]{1,0:T(8,128)(2,1)S(1)} %get-tuple-element.91), channel_id=1, source_target_pairs={{0,2},{2,0},{4,6},{6,4},{8,10},{10,8},{12,14},{14,12},{16,18},{18,... | collective-permute-start | bytes 1572872 | tf_op jit(solution)/shard_map/ppermute | solution.py:17
  152.9 4.4 %collective-permute-start.35 = (bf16[128,2048]{1,0:T(8,128)(2,1)S(1)}, bf16[128,2048]{1,0:T(8,128)(2,1)S(1)}, u32[]{:S(2)}, u32[]{:S(2)}) collective-permute-start(bf16[128,2048]{1,0:T(8,128)(2,1)S(1)} %get-tuple-element.89), channel_id=1, source_target_pairs={{0,2},{2,0},{4,6},{6,4},{8,10},{10,8},{12,14},{14,12},{16,18},{18,... | collective-permute-start | bytes 1572872 | tf_op jit(solution)/shard_map/ppermute | solution.py:17
  155.0 8.4 %collective-permute-start.37 = (bf16[64,2048]{1,0:T(8,128)(2,1)S(1)}, bf16[64,2048]{1,0:T(8,128)(2,1)S(1)}, u32[]{:S(2)}, u32[]{:S(2)}) collective-permute-start(bf16[64,2048]{1,0:T(8,128)(2,1)S(1)} %get-tuple-element.108), channel_id=1, source_target_pairs={{0,4},{2,6},{4,0},{6,2},{8,12},{10,14},{12,8},{14,10},{16,20},{18,... | collective-permute-start | bytes 786440 | tf_op jit(solution)/shard_map/ppermute | solution.py:17
  155.3 10.3 %collective-permute-start.41 = (bf16[128,2048]{1,0:T(8,128)(2,1)S(1)}, bf16[128,2048]{1,0:T(8,128)(2,1)S(1)}, u32[]{:S(2)}, u32[]{:S(2)}) collective-permute-start(bf16[128,2048]{1,0:T(8,128)(2,1)S(1)} %get-tuple-element.95), channel_id=1, source_target_pairs={{0,2},{2,0},{4,6},{6,4},{8,10},{10,8},{12,14},{14,12},{16,18},{18,... | collective-permute-start | bytes 1572872 | tf_op jit(solution)/shard_map/ppermute | solution.py:17
  155.3 19.4 %collective-permute-start.34 = (bf16[128,2048]{1,0:T(8,128)(2,1)S(1)}, bf16[128,2048]{1,0:T(8,128)(2,1)S(1)}, u32[]{:S(2)}, u32[]{:S(2)}) collective-permute-start(bf16[128,2048]{1,0:T(8,128)(2,1)S(1)} %get-tuple-element.85), channel_id=1, source_target_pairs={{0,2},{2,0},{4,6},{6,4},{8,10},{10,8},{12,14},{14,12},{16,18},{18,... | collective-permute-start | bytes 1572872 | tf_op jit(solution)/shard_map/ppermute | solution.py:17
  155.8 8.2 %collective-permute-start.38 = (bf16[64,2048]{1,0:T(8,128)(2,1)S(1)}, bf16[64,2048]{1,0:T(8,128)(2,1)S(1)}, u32[]{:S(2)}, u32[]{:S(2)}) collective-permute-start(bf16[64,2048]{1,0:T(8,128)(2,1)S(1)} %get-tuple-element.109), channel_id=1, source_target_pairs={{0,1},{1,0},{2,3},{3,2},{4,5},{5,4},{6,7},{7,6},{8,9},{9,8},{10,11... | collective-permute-start | bytes 786440 | tf_op jit(solution)/shard_map/ppermute | solution.py:17
  164.0 9.9 %collective-permute-start.39 = (bf16[64,2048]{1,0:T(8,128)(2,1)S(1)}, bf16[64,2048]{1,0:T(8,128)(2,1)S(1)}, u32[]{:S(2)}, u32[]{:S(2)}) collective-permute-start(bf16[64,2048]{1,0:T(8,128)(2,1)S(1)} %get-tuple-element.92), channel_id=1, source_target_pairs={{0,1},{1,0},{2,3},{3,2},{4,5},{5,4},{6,7},{7,6},{8,9},{9,8},{10,11... | collective-permute-start | bytes 786440 | tf_op jit(solution)/shard_map/ppermute | solution.py:17
  165.7 8.7 %collective-permute-start.42 = (bf16[64,2048]{1,0:T(8,128)(2,1)S(1)}, bf16[64,2048]{1,0:T(8,128)(2,1)S(1)}, u32[]{:S(2)}, u32[]{:S(2)}) collective-permute-start(bf16[64,2048]{1,0:T(8,128)(2,1)S(1)} %get-tuple-element.111), channel_id=1, source_target_pairs={{0,4},{2,6},{4,0},{6,2},{8,12},{10,14},{12,8},{14,10},{16,20},{18,... | collective-permute-start | bytes 786440 | tf_op jit(solution)/shard_map/ppermute | solution.py:17
  173.9 9.6 %slice-start.5 = ((s8[6291456]{0:T(1024)(128)(4,1)}), s8[4194304]{0:T(1024)(128)(4,1)S(1)}, s32[]{:S(2)}) async-start(s8[6291456]{0:T(1024)(128)(4,1)} %bitcast.12), calls=%async_computation.5 | async-start | bytes 8388608
  173.9 8.0 %collective-permute-start.40 = (bf16[64,2048]{1,0:T(8,128)(2,1)S(1)}, bf16[64,2048]{1,0:T(8,128)(2,1)S(1)}, u32[]{:S(2)}, u32[]{:S(2)}) collective-permute-start(bf16[64,2048]{1,0:T(8,128)(2,1)S(1)} %get-tuple-element.93), channel_id=1, source_target_pairs={{0,1},{1,0},{2,3},{3,2},{4,5},{5,4},{6,7},{7,6},{8,9},{9,8},{10,11... | collective-permute-start | bytes 786440 | tf_op jit(solution)/shard_map/ppermute | solution.py:17
  174.4 7.5 %collective-permute-start.43 = (bf16[64,2048]{1,0:T(8,128)(2,1)S(1)}, bf16[64,2048]{1,0:T(8,128)(2,1)S(1)}, u32[]{:S(2)}, u32[]{:S(2)}) collective-permute-start(bf16[64,2048]{1,0:T(8,128)(2,1)S(1)} %get-tuple-element.96), channel_id=1, source_target_pairs={{0,4},{2,6},{4,0},{6,2},{8,12},{10,14},{12,8},{14,10},{16,20},{18,... | collective-permute-start | bytes 786440 | tf_op jit(solution)/shard_map/ppermute | solution.py:17
  174.8 8.7 %slice-start.6 = ((s8[6291456]{0:T(1024)(128)(4,1)}), s8[2097152]{0:T(1024)(128)(4,1)S(1)}, s32[]{:S(2)}) async-start(s8[6291456]{0:T(1024)(128)(4,1)} %bitcast.12), calls=%async_computation.6 | async-start | bytes 4194304
  174.8 7.1 %collective-permute-start.44 = (bf16[64,2048]{1,0:T(8,128)(2,1)S(1)}, bf16[64,2048]{1,0:T(8,128)(2,1)S(1)}, u32[]{:S(2)}, u32[]{:S(2)}) collective-permute-start(bf16[64,2048]{1,0:T(8,128)(2,1)S(1)} %add_convert_fusion), channel_id=1, source_target_pairs={{0,8},{2,10},{4,12},{6,14},{8,0},{10,2},{12,4},{14,6},{16,24},{18,... | collective-permute-start | bytes 786440 | tf_op jit(solution)/shard_map/ppermute | solution.py:17
  182.0 8.0 %collective-permute-start.45 = (bf16[32,2048]{1,0:T(8,128)(2,1)S(1)}, bf16[32,2048]{1,0:T(8,128)(2,1)S(1)}, u32[]{:S(2)}, u32[]{:S(2)}) collective-permute-start(bf16[32,2048]{1,0:T(8,128)(2,1)S(1)} %add_convert_fusion.9), channel_id=1, source_target_pairs={{0,16},{2,18},{4,20},{6,22},{8,24},{10,26},{12,28},{14,30},{16,0},... | collective-permute-start | bytes 393224 | tf_op jit(solution)/shard_map/ppermute | solution.py:17
  (2 other events, 1.9 us)

commit v6 on v5

--- a/solution.py
+++ b/solution.py
@@ -91,7 +91,7 @@
     return ((step // blocks) ^ place[1]) * blocks + step % blocks
 
 
-def call(kernel, grid, ins, outs, place, scratch=(), mib=16, flops=0, reuse=None):
+def call(kernel, grid, ins, outs, place, scratch=(), mib=16, flops=0, reuse=None, weight=1e-6):
     total = sum(a.size * a.dtype.itemsize for a, _, _ in ins)
     for shape, kind, _, _ in outs:
         count = 1
@@ -120,7 +120,7 @@
         ),
         out_shape=[jax.ShapeDtypeStruct(shape, kind) for shape, kind, _, _ in outs],
         compiler_params=pltpu.CompilerParams(vmem_limit_bytes=mib * MIB),
-        cost_estimate=cost(flops, total),
+        cost_estimate=cost(flops * weight, total * weight),
         input_output_aliases={} if reuse is None else {1 + len(ins): 0},
     )(place, *arrays)
 
@@ -509,14 +509,15 @@
     far = join(gather_far(tokens)[1:])
     near_own = swap(tokens, "expert", 4)
     across = [swap(tokens, "expert", 2)]
-    w_in = dequant(place, in_codes[0], in_low[0], in_high[0])
+    extra = -(-3 * experts // 128) * 128
+    terms = prepare(place, routes, route_scores, extra)
+    w_in = dequant(place, in_codes[0], tie(in_low, terms)[0], in_high[0])
     w_down = dequant(place, down_codes, tie(down_low, w_in), down_high, halves)
     far = tie(far, w_in, w_down, across[0])
     near_far = swap(far, "expert", 4)
     middle = pack(place, [[far], [near_own]])
     across.append(swap(middle, "expert", 2))
-    extra = -(-3 * experts // 128) * 128
-    terms = join(gather_far(prepare(place, tie(routes, far), route_scores, extra)))
+    terms = join(gather_far(terms))
     near_far = tie(near_far, across[1], terms)
     across.append(swap(near_far, "expert", 2))
     first = pack(place, [[tokens], [middle], [near_far]])
@@ -569,7 +570,8 @@
         arrived.append([swap(other, "half", d + 1) for d, other in enumerate(others)])
 
     grad_in, kinds = [], []
-    arrived[0] = [tie(part, grads[1]) for part in arrived[0]]
+    down_grad = ranges_down(place, hidden, grads, down_codes, down_low.shape[1], halves)
+    arrived[0] = [tie(part, down_grad) for part in arrived[0]]
     for c in chunks:
         if c == 1:
             arrived[1] = [tie(part, grad_in[0]) for part in arrived[1]]
@@ -593,6 +595,11 @@
         for d in parts
         if d
     ]
+
+    def ranges(part, pieces, found, *after):
+        held = [tie(grad, *after) for grad in grad_in] if after else grad_in
+        return ranges_in(place, x, held, in_codes, in_low.shape[2], part, pieces, found)
+
     by_half = [pair[0] for pair in crossed]
     across_upper = swap(
         add([part[upper] for part in leave] + by_half).astype(BF16), "expert", 2
@@ -601,8 +608,12 @@
         swap(tie(add([part[upper] for part in keep]).astype(BF16), *by_half), "half", d)
         for d, keep in outer
     ]
+    in_grad = ranges(0, 2, None, *by_half)
     near = swap(
-        add([part[upper] for part in stay] + arrived_upper + [across_upper]).astype(BF16),
+        tie(
+            add([part[upper] for part in stay] + arrived_upper + [across_upper]).astype(BF16),
+            in_grad,
+        ),
         "expert",
         4,
     )
@@ -619,16 +630,13 @@
         )
         for (d, keep), pair in zip(outer, crossed)
     ]
+    in_grad = ranges(2, 4, in_grad)
+    near = tie(near, in_grad)
     grad_tokens = scatter_far(
         [part[lower] for part in stay] + arrived_lower + [across_lower, near]
     )
 
-    grads = [tie(grad, *grad_in) for grad in grads]
-    down_grad = ranges_down(place, hidden, grads, down_codes, down_low.shape[1], halves)
-    in_grad = None
-    pieces = 2
-    for part in range(pieces):
-        in_grad = ranges_in(place, x, grad_in, in_codes, in_low.shape[2], part, pieces, in_grad)
+    in_grad = ranges(3, 4, in_grad)
     return (grad_tokens.astype(BF16), in_grad[None], down_grad[None])
 
 

time: 191 us -> 183 us (0.958)
  local copies, waits for them, and re-layouts: 20.2 us -> 9.77 us
    unnamed x43 -> x24, local copies, waits for them, and re-layouts: 20.1 us -> 9.73 us
    pallas_call x20 -> x21, Pallas kernels: 54.4 us -> 55.6 us  [call(): pl.pallas_call(kernel, grid_spec=pltpu.PrefetchScalarGridSpec(num_scalar_...]
  transfers between devices with their start and end apart: 46 -> 46, of which waited for: 26 -> 31; matrix products, arithmetic and copies ran while one was open for 2% -> 2% of each run, Pallas kernels for 23% -> 25%
where the time goes in v6:
time: 183 us; the launch traced here: 182 us
  waiting for transfers between devices  70.2 us (38%)
  Pallas kernels  55.6 us (30%)
  starting transfers between devices  43.8 us (24%)
  local copies, waits for them, and re-layouts  9.77 us (5%)
  other arithmetic  2 us (1%)
    ppermute x46, waiting for transfers between devices, swap(): return lax.ppermute(array, axis, [(i, i ^ distance) for i in range(size)])  70.2 us
    pallas_call x21, Pallas kernels, call(): pl.pallas_call(kernel, grid_spec=pltpu.PrefetchScalarGridSpec(num_scalar_...  55.6 us
    ppermute x46, starting transfers between devices, swap(): return lax.ppermute(array, axis, [(i, i ^ distance) for i in range(size)])  43.8 us
    unnamed x24, local copies, waits for them, and re-layouts  9.73 us
  transfers between devices with their start and end apart: 46, of which 31 were waited for; matrix products, arithmetic and copies ran while one was open for 2% of the time, Pallas kernels for 25%

profile of v6, /device:TPU:0, one launch (start us, length us, event | category | flops | bytes accessed | tf_op | source)
XLA Modules:
  0.0 182.4 jit_solution(6948808163816429758)
XLA Ops:
  0.6 3.0 %collective-permute-start.1 = (bf16[32,4096]{1,0:T(8,128)(2,1)}, bf16[32,4096]{1,0:T(8,128)(2,1)S(1)}, u32[]{:S(2)}, u32[]{:S(2)}) collective-permute-start(bf16[32,4096]{1,0:T(8,128)(2,1)} %refs_0_.1), channel_id=1, source_target_pairs={{0,4},{2,6},{4,0},{6,2},{8,12},{10,14},{12,8},{14,10},{16,20},{18,... | collective-permute-start | bytes 786440 | tf_op jit(solution)/shard_map/ppermute | solution.py:17
  3.6 2.6 %collective-permute-start = (bf16[32,4096]{1,0:T(8,128)(2,1)}, bf16[32,4096]{1,0:T(8,128)(2,1)S(1)}, u32[]{:S(2)}, u32[]{:S(2)}) collective-permute-start(bf16[32,4096]{1,0:T(8,128)(2,1)} %refs_0_.1), channel_id=1, source_target_pairs={{0,16},{2,18},{4,20},{6,22},{8,24},{10,26},{12,28},{14,30},{16,0},... | collective-permute-start | bytes 786440 | tf_op jit(solution)/shard_map/ppermute | solution.py:17
  6.2 1.6 collective-permute-start.2
  7.8 0.8 copy.15.route_ref
  10.2 0.9 copy.18.high_ref
  11.1 4.6 %copy-done = bf16[1,2,4096,768]{3,2,1,0:T(8,128)(2,1)S(1)} copy-done((bf16[1,2,4096,768]{3,2,1,0:T(8,128)(2,1)S(1)}, bf16[1,2,4096,768]{3,2,1,0:T(8,128)(2,1)}, u32[]{:S(2)}) %copy-start) | copy-done | bytes 12582936
  15.7 0.9 copy-done.3
  16.6 0.9 copy-done.4
  17.5 3.7 %shard_map.122.w_ref.refs_3_ = bf16[4096,1536]{1,0:T(8,128)(2,1)S(1)} custom-call(s32[2]{0:T(128)S(1)} %pad_add_fusion.place_ref, bf16[2,4096,768]{2,1,0:T(8,128)(2,1)S(1)} %bitcast.7, f32[2,32,768]{2,1,0:T(8,128)S(1)} %bitcast.11, f32[2,32,768]{2,1,0:T(8,128)S(1)} %bitcast.12), custom_call_target="tpu_custom_call" | custom-call | bytes 25 | tf_op jit(solution)/shard_map/pallas_call | solution.py:112
  21.3 2.3 %shard_map.123.refs_2_.w_ref = bf16[1536,2048]{1,0:T(8,128)(2,1)S(1)} custom-call(s32[2]{0:T(128)S(1)} %pad_add_fusion.place_ref, bf16[1,1536,2048]{2,1,0:T(8,128)(2,1)S(1)} %copy-done.1, f32[1,12,2048]{2,1,0:T(8,128)S(1)} %copy.17.low_ref, f32[1,12,2048]{2,1,0:T(8,128)S(1)} %copy.18.high_ref), custom_call_target="tpu_custom_call" | custom-call | bytes 12 | tf_op jit(solution)/shard_map/pallas_call | solution.py:112
  25.3 4.7 %collective-permute-done.5 = bf16[32,128]{1,0:T(8,128)(2,1)S(1)} collective-permute-done((bf16[32,128]{1,0:T(8,128)(2,1)S(1)}, bf16[32,128]{1,0:T(8,128)(2,1)S(1)}, u32[]{:S(2)}, u32[]{:S(2)}) %collective-permute-start.5) | collective-permute-done | bytes 8224 | tf_op jit(solution)/shard_map/ppermute | solution.py:17
  29.9 2.0 %collective-permute-done.3.refs_2_ = bf16[32,4096]{1,0:T(8,128)(2,1)S(1)} collective-permute-done((bf16[32,4096]{1,0:T(8,128)(2,1)S(1)}, bf16[32,4096]{1,0:T(8,128)(2,1)S(1)}, u32[]{:S(2)}, u32[]{:S(2)}) %collective-permute-start.3) | collective-permute-done | bytes 262176 | tf_op jit(solution)/shard_map/ppermute | solution.py:17
  31.9 5.2 %collective-permute-done.4.refs_1_ = bf16[64,4096]{1,0:T(8,128)(2,1)S(1)} collective-permute-done((bf16[64,4096]{1,0:T(8,128)(2,1)S(1)}, bf16[64,4096]{1,0:T(8,128)(2,1)S(1)}, u32[]{:S(2)}, u32[]{:S(2)}) %collective-permute-start.4) | collective-permute-done | bytes 524320 | tf_op jit(solution)/shard_map/ppermute | solution.py:17
  38.9 1.6 collective-permute-done.6.other_ref.refs_1_
  40.5 4.1 %shard_map.126 = (bf16[256,768]{1,0:T(8,128)(2,1)S(1)}, f32[256,768]{1,0:T(8,128)S(1)}, f32[256,768]{1,0:T(8,128)S(1)}) custom-call(s32[2]{0:T(128)S(1)} %pad_add_fusion.place_ref, bf16[128,4096]{1,0:T(8,128)(2,1)S(1)} %shard_map.125.own_ref.refs_0_, bf16[128,4096]{1,0:T(8,128)(2,1)S(1)} %collective-permute-done.6.other_ref.refs_1_, ...), custom_call_target="tpu_custom_call" | custom-call | flops 3221 | bytes 16 | tf_op jit(solution)/shard_map/pallas_call | solution.py:112
  44.6 2.0 %collective-permute-done.12.refs_2_ = bf16[32,4096]{1,0:T(8,128)(2,1)S(1)} collective-permute-done((bf16[32,4096]{1,0:T(8,128)(2,1)S(1)}, bf16[32,4096]{1,0:T(8,128)(2,1)S(1)}, u32[]{:S(2)}, u32[]{:S(2)}) %collective-permute-start.12) | collective-permute-done | bytes 262176 | tf_op jit(solution)/shard_map/ppermute | solution.py:17
  47.2 1.6 collective-permute-start.7
  48.8 1.1 collective-permute-done.13.other_ref.refs_3_
  49.9 4.1 %shard_map.129 = (bf16[256,768]{1,0:T(8,128)(2,1)S(1)}, f32[256,768]{1,0:T(8,128)S(1)}, f32[256,768]{1,0:T(8,128)S(1)}) custom-call(s32[2]{0:T(128)S(1)} %pad_add_fusion.place_ref, bf16[128,4096]{1,0:T(8,128)(2,1)S(1)} %shard_map.128.own_ref.refs_2_, bf16[128,4096]{1,0:T(8,128)(2,1)S(1)} %collective-permute-done.13.other_ref.refs_3_, ...), custom_call_target="tpu_custom_call" | custom-call | flops 3221 | bytes 16 | tf_op jit(solution)/shard_map/pallas_call | solution.py:112
  54.0 1.6 collective-permute-start.14
  56.1 3.4 %collective-permute-done.9 = bf16[128,128]{1,0:T(8,128)(2,1)S(1)} collective-permute-done((bf16[128,128]{1,0:T(8,128)(2,1)S(1)}, bf16[128,128]{1,0:T(8,128)(2,1)S(1)}, u32[]{:S(2)}, u32[]{:S(2)}) %collective-permute-start.9) | collective-permute-done | bytes 32800 | tf_op jit(solution)/shard_map/ppermute | solution.py:17
  59.5 1.2 collective-permute-done.10.refs_4_.other_ref
  60.7 2.3 %shard_map.127 = (bf16[128,2048]{1,0:T(8,128)(2,1)S(1)}, bf16[128,2048]{1,0:T(8,128)(2,1)S(1)}) custom-call(s32[2]{0:T(128)S(1)} %pad_add_fusion.place_ref, bf16[256,768]{1,0:T(8,128)(2,1)S(1)} %get-tuple-element.57.refs_0_, bf16[256,768]{1,0:T(8,128)(2,1)S(1)} %collective-permute-done.7.refs_1_, bf16[1536,2048]{1,0:T(8,128)(2,1)S(1)} %shard_map.123.refs_2_.w_ref, ...), custom_call_target="tpu_custom_call" | custom-call | flops 1610 | bytes 8 | tf_op jit(solution)/shard_map/pallas_call | solution.py:112
  63.1 4.1 %collective-permute-done.14.refs_1_.refs_3_ = bf16[256,768]{1,0:T(8,128)(2,1)S(1)} collective-permute-done((bf16[256,768]{1,0:T(8,128)(2,1)S(1)}, bf16[256,768]{1,0:T(8,128)(2,1)S(1)}, u32[]{:S(2)}, u32[]{:S(2)}) %collective-permute-start.14) | collective-permute-done | bytes 393248 | tf_op jit(solution)/shard_map/ppermute | solution.py:17
  67.2 2.3 %shard_map.130 = (bf16[128,2048]{1,0:T(8,128)(2,1)S(1)}, bf16[128,2048]{1,0:T(8,128)(2,1)S(1)}) custom-call(s32[2]{0:T(128)S(1)} %pad_add_fusion.place_ref, bf16[256,768]{1,0:T(8,128)(2,1)S(1)} %get-tuple-element.61.refs_0_.refs_2_, bf16[256,768]{1,0:T(8,128)(2,1)S(1)} %collective-permute-done.14.refs_1_.refs_3_, ...), custom_call_target="tpu_custom_call" | custom-call | flops 1610 | bytes 8 | tf_op jit(solution)/shard_map/pallas_call | solution.py:112
  70.1 1.4 collective-permute-done.15
  72.2 1.5 collective-permute-start.16
  73.8 4.2 %collective-permute-done.17 = bf16[64,1024]{1,0:T(8,128)(2,1)S(1)} collective-permute-done((bf16[64,1024]{1,0:T(8,128)(2,1)S(1)}, bf16[64,1024]{1,0:T(8,128)(2,1)S(1)}, u32[]{:S(2)}, u32[]{:S(2)}) %collective-permute-start.17) | collective-permute-done | bytes 131104 | tf_op jit(solution)/shard_map/ppermute | solution.py:17
  78.0 2.0 %collective-permute-done.16 = bf16[64,1024]{1,0:T(8,128)(2,1)S(1)} collective-permute-done((bf16[64,1024]{1,0:T(8,128)(2,1)S(1)}, bf16[64,1024]{1,0:T(8,128)(2,1)S(1)}, u32[]{:S(2)}, u32[]{:S(2)}) %collective-permute-start.16) | collective-permute-done | bytes 131104 | tf_op jit(solution)/shard_map/ppermute | solution.py:17
  81.2 1.6 collective-permute-start.19
  82.8 3.8 %collective-permute-done.21 = bf16[64,1024]{1,0:T(8,128)(2,1)S(1)} collective-permute-done((bf16[64,1024]{1,0:T(8,128)(2,1)S(1)}, bf16[64,1024]{1,0:T(8,128)(2,1)S(1)}, u32[]{:S(2)}, u32[]{:S(2)}) %collective-permute-start.21) | collective-permute-done | bytes 131104 | tf_op jit(solution)/shard_map/ppermute | solution.py:17
  86.6 1.4 collective-permute-done.19
  88.4 2.6 %collective-permute-start.20 = (bf16[32,1024]{1,0:T(8,128)(2,1)S(1)}, bf16[32,1024]{1,0:T(8,128)(2,1)S(1)}, u32[]{:S(2)}, u32[]{:S(2)}) collective-permute-start(bf16[32,1024]{1,0:T(8,128)(2,1)S(1)} %get-tuple-element.109), channel_id=1, source_target_pairs={{0,16},{2,18},{4,20},{6,22},{8,24},{10,26},{12,28},{14,30},{16,0},... | collective-permute-start | bytes 196616 | tf_op jit(solution)/shard_map/ppermute | solution.py:17
  91.0 3.5 %collective-permute-done.22 = bf16[32,1024]{1,0:T(8,128)(2,1)S(1)} collective-permute-done((bf16[32,1024]{1,0:T(8,128)(2,1)S(1)}, bf16[32,1024]{1,0:T(8,128)(2,1)S(1)}, u32[]{:S(2)}, u32[]{:S(2)}) %collective-permute-start.22) | collective-permute-done | bytes 65568 | tf_op jit(solution)/shard_map/ppermute | solution.py:17
  94.6 1.4 collective-permute-done.20
  96.4 2.7 %collective-permute-start.23 = (bf16[32,1024]{1,0:T(8,128)(2,1)S(1)}, bf16[32,1024]{1,0:T(8,128)(2,1)S(1)}, u32[]{:S(2)}, u32[]{:S(2)}) collective-permute-start(bf16[32,1024]{1,0:T(8,128)(2,1)S(1)} %get-tuple-element.107.refs_0_), channel_id=1, source_target_pairs={{0,16},{2,18},{4,20},{6,22},{8,24},{10,26},{12,28},{14,30},{16,0},... | collective-permute-start | bytes 196616 | tf_op jit(solution)/shard_map/ppermute | solution.py:17
  99.1 2.9 %collective-permute-done.24.refs_3_ = bf16[32,1024]{1,0:T(8,128)(2,1)S(1)} collective-permute-done((bf16[32,1024]{1,0:T(8,128)(2,1)S(1)}, bf16[32,1024]{1,0:T(8,128)(2,1)S(1)}, u32[]{:S(2)}, u32[]{:S(2)}) %collective-permute-start.24) | collective-permute-done | bytes 65568 | tf_op jit(solution)/shard_map/ppermute | solution.py:17
  103.3 1.6 collective-permute-start.26
  105.1 2.1 %collective-permute-start.25 = (bf16[64,1024]{1,0:T(8,128)(2,1)S(1)}, bf16[64,1024]{1,0:T(8,128)(2,1)S(1)}, u32[]{:S(2)}, u32[]{:S(2)}) collective-permute-start(bf16[64,1024]{1,0:T(8,128)(2,1)S(1)} %pad_maximum_fusion), channel_id=1, source_target_pairs={{0,8},{2,10},{4,12},{6,14},{8,0},{10,2},{12,4},{14,6},{16,24},{18,... | collective-permute-start | bytes 393224 | tf_op jit(solution)/shard_map/ppermute | solution.py:17
  107.1 2.9 %collective-permute-done.27.refs_2_ = bf16[64,1024]{1,0:T(8,128)(2,1)S(1)} collective-permute-done((bf16[64,1024]{1,0:T(8,128)(2,1)S(1)}, bf16[64,1024]{1,0:T(8,128)(2,1)S(1)}, u32[]{:S(2)}, u32[]{:S(2)}) %collective-permute-start.27) | collective-permute-done | bytes 131104 | tf_op jit(solution)/shard_map/ppermute | solution.py:17
  110.0 1.4 collective-permute-done.25.refs_1_
  112.6 1.6 collective-permute-start.30
  114.2 2.6 %shard_map.133 = (bf16[256,2048]{1,0:T(8,128)(2,1)S(1)}, f32[256,768]{1,0:T(8,128)S(1)}, bf16[256,768]{1,0:T(8,128)(2,1)S(1)}) custom-call(s32[2]{0:T(128)S(1)} %pad_add_fusion.place_ref, bf16[128,2048]{1,0:T(8,128)(2,1)S(1)} %shard_map.132.err_own_ref, bf16[128,2048]{1,0:T(8,128)(2,1)S(1)} %collective-permute-done.28.err_other_ref, ...), custom_call_target="tpu_custom_call" | custom-call | flops 1610 | bytes 9 | tf_op jit(solution)/shard_map/pallas_call | solution.py:112
  116.8 1.6 collective-permute-done.31.refs_2_
  118.4 2.4 %collective-permute-done.30.refs_1_ = bf16[64,1024]{1,0:T(8,128)(2,1)S(1)} collective-permute-done((bf16[64,1024]{1,0:T(8,128)(2,1)S(1)}, bf16[64,1024]{1,0:T(8,128)(2,1)S(1)}, u32[]{:S(2)}, u32[]{:S(2)}) %collective-permute-start.30) | collective-permute-done | bytes 131104 | tf_op jit(solution)/shard_map/ppermute | solution.py:17
  121.4 1.6 collective-permute-start.29
  123.3 2.4 %shard_map.135 = (bf16[256,2048]{1,0:T(8,128)(2,1)S(1)}, f32[256,768]{1,0:T(8,128)S(1)}, bf16[256,768]{1,0:T(8,128)(2,1)S(1)}) custom-call(s32[2]{0:T(128)S(1)} %pad_add_fusion.place_ref, bf16[128,2048]{1,0:T(8,128)(2,1)S(1)} %shard_map.134.err_own_ref, bf16[128,2048]{1,0:T(8,128)(2,1)S(1)} %collective-permute-done.32.err_other_ref, ...), custom_call_target="tpu_custom_call" | custom-call | flops 1610 | bytes 9 | tf_op jit(solution)/shard_map/pallas_call | solution.py:112
  125.8 1.6 collective-permute-start.33
  127.4 5.6 %shard_map.136 = f32[2,12,2048]{2,1,0:T(8,128)S(1)} custom-call(s32[2]{0:T(128)S(1)} %pad_add_fusion.place_ref, bf16[256,768]{1,0:T(8,128)(2,1)S(1)} %get-tuple-element.57.refs_0_, bf16[256,768]{1,0:T(8,128)(2,1)S(1)} %collective-permute-done.7.refs_1_, bf16[256,768]{1,0:T(8,128)(2,1)S(1)} %get-tuple-element.61.refs_0_.refs_2_, ...), custom_call_target="tpu_custom_call" | custom-call | flops 3221 | bytes 10 | tf_op jit(solution)/shard_map/pallas_call | solution.py:112
  133.4 4.0 %shard_map.137 = (bf16[256,1536]{1,0:T(8,128)(2,1)S(1)}, bf16[128,2048]{1,0:T(8,128)(2,1)S(1)}, bf16[128,2048]{1,0:T(8,128)(2,1)S(1)}, bf16[128,2048]{1,0:T(8,128)(2,1)S(1)}, bf16[128,2048]{1,0:T(8,128)(2,1)S(1)}) custom-call(s32[2]{0:T(128)S(1)} %pad_add_fusion.place_ref, f32[256,768]{1,0:T(8,128)S(1)} %get-tuple-element.68.grad_own_ref, ...), custom_call_target="tpu_custom_call" | custom-call | flops 3221 | bytes 18 | tf_op jit(solution)/shard_map/pallas_call | solution.py:112
  137.5 3.9 %collective-permute-done.33.refs_0_ = bf16[256,768]{1,0:T(8,128)(2,1)S(1)} collective-permute-done((bf16[256,768]{1,0:T(8,128)(2,1)S(1)}, bf16[256,768]{1,0:T(8,128)(2,1)S(1)}, u32[]{:S(2)}, u32[]{:S(2)}) %collective-permute-start.33) | collective-permute-done | bytes 393248 | tf_op jit(solution)/shard_map/ppermute | solution.py:17
  141.4 4.0 %shard_map.138 = (bf16[256,1536]{1,0:T(8,128)(2,1)S(1)}, bf16[128,2048]{1,0:T(8,128)(2,1)S(1)}, bf16[128,2048]{1,0:T(8,128)(2,1)S(1)}, bf16[128,2048]{1,0:T(8,128)(2,1)S(1)}, bf16[128,2048]{1,0:T(8,128)(2,1)S(1)}) custom-call(s32[2]{0:T(128)S(1)} %pad_add_fusion.place_ref, f32[256,768]{1,0:T(8,128)S(1)} %get-tuple-element.78.grad_own_ref, ...), custom_call_target="tpu_custom_call" | custom-call | flops 3221 | bytes 18 | tf_op jit(solution)/shard_map/pallas_call | solution.py:112
  146.0 1.4 collective-permute-done.36
  148.6 1.5 collective-permute-start.38
  150.1 5.8 %collective-permute-done.37 = bf16[64,2048]{1,0:T(8,128)(2,1)S(1)} collective-permute-done((bf16[64,2048]{1,0:T(8,128)(2,1)S(1)}, bf16[64,2048]{1,0:T(8,128)(2,1)S(1)}, u32[]{:S(2)}, u32[]{:S(2)}) %collective-permute-start.37) | collective-permute-done | bytes 262176 | tf_op jit(solution)/shard_map/ppermute | solution.py:17
  156.8 1.5 collective-permute-start.39
  158.5 1.6 collective-permute-start.42
  160.1 6.3 %shard_map.139.refs_7_ = f32[4,32,768]{2,1,0:T(8,128)} custom-call(s32[2]{0:T(128)S(1)} %pad_add_fusion.place_ref, bf16[128,4096]{1,0:T(8,128)(2,1)S(1)} %shard_map.125.own_ref.refs_0_, bf16[128,4096]{1,0:T(8,128)(2,1)S(1)} %collective-permute-done.6.other_ref.refs_1_, bf16[128,4096]{1,0:T(8,128)(2,1)S(1)} %shard_map.128.own_ref.refs_2_, ...), custom_call_target="tpu_custom_call" | custom-call | flops 3221 | bytes 18 | tf_op jit(solution)/shard_map/pallas_call | solution.py:112
  167.1 0.8 collective-permute-start.44
  168.3 3.8 %shard_map.140.refs_7_ = f32[4,32,768]{2,1,0:T(8,128)} custom-call(s32[2]{0:T(128)S(1)} %pad_add_fusion.place_ref, bf16[128,4096]{1,0:T(8,128)(2,1)S(1)} %shard_map.125.own_ref.refs_0_, bf16[128,4096]{1,0:T(8,128)(2,1)S(1)} %collective-permute-done.6.other_ref.refs_1_, ...), custom_call_target="tpu_custom_call", output_to_operand_aliasing={{}: (8, {})} | custom-call | flops 1610 | bytes 18 | tf_op jit(solution)/shard_map/pallas_call | solution.py:112
  172.1 1.6 collective-permute-done.44
  174.3 2.2 %collective-permute-start.45 = (bf16[32,2048]{1,0:T(8,128)(2,1)S(1)}, bf16[32,2048]{1,0:T(8,128)(2,1)S(1)}, u32[]{:S(2)}, u32[]{:S(2)}) collective-permute-start(bf16[32,2048]{1,0:T(8,128)(2,1)S(1)} %add_convert_fusion.9), channel_id=1, source_target_pairs={{0,16},{2,18},{4,20},{6,22},{8,24},{10,26},{12,28},{14,30},{16,0},... | collective-permute-start | bytes 393224 | tf_op jit(solution)/shard_map/ppermute | solution.py:17
  176.5 0.8 copy.19
  177.3 3.8 %shard_map.141 = f32[4,32,768]{2,1,0:T(8,128)} custom-call(s32[2]{0:T(128)S(1)} %pad_add_fusion.place_ref, bf16[128,4096]{1,0:T(8,128)(2,1)S(1)} %shard_map.125.own_ref.refs_0_, bf16[128,4096]{1,0:T(8,128)(2,1)S(1)} %collective-permute-done.6.other_ref.refs_1_, bf16[128,4096]{1,0:T(8,128)(2,1)S(1)} %shard_map.128.own_ref.refs_2_, ...), custom_call_target="tpu_custom_call", output_to_operand_aliasing={{}: (8, {})} | custom-call | flops 1610 | bytes 18 | tf_op jit(solution)/shard_map/pallas_call | solution.py:112
  (92 shorter events, 19.4 us)
Async XLA Ops:
  0.6 23.0 %collective-permute-start.1 = (bf16[32,4096]{1,0:T(8,128)(2,1)}, bf16[32,4096]{1,0:T(8,128)(2,1)S(1)}, u32[]{:S(2)}, u32[]{:S(2)}) collective-permute-start(bf16[32,4096]{1,0:T(8,128)(2,1)} %refs_0_.1), channel_id=1, source_target_pairs={{0,4},{2,6},{4,0},{6,2},{8,12},{10,14},{12,8},{14,10},{16,20},{18,... | collective-permute-start | bytes 786440 | tf_op jit(solution)/shard_map/ppermute | solution.py:17
  3.6 20.0 %collective-permute-start = (bf16[32,4096]{1,0:T(8,128)(2,1)}, bf16[32,4096]{1,0:T(8,128)(2,1)S(1)}, u32[]{:S(2)}, u32[]{:S(2)}) collective-permute-start(bf16[32,4096]{1,0:T(8,128)(2,1)} %refs_0_.1), channel_id=1, source_target_pairs={{0,16},{2,18},{4,20},{6,22},{8,24},{10,26},{12,28},{14,30},{16,0},... | collective-permute-start | bytes 786440 | tf_op jit(solution)/shard_map/ppermute | solution.py:17
  6.2 17.4 %collective-permute-start.2 = (bf16[32,4096]{1,0:T(8,128)(2,1)}, bf16[32,4096]{1,0:T(8,128)(2,1)S(1)}, u32[]{:S(2)}, u32[]{:S(2)}) collective-permute-start(bf16[32,4096]{1,0:T(8,128)(2,1)} %refs_0_.1), channel_id=1, source_target_pairs={{0,8},{2,10},{4,12},{6,14},{8,0},{10,2},{12,4},{14,6},{16,24},{18,... | collective-permute-start | bytes 786440 | tf_op jit(solution)/shard_map/ppermute | solution.py:17
  11.1 4.6 %copy-start = (bf16[1,2,4096,768]{3,2,1,0:T(8,128)(2,1)S(1)}, bf16[1,2,4096,768]{3,2,1,0:T(8,128)(2,1)}, u32[]{:S(2)}) copy-start(bf16[1,2,4096,768]{3,2,1,0:T(8,128)(2,1)} %refs_6_.7) | copy-start | bytes 37748740
  15.7 0.9 copy-start.3
  16.6 0.9 copy-start.4
  17.5 3.8 %copy-start.6 = (f32[1,12,2048]{2,0,1:T(1,128)S(1)}, f32[1,12,2048]{2,0,1:T(1,128)}, u32[]{:S(2)}) copy-start(f32[1,12,2048]{2,0,1:T(1,128)} %param.18) | copy-start | bytes 294916
  17.5 3.8 %copy-start.1 = (bf16[1,1536,2048]{2,1,0:T(8,128)(2,1)S(1)}, bf16[1,1536,2048]{2,1,0:T(8,128)(2,1)}, u32[]{:S(2)}) copy-start(bf16[1,1536,2048]{2,1,0:T(8,128)(2,1)} %refs_6_.4) | copy-start | bytes 18874372
  21.3 15.8 %copy-start.2 = (bf16[32,4096]{1,0:T(8,128)(2,1)S(1)}, bf16[32,4096]{1,0:T(8,128)(2,1)}, u32[]{:S(2)}) copy-start(bf16[32,4096]{1,0:T(8,128)(2,1)} %refs_0_.1) | copy-start | bytes 786436
  24.2 12.9 %collective-permute-start.4 = (bf16[64,4096]{1,0:T(8,128)(2,1)S(1)}, bf16[64,4096]{1,0:T(8,128)(2,1)S(1)}, u32[]{:S(2)}, u32[]{:S(2)}) collective-permute-start(bf16[64,4096]{1,0:T(8,128)(2,1)S(1)} %shard_map.124.refs_1_), channel_id=1, source_target_pairs={{0,4},{2,6},{4,0},{6,2},{8,12},{10,14},{12,8},{14,10},{16,20},{18,... | collective-permute-start | bytes 1572872 | tf_op jit(solution)/shard_map/ppermute | solution.py:17
  24.8 7.1 %collective-permute-start.3 = (bf16[32,4096]{1,0:T(8,128)(2,1)S(1)}, bf16[32,4096]{1,0:T(8,128)(2,1)S(1)}, u32[]{:S(2)}, u32[]{:S(2)}) collective-permute-start(bf16[32,4096]{1,0:T(8,128)(2,1)S(1)} %collective-permute-done.refs_0_), channel_id=1, source_target_pairs={{0,8},{2,10},{4,12},{6,14},{8,0},{10,2},{12,4},{14,6},{16,24},{18,... | collective-permute-start | bytes 786440 | tf_op jit(solution)/shard_map/ppermute | solution.py:17
  25.3 4.7 %collective-permute-start.5 = (bf16[32,128]{1,0:T(8,128)(2,1)S(1)}, bf16[32,128]{1,0:T(8,128)(2,1)S(1)}, u32[]{:S(2)}, u32[]{:S(2)}) collective-permute-start(bf16[32,128]{1,0:T(8,128)(2,1)S(1)} %shard_map.121), channel_id=1, source_target_pairs={{0,16},{2,18},{4,20},{6,22},{8,24},{10,26},{12,28},{14,30},{16,0},... | collective-permute-start | bytes 24584 | tf_op jit(solution)/shard_map/ppermute | solution.py:17
  37.7 2.7 %collective-permute-start.6 = (bf16[128,4096]{1,0:T(8,128)(2,1)S(1)}, bf16[128,4096]{1,0:T(8,128)(2,1)S(1)}, u32[]{:S(2)}, u32[]{:S(2)}) collective-permute-start(bf16[128,4096]{1,0:T(8,128)(2,1)S(1)} %shard_map.125.own_ref.refs_0_), channel_id=1, source_target_pairs={{0,2},{2,0},{4,6},{6,4},{8,10},{10,8},{12,14},{14,12},{16,18},{18,... | collective-permute-start | bytes 3145736 | tf_op jit(solution)/shard_map/ppermute | solution.py:17
  37.8 8.7 %collective-permute-start.12 = (bf16[32,4096]{1,0:T(8,128)(2,1)S(1)}, bf16[32,4096]{1,0:T(8,128)(2,1)S(1)}, u32[]{:S(2)}, u32[]{:S(2)}) collective-permute-start(bf16[32,4096]{1,0:T(8,128)(2,1)S(1)} %collective-permute-done.3.refs_2_), channel_id=1, source_target_pairs={{0,4},{2,6},{4,0},{6,2},{8,12},{10,14},{12,8},{14,10},{16,20},{18,... | collective-permute-start | bytes 786440 | tf_op jit(solution)/shard_map/ppermute | solution.py:17
  38.4 6.1 %collective-permute-start.8 = (bf16[64,128]{1,0:T(8,128)(2,1)S(1)}, bf16[64,128]{1,0:T(8,128)(2,1)S(1)}, u32[]{:S(2)}, u32[]{:S(2)}) collective-permute-start(bf16[64,128]{1,0:T(8,128)(2,1)S(1)} %pad_maximum_fusion.4), channel_id=1, source_target_pairs={{0,8},{2,10},{4,12},{6,14},{8,0},{10,2},{12,4},{14,6},{16,24},{18,... | collective-permute-start | bytes 49160 | tf_op jit(solution)/shard_map/ppermute | solution.py:17
  47.2 2.7 %collective-permute-start.13 = (bf16[128,4096]{1,0:T(8,128)(2,1)S(1)}, bf16[128,4096]{1,0:T(8,128)(2,1)S(1)}, u32[]{:S(2)}, u32[]{:S(2)}) collective-permute-start(bf16[128,4096]{1,0:T(8,128)(2,1)S(1)} %shard_map.128.own_ref.refs_2_), channel_id=1, source_target_pairs={{0,2},{2,0},{4,6},{6,4},{8,10},{10,8},{12,14},{14,12},{16,18},{18,... | collective-permute-start | bytes 3145736 | tf_op jit(solution)/shard_map/ppermute | solution.py:17
  47.2 13.5 %collective-permute-start.7 = (bf16[256,768]{1,0:T(8,128)(2,1)S(1)}, bf16[256,768]{1,0:T(8,128)(2,1)S(1)}, u32[]{:S(2)}, u32[]{:S(2)}) collective-permute-start(bf16[256,768]{1,0:T(8,128)(2,1)S(1)} %get-tuple-element.57.refs_0_), channel_id=1, source_target_pairs={{0,1},{1,0},{2,3},{3,2},{4,5},{5,4},{6,7},{7,6},{8,9},{9,8},{10,11... | collective-permute-start | bytes 1179656 | tf_op jit(solution)/shard_map/ppermute | solution.py:17
  54.0 42.0 %copy-start.5 = (bf16[32,2048]{1,0:T(8,128)(2,1)S(1)}, bf16[32,2048]{1,0:T(8,128)(2,1)}, u32[]{:S(2)}) copy-start(bf16[32,2048]{1,0:T(8,128)(2,1)} %param.11) | copy-start | bytes 393220
  54.0 13.2 %collective-permute-start.14 = (bf16[256,768]{1,0:T(8,128)(2,1)S(1)}, bf16[256,768]{1,0:T(8,128)(2,1)S(1)}, u32[]{:S(2)}, u32[]{:S(2)}) collective-permute-start(bf16[256,768]{1,0:T(8,128)(2,1)S(1)} %get-tuple-element.61.refs_0_.refs_2_), channel_id=1, source_target_pairs={{0,1},{1,0},{2,3},{3,2},{4,5},{5,4},{6,7},{7,6},{8,9},{9,8},{10,11... | collective-permute-start | bytes 1179656 | tf_op jit(solution)/shard_map/ppermute | solution.py:17
  55.6 3.9 %collective-permute-start.9 = (bf16[128,128]{1,0:T(8,128)(2,1)S(1)}, bf16[128,128]{1,0:T(8,128)(2,1)S(1)}, u32[]{:S(2)}, u32[]{:S(2)}) collective-permute-start(bf16[128,128]{1,0:T(8,128)(2,1)S(1)} %pad_maximum_fusion.3), channel_id=1, source_target_pairs={{0,4},{2,6},{4,0},{6,2},{8,12},{10,14},{12,8},{14,10},{16,20},{18,... | collective-permute-start | bytes 98312 | tf_op jit(solution)/shard_map/ppermute | solution.py:17
  59.5 1.3 collective-permute-start.10
  69.5 2.0 %collective-permute-start.15 = (bf16[128,2048]{1,0:T(8,128)(2,1)S(1)}, bf16[128,2048]{1,0:T(8,128)(2,1)S(1)}, u32[]{:S(2)}, u32[]{:S(2)}) collective-permute-start(bf16[128,2048]{1,0:T(8,128)(2,1)S(1)} %get-tuple-element.64), channel_id=1, source_target_pairs={{0,2},{2,0},{4,6},{6,4},{8,10},{10,8},{12,14},{14,12},{16,18},{18,... | collective-permute-start | bytes 1572872 | tf_op jit(solution)/shard_map/ppermute | solution.py:17
  69.6 10.9 %collective-permute-start.11 = (bf16[128,2048]{1,0:T(8,128)(2,1)S(1)}, bf16[128,2048]{1,0:T(8,128)(2,1)S(1)}, u32[]{:S(2)}, u32[]{:S(2)}) collective-permute-start(bf16[128,2048]{1,0:T(8,128)(2,1)S(1)} %get-tuple-element.59), channel_id=1, source_target_pairs={{0,2},{2,0},{4,6},{6,4},{8,10},{10,8},{12,14},{14,12},{16,18},{18,... | collective-permute-start | bytes 1572872 | tf_op jit(solution)/shard_map/ppermute | solution.py:17
  71.6 6.4 %collective-permute-start.17 = (bf16[64,1024]{1,0:T(8,128)(2,1)S(1)}, bf16[64,1024]{1,0:T(8,128)(2,1)S(1)}, u32[]{:S(2)}, u32[]{:S(2)}) collective-permute-start(bf16[64,1024]{1,0:T(8,128)(2,1)S(1)} %get-tuple-element.118), channel_id=1, source_target_pairs={{0,4},{2,6},{4,0},{6,2},{8,12},{10,14},{12,8},{14,10},{16,20},{18,... | collective-permute-start | bytes 393224 | tf_op jit(solution)/shard_map/ppermute | solution.py:17
  72.2 7.8 %collective-permute-start.16 = (bf16[64,1024]{1,0:T(8,128)(2,1)S(1)}, bf16[64,1024]{1,0:T(8,128)(2,1)S(1)}, u32[]{:S(2)}, u32[]{:S(2)}) collective-permute-start(bf16[64,1024]{1,0:T(8,128)(2,1)S(1)} %get-tuple-element.119), channel_id=1, source_target_pairs={{0,4},{2,6},{4,0},{6,2},{8,12},{10,14},{12,8},{14,10},{16,20},{18,... | collective-permute-start | bytes 393224 | tf_op jit(solution)/shard_map/ppermute | solution.py:17
  80.0 8.0 %collective-permute-start.18 = (bf16[64,2048]{1,0:T(8,128)(2,1)S(1)}, bf16[64,2048]{1,0:T(8,128)(2,1)S(1)}, u32[]{:S(2)}, u32[]{:S(2)}) collective-permute-start(bf16[64,2048]{1,0:T(8,128)(2,1)S(1)} %add_convert_fusion.7), channel_id=1, source_target_pairs={{0,4},{2,6},{4,0},{6,2},{8,12},{10,14},{12,8},{14,10},{16,20},{18,... | collective-permute-start | bytes 786440 | tf_op jit(solution)/shard_map/ppermute | solution.py:17
  80.7 5.9 %collective-permute-start.21 = (bf16[64,1024]{1,0:T(8,128)(2,1)S(1)}, bf16[64,1024]{1,0:T(8,128)(2,1)S(1)}, u32[]{:S(2)}, u32[]{:S(2)}) collective-permute-start(bf16[64,1024]{1,0:T(8,128)(2,1)S(1)} %get-tuple-element.116), channel_id=1, source_target_pairs={{0,8},{2,10},{4,12},{6,14},{8,0},{10,2},{12,4},{14,6},{16,24},{18,... | collective-permute-start | bytes 393224 | tf_op jit(solution)/shard_map/ppermute | solution.py:17
  81.2 6.8 %collective-permute-start.19 = (bf16[64,1024]{1,0:T(8,128)(2,1)S(1)}, bf16[64,1024]{1,0:T(8,128)(2,1)S(1)}, u32[]{:S(2)}, u32[]{:S(2)}) collective-permute-start(bf16[64,1024]{1,0:T(8,128)(2,1)S(1)} %get-tuple-element.117), channel_id=1, source_target_pairs={{0,8},{2,10},{4,12},{6,14},{8,0},{10,2},{12,4},{14,6},{16,24},{18,... | collective-permute-start | bytes 393224 | tf_op jit(solution)/shard_map/ppermute | solution.py:17
  88.0 6.5 %collective-permute-start.22 = (bf16[32,1024]{1,0:T(8,128)(2,1)S(1)}, bf16[32,1024]{1,0:T(8,128)(2,1)S(1)}, u32[]{:S(2)}, u32[]{:S(2)}) collective-permute-start(bf16[32,1024]{1,0:T(8,128)(2,1)S(1)} %get-tuple-element.108), channel_id=1, source_target_pairs={{0,16},{2,18},{4,20},{6,22},{8,24},{10,26},{12,28},{14,30},{16,0},... | collective-permute-start | bytes 196616 | tf_op jit(solution)/shard_map/ppermute | solution.py:17
  88.4 7.5 %collective-permute-start.20 = (bf16[32,1024]{1,0:T(8,128)(2,1)S(1)}, bf16[32,1024]{1,0:T(8,128)(2,1)S(1)}, u32[]{:S(2)}, u32[]{:S(2)}) collective-permute-start(bf16[32,1024]{1,0:T(8,128)(2,1)S(1)} %get-tuple-element.109), channel_id=1, source_target_pairs={{0,16},{2,18},{4,20},{6,22},{8,24},{10,26},{12,28},{14,30},{16,0},... | collective-permute-start | bytes 196616 | tf_op jit(solution)/shard_map/ppermute | solution.py:17
  96.1 5.9 %collective-permute-start.24 = (bf16[32,1024]{1,0:T(8,128)(2,1)S(1)}, bf16[32,1024]{1,0:T(8,128)(2,1)S(1)}, u32[]{:S(2)}, u32[]{:S(2)}) collective-permute-start(bf16[32,1024]{1,0:T(8,128)(2,1)S(1)} %get-tuple-element.106.refs_1_), channel_id=1, source_target_pairs={{0,16},{2,18},{4,20},{6,22},{8,24},{10,26},{12,28},{14,30},{16,0},... | collective-permute-start | bytes 196616 | tf_op jit(solution)/shard_map/ppermute | solution.py:17
  96.4 6.4 %collective-permute-start.23 = (bf16[32,1024]{1,0:T(8,128)(2,1)S(1)}, bf16[32,1024]{1,0:T(8,128)(2,1)S(1)}, u32[]{:S(2)}, u32[]{:S(2)}) collective-permute-start(bf16[32,1024]{1,0:T(8,128)(2,1)S(1)} %get-tuple-element.107.refs_0_), channel_id=1, source_target_pairs={{0,16},{2,18},{4,20},{6,22},{8,24},{10,26},{12,28},{14,30},{16,0},... | collective-permute-start | bytes 196616 | tf_op jit(solution)/shard_map/ppermute | solution.py:17
  103.3 6.7 %collective-permute-start.26 = (bf16[64,2048]{1,0:T(8,128)(2,1)S(1)}, bf16[64,2048]{1,0:T(8,128)(2,1)S(1)}, u32[]{:S(2)}, u32[]{:S(2)}) collective-permute-start(bf16[64,2048]{1,0:T(8,128)(2,1)S(1)} %shard_map.131.refs_0_), channel_id=1, source_target_pairs={{0,4},{2,6},{4,0},{6,2},{8,12},{10,14},{12,8},{14,10},{16,20},{18,... | collective-permute-start | bytes 786440 | tf_op jit(solution)/shard_map/ppermute | solution.py:17
  105.0 5.0 %collective-permute-start.27 = (bf16[64,1024]{1,0:T(8,128)(2,1)S(1)}, bf16[64,1024]{1,0:T(8,128)(2,1)S(1)}, u32[]{:S(2)}, u32[]{:S(2)}) collective-permute-start(bf16[64,1024]{1,0:T(8,128)(2,1)S(1)} %pad_maximum_fusion.1), channel_id=1, source_target_pairs={{0,8},{2,10},{4,12},{6,14},{8,0},{10,2},{12,4},{14,6},{16,24},{18,... | collective-permute-start | bytes 393224 | tf_op jit(solution)/shard_map/ppermute | solution.py:17
  105.1 6.3 %collective-permute-start.25 = (bf16[64,1024]{1,0:T(8,128)(2,1)S(1)}, bf16[64,1024]{1,0:T(8,128)(2,1)S(1)}, u32[]{:S(2)}, u32[]{:S(2)}) collective-permute-start(bf16[64,1024]{1,0:T(8,128)(2,1)S(1)} %pad_maximum_fusion), channel_id=1, source_target_pairs={{0,8},{2,10},{4,12},{6,14},{8,0},{10,2},{12,4},{14,6},{16,24},{18,... | collective-permute-start | bytes 393224 | tf_op jit(solution)/shard_map/ppermute | solution.py:17
  112.0 2.2 %collective-permute-start.28 = (bf16[128,2048]{1,0:T(8,128)(2,1)S(1)}, bf16[128,2048]{1,0:T(8,128)(2,1)S(1)}, u32[]{:S(2)}, u32[]{:S(2)}) collective-permute-start(bf16[128,2048]{1,0:T(8,128)(2,1)S(1)} %shard_map.132.err_own_ref), channel_id=1, source_target_pairs={{0,2},{2,0},{4,6},{6,4},{8,10},{10,8},{12,14},{14,12},{16,18},{18,... | collective-permute-start | bytes 1572872 | tf_op jit(solution)/shard_map/ppermute | solution.py:17
  112.1 6.4 %collective-permute-start.31 = (bf16[64,1024]{1,0:T(8,128)(2,1)S(1)}, bf16[64,1024]{1,0:T(8,128)(2,1)S(1)}, u32[]{:S(2)}, u32[]{:S(2)}) collective-permute-start(bf16[64,1024]{1,0:T(8,128)(2,1)S(1)} %collective-permute-done.27.refs_2_), channel_id=1, source_target_pairs={{0,4},{2,6},{4,0},{6,2},{8,12},{10,14},{12,8},{14,10},{16,20},{18,... | collective-permute-start | bytes 393224 | tf_op jit(solution)/shard_map/ppermute | solution.py:17
  112.6 8.2 %collective-permute-start.30 = (bf16[64,1024]{1,0:T(8,128)(2,1)S(1)}, bf16[64,1024]{1,0:T(8,128)(2,1)S(1)}, u32[]{:S(2)}, u32[]{:S(2)}) collective-permute-start(bf16[64,1024]{1,0:T(8,128)(2,1)S(1)} %collective-permute-done.25.refs_1_), channel_id=1, source_target_pairs={{0,4},{2,6},{4,0},{6,2},{8,12},{10,14},{12,8},{14,10},{16,20},{18,... | collective-permute-start | bytes 393224 | tf_op jit(solution)/shard_map/ppermute | solution.py:17
  121.4 2.0 %collective-permute-start.32 = (bf16[128,2048]{1,0:T(8,128)(2,1)S(1)}, bf16[128,2048]{1,0:T(8,128)(2,1)S(1)}, u32[]{:S(2)}, u32[]{:S(2)}) collective-permute-start(bf16[128,2048]{1,0:T(8,128)(2,1)S(1)} %shard_map.134.err_own_ref), channel_id=1, source_target_pairs={{0,2},{2,0},{4,6},{6,4},{8,10},{10,8},{12,14},{14,12},{16,18},{18,... | collective-permute-start | bytes 1572872 | tf_op jit(solution)/shard_map/ppermute | solution.py:17
  121.4 12.0 %collective-permute-start.29 = (bf16[256,768]{1,0:T(8,128)(2,1)S(1)}, bf16[256,768]{1,0:T(8,128)(2,1)S(1)}, u32[]{:S(2)}, u32[]{:S(2)}) collective-permute-start(bf16[256,768]{1,0:T(8,128)(2,1)S(1)} %get-tuple-element.69), channel_id=1, source_target_pairs={{0,1},{1,0},{2,3},{3,2},{4,5},{5,4},{6,7},{7,6},{8,9},{9,8},{10,11... | collective-permute-start | bytes 1179656 | tf_op jit(solution)/shard_map/ppermute | solution.py:17
  125.8 15.6 %collective-permute-start.33 = (bf16[256,768]{1,0:T(8,128)(2,1)S(1)}, bf16[256,768]{1,0:T(8,128)(2,1)S(1)}, u32[]{:S(2)}, u32[]{:S(2)}) collective-permute-start(bf16[256,768]{1,0:T(8,128)(2,1)S(1)} %get-tuple-element.79), channel_id=1, source_target_pairs={{0,1},{1,0},{2,3},{3,2},{4,5},{5,4},{6,7},{7,6},{8,9},{9,8},{10,11... | collective-permute-start | bytes 1179656 | tf_op jit(solution)/shard_map/ppermute | solution.py:17
  133.4 26.7 %slice-start = ((s8[12582912]{0:T(1024)(128)(4,1)}), s8[4194304]{0:T(1024)(128)(4,1)S(1)}, s32[]{:S(2)}) async-start(s8[12582912]{0:T(1024)(128)(4,1)} %bitcast.8), calls=%async_computation | async-start | bytes 8388608
  133.4 26.7 %slice-start.1 = ((s8[12582912]{0:T(1024)(128)(4,1)}), s8[4194304]{0:T(1024)(128)(4,1)S(1)}, s32[]{:S(2)}) async-start(s8[12582912]{0:T(1024)(128)(4,1)} %bitcast.8), calls=%async_computation.1 | async-start | bytes 8388608
  141.4 18.7 %slice-start.2 = ((s8[12582912]{0:T(1024)(128)(4,1)}), s8[4194304]{0:T(1024)(128)(4,1)S(1)}, s32[]{:S(2)}) async-start(s8[12582912]{0:T(1024)(128)(4,1)} %bitcast.8), calls=%async_computation.2 | async-start | bytes 8388608
  145.4 2.0 %collective-permute-start.36 = (bf16[128,2048]{1,0:T(8,128)(2,1)S(1)}, bf16[128,2048]{1,0:T(8,128)(2,1)S(1)}, u32[]{:S(2)}, u32[]{:S(2)}) collective-permute-start(bf16[128,2048]{1,0:T(8,128)(2,1)S(1)} %get-tuple-element.93), channel_id=1, source_target_pairs={{0,2},{2,0},{4,6},{6,4},{8,10},{10,8},{12,14},{14,12},{16,18},{18,... | collective-permute-start | bytes 1572872 | tf_op jit(solution)/shard_map/ppermute | solution.py:17
  145.5 4.6 %collective-permute-start.35 = (bf16[128,2048]{1,0:T(8,128)(2,1)S(1)}, bf16[128,2048]{1,0:T(8,128)(2,1)S(1)}, u32[]{:S(2)}, u32[]{:S(2)}) collective-permute-start(bf16[128,2048]{1,0:T(8,128)(2,1)S(1)} %get-tuple-element.91), channel_id=1, source_target_pairs={{0,2},{2,0},{4,6},{6,4},{8,10},{10,8},{12,14},{14,12},{16,18},{18,... | collective-permute-start | bytes 1572872 | tf_op jit(solution)/shard_map/ppermute | solution.py:17
  147.5 8.4 %collective-permute-start.37 = (bf16[64,2048]{1,0:T(8,128)(2,1)S(1)}, bf16[64,2048]{1,0:T(8,128)(2,1)S(1)}, u32[]{:S(2)}, u32[]{:S(2)}) collective-permute-start(bf16[64,2048]{1,0:T(8,128)(2,1)S(1)} %get-tuple-element.112), channel_id=1, source_target_pairs={{0,4},{2,6},{4,0},{6,2},{8,12},{10,14},{12,8},{14,10},{16,20},{18,... | collective-permute-start | bytes 786440 | tf_op jit(solution)/shard_map/ppermute | solution.py:17
  148.1 10.2 %collective-permute-start.41 = (bf16[128,2048]{1,0:T(8,128)(2,1)S(1)}, bf16[128,2048]{1,0:T(8,128)(2,1)S(1)}, u32[]{:S(2)}, u32[]{:S(2)}) collective-permute-start(bf16[128,2048]{1,0:T(8,128)(2,1)S(1)} %get-tuple-element.97), channel_id=1, source_target_pairs={{0,2},{2,0},{4,6},{6,4},{8,10},{10,8},{12,14},{14,12},{16,18},{18,... | collective-permute-start | bytes 1572872 | tf_op jit(solution)/shard_map/ppermute | solution.py:17
  148.1 18.9 %collective-permute-start.34 = (bf16[128,2048]{1,0:T(8,128)(2,1)S(1)}, bf16[128,2048]{1,0:T(8,128)(2,1)S(1)}, u32[]{:S(2)}, u32[]{:S(2)}) collective-permute-start(bf16[128,2048]{1,0:T(8,128)(2,1)S(1)} %get-tuple-element.87), channel_id=1, source_target_pairs={{0,2},{2,0},{4,6},{6,4},{8,10},{10,8},{12,14},{14,12},{16,18},{18,... | collective-permute-start | bytes 1572872 | tf_op jit(solution)/shard_map/ppermute | solution.py:17
  148.6 8.2 %collective-permute-start.38 = (bf16[64,2048]{1,0:T(8,128)(2,1)S(1)}, bf16[64,2048]{1,0:T(8,128)(2,1)S(1)}, u32[]{:S(2)}, u32[]{:S(2)}) collective-permute-start(bf16[64,2048]{1,0:T(8,128)(2,1)S(1)} %get-tuple-element.113), channel_id=1, source_target_pairs={{0,1},{1,0},{2,3},{3,2},{4,5},{5,4},{6,7},{7,6},{8,9},{9,8},{10,11... | collective-permute-start | bytes 786440 | tf_op jit(solution)/shard_map/ppermute | solution.py:17
  156.8 9.6 %collective-permute-start.39 = (bf16[64,2048]{1,0:T(8,128)(2,1)S(1)}, bf16[64,2048]{1,0:T(8,128)(2,1)S(1)}, u32[]{:S(2)}, u32[]{:S(2)}) collective-permute-start(bf16[64,2048]{1,0:T(8,128)(2,1)S(1)} %get-tuple-element.94), channel_id=1, source_target_pairs={{0,1},{1,0},{2,3},{3,2},{4,5},{5,4},{6,7},{7,6},{8,9},{9,8},{10,11... | collective-permute-start | bytes 786440 | tf_op jit(solution)/shard_map/ppermute | solution.py:17
  158.5 8.4 %collective-permute-start.42 = (bf16[64,2048]{1,0:T(8,128)(2,1)S(1)}, bf16[64,2048]{1,0:T(8,128)(2,1)S(1)}, u32[]{:S(2)}, u32[]{:S(2)}) collective-permute-start(bf16[64,2048]{1,0:T(8,128)(2,1)S(1)} %get-tuple-element.114), channel_id=1, source_target_pairs={{0,4},{2,6},{4,0},{6,2},{8,12},{10,14},{12,8},{14,10},{16,20},{18,... | collective-permute-start | bytes 786440 | tf_op jit(solution)/shard_map/ppermute | solution.py:17
  166.4 7.2 %collective-permute-start.40 = (bf16[64,2048]{1,0:T(8,128)(2,1)S(1)}, bf16[64,2048]{1,0:T(8,128)(2,1)S(1)}, u32[]{:S(2)}, u32[]{:S(2)}) collective-permute-start(bf16[64,2048]{1,0:T(8,128)(2,1)S(1)} %get-tuple-element.95), channel_id=1, source_target_pairs={{0,1},{1,0},{2,3},{3,2},{4,5},{5,4},{6,7},{7,6},{8,9},{9,8},{10,11... | collective-permute-start | bytes 786440 | tf_op jit(solution)/shard_map/ppermute | solution.py:17
  167.1 6.6 %collective-permute-start.44 = (bf16[64,2048]{1,0:T(8,128)(2,1)S(1)}, bf16[64,2048]{1,0:T(8,128)(2,1)S(1)}, u32[]{:S(2)}, u32[]{:S(2)}) collective-permute-start(bf16[64,2048]{1,0:T(8,128)(2,1)S(1)} %add_convert_fusion), channel_id=1, source_target_pairs={{0,8},{2,10},{4,12},{6,14},{8,0},{10,2},{12,4},{14,6},{16,24},{18,... | collective-permute-start | bytes 786440 | tf_op jit(solution)/shard_map/ppermute | solution.py:17
  167.8 6.4 %collective-permute-start.43 = (bf16[64,2048]{1,0:T(8,128)(2,1)S(1)}, bf16[64,2048]{1,0:T(8,128)(2,1)S(1)}, u32[]{:S(2)}, u32[]{:S(2)}) collective-permute-start(bf16[64,2048]{1,0:T(8,128)(2,1)S(1)} %get-tuple-element.98), channel_id=1, source_target_pairs={{0,4},{2,6},{4,0},{6,2},{8,12},{10,14},{12,8},{14,10},{16,20},{18,... | collective-permute-start | bytes 786440 | tf_op jit(solution)/shard_map/ppermute | solution.py:17
  174.3 7.3 %collective-permute-start.45 = (bf16[32,2048]{1,0:T(8,128)(2,1)S(1)}, bf16[32,2048]{1,0:T(8,128)(2,1)S(1)}, u32[]{:S(2)}, u32[]{:S(2)}) collective-permute-start(bf16[32,2048]{1,0:T(8,128)(2,1)S(1)} %add_convert_fusion.9), channel_id=1, source_target_pairs={{0,16},{2,18},{4,20},{6,22},{8,24},{10,26},{12,28},{14,30},{16,0},... | collective-permute-start | bytes 393224 | tf_op jit(solution)/shard_map/ppermute | solution.py:17

commit v7 on v6

--- a/solution.py
+++ b/solution.py
@@ -35,10 +35,12 @@
     return parts[0] if len(parts) == 1 else jnp.concatenate(parts, axis=0)
 
 
-def gather_far(block):
+def gather_far(block, *after):
     parts = [block]
     for distance in far_distances():
         parts.append(swap(join(parts), "expert", distance))
+        if after:
+            parts[-1] = tie(parts[-1], *after)
     return parts
 
 
@@ -215,18 +217,27 @@
     return per, per * size
 
 
-def forward_in(place, x_own, x_other, w_in):
-    rows = x_own.shape[0]
+def height_of(parts):
+    return sum(part.shape[0] for part in parts)
+
+
+def stacked(refs):
+    return jnp.concatenate([ref[...] for ref in refs], axis=0)
+
+
+def forward_in(place, x, w_in):
+    rows = height_of(x)
     width, both = w_in.shape
     hidden = both // 2
     size = step_of(hidden)
 
-    def kernel(place_ref, own_ref, other_ref, w_ref, hidden_ref, slope_ref, act_ref):
-        x = jnp.concatenate([own_ref[...], other_ref[...]], axis=0)
+    def kernel(place_ref, *refs):
+        w_ref, hidden_ref, slope_ref, act_ref = refs[len(x) :]
+        left = stacked(refs[: len(x)])
 
         def body(start):
-            gate = dot(x, w_ref[:, pl.ds(start, size)])
-            up = dot(x, w_ref[:, pl.ds(hidden + start, size)])
+            gate = dot(left, w_ref[:, pl.ds(start, size)])
+            up = dot(left, w_ref[:, pl.ds(hidden + start, size)])
             sig = 1.0 / (1.0 + jnp.exp(-gate))
             act = gate * sig
             hidden_ref[:, pl.ds(start, size)] = (act * up).astype(BF16)
@@ -235,13 +246,13 @@
 
         tiles(hidden, body)
 
-    shape = (2 * rows, hidden)
+    shape = (rows, hidden)
     return resident(
         kernel,
-        [x_own, x_other, w_in],
+        [*x, w_in],
         [(shape, BF16), (shape, F32), (shape, F32)],
         place,
-        flops=4 * rows * width * both,
+        flops=2 * rows * width * both,
     )
 
 
@@ -283,17 +294,19 @@
 
 def backward_down(place, err_own, err_other, w_down, terms, c, halves):
     experts = lax.axis_size("expert")
-    rows, quarter = err_own.shape
+    rows, quarter = height_of(err_own), err_own[0].shape[1]
+    count = len(err_own)
     height = w_down.shape[0]
     own = height // halves
     size = step_of(own)
     held = slice(c * rows, (c + 1) * rows)
 
-    def kernel(place_ref, err_own_ref, err_other_ref, own_ref, other_ref, w_ref, grad_ref, *outs):
+    def kernel(place_ref, *refs):
+        own_ref, other_ref, w_ref, grad_ref, *outs = refs[2 * count :]
         weight = route_weight(own_ref[held, :], place_ref, experts)
-        grad_ref[:rows, :] = (weight * err_own_ref[...].astype(F32)).astype(BF16)
+        grad_ref[:rows, :] = (weight * stacked(refs[:count]).astype(F32)).astype(BF16)
         weight = route_weight(other_ref[held, :], place_ref, experts)
-        grad_ref[rows:, :] = (weight * err_other_ref[...].astype(F32)).astype(BF16)
+        grad_ref[rows:, :] = (weight * stacked(refs[count : 2 * count]).astype(F32)).astype(BF16)
         for d in reversed(range(halves)):
 
             def body(start):
@@ -306,7 +319,7 @@
     shape = (2 * rows, own)
     return resident(
         kernel,
-        [err_own, err_other, *terms, w_down],
+        [*err_own, *err_other, *terms, w_down],
         [((2 * rows, quarter), BF16), (shape, F32)] + [(shape, BF16)] * (halves - 1),
         place,
         flops=4 * rows * height * quarter,
@@ -364,39 +377,32 @@
             store(g, cols, low, high)
 
 
-def ranges_down(place, hidden, grads, codes, groups, halves):
+def ranges_down(place, hidden, grad, codes, groups, halves, found=None):
     _, height, quarter = codes.shape
     size = height // groups
     per, rows = hidden_rows(groups, size, halves)
     blocks = height // halves // rows
-    flat = [part for parts in hidden for part in parts]
-    chunks = len(grads)
-    tokens = grads[0].shape[0]
+    earlier = [] if found is None else [found]
 
     def kernel(place_ref, *refs):
-        hidden_refs = refs[: len(flat)]
-        grad_refs = refs[len(flat) : len(flat) + chunks]
-        code_ref, out_ref, right_ref = refs[len(flat) + chunks :]
+        hidden_refs = refs[:halves]
+        grad_ref, code_ref, *found_refs, out_ref = refs[halves:]
         step = pl.program_id(0)
         base = moved(step, blocks, place_ref) * per
 
-        @pl.when(step == 0)
-        def _():
-            for c in range(chunks):
-                right_ref[c * tokens : (c + 1) * tokens, :] = grad_refs[c][...]
-
         def store(g, cols, low, high):
-            out_ref[0, pl.ds(base + g, 1), cols] = low
-            out_ref[1, pl.ds(base + g, 1), cols] = high
+            for k, value in ((0, low), (1, high)):
+                for ref in found_refs:
+                    value += ref[k, pl.ds(base + g, 1), cols]
+                out_ref[k, pl.ds(base + g, 1), cols] = value
 
         for d in range(halves):
 
             @pl.when(step // blocks == d)
             def _():
-                left = [hidden_refs[c * halves + d][...] for c in range(chunks)]
                 range_tile(
-                    jnp.concatenate(left, axis=0),
-                    right_ref,
+                    hidden_refs[d][...],
+                    grad_ref,
                     size,
                     256,
                     lambda cut, cols: code_ref[0, cut, cols],
@@ -407,14 +413,16 @@
     return call(
         kernel,
         (height // rows,),
-        [(part, (part.shape[0], rows), lambda i, p: (0, i % blocks)) for part in flat]
-        + [(grad, pltpu.VMEM, None) for grad in grads]
-        + [(codes, (1, rows, quarter), lambda i, p: (0, moved(i, blocks, p), 0))],
+        [(part, (part.shape[0], rows), lambda i, p: (0, i % blocks)) for part in hidden]
+        + [
+            (grad, pltpu.VMEM, None),
+            (codes, (1, rows, quarter), lambda i, p: (0, moved(i, blocks, p), 0)),
+        ]
+        + [(array, pltpu.VMEM, None) for array in earlier],
         [(shape, F32, shape, whole3)],
         place,
-        scratch=[pltpu.VMEM((chunks * tokens, quarter), BF16)],
         mib=20,
-        flops=2 * sum(g.shape[0] for g in grads) * height * quarter,
+        flops=2 * grad.shape[0] * height * quarter,
     )[0]
 
 
@@ -425,7 +433,7 @@
     per = next(p for p in (4, 2, 1) if held % p == 0)
     rows = per * size
     blocks = held // per
-    flat = [array for pair in x for array in pair]
+    flat = [array for parts in x for array in parts]
     chunks = len(grads)
     tokens, both = grads[0].shape
     wide = 256 if hidden % 256 == 0 else hidden
@@ -508,29 +516,33 @@
 
     far = join(gather_far(tokens)[1:])
     near_own = swap(tokens, "expert", 4)
-    across = [swap(tokens, "expert", 2)]
+    across_own = swap(tokens, "expert", 2)
     extra = -(-3 * experts // 128) * 128
     terms = prepare(place, routes, route_scores, extra)
-    w_in = dequant(place, in_codes[0], tie(in_low, terms)[0], in_high[0])
-    w_down = dequant(place, down_codes, tie(down_low, w_in), down_high, halves)
-    far = tie(far, w_in, w_down, across[0])
+    near_own = tie(near_own, terms)
+    across_near = swap(near_own, "expert", 2)
+    w_in = dequant(place, in_codes[0], tie(in_low, near_own)[0], in_high[0])
+    far = tie(far, w_in, across_own, across_near)
     near_far = swap(far, "expert", 4)
-    middle = pack(place, [[far], [near_own]])
-    across.append(swap(middle, "expert", 2))
-    terms = join(gather_far(terms))
-    near_far = tie(near_far, across[1], terms)
-    across.append(swap(near_far, "expert", 2))
-    first = pack(place, [[tokens], [middle], [near_far]])
-    x = [(first, swap(first, "expert", 1))]
+    across_far = swap(far, "expert", 2)
+    w_down = dequant(place, down_codes, tie(down_low, far), down_high, halves)
+    first = pack(place, [[tokens], [tie(far, w_down)], [near_own]])
+    first_other = swap(first, "expert", 1)
+    terms = join(gather_far(terms, w_down))
+    near_far = tie(near_far, w_down, terms)
+    across_last = swap(near_far, "expert", 2)
+    near_other = swap(near_far, "expert", 1)
+    x = [[first, near_far, first_other, near_other]]
     near_terms = swap(terms, "expert", 4)
 
     hidden, slope, act = [], [], []
     for c in chunks:
         if c == 1:
-            across[2] = tie(across[2], hidden[0][0], near_terms)
-            second = pack(place, [[part] for part in across])
-            x.append((second, swap(second, "expert", 1)))
-        own, chunk_slope, chunk_act = forward_in(place, *x[c], w_in)
+            second = pack(place, [[across_own], [tie(across_far, near_other)], [across_near]])
+            second_other = swap(second, "expert", 1)
+            across_last = tie(across_last, hidden[0][0], near_terms, second_other)
+            x.append([second, across_last, second_other, swap(across_last, "expert", 1)])
+        own, chunk_slope, chunk_act = forward_in(place, x[c], w_in)
         hidden.append([own] + [swap(own, "half", d) for d in parts if d])
         slope.append(chunk_slope)
         act.append(chunk_act)
@@ -551,37 +563,42 @@
         (mixed[f] - target[:, cuts[f]].astype(F32)).astype(BF16) for f in range(len(cuts))
     ]
 
-    kept = [gather_far(part) for part in error]
-    near = [swap(join(part), "expert", 4) for part in kept]
-    kept = pack(place, [list(line) for line in zip(*kept)])
-    across = swap(kept, "expert", 2)
-    near = [tie(part, across) for part in near]
-    near_across = [swap(part, "expert", 2) for part in near]
-    first = pack(place, [[kept], near])
-    errors = [(first, swap(first, "expert", 1))]
+    kept = pack(place, [list(line) for line in zip(*[gather_far(part) for part in error])])
+    near = swap(kept, "expert", 4)
+    across_kept = swap(kept, "expert", 2)
+    kept_other = swap(kept, "expert", 1)
+    near = tie(near, across_kept, kept_other)
+    across_near = swap(near, "expert", 2)
+    across_other = swap(across_kept, "expert", 1)
+    errors = [([kept, near], [kept_other, swap(near, "expert", 1)])]
     grads, grad_own, arrived = [], [], []
+    down_groups = down_low.shape[1]
     for c in chunks:
         if c == 1:
-            second = pack(place, [[across], [tie(part, grads[0]) for part in near_across]])
-            errors.append((second, swap(second, "expert", 1)))
+            across_near = tie(across_near, grads[0], across_other)
+            down_grad = ranges_down(place, hidden[0], grads[0], down_codes, down_groups, halves)
+            last_other = tie(swap(across_near, "expert", 1), down_grad, *arrived[0])
+            errors.append(([across_kept, across_near], [across_other, last_other]))
         grad, own, *others = backward_down(place, *errors[c], w_down, terms, c, halves)
         grads.append(grad)
         grad_own.append(own)
         arrived.append([swap(other, "half", d + 1) for d, other in enumerate(others)])
 
     grad_in, kinds = [], []
-    down_grad = ranges_down(place, hidden, grads, down_codes, down_low.shape[1], halves)
-    arrived[0] = [tie(part, down_grad) for part in arrived[0]]
+    down_grad = ranges_down(
+        place, hidden[1], grads[1], down_codes, down_groups, halves, down_grad
+    )
     for c in chunks:
         if c == 1:
-            arrived[1] = [tie(part, grad_in[0]) for part in arrived[1]]
+            arrived[1] = [tie(part, grad_in[0], down_grad) for part in arrived[1]]
         grad, found = backward_hidden(
             place, grad_own[c], arrived[c], slope[c], act[c], w_in, halves
         )
         grad_in.append(grad)
         kinds.append(found)
     kinds[0] = [tie(part, grad_in[1]) for part in kinds[0]]
-    lower, upper = slice(0, first.shape[0] // 2), slice(first.shape[0] // 2, first.shape[0])
+    rows = height_of(errors[0][0])
+    lower, upper = slice(0, rows // 2), slice(rows // 2, rows)
     keep, go = [
         [[found[2 * d], swap(found[2 * d + 1], "expert", 1)] for d in parts] for found in kinds
     ]

time: 183 us -> 180 us (0.984)
  waiting for transfers between devices: 70.2 us -> 64.2 us
  starting transfers between devices: 43.8 us -> 47 us
    ppermute x46 -> x49, waiting for transfers between devices: 70.2 us -> 64.2 us  [swap(): return lax.ppermute(array, axis, [(i, i ^ distance) for i in range(size)])]
    ppermute x46 -> x49, starting transfers between devices: 43.8 us -> 47 us  [swap(): return lax.ppermute(array, axis, [(i, i ^ distance) for i in range(size)])]
    pallas_call x21 -> x19, Pallas kernels: 55.6 us -> 56.5 us  [call(): pl.pallas_call(kernel, grid_spec=pltpu.PrefetchScalarGridSpec(num_scalar_...]
    unnamed x24 -> x26, local copies, waits for them, and re-layouts: 9.73 us -> 8.85 us
  transfers between devices with their start and end apart: 46 -> 49, of which waited for: 31 -> 27; matrix products, arithmetic and copies ran while one was open for 2% -> 2% of each run, Pallas kernels for 25% -> 26%
where the time goes in v7:
time: 180 us
  waiting for transfers between devices  64.2 us (36%)
  Pallas kernels  56.5 us (31%)
  starting transfers between devices  47 us (26%)
  local copies, waits for them, and re-layouts  8.88 us (5%)
  other arithmetic  1.98 us (1%)
    ppermute x49, waiting for transfers between devices, swap(): return lax.ppermute(array, axis, [(i, i ^ distance) for i in range(size)])  64.2 us
    pallas_call x19, Pallas kernels, call(): pl.pallas_call(kernel, grid_spec=pltpu.PrefetchScalarGridSpec(num_scalar_...  56.5 us
    ppermute x49, starting transfers between devices, swap(): return lax.ppermute(array, axis, [(i, i ^ distance) for i in range(size)])  47 us
    unnamed x26, local copies, waits for them, and re-layouts  8.85 us
  transfers between devices with their start and end apart: 49, of which 27 were waited for; matrix products, arithmetic and copies ran while one was open for 2% of the time, Pallas kernels for 26%

profile of v7, /device:TPU:0, one launch (start us, length us, event | category | flops | bytes accessed | tf_op | source)
XLA Modules:
  0.0 179.6 jit_solution(15792572414848699608)
XLA Ops:
  0.6 3.1 %collective-permute-start.1 = (bf16[32,4096]{1,0:T(8,128)(2,1)}, bf16[32,4096]{1,0:T(8,128)(2,1)S(1)}, u32[]{:S(2)}, u32[]{:S(2)}) collective-permute-start(bf16[32,4096]{1,0:T(8,128)(2,1)} %refs_0_.1), channel_id=1, source_target_pairs={{0,8},{2,10},{4,12},{6,14},{8,0},{10,2},{12,4},{14,6},{16,24},{18,... | collective-permute-start | bytes 786440 | tf_op jit(solution)/shard_map/ppermute | solution.py:17
  3.7 1.5 collective-permute-start.2
  5.2 2.6 %collective-permute-start = (bf16[32,4096]{1,0:T(8,128)(2,1)}, bf16[32,4096]{1,0:T(8,128)(2,1)S(1)}, u32[]{:S(2)}, u32[]{:S(2)}) collective-permute-start(bf16[32,4096]{1,0:T(8,128)(2,1)} %refs_0_.1), channel_id=1, source_target_pairs={{0,16},{2,18},{4,20},{6,22},{8,24},{10,26},{12,28},{14,30},{16,0},... | collective-permute-start | bytes 786440 | tf_op jit(solution)/shard_map/ppermute | solution.py:17
  10.2 4.4 %collective-permute-done.1.refs_2_ = bf16[32,4096]{1,0:T(8,128)(2,1)S(1)} collective-permute-done((bf16[32,4096]{1,0:T(8,128)(2,1)}, bf16[32,4096]{1,0:T(8,128)(2,1)S(1)}, u32[]{:S(2)}, u32[]{:S(2)}) %collective-permute-start.1) | collective-permute-done | bytes 262176 | tf_op jit(solution)/shard_map/ppermute | solution.py:17
  14.5 2.6 %collective-permute-start.3 = (bf16[32,4096]{1,0:T(8,128)(2,1)S(1)}, bf16[32,4096]{1,0:T(8,128)(2,1)S(1)}, u32[]{:S(2)}, u32[]{:S(2)}) collective-permute-start(bf16[32,4096]{1,0:T(8,128)(2,1)S(1)} %collective-permute-done.1.refs_2_), channel_id=1, source_target_pairs={{0,4},{2,6},{4,0},{6,2},{8,12},{10,14},{12,8},{14,10},{16,20},{18,... | collective-permute-start | bytes 786440 | tf_op jit(solution)/shard_map/ppermute | solution.py:17
  17.1 4.6 %copy-done = bf16[1,2,4096,768]{3,2,1,0:T(8,128)(2,1)S(1)} copy-done((bf16[1,2,4096,768]{3,2,1,0:T(8,128)(2,1)S(1)}, bf16[1,2,4096,768]{3,2,1,0:T(8,128)(2,1)}, u32[]{:S(2)}) %copy-start) | copy-done | bytes 12582936
  23.6 3.7 %shard_map.122.refs_4_.refs_3_ = bf16[4096,1536]{1,0:T(8,128)(2,1)S(1)} custom-call(s32[2]{0:T(128)S(1)} %pad_add_fusion.place_ref, bf16[2,4096,768]{2,1,0:T(8,128)(2,1)S(1)} %bitcast.7, f32[2,32,768]{2,1,0:T(8,128)S(1)} %bitcast.11, f32[2,32,768]{2,1,0:T(8,128)S(1)} %bitcast.12), custom_call_target="tpu_custom_call" | custom-call | bytes 25 | tf_op jit(solution)/shard_map/pallas_call | solution.py:114
  27.4 3.0 %collective-permute-start.5 = (bf16[32,128]{1,0:T(8,128)(2,1)S(1)}, bf16[32,128]{1,0:T(8,128)(2,1)S(1)}, u32[]{:S(2)}, u32[]{:S(2)}) collective-permute-start(bf16[32,128]{1,0:T(8,128)(2,1)S(1)} %shard_map.121), channel_id=1, source_target_pairs={{0,16},{2,18},{4,20},{6,22},{8,24},{10,26},{12,28},{14,30},{16,0},... | collective-permute-start | bytes 24584 | tf_op jit(solution)/shard_map/ppermute | solution.py:17
  30.6 2.3 %shard_map.123.refs_2_.refs_6_ = bf16[1536,2048]{1,0:T(8,128)(2,1)S(1)} custom-call(s32[2]{0:T(128)S(1)} %pad_add_fusion.place_ref, bf16[1,1536,2048]{2,1,0:T(8,128)(2,1)S(1)} %copy-done.1, f32[1,12,2048]{2,1,0:T(8,128)S(1)} %copy.17.low_ref, f32[1,12,2048]{2,1,0:T(8,128)S(1)} %copy.18.high_ref), custom_call_target="tpu_custom_call" | custom-call | bytes 12 | tf_op jit(solution)/shard_map/pallas_call | solution.py:114
  32.9 1.5 collective-permute-done.4.refs_1_
  35.7 1.3 collective-permute-done.13.refs_1_
  38.4 4.1 %shard_map.125 = (bf16[256,768]{1,0:T(8,128)(2,1)S(1)}, f32[256,768]{1,0:T(8,128)S(1)}, f32[256,768]{1,0:T(8,128)S(1)}) custom-call(s32[2]{0:T(128)S(1)} %pad_add_fusion.place_ref, bf16[96,4096]{1,0:T(8,128)(2,1)S(1)} %shard_map.124.refs_0_, bf16[32,4096]{1,0:T(8,128)(2,1)S(1)} %collective-permute-done.4.refs_1_, ...), custom_call_target="tpu_custom_call" | custom-call | flops 3221 | bytes 16 | tf_op jit(solution)/shard_map/pallas_call | solution.py:114
  42.5 3.8 %collective-permute-done.14.refs_1_.refs_5_ = bf16[32,4096]{1,0:T(8,128)(2,1)S(1)} collective-permute-done((bf16[32,4096]{1,0:T(8,128)(2,1)S(1)}, bf16[32,4096]{1,0:T(8,128)(2,1)S(1)}, u32[]{:S(2)}, u32[]{:S(2)}) %collective-permute-start.14) | collective-permute-done | bytes 262176 | tf_op jit(solution)/shard_map/ppermute | solution.py:17
  46.4 1.5 collective-permute-start.8
  47.9 4.1 %shard_map.128 = (bf16[256,768]{1,0:T(8,128)(2,1)S(1)}, f32[256,768]{1,0:T(8,128)S(1)}, f32[256,768]{1,0:T(8,128)S(1)}) custom-call(s32[2]{0:T(128)S(1)} %pad_add_fusion.place_ref, bf16[96,4096]{1,0:T(8,128)(2,1)S(1)} %shard_map.127.refs_0_.refs_4_, bf16[32,4096]{1,0:T(8,128)(2,1)S(1)} %collective-permute-done.14.refs_1_.refs_5_, ...), custom_call_target="tpu_custom_call" | custom-call | flops 3221 | bytes 16 | tf_op jit(solution)/shard_map/pallas_call | solution.py:114
  52.0 1.6 collective-permute-start.17
  53.8 3.6 %collective-permute-done.10 = bf16[128,128]{1,0:T(8,128)(2,1)S(1)} collective-permute-done((bf16[128,128]{1,0:T(8,128)(2,1)S(1)}, bf16[128,128]{1,0:T(8,128)(2,1)S(1)}, u32[]{:S(2)}, u32[]{:S(2)}) %collective-permute-start.10) | collective-permute-done | bytes 32800 | tf_op jit(solution)/shard_map/ppermute | solution.py:17
  57.5 1.2 collective-permute-done.11.refs_4_.refs_5_
  58.8 2.3 %shard_map.126 = (bf16[128,2048]{1,0:T(8,128)(2,1)S(1)}, bf16[128,2048]{1,0:T(8,128)(2,1)S(1)}) custom-call(s32[2]{0:T(128)S(1)} %pad_add_fusion.place_ref, bf16[256,768]{1,0:T(8,128)(2,1)S(1)} %get-tuple-element.62.refs_0_, bf16[256,768]{1,0:T(8,128)(2,1)S(1)} %collective-permute-done.8.refs_1_, bf16[1536,2048]{1,0:T(8,128)(2,1)S(1)} %shard_map.123.refs_2_.refs_6_, ...), custom_call_target="tpu_custom_call" | custom-call | flops 1610 | bytes 8 | tf_op jit(solution)/shard_map/pallas_call | solution.py:114
  61.1 5.2 %collective-permute-done.17.refs_1_ = bf16[256,768]{1,0:T(8,128)(2,1)S(1)} collective-permute-done((bf16[256,768]{1,0:T(8,128)(2,1)S(1)}, bf16[256,768]{1,0:T(8,128)(2,1)S(1)}, u32[]{:S(2)}, u32[]{:S(2)}) %collective-permute-start.17) | collective-permute-done | bytes 393248 | tf_op jit(solution)/shard_map/ppermute | solution.py:17
  66.3 2.3 %shard_map.129 = (bf16[128,2048]{1,0:T(8,128)(2,1)S(1)}, bf16[128,2048]{1,0:T(8,128)(2,1)S(1)}) custom-call(s32[2]{0:T(128)S(1)} %pad_add_fusion.place_ref, bf16[256,768]{1,0:T(8,128)(2,1)S(1)} %get-tuple-element.67.refs_0_, bf16[256,768]{1,0:T(8,128)(2,1)S(1)} %collective-permute-done.17.refs_1_, bf16[1536,2048]{1,0:T(8,128)(2,1)S(1)} %shard_map.123.refs_2_.refs_6_, ...), custom_call_target="tpu_custom_call" | custom-call | flops 1610 | bytes 8 | tf_op jit(solution)/shard_map/pallas_call | solution.py:114
  69.2 1.4 collective-permute-done.18
  71.0 1.8 collective-permute-start.20
  72.9 4.2 %collective-permute-done.19 = bf16[64,1024]{1,0:T(8,128)(2,1)S(1)} collective-permute-done((bf16[64,1024]{1,0:T(8,128)(2,1)S(1)}, bf16[64,1024]{1,0:T(8,128)(2,1)S(1)}, u32[]{:S(2)}, u32[]{:S(2)}) %collective-permute-start.19) | collective-permute-done | bytes 131104 | tf_op jit(solution)/shard_map/ppermute | solution.py:17
  77.1 2.0 %collective-permute-done.20 = bf16[64,1024]{1,0:T(8,128)(2,1)S(1)} collective-permute-done((bf16[64,1024]{1,0:T(8,128)(2,1)S(1)}, bf16[64,1024]{1,0:T(8,128)(2,1)S(1)}, u32[]{:S(2)}, u32[]{:S(2)}) %collective-permute-start.20) | collective-permute-done | bytes 131104 | tf_op jit(solution)/shard_map/ppermute | solution.py:17
  80.0 1.6 collective-permute-start.24
  81.6 3.8 %collective-permute-done.22 = bf16[64,1024]{1,0:T(8,128)(2,1)S(1)} collective-permute-done((bf16[64,1024]{1,0:T(8,128)(2,1)S(1)}, bf16[64,1024]{1,0:T(8,128)(2,1)S(1)}, u32[]{:S(2)}, u32[]{:S(2)}) %collective-permute-start.22) | collective-permute-done | bytes 131104 | tf_op jit(solution)/shard_map/ppermute | solution.py:17
  85.4 1.4 collective-permute-done.24
  87.4 2.5 %collective-permute-start.25 = (bf16[32,1024]{1,0:T(8,128)(2,1)S(1)}, bf16[32,1024]{1,0:T(8,128)(2,1)S(1)}, u32[]{:S(2)}, u32[]{:S(2)}) collective-permute-start(bf16[32,1024]{1,0:T(8,128)(2,1)S(1)} %get-tuple-element.112), channel_id=1, source_target_pairs={{0,16},{2,18},{4,20},{6,22},{8,24},{10,26},{12,28},{14,30},{16,0},... | collective-permute-start | bytes 196616 | tf_op jit(solution)/shard_map/ppermute | solution.py:17
  89.9 2.8 %collective-permute-done.23 = bf16[32,1024]{1,0:T(8,128)(2,1)S(1)} collective-permute-done((bf16[32,1024]{1,0:T(8,128)(2,1)S(1)}, bf16[32,1024]{1,0:T(8,128)(2,1)S(1)}, u32[]{:S(2)}, u32[]{:S(2)}) %collective-permute-start.23) | collective-permute-done | bytes 65568 | tf_op jit(solution)/shard_map/ppermute | solution.py:17
  92.7 1.4 collective-permute-done.25
  94.2 1.1 collective-permute-start.26
  95.3 1.9 %collective-permute-start.27 = (bf16[32,1024]{1,0:T(8,128)(2,1)S(1)}, bf16[32,1024]{1,0:T(8,128)(2,1)S(1)}, u32[]{:S(2)}, u32[]{:S(2)}) collective-permute-start(bf16[32,1024]{1,0:T(8,128)(2,1)S(1)} %get-tuple-element.110.refs_1_), channel_id=1, source_target_pairs={{0,16},{2,18},{4,20},{6,22},{8,24},{10,26},{12,28},{14,30},{16,0},... | collective-permute-start | bytes 196616 | tf_op jit(solution)/shard_map/ppermute | solution.py:17
  97.2 2.7 %collective-permute-done.26.refs_2_ = bf16[32,1024]{1,0:T(8,128)(2,1)S(1)} collective-permute-done((bf16[32,1024]{1,0:T(8,128)(2,1)S(1)}, bf16[32,1024]{1,0:T(8,128)(2,1)S(1)}, u32[]{:S(2)}, u32[]{:S(2)}) %collective-permute-start.26) | collective-permute-done | bytes 65568 | tf_op jit(solution)/shard_map/ppermute | solution.py:17
  99.9 1.5 collective-permute-done.27.refs_3_
  102.0 1.8 %collective-permute-start.29 = (bf16[64,2048]{1,0:T(8,128)(2,1)S(1)}, bf16[64,2048]{1,0:T(8,128)(2,1)S(1)}, u32[]{:S(2)}, u32[]{:S(2)}) collective-permute-start(bf16[64,2048]{1,0:T(8,128)(2,1)S(1)} %shard_map.130.refs_0_), channel_id=1, source_target_pairs={{0,4},{2,6},{4,0},{6,2},{8,12},{10,14},{12,8},{14,10},{16,20},{18,... | collective-permute-start | bytes 786440 | tf_op jit(solution)/shard_map/ppermute | solution.py:17
  103.8 4.6 %collective-permute-done.28.refs_1_ = bf16[64,2048]{1,0:T(8,128)(2,1)S(1)} collective-permute-done((bf16[64,2048]{1,0:T(8,128)(2,1)S(1)}, bf16[64,2048]{1,0:T(8,128)(2,1)S(1)}, u32[]{:S(2)}, u32[]{:S(2)}) %collective-permute-start.28) | collective-permute-done | bytes 262176 | tf_op jit(solution)/shard_map/ppermute | solution.py:17
  108.4 1.8 collective-permute-start.33
  110.4 2.6 %shard_map.131 = (bf16[256,2048]{1,0:T(8,128)(2,1)S(1)}, f32[256,768]{1,0:T(8,128)S(1)}, bf16[256,768]{1,0:T(8,128)(2,1)S(1)}) custom-call(s32[2]{0:T(128)S(1)} %pad_add_fusion.place_ref, bf16[64,2048]{1,0:T(8,128)(2,1)S(1)} %shard_map.130.refs_0_, bf16[64,2048]{1,0:T(8,128)(2,1)S(1)} %collective-permute-done.28.refs_1_, ...), custom_call_target="tpu_custom_call" | custom-call | flops 1610 | bytes 9 | tf_op jit(solution)/shard_map/pallas_call | solution.py:114
  113.0 1.6 collective-permute-start.32
  114.6 2.5 %collective-permute-done.33.refs_1_ = bf16[64,2048]{1,0:T(8,128)(2,1)S(1)} collective-permute-done((bf16[64,2048]{1,0:T(8,128)(2,1)S(1)}, bf16[64,2048]{1,0:T(8,128)(2,1)S(1)}, u32[]{:S(2)}, u32[]{:S(2)}) %collective-permute-start.33) | collective-permute-done | bytes 262176 | tf_op jit(solution)/shard_map/ppermute | solution.py:17
  117.2 3.9 %shard_map.133.refs_4_ = f32[2,12,2048]{2,1,0:T(8,128)S(1)} custom-call(s32[2]{0:T(128)S(1)} %pad_add_fusion.place_ref, bf16[256,768]{1,0:T(8,128)(2,1)S(1)} %get-tuple-element.62.refs_0_, bf16[256,768]{1,0:T(8,128)(2,1)S(1)} %collective-permute-done.8.refs_1_, bf16[256,2048]{1,0:T(8,128)(2,1)S(1)} %get-tuple-element.78.refs_2_, ...), custom_call_target="tpu_custom_call" | custom-call | flops 1610 | bytes 8 | tf_op jit(solution)/shard_map/pallas_call | solution.py:114
  121.1 3.3 %collective-permute-done.32.refs_0_ = bf16[256,768]{1,0:T(8,128)(2,1)S(1)} collective-permute-done((bf16[256,768]{1,0:T(8,128)(2,1)S(1)}, bf16[256,768]{1,0:T(8,128)(2,1)S(1)}, u32[]{:S(2)}, u32[]{:S(2)}) %collective-permute-start.32) | collective-permute-done | bytes 393248 | tf_op jit(solution)/shard_map/ppermute | solution.py:17
  124.4 2.4 %shard_map.134 = (bf16[256,2048]{1,0:T(8,128)(2,1)S(1)}, f32[256,768]{1,0:T(8,128)S(1)}, bf16[256,768]{1,0:T(8,128)(2,1)S(1)}) custom-call(s32[2]{0:T(128)S(1)} %pad_add_fusion.place_ref, bf16[64,2048]{1,0:T(8,128)(2,1)S(1)} %collective-permute-done.29.refs_0_, bf16[64,2048]{1,0:T(8,128)(2,1)S(1)} %collective-permute-done.33.refs_1_, ...), custom_call_target="tpu_custom_call" | custom-call | flops 1610 | bytes 9 | tf_op jit(solution)/shard_map/pallas_call | solution.py:114
  126.8 1.6 collective-permute-start.36
  128.4 4.0 %shard_map.135 = f32[2,12,2048]{2,1,0:T(8,128)S(1)} custom-call(s32[2]{0:T(128)S(1)} %pad_add_fusion.place_ref, bf16[256,768]{1,0:T(8,128)(2,1)S(1)} %get-tuple-element.67.refs_0_, bf16[256,768]{1,0:T(8,128)(2,1)S(1)} %collective-permute-done.17.refs_1_, bf16[256,2048]{1,0:T(8,128)(2,1)S(1)} %get-tuple-element.84.refs_2_, ...), custom_call_target="tpu_custom_call" | custom-call | flops 1610 | bytes 8 | tf_op jit(solution)/shard_map/pallas_call | solution.py:114
  132.4 4.0 %shard_map.132 = (bf16[256,1536]{1,0:T(8,128)(2,1)S(1)}, bf16[128,2048]{1,0:T(8,128)(2,1)S(1)}, bf16[128,2048]{1,0:T(8,128)(2,1)S(1)}, bf16[128,2048]{1,0:T(8,128)(2,1)S(1)}, bf16[128,2048]{1,0:T(8,128)(2,1)S(1)}) custom-call(s32[2]{0:T(128)S(1)} %pad_add_fusion.place_ref, f32[256,768]{1,0:T(8,128)S(1)} %get-tuple-element.73.grad_own_ref, ...), custom_call_target="tpu_custom_call" | custom-call | flops 3221 | bytes 18 | tf_op jit(solution)/shard_map/pallas_call | solution.py:114
  136.5 1.0 collective-permute-done.36.refs_0_
  137.4 4.0 %shard_map.136 = (bf16[256,1536]{1,0:T(8,128)(2,1)S(1)}, bf16[128,2048]{1,0:T(8,128)(2,1)S(1)}, bf16[128,2048]{1,0:T(8,128)(2,1)S(1)}, bf16[128,2048]{1,0:T(8,128)(2,1)S(1)}, bf16[128,2048]{1,0:T(8,128)(2,1)S(1)}) custom-call(s32[2]{0:T(128)S(1)} %pad_add_fusion.place_ref, f32[256,768]{1,0:T(8,128)S(1)} %get-tuple-element.81.grad_own_ref, ...), custom_call_target="tpu_custom_call" | custom-call | flops 3221 | bytes 18 | tf_op jit(solution)/shard_map/pallas_call | solution.py:114
  142.0 1.4 collective-permute-done.39
  143.6 1.0 collective-permute-start.40
  145.1 1.5 collective-permute-start.41
  146.6 5.4 %collective-permute-done.40 = bf16[64,2048]{1,0:T(8,128)(2,1)S(1)} collective-permute-done((bf16[64,2048]{1,0:T(8,128)(2,1)S(1)}, bf16[64,2048]{1,0:T(8,128)(2,1)S(1)}, u32[]{:S(2)}, u32[]{:S(2)}) %collective-permute-start.40) | collective-permute-done | bytes 262176 | tf_op jit(solution)/shard_map/ppermute | solution.py:17
  152.2 1.1 collective-permute-done.41
  153.3 1.5 collective-permute-start.42
  155.0 1.2 collective-permute-start.45
  156.2 6.6 %shard_map.137.refs_11_ = f32[4,32,768]{2,1,0:T(8,128)} custom-call(s32[2]{0:T(128)S(1)} %pad_add_fusion.place_ref, bf16[96,4096]{1,0:T(8,128)(2,1)S(1)} %shard_map.124.refs_0_, bf16[32,4096]{1,0:T(8,128)(2,1)S(1)} %collective-permute-done.4.refs_1_, bf16[96,4096]{1,0:T(8,128)(2,1)S(1)} %collective-permute-done.6.refs_2_, ...), custom_call_target="tpu_custom_call" | custom-call | flops 3221 | bytes 18 | tf_op jit(solution)/shard_map/pallas_call | solution.py:114
  162.9 2.0 %collective-permute-start.47 = (bf16[64,2048]{1,0:T(8,128)(2,1)S(1)}, bf16[64,2048]{1,0:T(8,128)(2,1)S(1)}, u32[]{:S(2)}, u32[]{:S(2)}) collective-permute-start(bf16[64,2048]{1,0:T(8,128)(2,1)S(1)} %add_convert_fusion), channel_id=1, source_target_pairs={{0,8},{2,10},{4,12},{6,14},{8,0},{10,2},{12,4},{14,6},{16,24},{18,... | collective-permute-start | bytes 786440 | tf_op jit(solution)/shard_map/ppermute | solution.py:17
  165.4 1.0 collective-permute-start.46
  166.4 3.8 %shard_map.138.refs_11_ = f32[4,32,768]{2,1,0:T(8,128)} custom-call(s32[2]{0:T(128)S(1)} %pad_add_fusion.place_ref, bf16[96,4096]{1,0:T(8,128)(2,1)S(1)} %shard_map.124.refs_0_, bf16[32,4096]{1,0:T(8,128)(2,1)S(1)} %collective-permute-done.4.refs_1_, bf16[96,4096]{1,0:T(8,128)(2,1)S(1)} %collective-permute-done.6.refs_2_, ...), custom_call_target="tpu_custom_call", output_to_operand_aliasing={{}: (12, {})} | custom-call | flops 1610 | bytes 18 | tf_op jit(solution)/shard_map/pallas_call | solution.py:114
  170.2 1.2 collective-permute-done.43
  171.9 1.4 collective-permute-start.48
  174.1 3.8 %shard_map.139 = f32[4,32,768]{2,1,0:T(8,128)} custom-call(s32[2]{0:T(128)S(1)} %pad_add_fusion.place_ref, bf16[96,4096]{1,0:T(8,128)(2,1)S(1)} %shard_map.124.refs_0_, bf16[32,4096]{1,0:T(8,128)(2,1)S(1)} %collective-permute-done.4.refs_1_, bf16[96,4096]{1,0:T(8,128)(2,1)S(1)} %collective-permute-done.6.refs_2_, ...), custom_call_target="tpu_custom_call", output_to_operand_aliasing={{}: (12, {})} | custom-call | flops 1610 | bytes 18 | tf_op jit(solution)/shard_map/pallas_call | solution.py:114
  177.9 0.9 collective-permute-done.48
  (96 shorter events, 15.1 us)
Async XLA Ops:
  0.6 13.9 %collective-permute-start.1 = (bf16[32,4096]{1,0:T(8,128)(2,1)}, bf16[32,4096]{1,0:T(8,128)(2,1)S(1)}, u32[]{:S(2)}, u32[]{:S(2)}) collective-permute-start(bf16[32,4096]{1,0:T(8,128)(2,1)} %refs_0_.1), channel_id=1, source_target_pairs={{0,8},{2,10},{4,12},{6,14},{8,0},{10,2},{12,4},{14,6},{16,24},{18,... | collective-permute-start | bytes 786440 | tf_op jit(solution)/shard_map/ppermute | solution.py:17
  3.7 23.6 %collective-permute-start.2 = (bf16[32,4096]{1,0:T(8,128)(2,1)}, bf16[32,4096]{1,0:T(8,128)(2,1)S(1)}, u32[]{:S(2)}, u32[]{:S(2)}) collective-permute-start(bf16[32,4096]{1,0:T(8,128)(2,1)} %refs_0_.1), channel_id=1, source_target_pairs={{0,4},{2,6},{4,0},{6,2},{8,12},{10,14},{12,8},{14,10},{16,20},{18,... | collective-permute-start | bytes 786440 | tf_op jit(solution)/shard_map/ppermute | solution.py:17
  5.2 22.1 %collective-permute-start = (bf16[32,4096]{1,0:T(8,128)(2,1)}, bf16[32,4096]{1,0:T(8,128)(2,1)S(1)}, u32[]{:S(2)}, u32[]{:S(2)}) collective-permute-start(bf16[32,4096]{1,0:T(8,128)(2,1)} %refs_0_.1), channel_id=1, source_target_pairs={{0,16},{2,18},{4,20},{6,22},{8,24},{10,26},{12,28},{14,30},{16,0},... | collective-permute-start | bytes 786440 | tf_op jit(solution)/shard_map/ppermute | solution.py:17
  14.5 12.8 %collective-permute-start.3 = (bf16[32,4096]{1,0:T(8,128)(2,1)S(1)}, bf16[32,4096]{1,0:T(8,128)(2,1)S(1)}, u32[]{:S(2)}, u32[]{:S(2)}) collective-permute-start(bf16[32,4096]{1,0:T(8,128)(2,1)S(1)} %collective-permute-done.1.refs_2_), channel_id=1, source_target_pairs={{0,4},{2,6},{4,0},{6,2},{8,12},{10,14},{12,8},{14,10},{16,20},{18,... | collective-permute-start | bytes 786440 | tf_op jit(solution)/shard_map/ppermute | solution.py:17
  17.1 4.6 %copy-start = (bf16[1,2,4096,768]{3,2,1,0:T(8,128)(2,1)S(1)}, bf16[1,2,4096,768]{3,2,1,0:T(8,128)(2,1)}, u32[]{:S(2)}) copy-start(bf16[1,2,4096,768]{3,2,1,0:T(8,128)(2,1)} %refs_10_.5) | copy-start | bytes 37748740
  21.7 0.9 copy-start.3
  22.6 0.9 copy-start.4
  23.6 6.9 %copy-start.6 = (f32[1,12,2048]{2,0,1:T(1,128)S(1)}, f32[1,12,2048]{2,0,1:T(1,128)}, u32[]{:S(2)}) copy-start(f32[1,12,2048]{2,0,1:T(1,128)} %param.19) | copy-start | bytes 294916
  23.6 7.0 %copy-start.7 = (f32[1,12,2048]{2,0,1:T(1,128)S(1)}, f32[1,12,2048]{2,0,1:T(1,128)}, u32[]{:S(2)}) copy-start(f32[1,12,2048]{2,0,1:T(1,128)} %param.18) | copy-start | bytes 294916
  23.6 7.1 %copy-start.1 = (bf16[1,1536,2048]{2,1,0:T(8,128)(2,1)S(1)}, bf16[1,1536,2048]{2,1,0:T(8,128)(2,1)}, u32[]{:S(2)}) copy-start(bf16[1,1536,2048]{2,1,0:T(8,128)(2,1)} %refs_3_.3) | copy-start | bytes 18874372
  27.3 7.2 %copy-start.2 = (bf16[32,4096]{1,0:T(8,128)(2,1)S(1)}, bf16[32,4096]{1,0:T(8,128)(2,1)}, u32[]{:S(2)}) copy-start(bf16[32,4096]{1,0:T(8,128)(2,1)} %refs_0_.1) | copy-start | bytes 786436
  27.3 7.1 %collective-permute-start.4 = (bf16[32,4096]{1,0:T(8,128)(2,1)S(1)}, bf16[32,4096]{1,0:T(8,128)(2,1)S(1)}, u32[]{:S(2)}, u32[]{:S(2)}) collective-permute-start(bf16[32,4096]{1,0:T(8,128)(2,1)S(1)} %collective-permute-done.refs_1_), channel_id=1, source_target_pairs={{0,8},{2,10},{4,12},{6,14},{8,0},{10,2},{12,4},{14,6},{16,24},{18,... | collective-permute-start | bytes 786440 | tf_op jit(solution)/shard_map/ppermute | solution.py:17
  27.4 5.5 %collective-permute-start.5 = (bf16[32,128]{1,0:T(8,128)(2,1)S(1)}, bf16[32,128]{1,0:T(8,128)(2,1)S(1)}, u32[]{:S(2)}, u32[]{:S(2)}) collective-permute-start(bf16[32,128]{1,0:T(8,128)(2,1)S(1)} %shard_map.121), channel_id=1, source_target_pairs={{0,16},{2,18},{4,20},{6,22},{8,24},{10,26},{12,28},{14,30},{16,0},... | collective-permute-start | bytes 24584 | tf_op jit(solution)/shard_map/ppermute | solution.py:17
  30.5 6.4 %collective-permute-start.13 = (bf16[32,4096]{1,0:T(8,128)(2,1)S(1)}, bf16[32,4096]{1,0:T(8,128)(2,1)S(1)}, u32[]{:S(2)}, u32[]{:S(2)}) collective-permute-start(bf16[32,4096]{1,0:T(8,128)(2,1)S(1)} %collective-permute-done.refs_1_), channel_id=1, source_target_pairs={{0,4},{2,6},{4,0},{6,2},{8,12},{10,14},{12,8},{14,10},{16,20},{18,... | collective-permute-start | bytes 786440 | tf_op jit(solution)/shard_map/ppermute | solution.py:17
  34.5 2.5 %collective-permute-start.7 = (bf16[32,4096]{1,0:T(8,128)(2,1)S(1)}, bf16[32,4096]{1,0:T(8,128)(2,1)S(1)}, u32[]{:S(2)}, u32[]{:S(2)}) collective-permute-start(bf16[32,4096]{1,0:T(8,128)(2,1)S(1)} %collective-permute-done.4.refs_1_), channel_id=1, source_target_pairs={{0,2},{2,0},{4,6},{6,4},{8,10},{10,8},{12,14},{14,12},{16,18},{18,... | collective-permute-start | bytes 786440 | tf_op jit(solution)/shard_map/ppermute | solution.py:17
  35.1 3.4 %collective-permute-start.6 = (bf16[96,4096]{1,0:T(8,128)(2,1)S(1)}, bf16[96,4096]{1,0:T(8,128)(2,1)S(1)}, u32[]{:S(2)}, u32[]{:S(2)}) collective-permute-start(bf16[96,4096]{1,0:T(8,128)(2,1)S(1)} %shard_map.124.refs_0_), channel_id=1, source_target_pairs={{0,2},{2,0},{4,6},{6,4},{8,10},{10,8},{12,14},{14,12},{16,18},{18,... | collective-permute-start | bytes 2359304 | tf_op jit(solution)/shard_map/ppermute | solution.py:17
  37.5 8.8 %collective-permute-start.15 = (bf16[96,4096]{1,0:T(8,128)(2,1)S(1)}, bf16[96,4096]{1,0:T(8,128)(2,1)S(1)}, u32[]{:S(2)}, u32[]{:S(2)}) collective-permute-start(bf16[96,4096]{1,0:T(8,128)(2,1)S(1)} %shard_map.127.refs_0_.refs_4_), channel_id=1, source_target_pairs={{0,2},{2,0},{4,6},{6,4},{8,10},{10,8},{12,14},{14,12},{16,18},{18,... | collective-permute-start | bytes 2359304 | tf_op jit(solution)/shard_map/ppermute | solution.py:17
  37.6 8.7 %collective-permute-start.14 = (bf16[32,4096]{1,0:T(8,128)(2,1)S(1)}, bf16[32,4096]{1,0:T(8,128)(2,1)S(1)}, u32[]{:S(2)}, u32[]{:S(2)}) collective-permute-start(bf16[32,4096]{1,0:T(8,128)(2,1)S(1)} %collective-permute-done.4.refs_1_), channel_id=1, source_target_pairs={{0,4},{2,6},{4,0},{6,2},{8,12},{10,14},{12,8},{14,10},{16,20},{18,... | collective-permute-start | bytes 786440 | tf_op jit(solution)/shard_map/ppermute | solution.py:17
  37.9 4.6 %collective-permute-start.9 = (bf16[64,128]{1,0:T(8,128)(2,1)S(1)}, bf16[64,128]{1,0:T(8,128)(2,1)S(1)}, u32[]{:S(2)}, u32[]{:S(2)}) collective-permute-start(bf16[64,128]{1,0:T(8,128)(2,1)S(1)} %pad_maximum_fusion.2), channel_id=1, source_target_pairs={{0,8},{2,10},{4,12},{6,14},{8,0},{10,2},{12,4},{14,6},{16,24},{18,... | collective-permute-start | bytes 49160 | tf_op jit(solution)/shard_map/ppermute | solution.py:17
  46.4 1.5 collective-permute-start.16
  46.4 12.4 %collective-permute-start.8 = (bf16[256,768]{1,0:T(8,128)(2,1)S(1)}, bf16[256,768]{1,0:T(8,128)(2,1)S(1)}, u32[]{:S(2)}, u32[]{:S(2)}) collective-permute-start(bf16[256,768]{1,0:T(8,128)(2,1)S(1)} %get-tuple-element.62.refs_0_), channel_id=1, source_target_pairs={{0,1},{1,0},{2,3},{3,2},{4,5},{5,4},{6,7},{7,6},{8,9},{9,8},{10,11... | collective-permute-start | bytes 1179656 | tf_op jit(solution)/shard_map/ppermute | solution.py:17
  52.0 42.1 %copy-start.5 = (bf16[32,2048]{1,0:T(8,128)(2,1)S(1)}, bf16[32,2048]{1,0:T(8,128)(2,1)}, u32[]{:S(2)}) copy-start(bf16[32,2048]{1,0:T(8,128)(2,1)} %param.11) | copy-start | bytes 393220
  52.0 14.3 %collective-permute-start.17 = (bf16[256,768]{1,0:T(8,128)(2,1)S(1)}, bf16[256,768]{1,0:T(8,128)(2,1)S(1)}, u32[]{:S(2)}, u32[]{:S(2)}) collective-permute-start(bf16[256,768]{1,0:T(8,128)(2,1)S(1)} %get-tuple-element.67.refs_0_), channel_id=1, source_target_pairs={{0,1},{1,0},{2,3},{3,2},{4,5},{5,4},{6,7},{7,6},{8,9},{9,8},{10,11... | collective-permute-start | bytes 1179656 | tf_op jit(solution)/shard_map/ppermute | solution.py:17
  53.6 3.9 %collective-permute-start.10 = (bf16[128,128]{1,0:T(8,128)(2,1)S(1)}, bf16[128,128]{1,0:T(8,128)(2,1)S(1)}, u32[]{:S(2)}, u32[]{:S(2)}) collective-permute-start(bf16[128,128]{1,0:T(8,128)(2,1)S(1)} %pad_maximum_fusion.1), channel_id=1, source_target_pairs={{0,4},{2,6},{4,0},{6,2},{8,12},{10,14},{12,8},{14,10},{16,20},{18,... | collective-permute-start | bytes 98312 | tf_op jit(solution)/shard_map/ppermute | solution.py:17
  57.5 1.3 collective-permute-start.11
  68.6 2.0 %collective-permute-start.18 = (bf16[128,2048]{1,0:T(8,128)(2,1)S(1)}, bf16[128,2048]{1,0:T(8,128)(2,1)S(1)}, u32[]{:S(2)}, u32[]{:S(2)}) collective-permute-start(bf16[128,2048]{1,0:T(8,128)(2,1)S(1)} %get-tuple-element.70), channel_id=1, source_target_pairs={{0,2},{2,0},{4,6},{6,4},{8,10},{10,8},{12,14},{14,12},{16,18},{18,... | collective-permute-start | bytes 1572872 | tf_op jit(solution)/shard_map/ppermute | solution.py:17
  68.7 10.7 %collective-permute-start.12 = (bf16[128,2048]{1,0:T(8,128)(2,1)S(1)}, bf16[128,2048]{1,0:T(8,128)(2,1)S(1)}, u32[]{:S(2)}, u32[]{:S(2)}) collective-permute-start(bf16[128,2048]{1,0:T(8,128)(2,1)S(1)} %get-tuple-element.64), channel_id=1, source_target_pairs={{0,2},{2,0},{4,6},{6,4},{8,10},{10,8},{12,14},{14,12},{16,18},{18,... | collective-permute-start | bytes 1572872 | tf_op jit(solution)/shard_map/ppermute | solution.py:17
  70.7 6.4 %collective-permute-start.19 = (bf16[64,1024]{1,0:T(8,128)(2,1)S(1)}, bf16[64,1024]{1,0:T(8,128)(2,1)S(1)}, u32[]{:S(2)}, u32[]{:S(2)}) collective-permute-start(bf16[64,1024]{1,0:T(8,128)(2,1)S(1)} %get-tuple-element.123), channel_id=1, source_target_pairs={{0,4},{2,6},{4,0},{6,2},{8,12},{10,14},{12,8},{14,10},{16,20},{18,... | collective-permute-start | bytes 393224 | tf_op jit(solution)/shard_map/ppermute | solution.py:17
  71.0 8.1 %collective-permute-start.20 = (bf16[64,1024]{1,0:T(8,128)(2,1)S(1)}, bf16[64,1024]{1,0:T(8,128)(2,1)S(1)}, u32[]{:S(2)}, u32[]{:S(2)}) collective-permute-start(bf16[64,1024]{1,0:T(8,128)(2,1)S(1)} %get-tuple-element.122), channel_id=1, source_target_pairs={{0,4},{2,6},{4,0},{6,2},{8,12},{10,14},{12,8},{14,10},{16,20},{18,... | collective-permute-start | bytes 393224 | tf_op jit(solution)/shard_map/ppermute | solution.py:17
  79.1 7.7 %collective-permute-start.21 = (bf16[64,2048]{1,0:T(8,128)(2,1)S(1)}, bf16[64,2048]{1,0:T(8,128)(2,1)S(1)}, u32[]{:S(2)}, u32[]{:S(2)}) collective-permute-start(bf16[64,2048]{1,0:T(8,128)(2,1)S(1)} %add_convert_fusion.7), channel_id=1, source_target_pairs={{0,4},{2,6},{4,0},{6,2},{8,12},{10,14},{12,8},{14,10},{16,20},{18,... | collective-permute-start | bytes 786440 | tf_op jit(solution)/shard_map/ppermute | solution.py:17
  79.5 5.9 %collective-permute-start.22 = (bf16[64,1024]{1,0:T(8,128)(2,1)S(1)}, bf16[64,1024]{1,0:T(8,128)(2,1)S(1)}, u32[]{:S(2)}, u32[]{:S(2)}) collective-permute-start(bf16[64,1024]{1,0:T(8,128)(2,1)S(1)} %get-tuple-element.121), channel_id=1, source_target_pairs={{0,8},{2,10},{4,12},{6,14},{8,0},{10,2},{12,4},{14,6},{16,24},{18,... | collective-permute-start | bytes 393224 | tf_op jit(solution)/shard_map/ppermute | solution.py:17
  80.0 6.9 %collective-permute-start.24 = (bf16[64,1024]{1,0:T(8,128)(2,1)S(1)}, bf16[64,1024]{1,0:T(8,128)(2,1)S(1)}, u32[]{:S(2)}, u32[]{:S(2)}) collective-permute-start(bf16[64,1024]{1,0:T(8,128)(2,1)S(1)} %get-tuple-element.120), channel_id=1, source_target_pairs={{0,8},{2,10},{4,12},{6,14},{8,0},{10,2},{12,4},{14,6},{16,24},{18,... | collective-permute-start | bytes 393224 | tf_op jit(solution)/shard_map/ppermute | solution.py:17
  86.9 5.8 %collective-permute-start.23 = (bf16[32,1024]{1,0:T(8,128)(2,1)S(1)}, bf16[32,1024]{1,0:T(8,128)(2,1)S(1)}, u32[]{:S(2)}, u32[]{:S(2)}) collective-permute-start(bf16[32,1024]{1,0:T(8,128)(2,1)S(1)} %get-tuple-element.113), channel_id=1, source_target_pairs={{0,16},{2,18},{4,20},{6,22},{8,24},{10,26},{12,28},{14,30},{16,0},... | collective-permute-start | bytes 196616 | tf_op jit(solution)/shard_map/ppermute | solution.py:17
  87.4 6.7 %collective-permute-start.25 = (bf16[32,1024]{1,0:T(8,128)(2,1)S(1)}, bf16[32,1024]{1,0:T(8,128)(2,1)S(1)}, u32[]{:S(2)}, u32[]{:S(2)}) collective-permute-start(bf16[32,1024]{1,0:T(8,128)(2,1)S(1)} %get-tuple-element.112), channel_id=1, source_target_pairs={{0,16},{2,18},{4,20},{6,22},{8,24},{10,26},{12,28},{14,30},{16,0},... | collective-permute-start | bytes 196616 | tf_op jit(solution)/shard_map/ppermute | solution.py:17
  94.2 5.7 %collective-permute-start.26 = (bf16[32,1024]{1,0:T(8,128)(2,1)S(1)}, bf16[32,1024]{1,0:T(8,128)(2,1)S(1)}, u32[]{:S(2)}, u32[]{:S(2)}) collective-permute-start(bf16[32,1024]{1,0:T(8,128)(2,1)S(1)} %get-tuple-element.111.refs_0_), channel_id=1, source_target_pairs={{0,16},{2,18},{4,20},{6,22},{8,24},{10,26},{12,28},{14,30},{16,0},... | collective-permute-start | bytes 196616 | tf_op jit(solution)/shard_map/ppermute | solution.py:17
  95.3 6.1 %collective-permute-start.27 = (bf16[32,1024]{1,0:T(8,128)(2,1)S(1)}, bf16[32,1024]{1,0:T(8,128)(2,1)S(1)}, u32[]{:S(2)}, u32[]{:S(2)}) collective-permute-start(bf16[32,1024]{1,0:T(8,128)(2,1)S(1)} %get-tuple-element.110.refs_1_), channel_id=1, source_target_pairs={{0,16},{2,18},{4,20},{6,22},{8,24},{10,26},{12,28},{14,30},{16,0},... | collective-permute-start | bytes 196616 | tf_op jit(solution)/shard_map/ppermute | solution.py:17
  101.9 6.4 %collective-permute-start.28 = (bf16[64,2048]{1,0:T(8,128)(2,1)S(1)}, bf16[64,2048]{1,0:T(8,128)(2,1)S(1)}, u32[]{:S(2)}, u32[]{:S(2)}) collective-permute-start(bf16[64,2048]{1,0:T(8,128)(2,1)S(1)} %shard_map.130.refs_0_), channel_id=1, source_target_pairs={{0,8},{2,10},{4,12},{6,14},{8,0},{10,2},{12,4},{14,6},{16,24},{18,... | collective-permute-start | bytes 786440 | tf_op jit(solution)/shard_map/ppermute | solution.py:17
  102.0 6.4 %collective-permute-start.29 = (bf16[64,2048]{1,0:T(8,128)(2,1)S(1)}, bf16[64,2048]{1,0:T(8,128)(2,1)S(1)}, u32[]{:S(2)}, u32[]{:S(2)}) collective-permute-start(bf16[64,2048]{1,0:T(8,128)(2,1)S(1)} %shard_map.130.refs_0_), channel_id=1, source_target_pairs={{0,4},{2,6},{4,0},{6,2},{8,12},{10,14},{12,8},{14,10},{16,20},{18,... | collective-permute-start | bytes 786440 | tf_op jit(solution)/shard_map/ppermute | solution.py:17
  103.8 4.6 %collective-permute-start.30 = (bf16[64,2048]{1,0:T(8,128)(2,1)S(1)}, bf16[64,2048]{1,0:T(8,128)(2,1)S(1)}, u32[]{:S(2)}, u32[]{:S(2)}) collective-permute-start(bf16[64,2048]{1,0:T(8,128)(2,1)S(1)} %shard_map.130.refs_0_), channel_id=1, source_target_pairs={{0,2},{2,0},{4,6},{6,4},{8,10},{10,8},{12,14},{14,12},{16,18},{18,... | collective-permute-start | bytes 786440 | tf_op jit(solution)/shard_map/ppermute | solution.py:17
  108.4 2.0 %collective-permute-start.31 = (bf16[64,2048]{1,0:T(8,128)(2,1)S(1)}, bf16[64,2048]{1,0:T(8,128)(2,1)S(1)}, u32[]{:S(2)}, u32[]{:S(2)}) collective-permute-start(bf16[64,2048]{1,0:T(8,128)(2,1)S(1)} %collective-permute-done.28.refs_1_), channel_id=1, source_target_pairs={{0,2},{2,0},{4,6},{6,4},{8,10},{10,8},{12,14},{14,12},{16,18},{18,... | collective-permute-start | bytes 786440 | tf_op jit(solution)/shard_map/ppermute | solution.py:17
  108.4 8.7 %collective-permute-start.33 = (bf16[64,2048]{1,0:T(8,128)(2,1)S(1)}, bf16[64,2048]{1,0:T(8,128)(2,1)S(1)}, u32[]{:S(2)}, u32[]{:S(2)}) collective-permute-start(bf16[64,2048]{1,0:T(8,128)(2,1)S(1)} %collective-permute-done.28.refs_1_), channel_id=1, source_target_pairs={{0,4},{2,6},{4,0},{6,2},{8,12},{10,14},{12,8},{14,10},{16,20},{18,... | collective-permute-start | bytes 786440 | tf_op jit(solution)/shard_map/ppermute | solution.py:17
  110.2 7.0 %collective-permute-start.34 = (bf16[64,2048]{1,0:T(8,128)(2,1)S(1)}, bf16[64,2048]{1,0:T(8,128)(2,1)S(1)}, u32[]{:S(2)}, u32[]{:S(2)}) collective-permute-start(bf16[64,2048]{1,0:T(8,128)(2,1)S(1)} %collective-permute-done.29.refs_0_), channel_id=1, source_target_pairs={{0,2},{2,0},{4,6},{6,4},{8,10},{10,8},{12,14},{14,12},{16,18},{18,... | collective-permute-start | bytes 786440 | tf_op jit(solution)/shard_map/ppermute | solution.py:17
  113.0 11.4 %collective-permute-start.32 = (bf16[256,768]{1,0:T(8,128)(2,1)S(1)}, bf16[256,768]{1,0:T(8,128)(2,1)S(1)}, u32[]{:S(2)}, u32[]{:S(2)}) collective-permute-start(bf16[256,768]{1,0:T(8,128)(2,1)S(1)} %get-tuple-element.74), channel_id=1, source_target_pairs={{0,1},{1,0},{2,3},{3,2},{4,5},{5,4},{6,7},{7,6},{8,9},{9,8},{10,11... | collective-permute-start | bytes 1179656 | tf_op jit(solution)/shard_map/ppermute | solution.py:17
  117.2 3.9 %collective-permute-start.35 = (bf16[64,2048]{1,0:T(8,128)(2,1)S(1)}, bf16[64,2048]{1,0:T(8,128)(2,1)S(1)}, u32[]{:S(2)}, u32[]{:S(2)}) collective-permute-start(bf16[64,2048]{1,0:T(8,128)(2,1)S(1)} %collective-permute-done.33.refs_1_), channel_id=1, source_target_pairs={{0,2},{2,0},{4,6},{6,4},{8,10},{10,8},{12,14},{14,12},{16,18},{18,... | collective-permute-start | bytes 786440 | tf_op jit(solution)/shard_map/ppermute | solution.py:17
  126.8 10.6 %collective-permute-start.36 = (bf16[256,768]{1,0:T(8,128)(2,1)S(1)}, bf16[256,768]{1,0:T(8,128)(2,1)S(1)}, u32[]{:S(2)}, u32[]{:S(2)}) collective-permute-start(bf16[256,768]{1,0:T(8,128)(2,1)S(1)} %get-tuple-element.82), channel_id=1, source_target_pairs={{0,1},{1,0},{2,3},{3,2},{4,5},{5,4},{6,7},{7,6},{8,9},{9,8},{10,11... | collective-permute-start | bytes 1179656 | tf_op jit(solution)/shard_map/ppermute | solution.py:17
  132.4 23.7 %slice-start = ((s8[12582912]{0:T(1024)(128)(4,1)}), s8[4194304]{0:T(1024)(128)(4,1)S(1)}, s32[]{:S(2)}) async-start(s8[12582912]{0:T(1024)(128)(4,1)} %bitcast.8), calls=%async_computation | async-start | bytes 8388608
  132.4 23.7 %slice-start.1 = ((s8[12582912]{0:T(1024)(128)(4,1)}), s8[4194304]{0:T(1024)(128)(4,1)S(1)}, s32[]{:S(2)}) async-start(s8[12582912]{0:T(1024)(128)(4,1)} %bitcast.8), calls=%async_computation.1 | async-start | bytes 8388608
  137.4 18.7 %slice-start.2 = ((s8[12582912]{0:T(1024)(128)(4,1)}), s8[4194304]{0:T(1024)(128)(4,1)S(1)}, s32[]{:S(2)}) async-start(s8[12582912]{0:T(1024)(128)(4,1)} %bitcast.8), calls=%async_computation.2 | async-start | bytes 8388608
  141.5 2.0 %collective-permute-start.39 = (bf16[128,2048]{1,0:T(8,128)(2,1)S(1)}, bf16[128,2048]{1,0:T(8,128)(2,1)S(1)}, u32[]{:S(2)}, u32[]{:S(2)}) collective-permute-start(bf16[128,2048]{1,0:T(8,128)(2,1)S(1)} %get-tuple-element.97), channel_id=1, source_target_pairs={{0,2},{2,0},{4,6},{6,4},{8,10},{10,8},{12,14},{14,12},{16,18},{18,... | collective-permute-start | bytes 1572872 | tf_op jit(solution)/shard_map/ppermute | solution.py:17
  141.5 5.1 %collective-permute-start.38 = (bf16[128,2048]{1,0:T(8,128)(2,1)S(1)}, bf16[128,2048]{1,0:T(8,128)(2,1)S(1)}, u32[]{:S(2)}, u32[]{:S(2)}) collective-permute-start(bf16[128,2048]{1,0:T(8,128)(2,1)S(1)} %get-tuple-element.95), channel_id=1, source_target_pairs={{0,2},{2,0},{4,6},{6,4},{8,10},{10,8},{12,14},{14,12},{16,18},{18,... | collective-permute-start | bytes 1572872 | tf_op jit(solution)/shard_map/ppermute | solution.py:17
  143.6 8.4 %collective-permute-start.40 = (bf16[64,2048]{1,0:T(8,128)(2,1)S(1)}, bf16[64,2048]{1,0:T(8,128)(2,1)S(1)}, u32[]{:S(2)}, u32[]{:S(2)}) collective-permute-start(bf16[64,2048]{1,0:T(8,128)(2,1)S(1)} %get-tuple-element.116), channel_id=1, source_target_pairs={{0,4},{2,6},{4,0},{6,2},{8,12},{10,14},{12,8},{14,10},{16,20},{18,... | collective-permute-start | bytes 786440 | tf_op jit(solution)/shard_map/ppermute | solution.py:17
  144.6 10.3 %collective-permute-start.44 = (bf16[128,2048]{1,0:T(8,128)(2,1)S(1)}, bf16[128,2048]{1,0:T(8,128)(2,1)S(1)}, u32[]{:S(2)}, u32[]{:S(2)}) collective-permute-start(bf16[128,2048]{1,0:T(8,128)(2,1)S(1)} %get-tuple-element.101), channel_id=1, source_target_pairs={{0,2},{2,0},{4,6},{6,4},{8,10},{10,8},{12,14},{14,12},{16,18},{18,... | collective-permute-start | bytes 1572872 | tf_op jit(solution)/shard_map/ppermute | solution.py:17
  144.6 18.2 %collective-permute-start.37 = (bf16[128,2048]{1,0:T(8,128)(2,1)S(1)}, bf16[128,2048]{1,0:T(8,128)(2,1)S(1)}, u32[]{:S(2)}, u32[]{:S(2)}) collective-permute-start(bf16[128,2048]{1,0:T(8,128)(2,1)S(1)} %get-tuple-element.91), channel_id=1, source_target_pairs={{0,2},{2,0},{4,6},{6,4},{8,10},{10,8},{12,14},{14,12},{16,18},{18,... | collective-permute-start | bytes 1572872 | tf_op jit(solution)/shard_map/ppermute | solution.py:17
  145.1 8.2 %collective-permute-start.41 = (bf16[64,2048]{1,0:T(8,128)(2,1)S(1)}, bf16[64,2048]{1,0:T(8,128)(2,1)S(1)}, u32[]{:S(2)}, u32[]{:S(2)}) collective-permute-start(bf16[64,2048]{1,0:T(8,128)(2,1)S(1)} %get-tuple-element.117), channel_id=1, source_target_pairs={{0,1},{1,0},{2,3},{3,2},{4,5},{5,4},{6,7},{7,6},{8,9},{9,8},{10,11... | collective-permute-start | bytes 786440 | tf_op jit(solution)/shard_map/ppermute | solution.py:17
  153.3 9.5 %collective-permute-start.42 = (bf16[64,2048]{1,0:T(8,128)(2,1)S(1)}, bf16[64,2048]{1,0:T(8,128)(2,1)S(1)}, u32[]{:S(2)}, u32[]{:S(2)}) collective-permute-start(bf16[64,2048]{1,0:T(8,128)(2,1)S(1)} %get-tuple-element.98), channel_id=1, source_target_pairs={{0,1},{1,0},{2,3},{3,2},{4,5},{5,4},{6,7},{7,6},{8,9},{9,8},{10,11... | collective-permute-start | bytes 786440 | tf_op jit(solution)/shard_map/ppermute | solution.py:17
  155.0 7.8 %collective-permute-start.45 = (bf16[64,2048]{1,0:T(8,128)(2,1)S(1)}, bf16[64,2048]{1,0:T(8,128)(2,1)S(1)}, u32[]{:S(2)}, u32[]{:S(2)}) collective-permute-start(bf16[64,2048]{1,0:T(8,128)(2,1)S(1)} %get-tuple-element.118), channel_id=1, source_target_pairs={{0,4},{2,6},{4,0},{6,2},{8,12},{10,14},{12,8},{14,10},{16,20},{18,... | collective-permute-start | bytes 786440 | tf_op jit(solution)/shard_map/ppermute | solution.py:17
  162.9 7.3 %collective-permute-start.47 = (bf16[64,2048]{1,0:T(8,128)(2,1)S(1)}, bf16[64,2048]{1,0:T(8,128)(2,1)S(1)}, u32[]{:S(2)}, u32[]{:S(2)}) collective-permute-start(bf16[64,2048]{1,0:T(8,128)(2,1)S(1)} %add_convert_fusion), channel_id=1, source_target_pairs={{0,8},{2,10},{4,12},{6,14},{8,0},{10,2},{12,4},{14,6},{16,24},{18,... | collective-permute-start | bytes 786440 | tf_op jit(solution)/shard_map/ppermute | solution.py:17
  164.9 6.5 %collective-permute-start.43 = (bf16[64,2048]{1,0:T(8,128)(2,1)S(1)}, bf16[64,2048]{1,0:T(8,128)(2,1)S(1)}, u32[]{:S(2)}, u32[]{:S(2)}) collective-permute-start(bf16[64,2048]{1,0:T(8,128)(2,1)S(1)} %get-tuple-element.99), channel_id=1, source_target_pairs={{0,1},{1,0},{2,3},{3,2},{4,5},{5,4},{6,7},{7,6},{8,9},{9,8},{10,11... | collective-permute-start | bytes 786440 | tf_op jit(solution)/shard_map/ppermute | solution.py:17
  165.4 6.4 %collective-permute-start.46 = (bf16[64,2048]{1,0:T(8,128)(2,1)S(1)}, bf16[64,2048]{1,0:T(8,128)(2,1)S(1)}, u32[]{:S(2)}, u32[]{:S(2)}) collective-permute-start(bf16[64,2048]{1,0:T(8,128)(2,1)S(1)} %get-tuple-element.102), channel_id=1, source_target_pairs={{0,4},{2,6},{4,0},{6,2},{8,12},{10,14},{12,8},{14,10},{16,20},{18,... | collective-permute-start | bytes 786440 | tf_op jit(solution)/shard_map/ppermute | solution.py:17
  171.9 7.0 %collective-permute-start.48 = (bf16[32,2048]{1,0:T(8,128)(2,1)S(1)}, bf16[32,2048]{1,0:T(8,128)(2,1)S(1)}, u32[]{:S(2)}, u32[]{:S(2)}) collective-permute-start(bf16[32,2048]{1,0:T(8,128)(2,1)S(1)} %add_convert_fusion.9), channel_id=1, source_target_pairs={{0,16},{2,18},{4,20},{6,22},{8,24},{10,26},{12,28},{14,30},{16,0},... | collective-permute-start | bytes 393224 | tf_op jit(solution)/shard_map/ppermute | solution.py:17

commit v8 on v7

--- a/solution.py
+++ b/solution.py
@@ -35,12 +35,10 @@
     return parts[0] if len(parts) == 1 else jnp.concatenate(parts, axis=0)
 
 
-def gather_far(block, *after):
+def gather_far(block):
     parts = [block]
     for distance in far_distances():
         parts.append(swap(join(parts), "expert", distance))
-        if after:
-            parts[-1] = tie(parts[-1], *after)
     return parts
 
 
@@ -205,6 +203,60 @@
 
     return resident(
         kernel, [codes, low, high], [((height, count * cols), BF16)], place
+    )[0]
+
+
+def dequant_wide(place, codes, low, high, mib):
+    count, height, cols = codes.shape
+    groups = low.shape[1]
+    size = height // groups
+    per = next(p for p in (4, 2, 1) if groups % p == 0)
+    steps = groups // per
+    rows = per * size
+
+    def kernel(place_ref, code_hbm, low_hbm, high_hbm, out_ref, code_ref, low_ref, high_ref, sems):
+        ends = [
+            pltpu.make_async_copy(low_hbm, low_ref, sems.at[steps]),
+            pltpu.make_async_copy(high_hbm, high_ref, sems.at[steps + 1]),
+        ]
+        blocks = []
+        for i in range(steps):
+            held = slice(i * rows, (i + 1) * rows)
+            blocks.append(
+                pltpu.make_async_copy(code_hbm.at[:, held, :], code_ref.at[:, held, :], sems.at[i])
+            )
+        for copy in ends + blocks:
+            copy.start()
+        for copy in ends:
+            copy.wait()
+        for i in range(steps):
+            blocks[i].wait()
+
+            def group(j, carry):
+                at = i * per + j
+                held = pl.ds(pl.multiple_of(at * size, size), size)
+                for k in range(count):
+                    bottom = low_ref[k, pl.ds(at, 1), :]
+                    scale = (high_ref[k, pl.ds(at, 1), :] - bottom) * (1.0 / 255.0)
+                    vals = code_ref[k, held, :].astype(F32)
+                    out_ref[held, k * cols : (k + 1) * cols] = (bottom + scale * vals).astype(BF16)
+                return carry
+
+            lax.fori_loop(0, per, group, 0)
+
+    return call(
+        kernel,
+        (),
+        [(a, pltpu.HBM, None) for a in (codes, low, high)],
+        [((height, count * cols), BF16, pltpu.VMEM, None)],
+        place,
+        scratch=[
+            pltpu.VMEM(codes.shape, BF16),
+            pltpu.VMEM(low.shape, F32),
+            pltpu.VMEM(high.shape, F32),
+            pltpu.SemaphoreType.DMA((steps + 2,)),
+        ],
+        mib=mib,
     )[0]
 
 
@@ -521,15 +573,14 @@
     terms = prepare(place, routes, route_scores, extra)
     near_own = tie(near_own, terms)
     across_near = swap(near_own, "expert", 2)
-    w_in = dequant(place, in_codes[0], tie(in_low, near_own)[0], in_high[0])
-    far = tie(far, w_in, across_own, across_near)
+    terms = join(gather_far(terms))
+    far = tie(far, across_own, across_near, terms)
     near_far = swap(far, "expert", 4)
     across_far = swap(far, "expert", 2)
-    w_down = dequant(place, down_codes, tie(down_low, far), down_high, halves)
-    first = pack(place, [[tokens], [tie(far, w_down)], [near_own]])
+    w_in = dequant_wide(place, in_codes[0], tie(in_low, far)[0], in_high[0], 30)
+    near_far = tie(near_far, w_in)
+    first = pack(place, [[tokens], [far], [near_own]])
     first_other = swap(first, "expert", 1)
-    terms = join(gather_far(terms, w_down))
-    near_far = tie(near_far, w_down, terms)
     across_last = swap(near_far, "expert", 2)
     near_other = swap(near_far, "expert", 1)
     x = [[first, near_far, first_other, near_other]]
@@ -540,9 +591,11 @@
         if c == 1:
             second = pack(place, [[across_own], [tie(across_far, near_other)], [across_near]])
             second_other = swap(second, "expert", 1)
-            across_last = tie(across_last, hidden[0][0], near_terms, second_other)
+            across_last = tie(across_last, w_down, near_terms, second_other)
             x.append([second, across_last, second_other, swap(across_last, "expert", 1)])
         own, chunk_slope, chunk_act = forward_in(place, x[c], w_in)
+        if c == 0:
+            w_down = dequant(place, down_codes, tie(down_low, own), down_high, halves)
         hidden.append([own] + [swap(own, "half", d) for d in parts if d])
         slope.append(chunk_slope)
         act.append(chunk_act)

time: 180 us -> 179 us (level)
  local copies, waits for them, and re-layouts: 8.88 us -> 4.32 us
  Pallas kernels: 56.5 us -> 59.2 us
    unnamed x26, local copies, waits for them, and re-layouts: 8.85 us -> 4.29 us
    pallas_call x19, Pallas kernels: 56.5 us -> 59.2 us  [call(): pl.pallas_call(kernel, grid_spec=pltpu.PrefetchScalarGridSpec(num_scalar_...]
  transfers between devices with their start and end apart: 49 -> 49, of which waited for: 27 -> 29; matrix products, arithmetic and copies ran while one was open for 2% -> 2% of each run, Pallas kernels for 26% -> 28%
where the time goes in v8:
time: 179 us
  waiting for transfers between devices  63.4 us (35%)
  Pallas kernels  59.2 us (33%)
  starting transfers between devices  48.6 us (27%)
  local copies, waits for them, and re-layouts  4.32 us (2%)
  other arithmetic  1.98 us (1%)
    ppermute x49, waiting for transfers between devices, swap(): return lax.ppermute(array, axis, [(i, i ^ distance) for i in range(size)])  63.4 us
    pallas_call x19, Pallas kernels, call(): pl.pallas_call(kernel, grid_spec=pltpu.PrefetchScalarGridSpec(num_scalar_...  59.2 us
    ppermute x49, starting transfers between devices, swap(): return lax.ppermute(array, axis, [(i, i ^ distance) for i in range(size)])  48.6 us
    unnamed x26, local copies, waits for them, and re-layouts  4.29 us
  transfers between devices with their start and end apart: 49, of which 29 were waited for; matrix products, arithmetic and copies ran while one was open for 2% of the time, Pallas kernels for 28%

profile of v8, /device:TPU:0, one launch (start us, length us, event | category | flops | bytes accessed | tf_op | source)
XLA Modules:
  0.0 178.6 jit_solution(14567217262833571983)
XLA Ops:
  0.6 3.1 %collective-permute-start.2 = (bf16[32,4096]{1,0:T(8,128)(2,1)}, bf16[32,4096]{1,0:T(8,128)(2,1)S(1)}, u32[]{:S(2)}, u32[]{:S(2)}) collective-permute-start(bf16[32,4096]{1,0:T(8,128)(2,1)} %refs_0_.1), channel_id=1, source_target_pairs={{0,8},{2,10},{4,12},{6,14},{8,0},{10,2},{12,4},{14,6},{16,24},{18,... | collective-permute-start | bytes 786440 | tf_op jit(solution)/shard_map/ppermute | solution.py:17
  3.7 1.5 collective-permute-start.1
  5.2 2.6 %collective-permute-start = (bf16[32,4096]{1,0:T(8,128)(2,1)}, bf16[32,4096]{1,0:T(8,128)(2,1)S(1)}, u32[]{:S(2)}, u32[]{:S(2)}) collective-permute-start(bf16[32,4096]{1,0:T(8,128)(2,1)} %refs_0_.1), channel_id=1, source_target_pairs={{0,16},{2,18},{4,20},{6,22},{8,24},{10,26},{12,28},{14,30},{16,0},... | collective-permute-start | bytes 786440 | tf_op jit(solution)/shard_map/ppermute | solution.py:17
  10.2 4.4 %collective-permute-done.2.refs_2_ = bf16[32,4096]{1,0:T(8,128)(2,1)S(1)} collective-permute-done((bf16[32,4096]{1,0:T(8,128)(2,1)}, bf16[32,4096]{1,0:T(8,128)(2,1)S(1)}, u32[]{:S(2)}, u32[]{:S(2)}) %collective-permute-start.2) | collective-permute-done | bytes 262176 | tf_op jit(solution)/shard_map/ppermute | solution.py:17
  14.5 2.6 %collective-permute-start.3 = (bf16[32,4096]{1,0:T(8,128)(2,1)S(1)}, bf16[32,4096]{1,0:T(8,128)(2,1)S(1)}, u32[]{:S(2)}, u32[]{:S(2)}) collective-permute-start(bf16[32,4096]{1,0:T(8,128)(2,1)S(1)} %collective-permute-done.2.refs_2_), channel_id=1, source_target_pairs={{0,4},{2,6},{4,0},{6,2},{8,12},{10,14},{12,8},{14,10},{16,20},{18,... | collective-permute-start | bytes 786440 | tf_op jit(solution)/shard_map/ppermute | solution.py:17
  17.8 3.9 %collective-permute-done.4 = bf16[32,128]{1,0:T(8,128)(2,1)S(1)} collective-permute-done((bf16[32,128]{1,0:T(8,128)(2,1)S(1)}, bf16[32,128]{1,0:T(8,128)(2,1)S(1)}, u32[]{:S(2)}, u32[]{:S(2)}) %collective-permute-start.4) | collective-permute-done | bytes 8224 | tf_op jit(solution)/shard_map/ppermute | solution.py:17
  22.6 1.7 collective-permute-start.13
  24.3 0.9 copy-done.1
  25.2 0.9 copy-done.2
  26.2 6.2 %shard_map.123.refs_4_.refs_3_ = bf16[4096,1536]{1,0:T(8,128)(2,1)S(1)} custom-call(s32[2]{0:T(128)S(1)} %pad_add_fusion.place_ref, bf16[2,4096,768]{2,1,0:T(8,128)(2,1)} %bitcast.7, f32[2,32,768]{2,1,0:T(8,128)S(1)} %bitcast.13, f32[2,32,768]{2,1,0:T(8,128)S(1)} %bitcast.14), custom_call_target="tpu_custom_call" | custom-call | bytes 25 | tf_op jit(solution)/shard_map/pallas_call | solution.py:112
  35.1 2.0 %collective-permute-start.9 = (bf16[64,128]{1,0:T(8,128)(2,1)S(1)}, bf16[64,128]{1,0:T(8,128)(2,1)S(1)}, u32[]{:S(2)}, u32[]{:S(2)}) collective-permute-start(bf16[64,128]{1,0:T(8,128)(2,1)S(1)} %pad_maximum_fusion.2), channel_id=1, source_target_pairs={{0,8},{2,10},{4,12},{6,14},{8,0},{10,2},{12,4},{14,6},{16,24},{18,... | collective-permute-start | bytes 49160 | tf_op jit(solution)/shard_map/ppermute | solution.py:17
  37.1 4.1 %shard_map.124 = (bf16[256,768]{1,0:T(8,128)(2,1)S(1)}, f32[256,768]{1,0:T(8,128)S(1)}, f32[256,768]{1,0:T(8,128)S(1)}) custom-call(s32[2]{0:T(128)S(1)} %pad_add_fusion.place_ref, bf16[96,4096]{1,0:T(8,128)(2,1)S(1)} %shard_map.122.refs_0_, bf16[32,4096]{1,0:T(8,128)(2,1)S(1)} %collective-permute-done.5.refs_1_, ...), custom_call_target="tpu_custom_call" | custom-call | flops 3221 | bytes 16 | tf_op jit(solution)/shard_map/pallas_call | solution.py:112
  41.3 2.4 %shard_map.125.refs_2_.refs_6_ = bf16[1536,2048]{1,0:T(8,128)(2,1)S(1)} custom-call(s32[2]{0:T(128)S(1)} %pad_add_fusion.place_ref, bf16[1,1536,2048]{2,1,0:T(8,128)(2,1)S(1)} %bitcast.11, f32[1,12,2048]{2,1,0:T(8,128)S(1)} %copy.17.low_ref, f32[1,12,2048]{2,1,0:T(8,128)S(1)} %copy.18.high_ref), custom_call_target="tpu_custom_call" | custom-call | bytes 12 | tf_op jit(solution)/shard_map/pallas_call | solution.py:112
  43.9 1.6 collective-permute-start.8
  45.5 4.1 %shard_map.128 = (bf16[256,768]{1,0:T(8,128)(2,1)S(1)}, f32[256,768]{1,0:T(8,128)S(1)}, f32[256,768]{1,0:T(8,128)S(1)}) custom-call(s32[2]{0:T(128)S(1)} %pad_add_fusion.place_ref, bf16[96,4096]{1,0:T(8,128)(2,1)S(1)} %shard_map.127.refs_0_.refs_4_, bf16[32,4096]{1,0:T(8,128)(2,1)S(1)} %collective-permute-done.14.refs_1_.refs_5_, ...), custom_call_target="tpu_custom_call" | custom-call | flops 3221 | bytes 16 | tf_op jit(solution)/shard_map/pallas_call | solution.py:112
  49.5 1.5 collective-permute-start.17
  51.1 1.7 collective-permute-start.10
  52.8 2.2 %collective-permute-done.10 = bf16[128,128]{1,0:T(8,128)(2,1)S(1)} collective-permute-done((bf16[128,128]{1,0:T(8,128)(2,1)S(1)}, bf16[128,128]{1,0:T(8,128)(2,1)S(1)}, u32[]{:S(2)}, u32[]{:S(2)}) %collective-permute-start.10) | collective-permute-done | bytes 32800 | tf_op jit(solution)/shard_map/ppermute | solution.py:17
  55.0 1.2 collective-permute-done.11.refs_4_.refs_5_
  56.2 2.3 %shard_map.126 = (bf16[128,2048]{1,0:T(8,128)(2,1)S(1)}, bf16[128,2048]{1,0:T(8,128)(2,1)S(1)}) custom-call(s32[2]{0:T(128)S(1)} %pad_add_fusion.place_ref, bf16[256,768]{1,0:T(8,128)(2,1)S(1)} %get-tuple-element.57.refs_0_, bf16[256,768]{1,0:T(8,128)(2,1)S(1)} %collective-permute-done.8.refs_1_, bf16[1536,2048]{1,0:T(8,128)(2,1)S(1)} %shard_map.125.refs_2_.refs_6_, ...), custom_call_target="tpu_custom_call" | custom-call | flops 1610 | bytes 8 | tf_op jit(solution)/shard_map/pallas_call | solution.py:112
  58.6 5.2 %collective-permute-done.17.refs_1_ = bf16[256,768]{1,0:T(8,128)(2,1)S(1)} collective-permute-done((bf16[256,768]{1,0:T(8,128)(2,1)S(1)}, bf16[256,768]{1,0:T(8,128)(2,1)S(1)}, u32[]{:S(2)}, u32[]{:S(2)}) %collective-permute-start.17) | collective-permute-done | bytes 393248 | tf_op jit(solution)/shard_map/ppermute | solution.py:17
  63.8 2.3 %shard_map.129 = (bf16[128,2048]{1,0:T(8,128)(2,1)S(1)}, bf16[128,2048]{1,0:T(8,128)(2,1)S(1)}) custom-call(s32[2]{0:T(128)S(1)} %pad_add_fusion.place_ref, bf16[256,768]{1,0:T(8,128)(2,1)S(1)} %get-tuple-element.63.refs_0_, bf16[256,768]{1,0:T(8,128)(2,1)S(1)} %collective-permute-done.17.refs_1_, bf16[1536,2048]{1,0:T(8,128)(2,1)S(1)} %shard_map.125.refs_2_.refs_6_, ...), custom_call_target="tpu_custom_call" | custom-call | flops 1610 | bytes 8 | tf_op jit(solution)/shard_map/pallas_call | solution.py:112
  66.7 1.4 collective-permute-done.18
  68.2 1.8 %collective-permute-start.19 = (bf16[64,1024]{1,0:T(8,128)(2,1)S(1)}, bf16[64,1024]{1,0:T(8,128)(2,1)S(1)}, u32[]{:S(2)}, u32[]{:S(2)}) collective-permute-start(bf16[64,1024]{1,0:T(8,128)(2,1)S(1)} %get-tuple-element.119), channel_id=1, source_target_pairs={{0,4},{2,6},{4,0},{6,2},{8,12},{10,14},{12,8},{14,10},{16,20},{18,... | collective-permute-start | bytes 393224 | tf_op jit(solution)/shard_map/ppermute | solution.py:17
  70.4 4.2 %collective-permute-done.19 = bf16[64,1024]{1,0:T(8,128)(2,1)S(1)} collective-permute-done((bf16[64,1024]{1,0:T(8,128)(2,1)S(1)}, bf16[64,1024]{1,0:T(8,128)(2,1)S(1)}, u32[]{:S(2)}, u32[]{:S(2)}) %collective-permute-start.19) | collective-permute-done | bytes 131104 | tf_op jit(solution)/shard_map/ppermute | solution.py:17
  74.6 2.0 %collective-permute-done.20 = bf16[64,1024]{1,0:T(8,128)(2,1)S(1)} collective-permute-done((bf16[64,1024]{1,0:T(8,128)(2,1)S(1)}, bf16[64,1024]{1,0:T(8,128)(2,1)S(1)}, u32[]{:S(2)}, u32[]{:S(2)}) %collective-permute-start.20) | collective-permute-done | bytes 131104 | tf_op jit(solution)/shard_map/ppermute | solution.py:17
  76.6 1.7 collective-permute-start.21
  78.6 2.0 %collective-permute-start.24 = (bf16[64,1024]{1,0:T(8,128)(2,1)S(1)}, bf16[64,1024]{1,0:T(8,128)(2,1)S(1)}, u32[]{:S(2)}, u32[]{:S(2)}) collective-permute-start(bf16[64,1024]{1,0:T(8,128)(2,1)S(1)} %get-tuple-element.116), channel_id=1, source_target_pairs={{0,8},{2,10},{4,12},{6,14},{8,0},{10,2},{12,4},{14,6},{16,24},{18,... | collective-permute-start | bytes 393224 | tf_op jit(solution)/shard_map/ppermute | solution.py:17
  80.6 3.8 %collective-permute-done.22 = bf16[64,1024]{1,0:T(8,128)(2,1)S(1)} collective-permute-done((bf16[64,1024]{1,0:T(8,128)(2,1)S(1)}, bf16[64,1024]{1,0:T(8,128)(2,1)S(1)}, u32[]{:S(2)}, u32[]{:S(2)}) %collective-permute-start.22) | collective-permute-done | bytes 131104 | tf_op jit(solution)/shard_map/ppermute | solution.py:17
  84.4 1.4 collective-permute-done.24
  85.9 1.4 collective-permute-start.23
  87.3 1.6 collective-permute-start.25
  88.9 3.0 %collective-permute-done.23 = bf16[32,1024]{1,0:T(8,128)(2,1)S(1)} collective-permute-done((bf16[32,1024]{1,0:T(8,128)(2,1)S(1)}, bf16[32,1024]{1,0:T(8,128)(2,1)S(1)}, u32[]{:S(2)}, u32[]{:S(2)}) %collective-permute-start.23) | collective-permute-done | bytes 65568 | tf_op jit(solution)/shard_map/ppermute | solution.py:17
  92.7 1.6 collective-permute-start.26
  94.3 1.4 collective-permute-start.27
  95.7 2.5 %collective-permute-done.26.refs_2_ = bf16[32,1024]{1,0:T(8,128)(2,1)S(1)} collective-permute-done((bf16[32,1024]{1,0:T(8,128)(2,1)S(1)}, bf16[32,1024]{1,0:T(8,128)(2,1)S(1)}, u32[]{:S(2)}, u32[]{:S(2)}) %collective-permute-start.26) | collective-permute-done | bytes 65568 | tf_op jit(solution)/shard_map/ppermute | solution.py:17
  98.2 1.6 collective-permute-done.27.refs_3_
  100.3 3.3 %collective-permute-start.28 = (bf16[64,2048]{1,0:T(8,128)(2,1)S(1)}, bf16[64,2048]{1,0:T(8,128)(2,1)S(1)}, u32[]{:S(2)}, u32[]{:S(2)}) collective-permute-start(bf16[64,2048]{1,0:T(8,128)(2,1)S(1)} %shard_map.130.refs_0_), channel_id=1, source_target_pairs={{0,8},{2,10},{4,12},{6,14},{8,0},{10,2},{12,4},{14,6},{16,24},{18,... | collective-permute-start | bytes 786440 | tf_op jit(solution)/shard_map/ppermute | solution.py:17
  103.6 4.3 %collective-permute-done.28.refs_1_ = bf16[64,2048]{1,0:T(8,128)(2,1)S(1)} collective-permute-done((bf16[64,2048]{1,0:T(8,128)(2,1)S(1)}, bf16[64,2048]{1,0:T(8,128)(2,1)S(1)}, u32[]{:S(2)}, u32[]{:S(2)}) %collective-permute-start.28) | collective-permute-done | bytes 262176 | tf_op jit(solution)/shard_map/ppermute | solution.py:17
  107.9 2.0 %collective-permute-done.29.refs_0_ = bf16[64,2048]{1,0:T(8,128)(2,1)S(1)} collective-permute-done((bf16[64,2048]{1,0:T(8,128)(2,1)S(1)}, bf16[64,2048]{1,0:T(8,128)(2,1)S(1)}, u32[]{:S(2)}, u32[]{:S(2)}) %collective-permute-start.29) | collective-permute-done | bytes 262176 | tf_op jit(solution)/shard_map/ppermute | solution.py:17
  110.5 1.0 collective-permute-done.31.refs_3_
  111.5 2.4 %shard_map.131 = (bf16[256,2048]{1,0:T(8,128)(2,1)S(1)}, f32[256,768]{1,0:T(8,128)S(1)}, bf16[256,768]{1,0:T(8,128)(2,1)S(1)}) custom-call(s32[2]{0:T(128)S(1)} %pad_add_fusion.place_ref, bf16[64,2048]{1,0:T(8,128)(2,1)S(1)} %shard_map.130.refs_0_, bf16[64,2048]{1,0:T(8,128)(2,1)S(1)} %collective-permute-done.28.refs_1_, ...), custom_call_target="tpu_custom_call" | custom-call | flops 1610 | bytes 9 | tf_op jit(solution)/shard_map/pallas_call | solution.py:112
  113.9 1.6 collective-permute-start.32
  115.5 3.2 %collective-permute-done.33.refs_1_ = bf16[64,2048]{1,0:T(8,128)(2,1)S(1)} collective-permute-done((bf16[64,2048]{1,0:T(8,128)(2,1)S(1)}, bf16[64,2048]{1,0:T(8,128)(2,1)S(1)}, u32[]{:S(2)}, u32[]{:S(2)}) %collective-permute-start.33) | collective-permute-done | bytes 262176 | tf_op jit(solution)/shard_map/ppermute | solution.py:17
  118.7 4.1 %shard_map.133.refs_4_ = f32[2,12,2048]{2,1,0:T(8,128)S(1)} custom-call(s32[2]{0:T(128)S(1)} %pad_add_fusion.place_ref, bf16[256,768]{1,0:T(8,128)(2,1)S(1)} %get-tuple-element.57.refs_0_, bf16[256,768]{1,0:T(8,128)(2,1)S(1)} %collective-permute-done.8.refs_1_, bf16[256,2048]{1,0:T(8,128)(2,1)S(1)} %get-tuple-element.74.refs_2_, ...), custom_call_target="tpu_custom_call" | custom-call | flops 1610 | bytes 8 | tf_op jit(solution)/shard_map/pallas_call | solution.py:112
  122.8 2.3 %collective-permute-done.32.refs_0_ = bf16[256,768]{1,0:T(8,128)(2,1)S(1)} collective-permute-done((bf16[256,768]{1,0:T(8,128)(2,1)S(1)}, bf16[256,768]{1,0:T(8,128)(2,1)S(1)}, u32[]{:S(2)}, u32[]{:S(2)}) %collective-permute-start.32) | collective-permute-done | bytes 393248 | tf_op jit(solution)/shard_map/ppermute | solution.py:17
  125.1 2.4 %shard_map.134 = (bf16[256,2048]{1,0:T(8,128)(2,1)S(1)}, f32[256,768]{1,0:T(8,128)S(1)}, bf16[256,768]{1,0:T(8,128)(2,1)S(1)}) custom-call(s32[2]{0:T(128)S(1)} %pad_add_fusion.place_ref, bf16[64,2048]{1,0:T(8,128)(2,1)S(1)} %collective-permute-done.29.refs_0_, bf16[64,2048]{1,0:T(8,128)(2,1)S(1)} %collective-permute-done.33.refs_1_, ...), custom_call_target="tpu_custom_call" | custom-call | flops 1610 | bytes 9 | tf_op jit(solution)/shard_map/pallas_call | solution.py:112
  127.6 1.6 collective-permute-start.36
  129.2 4.0 %shard_map.135 = f32[2,12,2048]{2,1,0:T(8,128)S(1)} custom-call(s32[2]{0:T(128)S(1)} %pad_add_fusion.place_ref, bf16[256,768]{1,0:T(8,128)(2,1)S(1)} %get-tuple-element.63.refs_0_, bf16[256,768]{1,0:T(8,128)(2,1)S(1)} %collective-permute-done.17.refs_1_, bf16[256,2048]{1,0:T(8,128)(2,1)S(1)} %get-tuple-element.80.refs_2_, ...), custom_call_target="tpu_custom_call" | custom-call | flops 1610 | bytes 8 | tf_op jit(solution)/shard_map/pallas_call | solution.py:112
  133.2 4.0 %shard_map.132 = (bf16[256,1536]{1,0:T(8,128)(2,1)S(1)}, bf16[128,2048]{1,0:T(8,128)(2,1)S(1)}, bf16[128,2048]{1,0:T(8,128)(2,1)S(1)}, bf16[128,2048]{1,0:T(8,128)(2,1)S(1)}, bf16[128,2048]{1,0:T(8,128)(2,1)S(1)}) custom-call(s32[2]{0:T(128)S(1)} %pad_add_fusion.place_ref, f32[256,768]{1,0:T(8,128)S(1)} %get-tuple-element.69.grad_own_ref, ...), custom_call_target="tpu_custom_call" | custom-call | flops 3221 | bytes 18 | tf_op jit(solution)/shard_map/pallas_call | solution.py:112
  138.0 4.0 %shard_map.136 = (bf16[256,1536]{1,0:T(8,128)(2,1)S(1)}, bf16[128,2048]{1,0:T(8,128)(2,1)S(1)}, bf16[128,2048]{1,0:T(8,128)(2,1)S(1)}, bf16[128,2048]{1,0:T(8,128)(2,1)S(1)}, bf16[128,2048]{1,0:T(8,128)(2,1)S(1)}) custom-call(s32[2]{0:T(128)S(1)} %pad_add_fusion.place_ref, f32[256,768]{1,0:T(8,128)S(1)} %get-tuple-element.77.grad_own_ref, ...), custom_call_target="tpu_custom_call" | custom-call | flops 3221 | bytes 18 | tf_op jit(solution)/shard_map/pallas_call | solution.py:112
  142.6 1.4 collective-permute-done.39
  144.1 1.1 collective-permute-start.40
  145.7 1.5 collective-permute-start.41
  147.2 5.3 %collective-permute-done.40 = bf16[64,2048]{1,0:T(8,128)(2,1)S(1)} collective-permute-done((bf16[64,2048]{1,0:T(8,128)(2,1)S(1)}, bf16[64,2048]{1,0:T(8,128)(2,1)S(1)}, u32[]{:S(2)}, u32[]{:S(2)}) %collective-permute-start.40) | collective-permute-done | bytes 262176 | tf_op jit(solution)/shard_map/ppermute | solution.py:17
  152.7 1.2 collective-permute-done.41
  153.9 1.5 collective-permute-start.42
  155.6 1.1 collective-permute-start.45
  156.7 6.4 %shard_map.137.refs_11_ = f32[4,32,768]{2,1,0:T(8,128)} custom-call(s32[2]{0:T(128)S(1)} %pad_add_fusion.place_ref, bf16[96,4096]{1,0:T(8,128)(2,1)S(1)} %shard_map.122.refs_0_, bf16[32,4096]{1,0:T(8,128)(2,1)S(1)} %collective-permute-done.5.refs_1_, bf16[96,4096]{1,0:T(8,128)(2,1)S(1)} %collective-permute-done.6.refs_2_, ...), custom_call_target="tpu_custom_call" | custom-call | flops 3221 | bytes 18 | tf_op jit(solution)/shard_map/pallas_call | solution.py:112
  163.9 1.1 collective-permute-start.46
  165.0 4.1 %shard_map.138.refs_11_ = f32[4,32,768]{2,1,0:T(8,128)} custom-call(s32[2]{0:T(128)S(1)} %pad_add_fusion.place_ref, bf16[96,4096]{1,0:T(8,128)(2,1)S(1)} %shard_map.122.refs_0_, bf16[32,4096]{1,0:T(8,128)(2,1)S(1)} %collective-permute-done.5.refs_1_, bf16[96,4096]{1,0:T(8,128)(2,1)S(1)} %collective-permute-done.6.refs_2_, ...), custom_call_target="tpu_custom_call", output_to_operand_aliasing={{}: (12, {})} | custom-call | flops 1610 | bytes 18 | tf_op jit(solution)/shard_map/pallas_call | solution.py:112
  169.1 1.0 collective-permute-done.47
  172.3 3.8 %shard_map.139 = f32[4,32,768]{2,1,0:T(8,128)} custom-call(s32[2]{0:T(128)S(1)} %pad_add_fusion.place_ref, bf16[96,4096]{1,0:T(8,128)(2,1)S(1)} %shard_map.122.refs_0_, bf16[32,4096]{1,0:T(8,128)(2,1)S(1)} %collective-permute-done.5.refs_1_, bf16[96,4096]{1,0:T(8,128)(2,1)S(1)} %collective-permute-done.6.refs_2_, ...), custom_call_target="tpu_custom_call", output_to_operand_aliasing={{}: (12, {})} | custom-call | flops 1610 | bytes 18 | tf_op jit(solution)/shard_map/pallas_call | solution.py:112
  176.1 1.8 collective-permute-done.48
  (97 shorter events, 16.0 us)
Async XLA Ops:
  0.6 13.9 %collective-permute-start.2 = (bf16[32,4096]{1,0:T(8,128)(2,1)}, bf16[32,4096]{1,0:T(8,128)(2,1)S(1)}, u32[]{:S(2)}, u32[]{:S(2)}) collective-permute-start(bf16[32,4096]{1,0:T(8,128)(2,1)} %refs_0_.1), channel_id=1, source_target_pairs={{0,8},{2,10},{4,12},{6,14},{8,0},{10,2},{12,4},{14,6},{16,24},{18,... | collective-permute-start | bytes 786440 | tf_op jit(solution)/shard_map/ppermute | solution.py:17
  3.7 18.0 %collective-permute-start.1 = (bf16[32,4096]{1,0:T(8,128)(2,1)}, bf16[32,4096]{1,0:T(8,128)(2,1)S(1)}, u32[]{:S(2)}, u32[]{:S(2)}) collective-permute-start(bf16[32,4096]{1,0:T(8,128)(2,1)} %refs_0_.1), channel_id=1, source_target_pairs={{0,4},{2,6},{4,0},{6,2},{8,12},{10,14},{12,8},{14,10},{16,20},{18,... | collective-permute-start | bytes 786440 | tf_op jit(solution)/shard_map/ppermute | solution.py:17
  5.2 16.5 %collective-permute-start = (bf16[32,4096]{1,0:T(8,128)(2,1)}, bf16[32,4096]{1,0:T(8,128)(2,1)S(1)}, u32[]{:S(2)}, u32[]{:S(2)}) collective-permute-start(bf16[32,4096]{1,0:T(8,128)(2,1)} %refs_0_.1), channel_id=1, source_target_pairs={{0,16},{2,18},{4,20},{6,22},{8,24},{10,26},{12,28},{14,30},{16,0},... | collective-permute-start | bytes 786440 | tf_op jit(solution)/shard_map/ppermute | solution.py:17
  14.5 8.0 %collective-permute-start.3 = (bf16[32,4096]{1,0:T(8,128)(2,1)S(1)}, bf16[32,4096]{1,0:T(8,128)(2,1)S(1)}, u32[]{:S(2)}, u32[]{:S(2)}) collective-permute-start(bf16[32,4096]{1,0:T(8,128)(2,1)S(1)} %collective-permute-done.2.refs_2_), channel_id=1, source_target_pairs={{0,4},{2,6},{4,0},{6,2},{8,12},{10,14},{12,8},{14,10},{16,20},{18,... | collective-permute-start | bytes 786440 | tf_op jit(solution)/shard_map/ppermute | solution.py:17
  17.1 4.5 %collective-permute-start.4 = (bf16[32,128]{1,0:T(8,128)(2,1)S(1)}, bf16[32,128]{1,0:T(8,128)(2,1)S(1)}, u32[]{:S(2)}, u32[]{:S(2)}) collective-permute-start(bf16[32,128]{1,0:T(8,128)(2,1)S(1)} %shard_map.121), channel_id=1, source_target_pairs={{0,16},{2,18},{4,20},{6,22},{8,24},{10,26},{12,28},{14,30},{16,0},... | collective-permute-start | bytes 24584 | tf_op jit(solution)/shard_map/ppermute | solution.py:17
  22.6 9.8 %collective-permute-start.5 = (bf16[32,4096]{1,0:T(8,128)(2,1)S(1)}, bf16[32,4096]{1,0:T(8,128)(2,1)S(1)}, u32[]{:S(2)}, u32[]{:S(2)}) collective-permute-start(bf16[32,4096]{1,0:T(8,128)(2,1)S(1)} %collective-permute-done.refs_1_), channel_id=1, source_target_pairs={{0,8},{2,10},{4,12},{6,14},{8,0},{10,2},{12,4},{14,6},{16,24},{18,... | collective-permute-start | bytes 786440 | tf_op jit(solution)/shard_map/ppermute | solution.py:17
  22.6 11.0 %collective-permute-start.13 = (bf16[32,4096]{1,0:T(8,128)(2,1)S(1)}, bf16[32,4096]{1,0:T(8,128)(2,1)S(1)}, u32[]{:S(2)}, u32[]{:S(2)}) collective-permute-start(bf16[32,4096]{1,0:T(8,128)(2,1)S(1)} %collective-permute-done.refs_1_), channel_id=1, source_target_pairs={{0,4},{2,6},{4,0},{6,2},{8,12},{10,14},{12,8},{14,10},{16,20},{18,... | collective-permute-start | bytes 786440 | tf_op jit(solution)/shard_map/ppermute | solution.py:17
  24.3 0.9 copy-start.1
  25.2 0.9 copy-start.2
  26.2 6.3 %copy-start = (bf16[32,4096]{1,0:T(8,128)(2,1)S(1)}, bf16[32,4096]{1,0:T(8,128)(2,1)}, u32[]{:S(2)}) copy-start(bf16[32,4096]{1,0:T(8,128)(2,1)} %refs_0_.1) | copy-start | bytes 786436
  26.2 10.9 %copy-start.4 = (f32[1,12,2048]{2,0,1:T(1,128)S(1)}, f32[1,12,2048]{2,0,1:T(1,128)}, u32[]{:S(2)}) copy-start(f32[1,12,2048]{2,0,1:T(1,128)} %param.19) | copy-start | bytes 294916
  32.3 8.9 %copy-start.5 = (f32[1,12,2048]{2,0,1:T(1,128)S(1)}, f32[1,12,2048]{2,0,1:T(1,128)}, u32[]{:S(2)}) copy-start(f32[1,12,2048]{2,0,1:T(1,128)} %param.18) | copy-start | bytes 294916
  32.3 8.9 %slice-start.3 = ((s8[6291456]{0:T(1024)(128)(4,1)}), s8[4194304]{0:T(1024)(128)(4,1)S(1)}, s32[]{:S(2)}) async-start(s8[6291456]{0:T(1024)(128)(4,1)} %bitcast.10), calls=%async_computation.3 | async-start | bytes 8388608
  32.4 1.6 collective-permute-start.7
  33.0 4.1 %collective-permute-start.6 = (bf16[96,4096]{1,0:T(8,128)(2,1)S(1)}, bf16[96,4096]{1,0:T(8,128)(2,1)S(1)}, u32[]{:S(2)}, u32[]{:S(2)}) collective-permute-start(bf16[96,4096]{1,0:T(8,128)(2,1)S(1)} %shard_map.122.refs_0_), channel_id=1, source_target_pairs={{0,2},{2,0},{4,6},{6,4},{8,10},{10,8},{12,14},{14,12},{16,18},{18,... | collective-permute-start | bytes 2359304 | tf_op jit(solution)/shard_map/ppermute | solution.py:17
  34.6 9.2 %collective-permute-start.15 = (bf16[96,4096]{1,0:T(8,128)(2,1)S(1)}, bf16[96,4096]{1,0:T(8,128)(2,1)S(1)}, u32[]{:S(2)}, u32[]{:S(2)}) collective-permute-start(bf16[96,4096]{1,0:T(8,128)(2,1)S(1)} %shard_map.127.refs_0_.refs_4_), channel_id=1, source_target_pairs={{0,2},{2,0},{4,6},{6,4},{8,10},{10,8},{12,14},{14,12},{16,18},{18,... | collective-permute-start | bytes 2359304 | tf_op jit(solution)/shard_map/ppermute | solution.py:17
  34.8 9.0 %collective-permute-start.14 = (bf16[32,4096]{1,0:T(8,128)(2,1)S(1)}, bf16[32,4096]{1,0:T(8,128)(2,1)S(1)}, u32[]{:S(2)}, u32[]{:S(2)}) collective-permute-start(bf16[32,4096]{1,0:T(8,128)(2,1)S(1)} %collective-permute-done.5.refs_1_), channel_id=1, source_target_pairs={{0,4},{2,6},{4,0},{6,2},{8,12},{10,14},{12,8},{14,10},{16,20},{18,... | collective-permute-start | bytes 786440 | tf_op jit(solution)/shard_map/ppermute | solution.py:17
  35.1 8.7 %collective-permute-start.9 = (bf16[64,128]{1,0:T(8,128)(2,1)S(1)}, bf16[64,128]{1,0:T(8,128)(2,1)S(1)}, u32[]{:S(2)}, u32[]{:S(2)}) collective-permute-start(bf16[64,128]{1,0:T(8,128)(2,1)S(1)} %pad_maximum_fusion.2), channel_id=1, source_target_pairs={{0,8},{2,10},{4,12},{6,14},{8,0},{10,2},{12,4},{14,6},{16,24},{18,... | collective-permute-start | bytes 49160 | tf_op jit(solution)/shard_map/ppermute | solution.py:17
  37.1 4.2 %slice-start.4 = ((s8[6291456]{0:T(1024)(128)(4,1)}), s8[2097152]{0:T(1024)(128)(4,1)S(1)}, s32[]{:S(2)}) async-start(s8[6291456]{0:T(1024)(128)(4,1)} %bitcast.10), calls=%async_computation.4 | async-start | bytes 4194304
  43.8 1.7 collective-permute-start.16
  43.9 12.4 %collective-permute-start.8 = (bf16[256,768]{1,0:T(8,128)(2,1)S(1)}, bf16[256,768]{1,0:T(8,128)(2,1)S(1)}, u32[]{:S(2)}, u32[]{:S(2)}) collective-permute-start(bf16[256,768]{1,0:T(8,128)(2,1)S(1)} %get-tuple-element.57.refs_0_), channel_id=1, source_target_pairs={{0,1},{1,0},{2,3},{3,2},{4,5},{5,4},{6,7},{7,6},{8,9},{9,8},{10,11... | collective-permute-start | bytes 1179656 | tf_op jit(solution)/shard_map/ppermute | solution.py:17
  49.5 43.0 %copy-start.3 = (bf16[32,2048]{1,0:T(8,128)(2,1)S(1)}, bf16[32,2048]{1,0:T(8,128)(2,1)}, u32[]{:S(2)}) copy-start(bf16[32,2048]{1,0:T(8,128)(2,1)} %param.11) | copy-start | bytes 393220
  49.5 14.3 %collective-permute-start.17 = (bf16[256,768]{1,0:T(8,128)(2,1)S(1)}, bf16[256,768]{1,0:T(8,128)(2,1)S(1)}, u32[]{:S(2)}, u32[]{:S(2)}) collective-permute-start(bf16[256,768]{1,0:T(8,128)(2,1)S(1)} %get-tuple-element.63.refs_0_), channel_id=1, source_target_pairs={{0,1},{1,0},{2,3},{3,2},{4,5},{5,4},{6,7},{7,6},{8,9},{9,8},{10,11... | collective-permute-start | bytes 1179656 | tf_op jit(solution)/shard_map/ppermute | solution.py:17
  51.1 3.9 %collective-permute-start.10 = (bf16[128,128]{1,0:T(8,128)(2,1)S(1)}, bf16[128,128]{1,0:T(8,128)(2,1)S(1)}, u32[]{:S(2)}, u32[]{:S(2)}) collective-permute-start(bf16[128,128]{1,0:T(8,128)(2,1)S(1)} %pad_maximum_fusion.1), channel_id=1, source_target_pairs={{0,4},{2,6},{4,0},{6,2},{8,12},{10,14},{12,8},{14,10},{16,20},{18,... | collective-permute-start | bytes 98312 | tf_op jit(solution)/shard_map/ppermute | solution.py:17
  55.0 1.3 collective-permute-start.11
  66.2 2.0 %collective-permute-start.18 = (bf16[128,2048]{1,0:T(8,128)(2,1)S(1)}, bf16[128,2048]{1,0:T(8,128)(2,1)S(1)}, u32[]{:S(2)}, u32[]{:S(2)}) collective-permute-start(bf16[128,2048]{1,0:T(8,128)(2,1)S(1)} %get-tuple-element.66), channel_id=1, source_target_pairs={{0,2},{2,0},{4,6},{6,4},{8,10},{10,8},{12,14},{14,12},{16,18},{18,... | collective-permute-start | bytes 1572872 | tf_op jit(solution)/shard_map/ppermute | solution.py:17
  66.2 12.1 %collective-permute-start.12 = (bf16[128,2048]{1,0:T(8,128)(2,1)S(1)}, bf16[128,2048]{1,0:T(8,128)(2,1)S(1)}, u32[]{:S(2)}, u32[]{:S(2)}) collective-permute-start(bf16[128,2048]{1,0:T(8,128)(2,1)S(1)} %get-tuple-element.60), channel_id=1, source_target_pairs={{0,2},{2,0},{4,6},{6,4},{8,10},{10,8},{12,14},{14,12},{16,18},{18,... | collective-permute-start | bytes 1572872 | tf_op jit(solution)/shard_map/ppermute | solution.py:17
  68.2 6.4 %collective-permute-start.19 = (bf16[64,1024]{1,0:T(8,128)(2,1)S(1)}, bf16[64,1024]{1,0:T(8,128)(2,1)S(1)}, u32[]{:S(2)}, u32[]{:S(2)}) collective-permute-start(bf16[64,1024]{1,0:T(8,128)(2,1)S(1)} %get-tuple-element.119), channel_id=1, source_target_pairs={{0,4},{2,6},{4,0},{6,2},{8,12},{10,14},{12,8},{14,10},{16,20},{18,... | collective-permute-start | bytes 393224 | tf_op jit(solution)/shard_map/ppermute | solution.py:17
  70.0 6.6 %collective-permute-start.20 = (bf16[64,1024]{1,0:T(8,128)(2,1)S(1)}, bf16[64,1024]{1,0:T(8,128)(2,1)S(1)}, u32[]{:S(2)}, u32[]{:S(2)}) collective-permute-start(bf16[64,1024]{1,0:T(8,128)(2,1)S(1)} %get-tuple-element.118), channel_id=1, source_target_pairs={{0,4},{2,6},{4,0},{6,2},{8,12},{10,14},{12,8},{14,10},{16,20},{18,... | collective-permute-start | bytes 393224 | tf_op jit(solution)/shard_map/ppermute | solution.py:17
  76.6 9.2 %collective-permute-start.21 = (bf16[64,2048]{1,0:T(8,128)(2,1)S(1)}, bf16[64,2048]{1,0:T(8,128)(2,1)S(1)}, u32[]{:S(2)}, u32[]{:S(2)}) collective-permute-start(bf16[64,2048]{1,0:T(8,128)(2,1)S(1)} %add_convert_fusion.7), channel_id=1, source_target_pairs={{0,4},{2,6},{4,0},{6,2},{8,12},{10,14},{12,8},{14,10},{16,20},{18,... | collective-permute-start | bytes 786440 | tf_op jit(solution)/shard_map/ppermute | solution.py:17
  78.5 5.9 %collective-permute-start.22 = (bf16[64,1024]{1,0:T(8,128)(2,1)S(1)}, bf16[64,1024]{1,0:T(8,128)(2,1)S(1)}, u32[]{:S(2)}, u32[]{:S(2)}) collective-permute-start(bf16[64,1024]{1,0:T(8,128)(2,1)S(1)} %get-tuple-element.117), channel_id=1, source_target_pairs={{0,8},{2,10},{4,12},{6,14},{8,0},{10,2},{12,4},{14,6},{16,24},{18,... | collective-permute-start | bytes 393224 | tf_op jit(solution)/shard_map/ppermute | solution.py:17
  78.6 7.2 %collective-permute-start.24 = (bf16[64,1024]{1,0:T(8,128)(2,1)S(1)}, bf16[64,1024]{1,0:T(8,128)(2,1)S(1)}, u32[]{:S(2)}, u32[]{:S(2)}) collective-permute-start(bf16[64,1024]{1,0:T(8,128)(2,1)S(1)} %get-tuple-element.116), channel_id=1, source_target_pairs={{0,8},{2,10},{4,12},{6,14},{8,0},{10,2},{12,4},{14,6},{16,24},{18,... | collective-permute-start | bytes 393224 | tf_op jit(solution)/shard_map/ppermute | solution.py:17
  85.9 6.0 %collective-permute-start.23 = (bf16[32,1024]{1,0:T(8,128)(2,1)S(1)}, bf16[32,1024]{1,0:T(8,128)(2,1)S(1)}, u32[]{:S(2)}, u32[]{:S(2)}) collective-permute-start(bf16[32,1024]{1,0:T(8,128)(2,1)S(1)} %get-tuple-element.109), channel_id=1, source_target_pairs={{0,16},{2,18},{4,20},{6,22},{8,24},{10,26},{12,28},{14,30},{16,0},... | collective-permute-start | bytes 196616 | tf_op jit(solution)/shard_map/ppermute | solution.py:17
  87.3 5.2 %collective-permute-start.25 = (bf16[32,1024]{1,0:T(8,128)(2,1)S(1)}, bf16[32,1024]{1,0:T(8,128)(2,1)S(1)}, u32[]{:S(2)}, u32[]{:S(2)}) collective-permute-start(bf16[32,1024]{1,0:T(8,128)(2,1)S(1)} %get-tuple-element.108), channel_id=1, source_target_pairs={{0,16},{2,18},{4,20},{6,22},{8,24},{10,26},{12,28},{14,30},{16,0},... | collective-permute-start | bytes 196616 | tf_op jit(solution)/shard_map/ppermute | solution.py:17
  92.7 5.5 %collective-permute-start.26 = (bf16[32,1024]{1,0:T(8,128)(2,1)S(1)}, bf16[32,1024]{1,0:T(8,128)(2,1)S(1)}, u32[]{:S(2)}, u32[]{:S(2)}) collective-permute-start(bf16[32,1024]{1,0:T(8,128)(2,1)S(1)} %get-tuple-element.107.refs_0_), channel_id=1, source_target_pairs={{0,16},{2,18},{4,20},{6,22},{8,24},{10,26},{12,28},{14,30},{16,0},... | collective-permute-start | bytes 196616 | tf_op jit(solution)/shard_map/ppermute | solution.py:17
  94.3 5.4 %collective-permute-start.27 = (bf16[32,1024]{1,0:T(8,128)(2,1)S(1)}, bf16[32,1024]{1,0:T(8,128)(2,1)S(1)}, u32[]{:S(2)}, u32[]{:S(2)}) collective-permute-start(bf16[32,1024]{1,0:T(8,128)(2,1)S(1)} %get-tuple-element.106.refs_1_), channel_id=1, source_target_pairs={{0,16},{2,18},{4,20},{6,22},{8,24},{10,26},{12,28},{14,30},{16,0},... | collective-permute-start | bytes 196616 | tf_op jit(solution)/shard_map/ppermute | solution.py:17
  100.3 7.6 %collective-permute-start.28 = (bf16[64,2048]{1,0:T(8,128)(2,1)S(1)}, bf16[64,2048]{1,0:T(8,128)(2,1)S(1)}, u32[]{:S(2)}, u32[]{:S(2)}) collective-permute-start(bf16[64,2048]{1,0:T(8,128)(2,1)S(1)} %shard_map.130.refs_0_), channel_id=1, source_target_pairs={{0,8},{2,10},{4,12},{6,14},{8,0},{10,2},{12,4},{14,6},{16,24},{18,... | collective-permute-start | bytes 786440 | tf_op jit(solution)/shard_map/ppermute | solution.py:17
  103.6 6.4 %collective-permute-start.29 = (bf16[64,2048]{1,0:T(8,128)(2,1)S(1)}, bf16[64,2048]{1,0:T(8,128)(2,1)S(1)}, u32[]{:S(2)}, u32[]{:S(2)}) collective-permute-start(bf16[64,2048]{1,0:T(8,128)(2,1)S(1)} %shard_map.130.refs_0_), channel_id=1, source_target_pairs={{0,4},{2,6},{4,0},{6,2},{8,12},{10,14},{12,8},{14,10},{16,20},{18,... | collective-permute-start | bytes 786440 | tf_op jit(solution)/shard_map/ppermute | solution.py:17
  103.6 6.4 %collective-permute-start.30 = (bf16[64,2048]{1,0:T(8,128)(2,1)S(1)}, bf16[64,2048]{1,0:T(8,128)(2,1)S(1)}, u32[]{:S(2)}, u32[]{:S(2)}) collective-permute-start(bf16[64,2048]{1,0:T(8,128)(2,1)S(1)} %shard_map.130.refs_0_), channel_id=1, source_target_pairs={{0,2},{2,0},{4,6},{6,4},{8,10},{10,8},{12,14},{14,12},{16,18},{18,... | collective-permute-start | bytes 786440 | tf_op jit(solution)/shard_map/ppermute | solution.py:17
  110.0 1.5 collective-permute-start.31
  110.0 8.7 %collective-permute-start.33 = (bf16[64,2048]{1,0:T(8,128)(2,1)S(1)}, bf16[64,2048]{1,0:T(8,128)(2,1)S(1)}, u32[]{:S(2)}, u32[]{:S(2)}) collective-permute-start(bf16[64,2048]{1,0:T(8,128)(2,1)S(1)} %collective-permute-done.28.refs_1_), channel_id=1, source_target_pairs={{0,4},{2,6},{4,0},{6,2},{8,12},{10,14},{12,8},{14,10},{16,20},{18,... | collective-permute-start | bytes 786440 | tf_op jit(solution)/shard_map/ppermute | solution.py:17
  110.0 8.7 %collective-permute-start.34 = (bf16[64,2048]{1,0:T(8,128)(2,1)S(1)}, bf16[64,2048]{1,0:T(8,128)(2,1)S(1)}, u32[]{:S(2)}, u32[]{:S(2)}) collective-permute-start(bf16[64,2048]{1,0:T(8,128)(2,1)S(1)} %collective-permute-done.29.refs_0_), channel_id=1, source_target_pairs={{0,2},{2,0},{4,6},{6,4},{8,10},{10,8},{12,14},{14,12},{16,18},{18,... | collective-permute-start | bytes 786440 | tf_op jit(solution)/shard_map/ppermute | solution.py:17
  113.9 11.2 %collective-permute-start.32 = (bf16[256,768]{1,0:T(8,128)(2,1)S(1)}, bf16[256,768]{1,0:T(8,128)(2,1)S(1)}, u32[]{:S(2)}, u32[]{:S(2)}) collective-permute-start(bf16[256,768]{1,0:T(8,128)(2,1)S(1)} %get-tuple-element.70), channel_id=1, source_target_pairs={{0,1},{1,0},{2,3},{3,2},{4,5},{5,4},{6,7},{7,6},{8,9},{9,8},{10,11... | collective-permute-start | bytes 1179656 | tf_op jit(solution)/shard_map/ppermute | solution.py:17
  118.7 4.1 %collective-permute-start.35 = (bf16[64,2048]{1,0:T(8,128)(2,1)S(1)}, bf16[64,2048]{1,0:T(8,128)(2,1)S(1)}, u32[]{:S(2)}, u32[]{:S(2)}) collective-permute-start(bf16[64,2048]{1,0:T(8,128)(2,1)S(1)} %collective-permute-done.33.refs_1_), channel_id=1, source_target_pairs={{0,2},{2,0},{4,6},{6,4},{8,10},{10,8},{12,14},{14,12},{16,18},{18,... | collective-permute-start | bytes 786440 | tf_op jit(solution)/shard_map/ppermute | solution.py:17
  127.6 10.4 %collective-permute-start.36 = (bf16[256,768]{1,0:T(8,128)(2,1)S(1)}, bf16[256,768]{1,0:T(8,128)(2,1)S(1)}, u32[]{:S(2)}, u32[]{:S(2)}) collective-permute-start(bf16[256,768]{1,0:T(8,128)(2,1)S(1)} %get-tuple-element.78), channel_id=1, source_target_pairs={{0,1},{1,0},{2,3},{3,2},{4,5},{5,4},{6,7},{7,6},{8,9},{9,8},{10,11... | collective-permute-start | bytes 1179656 | tf_op jit(solution)/shard_map/ppermute | solution.py:17
  133.1 23.5 %slice-start = ((s8[12582912]{0:T(1024)(128)(4,1)}), s8[4194304]{0:T(1024)(128)(4,1)S(1)}, s32[]{:S(2)}) async-start(s8[12582912]{0:T(1024)(128)(4,1)} %bitcast.8), calls=%async_computation | async-start | bytes 8388608
  133.2 23.5 %slice-start.1 = ((s8[12582912]{0:T(1024)(128)(4,1)}), s8[4194304]{0:T(1024)(128)(4,1)S(1)}, s32[]{:S(2)}) async-start(s8[12582912]{0:T(1024)(128)(4,1)} %bitcast.8), calls=%async_computation.1 | async-start | bytes 8388608
  138.0 18.7 %slice-start.2 = ((s8[12582912]{0:T(1024)(128)(4,1)}), s8[4194304]{0:T(1024)(128)(4,1)S(1)}, s32[]{:S(2)}) async-start(s8[12582912]{0:T(1024)(128)(4,1)} %bitcast.8), calls=%async_computation.2 | async-start | bytes 8388608
  142.0 2.0 %collective-permute-start.39 = (bf16[128,2048]{1,0:T(8,128)(2,1)S(1)}, bf16[128,2048]{1,0:T(8,128)(2,1)S(1)}, u32[]{:S(2)}, u32[]{:S(2)}) collective-permute-start(bf16[128,2048]{1,0:T(8,128)(2,1)S(1)} %get-tuple-element.93), channel_id=1, source_target_pairs={{0,2},{2,0},{4,6},{6,4},{8,10},{10,8},{12,14},{14,12},{16,18},{18,... | collective-permute-start | bytes 1572872 | tf_op jit(solution)/shard_map/ppermute | solution.py:17
  142.1 5.2 %collective-permute-start.38 = (bf16[128,2048]{1,0:T(8,128)(2,1)S(1)}, bf16[128,2048]{1,0:T(8,128)(2,1)S(1)}, u32[]{:S(2)}, u32[]{:S(2)}) collective-permute-start(bf16[128,2048]{1,0:T(8,128)(2,1)S(1)} %get-tuple-element.91), channel_id=1, source_target_pairs={{0,2},{2,0},{4,6},{6,4},{8,10},{10,8},{12,14},{14,12},{16,18},{18,... | collective-permute-start | bytes 1572872 | tf_op jit(solution)/shard_map/ppermute | solution.py:17
  144.1 8.4 %collective-permute-start.40 = (bf16[64,2048]{1,0:T(8,128)(2,1)S(1)}, bf16[64,2048]{1,0:T(8,128)(2,1)S(1)}, u32[]{:S(2)}, u32[]{:S(2)}) collective-permute-start(bf16[64,2048]{1,0:T(8,128)(2,1)S(1)} %get-tuple-element.112), channel_id=1, source_target_pairs={{0,4},{2,6},{4,0},{6,2},{8,12},{10,14},{12,8},{14,10},{16,20},{18,... | collective-permute-start | bytes 786440 | tf_op jit(solution)/shard_map/ppermute | solution.py:17
  145.2 10.2 %collective-permute-start.44 = (bf16[128,2048]{1,0:T(8,128)(2,1)S(1)}, bf16[128,2048]{1,0:T(8,128)(2,1)S(1)}, u32[]{:S(2)}, u32[]{:S(2)}) collective-permute-start(bf16[128,2048]{1,0:T(8,128)(2,1)S(1)} %get-tuple-element.97), channel_id=1, source_target_pairs={{0,2},{2,0},{4,6},{6,4},{8,10},{10,8},{12,14},{14,12},{16,18},{18,... | collective-permute-start | bytes 1572872 | tf_op jit(solution)/shard_map/ppermute | solution.py:17
  145.2 17.9 %collective-permute-start.37 = (bf16[128,2048]{1,0:T(8,128)(2,1)S(1)}, bf16[128,2048]{1,0:T(8,128)(2,1)S(1)}, u32[]{:S(2)}, u32[]{:S(2)}) collective-permute-start(bf16[128,2048]{1,0:T(8,128)(2,1)S(1)} %get-tuple-element.87), channel_id=1, source_target_pairs={{0,2},{2,0},{4,6},{6,4},{8,10},{10,8},{12,14},{14,12},{16,18},{18,... | collective-permute-start | bytes 1572872 | tf_op jit(solution)/shard_map/ppermute | solution.py:17
  145.7 8.2 %collective-permute-start.41 = (bf16[64,2048]{1,0:T(8,128)(2,1)S(1)}, bf16[64,2048]{1,0:T(8,128)(2,1)S(1)}, u32[]{:S(2)}, u32[]{:S(2)}) collective-permute-start(bf16[64,2048]{1,0:T(8,128)(2,1)S(1)} %get-tuple-element.113), channel_id=1, source_target_pairs={{0,1},{1,0},{2,3},{3,2},{4,5},{5,4},{6,7},{7,6},{8,9},{9,8},{10,11... | collective-permute-start | bytes 786440 | tf_op jit(solution)/shard_map/ppermute | solution.py:17
  153.9 9.2 %collective-permute-start.42 = (bf16[64,2048]{1,0:T(8,128)(2,1)S(1)}, bf16[64,2048]{1,0:T(8,128)(2,1)S(1)}, u32[]{:S(2)}, u32[]{:S(2)}) collective-permute-start(bf16[64,2048]{1,0:T(8,128)(2,1)S(1)} %get-tuple-element.94), channel_id=1, source_target_pairs={{0,1},{1,0},{2,3},{3,2},{4,5},{5,4},{6,7},{7,6},{8,9},{9,8},{10,11... | collective-permute-start | bytes 786440 | tf_op jit(solution)/shard_map/ppermute | solution.py:17
  155.6 7.5 %collective-permute-start.45 = (bf16[64,2048]{1,0:T(8,128)(2,1)S(1)}, bf16[64,2048]{1,0:T(8,128)(2,1)S(1)}, u32[]{:S(2)}, u32[]{:S(2)}) collective-permute-start(bf16[64,2048]{1,0:T(8,128)(2,1)S(1)} %get-tuple-element.114), channel_id=1, source_target_pairs={{0,4},{2,6},{4,0},{6,2},{8,12},{10,14},{12,8},{14,10},{16,20},{18,... | collective-permute-start | bytes 786440 | tf_op jit(solution)/shard_map/ppermute | solution.py:17
  163.3 6.9 %collective-permute-start.47 = (bf16[64,2048]{1,0:T(8,128)(2,1)S(1)}, bf16[64,2048]{1,0:T(8,128)(2,1)S(1)}, u32[]{:S(2)}, u32[]{:S(2)}) collective-permute-start(bf16[64,2048]{1,0:T(8,128)(2,1)S(1)} %add_convert_fusion), channel_id=1, source_target_pairs={{0,8},{2,10},{4,12},{6,14},{8,0},{10,2},{12,4},{14,6},{16,24},{18,... | collective-permute-start | bytes 786440 | tf_op jit(solution)/shard_map/ppermute | solution.py:17
  163.4 6.8 %collective-permute-start.43 = (bf16[64,2048]{1,0:T(8,128)(2,1)S(1)}, bf16[64,2048]{1,0:T(8,128)(2,1)S(1)}, u32[]{:S(2)}, u32[]{:S(2)}) collective-permute-start(bf16[64,2048]{1,0:T(8,128)(2,1)S(1)} %get-tuple-element.95), channel_id=1, source_target_pairs={{0,1},{1,0},{2,3},{3,2},{4,5},{5,4},{6,7},{7,6},{8,9},{9,8},{10,11... | collective-permute-start | bytes 786440 | tf_op jit(solution)/shard_map/ppermute | solution.py:17
  163.9 6.5 %collective-permute-start.46 = (bf16[64,2048]{1,0:T(8,128)(2,1)S(1)}, bf16[64,2048]{1,0:T(8,128)(2,1)S(1)}, u32[]{:S(2)}, u32[]{:S(2)}) collective-permute-start(bf16[64,2048]{1,0:T(8,128)(2,1)S(1)} %get-tuple-element.98), channel_id=1, source_target_pairs={{0,4},{2,6},{4,0},{6,2},{8,12},{10,14},{12,8},{14,10},{16,20},{18,... | collective-permute-start | bytes 786440 | tf_op jit(solution)/shard_map/ppermute | solution.py:17
  170.5 7.3 %collective-permute-start.48 = (bf16[32,2048]{1,0:T(8,128)(2,1)S(1)}, bf16[32,2048]{1,0:T(8,128)(2,1)S(1)}, u32[]{:S(2)}, u32[]{:S(2)}) collective-permute-start(bf16[32,2048]{1,0:T(8,128)(2,1)S(1)} %add_convert_fusion.9), channel_id=1, source_target_pairs={{0,16},{2,18},{4,20},{6,22},{8,24},{10,26},{12,28},{14,30},{16,0},... | collective-permute-start | bytes 393224 | tf_op jit(solution)/shard_map/ppermute | solution.py:17

commit v9 on v8

--- a/solution.py
+++ b/solution.py
@@ -571,14 +571,14 @@
     across_own = swap(tokens, "expert", 2)
     extra = -(-3 * experts // 128) * 128
     terms = prepare(place, routes, route_scores, extra)
-    near_own = tie(near_own, terms)
+    w_in = dequant_wide(place, in_codes[0], tie(in_low, terms)[0], in_high[0], 30)
+    near_own = tie(near_own, w_in)
     across_near = swap(near_own, "expert", 2)
-    terms = join(gather_far(terms))
-    far = tie(far, across_own, across_near, terms)
+    far = tie(far, w_in, across_own)
     near_far = swap(far, "expert", 4)
     across_far = swap(far, "expert", 2)
-    w_in = dequant_wide(place, in_codes[0], tie(in_low, far)[0], in_high[0], 30)
-    near_far = tie(near_far, w_in)
+    terms = join(gather_far(terms))
+    near_far = tie(near_far, across_near, terms)
     first = pack(place, [[tokens], [far], [near_own]])
     first_other = swap(first, "expert", 1)
     across_last = swap(near_far, "expert", 2)
@@ -591,10 +591,10 @@
         if c == 1:
             second = pack(place, [[across_own], [tie(across_far, near_other)], [across_near]])
             second_other = swap(second, "expert", 1)
-            across_last = tie(across_last, w_down, near_terms, second_other)
+            across_last = tie(across_last, hidden[0][0], near_terms, second_other)
             x.append([second, across_last, second_other, swap(across_last, "expert", 1)])
         own, chunk_slope, chunk_act = forward_in(place, x[c], w_in)
-        if c == 0:
+        if c == 1:
             w_down = dequant(place, down_codes, tie(down_low, own), down_high, halves)
         hidden.append([own] + [swap(own, "half", d) for d in parts if d])
         slope.append(chunk_slope)

time: 179 us -> 177 us (0.989)
  waiting for transfers between devices: 63.4 us -> 57.4 us
  starting transfers between devices: 48.6 us -> 53.3 us
    ppermute x49, waiting for transfers between devices: 63.4 us -> 57.4 us  [swap(): return lax.ppermute(array, axis, [(i, i ^ distance) for i in range(size)])]
    ppermute x49, starting transfers between devices: 48.6 us -> 53.3 us  [swap(): return lax.ppermute(array, axis, [(i, i ^ distance) for i in range(size)])]
  transfers between devices with their start and end apart: 49 -> 49, of which waited for: 29 -> 28; matrix products, arithmetic and copies ran while one was open for 2% -> 2% of each run, Pallas kernels for 28% -> 28%
where the time goes in v9:
time: 177 us
  Pallas kernels  58.9 us (33%)
  waiting for transfers between devices  57.4 us (32%)
  starting transfers between devices  53.3 us (30%)
  local copies, waits for them, and re-layouts  4.32 us (2%)
  other arithmetic  1.98 us (1%)
    pallas_call x19, Pallas kernels, call(): pl.pallas_call(kernel, grid_spec=pltpu.PrefetchScalarGridSpec(num_scalar_...  58.9 us
    ppermute x49, waiting for transfers between devices, swap(): return lax.ppermute(array, axis, [(i, i ^ distance) for i in range(size)])  57.4 us
    ppermute x49, starting transfers between devices, swap(): return lax.ppermute(array, axis, [(i, i ^ distance) for i in range(size)])  53.3 us
    unnamed x26, local copies, waits for them, and re-layouts  4.28 us
  transfers between devices with their start and end apart: 49, of which 28 were waited for; matrix products, arithmetic and copies ran while one was open for 2% of the time, Pallas kernels for 28%

profile of v9, /device:TPU:0, one launch (start us, length us, event | category | flops | bytes accessed | tf_op | source)
XLA Modules:
  0.0 177.0 jit_solution(5466959225999906398)
XLA Ops:
  0.6 3.0 %collective-permute-start.1 = (bf16[32,4096]{1,0:T(8,128)(2,1)}, bf16[32,4096]{1,0:T(8,128)(2,1)S(1)}, u32[]{:S(2)}, u32[]{:S(2)}) collective-permute-start(bf16[32,4096]{1,0:T(8,128)(2,1)} %refs_0_.1), channel_id=1, source_target_pairs={{0,4},{2,6},{4,0},{6,2},{8,12},{10,14},{12,8},{14,10},{16,20},{18,... | collective-permute-start | bytes 786440 | tf_op jit(solution)/shard_map/ppermute | solution.py:17
  3.6 2.6 %collective-permute-start = (bf16[32,4096]{1,0:T(8,128)(2,1)}, bf16[32,4096]{1,0:T(8,128)(2,1)S(1)}, u32[]{:S(2)}, u32[]{:S(2)}) collective-permute-start(bf16[32,4096]{1,0:T(8,128)(2,1)} %refs_0_.1), channel_id=1, source_target_pairs={{0,16},{2,18},{4,20},{6,22},{8,24},{10,26},{12,28},{14,30},{16,0},... | collective-permute-start | bytes 786440 | tf_op jit(solution)/shard_map/ppermute | solution.py:17
  6.2 1.6 collective-permute-start.2
  10.2 0.9 copy-done.1
  11.1 0.9 copy-done.2
  12.0 6.2 %shard_map.122.refs_4_.refs_3_ = bf16[4096,1536]{1,0:T(8,128)(2,1)S(1)} custom-call(s32[2]{0:T(128)S(1)} %pad_add_fusion.place_ref, bf16[2,4096,768]{2,1,0:T(8,128)(2,1)} %bitcast.7, f32[2,32,768]{2,1,0:T(8,128)S(1)} %bitcast.13, f32[2,32,768]{2,1,0:T(8,128)S(1)} %bitcast.14), custom_call_target="tpu_custom_call" | custom-call | bytes 25 | tf_op jit(solution)/shard_map/pallas_call | solution.py:112
  19.4 3.3 %collective-permute-start.5 = (bf16[32,128]{1,0:T(8,128)(2,1)S(1)}, bf16[32,128]{1,0:T(8,128)(2,1)S(1)}, u32[]{:S(2)}, u32[]{:S(2)}) collective-permute-start(bf16[32,128]{1,0:T(8,128)(2,1)S(1)} %shard_map.121), channel_id=1, source_target_pairs={{0,16},{2,18},{4,20},{6,22},{8,24},{10,26},{12,28},{14,30},{16,0},... | collective-permute-start | bytes 24584 | tf_op jit(solution)/shard_map/ppermute | solution.py:17
  22.7 2.1 %collective-permute-done.5 = bf16[32,128]{1,0:T(8,128)(2,1)S(1)} collective-permute-done((bf16[32,128]{1,0:T(8,128)(2,1)S(1)}, bf16[32,128]{1,0:T(8,128)(2,1)S(1)}, u32[]{:S(2)}, u32[]{:S(2)}) %collective-permute-start.5) | collective-permute-done | bytes 8224 | tf_op jit(solution)/shard_map/ppermute | solution.py:17
  24.8 1.1 collective-permute-start.9
  25.9 1.1 collective-permute-done.4.refs_2_
  28.2 4.2 %collective-permute-done.9.refs_1_ = bf16[32,4096]{1,0:T(8,128)(2,1)S(1)} collective-permute-done((bf16[32,4096]{1,0:T(8,128)(2,1)S(1)}, bf16[32,4096]{1,0:T(8,128)(2,1)S(1)}, u32[]{:S(2)}, u32[]{:S(2)}) %collective-permute-start.9) | collective-permute-done | bytes 262176 | tf_op jit(solution)/shard_map/ppermute | solution.py:17
  33.8 3.8 %collective-permute-start.11 = (bf16[64,128]{1,0:T(8,128)(2,1)S(1)}, bf16[64,128]{1,0:T(8,128)(2,1)S(1)}, u32[]{:S(2)}, u32[]{:S(2)}) collective-permute-start(bf16[64,128]{1,0:T(8,128)(2,1)S(1)} %pad_maximum_fusion.2), channel_id=1, source_target_pairs={{0,8},{2,10},{4,12},{6,14},{8,0},{10,2},{12,4},{14,6},{16,24},{18,... | collective-permute-start | bytes 49160 | tf_op jit(solution)/shard_map/ppermute | solution.py:17
  37.6 4.1 %shard_map.124 = (bf16[256,768]{1,0:T(8,128)(2,1)S(1)}, f32[256,768]{1,0:T(8,128)S(1)}, f32[256,768]{1,0:T(8,128)S(1)}) custom-call(s32[2]{0:T(128)S(1)} %pad_add_fusion.place_ref, bf16[96,4096]{1,0:T(8,128)(2,1)S(1)} %shard_map.123.refs_0_, bf16[32,4096]{1,0:T(8,128)(2,1)S(1)} %collective-permute-done.3.refs_1_, ...), custom_call_target="tpu_custom_call" | custom-call | flops 3221 | bytes 16 | tf_op jit(solution)/shard_map/pallas_call | solution.py:112
  41.9 1.6 collective-permute-start.8
  43.5 4.1 %shard_map.126 = (bf16[256,768]{1,0:T(8,128)(2,1)S(1)}, f32[256,768]{1,0:T(8,128)S(1)}, f32[256,768]{1,0:T(8,128)S(1)}) custom-call(s32[2]{0:T(128)S(1)} %pad_add_fusion.place_ref, bf16[96,4096]{1,0:T(8,128)(2,1)S(1)} %shard_map.125.refs_0_.refs_4_, bf16[32,4096]{1,0:T(8,128)(2,1)S(1)} %collective-permute-done.10.refs_1_.refs_5_, ...), custom_call_target="tpu_custom_call" | custom-call | flops 3221 | bytes 16 | tf_op jit(solution)/shard_map/pallas_call | solution.py:112
  47.6 1.5 collective-permute-start.17
  49.1 1.3 collective-permute-start.14
  50.5 2.6 %collective-permute-done.14 = bf16[128,128]{1,0:T(8,128)(2,1)S(1)} collective-permute-done((bf16[128,128]{1,0:T(8,128)(2,1)S(1)}, bf16[128,128]{1,0:T(8,128)(2,1)S(1)}, u32[]{:S(2)}, u32[]{:S(2)}) %collective-permute-start.14) | collective-permute-done | bytes 32800 | tf_op jit(solution)/shard_map/ppermute | solution.py:17
  53.2 2.4 %shard_map.127.refs_2_.refs_6_ = bf16[1536,2048]{1,0:T(8,128)(2,1)S(1)} custom-call(s32[2]{0:T(128)S(1)} %pad_add_fusion.place_ref, bf16[1,1536,2048]{2,1,0:T(8,128)(2,1)S(1)} %bitcast.11, f32[1,12,2048]{2,1,0:T(8,128)S(1)} %copy.17.low_ref, f32[1,12,2048]{2,1,0:T(8,128)S(1)} %copy.18.high_ref), custom_call_target="tpu_custom_call" | custom-call | bytes 12 | tf_op jit(solution)/shard_map/pallas_call | solution.py:112
  55.7 2.3 %shard_map.128 = (bf16[128,2048]{1,0:T(8,128)(2,1)S(1)}, bf16[128,2048]{1,0:T(8,128)(2,1)S(1)}) custom-call(s32[2]{0:T(128)S(1)} %pad_add_fusion.place_ref, bf16[256,768]{1,0:T(8,128)(2,1)S(1)} %get-tuple-element.57.refs_0_, bf16[256,768]{1,0:T(8,128)(2,1)S(1)} %collective-permute-done.8.refs_1_, bf16[1536,2048]{1,0:T(8,128)(2,1)S(1)} %shard_map.127.refs_2_.refs_6_, ...), custom_call_target="tpu_custom_call" | custom-call | flops 1610 | bytes 8 | tf_op jit(solution)/shard_map/pallas_call | solution.py:112
  58.0 3.9 %collective-permute-done.17.refs_1_ = bf16[256,768]{1,0:T(8,128)(2,1)S(1)} collective-permute-done((bf16[256,768]{1,0:T(8,128)(2,1)S(1)}, bf16[256,768]{1,0:T(8,128)(2,1)S(1)}, u32[]{:S(2)}, u32[]{:S(2)}) %collective-permute-start.17) | collective-permute-done | bytes 393248 | tf_op jit(solution)/shard_map/ppermute | solution.py:17
  61.9 2.3 %shard_map.129 = (bf16[128,2048]{1,0:T(8,128)(2,1)S(1)}, bf16[128,2048]{1,0:T(8,128)(2,1)S(1)}) custom-call(s32[2]{0:T(128)S(1)} %pad_add_fusion.place_ref, bf16[256,768]{1,0:T(8,128)(2,1)S(1)} %get-tuple-element.60.refs_0_, bf16[256,768]{1,0:T(8,128)(2,1)S(1)} %collective-permute-done.17.refs_1_, bf16[1536,2048]{1,0:T(8,128)(2,1)S(1)} %shard_map.127.refs_2_.refs_6_, ...), custom_call_target="tpu_custom_call" | custom-call | flops 1610 | bytes 8 | tf_op jit(solution)/shard_map/pallas_call | solution.py:112
  64.8 1.4 collective-permute-done.18
  66.3 1.4 collective-permute-start.19
  68.4 4.2 %collective-permute-done.19 = bf16[64,1024]{1,0:T(8,128)(2,1)S(1)} collective-permute-done((bf16[64,1024]{1,0:T(8,128)(2,1)S(1)}, bf16[64,1024]{1,0:T(8,128)(2,1)S(1)}, u32[]{:S(2)}, u32[]{:S(2)}) %collective-permute-start.19) | collective-permute-done | bytes 131104 | tf_op jit(solution)/shard_map/ppermute | solution.py:17
  72.7 2.0 %collective-permute-done.20 = bf16[64,1024]{1,0:T(8,128)(2,1)S(1)} collective-permute-done((bf16[64,1024]{1,0:T(8,128)(2,1)S(1)}, bf16[64,1024]{1,0:T(8,128)(2,1)S(1)}, u32[]{:S(2)}, u32[]{:S(2)}) %collective-permute-start.20) | collective-permute-done | bytes 131104 | tf_op jit(solution)/shard_map/ppermute | solution.py:17
  74.7 1.3 collective-permute-start.21
  76.1 3.0 %collective-permute-start.22 = (bf16[64,1024]{1,0:T(8,128)(2,1)S(1)}, bf16[64,1024]{1,0:T(8,128)(2,1)S(1)}, u32[]{:S(2)}, u32[]{:S(2)}) collective-permute-start(bf16[64,1024]{1,0:T(8,128)(2,1)S(1)} %get-tuple-element.117), channel_id=1, source_target_pairs={{0,8},{2,10},{4,12},{6,14},{8,0},{10,2},{12,4},{14,6},{16,24},{18,... | collective-permute-start | bytes 393224 | tf_op jit(solution)/shard_map/ppermute | solution.py:17
  79.3 4.1 %collective-permute-done.22 = bf16[64,1024]{1,0:T(8,128)(2,1)S(1)} collective-permute-done((bf16[64,1024]{1,0:T(8,128)(2,1)S(1)}, bf16[64,1024]{1,0:T(8,128)(2,1)S(1)}, u32[]{:S(2)}, u32[]{:S(2)}) %collective-permute-start.22) | collective-permute-done | bytes 131104 | tf_op jit(solution)/shard_map/ppermute | solution.py:17
  83.3 1.4 collective-permute-done.24
  84.8 1.2 collective-permute-start.23
  86.1 1.7 collective-permute-start.25
  87.8 2.6 %collective-permute-done.23 = bf16[32,1024]{1,0:T(8,128)(2,1)S(1)} collective-permute-done((bf16[32,1024]{1,0:T(8,128)(2,1)S(1)}, bf16[32,1024]{1,0:T(8,128)(2,1)S(1)}, u32[]{:S(2)}, u32[]{:S(2)}) %collective-permute-start.23) | collective-permute-done | bytes 65568 | tf_op jit(solution)/shard_map/ppermute | solution.py:17
  90.4 2.2 %collective-permute-done.25 = bf16[32,1024]{1,0:T(8,128)(2,1)S(1)} collective-permute-done((bf16[32,1024]{1,0:T(8,128)(2,1)S(1)}, bf16[32,1024]{1,0:T(8,128)(2,1)S(1)}, u32[]{:S(2)}, u32[]{:S(2)}) %collective-permute-start.25) | collective-permute-done | bytes 65568 | tf_op jit(solution)/shard_map/ppermute | solution.py:17
  93.2 2.5 %collective-permute-start.27 = (bf16[32,1024]{1,0:T(8,128)(2,1)S(1)}, bf16[32,1024]{1,0:T(8,128)(2,1)S(1)}, u32[]{:S(2)}, u32[]{:S(2)}) collective-permute-start(bf16[32,1024]{1,0:T(8,128)(2,1)S(1)} %get-tuple-element.106.refs_1_), channel_id=1, source_target_pairs={{0,16},{2,18},{4,20},{6,22},{8,24},{10,26},{12,28},{14,30},{16,0},... | collective-permute-start | bytes 196616 | tf_op jit(solution)/shard_map/ppermute | solution.py:17
  95.7 2.8 %collective-permute-done.26.refs_2_ = bf16[32,1024]{1,0:T(8,128)(2,1)S(1)} collective-permute-done((bf16[32,1024]{1,0:T(8,128)(2,1)S(1)}, bf16[32,1024]{1,0:T(8,128)(2,1)S(1)}, u32[]{:S(2)}, u32[]{:S(2)}) %collective-permute-start.26) | collective-permute-done | bytes 65568 | tf_op jit(solution)/shard_map/ppermute | solution.py:17
  99.7 1.4 collective-permute-start.28
  101.1 1.5 collective-permute-start.29
  102.6 3.6 %collective-permute-done.28.refs_1_ = bf16[64,2048]{1,0:T(8,128)(2,1)S(1)} collective-permute-done((bf16[64,2048]{1,0:T(8,128)(2,1)S(1)}, bf16[64,2048]{1,0:T(8,128)(2,1)S(1)}, u32[]{:S(2)}, u32[]{:S(2)}) %collective-permute-start.28) | collective-permute-done | bytes 262176 | tf_op jit(solution)/shard_map/ppermute | solution.py:17
  106.2 1.3 collective-permute-done.29.refs_0_
  107.5 1.5 collective-permute-start.33
  109.2 2.4 %shard_map.131 = (bf16[256,2048]{1,0:T(8,128)(2,1)S(1)}, f32[256,768]{1,0:T(8,128)S(1)}, bf16[256,768]{1,0:T(8,128)(2,1)S(1)}) custom-call(s32[2]{0:T(128)S(1)} %pad_add_fusion.place_ref, bf16[64,2048]{1,0:T(8,128)(2,1)S(1)} %shard_map.130.refs_0_, bf16[64,2048]{1,0:T(8,128)(2,1)S(1)} %collective-permute-done.28.refs_1_, ...), custom_call_target="tpu_custom_call" | custom-call | flops 1610 | bytes 9 | tf_op jit(solution)/shard_map/pallas_call | solution.py:112
  111.6 1.6 collective-permute-start.32
  113.2 3.0 %collective-permute-done.33.refs_1_ = bf16[64,2048]{1,0:T(8,128)(2,1)S(1)} collective-permute-done((bf16[64,2048]{1,0:T(8,128)(2,1)S(1)}, bf16[64,2048]{1,0:T(8,128)(2,1)S(1)}, u32[]{:S(2)}, u32[]{:S(2)}) %collective-permute-start.33) | collective-permute-done | bytes 262176 | tf_op jit(solution)/shard_map/ppermute | solution.py:17
  116.2 3.9 %shard_map.133.refs_4_ = f32[2,12,2048]{2,1,0:T(8,128)S(1)} custom-call(s32[2]{0:T(128)S(1)} %pad_add_fusion.place_ref, bf16[256,768]{1,0:T(8,128)(2,1)S(1)} %get-tuple-element.57.refs_0_, bf16[256,768]{1,0:T(8,128)(2,1)S(1)} %collective-permute-done.8.refs_1_, bf16[256,2048]{1,0:T(8,128)(2,1)S(1)} %get-tuple-element.74.refs_2_, ...), custom_call_target="tpu_custom_call" | custom-call | flops 1610 | bytes 8 | tf_op jit(solution)/shard_map/pallas_call | solution.py:112
  120.1 2.8 %collective-permute-done.32.refs_0_ = bf16[256,768]{1,0:T(8,128)(2,1)S(1)} collective-permute-done((bf16[256,768]{1,0:T(8,128)(2,1)S(1)}, bf16[256,768]{1,0:T(8,128)(2,1)S(1)}, u32[]{:S(2)}, u32[]{:S(2)}) %collective-permute-start.32) | collective-permute-done | bytes 393248 | tf_op jit(solution)/shard_map/ppermute | solution.py:17
  123.0 2.4 %shard_map.134 = (bf16[256,2048]{1,0:T(8,128)(2,1)S(1)}, f32[256,768]{1,0:T(8,128)S(1)}, bf16[256,768]{1,0:T(8,128)(2,1)S(1)}) custom-call(s32[2]{0:T(128)S(1)} %pad_add_fusion.place_ref, bf16[64,2048]{1,0:T(8,128)(2,1)S(1)} %collective-permute-done.29.refs_0_, bf16[64,2048]{1,0:T(8,128)(2,1)S(1)} %collective-permute-done.33.refs_1_, ...), custom_call_target="tpu_custom_call" | custom-call | flops 1610 | bytes 9 | tf_op jit(solution)/shard_map/pallas_call | solution.py:112
  125.4 1.6 collective-permute-start.36
  127.0 4.2 %shard_map.135 = f32[2,12,2048]{2,1,0:T(8,128)S(1)} custom-call(s32[2]{0:T(128)S(1)} %pad_add_fusion.place_ref, bf16[256,768]{1,0:T(8,128)(2,1)S(1)} %get-tuple-element.60.refs_0_, bf16[256,768]{1,0:T(8,128)(2,1)S(1)} %collective-permute-done.17.refs_1_, bf16[256,2048]{1,0:T(8,128)(2,1)S(1)} %get-tuple-element.80.refs_2_, ...), custom_call_target="tpu_custom_call" | custom-call | flops 1610 | bytes 8 | tf_op jit(solution)/shard_map/pallas_call | solution.py:112
  131.2 4.0 %shard_map.132 = (bf16[256,1536]{1,0:T(8,128)(2,1)S(1)}, bf16[128,2048]{1,0:T(8,128)(2,1)S(1)}, bf16[128,2048]{1,0:T(8,128)(2,1)S(1)}, bf16[128,2048]{1,0:T(8,128)(2,1)S(1)}, bf16[128,2048]{1,0:T(8,128)(2,1)S(1)}) custom-call(s32[2]{0:T(128)S(1)} %pad_add_fusion.place_ref, f32[256,768]{1,0:T(8,128)S(1)} %get-tuple-element.69.grad_own_ref, ...), custom_call_target="tpu_custom_call" | custom-call | flops 3221 | bytes 18 | tf_op jit(solution)/shard_map/pallas_call | solution.py:112
  136.0 4.0 %shard_map.136 = (bf16[256,1536]{1,0:T(8,128)(2,1)S(1)}, bf16[128,2048]{1,0:T(8,128)(2,1)S(1)}, bf16[128,2048]{1,0:T(8,128)(2,1)S(1)}, bf16[128,2048]{1,0:T(8,128)(2,1)S(1)}, bf16[128,2048]{1,0:T(8,128)(2,1)S(1)}) custom-call(s32[2]{0:T(128)S(1)} %pad_add_fusion.place_ref, f32[256,768]{1,0:T(8,128)S(1)} %get-tuple-element.77.grad_own_ref, ...), custom_call_target="tpu_custom_call" | custom-call | flops 3221 | bytes 18 | tf_op jit(solution)/shard_map/pallas_call | solution.py:112
  140.6 1.4 collective-permute-done.39
  142.1 1.1 collective-permute-start.40
  143.7 1.5 collective-permute-start.41
  145.2 5.3 %collective-permute-done.40 = bf16[64,2048]{1,0:T(8,128)(2,1)S(1)} collective-permute-done((bf16[64,2048]{1,0:T(8,128)(2,1)S(1)}, bf16[64,2048]{1,0:T(8,128)(2,1)S(1)}, u32[]{:S(2)}, u32[]{:S(2)}) %collective-permute-start.40) | collective-permute-done | bytes 262176 | tf_op jit(solution)/shard_map/ppermute | solution.py:17
  150.7 1.2 collective-permute-done.41
  151.9 1.5 collective-permute-start.42
  153.6 1.1 collective-permute-start.45
  154.7 6.4 %shard_map.137.refs_11_ = f32[4,32,768]{2,1,0:T(8,128)} custom-call(s32[2]{0:T(128)S(1)} %pad_add_fusion.place_ref, bf16[96,4096]{1,0:T(8,128)(2,1)S(1)} %shard_map.123.refs_0_, bf16[32,4096]{1,0:T(8,128)(2,1)S(1)} %collective-permute-done.3.refs_1_, bf16[96,4096]{1,0:T(8,128)(2,1)S(1)} %collective-permute-done.6.refs_2_, ...), custom_call_target="tpu_custom_call" | custom-call | flops 3221 | bytes 18 | tf_op jit(solution)/shard_map/pallas_call | solution.py:112
  162.4 1.0 collective-permute-start.46
  163.4 3.8 %shard_map.138.refs_11_ = f32[4,32,768]{2,1,0:T(8,128)} custom-call(s32[2]{0:T(128)S(1)} %pad_add_fusion.place_ref, bf16[96,4096]{1,0:T(8,128)(2,1)S(1)} %shard_map.123.refs_0_, bf16[32,4096]{1,0:T(8,128)(2,1)S(1)} %collective-permute-done.3.refs_1_, bf16[96,4096]{1,0:T(8,128)(2,1)S(1)} %collective-permute-done.6.refs_2_, ...), custom_call_target="tpu_custom_call", output_to_operand_aliasing={{}: (12, {})} | custom-call | flops 1610 | bytes 18 | tf_op jit(solution)/shard_map/pallas_call | solution.py:112
  167.3 0.9 collective-permute-done.47
  168.9 1.8 %collective-permute-start.48 = (bf16[32,2048]{1,0:T(8,128)(2,1)S(1)}, bf16[32,2048]{1,0:T(8,128)(2,1)S(1)}, u32[]{:S(2)}, u32[]{:S(2)}) collective-permute-start(bf16[32,2048]{1,0:T(8,128)(2,1)S(1)} %add_convert_fusion.9), channel_id=1, source_target_pairs={{0,16},{2,18},{4,20},{6,22},{8,24},{10,26},{12,28},{14,30},{16,0},... | collective-permute-start | bytes 393224 | tf_op jit(solution)/shard_map/ppermute | solution.py:17
  171.6 3.8 %shard_map.139 = f32[4,32,768]{2,1,0:T(8,128)} custom-call(s32[2]{0:T(128)S(1)} %pad_add_fusion.place_ref, bf16[96,4096]{1,0:T(8,128)(2,1)S(1)} %shard_map.123.refs_0_, bf16[32,4096]{1,0:T(8,128)(2,1)S(1)} %collective-permute-done.3.refs_1_, bf16[96,4096]{1,0:T(8,128)(2,1)S(1)} %collective-permute-done.6.refs_2_, ...), custom_call_target="tpu_custom_call", output_to_operand_aliasing={{}: (12, {})} | custom-call | flops 1610 | bytes 18 | tf_op jit(solution)/shard_map/pallas_call | solution.py:112
  (97 shorter events, 17.0 us)
Async XLA Ops:
  0.6 17.6 %collective-permute-start.1 = (bf16[32,4096]{1,0:T(8,128)(2,1)}, bf16[32,4096]{1,0:T(8,128)(2,1)S(1)}, u32[]{:S(2)}, u32[]{:S(2)}) collective-permute-start(bf16[32,4096]{1,0:T(8,128)(2,1)} %refs_0_.1), channel_id=1, source_target_pairs={{0,4},{2,6},{4,0},{6,2},{8,12},{10,14},{12,8},{14,10},{16,20},{18,... | collective-permute-start | bytes 786440 | tf_op jit(solution)/shard_map/ppermute | solution.py:17
  3.6 14.6 %collective-permute-start = (bf16[32,4096]{1,0:T(8,128)(2,1)}, bf16[32,4096]{1,0:T(8,128)(2,1)S(1)}, u32[]{:S(2)}, u32[]{:S(2)}) collective-permute-start(bf16[32,4096]{1,0:T(8,128)(2,1)} %refs_0_.1), channel_id=1, source_target_pairs={{0,16},{2,18},{4,20},{6,22},{8,24},{10,26},{12,28},{14,30},{16,0},... | collective-permute-start | bytes 786440 | tf_op jit(solution)/shard_map/ppermute | solution.py:17
  6.2 12.7 %collective-permute-start.2 = (bf16[32,4096]{1,0:T(8,128)(2,1)}, bf16[32,4096]{1,0:T(8,128)(2,1)S(1)}, u32[]{:S(2)}, u32[]{:S(2)}) collective-permute-start(bf16[32,4096]{1,0:T(8,128)(2,1)} %refs_0_.1), channel_id=1, source_target_pairs={{0,8},{2,10},{4,12},{6,14},{8,0},{10,2},{12,4},{14,6},{16,24},{18,... | collective-permute-start | bytes 786440 | tf_op jit(solution)/shard_map/ppermute | solution.py:17
  10.2 0.9 copy-start.1
  11.1 0.9 copy-start.2
  12.0 15.0 %copy-start = (bf16[32,4096]{1,0:T(8,128)(2,1)S(1)}, bf16[32,4096]{1,0:T(8,128)(2,1)}, u32[]{:S(2)}) copy-start(bf16[32,4096]{1,0:T(8,128)(2,1)} %refs_0_.1) | copy-start | bytes 786436
  18.3 7.7 %collective-permute-start.3 = (bf16[32,4096]{1,0:T(8,128)(2,1)S(1)}, bf16[32,4096]{1,0:T(8,128)(2,1)S(1)}, u32[]{:S(2)}, u32[]{:S(2)}) collective-permute-start(bf16[32,4096]{1,0:T(8,128)(2,1)S(1)} %collective-permute-done.refs_1_), channel_id=1, source_target_pairs={{0,8},{2,10},{4,12},{6,14},{8,0},{10,2},{12,4},{14,6},{16,24},{18,... | collective-permute-start | bytes 786440 | tf_op jit(solution)/shard_map/ppermute | solution.py:17
  18.9 8.1 %collective-permute-start.4 = (bf16[32,4096]{1,0:T(8,128)(2,1)S(1)}, bf16[32,4096]{1,0:T(8,128)(2,1)S(1)}, u32[]{:S(2)}, u32[]{:S(2)}) collective-permute-start(bf16[32,4096]{1,0:T(8,128)(2,1)S(1)} %collective-permute-done.2.refs_2_), channel_id=1, source_target_pairs={{0,4},{2,6},{4,0},{6,2},{8,12},{10,14},{12,8},{14,10},{16,20},{18,... | collective-permute-start | bytes 786440 | tf_op jit(solution)/shard_map/ppermute | solution.py:17
  19.4 5.4 %collective-permute-start.5 = (bf16[32,128]{1,0:T(8,128)(2,1)S(1)}, bf16[32,128]{1,0:T(8,128)(2,1)S(1)}, u32[]{:S(2)}, u32[]{:S(2)}) collective-permute-start(bf16[32,128]{1,0:T(8,128)(2,1)S(1)} %shard_map.121), channel_id=1, source_target_pairs={{0,16},{2,18},{4,20},{6,22},{8,24},{10,26},{12,28},{14,30},{16,0},... | collective-permute-start | bytes 24584 | tf_op jit(solution)/shard_map/ppermute | solution.py:17
  24.8 7.6 %collective-permute-start.9 = (bf16[32,4096]{1,0:T(8,128)(2,1)S(1)}, bf16[32,4096]{1,0:T(8,128)(2,1)S(1)}, u32[]{:S(2)}, u32[]{:S(2)}) collective-permute-start(bf16[32,4096]{1,0:T(8,128)(2,1)S(1)} %collective-permute-done.refs_1_), channel_id=1, source_target_pairs={{0,4},{2,6},{4,0},{6,2},{8,12},{10,14},{12,8},{14,10},{16,20},{18,... | collective-permute-start | bytes 786440 | tf_op jit(solution)/shard_map/ppermute | solution.py:17
  27.0 5.4 %collective-permute-start.7 = (bf16[32,4096]{1,0:T(8,128)(2,1)S(1)}, bf16[32,4096]{1,0:T(8,128)(2,1)S(1)}, u32[]{:S(2)}, u32[]{:S(2)}) collective-permute-start(bf16[32,4096]{1,0:T(8,128)(2,1)S(1)} %collective-permute-done.3.refs_1_), channel_id=1, source_target_pairs={{0,2},{2,0},{4,6},{6,4},{8,10},{10,8},{12,14},{14,12},{16,18},{18,... | collective-permute-start | bytes 786440 | tf_op jit(solution)/shard_map/ppermute | solution.py:17
  27.7 9.9 %collective-permute-start.6 = (bf16[96,4096]{1,0:T(8,128)(2,1)S(1)}, bf16[96,4096]{1,0:T(8,128)(2,1)S(1)}, u32[]{:S(2)}, u32[]{:S(2)}) collective-permute-start(bf16[96,4096]{1,0:T(8,128)(2,1)S(1)} %shard_map.123.refs_0_), channel_id=1, source_target_pairs={{0,2},{2,0},{4,6},{6,4},{8,10},{10,8},{12,14},{14,12},{16,18},{18,... | collective-permute-start | bytes 2359304 | tf_op jit(solution)/shard_map/ppermute | solution.py:17
  33.1 20.0 %copy-start.4 = (f32[1,12,2048]{2,0,1:T(1,128)S(1)}, f32[1,12,2048]{2,0,1:T(1,128)}, u32[]{:S(2)}) copy-start(f32[1,12,2048]{2,0,1:T(1,128)} %param.19) | copy-start | bytes 294916
  33.1 20.0 %copy-start.5 = (f32[1,12,2048]{2,0,1:T(1,128)S(1)}, f32[1,12,2048]{2,0,1:T(1,128)}, u32[]{:S(2)}) copy-start(f32[1,12,2048]{2,0,1:T(1,128)} %param.18) | copy-start | bytes 294916
  33.1 20.1 %slice-start.3 = ((s8[6291456]{0:T(1024)(128)(4,1)}), s8[4194304]{0:T(1024)(128)(4,1)S(1)}, s32[]{:S(2)}) async-start(s8[6291456]{0:T(1024)(128)(4,1)} %bitcast.10), calls=%async_computation.3 | async-start | bytes 8388608
  33.1 8.8 %collective-permute-start.12 = (bf16[96,4096]{1,0:T(8,128)(2,1)S(1)}, bf16[96,4096]{1,0:T(8,128)(2,1)S(1)}, u32[]{:S(2)}, u32[]{:S(2)}) collective-permute-start(bf16[96,4096]{1,0:T(8,128)(2,1)S(1)} %shard_map.125.refs_0_.refs_4_), channel_id=1, source_target_pairs={{0,2},{2,0},{4,6},{6,4},{8,10},{10,8},{12,14},{14,12},{16,18},{18,... | collective-permute-start | bytes 2359304 | tf_op jit(solution)/shard_map/ppermute | solution.py:17
  33.2 8.7 %collective-permute-start.10 = (bf16[32,4096]{1,0:T(8,128)(2,1)S(1)}, bf16[32,4096]{1,0:T(8,128)(2,1)S(1)}, u32[]{:S(2)}, u32[]{:S(2)}) collective-permute-start(bf16[32,4096]{1,0:T(8,128)(2,1)S(1)} %collective-permute-done.3.refs_1_), channel_id=1, source_target_pairs={{0,4},{2,6},{4,0},{6,2},{8,12},{10,14},{12,8},{14,10},{16,20},{18,... | collective-permute-start | bytes 786440 | tf_op jit(solution)/shard_map/ppermute | solution.py:17
  33.8 7.9 %collective-permute-start.11 = (bf16[64,128]{1,0:T(8,128)(2,1)S(1)}, bf16[64,128]{1,0:T(8,128)(2,1)S(1)}, u32[]{:S(2)}, u32[]{:S(2)}) collective-permute-start(bf16[64,128]{1,0:T(8,128)(2,1)S(1)} %pad_maximum_fusion.2), channel_id=1, source_target_pairs={{0,8},{2,10},{4,12},{6,14},{8,0},{10,2},{12,4},{14,6},{16,24},{18,... | collective-permute-start | bytes 49160 | tf_op jit(solution)/shard_map/ppermute | solution.py:17
  41.9 11.3 %slice-start.4 = ((s8[6291456]{0:T(1024)(128)(4,1)}), s8[2097152]{0:T(1024)(128)(4,1)S(1)}, s32[]{:S(2)}) async-start(s8[6291456]{0:T(1024)(128)(4,1)} %bitcast.10), calls=%async_computation.4 | async-start | bytes 4194304
  41.9 1.6 collective-permute-start.13
  41.9 13.7 %collective-permute-start.8 = (bf16[256,768]{1,0:T(8,128)(2,1)S(1)}, bf16[256,768]{1,0:T(8,128)(2,1)S(1)}, u32[]{:S(2)}, u32[]{:S(2)}) collective-permute-start(bf16[256,768]{1,0:T(8,128)(2,1)S(1)} %get-tuple-element.57.refs_0_), channel_id=1, source_target_pairs={{0,1},{1,0},{2,3},{3,2},{4,5},{5,4},{6,7},{7,6},{8,9},{9,8},{10,11... | collective-permute-start | bytes 1179656 | tf_op jit(solution)/shard_map/ppermute | solution.py:17
  47.6 14.3 %collective-permute-start.17 = (bf16[256,768]{1,0:T(8,128)(2,1)S(1)}, bf16[256,768]{1,0:T(8,128)(2,1)S(1)}, u32[]{:S(2)}, u32[]{:S(2)}) collective-permute-start(bf16[256,768]{1,0:T(8,128)(2,1)S(1)} %get-tuple-element.60.refs_0_), channel_id=1, source_target_pairs={{0,1},{1,0},{2,3},{3,2},{4,5},{5,4},{6,7},{7,6},{8,9},{9,8},{10,11... | collective-permute-start | bytes 1179656 | tf_op jit(solution)/shard_map/ppermute | solution.py:17
  49.1 3.9 %collective-permute-start.14 = (bf16[128,128]{1,0:T(8,128)(2,1)S(1)}, bf16[128,128]{1,0:T(8,128)(2,1)S(1)}, u32[]{:S(2)}, u32[]{:S(2)}) collective-permute-start(bf16[128,128]{1,0:T(8,128)(2,1)S(1)} %pad_maximum_fusion.1), channel_id=1, source_target_pairs={{0,4},{2,6},{4,0},{6,2},{8,12},{10,14},{12,8},{14,10},{16,20},{18,... | collective-permute-start | bytes 98312 | tf_op jit(solution)/shard_map/ppermute | solution.py:17
  53.0 2.6 %collective-permute-start.15 = (bf16[256,128]{1,0:T(8,128)(2,1)S(1)}, bf16[256,128]{1,0:T(8,128)(2,1)S(1)}, u32[]{:S(2)}, u32[]{:S(2)}) collective-permute-start(bf16[256,128]{1,0:T(8,128)(2,1)S(1)} %pad_maximum_fusion.refs_3_.refs_4_), channel_id=1, source_target_pairs={{0,2},{2,0},{4,6},{6,4},{8,10},{10,8},{12,14},{14,12},{16,18},{18,... | collective-permute-start | bytes 196616 | tf_op jit(solution)/shard_map/ppermute | solution.py:17
  53.2 39.4 %copy-start.3 = (bf16[32,2048]{1,0:T(8,128)(2,1)S(1)}, bf16[32,2048]{1,0:T(8,128)(2,1)}, u32[]{:S(2)}) copy-start(bf16[32,2048]{1,0:T(8,128)(2,1)} %param.11) | copy-start | bytes 393220
  64.2 2.0 %collective-permute-start.18 = (bf16[128,2048]{1,0:T(8,128)(2,1)S(1)}, bf16[128,2048]{1,0:T(8,128)(2,1)S(1)}, u32[]{:S(2)}, u32[]{:S(2)}) collective-permute-start(bf16[128,2048]{1,0:T(8,128)(2,1)S(1)} %get-tuple-element.66), channel_id=1, source_target_pairs={{0,2},{2,0},{4,6},{6,4},{8,10},{10,8},{12,14},{14,12},{16,18},{18,... | collective-permute-start | bytes 1572872 | tf_op jit(solution)/shard_map/ppermute | solution.py:17
  64.3 11.7 %collective-permute-start.16 = (bf16[128,2048]{1,0:T(8,128)(2,1)S(1)}, bf16[128,2048]{1,0:T(8,128)(2,1)S(1)}, u32[]{:S(2)}, u32[]{:S(2)}) collective-permute-start(bf16[128,2048]{1,0:T(8,128)(2,1)S(1)} %get-tuple-element.63), channel_id=1, source_target_pairs={{0,2},{2,0},{4,6},{6,4},{8,10},{10,8},{12,14},{14,12},{16,18},{18,... | collective-permute-start | bytes 1572872 | tf_op jit(solution)/shard_map/ppermute | solution.py:17
  66.3 6.4 %collective-permute-start.19 = (bf16[64,1024]{1,0:T(8,128)(2,1)S(1)}, bf16[64,1024]{1,0:T(8,128)(2,1)S(1)}, u32[]{:S(2)}, u32[]{:S(2)}) collective-permute-start(bf16[64,1024]{1,0:T(8,128)(2,1)S(1)} %get-tuple-element.119), channel_id=1, source_target_pairs={{0,4},{2,6},{4,0},{6,2},{8,12},{10,14},{12,8},{14,10},{16,20},{18,... | collective-permute-start | bytes 393224 | tf_op jit(solution)/shard_map/ppermute | solution.py:17
  67.7 7.0 %collective-permute-start.20 = (bf16[64,1024]{1,0:T(8,128)(2,1)S(1)}, bf16[64,1024]{1,0:T(8,128)(2,1)S(1)}, u32[]{:S(2)}, u32[]{:S(2)}) collective-permute-start(bf16[64,1024]{1,0:T(8,128)(2,1)S(1)} %get-tuple-element.118), channel_id=1, source_target_pairs={{0,4},{2,6},{4,0},{6,2},{8,12},{10,14},{12,8},{14,10},{16,20},{18,... | collective-permute-start | bytes 393224 | tf_op jit(solution)/shard_map/ppermute | solution.py:17
  74.7 10.1 %collective-permute-start.21 = (bf16[64,2048]{1,0:T(8,128)(2,1)S(1)}, bf16[64,2048]{1,0:T(8,128)(2,1)S(1)}, u32[]{:S(2)}, u32[]{:S(2)}) collective-permute-start(bf16[64,2048]{1,0:T(8,128)(2,1)S(1)} %add_convert_fusion.7), channel_id=1, source_target_pairs={{0,4},{2,6},{4,0},{6,2},{8,12},{10,14},{12,8},{14,10},{16,20},{18,... | collective-permute-start | bytes 786440 | tf_op jit(solution)/shard_map/ppermute | solution.py:17
  76.1 7.2 %collective-permute-start.22 = (bf16[64,1024]{1,0:T(8,128)(2,1)S(1)}, bf16[64,1024]{1,0:T(8,128)(2,1)S(1)}, u32[]{:S(2)}, u32[]{:S(2)}) collective-permute-start(bf16[64,1024]{1,0:T(8,128)(2,1)S(1)} %get-tuple-element.117), channel_id=1, source_target_pairs={{0,8},{2,10},{4,12},{6,14},{8,0},{10,2},{12,4},{14,6},{16,24},{18,... | collective-permute-start | bytes 393224 | tf_op jit(solution)/shard_map/ppermute | solution.py:17
  79.2 5.6 %collective-permute-start.24 = (bf16[64,1024]{1,0:T(8,128)(2,1)S(1)}, bf16[64,1024]{1,0:T(8,128)(2,1)S(1)}, u32[]{:S(2)}, u32[]{:S(2)}) collective-permute-start(bf16[64,1024]{1,0:T(8,128)(2,1)S(1)} %get-tuple-element.116), channel_id=1, source_target_pairs={{0,8},{2,10},{4,12},{6,14},{8,0},{10,2},{12,4},{14,6},{16,24},{18,... | collective-permute-start | bytes 393224 | tf_op jit(solution)/shard_map/ppermute | solution.py:17
  84.8 5.6 %collective-permute-start.23 = (bf16[32,1024]{1,0:T(8,128)(2,1)S(1)}, bf16[32,1024]{1,0:T(8,128)(2,1)S(1)}, u32[]{:S(2)}, u32[]{:S(2)}) collective-permute-start(bf16[32,1024]{1,0:T(8,128)(2,1)S(1)} %get-tuple-element.109), channel_id=1, source_target_pairs={{0,16},{2,18},{4,20},{6,22},{8,24},{10,26},{12,28},{14,30},{16,0},... | collective-permute-start | bytes 196616 | tf_op jit(solution)/shard_map/ppermute | solution.py:17
  86.1 6.5 %collective-permute-start.25 = (bf16[32,1024]{1,0:T(8,128)(2,1)S(1)}, bf16[32,1024]{1,0:T(8,128)(2,1)S(1)}, u32[]{:S(2)}, u32[]{:S(2)}) collective-permute-start(bf16[32,1024]{1,0:T(8,128)(2,1)S(1)} %get-tuple-element.108), channel_id=1, source_target_pairs={{0,16},{2,18},{4,20},{6,22},{8,24},{10,26},{12,28},{14,30},{16,0},... | collective-permute-start | bytes 196616 | tf_op jit(solution)/shard_map/ppermute | solution.py:17
  92.7 5.8 %collective-permute-start.26 = (bf16[32,1024]{1,0:T(8,128)(2,1)S(1)}, bf16[32,1024]{1,0:T(8,128)(2,1)S(1)}, u32[]{:S(2)}, u32[]{:S(2)}) collective-permute-start(bf16[32,1024]{1,0:T(8,128)(2,1)S(1)} %get-tuple-element.107.refs_0_), channel_id=1, source_target_pairs={{0,16},{2,18},{4,20},{6,22},{8,24},{10,26},{12,28},{14,30},{16,0},... | collective-permute-start | bytes 196616 | tf_op jit(solution)/shard_map/ppermute | solution.py:17
  93.2 6.0 %collective-permute-start.27 = (bf16[32,1024]{1,0:T(8,128)(2,1)S(1)}, bf16[32,1024]{1,0:T(8,128)(2,1)S(1)}, u32[]{:S(2)}, u32[]{:S(2)}) collective-permute-start(bf16[32,1024]{1,0:T(8,128)(2,1)S(1)} %get-tuple-element.106.refs_1_), channel_id=1, source_target_pairs={{0,16},{2,18},{4,20},{6,22},{8,24},{10,26},{12,28},{14,30},{16,0},... | collective-permute-start | bytes 196616 | tf_op jit(solution)/shard_map/ppermute | solution.py:17
  99.7 6.4 %collective-permute-start.28 = (bf16[64,2048]{1,0:T(8,128)(2,1)S(1)}, bf16[64,2048]{1,0:T(8,128)(2,1)S(1)}, u32[]{:S(2)}, u32[]{:S(2)}) collective-permute-start(bf16[64,2048]{1,0:T(8,128)(2,1)S(1)} %shard_map.130.refs_0_), channel_id=1, source_target_pairs={{0,8},{2,10},{4,12},{6,14},{8,0},{10,2},{12,4},{14,6},{16,24},{18,... | collective-permute-start | bytes 786440 | tf_op jit(solution)/shard_map/ppermute | solution.py:17
  101.1 6.4 %collective-permute-start.29 = (bf16[64,2048]{1,0:T(8,128)(2,1)S(1)}, bf16[64,2048]{1,0:T(8,128)(2,1)S(1)}, u32[]{:S(2)}, u32[]{:S(2)}) collective-permute-start(bf16[64,2048]{1,0:T(8,128)(2,1)S(1)} %shard_map.130.refs_0_), channel_id=1, source_target_pairs={{0,4},{2,6},{4,0},{6,2},{8,12},{10,14},{12,8},{14,10},{16,20},{18,... | collective-permute-start | bytes 786440 | tf_op jit(solution)/shard_map/ppermute | solution.py:17
  102.6 4.9 %collective-permute-start.30 = (bf16[64,2048]{1,0:T(8,128)(2,1)S(1)}, bf16[64,2048]{1,0:T(8,128)(2,1)S(1)}, u32[]{:S(2)}, u32[]{:S(2)}) collective-permute-start(bf16[64,2048]{1,0:T(8,128)(2,1)S(1)} %shard_map.130.refs_0_), channel_id=1, source_target_pairs={{0,2},{2,0},{4,6},{6,4},{8,10},{10,8},{12,14},{14,12},{16,18},{18,... | collective-permute-start | bytes 786440 | tf_op jit(solution)/shard_map/ppermute | solution.py:17
  107.5 1.7 collective-permute-start.31
  107.5 8.7 %collective-permute-start.33 = (bf16[64,2048]{1,0:T(8,128)(2,1)S(1)}, bf16[64,2048]{1,0:T(8,128)(2,1)S(1)}, u32[]{:S(2)}, u32[]{:S(2)}) collective-permute-start(bf16[64,2048]{1,0:T(8,128)(2,1)S(1)} %collective-permute-done.28.refs_1_), channel_id=1, source_target_pairs={{0,4},{2,6},{4,0},{6,2},{8,12},{10,14},{12,8},{14,10},{16,20},{18,... | collective-permute-start | bytes 786440 | tf_op jit(solution)/shard_map/ppermute | solution.py:17
  109.0 7.3 %collective-permute-start.34 = (bf16[64,2048]{1,0:T(8,128)(2,1)S(1)}, bf16[64,2048]{1,0:T(8,128)(2,1)S(1)}, u32[]{:S(2)}, u32[]{:S(2)}) collective-permute-start(bf16[64,2048]{1,0:T(8,128)(2,1)S(1)} %collective-permute-done.29.refs_0_), channel_id=1, source_target_pairs={{0,2},{2,0},{4,6},{6,4},{8,10},{10,8},{12,14},{14,12},{16,18},{18,... | collective-permute-start | bytes 786440 | tf_op jit(solution)/shard_map/ppermute | solution.py:17
  111.6 11.4 %collective-permute-start.32 = (bf16[256,768]{1,0:T(8,128)(2,1)S(1)}, bf16[256,768]{1,0:T(8,128)(2,1)S(1)}, u32[]{:S(2)}, u32[]{:S(2)}) collective-permute-start(bf16[256,768]{1,0:T(8,128)(2,1)S(1)} %get-tuple-element.70), channel_id=1, source_target_pairs={{0,1},{1,0},{2,3},{3,2},{4,5},{5,4},{6,7},{7,6},{8,9},{9,8},{10,11... | collective-permute-start | bytes 1179656 | tf_op jit(solution)/shard_map/ppermute | solution.py:17
  116.2 3.9 %collective-permute-start.35 = (bf16[64,2048]{1,0:T(8,128)(2,1)S(1)}, bf16[64,2048]{1,0:T(8,128)(2,1)S(1)}, u32[]{:S(2)}, u32[]{:S(2)}) collective-permute-start(bf16[64,2048]{1,0:T(8,128)(2,1)S(1)} %collective-permute-done.33.refs_1_), channel_id=1, source_target_pairs={{0,2},{2,0},{4,6},{6,4},{8,10},{10,8},{12,14},{14,12},{16,18},{18,... | collective-permute-start | bytes 786440 | tf_op jit(solution)/shard_map/ppermute | solution.py:17
  125.4 10.6 %collective-permute-start.36 = (bf16[256,768]{1,0:T(8,128)(2,1)S(1)}, bf16[256,768]{1,0:T(8,128)(2,1)S(1)}, u32[]{:S(2)}, u32[]{:S(2)}) collective-permute-start(bf16[256,768]{1,0:T(8,128)(2,1)S(1)} %get-tuple-element.78), channel_id=1, source_target_pairs={{0,1},{1,0},{2,3},{3,2},{4,5},{5,4},{6,7},{7,6},{8,9},{9,8},{10,11... | collective-permute-start | bytes 1179656 | tf_op jit(solution)/shard_map/ppermute | solution.py:17
  131.2 23.5 %slice-start = ((s8[12582912]{0:T(1024)(128)(4,1)}), s8[4194304]{0:T(1024)(128)(4,1)S(1)}, s32[]{:S(2)}) async-start(s8[12582912]{0:T(1024)(128)(4,1)} %bitcast.8), calls=%async_computation | async-start | bytes 8388608
  131.2 23.5 %slice-start.1 = ((s8[12582912]{0:T(1024)(128)(4,1)}), s8[4194304]{0:T(1024)(128)(4,1)S(1)}, s32[]{:S(2)}) async-start(s8[12582912]{0:T(1024)(128)(4,1)} %bitcast.8), calls=%async_computation.1 | async-start | bytes 8388608
  136.0 18.7 %slice-start.2 = ((s8[12582912]{0:T(1024)(128)(4,1)}), s8[4194304]{0:T(1024)(128)(4,1)S(1)}, s32[]{:S(2)}) async-start(s8[12582912]{0:T(1024)(128)(4,1)} %bitcast.8), calls=%async_computation.2 | async-start | bytes 8388608
  140.0 2.0 %collective-permute-start.39 = (bf16[128,2048]{1,0:T(8,128)(2,1)S(1)}, bf16[128,2048]{1,0:T(8,128)(2,1)S(1)}, u32[]{:S(2)}, u32[]{:S(2)}) collective-permute-start(bf16[128,2048]{1,0:T(8,128)(2,1)S(1)} %get-tuple-element.93), channel_id=1, source_target_pairs={{0,2},{2,0},{4,6},{6,4},{8,10},{10,8},{12,14},{14,12},{16,18},{18,... | collective-permute-start | bytes 1572872 | tf_op jit(solution)/shard_map/ppermute | solution.py:17
  140.1 5.1 %collective-permute-start.38 = (bf16[128,2048]{1,0:T(8,128)(2,1)S(1)}, bf16[128,2048]{1,0:T(8,128)(2,1)S(1)}, u32[]{:S(2)}, u32[]{:S(2)}) collective-permute-start(bf16[128,2048]{1,0:T(8,128)(2,1)S(1)} %get-tuple-element.91), channel_id=1, source_target_pairs={{0,2},{2,0},{4,6},{6,4},{8,10},{10,8},{12,14},{14,12},{16,18},{18,... | collective-permute-start | bytes 1572872 | tf_op jit(solution)/shard_map/ppermute | solution.py:17
  142.1 8.4 %collective-permute-start.40 = (bf16[64,2048]{1,0:T(8,128)(2,1)S(1)}, bf16[64,2048]{1,0:T(8,128)(2,1)S(1)}, u32[]{:S(2)}, u32[]{:S(2)}) collective-permute-start(bf16[64,2048]{1,0:T(8,128)(2,1)S(1)} %get-tuple-element.112), channel_id=1, source_target_pairs={{0,4},{2,6},{4,0},{6,2},{8,12},{10,14},{12,8},{14,10},{16,20},{18,... | collective-permute-start | bytes 786440 | tf_op jit(solution)/shard_map/ppermute | solution.py:17
  143.1 10.2 %collective-permute-start.44 = (bf16[128,2048]{1,0:T(8,128)(2,1)S(1)}, bf16[128,2048]{1,0:T(8,128)(2,1)S(1)}, u32[]{:S(2)}, u32[]{:S(2)}) collective-permute-start(bf16[128,2048]{1,0:T(8,128)(2,1)S(1)} %get-tuple-element.97), channel_id=1, source_target_pairs={{0,2},{2,0},{4,6},{6,4},{8,10},{10,8},{12,14},{14,12},{16,18},{18,... | collective-permute-start | bytes 1572872 | tf_op jit(solution)/shard_map/ppermute | solution.py:17
  143.1 18.0 %collective-permute-start.37 = (bf16[128,2048]{1,0:T(8,128)(2,1)S(1)}, bf16[128,2048]{1,0:T(8,128)(2,1)S(1)}, u32[]{:S(2)}, u32[]{:S(2)}) collective-permute-start(bf16[128,2048]{1,0:T(8,128)(2,1)S(1)} %get-tuple-element.87), channel_id=1, source_target_pairs={{0,2},{2,0},{4,6},{6,4},{8,10},{10,8},{12,14},{14,12},{16,18},{18,... | collective-permute-start | bytes 1572872 | tf_op jit(solution)/shard_map/ppermute | solution.py:17
  143.7 8.2 %collective-permute-start.41 = (bf16[64,2048]{1,0:T(8,128)(2,1)S(1)}, bf16[64,2048]{1,0:T(8,128)(2,1)S(1)}, u32[]{:S(2)}, u32[]{:S(2)}) collective-permute-start(bf16[64,2048]{1,0:T(8,128)(2,1)S(1)} %get-tuple-element.113), channel_id=1, source_target_pairs={{0,1},{1,0},{2,3},{3,2},{4,5},{5,4},{6,7},{7,6},{8,9},{9,8},{10,11... | collective-permute-start | bytes 786440 | tf_op jit(solution)/shard_map/ppermute | solution.py:17
  151.9 9.2 %collective-permute-start.42 = (bf16[64,2048]{1,0:T(8,128)(2,1)S(1)}, bf16[64,2048]{1,0:T(8,128)(2,1)S(1)}, u32[]{:S(2)}, u32[]{:S(2)}) collective-permute-start(bf16[64,2048]{1,0:T(8,128)(2,1)S(1)} %get-tuple-element.94), channel_id=1, source_target_pairs={{0,1},{1,0},{2,3},{3,2},{4,5},{5,4},{6,7},{7,6},{8,9},{9,8},{10,11... | collective-permute-start | bytes 786440 | tf_op jit(solution)/shard_map/ppermute | solution.py:17
  153.6 7.5 %collective-permute-start.45 = (bf16[64,2048]{1,0:T(8,128)(2,1)S(1)}, bf16[64,2048]{1,0:T(8,128)(2,1)S(1)}, u32[]{:S(2)}, u32[]{:S(2)}) collective-permute-start(bf16[64,2048]{1,0:T(8,128)(2,1)S(1)} %get-tuple-element.114), channel_id=1, source_target_pairs={{0,4},{2,6},{4,0},{6,2},{8,12},{10,14},{12,8},{14,10},{16,20},{18,... | collective-permute-start | bytes 786440 | tf_op jit(solution)/shard_map/ppermute | solution.py:17
  161.3 6.9 %collective-permute-start.47 = (bf16[64,2048]{1,0:T(8,128)(2,1)S(1)}, bf16[64,2048]{1,0:T(8,128)(2,1)S(1)}, u32[]{:S(2)}, u32[]{:S(2)}) collective-permute-start(bf16[64,2048]{1,0:T(8,128)(2,1)S(1)} %add_convert_fusion), channel_id=1, source_target_pairs={{0,8},{2,10},{4,12},{6,14},{8,0},{10,2},{12,4},{14,6},{16,24},{18,... | collective-permute-start | bytes 786440 | tf_op jit(solution)/shard_map/ppermute | solution.py:17
  161.9 6.5 %collective-permute-start.43 = (bf16[64,2048]{1,0:T(8,128)(2,1)S(1)}, bf16[64,2048]{1,0:T(8,128)(2,1)S(1)}, u32[]{:S(2)}, u32[]{:S(2)}) collective-permute-start(bf16[64,2048]{1,0:T(8,128)(2,1)S(1)} %get-tuple-element.95), channel_id=1, source_target_pairs={{0,1},{1,0},{2,3},{3,2},{4,5},{5,4},{6,7},{7,6},{8,9},{9,8},{10,11... | collective-permute-start | bytes 786440 | tf_op jit(solution)/shard_map/ppermute | solution.py:17
  162.4 6.4 %collective-permute-start.46 = (bf16[64,2048]{1,0:T(8,128)(2,1)S(1)}, bf16[64,2048]{1,0:T(8,128)(2,1)S(1)}, u32[]{:S(2)}, u32[]{:S(2)}) collective-permute-start(bf16[64,2048]{1,0:T(8,128)(2,1)S(1)} %get-tuple-element.98), channel_id=1, source_target_pairs={{0,4},{2,6},{4,0},{6,2},{8,12},{10,14},{12,8},{14,10},{16,20},{18,... | collective-permute-start | bytes 786440 | tf_op jit(solution)/shard_map/ppermute | solution.py:17
  168.9 7.3 %collective-permute-start.48 = (bf16[32,2048]{1,0:T(8,128)(2,1)S(1)}, bf16[32,2048]{1,0:T(8,128)(2,1)S(1)}, u32[]{:S(2)}, u32[]{:S(2)}) collective-permute-start(bf16[32,2048]{1,0:T(8,128)(2,1)S(1)} %add_convert_fusion.9), channel_id=1, source_target_pairs={{0,16},{2,18},{4,20},{6,22},{8,24},{10,26},{12,28},{14,30},{16,0},... | collective-permute-start | bytes 393224 | tf_op jit(solution)/shard_map/ppermute | solution.py:17

commit v10 on v9

--- a/solution.py
+++ b/solution.py
@@ -577,21 +577,19 @@
     far = tie(far, w_in, across_own)
     near_far = swap(far, "expert", 4)
     across_far = swap(far, "expert", 2)
-    terms = join(gather_far(terms))
-    near_far = tie(near_far, across_near, terms)
+    near_far = tie(near_far, across_near)
     first = pack(place, [[tokens], [far], [near_own]])
     first_other = swap(first, "expert", 1)
     across_last = swap(near_far, "expert", 2)
     near_other = swap(near_far, "expert", 1)
     x = [[first, near_far, first_other, near_other]]
-    near_terms = swap(terms, "expert", 4)
 
     hidden, slope, act = [], [], []
     for c in chunks:
         if c == 1:
             second = pack(place, [[across_own], [tie(across_far, near_other)], [across_near]])
             second_other = swap(second, "expert", 1)
-            across_last = tie(across_last, hidden[0][0], near_terms, second_other)
+            across_last = tie(across_last, hidden[0][0], second_other)
             x.append([second, across_last, second_other, swap(across_last, "expert", 1)])
         own, chunk_slope, chunk_act = forward_in(place, x[c], w_in)
         if c == 1:
@@ -599,8 +597,9 @@
         hidden.append([own] + [swap(own, "half", d) for d in parts if d])
         slope.append(chunk_slope)
         act.append(chunk_act)
-    terms = jnp.concatenate([terms, near_terms], axis=0)
-    terms = jnp.concatenate([terms, swap(terms, "expert", 2)], axis=0)
+    terms = join(gather_far(tie(terms, hidden[1][0])))
+    for distance in (4, 2):
+        terms = jnp.concatenate([terms, swap(terms, "expert", distance)], axis=0)
     terms = (terms, swap(terms, "expert", 1))
 
     sums = []

time: 177 us -> 181 us (1.023)
  waiting for transfers between devices: 57.4 us -> 66.1 us
  starting transfers between devices: 53.3 us -> 48 us
    ppermute x49, waiting for transfers between devices: 57.4 us -> 66.1 us  [swap(): return lax.ppermute(array, axis, [(i, i ^ distance) for i in range(size)])]
    ppermute x49, starting transfers between devices: 53.3 us -> 48 us  [swap(): return lax.ppermute(array, axis, [(i, i ^ distance) for i in range(size)])]
    unnamed x26 -> x29, local copies, waits for them, and re-layouts: 4.28 us -> 4.3 us
  transfers between devices with their start and end apart: 49 -> 49, of which waited for: 28 -> 29; matrix products, arithmetic and copies ran while one was open for 2% -> 2% of each run, Pallas kernels for 28% -> 28%
where the time goes in v10:
time: 181 us; the launch traced here: 180 us
  waiting for transfers between devices  66.1 us (37%)
  Pallas kernels  58.9 us (33%)
  starting transfers between devices  48 us (27%)
  local copies, waits for them, and re-layouts  4.34 us (2%)
  other arithmetic  1.98 us (1%)
    ppermute x49, waiting for transfers between devices, swap(): return lax.ppermute(array, axis, [(i, i ^ distance) for i in range(size)])  66.1 us
    pallas_call x19, Pallas kernels, call(): pl.pallas_call(kernel, grid_spec=pltpu.PrefetchScalarGridSpec(num_scalar_...  58.9 us
    ppermute x49, starting transfers between devices, swap(): return lax.ppermute(array, axis, [(i, i ^ distance) for i in range(size)])  48 us
    unnamed x29, local copies, waits for them, and re-layouts  4.3 us
  transfers between devices with their start and end apart: 49, of which 29 were waited for; matrix products, arithmetic and copies ran while one was open for 2% of the time, Pallas kernels for 28%

profile of v10, /device:TPU:0, one launch (start us, length us, event | category | flops | bytes accessed | tf_op | source)
XLA Modules:
  0.0 180.4 jit_solution(11956904293310819363)
XLA Ops:
  0.6 3.0 %collective-permute-start.1 = (bf16[32,4096]{1,0:T(8,128)(2,1)}, bf16[32,4096]{1,0:T(8,128)(2,1)S(1)}, u32[]{:S(2)}, u32[]{:S(2)}) collective-permute-start(bf16[32,4096]{1,0:T(8,128)(2,1)} %refs_0_.1), channel_id=1, source_target_pairs={{0,4},{2,6},{4,0},{6,2},{8,12},{10,14},{12,8},{14,10},{16,20},{18,... | collective-permute-start | bytes 786440 | tf_op jit(solution)/shard_map/ppermute | solution.py:17
  3.6 2.6 %collective-permute-start = (bf16[32,4096]{1,0:T(8,128)(2,1)}, bf16[32,4096]{1,0:T(8,128)(2,1)S(1)}, u32[]{:S(2)}, u32[]{:S(2)}) collective-permute-start(bf16[32,4096]{1,0:T(8,128)(2,1)} %refs_0_.1), channel_id=1, source_target_pairs={{0,16},{2,18},{4,20},{6,22},{8,24},{10,26},{12,28},{14,30},{16,0},... | collective-permute-start | bytes 786440 | tf_op jit(solution)/shard_map/ppermute | solution.py:17
  6.2 1.6 collective-permute-start.2
  10.2 0.9 copy-done.1
  11.1 0.9 copy-done.2
  12.0 6.2 %shard_map.122.refs_4_.refs_3_ = bf16[4096,1536]{1,0:T(8,128)(2,1)S(1)} custom-call(s32[2]{0:T(128)S(1)} %pad_add_fusion.place_ref, bf16[2,4096,768]{2,1,0:T(8,128)(2,1)} %bitcast.7, f32[2,32,768]{2,1,0:T(8,128)S(1)} %bitcast.13, f32[2,32,768]{2,1,0:T(8,128)S(1)} %bitcast.14), custom_call_target="tpu_custom_call" | custom-call | bytes 25 | tf_op jit(solution)/shard_map/pallas_call | solution.py:112
  18.4 1.4 collective-permute-start.3
  20.4 1.5 collective-permute-start.8
  21.9 3.6 %collective-permute-done.3.refs_1_ = bf16[32,4096]{1,0:T(8,128)(2,1)S(1)} collective-permute-done((bf16[32,4096]{1,0:T(8,128)(2,1)S(1)}, bf16[32,4096]{1,0:T(8,128)(2,1)S(1)}, u32[]{:S(2)}, u32[]{:S(2)}) %collective-permute-start.3) | collective-permute-done | bytes 262176 | tf_op jit(solution)/shard_map/ppermute | solution.py:17
  25.5 3.6 %collective-permute-done.4.refs_2_ = bf16[32,4096]{1,0:T(8,128)(2,1)S(1)} collective-permute-done((bf16[32,4096]{1,0:T(8,128)(2,1)S(1)}, bf16[32,4096]{1,0:T(8,128)(2,1)S(1)}, u32[]{:S(2)}, u32[]{:S(2)}) %collective-permute-start.4) | collective-permute-done | bytes 262176 | tf_op jit(solution)/shard_map/ppermute | solution.py:17
  30.3 2.2 %collective-permute-done.8.refs_1_ = bf16[32,4096]{1,0:T(8,128)(2,1)S(1)} collective-permute-done((bf16[32,4096]{1,0:T(8,128)(2,1)S(1)}, bf16[32,4096]{1,0:T(8,128)(2,1)S(1)}, u32[]{:S(2)}, u32[]{:S(2)}) %collective-permute-start.8) | collective-permute-done | bytes 262176 | tf_op jit(solution)/shard_map/ppermute | solution.py:17
  33.8 4.1 %shard_map.124 = (bf16[256,768]{1,0:T(8,128)(2,1)S(1)}, f32[256,768]{1,0:T(8,128)S(1)}, f32[256,768]{1,0:T(8,128)S(1)}) custom-call(s32[2]{0:T(128)S(1)} %pad_add_fusion.place_ref, bf16[96,4096]{1,0:T(8,128)(2,1)S(1)} %shard_map.123.refs_0_, bf16[32,4096]{1,0:T(8,128)(2,1)S(1)} %collective-permute-done.3.refs_1_, ...), custom_call_target="tpu_custom_call" | custom-call | flops 3221 | bytes 16 | tf_op jit(solution)/shard_map/pallas_call | solution.py:112
  37.9 4.0 %collective-permute-done.9.refs_1_.refs_5_ = bf16[32,4096]{1,0:T(8,128)(2,1)S(1)} collective-permute-done((bf16[32,4096]{1,0:T(8,128)(2,1)S(1)}, bf16[32,4096]{1,0:T(8,128)(2,1)S(1)}, u32[]{:S(2)}, u32[]{:S(2)}) %collective-permute-start.9) | collective-permute-done | bytes 262176 | tf_op jit(solution)/shard_map/ppermute | solution.py:17
  41.9 1.6 collective-permute-start.7
  43.5 4.1 %shard_map.126 = (bf16[256,768]{1,0:T(8,128)(2,1)S(1)}, f32[256,768]{1,0:T(8,128)S(1)}, f32[256,768]{1,0:T(8,128)S(1)}) custom-call(s32[2]{0:T(128)S(1)} %pad_add_fusion.place_ref, bf16[96,4096]{1,0:T(8,128)(2,1)S(1)} %shard_map.125.refs_0_.refs_4_, bf16[32,4096]{1,0:T(8,128)(2,1)S(1)} %collective-permute-done.9.refs_1_.refs_5_, ...), custom_call_target="tpu_custom_call" | custom-call | flops 3221 | bytes 16 | tf_op jit(solution)/shard_map/pallas_call | solution.py:112
  47.6 3.3 %collective-permute-start.12 = (bf16[32,128]{1,0:T(8,128)(2,1)S(1)}, bf16[32,128]{1,0:T(8,128)(2,1)S(1)}, u32[]{:S(2)}, u32[]{:S(2)}) collective-permute-start(bf16[32,128]{1,0:T(8,128)(2,1)S(1)} %shard_map.121), channel_id=1, source_target_pairs={{0,16},{2,18},{4,20},{6,22},{8,24},{10,26},{12,28},{14,30},{16,0},... | collective-permute-start | bytes 24584 | tf_op jit(solution)/shard_map/ppermute | solution.py:17
  50.9 1.5 collective-permute-start.17
  52.9 3.4 %collective-permute-done.13 = bf16[64,128]{1,0:T(8,128)(2,1)S(1)} collective-permute-done((bf16[64,128]{1,0:T(8,128)(2,1)S(1)}, bf16[64,128]{1,0:T(8,128)(2,1)S(1)}, u32[]{:S(2)}, u32[]{:S(2)}) %collective-permute-start.13) | collective-permute-done | bytes 16416 | tf_op jit(solution)/shard_map/ppermute | solution.py:17
  56.9 3.4 %collective-permute-done.14 = bf16[128,128]{1,0:T(8,128)(2,1)S(1)} collective-permute-done((bf16[128,128]{1,0:T(8,128)(2,1)S(1)}, bf16[128,128]{1,0:T(8,128)(2,1)S(1)}, u32[]{:S(2)}, u32[]{:S(2)}) %collective-permute-start.14) | collective-permute-done | bytes 32800 | tf_op jit(solution)/shard_map/ppermute | solution.py:17
  60.4 2.4 %shard_map.127.refs_2_.refs_6_ = bf16[1536,2048]{1,0:T(8,128)(2,1)S(1)} custom-call(s32[2]{0:T(128)S(1)} %pad_add_fusion.place_ref, bf16[1,1536,2048]{2,1,0:T(8,128)(2,1)S(1)} %bitcast.11, f32[1,12,2048]{2,1,0:T(8,128)S(1)} %copy.17.low_ref, f32[1,12,2048]{2,1,0:T(8,128)S(1)} %copy.18.high_ref), custom_call_target="tpu_custom_call" | custom-call | bytes 12 | tf_op jit(solution)/shard_map/pallas_call | solution.py:112
  62.9 2.3 %shard_map.128 = (bf16[128,2048]{1,0:T(8,128)(2,1)S(1)}, bf16[128,2048]{1,0:T(8,128)(2,1)S(1)}) custom-call(s32[2]{0:T(128)S(1)} %pad_add_fusion.place_ref, bf16[256,768]{1,0:T(8,128)(2,1)S(1)} %get-tuple-element.58.refs_0_, bf16[256,768]{1,0:T(8,128)(2,1)S(1)} %collective-permute-done.7.refs_1_, bf16[1536,2048]{1,0:T(8,128)(2,1)S(1)} %shard_map.127.refs_2_.refs_6_, ...), custom_call_target="tpu_custom_call" | custom-call | flops 1610 | bytes 8 | tf_op jit(solution)/shard_map/pallas_call | solution.py:112
  65.2 2.3 %shard_map.129 = (bf16[128,2048]{1,0:T(8,128)(2,1)S(1)}, bf16[128,2048]{1,0:T(8,128)(2,1)S(1)}) custom-call(s32[2]{0:T(128)S(1)} %pad_add_fusion.place_ref, bf16[256,768]{1,0:T(8,128)(2,1)S(1)} %get-tuple-element.61.refs_0_, bf16[256,768]{1,0:T(8,128)(2,1)S(1)} %collective-permute-done.17.refs_1_, bf16[1536,2048]{1,0:T(8,128)(2,1)S(1)} %shard_map.127.refs_2_.refs_6_, ...), custom_call_target="tpu_custom_call" | custom-call | flops 1610 | bytes 8 | tf_op jit(solution)/shard_map/pallas_call | solution.py:112
  68.2 1.5 collective-permute-done.18
  70.3 1.5 collective-permute-start.20
  71.9 4.2 %collective-permute-done.19 = bf16[64,1024]{1,0:T(8,128)(2,1)S(1)} collective-permute-done((bf16[64,1024]{1,0:T(8,128)(2,1)S(1)}, bf16[64,1024]{1,0:T(8,128)(2,1)S(1)}, u32[]{:S(2)}, u32[]{:S(2)}) %collective-permute-start.19) | collective-permute-done | bytes 131104 | tf_op jit(solution)/shard_map/ppermute | solution.py:17
  76.1 2.3 %collective-permute-done.20 = bf16[64,1024]{1,0:T(8,128)(2,1)S(1)} collective-permute-done((bf16[64,1024]{1,0:T(8,128)(2,1)S(1)}, bf16[64,1024]{1,0:T(8,128)(2,1)S(1)}, u32[]{:S(2)}, u32[]{:S(2)}) %collective-permute-start.20) | collective-permute-done | bytes 131104 | tf_op jit(solution)/shard_map/ppermute | solution.py:17
  79.4 1.7 collective-permute-start.24
  81.1 4.1 %collective-permute-done.22 = bf16[64,1024]{1,0:T(8,128)(2,1)S(1)} collective-permute-done((bf16[64,1024]{1,0:T(8,128)(2,1)S(1)}, bf16[64,1024]{1,0:T(8,128)(2,1)S(1)}, u32[]{:S(2)}, u32[]{:S(2)}) %collective-permute-start.22) | collective-permute-done | bytes 131104 | tf_op jit(solution)/shard_map/ppermute | solution.py:17
  85.2 1.4 collective-permute-done.24
  86.7 3.1 %collective-permute-start.23 = (bf16[32,1024]{1,0:T(8,128)(2,1)S(1)}, bf16[32,1024]{1,0:T(8,128)(2,1)S(1)}, u32[]{:S(2)}, u32[]{:S(2)}) collective-permute-start(bf16[32,1024]{1,0:T(8,128)(2,1)S(1)} %get-tuple-element.111), channel_id=1, source_target_pairs={{0,16},{2,18},{4,20},{6,22},{8,24},{10,26},{12,28},{14,30},{16,0},... | collective-permute-start | bytes 196616 | tf_op jit(solution)/shard_map/ppermute | solution.py:17
  89.8 3.9 %collective-permute-done.23 = bf16[32,1024]{1,0:T(8,128)(2,1)S(1)} collective-permute-done((bf16[32,1024]{1,0:T(8,128)(2,1)S(1)}, bf16[32,1024]{1,0:T(8,128)(2,1)S(1)}, u32[]{:S(2)}, u32[]{:S(2)}) %collective-permute-start.23) | collective-permute-done | bytes 65568 | tf_op jit(solution)/shard_map/ppermute | solution.py:17
  93.8 1.5 collective-permute-done.25
  95.9 2.5 %collective-permute-start.27 = (bf16[32,1024]{1,0:T(8,128)(2,1)S(1)}, bf16[32,1024]{1,0:T(8,128)(2,1)S(1)}, u32[]{:S(2)}, u32[]{:S(2)}) collective-permute-start(bf16[32,1024]{1,0:T(8,128)(2,1)S(1)} %get-tuple-element.108.refs_1_), channel_id=1, source_target_pairs={{0,16},{2,18},{4,20},{6,22},{8,24},{10,26},{12,28},{14,30},{16,0},... | collective-permute-start | bytes 196616 | tf_op jit(solution)/shard_map/ppermute | solution.py:17
  98.4 2.7 %collective-permute-done.26.refs_2_ = bf16[32,1024]{1,0:T(8,128)(2,1)S(1)} collective-permute-done((bf16[32,1024]{1,0:T(8,128)(2,1)S(1)}, bf16[32,1024]{1,0:T(8,128)(2,1)S(1)}, u32[]{:S(2)}, u32[]{:S(2)}) %collective-permute-start.26) | collective-permute-done | bytes 65568 | tf_op jit(solution)/shard_map/ppermute | solution.py:17
  101.1 1.4 collective-permute-done.27.refs_3_
  103.7 1.5 collective-permute-start.29
  105.2 4.4 %collective-permute-done.28.refs_1_ = bf16[64,2048]{1,0:T(8,128)(2,1)S(1)} collective-permute-done((bf16[64,2048]{1,0:T(8,128)(2,1)S(1)}, bf16[64,2048]{1,0:T(8,128)(2,1)S(1)}, u32[]{:S(2)}, u32[]{:S(2)}) %collective-permute-start.28) | collective-permute-done | bytes 262176 | tf_op jit(solution)/shard_map/ppermute | solution.py:17
  110.0 1.5 collective-permute-start.33
  111.8 2.4 %shard_map.131 = (bf16[256,2048]{1,0:T(8,128)(2,1)S(1)}, f32[256,768]{1,0:T(8,128)S(1)}, bf16[256,768]{1,0:T(8,128)(2,1)S(1)}) custom-call(s32[2]{0:T(128)S(1)} %pad_add_fusion.place_ref, bf16[64,2048]{1,0:T(8,128)(2,1)S(1)} %shard_map.130.refs_0_, bf16[64,2048]{1,0:T(8,128)(2,1)S(1)} %collective-permute-done.28.refs_1_, ...), custom_call_target="tpu_custom_call" | custom-call | flops 1610 | bytes 9 | tf_op jit(solution)/shard_map/pallas_call | solution.py:112
  114.2 1.5 collective-permute-start.32
  115.7 3.0 %collective-permute-done.33.refs_1_ = bf16[64,2048]{1,0:T(8,128)(2,1)S(1)} collective-permute-done((bf16[64,2048]{1,0:T(8,128)(2,1)S(1)}, bf16[64,2048]{1,0:T(8,128)(2,1)S(1)}, u32[]{:S(2)}, u32[]{:S(2)}) %collective-permute-start.33) | collective-permute-done | bytes 262176 | tf_op jit(solution)/shard_map/ppermute | solution.py:17
  118.8 3.9 %shard_map.133.refs_4_ = f32[2,12,2048]{2,1,0:T(8,128)S(1)} custom-call(s32[2]{0:T(128)S(1)} %pad_add_fusion.place_ref, bf16[256,768]{1,0:T(8,128)(2,1)S(1)} %get-tuple-element.58.refs_0_, bf16[256,768]{1,0:T(8,128)(2,1)S(1)} %collective-permute-done.7.refs_1_, bf16[256,2048]{1,0:T(8,128)(2,1)S(1)} %get-tuple-element.76.refs_2_, ...), custom_call_target="tpu_custom_call" | custom-call | flops 1610 | bytes 8 | tf_op jit(solution)/shard_map/pallas_call | solution.py:112
  122.7 2.9 %collective-permute-done.32.refs_0_ = bf16[256,768]{1,0:T(8,128)(2,1)S(1)} collective-permute-done((bf16[256,768]{1,0:T(8,128)(2,1)S(1)}, bf16[256,768]{1,0:T(8,128)(2,1)S(1)}, u32[]{:S(2)}, u32[]{:S(2)}) %collective-permute-start.32) | collective-permute-done | bytes 393248 | tf_op jit(solution)/shard_map/ppermute | solution.py:17
  125.6 2.4 %shard_map.134 = (bf16[256,2048]{1,0:T(8,128)(2,1)S(1)}, f32[256,768]{1,0:T(8,128)S(1)}, bf16[256,768]{1,0:T(8,128)(2,1)S(1)}) custom-call(s32[2]{0:T(128)S(1)} %pad_add_fusion.place_ref, bf16[64,2048]{1,0:T(8,128)(2,1)S(1)} %collective-permute-done.29.refs_0_, bf16[64,2048]{1,0:T(8,128)(2,1)S(1)} %collective-permute-done.33.refs_1_, ...), custom_call_target="tpu_custom_call" | custom-call | flops 1610 | bytes 9 | tf_op jit(solution)/shard_map/pallas_call | solution.py:112
  128.0 1.5 collective-permute-start.36
  129.5 4.2 %shard_map.135 = f32[2,12,2048]{2,1,0:T(8,128)S(1)} custom-call(s32[2]{0:T(128)S(1)} %pad_add_fusion.place_ref, bf16[256,768]{1,0:T(8,128)(2,1)S(1)} %get-tuple-element.61.refs_0_, bf16[256,768]{1,0:T(8,128)(2,1)S(1)} %collective-permute-done.17.refs_1_, bf16[256,2048]{1,0:T(8,128)(2,1)S(1)} %get-tuple-element.82.refs_2_, ...), custom_call_target="tpu_custom_call" | custom-call | flops 1610 | bytes 8 | tf_op jit(solution)/shard_map/pallas_call | solution.py:112
  133.7 4.0 %shard_map.132 = (bf16[256,1536]{1,0:T(8,128)(2,1)S(1)}, bf16[128,2048]{1,0:T(8,128)(2,1)S(1)}, bf16[128,2048]{1,0:T(8,128)(2,1)S(1)}, bf16[128,2048]{1,0:T(8,128)(2,1)S(1)}, bf16[128,2048]{1,0:T(8,128)(2,1)S(1)}) custom-call(s32[2]{0:T(128)S(1)} %pad_add_fusion.place_ref, f32[256,768]{1,0:T(8,128)S(1)} %get-tuple-element.71.grad_own_ref, ...), custom_call_target="tpu_custom_call" | custom-call | flops 3221 | bytes 18 | tf_op jit(solution)/shard_map/pallas_call | solution.py:112
  138.5 4.0 %shard_map.136 = (bf16[256,1536]{1,0:T(8,128)(2,1)S(1)}, bf16[128,2048]{1,0:T(8,128)(2,1)S(1)}, bf16[128,2048]{1,0:T(8,128)(2,1)S(1)}, bf16[128,2048]{1,0:T(8,128)(2,1)S(1)}, bf16[128,2048]{1,0:T(8,128)(2,1)S(1)}) custom-call(s32[2]{0:T(128)S(1)} %pad_add_fusion.place_ref, f32[256,768]{1,0:T(8,128)S(1)} %get-tuple-element.79.grad_own_ref, ...), custom_call_target="tpu_custom_call" | custom-call | flops 3221 | bytes 18 | tf_op jit(solution)/shard_map/pallas_call | solution.py:112
  143.1 1.4 collective-permute-done.39
  144.7 1.1 collective-permute-start.40
  146.2 1.5 collective-permute-start.41
  147.7 5.4 %collective-permute-done.40 = bf16[64,2048]{1,0:T(8,128)(2,1)S(1)} collective-permute-done((bf16[64,2048]{1,0:T(8,128)(2,1)S(1)}, bf16[64,2048]{1,0:T(8,128)(2,1)S(1)}, u32[]{:S(2)}, u32[]{:S(2)}) %collective-permute-start.40) | collective-permute-done | bytes 262176 | tf_op jit(solution)/shard_map/ppermute | solution.py:17
  153.3 1.2 collective-permute-done.41
  154.5 1.5 collective-permute-start.42
  156.1 1.1 collective-permute-start.45
  157.2 6.4 %shard_map.137.refs_11_ = f32[4,32,768]{2,1,0:T(8,128)} custom-call(s32[2]{0:T(128)S(1)} %pad_add_fusion.place_ref, bf16[96,4096]{1,0:T(8,128)(2,1)S(1)} %shard_map.123.refs_0_, bf16[32,4096]{1,0:T(8,128)(2,1)S(1)} %collective-permute-done.3.refs_1_, bf16[96,4096]{1,0:T(8,128)(2,1)S(1)} %collective-permute-done.5.refs_2_, ...), custom_call_target="tpu_custom_call" | custom-call | flops 3221 | bytes 18 | tf_op jit(solution)/shard_map/pallas_call | solution.py:112
  163.8 1.5 collective-permute-start.47
  165.9 1.0 collective-permute-start.46
  166.9 3.8 %shard_map.138.refs_11_ = f32[4,32,768]{2,1,0:T(8,128)} custom-call(s32[2]{0:T(128)S(1)} %pad_add_fusion.place_ref, bf16[96,4096]{1,0:T(8,128)(2,1)S(1)} %shard_map.123.refs_0_, bf16[32,4096]{1,0:T(8,128)(2,1)S(1)} %collective-permute-done.3.refs_1_, bf16[96,4096]{1,0:T(8,128)(2,1)S(1)} %collective-permute-done.5.refs_2_, ...), custom_call_target="tpu_custom_call", output_to_operand_aliasing={{}: (12, {})} | custom-call | flops 1610 | bytes 18 | tf_op jit(solution)/shard_map/pallas_call | solution.py:112
  170.7 1.1 collective-permute-done.43
  172.4 1.2 collective-permute-start.48
  173.6 0.8 copy.19
  174.4 3.8 %shard_map.139 = f32[4,32,768]{2,1,0:T(8,128)} custom-call(s32[2]{0:T(128)S(1)} %pad_add_fusion.place_ref, bf16[96,4096]{1,0:T(8,128)(2,1)S(1)} %shard_map.123.refs_0_, bf16[32,4096]{1,0:T(8,128)(2,1)S(1)} %collective-permute-done.3.refs_1_, bf16[96,4096]{1,0:T(8,128)(2,1)S(1)} %collective-permute-done.5.refs_2_, ...), custom_call_target="tpu_custom_call", output_to_operand_aliasing={{}: (12, {})} | custom-call | flops 1610 | bytes 18 | tf_op jit(solution)/shard_map/pallas_call | solution.py:112
  178.3 1.4 collective-permute-done.48
  (100 shorter events, 16.1 us)
Async XLA Ops:
  0.6 17.6 %collective-permute-start.1 = (bf16[32,4096]{1,0:T(8,128)(2,1)}, bf16[32,4096]{1,0:T(8,128)(2,1)S(1)}, u32[]{:S(2)}, u32[]{:S(2)}) collective-permute-start(bf16[32,4096]{1,0:T(8,128)(2,1)} %refs_0_.1), channel_id=1, source_target_pairs={{0,4},{2,6},{4,0},{6,2},{8,12},{10,14},{12,8},{14,10},{16,20},{18,... | collective-permute-start | bytes 786440 | tf_op jit(solution)/shard_map/ppermute | solution.py:17
  3.6 14.6 %collective-permute-start = (bf16[32,4096]{1,0:T(8,128)(2,1)}, bf16[32,4096]{1,0:T(8,128)(2,1)S(1)}, u32[]{:S(2)}, u32[]{:S(2)}) collective-permute-start(bf16[32,4096]{1,0:T(8,128)(2,1)} %refs_0_.1), channel_id=1, source_target_pairs={{0,16},{2,18},{4,20},{6,22},{8,24},{10,26},{12,28},{14,30},{16,0},... | collective-permute-start | bytes 786440 | tf_op jit(solution)/shard_map/ppermute | solution.py:17
  6.2 12.2 %collective-permute-start.2 = (bf16[32,4096]{1,0:T(8,128)(2,1)}, bf16[32,4096]{1,0:T(8,128)(2,1)S(1)}, u32[]{:S(2)}, u32[]{:S(2)}) collective-permute-start(bf16[32,4096]{1,0:T(8,128)(2,1)} %refs_0_.1), channel_id=1, source_target_pairs={{0,8},{2,10},{4,12},{6,14},{8,0},{10,2},{12,4},{14,6},{16,24},{18,... | collective-permute-start | bytes 786440 | tf_op jit(solution)/shard_map/ppermute | solution.py:17
  10.2 0.9 copy-start.1
  11.1 0.9 copy-start.2
  12.0 17.1 %copy-start = (bf16[32,4096]{1,0:T(8,128)(2,1)S(1)}, bf16[32,4096]{1,0:T(8,128)(2,1)}, u32[]{:S(2)}) copy-start(bf16[32,4096]{1,0:T(8,128)(2,1)} %refs_0_.1) | copy-start | bytes 786436
  18.4 7.1 %collective-permute-start.3 = (bf16[32,4096]{1,0:T(8,128)(2,1)S(1)}, bf16[32,4096]{1,0:T(8,128)(2,1)S(1)}, u32[]{:S(2)}, u32[]{:S(2)}) collective-permute-start(bf16[32,4096]{1,0:T(8,128)(2,1)S(1)} %collective-permute-done.refs_1_), channel_id=1, source_target_pairs={{0,8},{2,10},{4,12},{6,14},{8,0},{10,2},{12,4},{14,6},{16,24},{18,... | collective-permute-start | bytes 786440 | tf_op jit(solution)/shard_map/ppermute | solution.py:17
  19.9 9.2 %collective-permute-start.4 = (bf16[32,4096]{1,0:T(8,128)(2,1)S(1)}, bf16[32,4096]{1,0:T(8,128)(2,1)S(1)}, u32[]{:S(2)}, u32[]{:S(2)}) collective-permute-start(bf16[32,4096]{1,0:T(8,128)(2,1)S(1)} %collective-permute-done.2.refs_2_), channel_id=1, source_target_pairs={{0,4},{2,6},{4,0},{6,2},{8,12},{10,14},{12,8},{14,10},{16,20},{18,... | collective-permute-start | bytes 786440 | tf_op jit(solution)/shard_map/ppermute | solution.py:17
  20.4 12.1 %collective-permute-start.8 = (bf16[32,4096]{1,0:T(8,128)(2,1)S(1)}, bf16[32,4096]{1,0:T(8,128)(2,1)S(1)}, u32[]{:S(2)}, u32[]{:S(2)}) collective-permute-start(bf16[32,4096]{1,0:T(8,128)(2,1)S(1)} %collective-permute-done.refs_1_), channel_id=1, source_target_pairs={{0,4},{2,6},{4,0},{6,2},{8,12},{10,14},{12,8},{14,10},{16,20},{18,... | collective-permute-start | bytes 786440 | tf_op jit(solution)/shard_map/ppermute | solution.py:17
  29.1 3.4 %collective-permute-start.6 = (bf16[32,4096]{1,0:T(8,128)(2,1)S(1)}, bf16[32,4096]{1,0:T(8,128)(2,1)S(1)}, u32[]{:S(2)}, u32[]{:S(2)}) collective-permute-start(bf16[32,4096]{1,0:T(8,128)(2,1)S(1)} %collective-permute-done.3.refs_1_), channel_id=1, source_target_pairs={{0,2},{2,0},{4,6},{6,4},{8,10},{10,8},{12,14},{14,12},{16,18},{18,... | collective-permute-start | bytes 786440 | tf_op jit(solution)/shard_map/ppermute | solution.py:17
  29.7 4.1 %collective-permute-start.5 = (bf16[96,4096]{1,0:T(8,128)(2,1)S(1)}, bf16[96,4096]{1,0:T(8,128)(2,1)S(1)}, u32[]{:S(2)}, u32[]{:S(2)}) collective-permute-start(bf16[96,4096]{1,0:T(8,128)(2,1)S(1)} %shard_map.123.refs_0_), channel_id=1, source_target_pairs={{0,2},{2,0},{4,6},{6,4},{8,10},{10,8},{12,14},{14,12},{16,18},{18,... | collective-permute-start | bytes 2359304 | tf_op jit(solution)/shard_map/ppermute | solution.py:17
  33.1 27.2 %copy-start.4 = (f32[1,12,2048]{2,0,1:T(1,128)S(1)}, f32[1,12,2048]{2,0,1:T(1,128)}, u32[]{:S(2)}) copy-start(f32[1,12,2048]{2,0,1:T(1,128)} %param.19) | copy-start | bytes 294916
  33.1 27.2 %copy-start.5 = (f32[1,12,2048]{2,0,1:T(1,128)S(1)}, f32[1,12,2048]{2,0,1:T(1,128)}, u32[]{:S(2)}) copy-start(f32[1,12,2048]{2,0,1:T(1,128)} %param.18) | copy-start | bytes 294916
  33.1 27.2 %slice-start.3 = ((s8[6291456]{0:T(1024)(128)(4,1)}), s8[4194304]{0:T(1024)(128)(4,1)S(1)}, s32[]{:S(2)}) async-start(s8[6291456]{0:T(1024)(128)(4,1)} %bitcast.10), calls=%async_computation.3 | async-start | bytes 8388608
  33.1 8.8 %collective-permute-start.10 = (bf16[96,4096]{1,0:T(8,128)(2,1)S(1)}, bf16[96,4096]{1,0:T(8,128)(2,1)S(1)}, u32[]{:S(2)}, u32[]{:S(2)}) collective-permute-start(bf16[96,4096]{1,0:T(8,128)(2,1)S(1)} %shard_map.125.refs_0_.refs_4_), channel_id=1, source_target_pairs={{0,2},{2,0},{4,6},{6,4},{8,10},{10,8},{12,14},{14,12},{16,18},{18,... | collective-permute-start | bytes 2359304 | tf_op jit(solution)/shard_map/ppermute | solution.py:17
  33.2 8.7 %collective-permute-start.9 = (bf16[32,4096]{1,0:T(8,128)(2,1)S(1)}, bf16[32,4096]{1,0:T(8,128)(2,1)S(1)}, u32[]{:S(2)}, u32[]{:S(2)}) collective-permute-start(bf16[32,4096]{1,0:T(8,128)(2,1)S(1)} %collective-permute-done.3.refs_1_), channel_id=1, source_target_pairs={{0,4},{2,6},{4,0},{6,2},{8,12},{10,14},{12,8},{14,10},{16,20},{18,... | collective-permute-start | bytes 786440 | tf_op jit(solution)/shard_map/ppermute | solution.py:17
  41.9 18.4 %slice-start.4 = ((s8[6291456]{0:T(1024)(128)(4,1)}), s8[2097152]{0:T(1024)(128)(4,1)S(1)}, s32[]{:S(2)}) async-start(s8[6291456]{0:T(1024)(128)(4,1)} %bitcast.10), calls=%async_computation.4 | async-start | bytes 4194304
  41.9 1.6 collective-permute-start.11
  41.9 20.9 %collective-permute-start.7 = (bf16[256,768]{1,0:T(8,128)(2,1)S(1)}, bf16[256,768]{1,0:T(8,128)(2,1)S(1)}, u32[]{:S(2)}, u32[]{:S(2)}) collective-permute-start(bf16[256,768]{1,0:T(8,128)(2,1)S(1)} %get-tuple-element.58.refs_0_), channel_id=1, source_target_pairs={{0,1},{1,0},{2,3},{3,2},{4,5},{5,4},{6,7},{7,6},{8,9},{9,8},{10,11... | collective-permute-start | bytes 1179656 | tf_op jit(solution)/shard_map/ppermute | solution.py:17
  47.6 5.0 %collective-permute-start.12 = (bf16[32,128]{1,0:T(8,128)(2,1)S(1)}, bf16[32,128]{1,0:T(8,128)(2,1)S(1)}, u32[]{:S(2)}, u32[]{:S(2)}) collective-permute-start(bf16[32,128]{1,0:T(8,128)(2,1)S(1)} %shard_map.121), channel_id=1, source_target_pairs={{0,16},{2,18},{4,20},{6,22},{8,24},{10,26},{12,28},{14,30},{16,0},... | collective-permute-start | bytes 24584 | tf_op jit(solution)/shard_map/ppermute | solution.py:17
  50.9 14.3 %collective-permute-start.17 = (bf16[256,768]{1,0:T(8,128)(2,1)S(1)}, bf16[256,768]{1,0:T(8,128)(2,1)S(1)}, u32[]{:S(2)}, u32[]{:S(2)}) collective-permute-start(bf16[256,768]{1,0:T(8,128)(2,1)S(1)} %get-tuple-element.61.refs_0_), channel_id=1, source_target_pairs={{0,1},{1,0},{2,3},{3,2},{4,5},{5,4},{6,7},{7,6},{8,9},{9,8},{10,11... | collective-permute-start | bytes 1179656 | tf_op jit(solution)/shard_map/ppermute | solution.py:17
  52.6 3.7 %collective-permute-start.13 = (bf16[64,128]{1,0:T(8,128)(2,1)S(1)}, bf16[64,128]{1,0:T(8,128)(2,1)S(1)}, u32[]{:S(2)}, u32[]{:S(2)}) collective-permute-start(bf16[64,128]{1,0:T(8,128)(2,1)S(1)} %pad_maximum_fusion.1), channel_id=1, source_target_pairs={{0,8},{2,10},{4,12},{6,14},{8,0},{10,2},{12,4},{14,6},{16,24},{18,... | collective-permute-start | bytes 49160 | tf_op jit(solution)/shard_map/ppermute | solution.py:17
  56.3 3.9 %collective-permute-start.14 = (bf16[128,128]{1,0:T(8,128)(2,1)S(1)}, bf16[128,128]{1,0:T(8,128)(2,1)S(1)}, u32[]{:S(2)}, u32[]{:S(2)}) collective-permute-start(bf16[128,128]{1,0:T(8,128)(2,1)S(1)} %pad_maximum_fusion), channel_id=1, source_target_pairs={{0,4},{2,6},{4,0},{6,2},{8,12},{10,14},{12,8},{14,10},{16,20},{18,... | collective-permute-start | bytes 98312 | tf_op jit(solution)/shard_map/ppermute | solution.py:17
  60.2 2.6 %collective-permute-start.15 = (bf16[256,128]{1,0:T(8,128)(2,1)S(1)}, bf16[256,128]{1,0:T(8,128)(2,1)S(1)}, u32[]{:S(2)}, u32[]{:S(2)}) collective-permute-start(bf16[256,128]{1,0:T(8,128)(2,1)S(1)} %constant_dynamic-update-slice_fusion.refs_3_.refs_4_), channel_id=1, source_target_pairs={{0,2},{2,0},{4,6},{6,4},{8,10},{10,8},{12,14},{14,12},{16,18},{18,... | collective-permute-start | bytes 196616 | tf_op jit(solution)/shard_map/ppermute | solution.py:17
  60.4 34.9 %copy-start.3 = (bf16[32,2048]{1,0:T(8,128)(2,1)S(1)}, bf16[32,2048]{1,0:T(8,128)(2,1)}, u32[]{:S(2)}) copy-start(bf16[32,2048]{1,0:T(8,128)(2,1)} %param.11) | copy-start | bytes 393220
  67.5 2.1 %collective-permute-start.18 = (bf16[128,2048]{1,0:T(8,128)(2,1)S(1)}, bf16[128,2048]{1,0:T(8,128)(2,1)S(1)}, u32[]{:S(2)}, u32[]{:S(2)}) collective-permute-start(bf16[128,2048]{1,0:T(8,128)(2,1)S(1)} %get-tuple-element.68), channel_id=1, source_target_pairs={{0,2},{2,0},{4,6},{6,4},{8,10},{10,8},{12,14},{14,12},{16,18},{18,... | collective-permute-start | bytes 1572872 | tf_op jit(solution)/shard_map/ppermute | solution.py:17
  68.1 10.8 %collective-permute-start.16 = (bf16[128,2048]{1,0:T(8,128)(2,1)S(1)}, bf16[128,2048]{1,0:T(8,128)(2,1)S(1)}, u32[]{:S(2)}, u32[]{:S(2)}) collective-permute-start(bf16[128,2048]{1,0:T(8,128)(2,1)S(1)} %get-tuple-element.65), channel_id=1, source_target_pairs={{0,2},{2,0},{4,6},{6,4},{8,10},{10,8},{12,14},{14,12},{16,18},{18,... | collective-permute-start | bytes 1572872 | tf_op jit(solution)/shard_map/ppermute | solution.py:17
  69.7 6.4 %collective-permute-start.19 = (bf16[64,1024]{1,0:T(8,128)(2,1)S(1)}, bf16[64,1024]{1,0:T(8,128)(2,1)S(1)}, u32[]{:S(2)}, u32[]{:S(2)}) collective-permute-start(bf16[64,1024]{1,0:T(8,128)(2,1)S(1)} %get-tuple-element.121), channel_id=1, source_target_pairs={{0,4},{2,6},{4,0},{6,2},{8,12},{10,14},{12,8},{14,10},{16,20},{18,... | collective-permute-start | bytes 393224 | tf_op jit(solution)/shard_map/ppermute | solution.py:17
  70.3 8.0 %collective-permute-start.20 = (bf16[64,1024]{1,0:T(8,128)(2,1)S(1)}, bf16[64,1024]{1,0:T(8,128)(2,1)S(1)}, u32[]{:S(2)}, u32[]{:S(2)}) collective-permute-start(bf16[64,1024]{1,0:T(8,128)(2,1)S(1)} %get-tuple-element.120), channel_id=1, source_target_pairs={{0,4},{2,6},{4,0},{6,2},{8,12},{10,14},{12,8},{14,10},{16,20},{18,... | collective-permute-start | bytes 393224 | tf_op jit(solution)/shard_map/ppermute | solution.py:17
  78.4 8.2 %collective-permute-start.21 = (bf16[64,2048]{1,0:T(8,128)(2,1)S(1)}, bf16[64,2048]{1,0:T(8,128)(2,1)S(1)}, u32[]{:S(2)}, u32[]{:S(2)}) collective-permute-start(bf16[64,2048]{1,0:T(8,128)(2,1)S(1)} %add_convert_fusion.7), channel_id=1, source_target_pairs={{0,4},{2,6},{4,0},{6,2},{8,12},{10,14},{12,8},{14,10},{16,20},{18,... | collective-permute-start | bytes 786440 | tf_op jit(solution)/shard_map/ppermute | solution.py:17
  79.0 6.1 %collective-permute-start.22 = (bf16[64,1024]{1,0:T(8,128)(2,1)S(1)}, bf16[64,1024]{1,0:T(8,128)(2,1)S(1)}, u32[]{:S(2)}, u32[]{:S(2)}) collective-permute-start(bf16[64,1024]{1,0:T(8,128)(2,1)S(1)} %get-tuple-element.119), channel_id=1, source_target_pairs={{0,8},{2,10},{4,12},{6,14},{8,0},{10,2},{12,4},{14,6},{16,24},{18,... | collective-permute-start | bytes 393224 | tf_op jit(solution)/shard_map/ppermute | solution.py:17
  79.4 7.2 %collective-permute-start.24 = (bf16[64,1024]{1,0:T(8,128)(2,1)S(1)}, bf16[64,1024]{1,0:T(8,128)(2,1)S(1)}, u32[]{:S(2)}, u32[]{:S(2)}) collective-permute-start(bf16[64,1024]{1,0:T(8,128)(2,1)S(1)} %get-tuple-element.118), channel_id=1, source_target_pairs={{0,8},{2,10},{4,12},{6,14},{8,0},{10,2},{12,4},{14,6},{16,24},{18,... | collective-permute-start | bytes 393224 | tf_op jit(solution)/shard_map/ppermute | solution.py:17
  86.7 7.1 %collective-permute-start.23 = (bf16[32,1024]{1,0:T(8,128)(2,1)S(1)}, bf16[32,1024]{1,0:T(8,128)(2,1)S(1)}, u32[]{:S(2)}, u32[]{:S(2)}) collective-permute-start(bf16[32,1024]{1,0:T(8,128)(2,1)S(1)} %get-tuple-element.111), channel_id=1, source_target_pairs={{0,16},{2,18},{4,20},{6,22},{8,24},{10,26},{12,28},{14,30},{16,0},... | collective-permute-start | bytes 196616 | tf_op jit(solution)/shard_map/ppermute | solution.py:17
  89.8 5.5 %collective-permute-start.25 = (bf16[32,1024]{1,0:T(8,128)(2,1)S(1)}, bf16[32,1024]{1,0:T(8,128)(2,1)S(1)}, u32[]{:S(2)}, u32[]{:S(2)}) collective-permute-start(bf16[32,1024]{1,0:T(8,128)(2,1)S(1)} %get-tuple-element.110), channel_id=1, source_target_pairs={{0,16},{2,18},{4,20},{6,22},{8,24},{10,26},{12,28},{14,30},{16,0},... | collective-permute-start | bytes 196616 | tf_op jit(solution)/shard_map/ppermute | solution.py:17
  95.4 5.7 %collective-permute-start.26 = (bf16[32,1024]{1,0:T(8,128)(2,1)S(1)}, bf16[32,1024]{1,0:T(8,128)(2,1)S(1)}, u32[]{:S(2)}, u32[]{:S(2)}) collective-permute-start(bf16[32,1024]{1,0:T(8,128)(2,1)S(1)} %get-tuple-element.109.refs_0_), channel_id=1, source_target_pairs={{0,16},{2,18},{4,20},{6,22},{8,24},{10,26},{12,28},{14,30},{16,0},... | collective-permute-start | bytes 196616 | tf_op jit(solution)/shard_map/ppermute | solution.py:17
  95.9 6.6 %collective-permute-start.27 = (bf16[32,1024]{1,0:T(8,128)(2,1)S(1)}, bf16[32,1024]{1,0:T(8,128)(2,1)S(1)}, u32[]{:S(2)}, u32[]{:S(2)}) collective-permute-start(bf16[32,1024]{1,0:T(8,128)(2,1)S(1)} %get-tuple-element.108.refs_1_), channel_id=1, source_target_pairs={{0,16},{2,18},{4,20},{6,22},{8,24},{10,26},{12,28},{14,30},{16,0},... | collective-permute-start | bytes 196616 | tf_op jit(solution)/shard_map/ppermute | solution.py:17
  103.0 6.5 %collective-permute-start.28 = (bf16[64,2048]{1,0:T(8,128)(2,1)S(1)}, bf16[64,2048]{1,0:T(8,128)(2,1)S(1)}, u32[]{:S(2)}, u32[]{:S(2)}) collective-permute-start(bf16[64,2048]{1,0:T(8,128)(2,1)S(1)} %shard_map.130.refs_0_), channel_id=1, source_target_pairs={{0,8},{2,10},{4,12},{6,14},{8,0},{10,2},{12,4},{14,6},{16,24},{18,... | collective-permute-start | bytes 786440 | tf_op jit(solution)/shard_map/ppermute | solution.py:17
  103.7 6.4 %collective-permute-start.29 = (bf16[64,2048]{1,0:T(8,128)(2,1)S(1)}, bf16[64,2048]{1,0:T(8,128)(2,1)S(1)}, u32[]{:S(2)}, u32[]{:S(2)}) collective-permute-start(bf16[64,2048]{1,0:T(8,128)(2,1)S(1)} %shard_map.130.refs_0_), channel_id=1, source_target_pairs={{0,4},{2,6},{4,0},{6,2},{8,12},{10,14},{12,8},{14,10},{16,20},{18,... | collective-permute-start | bytes 786440 | tf_op jit(solution)/shard_map/ppermute | solution.py:17
  105.2 4.9 %collective-permute-start.30 = (bf16[64,2048]{1,0:T(8,128)(2,1)S(1)}, bf16[64,2048]{1,0:T(8,128)(2,1)S(1)}, u32[]{:S(2)}, u32[]{:S(2)}) collective-permute-start(bf16[64,2048]{1,0:T(8,128)(2,1)S(1)} %shard_map.130.refs_0_), channel_id=1, source_target_pairs={{0,2},{2,0},{4,6},{6,4},{8,10},{10,8},{12,14},{14,12},{16,18},{18,... | collective-permute-start | bytes 786440 | tf_op jit(solution)/shard_map/ppermute | solution.py:17
  110.0 1.7 collective-permute-start.31
  110.0 8.7 %collective-permute-start.33 = (bf16[64,2048]{1,0:T(8,128)(2,1)S(1)}, bf16[64,2048]{1,0:T(8,128)(2,1)S(1)}, u32[]{:S(2)}, u32[]{:S(2)}) collective-permute-start(bf16[64,2048]{1,0:T(8,128)(2,1)S(1)} %collective-permute-done.28.refs_1_), channel_id=1, source_target_pairs={{0,4},{2,6},{4,0},{6,2},{8,12},{10,14},{12,8},{14,10},{16,20},{18,... | collective-permute-start | bytes 786440 | tf_op jit(solution)/shard_map/ppermute | solution.py:17
  111.5 7.2 %collective-permute-start.34 = (bf16[64,2048]{1,0:T(8,128)(2,1)S(1)}, bf16[64,2048]{1,0:T(8,128)(2,1)S(1)}, u32[]{:S(2)}, u32[]{:S(2)}) collective-permute-start(bf16[64,2048]{1,0:T(8,128)(2,1)S(1)} %collective-permute-done.29.refs_0_), channel_id=1, source_target_pairs={{0,2},{2,0},{4,6},{6,4},{8,10},{10,8},{12,14},{14,12},{16,18},{18,... | collective-permute-start | bytes 786440 | tf_op jit(solution)/shard_map/ppermute | solution.py:17
  114.2 11.4 %collective-permute-start.32 = (bf16[256,768]{1,0:T(8,128)(2,1)S(1)}, bf16[256,768]{1,0:T(8,128)(2,1)S(1)}, u32[]{:S(2)}, u32[]{:S(2)}) collective-permute-start(bf16[256,768]{1,0:T(8,128)(2,1)S(1)} %get-tuple-element.72), channel_id=1, source_target_pairs={{0,1},{1,0},{2,3},{3,2},{4,5},{5,4},{6,7},{7,6},{8,9},{9,8},{10,11... | collective-permute-start | bytes 1179656 | tf_op jit(solution)/shard_map/ppermute | solution.py:17
  118.8 3.9 %collective-permute-start.35 = (bf16[64,2048]{1,0:T(8,128)(2,1)S(1)}, bf16[64,2048]{1,0:T(8,128)(2,1)S(1)}, u32[]{:S(2)}, u32[]{:S(2)}) collective-permute-start(bf16[64,2048]{1,0:T(8,128)(2,1)S(1)} %collective-permute-done.33.refs_1_), channel_id=1, source_target_pairs={{0,2},{2,0},{4,6},{6,4},{8,10},{10,8},{12,14},{14,12},{16,18},{18,... | collective-permute-start | bytes 786440 | tf_op jit(solution)/shard_map/ppermute | solution.py:17
  128.0 10.6 %collective-permute-start.36 = (bf16[256,768]{1,0:T(8,128)(2,1)S(1)}, bf16[256,768]{1,0:T(8,128)(2,1)S(1)}, u32[]{:S(2)}, u32[]{:S(2)}) collective-permute-start(bf16[256,768]{1,0:T(8,128)(2,1)S(1)} %get-tuple-element.80), channel_id=1, source_target_pairs={{0,1},{1,0},{2,3},{3,2},{4,5},{5,4},{6,7},{7,6},{8,9},{9,8},{10,11... | collective-permute-start | bytes 1179656 | tf_op jit(solution)/shard_map/ppermute | solution.py:17
  133.7 23.5 %slice-start = ((s8[12582912]{0:T(1024)(128)(4,1)}), s8[4194304]{0:T(1024)(128)(4,1)S(1)}, s32[]{:S(2)}) async-start(s8[12582912]{0:T(1024)(128)(4,1)} %bitcast.8), calls=%async_computation | async-start | bytes 8388608
  133.7 23.5 %slice-start.1 = ((s8[12582912]{0:T(1024)(128)(4,1)}), s8[4194304]{0:T(1024)(128)(4,1)S(1)}, s32[]{:S(2)}) async-start(s8[12582912]{0:T(1024)(128)(4,1)} %bitcast.8), calls=%async_computation.1 | async-start | bytes 8388608
  138.5 18.7 %slice-start.2 = ((s8[12582912]{0:T(1024)(128)(4,1)}), s8[4194304]{0:T(1024)(128)(4,1)S(1)}, s32[]{:S(2)}) async-start(s8[12582912]{0:T(1024)(128)(4,1)} %bitcast.8), calls=%async_computation.2 | async-start | bytes 8388608
  142.6 2.0 %collective-permute-start.39 = (bf16[128,2048]{1,0:T(8,128)(2,1)S(1)}, bf16[128,2048]{1,0:T(8,128)(2,1)S(1)}, u32[]{:S(2)}, u32[]{:S(2)}) collective-permute-start(bf16[128,2048]{1,0:T(8,128)(2,1)S(1)} %get-tuple-element.95), channel_id=1, source_target_pairs={{0,2},{2,0},{4,6},{6,4},{8,10},{10,8},{12,14},{14,12},{16,18},{18,... | collective-permute-start | bytes 1572872 | tf_op jit(solution)/shard_map/ppermute | solution.py:17
  142.7 5.1 %collective-permute-start.38 = (bf16[128,2048]{1,0:T(8,128)(2,1)S(1)}, bf16[128,2048]{1,0:T(8,128)(2,1)S(1)}, u32[]{:S(2)}, u32[]{:S(2)}) collective-permute-start(bf16[128,2048]{1,0:T(8,128)(2,1)S(1)} %get-tuple-element.93), channel_id=1, source_target_pairs={{0,2},{2,0},{4,6},{6,4},{8,10},{10,8},{12,14},{14,12},{16,18},{18,... | collective-permute-start | bytes 1572872 | tf_op jit(solution)/shard_map/ppermute | solution.py:17
  144.7 8.4 %collective-permute-start.40 = (bf16[64,2048]{1,0:T(8,128)(2,1)S(1)}, bf16[64,2048]{1,0:T(8,128)(2,1)S(1)}, u32[]{:S(2)}, u32[]{:S(2)}) collective-permute-start(bf16[64,2048]{1,0:T(8,128)(2,1)S(1)} %get-tuple-element.114), channel_id=1, source_target_pairs={{0,4},{2,6},{4,0},{6,2},{8,12},{10,14},{12,8},{14,10},{16,20},{18,... | collective-permute-start | bytes 786440 | tf_op jit(solution)/shard_map/ppermute | solution.py:17
  145.7 10.2 %collective-permute-start.44 = (bf16[128,2048]{1,0:T(8,128)(2,1)S(1)}, bf16[128,2048]{1,0:T(8,128)(2,1)S(1)}, u32[]{:S(2)}, u32[]{:S(2)}) collective-permute-start(bf16[128,2048]{1,0:T(8,128)(2,1)S(1)} %get-tuple-element.99), channel_id=1, source_target_pairs={{0,2},{2,0},{4,6},{6,4},{8,10},{10,8},{12,14},{14,12},{16,18},{18,... | collective-permute-start | bytes 1572872 | tf_op jit(solution)/shard_map/ppermute | solution.py:17
  145.7 17.9 %collective-permute-start.37 = (bf16[128,2048]{1,0:T(8,128)(2,1)S(1)}, bf16[128,2048]{1,0:T(8,128)(2,1)S(1)}, u32[]{:S(2)}, u32[]{:S(2)}) collective-permute-start(bf16[128,2048]{1,0:T(8,128)(2,1)S(1)} %get-tuple-element.89), channel_id=1, source_target_pairs={{0,2},{2,0},{4,6},{6,4},{8,10},{10,8},{12,14},{14,12},{16,18},{18,... | collective-permute-start | bytes 1572872 | tf_op jit(solution)/shard_map/ppermute | solution.py:17
  146.2 8.2 %collective-permute-start.41 = (bf16[64,2048]{1,0:T(8,128)(2,1)S(1)}, bf16[64,2048]{1,0:T(8,128)(2,1)S(1)}, u32[]{:S(2)}, u32[]{:S(2)}) collective-permute-start(bf16[64,2048]{1,0:T(8,128)(2,1)S(1)} %get-tuple-element.115), channel_id=1, source_target_pairs={{0,1},{1,0},{2,3},{3,2},{4,5},{5,4},{6,7},{7,6},{8,9},{9,8},{10,11... | collective-permute-start | bytes 786440 | tf_op jit(solution)/shard_map/ppermute | solution.py:17
  154.5 9.2 %collective-permute-start.42 = (bf16[64,2048]{1,0:T(8,128)(2,1)S(1)}, bf16[64,2048]{1,0:T(8,128)(2,1)S(1)}, u32[]{:S(2)}, u32[]{:S(2)}) collective-permute-start(bf16[64,2048]{1,0:T(8,128)(2,1)S(1)} %get-tuple-element.96), channel_id=1, source_target_pairs={{0,1},{1,0},{2,3},{3,2},{4,5},{5,4},{6,7},{7,6},{8,9},{9,8},{10,11... | collective-permute-start | bytes 786440 | tf_op jit(solution)/shard_map/ppermute | solution.py:17
  156.1 7.5 %collective-permute-start.45 = (bf16[64,2048]{1,0:T(8,128)(2,1)S(1)}, bf16[64,2048]{1,0:T(8,128)(2,1)S(1)}, u32[]{:S(2)}, u32[]{:S(2)}) collective-permute-start(bf16[64,2048]{1,0:T(8,128)(2,1)S(1)} %get-tuple-element.116), channel_id=1, source_target_pairs={{0,4},{2,6},{4,0},{6,2},{8,12},{10,14},{12,8},{14,10},{16,20},{18,... | collective-permute-start | bytes 786440 | tf_op jit(solution)/shard_map/ppermute | solution.py:17
  163.8 6.9 %collective-permute-start.47 = (bf16[64,2048]{1,0:T(8,128)(2,1)S(1)}, bf16[64,2048]{1,0:T(8,128)(2,1)S(1)}, u32[]{:S(2)}, u32[]{:S(2)}) collective-permute-start(bf16[64,2048]{1,0:T(8,128)(2,1)S(1)} %add_convert_fusion), channel_id=1, source_target_pairs={{0,8},{2,10},{4,12},{6,14},{8,0},{10,2},{12,4},{14,6},{16,24},{18,... | collective-permute-start | bytes 786440 | tf_op jit(solution)/shard_map/ppermute | solution.py:17
  165.3 6.5 %collective-permute-start.43 = (bf16[64,2048]{1,0:T(8,128)(2,1)S(1)}, bf16[64,2048]{1,0:T(8,128)(2,1)S(1)}, u32[]{:S(2)}, u32[]{:S(2)}) collective-permute-start(bf16[64,2048]{1,0:T(8,128)(2,1)S(1)} %get-tuple-element.97), channel_id=1, source_target_pairs={{0,1},{1,0},{2,3},{3,2},{4,5},{5,4},{6,7},{7,6},{8,9},{9,8},{10,11... | collective-permute-start | bytes 786440 | tf_op jit(solution)/shard_map/ppermute | solution.py:17
  165.9 6.4 %collective-permute-start.46 = (bf16[64,2048]{1,0:T(8,128)(2,1)S(1)}, bf16[64,2048]{1,0:T(8,128)(2,1)S(1)}, u32[]{:S(2)}, u32[]{:S(2)}) collective-permute-start(bf16[64,2048]{1,0:T(8,128)(2,1)S(1)} %get-tuple-element.100), channel_id=1, source_target_pairs={{0,4},{2,6},{4,0},{6,2},{8,12},{10,14},{12,8},{14,10},{16,20},{18,... | collective-permute-start | bytes 786440 | tf_op jit(solution)/shard_map/ppermute | solution.py:17
  172.4 7.3 %collective-permute-start.48 = (bf16[32,2048]{1,0:T(8,128)(2,1)S(1)}, bf16[32,2048]{1,0:T(8,128)(2,1)S(1)}, u32[]{:S(2)}, u32[]{:S(2)}) collective-permute-start(bf16[32,2048]{1,0:T(8,128)(2,1)S(1)} %add_convert_fusion.9), channel_id=1, source_target_pairs={{0,16},{2,18},{4,20},{6,22},{8,24},{10,26},{12,28},{14,30},{16,0},... | collective-permute-start | bytes 393224 | tf_op jit(solution)/shard_map/ppermute | solution.py:17

commit v11 on v10

--- a/solution.py
+++ b/solution.py
@@ -277,15 +277,25 @@
     return jnp.concatenate([ref[...] for ref in refs], axis=0)
 
 
+def rows_of(array, start=0, stop=None):
+    return (array, start, array.shape[0] if stop is None else stop)
+
+
+def stacked_rows(refs, pieces):
+    return jnp.concatenate(
+        [ref[start:stop, :] for ref, (_, start, stop) in zip(refs, pieces)], axis=0
+    )
+
+
 def forward_in(place, x, w_in):
-    rows = height_of(x)
+    rows = sum(stop - start for _, start, stop in x)
     width, both = w_in.shape
     hidden = both // 2
     size = step_of(hidden)
 
     def kernel(place_ref, *refs):
         w_ref, hidden_ref, slope_ref, act_ref = refs[len(x) :]
-        left = stacked(refs[: len(x)])
+        left = stacked_rows(refs[: len(x)], x)
 
         def body(start):
             gate = dot(left, w_ref[:, pl.ds(start, size)])
@@ -301,7 +311,7 @@
     shape = (rows, hidden)
     return resident(
         kernel,
-        [*x, w_in],
+        [*[array for array, _, _ in x], w_in],
         [(shape, BF16), (shape, F32), (shape, F32)],
         place,
         flops=2 * rows * width * both,
@@ -485,7 +495,7 @@
     per = next(p for p in (4, 2, 1) if held % p == 0)
     rows = per * size
     blocks = held // per
-    flat = [array for parts in x for array in parts]
+    flat = [piece for parts in x for piece in parts]
     chunks = len(grads)
     tokens, both = grads[0].shape
     wide = 256 if hidden % 256 == 0 else hidden
@@ -514,14 +524,14 @@
             out_ref[2 * k, pl.ds(base + g, 1), cols] = low
             out_ref[2 * k + 1, pl.ds(base + g, 1), cols] = high
 
-        left = jnp.concatenate([ref[...] for ref in x_refs], axis=0)
+        left = stacked_rows(x_refs, flat)
         range_tile(left, right_ref, size, wide, codes_at, store)
 
     shape = (4, groups, hidden)
     return call(
         kernel,
         (blocks,),
-        [(a, (a.shape[0], rows), lambda i, p: (0, part * blocks + i)) for a in flat]
+        [(a, (a.shape[0], rows), lambda i, p: (0, part * blocks + i)) for a, _, _ in flat]
         + [(grad, pltpu.VMEM, None) for grad in grads]
         + [(codes, (1, 2, rows, hidden), lambda i, p: (0, 0, part * blocks + i, 0))],
         [(shape, F32, (4, held, hidden), lambda i, p: (0, part, 0))],
@@ -576,28 +586,38 @@
     across_near = swap(near_own, "expert", 2)
     far = tie(far, w_in, across_own)
     near_far = swap(far, "expert", 4)
-    across_far = swap(far, "expert", 2)
-    near_far = tie(near_far, across_near)
-    first = pack(place, [[tokens], [far], [near_own]])
-    first_other = swap(first, "expert", 1)
-    across_last = swap(near_far, "expert", 2)
+    terms = join(gather_far(terms))
+    near_far = tie(near_far, across_near, terms)
+    last = pack(place, [[far], [near_far]])
+    across_last = swap(last, "expert", 2)
+    first = pack(place, [[tokens], [tie(far, terms)], [near_own]])
     near_other = swap(near_far, "expert", 1)
-    x = [[first, near_far, first_other, near_other]]
+    x = [[rows_of(part) for part in (first, near_far, swap(first, "expert", 1), near_other)]]
 
     hidden, slope, act = [], [], []
     for c in chunks:
         if c == 1:
-            second = pack(place, [[across_own], [tie(across_far, near_other)], [across_near]])
+            second = pack(place, [[across_own], [tie(across_near, near_other)]])
             second_other = swap(second, "expert", 1)
-            across_last = tie(across_last, hidden[0][0], second_other)
-            x.append([second, across_last, second_other, swap(across_last, "expert", 1)])
+            across_last = tie(across_last, w_down, second_other)
+            last_other = swap(across_last, "expert", 1)
+            size = tokens.shape[0]
+            x.append([])
+            for early, late in ((second, across_last), (second_other, last_other)):
+                count = late.shape[0] // 2
+                x[1] += [
+                    rows_of(early, 0, size),
+                    rows_of(late, 0, count),
+                    rows_of(early, size),
+                    rows_of(late, count),
+                ]
         own, chunk_slope, chunk_act = forward_in(place, x[c], w_in)
-        if c == 1:
+        if c == 0:
             w_down = dequant(place, down_codes, tie(down_low, own), down_high, halves)
         hidden.append([own] + [swap(own, "half", d) for d in parts if d])
         slope.append(chunk_slope)
         act.append(chunk_act)
-    terms = join(gather_far(tie(terms, hidden[1][0])))
+    terms = tie(terms, hidden[1][0])
     for distance in (4, 2):
         terms = jnp.concatenate([terms, swap(terms, "expert", distance)], axis=0)
     terms = (terms, swap(terms, "expert", 1))

time: 181 us -> 176 us (0.972)
  waiting for transfers between devices: 66.1 us -> 58.6 us
  starting transfers between devices: 48 us -> 50.1 us
    ppermute x49 -> x48, waiting for transfers between devices: 66.1 us -> 58.6 us  [swap(): return lax.ppermute(array, axis, [(i, i ^ distance) for i in range(size)])]
    ppermute x49 -> x48, starting transfers between devices: 48 us -> 50.1 us  [swap(): return lax.ppermute(array, axis, [(i, i ^ distance) for i in range(size)])]
    pallas_call x19 -> x20, Pallas kernels: 58.9 us -> 60.1 us  [call(): pl.pallas_call(kernel, grid_spec=pltpu.PrefetchScalarGridSpec(num_scalar_...]
    unnamed x29 -> x28, local copies, waits for them, and re-layouts: 4.3 us -> 4.29 us
  transfers between devices with their start and end apart: 49 -> 48, of which waited for: 29 -> 30; matrix products, arithmetic and copies ran while one was open for 2% -> 2% of each run, Pallas kernels for 28% -> 29%
where the time goes in v11:
time: 176 us
  Pallas kernels  60.1 us (34%)
  waiting for transfers between devices  58.6 us (33%)
  starting transfers between devices  50.1 us (28%)
  local copies, waits for them, and re-layouts  4.34 us (2%)
  other arithmetic  1.99 us (1%)
    pallas_call x20, Pallas kernels, call(): pl.pallas_call(kernel, grid_spec=pltpu.PrefetchScalarGridSpec(num_scalar_...  60.1 us
    ppermute x48, waiting for transfers between devices, swap(): return lax.ppermute(array, axis, [(i, i ^ distance) for i in range(size)])  58.6 us
    ppermute x48, starting transfers between devices, swap(): return lax.ppermute(array, axis, [(i, i ^ distance) for i in range(size)])  50.1 us
    unnamed x28, local copies, waits for them, and re-layouts  4.29 us
  transfers between devices with their start and end apart: 48, of which 30 were waited for; matrix products, arithmetic and copies ran while one was open for 2% of the time, Pallas kernels for 29%

profile of v11, /device:TPU:0, one launch (start us, length us, event | category | flops | bytes accessed | tf_op | source)
XLA Modules:
  0.0 176.2 jit_solution(12803318884282149008)
XLA Ops:
  0.6 3.0 %collective-permute-start.1 = (bf16[32,4096]{1,0:T(8,128)(2,1)}, bf16[32,4096]{1,0:T(8,128)(2,1)S(1)}, u32[]{:S(2)}, u32[]{:S(2)}) collective-permute-start(bf16[32,4096]{1,0:T(8,128)(2,1)} %refs_0_.1), channel_id=1, source_target_pairs={{0,4},{2,6},{4,0},{6,2},{8,12},{10,14},{12,8},{14,10},{16,20},{18,... | collective-permute-start | bytes 786440 | tf_op jit(solution)/shard_map/ppermute | solution.py:17
  3.6 2.6 %collective-permute-start = (bf16[32,4096]{1,0:T(8,128)(2,1)}, bf16[32,4096]{1,0:T(8,128)(2,1)S(1)}, u32[]{:S(2)}, u32[]{:S(2)}) collective-permute-start(bf16[32,4096]{1,0:T(8,128)(2,1)} %refs_0_.1), channel_id=1, source_target_pairs={{0,16},{2,18},{4,20},{6,22},{8,24},{10,26},{12,28},{14,30},{16,0},... | collective-permute-start | bytes 786440 | tf_op jit(solution)/shard_map/ppermute | solution.py:17
  6.2 1.6 collective-permute-start.3
  10.2 0.9 copy-done.1
  11.1 0.9 copy-done.2
  12.0 6.2 %shard_map.122.refs_4_.refs_8_.refs_3_ = bf16[4096,1536]{1,0:T(8,128)(2,1)S(1)} custom-call(s32[2]{0:T(128)S(1)} %pad_add_fusion.place_ref, bf16[2,4096,768]{2,1,0:T(8,128)(2,1)} %bitcast.7, f32[2,32,768]{2,1,0:T(8,128)S(1)} %bitcast.13, f32[2,32,768]{2,1,0:T(8,128)S(1)} %bitcast.14), custom_call_target="tpu_custom_call" | custom-call | bytes 25 | tf_op jit(solution)/shard_map/pallas_call | solution.py:112
  18.4 1.4 collective-permute-start.4
  20.4 2.3 %collective-permute-start.2 = (bf16[32,128]{1,0:T(8,128)(2,1)S(1)}, bf16[32,128]{1,0:T(8,128)(2,1)S(1)}, u32[]{:S(2)}, u32[]{:S(2)}) collective-permute-start(bf16[32,128]{1,0:T(8,128)(2,1)S(1)} %shard_map.121), channel_id=1, source_target_pairs={{0,16},{2,18},{4,20},{6,22},{8,24},{10,26},{12,28},{14,30},{16,0},... | collective-permute-start | bytes 24584 | tf_op jit(solution)/shard_map/ppermute | solution.py:17
  22.7 2.3 %collective-permute-done.2 = bf16[32,128]{1,0:T(8,128)(2,1)S(1)} collective-permute-done((bf16[32,128]{1,0:T(8,128)(2,1)S(1)}, bf16[32,128]{1,0:T(8,128)(2,1)S(1)}, u32[]{:S(2)}, u32[]{:S(2)}) %collective-permute-start.2) | collective-permute-done | bytes 8224 | tf_op jit(solution)/shard_map/ppermute | solution.py:17
  25.7 1.1 collective-permute-done.5.refs_1_
  27.4 0.8 collective-permute-start.9
  29.2 4.1 %shard_map.124 = (bf16[256,768]{1,0:T(8,128)(2,1)S(1)}, f32[256,768]{1,0:T(8,128)S(1)}, f32[256,768]{1,0:T(8,128)S(1)}) custom-call(s32[2]{0:T(128)S(1)} %pad_add_fusion.place_ref, bf16[96,4096]{1,0:T(8,128)(2,1)S(1)} %shard_map.123.refs_0_, bf16[32,4096]{1,0:T(8,128)(2,1)S(1)} %collective-permute-done.4.refs_1_, ...), custom_call_target="tpu_custom_call" | custom-call | flops 3221 | bytes 16 | tf_op jit(solution)/shard_map/pallas_call | solution.py:112
  33.4 2.4 %shard_map.125.refs_2_.refs_6_ = bf16[1536,2048]{1,0:T(8,128)(2,1)S(1)} custom-call(s32[2]{0:T(128)S(1)} %pad_add_fusion.place_ref, bf16[1,1536,2048]{2,1,0:T(8,128)(2,1)S(1)} %bitcast.11, f32[1,12,2048]{2,1,0:T(8,128)S(1)} %copy.17.low_ref, f32[1,12,2048]{2,1,0:T(8,128)S(1)} %copy.18.high_ref), custom_call_target="tpu_custom_call" | custom-call | bytes 12 | tf_op jit(solution)/shard_map/pallas_call | solution.py:112
  35.9 6.0 %collective-permute-done.9.refs_1_.refs_3_.refs_5_.refs_7_ = bf16[64,4096]{1,0:T(8,128)(2,1)S(1)} collective-permute-done((bf16[64,4096]{1,0:T(8,128)(2,1)S(1)}, bf16[64,4096]{1,0:T(8,128)(2,1)S(1)}, u32[]{:S(2)}, u32[]{:S(2)}) %collective-permute-start.9) | collective-permute-done | bytes 524320 | tf_op jit(solution)/shard_map/ppermute | solution.py:17
  41.8 1.5 collective-permute-start.8
  43.8 4.1 %shard_map.128 = (bf16[256,768]{1,0:T(8,128)(2,1)S(1)}, f32[256,768]{1,0:T(8,128)S(1)}, f32[256,768]{1,0:T(8,128)S(1)}) custom-call(s32[2]{0:T(128)S(1)} %pad_add_fusion.place_ref, bf16[64,4096]{1,0:T(8,128)(2,1)S(1)} %shard_map.126.refs_0_.refs_2_.refs_4_.refs_6_, bf16[64,4096]{1,0:T(8,128)(2,1)S(1)} %collective-permute-done.9.refs_1_.refs_3_.refs_5_.refs_7_, ...), custom_call_target="tpu_custom_call" | custom-call | flops 3221 | bytes 18 | tf_op jit(solution)/shard_map/pallas_call | solution.py:112
  47.8 2.8 %collective-permute-start.12 = (bf16[64,128]{1,0:T(8,128)(2,1)S(1)}, bf16[64,128]{1,0:T(8,128)(2,1)S(1)}, u32[]{:S(2)}, u32[]{:S(2)}) collective-permute-start(bf16[64,128]{1,0:T(8,128)(2,1)S(1)} %pad_maximum_fusion.1), channel_id=1, source_target_pairs={{0,8},{2,10},{4,12},{6,14},{8,0},{10,2},{12,4},{14,6},{16,24},{18,... | collective-permute-start | bytes 49160 | tf_op jit(solution)/shard_map/ppermute | solution.py:17
  50.7 1.5 collective-permute-start.16
  52.9 3.4 %collective-permute-done.13 = bf16[128,128]{1,0:T(8,128)(2,1)S(1)} collective-permute-done((bf16[128,128]{1,0:T(8,128)(2,1)S(1)}, bf16[128,128]{1,0:T(8,128)(2,1)S(1)}, u32[]{:S(2)}, u32[]{:S(2)}) %collective-permute-start.13) | collective-permute-done | bytes 32800 | tf_op jit(solution)/shard_map/ppermute | solution.py:17
  56.3 1.2 collective-permute-done.14.refs_4_.refs_5_
  57.6 2.3 %shard_map.129 = (bf16[128,2048]{1,0:T(8,128)(2,1)S(1)}, bf16[128,2048]{1,0:T(8,128)(2,1)S(1)}) custom-call(s32[2]{0:T(128)S(1)} %pad_add_fusion.place_ref, bf16[256,768]{1,0:T(8,128)(2,1)S(1)} %get-tuple-element.60.refs_0_, bf16[256,768]{1,0:T(8,128)(2,1)S(1)} %collective-permute-done.8.refs_1_, bf16[1536,2048]{1,0:T(8,128)(2,1)S(1)} %shard_map.125.refs_2_.refs_6_, ...), custom_call_target="tpu_custom_call" | custom-call | flops 1610 | bytes 8 | tf_op jit(solution)/shard_map/pallas_call | solution.py:112
  59.9 1.9 %collective-permute-done.16.refs_1_ = bf16[256,768]{1,0:T(8,128)(2,1)S(1)} collective-permute-done((bf16[256,768]{1,0:T(8,128)(2,1)S(1)}, bf16[256,768]{1,0:T(8,128)(2,1)S(1)}, u32[]{:S(2)}, u32[]{:S(2)}) %collective-permute-start.16) | collective-permute-done | bytes 393248 | tf_op jit(solution)/shard_map/ppermute | solution.py:17
  61.8 2.3 %shard_map.130 = (bf16[128,2048]{1,0:T(8,128)(2,1)S(1)}, bf16[128,2048]{1,0:T(8,128)(2,1)S(1)}) custom-call(s32[2]{0:T(128)S(1)} %pad_add_fusion.place_ref, bf16[256,768]{1,0:T(8,128)(2,1)S(1)} %get-tuple-element.64.refs_0_, bf16[256,768]{1,0:T(8,128)(2,1)S(1)} %collective-permute-done.16.refs_1_, bf16[1536,2048]{1,0:T(8,128)(2,1)S(1)} %shard_map.125.refs_2_.refs_6_, ...), custom_call_target="tpu_custom_call" | custom-call | flops 1610 | bytes 8 | tf_op jit(solution)/shard_map/pallas_call | solution.py:112
  64.7 1.4 collective-permute-done.17
  66.8 1.5 collective-permute-start.19
  68.4 4.2 %collective-permute-done.18 = bf16[64,1024]{1,0:T(8,128)(2,1)S(1)} collective-permute-done((bf16[64,1024]{1,0:T(8,128)(2,1)S(1)}, bf16[64,1024]{1,0:T(8,128)(2,1)S(1)}, u32[]{:S(2)}, u32[]{:S(2)}) %collective-permute-start.18) | collective-permute-done | bytes 131104 | tf_op jit(solution)/shard_map/ppermute | solution.py:17
  72.6 2.0 %collective-permute-done.19 = bf16[64,1024]{1,0:T(8,128)(2,1)S(1)} collective-permute-done((bf16[64,1024]{1,0:T(8,128)(2,1)S(1)}, bf16[64,1024]{1,0:T(8,128)(2,1)S(1)}, u32[]{:S(2)}, u32[]{:S(2)}) %collective-permute-start.19) | collective-permute-done | bytes 131104 | tf_op jit(solution)/shard_map/ppermute | solution.py:17
  75.3 2.8 %collective-permute-start.21 = (bf16[64,1024]{1,0:T(8,128)(2,1)S(1)}, bf16[64,1024]{1,0:T(8,128)(2,1)S(1)}, u32[]{:S(2)}, u32[]{:S(2)}) collective-permute-start(bf16[64,1024]{1,0:T(8,128)(2,1)S(1)} %get-tuple-element.121), channel_id=1, source_target_pairs={{0,8},{2,10},{4,12},{6,14},{8,0},{10,2},{12,4},{14,6},{16,24},{18,... | collective-permute-start | bytes 393224 | tf_op jit(solution)/shard_map/ppermute | solution.py:17
  78.2 4.1 %collective-permute-done.21 = bf16[64,1024]{1,0:T(8,128)(2,1)S(1)} collective-permute-done((bf16[64,1024]{1,0:T(8,128)(2,1)S(1)}, bf16[64,1024]{1,0:T(8,128)(2,1)S(1)}, u32[]{:S(2)}, u32[]{:S(2)}) %collective-permute-start.21) | collective-permute-done | bytes 131104 | tf_op jit(solution)/shard_map/ppermute | solution.py:17
  82.2 1.4 collective-permute-done.23
  83.7 2.3 %collective-permute-start.22 = (bf16[32,1024]{1,0:T(8,128)(2,1)S(1)}, bf16[32,1024]{1,0:T(8,128)(2,1)S(1)}, u32[]{:S(2)}, u32[]{:S(2)}) collective-permute-start(bf16[32,1024]{1,0:T(8,128)(2,1)S(1)} %get-tuple-element.113), channel_id=1, source_target_pairs={{0,16},{2,18},{4,20},{6,22},{8,24},{10,26},{12,28},{14,30},{16,0},... | collective-permute-start | bytes 196616 | tf_op jit(solution)/shard_map/ppermute | solution.py:17
  86.7 2.6 %collective-permute-done.22 = bf16[32,1024]{1,0:T(8,128)(2,1)S(1)} collective-permute-done((bf16[32,1024]{1,0:T(8,128)(2,1)S(1)}, bf16[32,1024]{1,0:T(8,128)(2,1)S(1)}, u32[]{:S(2)}, u32[]{:S(2)}) %collective-permute-start.22) | collective-permute-done | bytes 65568 | tf_op jit(solution)/shard_map/ppermute | solution.py:17
  89.3 2.4 %collective-permute-done.24 = bf16[32,1024]{1,0:T(8,128)(2,1)S(1)} collective-permute-done((bf16[32,1024]{1,0:T(8,128)(2,1)S(1)}, bf16[32,1024]{1,0:T(8,128)(2,1)S(1)}, u32[]{:S(2)}, u32[]{:S(2)}) %collective-permute-start.24) | collective-permute-done | bytes 65568 | tf_op jit(solution)/shard_map/ppermute | solution.py:17
  92.1 2.8 %collective-permute-start.26 = (bf16[32,1024]{1,0:T(8,128)(2,1)S(1)}, bf16[32,1024]{1,0:T(8,128)(2,1)S(1)}, u32[]{:S(2)}, u32[]{:S(2)}) collective-permute-start(bf16[32,1024]{1,0:T(8,128)(2,1)S(1)} %get-tuple-element.110.refs_1_), channel_id=1, source_target_pairs={{0,16},{2,18},{4,20},{6,22},{8,24},{10,26},{12,28},{14,30},{16,0},... | collective-permute-start | bytes 196616 | tf_op jit(solution)/shard_map/ppermute | solution.py:17
  94.9 2.3 %collective-permute-done.25.refs_2_ = bf16[32,1024]{1,0:T(8,128)(2,1)S(1)} collective-permute-done((bf16[32,1024]{1,0:T(8,128)(2,1)S(1)}, bf16[32,1024]{1,0:T(8,128)(2,1)S(1)}, u32[]{:S(2)}, u32[]{:S(2)}) %collective-permute-start.25) | collective-permute-done | bytes 65568 | tf_op jit(solution)/shard_map/ppermute | solution.py:17
  98.5 1.8 %collective-permute-start.27 = (bf16[64,2048]{1,0:T(8,128)(2,1)S(1)}, bf16[64,2048]{1,0:T(8,128)(2,1)S(1)}, u32[]{:S(2)}, u32[]{:S(2)}) collective-permute-start(bf16[64,2048]{1,0:T(8,128)(2,1)S(1)} %shard_map.131.refs_0_), channel_id=1, source_target_pairs={{0,8},{2,10},{4,12},{6,14},{8,0},{10,2},{12,4},{14,6},{16,24},{18,... | collective-permute-start | bytes 786440 | tf_op jit(solution)/shard_map/ppermute | solution.py:17
  100.3 1.5 collective-permute-start.28
  101.9 3.1 %collective-permute-done.27.refs_1_ = bf16[64,2048]{1,0:T(8,128)(2,1)S(1)} collective-permute-done((bf16[64,2048]{1,0:T(8,128)(2,1)S(1)}, bf16[64,2048]{1,0:T(8,128)(2,1)S(1)}, u32[]{:S(2)}, u32[]{:S(2)}) %collective-permute-start.27) | collective-permute-done | bytes 262176 | tf_op jit(solution)/shard_map/ppermute | solution.py:17
  104.9 1.8 %collective-permute-done.28.refs_0_ = bf16[64,2048]{1,0:T(8,128)(2,1)S(1)} collective-permute-done((bf16[64,2048]{1,0:T(8,128)(2,1)S(1)}, bf16[64,2048]{1,0:T(8,128)(2,1)S(1)}, u32[]{:S(2)}, u32[]{:S(2)}) %collective-permute-start.28) | collective-permute-done | bytes 262176 | tf_op jit(solution)/shard_map/ppermute | solution.py:17
  106.7 1.5 collective-permute-start.32
  108.5 2.4 %shard_map.132 = (bf16[256,2048]{1,0:T(8,128)(2,1)S(1)}, f32[256,768]{1,0:T(8,128)S(1)}, bf16[256,768]{1,0:T(8,128)(2,1)S(1)}) custom-call(s32[2]{0:T(128)S(1)} %pad_add_fusion.place_ref, bf16[64,2048]{1,0:T(8,128)(2,1)S(1)} %shard_map.131.refs_0_, bf16[64,2048]{1,0:T(8,128)(2,1)S(1)} %collective-permute-done.27.refs_1_, ...), custom_call_target="tpu_custom_call" | custom-call | flops 1610 | bytes 9 | tf_op jit(solution)/shard_map/pallas_call | solution.py:112
  110.9 1.6 collective-permute-start.31
  112.5 2.9 %collective-permute-done.32.refs_1_ = bf16[64,2048]{1,0:T(8,128)(2,1)S(1)} collective-permute-done((bf16[64,2048]{1,0:T(8,128)(2,1)S(1)}, bf16[64,2048]{1,0:T(8,128)(2,1)S(1)}, u32[]{:S(2)}, u32[]{:S(2)}) %collective-permute-start.32) | collective-permute-done | bytes 262176 | tf_op jit(solution)/shard_map/ppermute | solution.py:17
  115.4 4.1 %shard_map.134.refs_4_ = f32[2,12,2048]{2,1,0:T(8,128)S(1)} custom-call(s32[2]{0:T(128)S(1)} %pad_add_fusion.place_ref, bf16[256,768]{1,0:T(8,128)(2,1)S(1)} %get-tuple-element.60.refs_0_, bf16[256,768]{1,0:T(8,128)(2,1)S(1)} %collective-permute-done.8.refs_1_, bf16[256,2048]{1,0:T(8,128)(2,1)S(1)} %get-tuple-element.78.refs_2_, ...), custom_call_target="tpu_custom_call" | custom-call | flops 1610 | bytes 8 | tf_op jit(solution)/shard_map/pallas_call | solution.py:112
  119.6 2.7 %collective-permute-done.31.refs_0_ = bf16[256,768]{1,0:T(8,128)(2,1)S(1)} collective-permute-done((bf16[256,768]{1,0:T(8,128)(2,1)S(1)}, bf16[256,768]{1,0:T(8,128)(2,1)S(1)}, u32[]{:S(2)}, u32[]{:S(2)}) %collective-permute-start.31) | collective-permute-done | bytes 393248 | tf_op jit(solution)/shard_map/ppermute | solution.py:17
  122.3 2.4 %shard_map.135 = (bf16[256,2048]{1,0:T(8,128)(2,1)S(1)}, f32[256,768]{1,0:T(8,128)S(1)}, bf16[256,768]{1,0:T(8,128)(2,1)S(1)}) custom-call(s32[2]{0:T(128)S(1)} %pad_add_fusion.place_ref, bf16[64,2048]{1,0:T(8,128)(2,1)S(1)} %collective-permute-done.28.refs_0_, bf16[64,2048]{1,0:T(8,128)(2,1)S(1)} %collective-permute-done.32.refs_1_, ...), custom_call_target="tpu_custom_call" | custom-call | flops 1610 | bytes 9 | tf_op jit(solution)/shard_map/pallas_call | solution.py:112
  124.7 1.6 collective-permute-start.35
  126.3 4.0 %shard_map.136 = f32[2,12,2048]{2,1,0:T(8,128)S(1)} custom-call(s32[2]{0:T(128)S(1)} %pad_add_fusion.place_ref, bf16[256,768]{1,0:T(8,128)(2,1)S(1)} %get-tuple-element.64.refs_0_, bf16[256,768]{1,0:T(8,128)(2,1)S(1)} %collective-permute-done.16.refs_1_, bf16[256,2048]{1,0:T(8,128)(2,1)S(1)} %get-tuple-element.84.refs_2_, ...), custom_call_target="tpu_custom_call" | custom-call | flops 1610 | bytes 8 | tf_op jit(solution)/shard_map/pallas_call | solution.py:112
  130.3 4.0 %shard_map.133 = (bf16[256,1536]{1,0:T(8,128)(2,1)S(1)}, bf16[128,2048]{1,0:T(8,128)(2,1)S(1)}, bf16[128,2048]{1,0:T(8,128)(2,1)S(1)}, bf16[128,2048]{1,0:T(8,128)(2,1)S(1)}, bf16[128,2048]{1,0:T(8,128)(2,1)S(1)}) custom-call(s32[2]{0:T(128)S(1)} %pad_add_fusion.place_ref, f32[256,768]{1,0:T(8,128)S(1)} %get-tuple-element.73.grad_own_ref, ...), custom_call_target="tpu_custom_call" | custom-call | flops 3221 | bytes 18 | tf_op jit(solution)/shard_map/pallas_call | solution.py:112
  134.3 0.9 collective-permute-done.35.refs_0_
  135.3 4.0 %shard_map.137 = (bf16[256,1536]{1,0:T(8,128)(2,1)S(1)}, bf16[128,2048]{1,0:T(8,128)(2,1)S(1)}, bf16[128,2048]{1,0:T(8,128)(2,1)S(1)}, bf16[128,2048]{1,0:T(8,128)(2,1)S(1)}, bf16[128,2048]{1,0:T(8,128)(2,1)S(1)}) custom-call(s32[2]{0:T(128)S(1)} %pad_add_fusion.place_ref, f32[256,768]{1,0:T(8,128)S(1)} %get-tuple-element.81.grad_own_ref, ...), custom_call_target="tpu_custom_call" | custom-call | flops 3221 | bytes 18 | tf_op jit(solution)/shard_map/pallas_call | solution.py:112
  139.9 1.4 collective-permute-done.38
  141.4 1.1 collective-permute-start.39
  143.0 1.5 collective-permute-start.40
  144.5 5.3 %collective-permute-done.39 = bf16[64,2048]{1,0:T(8,128)(2,1)S(1)} collective-permute-done((bf16[64,2048]{1,0:T(8,128)(2,1)S(1)}, bf16[64,2048]{1,0:T(8,128)(2,1)S(1)}, u32[]{:S(2)}, u32[]{:S(2)}) %collective-permute-start.39) | collective-permute-done | bytes 262176 | tf_op jit(solution)/shard_map/ppermute | solution.py:17
  150.0 1.2 collective-permute-done.40
  151.2 1.5 collective-permute-start.41
  152.9 1.1 collective-permute-start.44
  154.0 6.6 %shard_map.138.refs_15_ = f32[4,32,768]{2,1,0:T(8,128)} custom-call(s32[2]{0:T(128)S(1)} %pad_add_fusion.place_ref, bf16[96,4096]{1,0:T(8,128)(2,1)S(1)} %shard_map.123.refs_0_, bf16[32,4096]{1,0:T(8,128)(2,1)S(1)} %collective-permute-done.4.refs_1_, bf16[96,4096]{1,0:T(8,128)(2,1)S(1)} %collective-permute-done.6.refs_2_, ...), custom_call_target="tpu_custom_call" | custom-call | flops 3221 | bytes 20 | tf_op jit(solution)/shard_map/pallas_call | solution.py:112
  161.5 1.0 collective-permute-start.45
  162.5 4.2 %shard_map.139.refs_15_ = f32[4,32,768]{2,1,0:T(8,128)} custom-call(s32[2]{0:T(128)S(1)} %pad_add_fusion.place_ref, bf16[96,4096]{1,0:T(8,128)(2,1)S(1)} %shard_map.123.refs_0_, bf16[32,4096]{1,0:T(8,128)(2,1)S(1)} %collective-permute-done.4.refs_1_, bf16[96,4096]{1,0:T(8,128)(2,1)S(1)} %collective-permute-done.6.refs_2_, ...), custom_call_target="tpu_custom_call", output_to_operand_aliasing={{}: (16, {})} | custom-call | flops 1610 | bytes 20 | tf_op jit(solution)/shard_map/pallas_call | solution.py:112
  166.7 0.9 collective-permute-done.46
  168.0 2.7 %collective-permute-start.47 = (bf16[32,2048]{1,0:T(8,128)(2,1)S(1)}, bf16[32,2048]{1,0:T(8,128)(2,1)S(1)}, u32[]{:S(2)}, u32[]{:S(2)}) collective-permute-start(bf16[32,2048]{1,0:T(8,128)(2,1)S(1)} %add_convert_fusion.9), channel_id=1, source_target_pairs={{0,16},{2,18},{4,20},{6,22},{8,24},{10,26},{12,28},{14,30},{16,0},... | collective-permute-start | bytes 393224 | tf_op jit(solution)/shard_map/ppermute | solution.py:17
  171.5 3.9 %shard_map.140 = f32[4,32,768]{2,1,0:T(8,128)} custom-call(s32[2]{0:T(128)S(1)} %pad_add_fusion.place_ref, bf16[96,4096]{1,0:T(8,128)(2,1)S(1)} %shard_map.123.refs_0_, bf16[32,4096]{1,0:T(8,128)(2,1)S(1)} %collective-permute-done.4.refs_1_, bf16[96,4096]{1,0:T(8,128)(2,1)S(1)} %collective-permute-done.6.refs_2_, ...), custom_call_target="tpu_custom_call", output_to_operand_aliasing={{}: (16, {})} | custom-call | flops 1610 | bytes 20 | tf_op jit(solution)/shard_map/pallas_call | solution.py:112
  (98 shorter events, 15.7 us)
Async XLA Ops:
  0.6 17.6 %collective-permute-start.1 = (bf16[32,4096]{1,0:T(8,128)(2,1)}, bf16[32,4096]{1,0:T(8,128)(2,1)S(1)}, u32[]{:S(2)}, u32[]{:S(2)}) collective-permute-start(bf16[32,4096]{1,0:T(8,128)(2,1)} %refs_0_.1), channel_id=1, source_target_pairs={{0,4},{2,6},{4,0},{6,2},{8,12},{10,14},{12,8},{14,10},{16,20},{18,... | collective-permute-start | bytes 786440 | tf_op jit(solution)/shard_map/ppermute | solution.py:17
  3.6 14.6 %collective-permute-start = (bf16[32,4096]{1,0:T(8,128)(2,1)}, bf16[32,4096]{1,0:T(8,128)(2,1)S(1)}, u32[]{:S(2)}, u32[]{:S(2)}) collective-permute-start(bf16[32,4096]{1,0:T(8,128)(2,1)} %refs_0_.1), channel_id=1, source_target_pairs={{0,16},{2,18},{4,20},{6,22},{8,24},{10,26},{12,28},{14,30},{16,0},... | collective-permute-start | bytes 786440 | tf_op jit(solution)/shard_map/ppermute | solution.py:17
  6.2 12.2 %collective-permute-start.3 = (bf16[32,4096]{1,0:T(8,128)(2,1)}, bf16[32,4096]{1,0:T(8,128)(2,1)S(1)}, u32[]{:S(2)}, u32[]{:S(2)}) collective-permute-start(bf16[32,4096]{1,0:T(8,128)(2,1)} %refs_0_.1), channel_id=1, source_target_pairs={{0,8},{2,10},{4,12},{6,14},{8,0},{10,2},{12,4},{14,6},{16,24},{18,... | collective-permute-start | bytes 786440 | tf_op jit(solution)/shard_map/ppermute | solution.py:17
  10.2 0.9 copy-start.1
  11.1 0.9 copy-start.2
  12.0 13.0 %copy-start = (bf16[32,4096]{1,0:T(8,128)(2,1)S(1)}, bf16[32,4096]{1,0:T(8,128)(2,1)}, u32[]{:S(2)}) copy-start(bf16[32,4096]{1,0:T(8,128)(2,1)} %refs_0_.1) | copy-start | bytes 786436
  12.0 17.2 %copy-start.4 = (f32[1,12,2048]{2,0,1:T(1,128)S(1)}, f32[1,12,2048]{2,0,1:T(1,128)}, u32[]{:S(2)}) copy-start(f32[1,12,2048]{2,0,1:T(1,128)} %param.19) | copy-start | bytes 294916
  18.2 15.1 %copy-start.5 = (f32[1,12,2048]{2,0,1:T(1,128)S(1)}, f32[1,12,2048]{2,0,1:T(1,128)}, u32[]{:S(2)}) copy-start(f32[1,12,2048]{2,0,1:T(1,128)} %param.18) | copy-start | bytes 294916
  18.2 15.2 %slice-start.3 = ((s8[6291456]{0:T(1024)(128)(4,1)}), s8[4194304]{0:T(1024)(128)(4,1)S(1)}, s32[]{:S(2)}) async-start(s8[6291456]{0:T(1024)(128)(4,1)} %bitcast.10), calls=%async_computation.3 | async-start | bytes 8388608
  18.4 7.3 %collective-permute-start.4 = (bf16[32,4096]{1,0:T(8,128)(2,1)S(1)}, bf16[32,4096]{1,0:T(8,128)(2,1)S(1)}, u32[]{:S(2)}, u32[]{:S(2)}) collective-permute-start(bf16[32,4096]{1,0:T(8,128)(2,1)S(1)} %collective-permute-done.refs_1_.refs_0_), channel_id=1, source_target_pairs={{0,8},{2,10},{4,12},{6,14},{8,0},{10,2},{12,4},{14,6},{16,24},{18,... | collective-permute-start | bytes 786440 | tf_op jit(solution)/shard_map/ppermute | solution.py:17
  19.9 7.0 %collective-permute-start.5 = (bf16[32,4096]{1,0:T(8,128)(2,1)S(1)}, bf16[32,4096]{1,0:T(8,128)(2,1)S(1)}, u32[]{:S(2)}, u32[]{:S(2)}) collective-permute-start(bf16[32,4096]{1,0:T(8,128)(2,1)S(1)} %collective-permute-done.3.refs_2_), channel_id=1, source_target_pairs={{0,4},{2,6},{4,0},{6,2},{8,12},{10,14},{12,8},{14,10},{16,20},{18,... | collective-permute-start | bytes 786440 | tf_op jit(solution)/shard_map/ppermute | solution.py:17
  20.4 4.7 %collective-permute-start.2 = (bf16[32,128]{1,0:T(8,128)(2,1)S(1)}, bf16[32,128]{1,0:T(8,128)(2,1)S(1)}, u32[]{:S(2)}, u32[]{:S(2)}) collective-permute-start(bf16[32,128]{1,0:T(8,128)(2,1)S(1)} %shard_map.121), channel_id=1, source_target_pairs={{0,16},{2,18},{4,20},{6,22},{8,24},{10,26},{12,28},{14,30},{16,0},... | collective-permute-start | bytes 24584 | tf_op jit(solution)/shard_map/ppermute | solution.py:17
  25.7 3.6 %collective-permute-start.6 = (bf16[96,4096]{1,0:T(8,128)(2,1)S(1)}, bf16[96,4096]{1,0:T(8,128)(2,1)S(1)}, u32[]{:S(2)}, u32[]{:S(2)}) collective-permute-start(bf16[96,4096]{1,0:T(8,128)(2,1)S(1)} %shard_map.123.refs_0_), channel_id=1, source_target_pairs={{0,2},{2,0},{4,6},{6,4},{8,10},{10,8},{12,14},{14,12},{16,18},{18,... | collective-permute-start | bytes 2359304 | tf_op jit(solution)/shard_map/ppermute | solution.py:17
  26.9 1.5 collective-permute-start.7
  27.4 14.4 %collective-permute-start.9 = (bf16[64,4096]{1,0:T(8,128)(2,1)S(1)}, bf16[64,4096]{1,0:T(8,128)(2,1)S(1)}, u32[]{:S(2)}, u32[]{:S(2)}) collective-permute-start(bf16[64,4096]{1,0:T(8,128)(2,1)S(1)} %shard_map.127), channel_id=1, source_target_pairs={{0,4},{2,6},{4,0},{6,2},{8,12},{10,14},{12,8},{14,10},{16,20},{18,... | collective-permute-start | bytes 1572872 | tf_op jit(solution)/shard_map/ppermute | solution.py:17
  29.0 12.9 %collective-permute-start.10 = (bf16[64,4096]{1,0:T(8,128)(2,1)S(1)}, bf16[64,4096]{1,0:T(8,128)(2,1)S(1)}, u32[]{:S(2)}, u32[]{:S(2)}) collective-permute-start(bf16[64,4096]{1,0:T(8,128)(2,1)S(1)} %shard_map.126.refs_0_.refs_2_.refs_4_.refs_6_), channel_id=1, source_target_pairs={{0,2},{2,0},{4,6},{6,4},{8,10},{10,8},{12,14},{14,12},{16,18},{18,... | collective-permute-start | bytes 1572872 | tf_op jit(solution)/shard_map/ppermute | solution.py:17
  29.2 4.2 %slice-start.4 = ((s8[6291456]{0:T(1024)(128)(4,1)}), s8[2097152]{0:T(1024)(128)(4,1)S(1)}, s32[]{:S(2)}) async-start(s8[6291456]{0:T(1024)(128)(4,1)} %bitcast.10), calls=%async_computation.4 | async-start | bytes 4194304
  41.8 1.9 %collective-permute-start.11 = (bf16[64,4096]{1,0:T(8,128)(2,1)S(1)}, bf16[64,4096]{1,0:T(8,128)(2,1)S(1)}, u32[]{:S(2)}, u32[]{:S(2)}) collective-permute-start(bf16[64,4096]{1,0:T(8,128)(2,1)S(1)} %collective-permute-done.9.refs_1_.refs_3_.refs_5_.refs_7_), channel_id=1, source_target_pairs={{0,2},{2,0},{4,6},{6,4},{8,10},{10,8},{12,14},{14,12},{16,18},{18,... | collective-permute-start | bytes 1572872 | tf_op jit(solution)/shard_map/ppermute | solution.py:17
  41.8 14.5 %collective-permute-start.8 = (bf16[256,768]{1,0:T(8,128)(2,1)S(1)}, bf16[256,768]{1,0:T(8,128)(2,1)S(1)}, u32[]{:S(2)}, u32[]{:S(2)}) collective-permute-start(bf16[256,768]{1,0:T(8,128)(2,1)S(1)} %get-tuple-element.60.refs_0_), channel_id=1, source_target_pairs={{0,1},{1,0},{2,3},{3,2},{4,5},{5,4},{6,7},{7,6},{8,9},{9,8},{10,11... | collective-permute-start | bytes 1179656 | tf_op jit(solution)/shard_map/ppermute | solution.py:17
  47.8 43.9 %copy-start.3 = (bf16[32,2048]{1,0:T(8,128)(2,1)S(1)}, bf16[32,2048]{1,0:T(8,128)(2,1)}, u32[]{:S(2)}) copy-start(bf16[32,2048]{1,0:T(8,128)(2,1)} %param.11) | copy-start | bytes 393220
  47.8 4.5 %collective-permute-start.12 = (bf16[64,128]{1,0:T(8,128)(2,1)S(1)}, bf16[64,128]{1,0:T(8,128)(2,1)S(1)}, u32[]{:S(2)}, u32[]{:S(2)}) collective-permute-start(bf16[64,128]{1,0:T(8,128)(2,1)S(1)} %pad_maximum_fusion.1), channel_id=1, source_target_pairs={{0,8},{2,10},{4,12},{6,14},{8,0},{10,2},{12,4},{14,6},{16,24},{18,... | collective-permute-start | bytes 49160 | tf_op jit(solution)/shard_map/ppermute | solution.py:17
  50.7 11.1 %collective-permute-start.16 = (bf16[256,768]{1,0:T(8,128)(2,1)S(1)}, bf16[256,768]{1,0:T(8,128)(2,1)S(1)}, u32[]{:S(2)}, u32[]{:S(2)}) collective-permute-start(bf16[256,768]{1,0:T(8,128)(2,1)S(1)} %get-tuple-element.64.refs_0_), channel_id=1, source_target_pairs={{0,1},{1,0},{2,3},{3,2},{4,5},{5,4},{6,7},{7,6},{8,9},{9,8},{10,11... | collective-permute-start | bytes 1179656 | tf_op jit(solution)/shard_map/ppermute | solution.py:17
  52.4 3.9 %collective-permute-start.13 = (bf16[128,128]{1,0:T(8,128)(2,1)S(1)}, bf16[128,128]{1,0:T(8,128)(2,1)S(1)}, u32[]{:S(2)}, u32[]{:S(2)}) collective-permute-start(bf16[128,128]{1,0:T(8,128)(2,1)S(1)} %pad_maximum_fusion), channel_id=1, source_target_pairs={{0,4},{2,6},{4,0},{6,2},{8,12},{10,14},{12,8},{14,10},{16,20},{18,... | collective-permute-start | bytes 98312 | tf_op jit(solution)/shard_map/ppermute | solution.py:17
  56.3 1.3 collective-permute-start.14
  64.1 2.0 %collective-permute-start.17 = (bf16[128,2048]{1,0:T(8,128)(2,1)S(1)}, bf16[128,2048]{1,0:T(8,128)(2,1)S(1)}, u32[]{:S(2)}, u32[]{:S(2)}) collective-permute-start(bf16[128,2048]{1,0:T(8,128)(2,1)S(1)} %get-tuple-element.70), channel_id=1, source_target_pairs={{0,2},{2,0},{4,6},{6,4},{8,10},{10,8},{12,14},{14,12},{16,18},{18,... | collective-permute-start | bytes 1572872 | tf_op jit(solution)/shard_map/ppermute | solution.py:17
  64.2 10.9 %collective-permute-start.15 = (bf16[128,2048]{1,0:T(8,128)(2,1)S(1)}, bf16[128,2048]{1,0:T(8,128)(2,1)S(1)}, u32[]{:S(2)}, u32[]{:S(2)}) collective-permute-start(bf16[128,2048]{1,0:T(8,128)(2,1)S(1)} %get-tuple-element.67), channel_id=1, source_target_pairs={{0,2},{2,0},{4,6},{6,4},{8,10},{10,8},{12,14},{14,12},{16,18},{18,... | collective-permute-start | bytes 1572872 | tf_op jit(solution)/shard_map/ppermute | solution.py:17
  66.2 6.4 %collective-permute-start.18 = (bf16[64,1024]{1,0:T(8,128)(2,1)S(1)}, bf16[64,1024]{1,0:T(8,128)(2,1)S(1)}, u32[]{:S(2)}, u32[]{:S(2)}) collective-permute-start(bf16[64,1024]{1,0:T(8,128)(2,1)S(1)} %get-tuple-element.123), channel_id=1, source_target_pairs={{0,4},{2,6},{4,0},{6,2},{8,12},{10,14},{12,8},{14,10},{16,20},{18,... | collective-permute-start | bytes 393224 | tf_op jit(solution)/shard_map/ppermute | solution.py:17
  66.8 7.8 %collective-permute-start.19 = (bf16[64,1024]{1,0:T(8,128)(2,1)S(1)}, bf16[64,1024]{1,0:T(8,128)(2,1)S(1)}, u32[]{:S(2)}, u32[]{:S(2)}) collective-permute-start(bf16[64,1024]{1,0:T(8,128)(2,1)S(1)} %get-tuple-element.122), channel_id=1, source_target_pairs={{0,4},{2,6},{4,0},{6,2},{8,12},{10,14},{12,8},{14,10},{16,20},{18,... | collective-permute-start | bytes 393224 | tf_op jit(solution)/shard_map/ppermute | solution.py:17
  74.6 9.0 %collective-permute-start.20 = (bf16[64,2048]{1,0:T(8,128)(2,1)S(1)}, bf16[64,2048]{1,0:T(8,128)(2,1)S(1)}, u32[]{:S(2)}, u32[]{:S(2)}) collective-permute-start(bf16[64,2048]{1,0:T(8,128)(2,1)S(1)} %add_convert_fusion.7), channel_id=1, source_target_pairs={{0,4},{2,6},{4,0},{6,2},{8,12},{10,14},{12,8},{14,10},{16,20},{18,... | collective-permute-start | bytes 786440 | tf_op jit(solution)/shard_map/ppermute | solution.py:17
  75.3 7.0 %collective-permute-start.21 = (bf16[64,1024]{1,0:T(8,128)(2,1)S(1)}, bf16[64,1024]{1,0:T(8,128)(2,1)S(1)}, u32[]{:S(2)}, u32[]{:S(2)}) collective-permute-start(bf16[64,1024]{1,0:T(8,128)(2,1)S(1)} %get-tuple-element.121), channel_id=1, source_target_pairs={{0,8},{2,10},{4,12},{6,14},{8,0},{10,2},{12,4},{14,6},{16,24},{18,... | collective-permute-start | bytes 393224 | tf_op jit(solution)/shard_map/ppermute | solution.py:17
  78.1 5.6 %collective-permute-start.23 = (bf16[64,1024]{1,0:T(8,128)(2,1)S(1)}, bf16[64,1024]{1,0:T(8,128)(2,1)S(1)}, u32[]{:S(2)}, u32[]{:S(2)}) collective-permute-start(bf16[64,1024]{1,0:T(8,128)(2,1)S(1)} %get-tuple-element.120), channel_id=1, source_target_pairs={{0,8},{2,10},{4,12},{6,14},{8,0},{10,2},{12,4},{14,6},{16,24},{18,... | collective-permute-start | bytes 393224 | tf_op jit(solution)/shard_map/ppermute | solution.py:17
  83.7 5.6 %collective-permute-start.22 = (bf16[32,1024]{1,0:T(8,128)(2,1)S(1)}, bf16[32,1024]{1,0:T(8,128)(2,1)S(1)}, u32[]{:S(2)}, u32[]{:S(2)}) collective-permute-start(bf16[32,1024]{1,0:T(8,128)(2,1)S(1)} %get-tuple-element.113), channel_id=1, source_target_pairs={{0,16},{2,18},{4,20},{6,22},{8,24},{10,26},{12,28},{14,30},{16,0},... | collective-permute-start | bytes 196616 | tf_op jit(solution)/shard_map/ppermute | solution.py:17
  86.0 5.8 %collective-permute-start.24 = (bf16[32,1024]{1,0:T(8,128)(2,1)S(1)}, bf16[32,1024]{1,0:T(8,128)(2,1)S(1)}, u32[]{:S(2)}, u32[]{:S(2)}) collective-permute-start(bf16[32,1024]{1,0:T(8,128)(2,1)S(1)} %get-tuple-element.112), channel_id=1, source_target_pairs={{0,16},{2,18},{4,20},{6,22},{8,24},{10,26},{12,28},{14,30},{16,0},... | collective-permute-start | bytes 196616 | tf_op jit(solution)/shard_map/ppermute | solution.py:17
  91.9 5.3 %collective-permute-start.25 = (bf16[32,1024]{1,0:T(8,128)(2,1)S(1)}, bf16[32,1024]{1,0:T(8,128)(2,1)S(1)}, u32[]{:S(2)}, u32[]{:S(2)}) collective-permute-start(bf16[32,1024]{1,0:T(8,128)(2,1)S(1)} %get-tuple-element.111.refs_0_), channel_id=1, source_target_pairs={{0,16},{2,18},{4,20},{6,22},{8,24},{10,26},{12,28},{14,30},{16,0},... | collective-permute-start | bytes 196616 | tf_op jit(solution)/shard_map/ppermute | solution.py:17
  92.1 5.8 %collective-permute-start.26 = (bf16[32,1024]{1,0:T(8,128)(2,1)S(1)}, bf16[32,1024]{1,0:T(8,128)(2,1)S(1)}, u32[]{:S(2)}, u32[]{:S(2)}) collective-permute-start(bf16[32,1024]{1,0:T(8,128)(2,1)S(1)} %get-tuple-element.110.refs_1_), channel_id=1, source_target_pairs={{0,16},{2,18},{4,20},{6,22},{8,24},{10,26},{12,28},{14,30},{16,0},... | collective-permute-start | bytes 196616 | tf_op jit(solution)/shard_map/ppermute | solution.py:17
  98.5 6.4 %collective-permute-start.27 = (bf16[64,2048]{1,0:T(8,128)(2,1)S(1)}, bf16[64,2048]{1,0:T(8,128)(2,1)S(1)}, u32[]{:S(2)}, u32[]{:S(2)}) collective-permute-start(bf16[64,2048]{1,0:T(8,128)(2,1)S(1)} %shard_map.131.refs_0_), channel_id=1, source_target_pairs={{0,8},{2,10},{4,12},{6,14},{8,0},{10,2},{12,4},{14,6},{16,24},{18,... | collective-permute-start | bytes 786440 | tf_op jit(solution)/shard_map/ppermute | solution.py:17
  100.3 6.4 %collective-permute-start.28 = (bf16[64,2048]{1,0:T(8,128)(2,1)S(1)}, bf16[64,2048]{1,0:T(8,128)(2,1)S(1)}, u32[]{:S(2)}, u32[]{:S(2)}) collective-permute-start(bf16[64,2048]{1,0:T(8,128)(2,1)S(1)} %shard_map.131.refs_0_), channel_id=1, source_target_pairs={{0,4},{2,6},{4,0},{6,2},{8,12},{10,14},{12,8},{14,10},{16,20},{18,... | collective-permute-start | bytes 786440 | tf_op jit(solution)/shard_map/ppermute | solution.py:17
  101.9 4.8 %collective-permute-start.29 = (bf16[64,2048]{1,0:T(8,128)(2,1)S(1)}, bf16[64,2048]{1,0:T(8,128)(2,1)S(1)}, u32[]{:S(2)}, u32[]{:S(2)}) collective-permute-start(bf16[64,2048]{1,0:T(8,128)(2,1)S(1)} %shard_map.131.refs_0_), channel_id=1, source_target_pairs={{0,2},{2,0},{4,6},{6,4},{8,10},{10,8},{12,14},{14,12},{16,18},{18,... | collective-permute-start | bytes 786440 | tf_op jit(solution)/shard_map/ppermute | solution.py:17
  106.7 1.8 %collective-permute-start.30 = (bf16[64,2048]{1,0:T(8,128)(2,1)S(1)}, bf16[64,2048]{1,0:T(8,128)(2,1)S(1)}, u32[]{:S(2)}, u32[]{:S(2)}) collective-permute-start(bf16[64,2048]{1,0:T(8,128)(2,1)S(1)} %collective-permute-done.27.refs_1_), channel_id=1, source_target_pairs={{0,2},{2,0},{4,6},{6,4},{8,10},{10,8},{12,14},{14,12},{16,18},{18,... | collective-permute-start | bytes 786440 | tf_op jit(solution)/shard_map/ppermute | solution.py:17
  106.7 8.7 %collective-permute-start.32 = (bf16[64,2048]{1,0:T(8,128)(2,1)S(1)}, bf16[64,2048]{1,0:T(8,128)(2,1)S(1)}, u32[]{:S(2)}, u32[]{:S(2)}) collective-permute-start(bf16[64,2048]{1,0:T(8,128)(2,1)S(1)} %collective-permute-done.27.refs_1_), channel_id=1, source_target_pairs={{0,4},{2,6},{4,0},{6,2},{8,12},{10,14},{12,8},{14,10},{16,20},{18,... | collective-permute-start | bytes 786440 | tf_op jit(solution)/shard_map/ppermute | solution.py:17
  108.3 7.2 %collective-permute-start.33 = (bf16[64,2048]{1,0:T(8,128)(2,1)S(1)}, bf16[64,2048]{1,0:T(8,128)(2,1)S(1)}, u32[]{:S(2)}, u32[]{:S(2)}) collective-permute-start(bf16[64,2048]{1,0:T(8,128)(2,1)S(1)} %collective-permute-done.28.refs_0_), channel_id=1, source_target_pairs={{0,2},{2,0},{4,6},{6,4},{8,10},{10,8},{12,14},{14,12},{16,18},{18,... | collective-permute-start | bytes 786440 | tf_op jit(solution)/shard_map/ppermute | solution.py:17
  110.9 11.4 %collective-permute-start.31 = (bf16[256,768]{1,0:T(8,128)(2,1)S(1)}, bf16[256,768]{1,0:T(8,128)(2,1)S(1)}, u32[]{:S(2)}, u32[]{:S(2)}) collective-permute-start(bf16[256,768]{1,0:T(8,128)(2,1)S(1)} %get-tuple-element.74), channel_id=1, source_target_pairs={{0,1},{1,0},{2,3},{3,2},{4,5},{5,4},{6,7},{7,6},{8,9},{9,8},{10,11... | collective-permute-start | bytes 1179656 | tf_op jit(solution)/shard_map/ppermute | solution.py:17
  115.4 4.1 %collective-permute-start.34 = (bf16[64,2048]{1,0:T(8,128)(2,1)S(1)}, bf16[64,2048]{1,0:T(8,128)(2,1)S(1)}, u32[]{:S(2)}, u32[]{:S(2)}) collective-permute-start(bf16[64,2048]{1,0:T(8,128)(2,1)S(1)} %collective-permute-done.32.refs_1_), channel_id=1, source_target_pairs={{0,2},{2,0},{4,6},{6,4},{8,10},{10,8},{12,14},{14,12},{16,18},{18,... | collective-permute-start | bytes 786440 | tf_op jit(solution)/shard_map/ppermute | solution.py:17
  124.7 10.6 %collective-permute-start.35 = (bf16[256,768]{1,0:T(8,128)(2,1)S(1)}, bf16[256,768]{1,0:T(8,128)(2,1)S(1)}, u32[]{:S(2)}, u32[]{:S(2)}) collective-permute-start(bf16[256,768]{1,0:T(8,128)(2,1)S(1)} %get-tuple-element.82), channel_id=1, source_target_pairs={{0,1},{1,0},{2,3},{3,2},{4,5},{5,4},{6,7},{7,6},{8,9},{9,8},{10,11... | collective-permute-start | bytes 1179656 | tf_op jit(solution)/shard_map/ppermute | solution.py:17
  130.3 23.7 %slice-start = ((s8[12582912]{0:T(1024)(128)(4,1)}), s8[4194304]{0:T(1024)(128)(4,1)S(1)}, s32[]{:S(2)}) async-start(s8[12582912]{0:T(1024)(128)(4,1)} %bitcast.8), calls=%async_computation | async-start | bytes 8388608
  130.3 23.7 %slice-start.1 = ((s8[12582912]{0:T(1024)(128)(4,1)}), s8[4194304]{0:T(1024)(128)(4,1)S(1)}, s32[]{:S(2)}) async-start(s8[12582912]{0:T(1024)(128)(4,1)} %bitcast.8), calls=%async_computation.1 | async-start | bytes 8388608
  135.3 18.7 %slice-start.2 = ((s8[12582912]{0:T(1024)(128)(4,1)}), s8[4194304]{0:T(1024)(128)(4,1)S(1)}, s32[]{:S(2)}) async-start(s8[12582912]{0:T(1024)(128)(4,1)} %bitcast.8), calls=%async_computation.2 | async-start | bytes 8388608
  139.3 2.0 %collective-permute-start.38 = (bf16[128,2048]{1,0:T(8,128)(2,1)S(1)}, bf16[128,2048]{1,0:T(8,128)(2,1)S(1)}, u32[]{:S(2)}, u32[]{:S(2)}) collective-permute-start(bf16[128,2048]{1,0:T(8,128)(2,1)S(1)} %get-tuple-element.97), channel_id=1, source_target_pairs={{0,2},{2,0},{4,6},{6,4},{8,10},{10,8},{12,14},{14,12},{16,18},{18,... | collective-permute-start | bytes 1572872 | tf_op jit(solution)/shard_map/ppermute | solution.py:17
  139.4 5.1 %collective-permute-start.37 = (bf16[128,2048]{1,0:T(8,128)(2,1)S(1)}, bf16[128,2048]{1,0:T(8,128)(2,1)S(1)}, u32[]{:S(2)}, u32[]{:S(2)}) collective-permute-start(bf16[128,2048]{1,0:T(8,128)(2,1)S(1)} %get-tuple-element.95), channel_id=1, source_target_pairs={{0,2},{2,0},{4,6},{6,4},{8,10},{10,8},{12,14},{14,12},{16,18},{18,... | collective-permute-start | bytes 1572872 | tf_op jit(solution)/shard_map/ppermute | solution.py:17
  141.4 8.4 %collective-permute-start.39 = (bf16[64,2048]{1,0:T(8,128)(2,1)S(1)}, bf16[64,2048]{1,0:T(8,128)(2,1)S(1)}, u32[]{:S(2)}, u32[]{:S(2)}) collective-permute-start(bf16[64,2048]{1,0:T(8,128)(2,1)S(1)} %get-tuple-element.116), channel_id=1, source_target_pairs={{0,4},{2,6},{4,0},{6,2},{8,12},{10,14},{12,8},{14,10},{16,20},{18,... | collective-permute-start | bytes 786440 | tf_op jit(solution)/shard_map/ppermute | solution.py:17
  142.5 10.2 %collective-permute-start.43 = (bf16[128,2048]{1,0:T(8,128)(2,1)S(1)}, bf16[128,2048]{1,0:T(8,128)(2,1)S(1)}, u32[]{:S(2)}, u32[]{:S(2)}) collective-permute-start(bf16[128,2048]{1,0:T(8,128)(2,1)S(1)} %get-tuple-element.101), channel_id=1, source_target_pairs={{0,2},{2,0},{4,6},{6,4},{8,10},{10,8},{12,14},{14,12},{16,18},{18,... | collective-permute-start | bytes 1572872 | tf_op jit(solution)/shard_map/ppermute | solution.py:17
  142.5 18.1 %collective-permute-start.36 = (bf16[128,2048]{1,0:T(8,128)(2,1)S(1)}, bf16[128,2048]{1,0:T(8,128)(2,1)S(1)}, u32[]{:S(2)}, u32[]{:S(2)}) collective-permute-start(bf16[128,2048]{1,0:T(8,128)(2,1)S(1)} %get-tuple-element.91), channel_id=1, source_target_pairs={{0,2},{2,0},{4,6},{6,4},{8,10},{10,8},{12,14},{14,12},{16,18},{18,... | collective-permute-start | bytes 1572872 | tf_op jit(solution)/shard_map/ppermute | solution.py:17
  143.0 8.2 %collective-permute-start.40 = (bf16[64,2048]{1,0:T(8,128)(2,1)S(1)}, bf16[64,2048]{1,0:T(8,128)(2,1)S(1)}, u32[]{:S(2)}, u32[]{:S(2)}) collective-permute-start(bf16[64,2048]{1,0:T(8,128)(2,1)S(1)} %get-tuple-element.117), channel_id=1, source_target_pairs={{0,1},{1,0},{2,3},{3,2},{4,5},{5,4},{6,7},{7,6},{8,9},{9,8},{10,11... | collective-permute-start | bytes 786440 | tf_op jit(solution)/shard_map/ppermute | solution.py:17
  151.2 9.4 %collective-permute-start.41 = (bf16[64,2048]{1,0:T(8,128)(2,1)S(1)}, bf16[64,2048]{1,0:T(8,128)(2,1)S(1)}, u32[]{:S(2)}, u32[]{:S(2)}) collective-permute-start(bf16[64,2048]{1,0:T(8,128)(2,1)S(1)} %get-tuple-element.98), channel_id=1, source_target_pairs={{0,1},{1,0},{2,3},{3,2},{4,5},{5,4},{6,7},{7,6},{8,9},{9,8},{10,11... | collective-permute-start | bytes 786440 | tf_op jit(solution)/shard_map/ppermute | solution.py:17
  152.9 7.7 %collective-permute-start.44 = (bf16[64,2048]{1,0:T(8,128)(2,1)S(1)}, bf16[64,2048]{1,0:T(8,128)(2,1)S(1)}, u32[]{:S(2)}, u32[]{:S(2)}) collective-permute-start(bf16[64,2048]{1,0:T(8,128)(2,1)S(1)} %get-tuple-element.118), channel_id=1, source_target_pairs={{0,4},{2,6},{4,0},{6,2},{8,12},{10,14},{12,8},{14,10},{16,20},{18,... | collective-permute-start | bytes 786440 | tf_op jit(solution)/shard_map/ppermute | solution.py:17
  160.8 6.9 %collective-permute-start.46 = (bf16[64,2048]{1,0:T(8,128)(2,1)S(1)}, bf16[64,2048]{1,0:T(8,128)(2,1)S(1)}, u32[]{:S(2)}, u32[]{:S(2)}) collective-permute-start(bf16[64,2048]{1,0:T(8,128)(2,1)S(1)} %add_convert_fusion), channel_id=1, source_target_pairs={{0,8},{2,10},{4,12},{6,14},{8,0},{10,2},{12,4},{14,6},{16,24},{18,... | collective-permute-start | bytes 786440 | tf_op jit(solution)/shard_map/ppermute | solution.py:17
  161.0 6.7 %collective-permute-start.42 = (bf16[64,2048]{1,0:T(8,128)(2,1)S(1)}, bf16[64,2048]{1,0:T(8,128)(2,1)S(1)}, u32[]{:S(2)}, u32[]{:S(2)}) collective-permute-start(bf16[64,2048]{1,0:T(8,128)(2,1)S(1)} %get-tuple-element.99), channel_id=1, source_target_pairs={{0,1},{1,0},{2,3},{3,2},{4,5},{5,4},{6,7},{7,6},{8,9},{9,8},{10,11... | collective-permute-start | bytes 786440 | tf_op jit(solution)/shard_map/ppermute | solution.py:17
  161.5 6.4 %collective-permute-start.45 = (bf16[64,2048]{1,0:T(8,128)(2,1)S(1)}, bf16[64,2048]{1,0:T(8,128)(2,1)S(1)}, u32[]{:S(2)}, u32[]{:S(2)}) collective-permute-start(bf16[64,2048]{1,0:T(8,128)(2,1)S(1)} %get-tuple-element.102), channel_id=1, source_target_pairs={{0,4},{2,6},{4,0},{6,2},{8,12},{10,14},{12,8},{14,10},{16,20},{18,... | collective-permute-start | bytes 786440 | tf_op jit(solution)/shard_map/ppermute | solution.py:17
  168.0 7.4 %collective-permute-start.47 = (bf16[32,2048]{1,0:T(8,128)(2,1)S(1)}, bf16[32,2048]{1,0:T(8,128)(2,1)S(1)}, u32[]{:S(2)}, u32[]{:S(2)}) collective-permute-start(bf16[32,2048]{1,0:T(8,128)(2,1)S(1)} %add_convert_fusion.9), channel_id=1, source_target_pairs={{0,16},{2,18},{4,20},{6,22},{8,24},{10,26},{12,28},{14,30},{16,0},... | collective-permute-start | bytes 393224 | tf_op jit(solution)/shard_map/ppermute | solution.py:17

commit v12 on v11

--- a/solution.py
+++ b/solution.py
@@ -599,7 +599,7 @@
         if c == 1:
             second = pack(place, [[across_own], [tie(across_near, near_other)]])
             second_other = swap(second, "expert", 1)
-            across_last = tie(across_last, w_down, second_other)
+            across_last = tie(across_last, w_down, second_other, near_terms, *hidden[0][1:])
             last_other = swap(across_last, "expert", 1)
             size = tokens.shape[0]
             x.append([])
@@ -614,12 +614,12 @@
         own, chunk_slope, chunk_act = forward_in(place, x[c], w_in)
         if c == 0:
             w_down = dequant(place, down_codes, tie(down_low, own), down_high, halves)
+            near_terms = swap(tie(terms, w_down), "expert", 4)
         hidden.append([own] + [swap(own, "half", d) for d in parts if d])
         slope.append(chunk_slope)
         act.append(chunk_act)
-    terms = tie(terms, hidden[1][0])
-    for distance in (4, 2):
-        terms = jnp.concatenate([terms, swap(terms, "expert", distance)], axis=0)
+    terms = jnp.concatenate([terms, tie(near_terms, hidden[1][0])], axis=0)
+    terms = jnp.concatenate([terms, swap(terms, "expert", 2)], axis=0)
     terms = (terms, swap(terms, "expert", 1))
 
     sums = []

time: 176 us -> 178 us (1.011)
  waiting for transfers between devices: 58.6 us -> 66 us
  starting transfers between devices: 50.1 us -> 44.6 us
    ppermute x48, waiting for transfers between devices: 58.6 us -> 66 us  [swap(): return lax.ppermute(array, axis, [(i, i ^ distance) for i in range(size)])]
    ppermute x48, starting transfers between devices: 50.1 us -> 44.6 us  [swap(): return lax.ppermute(array, axis, [(i, i ^ distance) for i in range(size)])]
    unnamed x28 -> x26, local copies, waits for them, and re-layouts: 4.29 us -> 4.29 us
  transfers between devices with their start and end apart: 48 -> 48, of which waited for: 30 -> 31; matrix products, arithmetic and copies ran while one was open for 2% -> 2% of each run, Pallas kernels for 29% -> 26%
where the time goes in v12:
time: 178 us
  waiting for transfers between devices  66 us (37%)
  Pallas kernels  60.1 us (34%)
  starting transfers between devices  44.6 us (25%)
  local copies, waits for them, and re-layouts  4.32 us (2%)
  other arithmetic  1.98 us (1%)
    ppermute x48, waiting for transfers between devices, swap(): return lax.ppermute(array, axis, [(i, i ^ distance) for i in range(size)])  66 us
    pallas_call x20, Pallas kernels, call(): pl.pallas_call(kernel, grid_spec=pltpu.PrefetchScalarGridSpec(num_scalar_...  60.1 us
    ppermute x48, starting transfers between devices, swap(): return lax.ppermute(array, axis, [(i, i ^ distance) for i in range(size)])  44.6 us
    unnamed x26, local copies, waits for them, and re-layouts  4.29 us
  transfers between devices with their start and end apart: 48, of which 31 were waited for; matrix products, arithmetic and copies ran while one was open for 2% of the time, Pallas kernels for 26%

profile of v12, /device:TPU:0, one launch (start us, length us, event | category | flops | bytes accessed | tf_op | source)
XLA Modules:
  0.0 178.2 jit_solution(3603402736588852837)
XLA Ops:
  0.6 3.0 %collective-permute-start.1 = (bf16[32,4096]{1,0:T(8,128)(2,1)}, bf16[32,4096]{1,0:T(8,128)(2,1)S(1)}, u32[]{:S(2)}, u32[]{:S(2)}) collective-permute-start(bf16[32,4096]{1,0:T(8,128)(2,1)} %refs_0_.1), channel_id=1, source_target_pairs={{0,4},{2,6},{4,0},{6,2},{8,12},{10,14},{12,8},{14,10},{16,20},{18,... | collective-permute-start | bytes 786440 | tf_op jit(solution)/shard_map/ppermute | solution.py:17
  3.6 2.6 %collective-permute-start = (bf16[32,4096]{1,0:T(8,128)(2,1)}, bf16[32,4096]{1,0:T(8,128)(2,1)S(1)}, u32[]{:S(2)}, u32[]{:S(2)}) collective-permute-start(bf16[32,4096]{1,0:T(8,128)(2,1)} %refs_0_.1), channel_id=1, source_target_pairs={{0,16},{2,18},{4,20},{6,22},{8,24},{10,26},{12,28},{14,30},{16,0},... | collective-permute-start | bytes 786440 | tf_op jit(solution)/shard_map/ppermute | solution.py:17
  6.2 1.6 collective-permute-start.3
  10.6 0.9 copy-done.1
  11.5 0.9 copy-done.2
  12.4 6.2 %shard_map.122.refs_4_.refs_8_.refs_3_ = bf16[4096,1536]{1,0:T(8,128)(2,1)S(1)} custom-call(s32[2]{0:T(128)S(1)} %pad_add_fusion.place_ref, bf16[2,4096,768]{2,1,0:T(8,128)(2,1)} %bitcast.7, f32[2,32,768]{2,1,0:T(8,128)S(1)} %bitcast.13, f32[2,32,768]{2,1,0:T(8,128)S(1)} %bitcast.14), custom_call_target="tpu_custom_call" | custom-call | bytes 25 | tf_op jit(solution)/shard_map/pallas_call | solution.py:112
  19.4 1.4 collective-permute-start.4
  21.3 6.8 %collective-permute-done.4.refs_1_ = bf16[32,4096]{1,0:T(8,128)(2,1)S(1)} collective-permute-done((bf16[32,4096]{1,0:T(8,128)(2,1)S(1)}, bf16[32,4096]{1,0:T(8,128)(2,1)S(1)}, u32[]{:S(2)}, u32[]{:S(2)}) %collective-permute-start.4) | collective-permute-done | bytes 262176 | tf_op jit(solution)/shard_map/ppermute | solution.py:17
  28.1 1.0 collective-permute-done.5.refs_1_
  31.4 4.1 %shard_map.124 = (bf16[256,768]{1,0:T(8,128)(2,1)S(1)}, f32[256,768]{1,0:T(8,128)S(1)}, f32[256,768]{1,0:T(8,128)S(1)}) custom-call(s32[2]{0:T(128)S(1)} %pad_add_fusion.place_ref, bf16[96,4096]{1,0:T(8,128)(2,1)S(1)} %shard_map.123.refs_0_, bf16[32,4096]{1,0:T(8,128)(2,1)S(1)} %collective-permute-done.4.refs_1_, ...), custom_call_target="tpu_custom_call" | custom-call | flops 3221 | bytes 16 | tf_op jit(solution)/shard_map/pallas_call | solution.py:112
  35.5 1.6 collective-permute-start.8
  37.2 2.4 %shard_map.125.refs_2_.refs_6_ = bf16[1536,2048]{1,0:T(8,128)(2,1)S(1)} custom-call(s32[2]{0:T(128)S(1)} %pad_add_fusion.place_ref, bf16[1,1536,2048]{2,1,0:T(8,128)(2,1)S(1)} %bitcast.11, f32[1,12,2048]{2,1,0:T(8,128)S(1)} %copy.17.low_ref, f32[1,12,2048]{2,1,0:T(8,128)S(1)} %copy.18.high_ref), custom_call_target="tpu_custom_call" | custom-call | bytes 12 | tf_op jit(solution)/shard_map/pallas_call | solution.py:112
  40.5 3.6 %collective-permute-done.10.refs_1_.refs_3_.refs_5_.refs_7_ = bf16[64,4096]{1,0:T(8,128)(2,1)S(1)} collective-permute-done((bf16[64,4096]{1,0:T(8,128)(2,1)S(1)}, bf16[64,4096]{1,0:T(8,128)(2,1)S(1)}, u32[]{:S(2)}, u32[]{:S(2)}) %collective-permute-start.10) | collective-permute-done | bytes 524320 | tf_op jit(solution)/shard_map/ppermute | solution.py:17
  44.1 2.9 %collective-permute-done.8.refs_1_ = bf16[256,768]{1,0:T(8,128)(2,1)S(1)} collective-permute-done((bf16[256,768]{1,0:T(8,128)(2,1)S(1)}, bf16[256,768]{1,0:T(8,128)(2,1)S(1)}, u32[]{:S(2)}, u32[]{:S(2)}) %collective-permute-start.8) | collective-permute-done | bytes 393248 | tf_op jit(solution)/shard_map/ppermute | solution.py:17
  47.0 1.9 %collective-permute-done.12.refs_5_.refs_7_.refs_9_.refs_11_ = bf16[64,4096]{1,0:T(8,128)(2,1)S(1)} collective-permute-done((bf16[64,4096]{1,0:T(8,128)(2,1)S(1)}, bf16[64,4096]{1,0:T(8,128)(2,1)S(1)}, u32[]{:S(2)}, u32[]{:S(2)}) %collective-permute-start.12) | collective-permute-done | bytes 524320 | tf_op jit(solution)/shard_map/ppermute | solution.py:17
  48.9 4.1 %shard_map.128 = (bf16[256,768]{1,0:T(8,128)(2,1)S(1)}, f32[256,768]{1,0:T(8,128)S(1)}, f32[256,768]{1,0:T(8,128)S(1)}) custom-call(s32[2]{0:T(128)S(1)} %pad_add_fusion.place_ref, bf16[64,4096]{1,0:T(8,128)(2,1)S(1)} %shard_map.126.refs_0_.refs_2_.refs_4_.refs_6_, bf16[64,4096]{1,0:T(8,128)(2,1)S(1)} %collective-permute-done.10.refs_1_.refs_3_.refs_5_.refs_7_, ...), custom_call_target="tpu_custom_call" | custom-call | flops 3221 | bytes 18 | tf_op jit(solution)/shard_map/pallas_call | solution.py:112
  53.0 1.6 collective-permute-start.16
  54.6 1.1 collective-permute-start.13
  55.7 2.8 %collective-permute-done.13 = bf16[128,128]{1,0:T(8,128)(2,1)S(1)} collective-permute-done((bf16[128,128]{1,0:T(8,128)(2,1)S(1)}, bf16[128,128]{1,0:T(8,128)(2,1)S(1)}, u32[]{:S(2)}, u32[]{:S(2)}) %collective-permute-start.13) | collective-permute-done | bytes 32800 | tf_op jit(solution)/shard_map/ppermute | solution.py:17
  58.5 1.2 collective-permute-done.14.refs_4_.refs_5_
  59.7 2.3 %shard_map.129 = (bf16[128,2048]{1,0:T(8,128)(2,1)S(1)}, bf16[128,2048]{1,0:T(8,128)(2,1)S(1)}) custom-call(s32[2]{0:T(128)S(1)} %pad_add_fusion.place_ref, bf16[256,768]{1,0:T(8,128)(2,1)S(1)} %get-tuple-element.61.refs_0_, bf16[256,768]{1,0:T(8,128)(2,1)S(1)} %collective-permute-done.8.refs_1_, bf16[1536,2048]{1,0:T(8,128)(2,1)S(1)} %shard_map.125.refs_2_.refs_6_, ...), custom_call_target="tpu_custom_call" | custom-call | flops 1610 | bytes 8 | tf_op jit(solution)/shard_map/pallas_call | solution.py:112
  62.1 2.1 %collective-permute-done.16.refs_1_ = bf16[256,768]{1,0:T(8,128)(2,1)S(1)} collective-permute-done((bf16[256,768]{1,0:T(8,128)(2,1)S(1)}, bf16[256,768]{1,0:T(8,128)(2,1)S(1)}, u32[]{:S(2)}, u32[]{:S(2)}) %collective-permute-start.16) | collective-permute-done | bytes 393248 | tf_op jit(solution)/shard_map/ppermute | solution.py:17
  64.2 2.3 %shard_map.130 = (bf16[128,2048]{1,0:T(8,128)(2,1)S(1)}, bf16[128,2048]{1,0:T(8,128)(2,1)S(1)}) custom-call(s32[2]{0:T(128)S(1)} %pad_add_fusion.place_ref, bf16[256,768]{1,0:T(8,128)(2,1)S(1)} %get-tuple-element.66.refs_0_, bf16[256,768]{1,0:T(8,128)(2,1)S(1)} %collective-permute-done.16.refs_1_, bf16[1536,2048]{1,0:T(8,128)(2,1)S(1)} %shard_map.125.refs_2_.refs_6_, ...), custom_call_target="tpu_custom_call" | custom-call | flops 1610 | bytes 8 | tf_op jit(solution)/shard_map/pallas_call | solution.py:112
  67.1 1.4 collective-permute-done.17
  68.6 1.2 collective-permute-start.18
  69.8 0.9 collective-permute-start.19
  70.7 4.2 %collective-permute-done.18 = bf16[64,1024]{1,0:T(8,128)(2,1)S(1)} collective-permute-done((bf16[64,1024]{1,0:T(8,128)(2,1)S(1)}, bf16[64,1024]{1,0:T(8,128)(2,1)S(1)}, u32[]{:S(2)}, u32[]{:S(2)}) %collective-permute-start.18) | collective-permute-done | bytes 131104 | tf_op jit(solution)/shard_map/ppermute | solution.py:17
  75.0 2.0 %collective-permute-done.19 = bf16[64,1024]{1,0:T(8,128)(2,1)S(1)} collective-permute-done((bf16[64,1024]{1,0:T(8,128)(2,1)S(1)}, bf16[64,1024]{1,0:T(8,128)(2,1)S(1)}, u32[]{:S(2)}, u32[]{:S(2)}) %collective-permute-start.19) | collective-permute-done | bytes 131104 | tf_op jit(solution)/shard_map/ppermute | solution.py:17
  77.0 1.1 collective-permute-start.20
  79.1 1.3 collective-permute-start.23
  80.4 3.8 %collective-permute-done.21 = bf16[64,1024]{1,0:T(8,128)(2,1)S(1)} collective-permute-done((bf16[64,1024]{1,0:T(8,128)(2,1)S(1)}, bf16[64,1024]{1,0:T(8,128)(2,1)S(1)}, u32[]{:S(2)}, u32[]{:S(2)}) %collective-permute-start.21) | collective-permute-done | bytes 131104 | tf_op jit(solution)/shard_map/ppermute | solution.py:17
  84.2 1.4 collective-permute-done.23
  85.7 2.7 %collective-permute-start.22 = (bf16[32,1024]{1,0:T(8,128)(2,1)S(1)}, bf16[32,1024]{1,0:T(8,128)(2,1)S(1)}, u32[]{:S(2)}, u32[]{:S(2)}) collective-permute-start(bf16[32,1024]{1,0:T(8,128)(2,1)S(1)} %get-tuple-element.115), channel_id=1, source_target_pairs={{0,16},{2,18},{4,20},{6,22},{8,24},{10,26},{12,28},{14,30},{16,0},... | collective-permute-start | bytes 196616 | tf_op jit(solution)/shard_map/ppermute | solution.py:17
  88.6 3.8 %collective-permute-done.22 = bf16[32,1024]{1,0:T(8,128)(2,1)S(1)} collective-permute-done((bf16[32,1024]{1,0:T(8,128)(2,1)S(1)}, bf16[32,1024]{1,0:T(8,128)(2,1)S(1)}, u32[]{:S(2)}, u32[]{:S(2)}) %collective-permute-start.22) | collective-permute-done | bytes 65568 | tf_op jit(solution)/shard_map/ppermute | solution.py:17
  92.4 1.8 collective-permute-done.24
  94.5 2.8 %collective-permute-start.26 = (bf16[32,1024]{1,0:T(8,128)(2,1)S(1)}, bf16[32,1024]{1,0:T(8,128)(2,1)S(1)}, u32[]{:S(2)}, u32[]{:S(2)}) collective-permute-start(bf16[32,1024]{1,0:T(8,128)(2,1)S(1)} %get-tuple-element.112.refs_1_), channel_id=1, source_target_pairs={{0,16},{2,18},{4,20},{6,22},{8,24},{10,26},{12,28},{14,30},{16,0},... | collective-permute-start | bytes 196616 | tf_op jit(solution)/shard_map/ppermute | solution.py:17
  97.3 2.5 %collective-permute-done.25.refs_2_ = bf16[32,1024]{1,0:T(8,128)(2,1)S(1)} collective-permute-done((bf16[32,1024]{1,0:T(8,128)(2,1)S(1)}, bf16[32,1024]{1,0:T(8,128)(2,1)S(1)}, u32[]{:S(2)}, u32[]{:S(2)}) %collective-permute-start.25) | collective-permute-done | bytes 65568 | tf_op jit(solution)/shard_map/ppermute | solution.py:17
  101.1 1.3 collective-permute-start.27
  102.4 0.9 collective-permute-start.28
  103.3 4.2 %collective-permute-done.27.refs_1_ = bf16[64,2048]{1,0:T(8,128)(2,1)S(1)} collective-permute-done((bf16[64,2048]{1,0:T(8,128)(2,1)S(1)}, bf16[64,2048]{1,0:T(8,128)(2,1)S(1)}, u32[]{:S(2)}, u32[]{:S(2)}) %collective-permute-start.27) | collective-permute-done | bytes 262176 | tf_op jit(solution)/shard_map/ppermute | solution.py:17
  107.5 1.3 collective-permute-done.28.refs_0_
  108.8 0.9 collective-permute-start.32
  110.3 2.4 %shard_map.132 = (bf16[256,2048]{1,0:T(8,128)(2,1)S(1)}, f32[256,768]{1,0:T(8,128)S(1)}, bf16[256,768]{1,0:T(8,128)(2,1)S(1)}) custom-call(s32[2]{0:T(128)S(1)} %pad_add_fusion.place_ref, bf16[64,2048]{1,0:T(8,128)(2,1)S(1)} %shard_map.131.refs_0_, bf16[64,2048]{1,0:T(8,128)(2,1)S(1)} %collective-permute-done.27.refs_1_, ...), custom_call_target="tpu_custom_call" | custom-call | flops 1610 | bytes 9 | tf_op jit(solution)/shard_map/pallas_call | solution.py:112
  112.7 1.6 collective-permute-start.31
  114.3 3.2 %collective-permute-done.32.refs_1_ = bf16[64,2048]{1,0:T(8,128)(2,1)S(1)} collective-permute-done((bf16[64,2048]{1,0:T(8,128)(2,1)S(1)}, bf16[64,2048]{1,0:T(8,128)(2,1)S(1)}, u32[]{:S(2)}, u32[]{:S(2)}) %collective-permute-start.32) | collective-permute-done | bytes 262176 | tf_op jit(solution)/shard_map/ppermute | solution.py:17
  117.5 4.1 %shard_map.134.refs_4_ = f32[2,12,2048]{2,1,0:T(8,128)S(1)} custom-call(s32[2]{0:T(128)S(1)} %pad_add_fusion.place_ref, bf16[256,768]{1,0:T(8,128)(2,1)S(1)} %get-tuple-element.61.refs_0_, bf16[256,768]{1,0:T(8,128)(2,1)S(1)} %collective-permute-done.8.refs_1_, bf16[256,2048]{1,0:T(8,128)(2,1)S(1)} %get-tuple-element.80.refs_2_, ...), custom_call_target="tpu_custom_call" | custom-call | flops 1610 | bytes 8 | tf_op jit(solution)/shard_map/pallas_call | solution.py:112
  121.6 2.3 %collective-permute-done.31.refs_0_ = bf16[256,768]{1,0:T(8,128)(2,1)S(1)} collective-permute-done((bf16[256,768]{1,0:T(8,128)(2,1)S(1)}, bf16[256,768]{1,0:T(8,128)(2,1)S(1)}, u32[]{:S(2)}, u32[]{:S(2)}) %collective-permute-start.31) | collective-permute-done | bytes 393248 | tf_op jit(solution)/shard_map/ppermute | solution.py:17
  124.0 2.4 %shard_map.135 = (bf16[256,2048]{1,0:T(8,128)(2,1)S(1)}, f32[256,768]{1,0:T(8,128)S(1)}, bf16[256,768]{1,0:T(8,128)(2,1)S(1)}) custom-call(s32[2]{0:T(128)S(1)} %pad_add_fusion.place_ref, bf16[64,2048]{1,0:T(8,128)(2,1)S(1)} %collective-permute-done.28.refs_0_, bf16[64,2048]{1,0:T(8,128)(2,1)S(1)} %collective-permute-done.32.refs_1_, ...), custom_call_target="tpu_custom_call" | custom-call | flops 1610 | bytes 9 | tf_op jit(solution)/shard_map/pallas_call | solution.py:112
  126.4 1.6 collective-permute-start.35
  128.0 4.0 %shard_map.136 = f32[2,12,2048]{2,1,0:T(8,128)S(1)} custom-call(s32[2]{0:T(128)S(1)} %pad_add_fusion.place_ref, bf16[256,768]{1,0:T(8,128)(2,1)S(1)} %get-tuple-element.66.refs_0_, bf16[256,768]{1,0:T(8,128)(2,1)S(1)} %collective-permute-done.16.refs_1_, bf16[256,2048]{1,0:T(8,128)(2,1)S(1)} %get-tuple-element.86.refs_2_, ...), custom_call_target="tpu_custom_call" | custom-call | flops 1610 | bytes 8 | tf_op jit(solution)/shard_map/pallas_call | solution.py:112
  132.0 4.0 %shard_map.133 = (bf16[256,1536]{1,0:T(8,128)(2,1)S(1)}, bf16[128,2048]{1,0:T(8,128)(2,1)S(1)}, bf16[128,2048]{1,0:T(8,128)(2,1)S(1)}, bf16[128,2048]{1,0:T(8,128)(2,1)S(1)}, bf16[128,2048]{1,0:T(8,128)(2,1)S(1)}) custom-call(s32[2]{0:T(128)S(1)} %pad_add_fusion.place_ref, f32[256,768]{1,0:T(8,128)S(1)} %get-tuple-element.75.grad_own_ref, ...), custom_call_target="tpu_custom_call" | custom-call | flops 3221 | bytes 18 | tf_op jit(solution)/shard_map/pallas_call | solution.py:112
  136.8 4.0 %shard_map.137 = (bf16[256,1536]{1,0:T(8,128)(2,1)S(1)}, bf16[128,2048]{1,0:T(8,128)(2,1)S(1)}, bf16[128,2048]{1,0:T(8,128)(2,1)S(1)}, bf16[128,2048]{1,0:T(8,128)(2,1)S(1)}, bf16[128,2048]{1,0:T(8,128)(2,1)S(1)}) custom-call(s32[2]{0:T(128)S(1)} %pad_add_fusion.place_ref, f32[256,768]{1,0:T(8,128)S(1)} %get-tuple-element.83.grad_own_ref, ...), custom_call_target="tpu_custom_call" | custom-call | flops 3221 | bytes 18 | tf_op jit(solution)/shard_map/pallas_call | solution.py:112
  141.4 1.4 collective-permute-done.38
  142.9 0.9 collective-permute-start.39
  144.4 1.5 collective-permute-start.40
  145.9 5.4 %collective-permute-done.39 = bf16[64,2048]{1,0:T(8,128)(2,1)S(1)} collective-permute-done((bf16[64,2048]{1,0:T(8,128)(2,1)S(1)}, bf16[64,2048]{1,0:T(8,128)(2,1)S(1)}, u32[]{:S(2)}, u32[]{:S(2)}) %collective-permute-start.39) | collective-permute-done | bytes 262176 | tf_op jit(solution)/shard_map/ppermute | solution.py:17
  151.5 1.1 collective-permute-done.40
  152.6 1.5 collective-permute-start.41
  154.3 1.2 collective-permute-start.44
  155.5 6.6 %shard_map.138.refs_15_ = f32[4,32,768]{2,1,0:T(8,128)} custom-call(s32[2]{0:T(128)S(1)} %pad_add_fusion.place_ref, bf16[96,4096]{1,0:T(8,128)(2,1)S(1)} %shard_map.123.refs_0_, bf16[32,4096]{1,0:T(8,128)(2,1)S(1)} %collective-permute-done.4.refs_1_, bf16[96,4096]{1,0:T(8,128)(2,1)S(1)} %collective-permute-done.6.refs_2_, ...), custom_call_target="tpu_custom_call" | custom-call | flops 3221 | bytes 20 | tf_op jit(solution)/shard_map/pallas_call | solution.py:112
  163.6 0.9 collective-permute-start.45
  164.5 4.2 %shard_map.139.refs_15_ = f32[4,32,768]{2,1,0:T(8,128)} custom-call(s32[2]{0:T(128)S(1)} %pad_add_fusion.place_ref, bf16[96,4096]{1,0:T(8,128)(2,1)S(1)} %shard_map.123.refs_0_, bf16[32,4096]{1,0:T(8,128)(2,1)S(1)} %collective-permute-done.4.refs_1_, bf16[96,4096]{1,0:T(8,128)(2,1)S(1)} %collective-permute-done.6.refs_2_, ...), custom_call_target="tpu_custom_call", output_to_operand_aliasing={{}: (16, {})} | custom-call | flops 1610 | bytes 20 | tf_op jit(solution)/shard_map/pallas_call | solution.py:112
  170.1 2.3 %collective-permute-start.47 = (bf16[32,2048]{1,0:T(8,128)(2,1)S(1)}, bf16[32,2048]{1,0:T(8,128)(2,1)S(1)}, u32[]{:S(2)}, u32[]{:S(2)}) collective-permute-start(bf16[32,2048]{1,0:T(8,128)(2,1)S(1)} %add_convert_fusion.9), channel_id=1, source_target_pairs={{0,16},{2,18},{4,20},{6,22},{8,24},{10,26},{12,28},{14,30},{16,0},... | collective-permute-start | bytes 393224 | tf_op jit(solution)/shard_map/ppermute | solution.py:17
  173.2 3.9 %shard_map.140 = f32[4,32,768]{2,1,0:T(8,128)} custom-call(s32[2]{0:T(128)S(1)} %pad_add_fusion.place_ref, bf16[96,4096]{1,0:T(8,128)(2,1)S(1)} %shard_map.123.refs_0_, bf16[32,4096]{1,0:T(8,128)(2,1)S(1)} %collective-permute-done.4.refs_1_, bf16[96,4096]{1,0:T(8,128)(2,1)S(1)} %collective-permute-done.6.refs_2_, ...), custom_call_target="tpu_custom_call", output_to_operand_aliasing={{}: (16, {})} | custom-call | flops 1610 | bytes 20 | tf_op jit(solution)/shard_map/pallas_call | solution.py:112
  (96 shorter events, 18.5 us)
Async XLA Ops:
  0.6 18.0 %collective-permute-start.1 = (bf16[32,4096]{1,0:T(8,128)(2,1)}, bf16[32,4096]{1,0:T(8,128)(2,1)S(1)}, u32[]{:S(2)}, u32[]{:S(2)}) collective-permute-start(bf16[32,4096]{1,0:T(8,128)(2,1)} %refs_0_.1), channel_id=1, source_target_pairs={{0,4},{2,6},{4,0},{6,2},{8,12},{10,14},{12,8},{14,10},{16,20},{18,... | collective-permute-start | bytes 786440 | tf_op jit(solution)/shard_map/ppermute | solution.py:17
  3.6 15.0 %collective-permute-start = (bf16[32,4096]{1,0:T(8,128)(2,1)}, bf16[32,4096]{1,0:T(8,128)(2,1)S(1)}, u32[]{:S(2)}, u32[]{:S(2)}) collective-permute-start(bf16[32,4096]{1,0:T(8,128)(2,1)} %refs_0_.1), channel_id=1, source_target_pairs={{0,16},{2,18},{4,20},{6,22},{8,24},{10,26},{12,28},{14,30},{16,0},... | collective-permute-start | bytes 786440 | tf_op jit(solution)/shard_map/ppermute | solution.py:17
  6.2 12.4 %collective-permute-start.3 = (bf16[32,4096]{1,0:T(8,128)(2,1)}, bf16[32,4096]{1,0:T(8,128)(2,1)S(1)}, u32[]{:S(2)}, u32[]{:S(2)}) collective-permute-start(bf16[32,4096]{1,0:T(8,128)(2,1)} %refs_0_.1), channel_id=1, source_target_pairs={{0,8},{2,10},{4,12},{6,14},{8,0},{10,2},{12,4},{14,6},{16,24},{18,... | collective-permute-start | bytes 786440 | tf_op jit(solution)/shard_map/ppermute | solution.py:17
  10.2 8.5 %collective-permute-start.2 = (bf16[32,128]{1,0:T(8,128)(2,1)S(1)}, bf16[32,128]{1,0:T(8,128)(2,1)S(1)}, u32[]{:S(2)}, u32[]{:S(2)}) collective-permute-start(bf16[32,128]{1,0:T(8,128)(2,1)S(1)} %shard_map.121), channel_id=1, source_target_pairs={{0,16},{2,18},{4,20},{6,22},{8,24},{10,26},{12,28},{14,30},{16,0},... | collective-permute-start | bytes 24584 | tf_op jit(solution)/shard_map/ppermute | solution.py:17
  10.6 0.9 copy-start.1
  11.5 0.9 copy-start.2
  12.4 6.3 %copy-start = (bf16[32,4096]{1,0:T(8,128)(2,1)S(1)}, bf16[32,4096]{1,0:T(8,128)(2,1)}, u32[]{:S(2)}) copy-start(bf16[32,4096]{1,0:T(8,128)(2,1)} %refs_0_.1) | copy-start | bytes 786436
  18.6 18.5 %copy-start.4 = (f32[1,12,2048]{2,0,1:T(1,128)S(1)}, f32[1,12,2048]{2,0,1:T(1,128)}, u32[]{:S(2)}) copy-start(f32[1,12,2048]{2,0,1:T(1,128)} %param.19) | copy-start | bytes 294916
  18.6 18.6 %copy-start.5 = (f32[1,12,2048]{2,0,1:T(1,128)S(1)}, f32[1,12,2048]{2,0,1:T(1,128)}, u32[]{:S(2)}) copy-start(f32[1,12,2048]{2,0,1:T(1,128)} %param.18) | copy-start | bytes 294916
  18.6 18.6 %slice-start.3 = ((s8[6291456]{0:T(1024)(128)(4,1)}), s8[4194304]{0:T(1024)(128)(4,1)S(1)}, s32[]{:S(2)}) async-start(s8[6291456]{0:T(1024)(128)(4,1)} %bitcast.10), calls=%async_computation.3 | async-start | bytes 8388608
  19.3 12.2 %collective-permute-start.6 = (bf16[96,4096]{1,0:T(8,128)(2,1)S(1)}, bf16[96,4096]{1,0:T(8,128)(2,1)S(1)}, u32[]{:S(2)}, u32[]{:S(2)}) collective-permute-start(bf16[96,4096]{1,0:T(8,128)(2,1)S(1)} %shard_map.123.refs_0_), channel_id=1, source_target_pairs={{0,2},{2,0},{4,6},{6,4},{8,10},{10,8},{12,14},{14,12},{16,18},{18,... | collective-permute-start | bytes 2359304 | tf_op jit(solution)/shard_map/ppermute | solution.py:17
  19.4 8.7 %collective-permute-start.4 = (bf16[32,4096]{1,0:T(8,128)(2,1)S(1)}, bf16[32,4096]{1,0:T(8,128)(2,1)S(1)}, u32[]{:S(2)}, u32[]{:S(2)}) collective-permute-start(bf16[32,4096]{1,0:T(8,128)(2,1)S(1)} %collective-permute-done.refs_1_.refs_0_), channel_id=1, source_target_pairs={{0,8},{2,10},{4,12},{6,14},{8,0},{10,2},{12,4},{14,6},{16,24},{18,... | collective-permute-start | bytes 786440 | tf_op jit(solution)/shard_map/ppermute | solution.py:17
  20.7 8.4 %collective-permute-start.5 = (bf16[32,4096]{1,0:T(8,128)(2,1)S(1)}, bf16[32,4096]{1,0:T(8,128)(2,1)S(1)}, u32[]{:S(2)}, u32[]{:S(2)}) collective-permute-start(bf16[32,4096]{1,0:T(8,128)(2,1)S(1)} %collective-permute-done.3.refs_2_), channel_id=1, source_target_pairs={{0,4},{2,6},{4,0},{6,2},{8,12},{10,14},{12,8},{14,10},{16,20},{18,... | collective-permute-start | bytes 786440 | tf_op jit(solution)/shard_map/ppermute | solution.py:17
  29.1 1.5 collective-permute-start.7
  29.7 14.4 %collective-permute-start.10 = (bf16[64,4096]{1,0:T(8,128)(2,1)S(1)}, bf16[64,4096]{1,0:T(8,128)(2,1)S(1)}, u32[]{:S(2)}, u32[]{:S(2)}) collective-permute-start(bf16[64,4096]{1,0:T(8,128)(2,1)S(1)} %shard_map.127), channel_id=1, source_target_pairs={{0,4},{2,6},{4,0},{6,2},{8,12},{10,14},{12,8},{14,10},{16,20},{18,... | collective-permute-start | bytes 1572872 | tf_op jit(solution)/shard_map/ppermute | solution.py:17
  31.2 6.0 %slice-start.4 = ((s8[6291456]{0:T(1024)(128)(4,1)}), s8[2097152]{0:T(1024)(128)(4,1)S(1)}, s32[]{:S(2)}) async-start(s8[6291456]{0:T(1024)(128)(4,1)} %bitcast.10), calls=%async_computation.4 | async-start | bytes 4194304
  31.2 12.9 %collective-permute-start.11 = (bf16[64,4096]{1,0:T(8,128)(2,1)S(1)}, bf16[64,4096]{1,0:T(8,128)(2,1)S(1)}, u32[]{:S(2)}, u32[]{:S(2)}) collective-permute-start(bf16[64,4096]{1,0:T(8,128)(2,1)S(1)} %shard_map.126.refs_0_.refs_2_.refs_4_.refs_6_), channel_id=1, source_target_pairs={{0,2},{2,0},{4,6},{6,4},{8,10},{10,8},{12,14},{14,12},{16,18},{18,... | collective-permute-start | bytes 1572872 | tf_op jit(solution)/shard_map/ppermute | solution.py:17
  35.5 11.5 %collective-permute-start.8 = (bf16[256,768]{1,0:T(8,128)(2,1)S(1)}, bf16[256,768]{1,0:T(8,128)(2,1)S(1)}, u32[]{:S(2)}, u32[]{:S(2)}) collective-permute-start(bf16[256,768]{1,0:T(8,128)(2,1)S(1)} %get-tuple-element.61.refs_0_), channel_id=1, source_target_pairs={{0,1},{1,0},{2,3},{3,2},{4,5},{5,4},{6,7},{7,6},{8,9},{9,8},{10,11... | collective-permute-start | bytes 1179656 | tf_op jit(solution)/shard_map/ppermute | solution.py:17
  39.7 4.4 %collective-permute-start.9 = (bf16[64,128]{1,0:T(8,128)(2,1)S(1)}, bf16[64,128]{1,0:T(8,128)(2,1)S(1)}, u32[]{:S(2)}, u32[]{:S(2)}) collective-permute-start(bf16[64,128]{1,0:T(8,128)(2,1)S(1)} %pad_maximum_fusion.2), channel_id=1, source_target_pairs={{0,8},{2,10},{4,12},{6,14},{8,0},{10,2},{12,4},{14,6},{16,24},{18,... | collective-permute-start | bytes 49160 | tf_op jit(solution)/shard_map/ppermute | solution.py:17
  47.0 1.9 %collective-permute-start.12 = (bf16[64,4096]{1,0:T(8,128)(2,1)S(1)}, bf16[64,4096]{1,0:T(8,128)(2,1)S(1)}, u32[]{:S(2)}, u32[]{:S(2)}) collective-permute-start(bf16[64,4096]{1,0:T(8,128)(2,1)S(1)} %collective-permute-done.10.refs_1_.refs_3_.refs_5_.refs_7_), channel_id=1, source_target_pairs={{0,2},{2,0},{4,6},{6,4},{8,10},{10,8},{12,14},{14,12},{16,18},{18,... | collective-permute-start | bytes 1572872 | tf_op jit(solution)/shard_map/ppermute | solution.py:17
  53.0 41.3 %copy-start.3 = (bf16[32,2048]{1,0:T(8,128)(2,1)S(1)}, bf16[32,2048]{1,0:T(8,128)(2,1)}, u32[]{:S(2)}) copy-start(bf16[32,2048]{1,0:T(8,128)(2,1)} %param.11) | copy-start | bytes 393220
  53.0 11.2 %collective-permute-start.16 = (bf16[256,768]{1,0:T(8,128)(2,1)S(1)}, bf16[256,768]{1,0:T(8,128)(2,1)S(1)}, u32[]{:S(2)}, u32[]{:S(2)}) collective-permute-start(bf16[256,768]{1,0:T(8,128)(2,1)S(1)} %get-tuple-element.66.refs_0_), channel_id=1, source_target_pairs={{0,1},{1,0},{2,3},{3,2},{4,5},{5,4},{6,7},{7,6},{8,9},{9,8},{10,11... | collective-permute-start | bytes 1179656 | tf_op jit(solution)/shard_map/ppermute | solution.py:17
  54.6 3.9 %collective-permute-start.13 = (bf16[128,128]{1,0:T(8,128)(2,1)S(1)}, bf16[128,128]{1,0:T(8,128)(2,1)S(1)}, u32[]{:S(2)}, u32[]{:S(2)}) collective-permute-start(bf16[128,128]{1,0:T(8,128)(2,1)S(1)} %pad_maximum_fusion.1), channel_id=1, source_target_pairs={{0,4},{2,6},{4,0},{6,2},{8,12},{10,14},{12,8},{14,10},{16,20},{18,... | collective-permute-start | bytes 98312 | tf_op jit(solution)/shard_map/ppermute | solution.py:17
  58.5 1.3 collective-permute-start.14
  66.5 2.0 %collective-permute-start.17 = (bf16[128,2048]{1,0:T(8,128)(2,1)S(1)}, bf16[128,2048]{1,0:T(8,128)(2,1)S(1)}, u32[]{:S(2)}, u32[]{:S(2)}) collective-permute-start(bf16[128,2048]{1,0:T(8,128)(2,1)S(1)} %get-tuple-element.72), channel_id=1, source_target_pairs={{0,2},{2,0},{4,6},{6,4},{8,10},{10,8},{12,14},{14,12},{16,18},{18,... | collective-permute-start | bytes 1572872 | tf_op jit(solution)/shard_map/ppermute | solution.py:17
  66.6 11.5 %collective-permute-start.15 = (bf16[128,2048]{1,0:T(8,128)(2,1)S(1)}, bf16[128,2048]{1,0:T(8,128)(2,1)S(1)}, u32[]{:S(2)}, u32[]{:S(2)}) collective-permute-start(bf16[128,2048]{1,0:T(8,128)(2,1)S(1)} %get-tuple-element.69), channel_id=1, source_target_pairs={{0,2},{2,0},{4,6},{6,4},{8,10},{10,8},{12,14},{14,12},{16,18},{18,... | collective-permute-start | bytes 1572872 | tf_op jit(solution)/shard_map/ppermute | solution.py:17
  68.6 6.4 %collective-permute-start.18 = (bf16[64,1024]{1,0:T(8,128)(2,1)S(1)}, bf16[64,1024]{1,0:T(8,128)(2,1)S(1)}, u32[]{:S(2)}, u32[]{:S(2)}) collective-permute-start(bf16[64,1024]{1,0:T(8,128)(2,1)S(1)} %get-tuple-element.125), channel_id=1, source_target_pairs={{0,4},{2,6},{4,0},{6,2},{8,12},{10,14},{12,8},{14,10},{16,20},{18,... | collective-permute-start | bytes 393224 | tf_op jit(solution)/shard_map/ppermute | solution.py:17
  69.8 7.2 %collective-permute-start.19 = (bf16[64,1024]{1,0:T(8,128)(2,1)S(1)}, bf16[64,1024]{1,0:T(8,128)(2,1)S(1)}, u32[]{:S(2)}, u32[]{:S(2)}) collective-permute-start(bf16[64,1024]{1,0:T(8,128)(2,1)S(1)} %get-tuple-element.124), channel_id=1, source_target_pairs={{0,4},{2,6},{4,0},{6,2},{8,12},{10,14},{12,8},{14,10},{16,20},{18,... | collective-permute-start | bytes 393224 | tf_op jit(solution)/shard_map/ppermute | solution.py:17
  77.0 8.6 %collective-permute-start.20 = (bf16[64,2048]{1,0:T(8,128)(2,1)S(1)}, bf16[64,2048]{1,0:T(8,128)(2,1)S(1)}, u32[]{:S(2)}, u32[]{:S(2)}) collective-permute-start(bf16[64,2048]{1,0:T(8,128)(2,1)S(1)} %add_convert_fusion.7), channel_id=1, source_target_pairs={{0,4},{2,6},{4,0},{6,2},{8,12},{10,14},{12,8},{14,10},{16,20},{18,... | collective-permute-start | bytes 786440 | tf_op jit(solution)/shard_map/ppermute | solution.py:17
  78.3 5.9 %collective-permute-start.21 = (bf16[64,1024]{1,0:T(8,128)(2,1)S(1)}, bf16[64,1024]{1,0:T(8,128)(2,1)S(1)}, u32[]{:S(2)}, u32[]{:S(2)}) collective-permute-start(bf16[64,1024]{1,0:T(8,128)(2,1)S(1)} %get-tuple-element.123), channel_id=1, source_target_pairs={{0,8},{2,10},{4,12},{6,14},{8,0},{10,2},{12,4},{14,6},{16,24},{18,... | collective-permute-start | bytes 393224 | tf_op jit(solution)/shard_map/ppermute | solution.py:17
  79.1 6.5 %collective-permute-start.23 = (bf16[64,1024]{1,0:T(8,128)(2,1)S(1)}, bf16[64,1024]{1,0:T(8,128)(2,1)S(1)}, u32[]{:S(2)}, u32[]{:S(2)}) collective-permute-start(bf16[64,1024]{1,0:T(8,128)(2,1)S(1)} %get-tuple-element.122), channel_id=1, source_target_pairs={{0,8},{2,10},{4,12},{6,14},{8,0},{10,2},{12,4},{14,6},{16,24},{18,... | collective-permute-start | bytes 393224 | tf_op jit(solution)/shard_map/ppermute | solution.py:17
  85.7 6.8 %collective-permute-start.22 = (bf16[32,1024]{1,0:T(8,128)(2,1)S(1)}, bf16[32,1024]{1,0:T(8,128)(2,1)S(1)}, u32[]{:S(2)}, u32[]{:S(2)}) collective-permute-start(bf16[32,1024]{1,0:T(8,128)(2,1)S(1)} %get-tuple-element.115), channel_id=1, source_target_pairs={{0,16},{2,18},{4,20},{6,22},{8,24},{10,26},{12,28},{14,30},{16,0},... | collective-permute-start | bytes 196616 | tf_op jit(solution)/shard_map/ppermute | solution.py:17
  88.3 5.9 %collective-permute-start.24 = (bf16[32,1024]{1,0:T(8,128)(2,1)S(1)}, bf16[32,1024]{1,0:T(8,128)(2,1)S(1)}, u32[]{:S(2)}, u32[]{:S(2)}) collective-permute-start(bf16[32,1024]{1,0:T(8,128)(2,1)S(1)} %get-tuple-element.114), channel_id=1, source_target_pairs={{0,16},{2,18},{4,20},{6,22},{8,24},{10,26},{12,28},{14,30},{16,0},... | collective-permute-start | bytes 196616 | tf_op jit(solution)/shard_map/ppermute | solution.py:17
  94.3 5.5 %collective-permute-start.25 = (bf16[32,1024]{1,0:T(8,128)(2,1)S(1)}, bf16[32,1024]{1,0:T(8,128)(2,1)S(1)}, u32[]{:S(2)}, u32[]{:S(2)}) collective-permute-start(bf16[32,1024]{1,0:T(8,128)(2,1)S(1)} %get-tuple-element.113.refs_0_), channel_id=1, source_target_pairs={{0,16},{2,18},{4,20},{6,22},{8,24},{10,26},{12,28},{14,30},{16,0},... | collective-permute-start | bytes 196616 | tf_op jit(solution)/shard_map/ppermute | solution.py:17
  94.5 6.0 %collective-permute-start.26 = (bf16[32,1024]{1,0:T(8,128)(2,1)S(1)}, bf16[32,1024]{1,0:T(8,128)(2,1)S(1)}, u32[]{:S(2)}, u32[]{:S(2)}) collective-permute-start(bf16[32,1024]{1,0:T(8,128)(2,1)S(1)} %get-tuple-element.112.refs_1_), channel_id=1, source_target_pairs={{0,16},{2,18},{4,20},{6,22},{8,24},{10,26},{12,28},{14,30},{16,0},... | collective-permute-start | bytes 196616 | tf_op jit(solution)/shard_map/ppermute | solution.py:17
  101.1 6.4 %collective-permute-start.27 = (bf16[64,2048]{1,0:T(8,128)(2,1)S(1)}, bf16[64,2048]{1,0:T(8,128)(2,1)S(1)}, u32[]{:S(2)}, u32[]{:S(2)}) collective-permute-start(bf16[64,2048]{1,0:T(8,128)(2,1)S(1)} %shard_map.131.refs_0_), channel_id=1, source_target_pairs={{0,8},{2,10},{4,12},{6,14},{8,0},{10,2},{12,4},{14,6},{16,24},{18,... | collective-permute-start | bytes 786440 | tf_op jit(solution)/shard_map/ppermute | solution.py:17
  102.4 6.4 %collective-permute-start.28 = (bf16[64,2048]{1,0:T(8,128)(2,1)S(1)}, bf16[64,2048]{1,0:T(8,128)(2,1)S(1)}, u32[]{:S(2)}, u32[]{:S(2)}) collective-permute-start(bf16[64,2048]{1,0:T(8,128)(2,1)S(1)} %shard_map.131.refs_0_), channel_id=1, source_target_pairs={{0,4},{2,6},{4,0},{6,2},{8,12},{10,14},{12,8},{14,10},{16,20},{18,... | collective-permute-start | bytes 786440 | tf_op jit(solution)/shard_map/ppermute | solution.py:17
  103.3 5.5 %collective-permute-start.29 = (bf16[64,2048]{1,0:T(8,128)(2,1)S(1)}, bf16[64,2048]{1,0:T(8,128)(2,1)S(1)}, u32[]{:S(2)}, u32[]{:S(2)}) collective-permute-start(bf16[64,2048]{1,0:T(8,128)(2,1)S(1)} %shard_map.131.refs_0_), channel_id=1, source_target_pairs={{0,2},{2,0},{4,6},{6,4},{8,10},{10,8},{12,14},{14,12},{16,18},{18,... | collective-permute-start | bytes 786440 | tf_op jit(solution)/shard_map/ppermute | solution.py:17
  108.8 1.5 collective-permute-start.30
  108.8 8.7 %collective-permute-start.32 = (bf16[64,2048]{1,0:T(8,128)(2,1)S(1)}, bf16[64,2048]{1,0:T(8,128)(2,1)S(1)}, u32[]{:S(2)}, u32[]{:S(2)}) collective-permute-start(bf16[64,2048]{1,0:T(8,128)(2,1)S(1)} %collective-permute-done.27.refs_1_), channel_id=1, source_target_pairs={{0,4},{2,6},{4,0},{6,2},{8,12},{10,14},{12,8},{14,10},{16,20},{18,... | collective-permute-start | bytes 786440 | tf_op jit(solution)/shard_map/ppermute | solution.py:17
  109.7 7.8 %collective-permute-start.33 = (bf16[64,2048]{1,0:T(8,128)(2,1)S(1)}, bf16[64,2048]{1,0:T(8,128)(2,1)S(1)}, u32[]{:S(2)}, u32[]{:S(2)}) collective-permute-start(bf16[64,2048]{1,0:T(8,128)(2,1)S(1)} %collective-permute-done.28.refs_0_), channel_id=1, source_target_pairs={{0,2},{2,0},{4,6},{6,4},{8,10},{10,8},{12,14},{14,12},{16,18},{18,... | collective-permute-start | bytes 786440 | tf_op jit(solution)/shard_map/ppermute | solution.py:17
  112.7 11.2 %collective-permute-start.31 = (bf16[256,768]{1,0:T(8,128)(2,1)S(1)}, bf16[256,768]{1,0:T(8,128)(2,1)S(1)}, u32[]{:S(2)}, u32[]{:S(2)}) collective-permute-start(bf16[256,768]{1,0:T(8,128)(2,1)S(1)} %get-tuple-element.76), channel_id=1, source_target_pairs={{0,1},{1,0},{2,3},{3,2},{4,5},{5,4},{6,7},{7,6},{8,9},{9,8},{10,11... | collective-permute-start | bytes 1179656 | tf_op jit(solution)/shard_map/ppermute | solution.py:17
  117.5 4.1 %collective-permute-start.34 = (bf16[64,2048]{1,0:T(8,128)(2,1)S(1)}, bf16[64,2048]{1,0:T(8,128)(2,1)S(1)}, u32[]{:S(2)}, u32[]{:S(2)}) collective-permute-start(bf16[64,2048]{1,0:T(8,128)(2,1)S(1)} %collective-permute-done.32.refs_1_), channel_id=1, source_target_pairs={{0,2},{2,0},{4,6},{6,4},{8,10},{10,8},{12,14},{14,12},{16,18},{18,... | collective-permute-start | bytes 786440 | tf_op jit(solution)/shard_map/ppermute | solution.py:17
  126.4 10.4 %collective-permute-start.35 = (bf16[256,768]{1,0:T(8,128)(2,1)S(1)}, bf16[256,768]{1,0:T(8,128)(2,1)S(1)}, u32[]{:S(2)}, u32[]{:S(2)}) collective-permute-start(bf16[256,768]{1,0:T(8,128)(2,1)S(1)} %get-tuple-element.84), channel_id=1, source_target_pairs={{0,1},{1,0},{2,3},{3,2},{4,5},{5,4},{6,7},{7,6},{8,9},{9,8},{10,11... | collective-permute-start | bytes 1179656 | tf_op jit(solution)/shard_map/ppermute | solution.py:17
  132.0 23.5 %slice-start = ((s8[12582912]{0:T(1024)(128)(4,1)}), s8[4194304]{0:T(1024)(128)(4,1)S(1)}, s32[]{:S(2)}) async-start(s8[12582912]{0:T(1024)(128)(4,1)} %bitcast.8), calls=%async_computation | async-start | bytes 8388608
  132.0 23.5 %slice-start.1 = ((s8[12582912]{0:T(1024)(128)(4,1)}), s8[4194304]{0:T(1024)(128)(4,1)S(1)}, s32[]{:S(2)}) async-start(s8[12582912]{0:T(1024)(128)(4,1)} %bitcast.8), calls=%async_computation.1 | async-start | bytes 8388608
  136.8 18.7 %slice-start.2 = ((s8[12582912]{0:T(1024)(128)(4,1)}), s8[4194304]{0:T(1024)(128)(4,1)S(1)}, s32[]{:S(2)}) async-start(s8[12582912]{0:T(1024)(128)(4,1)} %bitcast.8), calls=%async_computation.2 | async-start | bytes 8388608
  140.8 2.0 %collective-permute-start.38 = (bf16[128,2048]{1,0:T(8,128)(2,1)S(1)}, bf16[128,2048]{1,0:T(8,128)(2,1)S(1)}, u32[]{:S(2)}, u32[]{:S(2)}) collective-permute-start(bf16[128,2048]{1,0:T(8,128)(2,1)S(1)} %get-tuple-element.99), channel_id=1, source_target_pairs={{0,2},{2,0},{4,6},{6,4},{8,10},{10,8},{12,14},{14,12},{16,18},{18,... | collective-permute-start | bytes 1572872 | tf_op jit(solution)/shard_map/ppermute | solution.py:17
  140.9 5.0 %collective-permute-start.37 = (bf16[128,2048]{1,0:T(8,128)(2,1)S(1)}, bf16[128,2048]{1,0:T(8,128)(2,1)S(1)}, u32[]{:S(2)}, u32[]{:S(2)}) collective-permute-start(bf16[128,2048]{1,0:T(8,128)(2,1)S(1)} %get-tuple-element.97), channel_id=1, source_target_pairs={{0,2},{2,0},{4,6},{6,4},{8,10},{10,8},{12,14},{14,12},{16,18},{18,... | collective-permute-start | bytes 1572872 | tf_op jit(solution)/shard_map/ppermute | solution.py:17
  142.9 8.4 %collective-permute-start.39 = (bf16[64,2048]{1,0:T(8,128)(2,1)S(1)}, bf16[64,2048]{1,0:T(8,128)(2,1)S(1)}, u32[]{:S(2)}, u32[]{:S(2)}) collective-permute-start(bf16[64,2048]{1,0:T(8,128)(2,1)S(1)} %get-tuple-element.118), channel_id=1, source_target_pairs={{0,4},{2,6},{4,0},{6,2},{8,12},{10,14},{12,8},{14,10},{16,20},{18,... | collective-permute-start | bytes 786440 | tf_op jit(solution)/shard_map/ppermute | solution.py:17
  143.9 10.2 %collective-permute-start.43 = (bf16[128,2048]{1,0:T(8,128)(2,1)S(1)}, bf16[128,2048]{1,0:T(8,128)(2,1)S(1)}, u32[]{:S(2)}, u32[]{:S(2)}) collective-permute-start(bf16[128,2048]{1,0:T(8,128)(2,1)S(1)} %get-tuple-element.103), channel_id=1, source_target_pairs={{0,2},{2,0},{4,6},{6,4},{8,10},{10,8},{12,14},{14,12},{16,18},{18,... | collective-permute-start | bytes 1572872 | tf_op jit(solution)/shard_map/ppermute | solution.py:17
  143.9 18.3 %collective-permute-start.36 = (bf16[128,2048]{1,0:T(8,128)(2,1)S(1)}, bf16[128,2048]{1,0:T(8,128)(2,1)S(1)}, u32[]{:S(2)}, u32[]{:S(2)}) collective-permute-start(bf16[128,2048]{1,0:T(8,128)(2,1)S(1)} %get-tuple-element.93), channel_id=1, source_target_pairs={{0,2},{2,0},{4,6},{6,4},{8,10},{10,8},{12,14},{14,12},{16,18},{18,... | collective-permute-start | bytes 1572872 | tf_op jit(solution)/shard_map/ppermute | solution.py:17
  144.4 8.2 %collective-permute-start.40 = (bf16[64,2048]{1,0:T(8,128)(2,1)S(1)}, bf16[64,2048]{1,0:T(8,128)(2,1)S(1)}, u32[]{:S(2)}, u32[]{:S(2)}) collective-permute-start(bf16[64,2048]{1,0:T(8,128)(2,1)S(1)} %get-tuple-element.119), channel_id=1, source_target_pairs={{0,1},{1,0},{2,3},{3,2},{4,5},{5,4},{6,7},{7,6},{8,9},{9,8},{10,11... | collective-permute-start | bytes 786440 | tf_op jit(solution)/shard_map/ppermute | solution.py:17
  152.6 9.6 %collective-permute-start.41 = (bf16[64,2048]{1,0:T(8,128)(2,1)S(1)}, bf16[64,2048]{1,0:T(8,128)(2,1)S(1)}, u32[]{:S(2)}, u32[]{:S(2)}) collective-permute-start(bf16[64,2048]{1,0:T(8,128)(2,1)S(1)} %get-tuple-element.100), channel_id=1, source_target_pairs={{0,1},{1,0},{2,3},{3,2},{4,5},{5,4},{6,7},{7,6},{8,9},{9,8},{10,11... | collective-permute-start | bytes 786440 | tf_op jit(solution)/shard_map/ppermute | solution.py:17
  154.3 7.8 %collective-permute-start.44 = (bf16[64,2048]{1,0:T(8,128)(2,1)S(1)}, bf16[64,2048]{1,0:T(8,128)(2,1)S(1)}, u32[]{:S(2)}, u32[]{:S(2)}) collective-permute-start(bf16[64,2048]{1,0:T(8,128)(2,1)S(1)} %get-tuple-element.120), channel_id=1, source_target_pairs={{0,4},{2,6},{4,0},{6,2},{8,12},{10,14},{12,8},{14,10},{16,20},{18,... | collective-permute-start | bytes 786440 | tf_op jit(solution)/shard_map/ppermute | solution.py:17
  162.3 6.9 %collective-permute-start.46 = (bf16[64,2048]{1,0:T(8,128)(2,1)S(1)}, bf16[64,2048]{1,0:T(8,128)(2,1)S(1)}, u32[]{:S(2)}, u32[]{:S(2)}) collective-permute-start(bf16[64,2048]{1,0:T(8,128)(2,1)S(1)} %add_convert_fusion), channel_id=1, source_target_pairs={{0,8},{2,10},{4,12},{6,14},{8,0},{10,2},{12,4},{14,6},{16,24},{18,... | collective-permute-start | bytes 786440 | tf_op jit(solution)/shard_map/ppermute | solution.py:17
  163.1 6.5 %collective-permute-start.42 = (bf16[64,2048]{1,0:T(8,128)(2,1)S(1)}, bf16[64,2048]{1,0:T(8,128)(2,1)S(1)}, u32[]{:S(2)}, u32[]{:S(2)}) collective-permute-start(bf16[64,2048]{1,0:T(8,128)(2,1)S(1)} %get-tuple-element.101), channel_id=1, source_target_pairs={{0,1},{1,0},{2,3},{3,2},{4,5},{5,4},{6,7},{7,6},{8,9},{9,8},{10,11... | collective-permute-start | bytes 786440 | tf_op jit(solution)/shard_map/ppermute | solution.py:17
  163.6 6.4 %collective-permute-start.45 = (bf16[64,2048]{1,0:T(8,128)(2,1)S(1)}, bf16[64,2048]{1,0:T(8,128)(2,1)S(1)}, u32[]{:S(2)}, u32[]{:S(2)}) collective-permute-start(bf16[64,2048]{1,0:T(8,128)(2,1)S(1)} %get-tuple-element.104), channel_id=1, source_target_pairs={{0,4},{2,6},{4,0},{6,2},{8,12},{10,14},{12,8},{14,10},{16,20},{18,... | collective-permute-start | bytes 786440 | tf_op jit(solution)/shard_map/ppermute | solution.py:17
  170.1 7.3 %collective-permute-start.47 = (bf16[32,2048]{1,0:T(8,128)(2,1)S(1)}, bf16[32,2048]{1,0:T(8,128)(2,1)S(1)}, u32[]{:S(2)}, u32[]{:S(2)}) collective-permute-start(bf16[32,2048]{1,0:T(8,128)(2,1)S(1)} %add_convert_fusion.9), channel_id=1, source_target_pairs={{0,16},{2,18},{4,20},{6,22},{8,24},{10,26},{12,28},{14,30},{16,0},... | collective-permute-start | bytes 393224 | tf_op jit(solution)/shard_map/ppermute | solution.py:17

commit v13 on v12

--- a/solution.py
+++ b/solution.py
@@ -599,7 +599,7 @@
         if c == 1:
             second = pack(place, [[across_own], [tie(across_near, near_other)]])
             second_other = swap(second, "expert", 1)
-            across_last = tie(across_last, w_down, second_other, near_terms, *hidden[0][1:])
+            across_last = tie(across_last, w_down, second_other, near_terms)
             last_other = swap(across_last, "expert", 1)
             size = tokens.shape[0]
             x.append([])

time: 178 us -> 176 us (0.989)
  waiting for transfers between devices: 66 us -> 57.5 us
  starting transfers between devices: 44.6 us -> 51.2 us
    ppermute x48, waiting for transfers between devices: 66 us -> 57.5 us  [swap(): return lax.ppermute(array, axis, [(i, i ^ distance) for i in range(size)])]
    ppermute x48, starting transfers between devices: 44.6 us -> 51.2 us  [swap(): return lax.ppermute(array, axis, [(i, i ^ distance) for i in range(size)])]
  transfers between devices with their start and end apart: 48 -> 48, of which waited for: 31 -> 30; matrix products, arithmetic and copies ran while one was open for 2% -> 2% of each run, Pallas kernels for 26% -> 29%
where the time goes in v13:
time: 176 us
  Pallas kernels  60.1 us (34%)
  waiting for transfers between devices  57.5 us (33%)
  starting transfers between devices  51.2 us (29%)
  local copies, waits for them, and re-layouts  4.32 us (2%)
  other arithmetic  1.99 us (1%)
    pallas_call x20, Pallas kernels, call(): pl.pallas_call(kernel, grid_spec=pltpu.PrefetchScalarGridSpec(num_scalar_...  60.1 us
    ppermute x48, waiting for transfers between devices, swap(): return lax.ppermute(array, axis, [(i, i ^ distance) for i in range(size)])  57.5 us
    ppermute x48, starting transfers between devices, swap(): return lax.ppermute(array, axis, [(i, i ^ distance) for i in range(size)])  51.2 us
    unnamed x26, local copies, waits for them, and re-layouts  4.28 us
  transfers between devices with their start and end apart: 48, of which 30 were waited for; matrix products, arithmetic and copies ran while one was open for 2% of the time, Pallas kernels for 29%

profile of v13, /device:TPU:0, one launch (start us, length us, event | category | flops | bytes accessed | tf_op | source)
XLA Modules:
  0.0 176.2 jit_solution(4239460799687554675)
XLA Ops:
  0.6 3.0 %collective-permute-start.1 = (bf16[32,4096]{1,0:T(8,128)(2,1)}, bf16[32,4096]{1,0:T(8,128)(2,1)S(1)}, u32[]{:S(2)}, u32[]{:S(2)}) collective-permute-start(bf16[32,4096]{1,0:T(8,128)(2,1)} %refs_0_.1), channel_id=1, source_target_pairs={{0,4},{2,6},{4,0},{6,2},{8,12},{10,14},{12,8},{14,10},{16,20},{18,... | collective-permute-start | bytes 786440 | tf_op jit(solution)/shard_map/ppermute | solution.py:17
  3.6 2.6 %collective-permute-start = (bf16[32,4096]{1,0:T(8,128)(2,1)}, bf16[32,4096]{1,0:T(8,128)(2,1)S(1)}, u32[]{:S(2)}, u32[]{:S(2)}) collective-permute-start(bf16[32,4096]{1,0:T(8,128)(2,1)} %refs_0_.1), channel_id=1, source_target_pairs={{0,16},{2,18},{4,20},{6,22},{8,24},{10,26},{12,28},{14,30},{16,0},... | collective-permute-start | bytes 786440 | tf_op jit(solution)/shard_map/ppermute | solution.py:17
  6.2 1.6 collective-permute-start.3
  10.2 0.9 copy-done.1
  11.1 0.9 copy-done.2
  12.0 6.2 %shard_map.122.refs_4_.refs_8_.refs_3_ = bf16[4096,1536]{1,0:T(8,128)(2,1)S(1)} custom-call(s32[2]{0:T(128)S(1)} %pad_add_fusion.place_ref, bf16[2,4096,768]{2,1,0:T(8,128)(2,1)} %bitcast.7, f32[2,32,768]{2,1,0:T(8,128)S(1)} %bitcast.13, f32[2,32,768]{2,1,0:T(8,128)S(1)} %bitcast.14), custom_call_target="tpu_custom_call" | custom-call | bytes 25 | tf_op jit(solution)/shard_map/pallas_call | solution.py:112
  18.4 1.4 collective-permute-start.4
  20.4 2.3 %collective-permute-start.2 = (bf16[32,128]{1,0:T(8,128)(2,1)S(1)}, bf16[32,128]{1,0:T(8,128)(2,1)S(1)}, u32[]{:S(2)}, u32[]{:S(2)}) collective-permute-start(bf16[32,128]{1,0:T(8,128)(2,1)S(1)} %shard_map.121), channel_id=1, source_target_pairs={{0,16},{2,18},{4,20},{6,22},{8,24},{10,26},{12,28},{14,30},{16,0},... | collective-permute-start | bytes 24584 | tf_op jit(solution)/shard_map/ppermute | solution.py:17
  22.7 2.3 %collective-permute-done.2 = bf16[32,128]{1,0:T(8,128)(2,1)S(1)} collective-permute-done((bf16[32,128]{1,0:T(8,128)(2,1)S(1)}, bf16[32,128]{1,0:T(8,128)(2,1)S(1)}, u32[]{:S(2)}, u32[]{:S(2)}) %collective-permute-start.2) | collective-permute-done | bytes 8224 | tf_op jit(solution)/shard_map/ppermute | solution.py:17
  25.7 1.1 collective-permute-done.5.refs_1_
  27.4 0.8 collective-permute-start.10
  29.2 4.1 %shard_map.124 = (bf16[256,768]{1,0:T(8,128)(2,1)S(1)}, f32[256,768]{1,0:T(8,128)S(1)}, f32[256,768]{1,0:T(8,128)S(1)}) custom-call(s32[2]{0:T(128)S(1)} %pad_add_fusion.place_ref, bf16[96,4096]{1,0:T(8,128)(2,1)S(1)} %shard_map.123.refs_0_, bf16[32,4096]{1,0:T(8,128)(2,1)S(1)} %collective-permute-done.4.refs_1_, ...), custom_call_target="tpu_custom_call" | custom-call | flops 3221 | bytes 16 | tf_op jit(solution)/shard_map/pallas_call | solution.py:112
  33.4 2.4 %shard_map.125.refs_2_.refs_6_ = bf16[1536,2048]{1,0:T(8,128)(2,1)S(1)} custom-call(s32[2]{0:T(128)S(1)} %pad_add_fusion.place_ref, bf16[1,1536,2048]{2,1,0:T(8,128)(2,1)S(1)} %bitcast.11, f32[1,12,2048]{2,1,0:T(8,128)S(1)} %copy.17.low_ref, f32[1,12,2048]{2,1,0:T(8,128)S(1)} %copy.18.high_ref), custom_call_target="tpu_custom_call" | custom-call | bytes 12 | tf_op jit(solution)/shard_map/pallas_call | solution.py:112
  35.9 3.9 %collective-permute-start.9 = (bf16[64,128]{1,0:T(8,128)(2,1)S(1)}, bf16[64,128]{1,0:T(8,128)(2,1)S(1)}, u32[]{:S(2)}, u32[]{:S(2)}) collective-permute-start(bf16[64,128]{1,0:T(8,128)(2,1)S(1)} %pad_maximum_fusion.2), channel_id=1, source_target_pairs={{0,8},{2,10},{4,12},{6,14},{8,0},{10,2},{12,4},{14,6},{16,24},{18,... | collective-permute-start | bytes 49160 | tf_op jit(solution)/shard_map/ppermute | solution.py:17
  39.7 2.1 %collective-permute-done.10.refs_1_.refs_3_.refs_5_.refs_7_ = bf16[64,4096]{1,0:T(8,128)(2,1)S(1)} collective-permute-done((bf16[64,4096]{1,0:T(8,128)(2,1)S(1)}, bf16[64,4096]{1,0:T(8,128)(2,1)S(1)}, u32[]{:S(2)}, u32[]{:S(2)}) %collective-permute-start.10) | collective-permute-done | bytes 524320 | tf_op jit(solution)/shard_map/ppermute | solution.py:17
  41.9 1.6 collective-permute-start.8
  43.8 4.1 %shard_map.128 = (bf16[256,768]{1,0:T(8,128)(2,1)S(1)}, f32[256,768]{1,0:T(8,128)S(1)}, f32[256,768]{1,0:T(8,128)S(1)}) custom-call(s32[2]{0:T(128)S(1)} %pad_add_fusion.place_ref, bf16[64,4096]{1,0:T(8,128)(2,1)S(1)} %shard_map.126.refs_0_.refs_2_.refs_4_.refs_6_, bf16[64,4096]{1,0:T(8,128)(2,1)S(1)} %collective-permute-done.10.refs_1_.refs_3_.refs_5_.refs_7_, ...), custom_call_target="tpu_custom_call" | custom-call | flops 3221 | bytes 18 | tf_op jit(solution)/shard_map/pallas_call | solution.py:112
  47.9 1.6 collective-permute-start.16
  50.0 3.4 %collective-permute-done.13 = bf16[128,128]{1,0:T(8,128)(2,1)S(1)} collective-permute-done((bf16[128,128]{1,0:T(8,128)(2,1)S(1)}, bf16[128,128]{1,0:T(8,128)(2,1)S(1)}, u32[]{:S(2)}, u32[]{:S(2)}) %collective-permute-start.13) | collective-permute-done | bytes 32800 | tf_op jit(solution)/shard_map/ppermute | solution.py:17
  54.6 2.3 %shard_map.129 = (bf16[128,2048]{1,0:T(8,128)(2,1)S(1)}, bf16[128,2048]{1,0:T(8,128)(2,1)S(1)}) custom-call(s32[2]{0:T(128)S(1)} %pad_add_fusion.place_ref, bf16[256,768]{1,0:T(8,128)(2,1)S(1)} %get-tuple-element.61.refs_0_, bf16[256,768]{1,0:T(8,128)(2,1)S(1)} %collective-permute-done.8.refs_1_, bf16[1536,2048]{1,0:T(8,128)(2,1)S(1)} %shard_map.125.refs_2_.refs_6_, ...), custom_call_target="tpu_custom_call" | custom-call | flops 1610 | bytes 8 | tf_op jit(solution)/shard_map/pallas_call | solution.py:112
  57.0 4.9 %collective-permute-done.16.refs_1_ = bf16[256,768]{1,0:T(8,128)(2,1)S(1)} collective-permute-done((bf16[256,768]{1,0:T(8,128)(2,1)S(1)}, bf16[256,768]{1,0:T(8,128)(2,1)S(1)}, u32[]{:S(2)}, u32[]{:S(2)}) %collective-permute-start.16) | collective-permute-done | bytes 393248 | tf_op jit(solution)/shard_map/ppermute | solution.py:17
  61.8 2.3 %shard_map.130 = (bf16[128,2048]{1,0:T(8,128)(2,1)S(1)}, bf16[128,2048]{1,0:T(8,128)(2,1)S(1)}) custom-call(s32[2]{0:T(128)S(1)} %pad_add_fusion.place_ref, bf16[256,768]{1,0:T(8,128)(2,1)S(1)} %get-tuple-element.66.refs_0_, bf16[256,768]{1,0:T(8,128)(2,1)S(1)} %collective-permute-done.16.refs_1_, bf16[1536,2048]{1,0:T(8,128)(2,1)S(1)} %shard_map.125.refs_2_.refs_6_, ...), custom_call_target="tpu_custom_call" | custom-call | flops 1610 | bytes 8 | tf_op jit(solution)/shard_map/pallas_call | solution.py:112
  64.7 1.4 collective-permute-done.17
  66.8 1.5 collective-permute-start.19
  68.4 4.2 %collective-permute-done.18 = bf16[64,1024]{1,0:T(8,128)(2,1)S(1)} collective-permute-done((bf16[64,1024]{1,0:T(8,128)(2,1)S(1)}, bf16[64,1024]{1,0:T(8,128)(2,1)S(1)}, u32[]{:S(2)}, u32[]{:S(2)}) %collective-permute-start.18) | collective-permute-done | bytes 131104 | tf_op jit(solution)/shard_map/ppermute | solution.py:17
  72.6 2.0 %collective-permute-done.19 = bf16[64,1024]{1,0:T(8,128)(2,1)S(1)} collective-permute-done((bf16[64,1024]{1,0:T(8,128)(2,1)S(1)}, bf16[64,1024]{1,0:T(8,128)(2,1)S(1)}, u32[]{:S(2)}, u32[]{:S(2)}) %collective-permute-start.19) | collective-permute-done | bytes 131104 | tf_op jit(solution)/shard_map/ppermute | solution.py:17
  75.3 2.8 %collective-permute-start.21 = (bf16[64,1024]{1,0:T(8,128)(2,1)S(1)}, bf16[64,1024]{1,0:T(8,128)(2,1)S(1)}, u32[]{:S(2)}, u32[]{:S(2)}) collective-permute-start(bf16[64,1024]{1,0:T(8,128)(2,1)S(1)} %get-tuple-element.123), channel_id=1, source_target_pairs={{0,8},{2,10},{4,12},{6,14},{8,0},{10,2},{12,4},{14,6},{16,24},{18,... | collective-permute-start | bytes 393224 | tf_op jit(solution)/shard_map/ppermute | solution.py:17
  78.2 4.1 %collective-permute-done.21 = bf16[64,1024]{1,0:T(8,128)(2,1)S(1)} collective-permute-done((bf16[64,1024]{1,0:T(8,128)(2,1)S(1)}, bf16[64,1024]{1,0:T(8,128)(2,1)S(1)}, u32[]{:S(2)}, u32[]{:S(2)}) %collective-permute-start.21) | collective-permute-done | bytes 131104 | tf_op jit(solution)/shard_map/ppermute | solution.py:17
  82.2 1.4 collective-permute-done.23
  83.7 2.3 %collective-permute-start.22 = (bf16[32,1024]{1,0:T(8,128)(2,1)S(1)}, bf16[32,1024]{1,0:T(8,128)(2,1)S(1)}, u32[]{:S(2)}, u32[]{:S(2)}) collective-permute-start(bf16[32,1024]{1,0:T(8,128)(2,1)S(1)} %get-tuple-element.115), channel_id=1, source_target_pairs={{0,16},{2,18},{4,20},{6,22},{8,24},{10,26},{12,28},{14,30},{16,0},... | collective-permute-start | bytes 196616 | tf_op jit(solution)/shard_map/ppermute | solution.py:17
  86.7 2.6 %collective-permute-done.22 = bf16[32,1024]{1,0:T(8,128)(2,1)S(1)} collective-permute-done((bf16[32,1024]{1,0:T(8,128)(2,1)S(1)}, bf16[32,1024]{1,0:T(8,128)(2,1)S(1)}, u32[]{:S(2)}, u32[]{:S(2)}) %collective-permute-start.22) | collective-permute-done | bytes 65568 | tf_op jit(solution)/shard_map/ppermute | solution.py:17
  89.3 2.4 %collective-permute-done.24 = bf16[32,1024]{1,0:T(8,128)(2,1)S(1)} collective-permute-done((bf16[32,1024]{1,0:T(8,128)(2,1)S(1)}, bf16[32,1024]{1,0:T(8,128)(2,1)S(1)}, u32[]{:S(2)}, u32[]{:S(2)}) %collective-permute-start.24) | collective-permute-done | bytes 65568 | tf_op jit(solution)/shard_map/ppermute | solution.py:17
  92.1 2.7 %collective-permute-start.26 = (bf16[32,1024]{1,0:T(8,128)(2,1)S(1)}, bf16[32,1024]{1,0:T(8,128)(2,1)S(1)}, u32[]{:S(2)}, u32[]{:S(2)}) collective-permute-start(bf16[32,1024]{1,0:T(8,128)(2,1)S(1)} %get-tuple-element.112.refs_1_), channel_id=1, source_target_pairs={{0,16},{2,18},{4,20},{6,22},{8,24},{10,26},{12,28},{14,30},{16,0},... | collective-permute-start | bytes 196616 | tf_op jit(solution)/shard_map/ppermute | solution.py:17
  94.9 2.3 %collective-permute-done.25.refs_2_ = bf16[32,1024]{1,0:T(8,128)(2,1)S(1)} collective-permute-done((bf16[32,1024]{1,0:T(8,128)(2,1)S(1)}, bf16[32,1024]{1,0:T(8,128)(2,1)S(1)}, u32[]{:S(2)}, u32[]{:S(2)}) %collective-permute-start.25) | collective-permute-done | bytes 65568 | tf_op jit(solution)/shard_map/ppermute | solution.py:17
  98.5 1.8 %collective-permute-start.27 = (bf16[64,2048]{1,0:T(8,128)(2,1)S(1)}, bf16[64,2048]{1,0:T(8,128)(2,1)S(1)}, u32[]{:S(2)}, u32[]{:S(2)}) collective-permute-start(bf16[64,2048]{1,0:T(8,128)(2,1)S(1)} %shard_map.131.refs_0_), channel_id=1, source_target_pairs={{0,8},{2,10},{4,12},{6,14},{8,0},{10,2},{12,4},{14,6},{16,24},{18,... | collective-permute-start | bytes 786440 | tf_op jit(solution)/shard_map/ppermute | solution.py:17
  100.3 1.5 collective-permute-start.28
  101.9 3.1 %collective-permute-done.27.refs_1_ = bf16[64,2048]{1,0:T(8,128)(2,1)S(1)} collective-permute-done((bf16[64,2048]{1,0:T(8,128)(2,1)S(1)}, bf16[64,2048]{1,0:T(8,128)(2,1)S(1)}, u32[]{:S(2)}, u32[]{:S(2)}) %collective-permute-start.27) | collective-permute-done | bytes 262176 | tf_op jit(solution)/shard_map/ppermute | solution.py:17
  104.9 1.8 %collective-permute-done.28.refs_0_ = bf16[64,2048]{1,0:T(8,128)(2,1)S(1)} collective-permute-done((bf16[64,2048]{1,0:T(8,128)(2,1)S(1)}, bf16[64,2048]{1,0:T(8,128)(2,1)S(1)}, u32[]{:S(2)}, u32[]{:S(2)}) %collective-permute-start.28) | collective-permute-done | bytes 262176 | tf_op jit(solution)/shard_map/ppermute | solution.py:17
  106.7 1.5 collective-permute-start.32
  108.5 2.4 %shard_map.132 = (bf16[256,2048]{1,0:T(8,128)(2,1)S(1)}, f32[256,768]{1,0:T(8,128)S(1)}, bf16[256,768]{1,0:T(8,128)(2,1)S(1)}) custom-call(s32[2]{0:T(128)S(1)} %pad_add_fusion.place_ref, bf16[64,2048]{1,0:T(8,128)(2,1)S(1)} %shard_map.131.refs_0_, bf16[64,2048]{1,0:T(8,128)(2,1)S(1)} %collective-permute-done.27.refs_1_, ...), custom_call_target="tpu_custom_call" | custom-call | flops 1610 | bytes 9 | tf_op jit(solution)/shard_map/pallas_call | solution.py:112
  110.9 1.6 collective-permute-start.31
  112.5 2.9 %collective-permute-done.32.refs_1_ = bf16[64,2048]{1,0:T(8,128)(2,1)S(1)} collective-permute-done((bf16[64,2048]{1,0:T(8,128)(2,1)S(1)}, bf16[64,2048]{1,0:T(8,128)(2,1)S(1)}, u32[]{:S(2)}, u32[]{:S(2)}) %collective-permute-start.32) | collective-permute-done | bytes 262176 | tf_op jit(solution)/shard_map/ppermute | solution.py:17
  115.4 4.1 %shard_map.134.refs_4_ = f32[2,12,2048]{2,1,0:T(8,128)S(1)} custom-call(s32[2]{0:T(128)S(1)} %pad_add_fusion.place_ref, bf16[256,768]{1,0:T(8,128)(2,1)S(1)} %get-tuple-element.61.refs_0_, bf16[256,768]{1,0:T(8,128)(2,1)S(1)} %collective-permute-done.8.refs_1_, bf16[256,2048]{1,0:T(8,128)(2,1)S(1)} %get-tuple-element.80.refs_2_, ...), custom_call_target="tpu_custom_call" | custom-call | flops 1610 | bytes 8 | tf_op jit(solution)/shard_map/pallas_call | solution.py:112
  119.6 2.7 %collective-permute-done.31.refs_0_ = bf16[256,768]{1,0:T(8,128)(2,1)S(1)} collective-permute-done((bf16[256,768]{1,0:T(8,128)(2,1)S(1)}, bf16[256,768]{1,0:T(8,128)(2,1)S(1)}, u32[]{:S(2)}, u32[]{:S(2)}) %collective-permute-start.31) | collective-permute-done | bytes 393248 | tf_op jit(solution)/shard_map/ppermute | solution.py:17
  122.3 2.4 %shard_map.135 = (bf16[256,2048]{1,0:T(8,128)(2,1)S(1)}, f32[256,768]{1,0:T(8,128)S(1)}, bf16[256,768]{1,0:T(8,128)(2,1)S(1)}) custom-call(s32[2]{0:T(128)S(1)} %pad_add_fusion.place_ref, bf16[64,2048]{1,0:T(8,128)(2,1)S(1)} %collective-permute-done.28.refs_0_, bf16[64,2048]{1,0:T(8,128)(2,1)S(1)} %collective-permute-done.32.refs_1_, ...), custom_call_target="tpu_custom_call" | custom-call | flops 1610 | bytes 9 | tf_op jit(solution)/shard_map/pallas_call | solution.py:112
  124.7 1.6 collective-permute-start.35
  126.3 4.0 %shard_map.136 = f32[2,12,2048]{2,1,0:T(8,128)S(1)} custom-call(s32[2]{0:T(128)S(1)} %pad_add_fusion.place_ref, bf16[256,768]{1,0:T(8,128)(2,1)S(1)} %get-tuple-element.66.refs_0_, bf16[256,768]{1,0:T(8,128)(2,1)S(1)} %collective-permute-done.16.refs_1_, bf16[256,2048]{1,0:T(8,128)(2,1)S(1)} %get-tuple-element.86.refs_2_, ...), custom_call_target="tpu_custom_call" | custom-call | flops 1610 | bytes 8 | tf_op jit(solution)/shard_map/pallas_call | solution.py:112
  130.3 4.0 %shard_map.133 = (bf16[256,1536]{1,0:T(8,128)(2,1)S(1)}, bf16[128,2048]{1,0:T(8,128)(2,1)S(1)}, bf16[128,2048]{1,0:T(8,128)(2,1)S(1)}, bf16[128,2048]{1,0:T(8,128)(2,1)S(1)}, bf16[128,2048]{1,0:T(8,128)(2,1)S(1)}) custom-call(s32[2]{0:T(128)S(1)} %pad_add_fusion.place_ref, f32[256,768]{1,0:T(8,128)S(1)} %get-tuple-element.75.grad_own_ref, ...), custom_call_target="tpu_custom_call" | custom-call | flops 3221 | bytes 18 | tf_op jit(solution)/shard_map/pallas_call | solution.py:112
  134.3 0.9 collective-permute-done.35.refs_0_
  135.3 4.0 %shard_map.137 = (bf16[256,1536]{1,0:T(8,128)(2,1)S(1)}, bf16[128,2048]{1,0:T(8,128)(2,1)S(1)}, bf16[128,2048]{1,0:T(8,128)(2,1)S(1)}, bf16[128,2048]{1,0:T(8,128)(2,1)S(1)}, bf16[128,2048]{1,0:T(8,128)(2,1)S(1)}) custom-call(s32[2]{0:T(128)S(1)} %pad_add_fusion.place_ref, f32[256,768]{1,0:T(8,128)S(1)} %get-tuple-element.83.grad_own_ref, ...), custom_call_target="tpu_custom_call" | custom-call | flops 3221 | bytes 18 | tf_op jit(solution)/shard_map/pallas_call | solution.py:112
  139.9 1.4 collective-permute-done.38
  141.4 1.1 collective-permute-start.39
  143.0 1.5 collective-permute-start.40
  144.5 5.3 %collective-permute-done.39 = bf16[64,2048]{1,0:T(8,128)(2,1)S(1)} collective-permute-done((bf16[64,2048]{1,0:T(8,128)(2,1)S(1)}, bf16[64,2048]{1,0:T(8,128)(2,1)S(1)}, u32[]{:S(2)}, u32[]{:S(2)}) %collective-permute-start.39) | collective-permute-done | bytes 262176 | tf_op jit(solution)/shard_map/ppermute | solution.py:17
  150.0 1.2 collective-permute-done.40
  151.2 1.5 collective-permute-start.41
  152.9 1.1 collective-permute-start.44
  154.0 6.6 %shard_map.138.refs_15_ = f32[4,32,768]{2,1,0:T(8,128)} custom-call(s32[2]{0:T(128)S(1)} %pad_add_fusion.place_ref, bf16[96,4096]{1,0:T(8,128)(2,1)S(1)} %shard_map.123.refs_0_, bf16[32,4096]{1,0:T(8,128)(2,1)S(1)} %collective-permute-done.4.refs_1_, bf16[96,4096]{1,0:T(8,128)(2,1)S(1)} %collective-permute-done.6.refs_2_, ...), custom_call_target="tpu_custom_call" | custom-call | flops 3221 | bytes 20 | tf_op jit(solution)/shard_map/pallas_call | solution.py:112
  161.5 1.0 collective-permute-start.45
  162.5 4.2 %shard_map.139.refs_15_ = f32[4,32,768]{2,1,0:T(8,128)} custom-call(s32[2]{0:T(128)S(1)} %pad_add_fusion.place_ref, bf16[96,4096]{1,0:T(8,128)(2,1)S(1)} %shard_map.123.refs_0_, bf16[32,4096]{1,0:T(8,128)(2,1)S(1)} %collective-permute-done.4.refs_1_, bf16[96,4096]{1,0:T(8,128)(2,1)S(1)} %collective-permute-done.6.refs_2_, ...), custom_call_target="tpu_custom_call", output_to_operand_aliasing={{}: (16, {})} | custom-call | flops 1610 | bytes 20 | tf_op jit(solution)/shard_map/pallas_call | solution.py:112
  166.7 0.9 collective-permute-done.46
  168.0 2.7 %collective-permute-start.47 = (bf16[32,2048]{1,0:T(8,128)(2,1)S(1)}, bf16[32,2048]{1,0:T(8,128)(2,1)S(1)}, u32[]{:S(2)}, u32[]{:S(2)}) collective-permute-start(bf16[32,2048]{1,0:T(8,128)(2,1)S(1)} %add_convert_fusion.9), channel_id=1, source_target_pairs={{0,16},{2,18},{4,20},{6,22},{8,24},{10,26},{12,28},{14,30},{16,0},... | collective-permute-start | bytes 393224 | tf_op jit(solution)/shard_map/ppermute | solution.py:17
  170.7 0.8 copy.19
  171.5 3.9 %shard_map.140 = f32[4,32,768]{2,1,0:T(8,128)} custom-call(s32[2]{0:T(128)S(1)} %pad_add_fusion.place_ref, bf16[96,4096]{1,0:T(8,128)(2,1)S(1)} %shard_map.123.refs_0_, bf16[32,4096]{1,0:T(8,128)(2,1)S(1)} %collective-permute-done.4.refs_1_, bf16[96,4096]{1,0:T(8,128)(2,1)S(1)} %collective-permute-done.6.refs_2_, ...), custom_call_target="tpu_custom_call", output_to_operand_aliasing={{}: (16, {})} | custom-call | flops 1610 | bytes 20 | tf_op jit(solution)/shard_map/pallas_call | solution.py:112
  (96 shorter events, 15.9 us)
Async XLA Ops:
  0.6 17.6 %collective-permute-start.1 = (bf16[32,4096]{1,0:T(8,128)(2,1)}, bf16[32,4096]{1,0:T(8,128)(2,1)S(1)}, u32[]{:S(2)}, u32[]{:S(2)}) collective-permute-start(bf16[32,4096]{1,0:T(8,128)(2,1)} %refs_0_.1), channel_id=1, source_target_pairs={{0,4},{2,6},{4,0},{6,2},{8,12},{10,14},{12,8},{14,10},{16,20},{18,... | collective-permute-start | bytes 786440 | tf_op jit(solution)/shard_map/ppermute | solution.py:17
  3.6 14.6 %collective-permute-start = (bf16[32,4096]{1,0:T(8,128)(2,1)}, bf16[32,4096]{1,0:T(8,128)(2,1)S(1)}, u32[]{:S(2)}, u32[]{:S(2)}) collective-permute-start(bf16[32,4096]{1,0:T(8,128)(2,1)} %refs_0_.1), channel_id=1, source_target_pairs={{0,16},{2,18},{4,20},{6,22},{8,24},{10,26},{12,28},{14,30},{16,0},... | collective-permute-start | bytes 786440 | tf_op jit(solution)/shard_map/ppermute | solution.py:17
  6.2 12.2 %collective-permute-start.3 = (bf16[32,4096]{1,0:T(8,128)(2,1)}, bf16[32,4096]{1,0:T(8,128)(2,1)S(1)}, u32[]{:S(2)}, u32[]{:S(2)}) collective-permute-start(bf16[32,4096]{1,0:T(8,128)(2,1)} %refs_0_.1), channel_id=1, source_target_pairs={{0,8},{2,10},{4,12},{6,14},{8,0},{10,2},{12,4},{14,6},{16,24},{18,... | collective-permute-start | bytes 786440 | tf_op jit(solution)/shard_map/ppermute | solution.py:17
  10.2 0.9 copy-start.1
  11.1 0.9 copy-start.2
  12.0 13.0 %copy-start = (bf16[32,4096]{1,0:T(8,128)(2,1)S(1)}, bf16[32,4096]{1,0:T(8,128)(2,1)}, u32[]{:S(2)}) copy-start(bf16[32,4096]{1,0:T(8,128)(2,1)} %refs_0_.1) | copy-start | bytes 786436
  12.0 17.2 %copy-start.4 = (f32[1,12,2048]{2,0,1:T(1,128)S(1)}, f32[1,12,2048]{2,0,1:T(1,128)}, u32[]{:S(2)}) copy-start(f32[1,12,2048]{2,0,1:T(1,128)} %param.19) | copy-start | bytes 294916
  18.2 15.1 %copy-start.5 = (f32[1,12,2048]{2,0,1:T(1,128)S(1)}, f32[1,12,2048]{2,0,1:T(1,128)}, u32[]{:S(2)}) copy-start(f32[1,12,2048]{2,0,1:T(1,128)} %param.18) | copy-start | bytes 294916
  18.2 15.2 %slice-start.3 = ((s8[6291456]{0:T(1024)(128)(4,1)}), s8[4194304]{0:T(1024)(128)(4,1)S(1)}, s32[]{:S(2)}) async-start(s8[6291456]{0:T(1024)(128)(4,1)} %bitcast.10), calls=%async_computation.3 | async-start | bytes 8388608
  18.4 7.3 %collective-permute-start.4 = (bf16[32,4096]{1,0:T(8,128)(2,1)S(1)}, bf16[32,4096]{1,0:T(8,128)(2,1)S(1)}, u32[]{:S(2)}, u32[]{:S(2)}) collective-permute-start(bf16[32,4096]{1,0:T(8,128)(2,1)S(1)} %collective-permute-done.refs_1_.refs_0_), channel_id=1, source_target_pairs={{0,8},{2,10},{4,12},{6,14},{8,0},{10,2},{12,4},{14,6},{16,24},{18,... | collective-permute-start | bytes 786440 | tf_op jit(solution)/shard_map/ppermute | solution.py:17
  19.9 7.0 %collective-permute-start.5 = (bf16[32,4096]{1,0:T(8,128)(2,1)S(1)}, bf16[32,4096]{1,0:T(8,128)(2,1)S(1)}, u32[]{:S(2)}, u32[]{:S(2)}) collective-permute-start(bf16[32,4096]{1,0:T(8,128)(2,1)S(1)} %collective-permute-done.3.refs_2_), channel_id=1, source_target_pairs={{0,4},{2,6},{4,0},{6,2},{8,12},{10,14},{12,8},{14,10},{16,20},{18,... | collective-permute-start | bytes 786440 | tf_op jit(solution)/shard_map/ppermute | solution.py:17
  20.4 4.7 %collective-permute-start.2 = (bf16[32,128]{1,0:T(8,128)(2,1)S(1)}, bf16[32,128]{1,0:T(8,128)(2,1)S(1)}, u32[]{:S(2)}, u32[]{:S(2)}) collective-permute-start(bf16[32,128]{1,0:T(8,128)(2,1)S(1)} %shard_map.121), channel_id=1, source_target_pairs={{0,16},{2,18},{4,20},{6,22},{8,24},{10,26},{12,28},{14,30},{16,0},... | collective-permute-start | bytes 24584 | tf_op jit(solution)/shard_map/ppermute | solution.py:17
  25.7 3.6 %collective-permute-start.6 = (bf16[96,4096]{1,0:T(8,128)(2,1)S(1)}, bf16[96,4096]{1,0:T(8,128)(2,1)S(1)}, u32[]{:S(2)}, u32[]{:S(2)}) collective-permute-start(bf16[96,4096]{1,0:T(8,128)(2,1)S(1)} %shard_map.123.refs_0_), channel_id=1, source_target_pairs={{0,2},{2,0},{4,6},{6,4},{8,10},{10,8},{12,14},{14,12},{16,18},{18,... | collective-permute-start | bytes 2359304 | tf_op jit(solution)/shard_map/ppermute | solution.py:17
  26.9 1.5 collective-permute-start.7
  27.4 14.4 %collective-permute-start.10 = (bf16[64,4096]{1,0:T(8,128)(2,1)S(1)}, bf16[64,4096]{1,0:T(8,128)(2,1)S(1)}, u32[]{:S(2)}, u32[]{:S(2)}) collective-permute-start(bf16[64,4096]{1,0:T(8,128)(2,1)S(1)} %shard_map.127), channel_id=1, source_target_pairs={{0,4},{2,6},{4,0},{6,2},{8,12},{10,14},{12,8},{14,10},{16,20},{18,... | collective-permute-start | bytes 1572872 | tf_op jit(solution)/shard_map/ppermute | solution.py:17
  29.0 12.9 %collective-permute-start.11 = (bf16[64,4096]{1,0:T(8,128)(2,1)S(1)}, bf16[64,4096]{1,0:T(8,128)(2,1)S(1)}, u32[]{:S(2)}, u32[]{:S(2)}) collective-permute-start(bf16[64,4096]{1,0:T(8,128)(2,1)S(1)} %shard_map.126.refs_0_.refs_2_.refs_4_.refs_6_), channel_id=1, source_target_pairs={{0,2},{2,0},{4,6},{6,4},{8,10},{10,8},{12,14},{14,12},{16,18},{18,... | collective-permute-start | bytes 1572872 | tf_op jit(solution)/shard_map/ppermute | solution.py:17
  29.2 4.2 %slice-start.4 = ((s8[6291456]{0:T(1024)(128)(4,1)}), s8[2097152]{0:T(1024)(128)(4,1)S(1)}, s32[]{:S(2)}) async-start(s8[6291456]{0:T(1024)(128)(4,1)} %bitcast.10), calls=%async_computation.4 | async-start | bytes 4194304
  35.9 6.0 %collective-permute-start.9 = (bf16[64,128]{1,0:T(8,128)(2,1)S(1)}, bf16[64,128]{1,0:T(8,128)(2,1)S(1)}, u32[]{:S(2)}, u32[]{:S(2)}) collective-permute-start(bf16[64,128]{1,0:T(8,128)(2,1)S(1)} %pad_maximum_fusion.2), channel_id=1, source_target_pairs={{0,8},{2,10},{4,12},{6,14},{8,0},{10,2},{12,4},{14,6},{16,24},{18,... | collective-permute-start | bytes 49160 | tf_op jit(solution)/shard_map/ppermute | solution.py:17
  41.8 1.9 %collective-permute-start.12 = (bf16[64,4096]{1,0:T(8,128)(2,1)S(1)}, bf16[64,4096]{1,0:T(8,128)(2,1)S(1)}, u32[]{:S(2)}, u32[]{:S(2)}) collective-permute-start(bf16[64,4096]{1,0:T(8,128)(2,1)S(1)} %collective-permute-done.10.refs_1_.refs_3_.refs_5_.refs_7_), channel_id=1, source_target_pairs={{0,2},{2,0},{4,6},{6,4},{8,10},{10,8},{12,14},{14,12},{16,18},{18,... | collective-permute-start | bytes 1572872 | tf_op jit(solution)/shard_map/ppermute | solution.py:17
  41.9 12.0 %collective-permute-start.8 = (bf16[256,768]{1,0:T(8,128)(2,1)S(1)}, bf16[256,768]{1,0:T(8,128)(2,1)S(1)}, u32[]{:S(2)}, u32[]{:S(2)}) collective-permute-start(bf16[256,768]{1,0:T(8,128)(2,1)S(1)} %get-tuple-element.61.refs_0_), channel_id=1, source_target_pairs={{0,1},{1,0},{2,3},{3,2},{4,5},{5,4},{6,7},{7,6},{8,9},{9,8},{10,11... | collective-permute-start | bytes 1179656 | tf_op jit(solution)/shard_map/ppermute | solution.py:17
  47.8 43.9 %copy-start.3 = (bf16[32,2048]{1,0:T(8,128)(2,1)S(1)}, bf16[32,2048]{1,0:T(8,128)(2,1)}, u32[]{:S(2)}) copy-start(bf16[32,2048]{1,0:T(8,128)(2,1)} %param.11) | copy-start | bytes 393220
  47.9 14.0 %collective-permute-start.16 = (bf16[256,768]{1,0:T(8,128)(2,1)S(1)}, bf16[256,768]{1,0:T(8,128)(2,1)S(1)}, u32[]{:S(2)}, u32[]{:S(2)}) collective-permute-start(bf16[256,768]{1,0:T(8,128)(2,1)S(1)} %get-tuple-element.66.refs_0_), channel_id=1, source_target_pairs={{0,1},{1,0},{2,3},{3,2},{4,5},{5,4},{6,7},{7,6},{8,9},{9,8},{10,11... | collective-permute-start | bytes 1179656 | tf_op jit(solution)/shard_map/ppermute | solution.py:17
  49.4 3.9 %collective-permute-start.13 = (bf16[128,128]{1,0:T(8,128)(2,1)S(1)}, bf16[128,128]{1,0:T(8,128)(2,1)S(1)}, u32[]{:S(2)}, u32[]{:S(2)}) collective-permute-start(bf16[128,128]{1,0:T(8,128)(2,1)S(1)} %pad_maximum_fusion.1), channel_id=1, source_target_pairs={{0,4},{2,6},{4,0},{6,2},{8,12},{10,14},{12,8},{14,10},{16,20},{18,... | collective-permute-start | bytes 98312 | tf_op jit(solution)/shard_map/ppermute | solution.py:17
  53.4 1.3 collective-permute-start.14
  64.1 2.0 %collective-permute-start.17 = (bf16[128,2048]{1,0:T(8,128)(2,1)S(1)}, bf16[128,2048]{1,0:T(8,128)(2,1)S(1)}, u32[]{:S(2)}, u32[]{:S(2)}) collective-permute-start(bf16[128,2048]{1,0:T(8,128)(2,1)S(1)} %get-tuple-element.72), channel_id=1, source_target_pairs={{0,2},{2,0},{4,6},{6,4},{8,10},{10,8},{12,14},{14,12},{16,18},{18,... | collective-permute-start | bytes 1572872 | tf_op jit(solution)/shard_map/ppermute | solution.py:17
  64.2 10.9 %collective-permute-start.15 = (bf16[128,2048]{1,0:T(8,128)(2,1)S(1)}, bf16[128,2048]{1,0:T(8,128)(2,1)S(1)}, u32[]{:S(2)}, u32[]{:S(2)}) collective-permute-start(bf16[128,2048]{1,0:T(8,128)(2,1)S(1)} %get-tuple-element.69), channel_id=1, source_target_pairs={{0,2},{2,0},{4,6},{6,4},{8,10},{10,8},{12,14},{14,12},{16,18},{18,... | collective-permute-start | bytes 1572872 | tf_op jit(solution)/shard_map/ppermute | solution.py:17
  66.2 6.4 %collective-permute-start.18 = (bf16[64,1024]{1,0:T(8,128)(2,1)S(1)}, bf16[64,1024]{1,0:T(8,128)(2,1)S(1)}, u32[]{:S(2)}, u32[]{:S(2)}) collective-permute-start(bf16[64,1024]{1,0:T(8,128)(2,1)S(1)} %get-tuple-element.125), channel_id=1, source_target_pairs={{0,4},{2,6},{4,0},{6,2},{8,12},{10,14},{12,8},{14,10},{16,20},{18,... | collective-permute-start | bytes 393224 | tf_op jit(solution)/shard_map/ppermute | solution.py:17
  66.8 7.8 %collective-permute-start.19 = (bf16[64,1024]{1,0:T(8,128)(2,1)S(1)}, bf16[64,1024]{1,0:T(8,128)(2,1)S(1)}, u32[]{:S(2)}, u32[]{:S(2)}) collective-permute-start(bf16[64,1024]{1,0:T(8,128)(2,1)S(1)} %get-tuple-element.124), channel_id=1, source_target_pairs={{0,4},{2,6},{4,0},{6,2},{8,12},{10,14},{12,8},{14,10},{16,20},{18,... | collective-permute-start | bytes 393224 | tf_op jit(solution)/shard_map/ppermute | solution.py:17
  74.6 9.0 %collective-permute-start.20 = (bf16[64,2048]{1,0:T(8,128)(2,1)S(1)}, bf16[64,2048]{1,0:T(8,128)(2,1)S(1)}, u32[]{:S(2)}, u32[]{:S(2)}) collective-permute-start(bf16[64,2048]{1,0:T(8,128)(2,1)S(1)} %add_convert_fusion.7), channel_id=1, source_target_pairs={{0,4},{2,6},{4,0},{6,2},{8,12},{10,14},{12,8},{14,10},{16,20},{18,... | collective-permute-start | bytes 786440 | tf_op jit(solution)/shard_map/ppermute | solution.py:17
  75.3 7.0 %collective-permute-start.21 = (bf16[64,1024]{1,0:T(8,128)(2,1)S(1)}, bf16[64,1024]{1,0:T(8,128)(2,1)S(1)}, u32[]{:S(2)}, u32[]{:S(2)}) collective-permute-start(bf16[64,1024]{1,0:T(8,128)(2,1)S(1)} %get-tuple-element.123), channel_id=1, source_target_pairs={{0,8},{2,10},{4,12},{6,14},{8,0},{10,2},{12,4},{14,6},{16,24},{18,... | collective-permute-start | bytes 393224 | tf_op jit(solution)/shard_map/ppermute | solution.py:17
  78.1 5.6 %collective-permute-start.23 = (bf16[64,1024]{1,0:T(8,128)(2,1)S(1)}, bf16[64,1024]{1,0:T(8,128)(2,1)S(1)}, u32[]{:S(2)}, u32[]{:S(2)}) collective-permute-start(bf16[64,1024]{1,0:T(8,128)(2,1)S(1)} %get-tuple-element.122), channel_id=1, source_target_pairs={{0,8},{2,10},{4,12},{6,14},{8,0},{10,2},{12,4},{14,6},{16,24},{18,... | collective-permute-start | bytes 393224 | tf_op jit(solution)/shard_map/ppermute | solution.py:17
  83.7 5.6 %collective-permute-start.22 = (bf16[32,1024]{1,0:T(8,128)(2,1)S(1)}, bf16[32,1024]{1,0:T(8,128)(2,1)S(1)}, u32[]{:S(2)}, u32[]{:S(2)}) collective-permute-start(bf16[32,1024]{1,0:T(8,128)(2,1)S(1)} %get-tuple-element.115), channel_id=1, source_target_pairs={{0,16},{2,18},{4,20},{6,22},{8,24},{10,26},{12,28},{14,30},{16,0},... | collective-permute-start | bytes 196616 | tf_op jit(solution)/shard_map/ppermute | solution.py:17
  86.0 5.8 %collective-permute-start.24 = (bf16[32,1024]{1,0:T(8,128)(2,1)S(1)}, bf16[32,1024]{1,0:T(8,128)(2,1)S(1)}, u32[]{:S(2)}, u32[]{:S(2)}) collective-permute-start(bf16[32,1024]{1,0:T(8,128)(2,1)S(1)} %get-tuple-element.114), channel_id=1, source_target_pairs={{0,16},{2,18},{4,20},{6,22},{8,24},{10,26},{12,28},{14,30},{16,0},... | collective-permute-start | bytes 196616 | tf_op jit(solution)/shard_map/ppermute | solution.py:17
  91.9 5.3 %collective-permute-start.25 = (bf16[32,1024]{1,0:T(8,128)(2,1)S(1)}, bf16[32,1024]{1,0:T(8,128)(2,1)S(1)}, u32[]{:S(2)}, u32[]{:S(2)}) collective-permute-start(bf16[32,1024]{1,0:T(8,128)(2,1)S(1)} %get-tuple-element.113.refs_0_), channel_id=1, source_target_pairs={{0,16},{2,18},{4,20},{6,22},{8,24},{10,26},{12,28},{14,30},{16,0},... | collective-permute-start | bytes 196616 | tf_op jit(solution)/shard_map/ppermute | solution.py:17
  92.1 5.8 %collective-permute-start.26 = (bf16[32,1024]{1,0:T(8,128)(2,1)S(1)}, bf16[32,1024]{1,0:T(8,128)(2,1)S(1)}, u32[]{:S(2)}, u32[]{:S(2)}) collective-permute-start(bf16[32,1024]{1,0:T(8,128)(2,1)S(1)} %get-tuple-element.112.refs_1_), channel_id=1, source_target_pairs={{0,16},{2,18},{4,20},{6,22},{8,24},{10,26},{12,28},{14,30},{16,0},... | collective-permute-start | bytes 196616 | tf_op jit(solution)/shard_map/ppermute | solution.py:17
  98.5 6.4 %collective-permute-start.27 = (bf16[64,2048]{1,0:T(8,128)(2,1)S(1)}, bf16[64,2048]{1,0:T(8,128)(2,1)S(1)}, u32[]{:S(2)}, u32[]{:S(2)}) collective-permute-start(bf16[64,2048]{1,0:T(8,128)(2,1)S(1)} %shard_map.131.refs_0_), channel_id=1, source_target_pairs={{0,8},{2,10},{4,12},{6,14},{8,0},{10,2},{12,4},{14,6},{16,24},{18,... | collective-permute-start | bytes 786440 | tf_op jit(solution)/shard_map/ppermute | solution.py:17
  100.3 6.4 %collective-permute-start.28 = (bf16[64,2048]{1,0:T(8,128)(2,1)S(1)}, bf16[64,2048]{1,0:T(8,128)(2,1)S(1)}, u32[]{:S(2)}, u32[]{:S(2)}) collective-permute-start(bf16[64,2048]{1,0:T(8,128)(2,1)S(1)} %shard_map.131.refs_0_), channel_id=1, source_target_pairs={{0,4},{2,6},{4,0},{6,2},{8,12},{10,14},{12,8},{14,10},{16,20},{18,... | collective-permute-start | bytes 786440 | tf_op jit(solution)/shard_map/ppermute | solution.py:17
  101.9 4.8 %collective-permute-start.29 = (bf16[64,2048]{1,0:T(8,128)(2,1)S(1)}, bf16[64,2048]{1,0:T(8,128)(2,1)S(1)}, u32[]{:S(2)}, u32[]{:S(2)}) collective-permute-start(bf16[64,2048]{1,0:T(8,128)(2,1)S(1)} %shard_map.131.refs_0_), channel_id=1, source_target_pairs={{0,2},{2,0},{4,6},{6,4},{8,10},{10,8},{12,14},{14,12},{16,18},{18,... | collective-permute-start | bytes 786440 | tf_op jit(solution)/shard_map/ppermute | solution.py:17
  106.7 1.8 %collective-permute-start.30 = (bf16[64,2048]{1,0:T(8,128)(2,1)S(1)}, bf16[64,2048]{1,0:T(8,128)(2,1)S(1)}, u32[]{:S(2)}, u32[]{:S(2)}) collective-permute-start(bf16[64,2048]{1,0:T(8,128)(2,1)S(1)} %collective-permute-done.27.refs_1_), channel_id=1, source_target_pairs={{0,2},{2,0},{4,6},{6,4},{8,10},{10,8},{12,14},{14,12},{16,18},{18,... | collective-permute-start | bytes 786440 | tf_op jit(solution)/shard_map/ppermute | solution.py:17
  106.7 8.7 %collective-permute-start.32 = (bf16[64,2048]{1,0:T(8,128)(2,1)S(1)}, bf16[64,2048]{1,0:T(8,128)(2,1)S(1)}, u32[]{:S(2)}, u32[]{:S(2)}) collective-permute-start(bf16[64,2048]{1,0:T(8,128)(2,1)S(1)} %collective-permute-done.27.refs_1_), channel_id=1, source_target_pairs={{0,4},{2,6},{4,0},{6,2},{8,12},{10,14},{12,8},{14,10},{16,20},{18,... | collective-permute-start | bytes 786440 | tf_op jit(solution)/shard_map/ppermute | solution.py:17
  108.3 7.2 %collective-permute-start.33 = (bf16[64,2048]{1,0:T(8,128)(2,1)S(1)}, bf16[64,2048]{1,0:T(8,128)(2,1)S(1)}, u32[]{:S(2)}, u32[]{:S(2)}) collective-permute-start(bf16[64,2048]{1,0:T(8,128)(2,1)S(1)} %collective-permute-done.28.refs_0_), channel_id=1, source_target_pairs={{0,2},{2,0},{4,6},{6,4},{8,10},{10,8},{12,14},{14,12},{16,18},{18,... | collective-permute-start | bytes 786440 | tf_op jit(solution)/shard_map/ppermute | solution.py:17
  110.9 11.4 %collective-permute-start.31 = (bf16[256,768]{1,0:T(8,128)(2,1)S(1)}, bf16[256,768]{1,0:T(8,128)(2,1)S(1)}, u32[]{:S(2)}, u32[]{:S(2)}) collective-permute-start(bf16[256,768]{1,0:T(8,128)(2,1)S(1)} %get-tuple-element.76), channel_id=1, source_target_pairs={{0,1},{1,0},{2,3},{3,2},{4,5},{5,4},{6,7},{7,6},{8,9},{9,8},{10,11... | collective-permute-start | bytes 1179656 | tf_op jit(solution)/shard_map/ppermute | solution.py:17
  115.4 4.1 %collective-permute-start.34 = (bf16[64,2048]{1,0:T(8,128)(2,1)S(1)}, bf16[64,2048]{1,0:T(8,128)(2,1)S(1)}, u32[]{:S(2)}, u32[]{:S(2)}) collective-permute-start(bf16[64,2048]{1,0:T(8,128)(2,1)S(1)} %collective-permute-done.32.refs_1_), channel_id=1, source_target_pairs={{0,2},{2,0},{4,6},{6,4},{8,10},{10,8},{12,14},{14,12},{16,18},{18,... | collective-permute-start | bytes 786440 | tf_op jit(solution)/shard_map/ppermute | solution.py:17
  124.7 10.6 %collective-permute-start.35 = (bf16[256,768]{1,0:T(8,128)(2,1)S(1)}, bf16[256,768]{1,0:T(8,128)(2,1)S(1)}, u32[]{:S(2)}, u32[]{:S(2)}) collective-permute-start(bf16[256,768]{1,0:T(8,128)(2,1)S(1)} %get-tuple-element.84), channel_id=1, source_target_pairs={{0,1},{1,0},{2,3},{3,2},{4,5},{5,4},{6,7},{7,6},{8,9},{9,8},{10,11... | collective-permute-start | bytes 1179656 | tf_op jit(solution)/shard_map/ppermute | solution.py:17
  130.3 23.7 %slice-start = ((s8[12582912]{0:T(1024)(128)(4,1)}), s8[4194304]{0:T(1024)(128)(4,1)S(1)}, s32[]{:S(2)}) async-start(s8[12582912]{0:T(1024)(128)(4,1)} %bitcast.8), calls=%async_computation | async-start | bytes 8388608
  130.3 23.7 %slice-start.1 = ((s8[12582912]{0:T(1024)(128)(4,1)}), s8[4194304]{0:T(1024)(128)(4,1)S(1)}, s32[]{:S(2)}) async-start(s8[12582912]{0:T(1024)(128)(4,1)} %bitcast.8), calls=%async_computation.1 | async-start | bytes 8388608
  135.3 18.7 %slice-start.2 = ((s8[12582912]{0:T(1024)(128)(4,1)}), s8[4194304]{0:T(1024)(128)(4,1)S(1)}, s32[]{:S(2)}) async-start(s8[12582912]{0:T(1024)(128)(4,1)} %bitcast.8), calls=%async_computation.2 | async-start | bytes 8388608
  139.3 2.0 %collective-permute-start.38 = (bf16[128,2048]{1,0:T(8,128)(2,1)S(1)}, bf16[128,2048]{1,0:T(8,128)(2,1)S(1)}, u32[]{:S(2)}, u32[]{:S(2)}) collective-permute-start(bf16[128,2048]{1,0:T(8,128)(2,1)S(1)} %get-tuple-element.99), channel_id=1, source_target_pairs={{0,2},{2,0},{4,6},{6,4},{8,10},{10,8},{12,14},{14,12},{16,18},{18,... | collective-permute-start | bytes 1572872 | tf_op jit(solution)/shard_map/ppermute | solution.py:17
  139.4 5.1 %collective-permute-start.37 = (bf16[128,2048]{1,0:T(8,128)(2,1)S(1)}, bf16[128,2048]{1,0:T(8,128)(2,1)S(1)}, u32[]{:S(2)}, u32[]{:S(2)}) collective-permute-start(bf16[128,2048]{1,0:T(8,128)(2,1)S(1)} %get-tuple-element.97), channel_id=1, source_target_pairs={{0,2},{2,0},{4,6},{6,4},{8,10},{10,8},{12,14},{14,12},{16,18},{18,... | collective-permute-start | bytes 1572872 | tf_op jit(solution)/shard_map/ppermute | solution.py:17
  141.4 8.4 %collective-permute-start.39 = (bf16[64,2048]{1,0:T(8,128)(2,1)S(1)}, bf16[64,2048]{1,0:T(8,128)(2,1)S(1)}, u32[]{:S(2)}, u32[]{:S(2)}) collective-permute-start(bf16[64,2048]{1,0:T(8,128)(2,1)S(1)} %get-tuple-element.118), channel_id=1, source_target_pairs={{0,4},{2,6},{4,0},{6,2},{8,12},{10,14},{12,8},{14,10},{16,20},{18,... | collective-permute-start | bytes 786440 | tf_op jit(solution)/shard_map/ppermute | solution.py:17
  142.5 10.2 %collective-permute-start.43 = (bf16[128,2048]{1,0:T(8,128)(2,1)S(1)}, bf16[128,2048]{1,0:T(8,128)(2,1)S(1)}, u32[]{:S(2)}, u32[]{:S(2)}) collective-permute-start(bf16[128,2048]{1,0:T(8,128)(2,1)S(1)} %get-tuple-element.103), channel_id=1, source_target_pairs={{0,2},{2,0},{4,6},{6,4},{8,10},{10,8},{12,14},{14,12},{16,18},{18,... | collective-permute-start | bytes 1572872 | tf_op jit(solution)/shard_map/ppermute | solution.py:17
  142.5 18.1 %collective-permute-start.36 = (bf16[128,2048]{1,0:T(8,128)(2,1)S(1)}, bf16[128,2048]{1,0:T(8,128)(2,1)S(1)}, u32[]{:S(2)}, u32[]{:S(2)}) collective-permute-start(bf16[128,2048]{1,0:T(8,128)(2,1)S(1)} %get-tuple-element.93), channel_id=1, source_target_pairs={{0,2},{2,0},{4,6},{6,4},{8,10},{10,8},{12,14},{14,12},{16,18},{18,... | collective-permute-start | bytes 1572872 | tf_op jit(solution)/shard_map/ppermute | solution.py:17
  143.0 8.2 %collective-permute-start.40 = (bf16[64,2048]{1,0:T(8,128)(2,1)S(1)}, bf16[64,2048]{1,0:T(8,128)(2,1)S(1)}, u32[]{:S(2)}, u32[]{:S(2)}) collective-permute-start(bf16[64,2048]{1,0:T(8,128)(2,1)S(1)} %get-tuple-element.119), channel_id=1, source_target_pairs={{0,1},{1,0},{2,3},{3,2},{4,5},{5,4},{6,7},{7,6},{8,9},{9,8},{10,11... | collective-permute-start | bytes 786440 | tf_op jit(solution)/shard_map/ppermute | solution.py:17
  151.2 9.4 %collective-permute-start.41 = (bf16[64,2048]{1,0:T(8,128)(2,1)S(1)}, bf16[64,2048]{1,0:T(8,128)(2,1)S(1)}, u32[]{:S(2)}, u32[]{:S(2)}) collective-permute-start(bf16[64,2048]{1,0:T(8,128)(2,1)S(1)} %get-tuple-element.100), channel_id=1, source_target_pairs={{0,1},{1,0},{2,3},{3,2},{4,5},{5,4},{6,7},{7,6},{8,9},{9,8},{10,11... | collective-permute-start | bytes 786440 | tf_op jit(solution)/shard_map/ppermute | solution.py:17
  152.9 7.7 %collective-permute-start.44 = (bf16[64,2048]{1,0:T(8,128)(2,1)S(1)}, bf16[64,2048]{1,0:T(8,128)(2,1)S(1)}, u32[]{:S(2)}, u32[]{:S(2)}) collective-permute-start(bf16[64,2048]{1,0:T(8,128)(2,1)S(1)} %get-tuple-element.120), channel_id=1, source_target_pairs={{0,4},{2,6},{4,0},{6,2},{8,12},{10,14},{12,8},{14,10},{16,20},{18,... | collective-permute-start | bytes 786440 | tf_op jit(solution)/shard_map/ppermute | solution.py:17
  160.8 6.9 %collective-permute-start.46 = (bf16[64,2048]{1,0:T(8,128)(2,1)S(1)}, bf16[64,2048]{1,0:T(8,128)(2,1)S(1)}, u32[]{:S(2)}, u32[]{:S(2)}) collective-permute-start(bf16[64,2048]{1,0:T(8,128)(2,1)S(1)} %add_convert_fusion), channel_id=1, source_target_pairs={{0,8},{2,10},{4,12},{6,14},{8,0},{10,2},{12,4},{14,6},{16,24},{18,... | collective-permute-start | bytes 786440 | tf_op jit(solution)/shard_map/ppermute | solution.py:17
  161.0 6.7 %collective-permute-start.42 = (bf16[64,2048]{1,0:T(8,128)(2,1)S(1)}, bf16[64,2048]{1,0:T(8,128)(2,1)S(1)}, u32[]{:S(2)}, u32[]{:S(2)}) collective-permute-start(bf16[64,2048]{1,0:T(8,128)(2,1)S(1)} %get-tuple-element.101), channel_id=1, source_target_pairs={{0,1},{1,0},{2,3},{3,2},{4,5},{5,4},{6,7},{7,6},{8,9},{9,8},{10,11... | collective-permute-start | bytes 786440 | tf_op jit(solution)/shard_map/ppermute | solution.py:17
  161.5 6.4 %collective-permute-start.45 = (bf16[64,2048]{1,0:T(8,128)(2,1)S(1)}, bf16[64,2048]{1,0:T(8,128)(2,1)S(1)}, u32[]{:S(2)}, u32[]{:S(2)}) collective-permute-start(bf16[64,2048]{1,0:T(8,128)(2,1)S(1)} %get-tuple-element.104), channel_id=1, source_target_pairs={{0,4},{2,6},{4,0},{6,2},{8,12},{10,14},{12,8},{14,10},{16,20},{18,... | collective-permute-start | bytes 786440 | tf_op jit(solution)/shard_map/ppermute | solution.py:17
  168.0 7.4 %collective-permute-start.47 = (bf16[32,2048]{1,0:T(8,128)(2,1)S(1)}, bf16[32,2048]{1,0:T(8,128)(2,1)S(1)}, u32[]{:S(2)}, u32[]{:S(2)}) collective-permute-start(bf16[32,2048]{1,0:T(8,128)(2,1)S(1)} %add_convert_fusion.9), channel_id=1, source_target_pairs={{0,16},{2,18},{4,20},{6,22},{8,24},{10,26},{12,28},{14,30},{16,0},... | collective-permute-start | bytes 393224 | tf_op jit(solution)/shard_map/ppermute | solution.py:17

commit v14 on v13

--- a/solution.py
+++ b/solution.py
@@ -691,7 +691,12 @@
 
     by_half = [pair[0] for pair in crossed]
     across_upper = swap(
-        add([part[upper] for part in leave] + by_half).astype(BF16), "expert", 2
+        tie(
+            add([part[upper] for part in leave] + by_half).astype(BF16),
+            *[pair[1] for pair in crossed],
+        ),
+        "expert",
+        2,
     )
     arrived_upper = [
         swap(tie(add([part[upper] for part in keep]).astype(BF16), *by_half), "half", d)
@@ -711,9 +716,7 @@
     )
     arrived_lower = [
         swap(
-            tie(
-                add([part[lower] for part in keep] + [pair[1]]).astype(BF16), *arrived_upper
-            ),
+            add([part[lower] for part in keep] + [tie(pair[1], *arrived_upper)]).astype(BF16),
             "half",
             d,
         )

time: 176 us -> 175 us (level)
  transfers between devices with their start and end apart: 48 -> 48, of which waited for: 30 -> 29; matrix products, arithmetic and copies ran while one was open for 2% -> 2% of each run, Pallas kernels for 29% -> 29%
where the time goes in v14:
time: 175 us
  Pallas kernels  60.2 us (34%)
  waiting for transfers between devices  56.3 us (32%)
  starting transfers between devices  51.2 us (29%)
  local copies, waits for them, and re-layouts  4.32 us (2%)
  other arithmetic  1.97 us (1%)
    pallas_call x20, Pallas kernels, call(): pl.pallas_call(kernel, grid_spec=pltpu.PrefetchScalarGridSpec(num_scalar_...  60.2 us
    ppermute x48, waiting for transfers between devices, swap(): return lax.ppermute(array, axis, [(i, i ^ distance) for i in range(size)])  56.3 us
    ppermute x48, starting transfers between devices, swap(): return lax.ppermute(array, axis, [(i, i ^ distance) for i in range(size)])  51.2 us
    unnamed x26, local copies, waits for them, and re-layouts  4.28 us
  transfers between devices with their start and end apart: 48, of which 29 were waited for; matrix products, arithmetic and copies ran while one was open for 2% of the time, Pallas kernels for 29%

profile of v14, /device:TPU:0, one launch (start us, length us, event | category | flops | bytes accessed | tf_op | source)
XLA Modules:
  0.0 175.0 jit_solution(2232300492466417292)
XLA Ops:
  0.6 3.0 %collective-permute-start.1 = (bf16[32,4096]{1,0:T(8,128)(2,1)}, bf16[32,4096]{1,0:T(8,128)(2,1)S(1)}, u32[]{:S(2)}, u32[]{:S(2)}) collective-permute-start(bf16[32,4096]{1,0:T(8,128)(2,1)} %refs_0_.1), channel_id=1, source_target_pairs={{0,4},{2,6},{4,0},{6,2},{8,12},{10,14},{12,8},{14,10},{16,20},{18,... | collective-permute-start | bytes 786440 | tf_op jit(solution)/shard_map/ppermute | solution.py:17
  3.6 2.6 %collective-permute-start = (bf16[32,4096]{1,0:T(8,128)(2,1)}, bf16[32,4096]{1,0:T(8,128)(2,1)S(1)}, u32[]{:S(2)}, u32[]{:S(2)}) collective-permute-start(bf16[32,4096]{1,0:T(8,128)(2,1)} %refs_0_.1), channel_id=1, source_target_pairs={{0,16},{2,18},{4,20},{6,22},{8,24},{10,26},{12,28},{14,30},{16,0},... | collective-permute-start | bytes 786440 | tf_op jit(solution)/shard_map/ppermute | solution.py:17
  6.2 1.6 collective-permute-start.3
  10.2 0.9 copy-done.1
  11.1 0.9 copy-done.2
  12.0 6.2 %shard_map.122.refs_4_.refs_8_.refs_3_ = bf16[4096,1536]{1,0:T(8,128)(2,1)S(1)} custom-call(s32[2]{0:T(128)S(1)} %pad_add_fusion.place_ref, bf16[2,4096,768]{2,1,0:T(8,128)(2,1)} %bitcast.7, f32[2,32,768]{2,1,0:T(8,128)S(1)} %bitcast.13, f32[2,32,768]{2,1,0:T(8,128)S(1)} %bitcast.14), custom_call_target="tpu_custom_call" | custom-call | bytes 25 | tf_op jit(solution)/shard_map/pallas_call | solution.py:112
  18.4 1.4 collective-permute-start.4
  20.4 2.3 %collective-permute-start.2 = (bf16[32,128]{1,0:T(8,128)(2,1)S(1)}, bf16[32,128]{1,0:T(8,128)(2,1)S(1)}, u32[]{:S(2)}, u32[]{:S(2)}) collective-permute-start(bf16[32,128]{1,0:T(8,128)(2,1)S(1)} %shard_map.121), channel_id=1, source_target_pairs={{0,16},{2,18},{4,20},{6,22},{8,24},{10,26},{12,28},{14,30},{16,0},... | collective-permute-start | bytes 24584 | tf_op jit(solution)/shard_map/ppermute | solution.py:17
  22.7 2.3 %collective-permute-done.2 = bf16[32,128]{1,0:T(8,128)(2,1)S(1)} collective-permute-done((bf16[32,128]{1,0:T(8,128)(2,1)S(1)}, bf16[32,128]{1,0:T(8,128)(2,1)S(1)}, u32[]{:S(2)}, u32[]{:S(2)}) %collective-permute-start.2) | collective-permute-done | bytes 8224 | tf_op jit(solution)/shard_map/ppermute | solution.py:17
  25.7 1.1 collective-permute-done.5.refs_1_
  27.4 0.8 collective-permute-start.10
  29.2 4.1 %shard_map.124 = (bf16[256,768]{1,0:T(8,128)(2,1)S(1)}, f32[256,768]{1,0:T(8,128)S(1)}, f32[256,768]{1,0:T(8,128)S(1)}) custom-call(s32[2]{0:T(128)S(1)} %pad_add_fusion.place_ref, bf16[96,4096]{1,0:T(8,128)(2,1)S(1)} %shard_map.123.refs_0_, bf16[32,4096]{1,0:T(8,128)(2,1)S(1)} %collective-permute-done.4.refs_1_, ...), custom_call_target="tpu_custom_call" | custom-call | flops 3221 | bytes 16 | tf_op jit(solution)/shard_map/pallas_call | solution.py:112
  33.4 2.4 %shard_map.125.refs_2_.refs_6_ = bf16[1536,2048]{1,0:T(8,128)(2,1)S(1)} custom-call(s32[2]{0:T(128)S(1)} %pad_add_fusion.place_ref, bf16[1,1536,2048]{2,1,0:T(8,128)(2,1)S(1)} %bitcast.11, f32[1,12,2048]{2,1,0:T(8,128)S(1)} %copy.17.low_ref, f32[1,12,2048]{2,1,0:T(8,128)S(1)} %copy.18.high_ref), custom_call_target="tpu_custom_call" | custom-call | bytes 12 | tf_op jit(solution)/shard_map/pallas_call | solution.py:112
  35.9 3.9 %collective-permute-start.9 = (bf16[64,128]{1,0:T(8,128)(2,1)S(1)}, bf16[64,128]{1,0:T(8,128)(2,1)S(1)}, u32[]{:S(2)}, u32[]{:S(2)}) collective-permute-start(bf16[64,128]{1,0:T(8,128)(2,1)S(1)} %pad_maximum_fusion.2), channel_id=1, source_target_pairs={{0,8},{2,10},{4,12},{6,14},{8,0},{10,2},{12,4},{14,6},{16,24},{18,... | collective-permute-start | bytes 49160 | tf_op jit(solution)/shard_map/ppermute | solution.py:17
  39.7 2.1 %collective-permute-done.10.refs_1_.refs_3_.refs_5_.refs_7_ = bf16[64,4096]{1,0:T(8,128)(2,1)S(1)} collective-permute-done((bf16[64,4096]{1,0:T(8,128)(2,1)S(1)}, bf16[64,4096]{1,0:T(8,128)(2,1)S(1)}, u32[]{:S(2)}, u32[]{:S(2)}) %collective-permute-start.10) | collective-permute-done | bytes 524320 | tf_op jit(solution)/shard_map/ppermute | solution.py:17
  41.9 1.6 collective-permute-start.8
  43.8 4.1 %shard_map.128 = (bf16[256,768]{1,0:T(8,128)(2,1)S(1)}, f32[256,768]{1,0:T(8,128)S(1)}, f32[256,768]{1,0:T(8,128)S(1)}) custom-call(s32[2]{0:T(128)S(1)} %pad_add_fusion.place_ref, bf16[64,4096]{1,0:T(8,128)(2,1)S(1)} %shard_map.126.refs_0_.refs_2_.refs_4_.refs_6_, bf16[64,4096]{1,0:T(8,128)(2,1)S(1)} %collective-permute-done.10.refs_1_.refs_3_.refs_5_.refs_7_, ...), custom_call_target="tpu_custom_call" | custom-call | flops 3221 | bytes 18 | tf_op jit(solution)/shard_map/pallas_call | solution.py:112
  47.9 1.6 collective-permute-start.16
  50.0 3.4 %collective-permute-done.13 = bf16[128,128]{1,0:T(8,128)(2,1)S(1)} collective-permute-done((bf16[128,128]{1,0:T(8,128)(2,1)S(1)}, bf16[128,128]{1,0:T(8,128)(2,1)S(1)}, u32[]{:S(2)}, u32[]{:S(2)}) %collective-permute-start.13) | collective-permute-done | bytes 32800 | tf_op jit(solution)/shard_map/ppermute | solution.py:17
  53.8 0.8 collective-permute-done.14.refs_4_.refs_5_
  54.6 2.3 %shard_map.129 = (bf16[128,2048]{1,0:T(8,128)(2,1)S(1)}, bf16[128,2048]{1,0:T(8,128)(2,1)S(1)}) custom-call(s32[2]{0:T(128)S(1)} %pad_add_fusion.place_ref, bf16[256,768]{1,0:T(8,128)(2,1)S(1)} %get-tuple-element.62.refs_0_, bf16[256,768]{1,0:T(8,128)(2,1)S(1)} %collective-permute-done.8.refs_1_, bf16[1536,2048]{1,0:T(8,128)(2,1)S(1)} %shard_map.125.refs_2_.refs_6_, ...), custom_call_target="tpu_custom_call" | custom-call | flops 1610 | bytes 8 | tf_op jit(solution)/shard_map/pallas_call | solution.py:112
  57.0 4.9 %collective-permute-done.16.refs_1_ = bf16[256,768]{1,0:T(8,128)(2,1)S(1)} collective-permute-done((bf16[256,768]{1,0:T(8,128)(2,1)S(1)}, bf16[256,768]{1,0:T(8,128)(2,1)S(1)}, u32[]{:S(2)}, u32[]{:S(2)}) %collective-permute-start.16) | collective-permute-done | bytes 393248 | tf_op jit(solution)/shard_map/ppermute | solution.py:17
  61.8 2.3 %shard_map.130 = (bf16[128,2048]{1,0:T(8,128)(2,1)S(1)}, bf16[128,2048]{1,0:T(8,128)(2,1)S(1)}) custom-call(s32[2]{0:T(128)S(1)} %pad_add_fusion.place_ref, bf16[256,768]{1,0:T(8,128)(2,1)S(1)} %get-tuple-element.67.refs_0_, bf16[256,768]{1,0:T(8,128)(2,1)S(1)} %collective-permute-done.16.refs_1_, bf16[1536,2048]{1,0:T(8,128)(2,1)S(1)} %shard_map.125.refs_2_.refs_6_, ...), custom_call_target="tpu_custom_call" | custom-call | flops 1610 | bytes 8 | tf_op jit(solution)/shard_map/pallas_call | solution.py:112
  64.7 1.4 collective-permute-done.17
  66.8 1.5 collective-permute-start.19
  68.4 4.2 %collective-permute-done.18 = bf16[64,1024]{1,0:T(8,128)(2,1)S(1)} collective-permute-done((bf16[64,1024]{1,0:T(8,128)(2,1)S(1)}, bf16[64,1024]{1,0:T(8,128)(2,1)S(1)}, u32[]{:S(2)}, u32[]{:S(2)}) %collective-permute-start.18) | collective-permute-done | bytes 131104 | tf_op jit(solution)/shard_map/ppermute | solution.py:17
  72.6 2.0 %collective-permute-done.19 = bf16[64,1024]{1,0:T(8,128)(2,1)S(1)} collective-permute-done((bf16[64,1024]{1,0:T(8,128)(2,1)S(1)}, bf16[64,1024]{1,0:T(8,128)(2,1)S(1)}, u32[]{:S(2)}, u32[]{:S(2)}) %collective-permute-start.19) | collective-permute-done | bytes 131104 | tf_op jit(solution)/shard_map/ppermute | solution.py:17
  75.3 2.8 %collective-permute-start.21 = (bf16[64,1024]{1,0:T(8,128)(2,1)S(1)}, bf16[64,1024]{1,0:T(8,128)(2,1)S(1)}, u32[]{:S(2)}, u32[]{:S(2)}) collective-permute-start(bf16[64,1024]{1,0:T(8,128)(2,1)S(1)} %get-tuple-element.123), channel_id=1, source_target_pairs={{0,8},{2,10},{4,12},{6,14},{8,0},{10,2},{12,4},{14,6},{16,24},{18,... | collective-permute-start | bytes 393224 | tf_op jit(solution)/shard_map/ppermute | solution.py:17
  78.2 4.1 %collective-permute-done.21 = bf16[64,1024]{1,0:T(8,128)(2,1)S(1)} collective-permute-done((bf16[64,1024]{1,0:T(8,128)(2,1)S(1)}, bf16[64,1024]{1,0:T(8,128)(2,1)S(1)}, u32[]{:S(2)}, u32[]{:S(2)}) %collective-permute-start.21) | collective-permute-done | bytes 131104 | tf_op jit(solution)/shard_map/ppermute | solution.py:17
  82.2 1.4 collective-permute-done.23
  83.7 2.3 %collective-permute-start.22 = (bf16[32,1024]{1,0:T(8,128)(2,1)S(1)}, bf16[32,1024]{1,0:T(8,128)(2,1)S(1)}, u32[]{:S(2)}, u32[]{:S(2)}) collective-permute-start(bf16[32,1024]{1,0:T(8,128)(2,1)S(1)} %get-tuple-element.117), channel_id=1, source_target_pairs={{0,16},{2,18},{4,20},{6,22},{8,24},{10,26},{12,28},{14,30},{16,0},... | collective-permute-start | bytes 196616 | tf_op jit(solution)/shard_map/ppermute | solution.py:17
  86.7 2.6 %collective-permute-done.22 = bf16[32,1024]{1,0:T(8,128)(2,1)S(1)} collective-permute-done((bf16[32,1024]{1,0:T(8,128)(2,1)S(1)}, bf16[32,1024]{1,0:T(8,128)(2,1)S(1)}, u32[]{:S(2)}, u32[]{:S(2)}) %collective-permute-start.22) | collective-permute-done | bytes 65568 | tf_op jit(solution)/shard_map/ppermute | solution.py:17
  89.3 2.4 %collective-permute-done.24 = bf16[32,1024]{1,0:T(8,128)(2,1)S(1)} collective-permute-done((bf16[32,1024]{1,0:T(8,128)(2,1)S(1)}, bf16[32,1024]{1,0:T(8,128)(2,1)S(1)}, u32[]{:S(2)}, u32[]{:S(2)}) %collective-permute-start.24) | collective-permute-done | bytes 65568 | tf_op jit(solution)/shard_map/ppermute | solution.py:17
  92.1 2.7 %collective-permute-start.26 = (bf16[32,1024]{1,0:T(8,128)(2,1)S(1)}, bf16[32,1024]{1,0:T(8,128)(2,1)S(1)}, u32[]{:S(2)}, u32[]{:S(2)}) collective-permute-start(bf16[32,1024]{1,0:T(8,128)(2,1)S(1)} %get-tuple-element.114.refs_1_), channel_id=1, source_target_pairs={{0,16},{2,18},{4,20},{6,22},{8,24},{10,26},{12,28},{14,30},{16,0},... | collective-permute-start | bytes 196616 | tf_op jit(solution)/shard_map/ppermute | solution.py:17
  94.9 2.3 %collective-permute-done.25.refs_2_ = bf16[32,1024]{1,0:T(8,128)(2,1)S(1)} collective-permute-done((bf16[32,1024]{1,0:T(8,128)(2,1)S(1)}, bf16[32,1024]{1,0:T(8,128)(2,1)S(1)}, u32[]{:S(2)}, u32[]{:S(2)}) %collective-permute-start.25) | collective-permute-done | bytes 65568 | tf_op jit(solution)/shard_map/ppermute | solution.py:17
  98.5 1.8 %collective-permute-start.27 = (bf16[64,2048]{1,0:T(8,128)(2,1)S(1)}, bf16[64,2048]{1,0:T(8,128)(2,1)S(1)}, u32[]{:S(2)}, u32[]{:S(2)}) collective-permute-start(bf16[64,2048]{1,0:T(8,128)(2,1)S(1)} %shard_map.131.refs_0_), channel_id=1, source_target_pairs={{0,8},{2,10},{4,12},{6,14},{8,0},{10,2},{12,4},{14,6},{16,24},{18,... | collective-permute-start | bytes 786440 | tf_op jit(solution)/shard_map/ppermute | solution.py:17
  100.3 1.5 collective-permute-start.28
  101.9 3.1 %collective-permute-done.27.refs_1_ = bf16[64,2048]{1,0:T(8,128)(2,1)S(1)} collective-permute-done((bf16[64,2048]{1,0:T(8,128)(2,1)S(1)}, bf16[64,2048]{1,0:T(8,128)(2,1)S(1)}, u32[]{:S(2)}, u32[]{:S(2)}) %collective-permute-start.27) | collective-permute-done | bytes 262176 | tf_op jit(solution)/shard_map/ppermute | solution.py:17
  104.9 1.8 %collective-permute-done.28.refs_0_ = bf16[64,2048]{1,0:T(8,128)(2,1)S(1)} collective-permute-done((bf16[64,2048]{1,0:T(8,128)(2,1)S(1)}, bf16[64,2048]{1,0:T(8,128)(2,1)S(1)}, u32[]{:S(2)}, u32[]{:S(2)}) %collective-permute-start.28) | collective-permute-done | bytes 262176 | tf_op jit(solution)/shard_map/ppermute | solution.py:17
  106.7 1.5 collective-permute-start.32
  108.5 2.4 %shard_map.132 = (bf16[256,2048]{1,0:T(8,128)(2,1)S(1)}, f32[256,768]{1,0:T(8,128)S(1)}, bf16[256,768]{1,0:T(8,128)(2,1)S(1)}) custom-call(s32[2]{0:T(128)S(1)} %pad_add_fusion.place_ref, bf16[64,2048]{1,0:T(8,128)(2,1)S(1)} %shard_map.131.refs_0_, bf16[64,2048]{1,0:T(8,128)(2,1)S(1)} %collective-permute-done.27.refs_1_, ...), custom_call_target="tpu_custom_call" | custom-call | flops 1610 | bytes 9 | tf_op jit(solution)/shard_map/pallas_call | solution.py:112
  110.9 1.6 collective-permute-start.31
  112.5 2.9 %collective-permute-done.32.refs_1_ = bf16[64,2048]{1,0:T(8,128)(2,1)S(1)} collective-permute-done((bf16[64,2048]{1,0:T(8,128)(2,1)S(1)}, bf16[64,2048]{1,0:T(8,128)(2,1)S(1)}, u32[]{:S(2)}, u32[]{:S(2)}) %collective-permute-start.32) | collective-permute-done | bytes 262176 | tf_op jit(solution)/shard_map/ppermute | solution.py:17
  115.4 4.1 %shard_map.134.refs_4_ = f32[2,12,2048]{2,1,0:T(8,128)S(1)} custom-call(s32[2]{0:T(128)S(1)} %pad_add_fusion.place_ref, bf16[256,768]{1,0:T(8,128)(2,1)S(1)} %get-tuple-element.62.refs_0_, bf16[256,768]{1,0:T(8,128)(2,1)S(1)} %collective-permute-done.8.refs_1_, bf16[256,2048]{1,0:T(8,128)(2,1)S(1)} %get-tuple-element.81.refs_2_, ...), custom_call_target="tpu_custom_call" | custom-call | flops 1610 | bytes 8 | tf_op jit(solution)/shard_map/pallas_call | solution.py:112
  119.6 2.7 %collective-permute-done.31.refs_0_ = bf16[256,768]{1,0:T(8,128)(2,1)S(1)} collective-permute-done((bf16[256,768]{1,0:T(8,128)(2,1)S(1)}, bf16[256,768]{1,0:T(8,128)(2,1)S(1)}, u32[]{:S(2)}, u32[]{:S(2)}) %collective-permute-start.31) | collective-permute-done | bytes 393248 | tf_op jit(solution)/shard_map/ppermute | solution.py:17
  122.3 2.4 %shard_map.135 = (bf16[256,2048]{1,0:T(8,128)(2,1)S(1)}, f32[256,768]{1,0:T(8,128)S(1)}, bf16[256,768]{1,0:T(8,128)(2,1)S(1)}) custom-call(s32[2]{0:T(128)S(1)} %pad_add_fusion.place_ref, bf16[64,2048]{1,0:T(8,128)(2,1)S(1)} %collective-permute-done.28.refs_0_, bf16[64,2048]{1,0:T(8,128)(2,1)S(1)} %collective-permute-done.32.refs_1_, ...), custom_call_target="tpu_custom_call" | custom-call | flops 1610 | bytes 9 | tf_op jit(solution)/shard_map/pallas_call | solution.py:112
  124.7 1.6 collective-permute-start.35
  126.3 4.0 %shard_map.136 = f32[2,12,2048]{2,1,0:T(8,128)S(1)} custom-call(s32[2]{0:T(128)S(1)} %pad_add_fusion.place_ref, bf16[256,768]{1,0:T(8,128)(2,1)S(1)} %get-tuple-element.67.refs_0_, bf16[256,768]{1,0:T(8,128)(2,1)S(1)} %collective-permute-done.16.refs_1_, bf16[256,2048]{1,0:T(8,128)(2,1)S(1)} %get-tuple-element.87.refs_2_, ...), custom_call_target="tpu_custom_call" | custom-call | flops 1610 | bytes 8 | tf_op jit(solution)/shard_map/pallas_call | solution.py:112
  130.3 4.0 %shard_map.133 = (bf16[256,1536]{1,0:T(8,128)(2,1)S(1)}, bf16[128,2048]{1,0:T(8,128)(2,1)S(1)}, bf16[128,2048]{1,0:T(8,128)(2,1)S(1)}, bf16[128,2048]{1,0:T(8,128)(2,1)S(1)}, bf16[128,2048]{1,0:T(8,128)(2,1)S(1)}) custom-call(s32[2]{0:T(128)S(1)} %pad_add_fusion.place_ref, f32[256,768]{1,0:T(8,128)S(1)} %get-tuple-element.76.grad_own_ref, ...), custom_call_target="tpu_custom_call" | custom-call | flops 3221 | bytes 18 | tf_op jit(solution)/shard_map/pallas_call | solution.py:112
  134.3 0.9 collective-permute-done.35.refs_0_
  135.3 4.0 %shard_map.137 = (bf16[256,1536]{1,0:T(8,128)(2,1)S(1)}, bf16[128,2048]{1,0:T(8,128)(2,1)S(1)}, bf16[128,2048]{1,0:T(8,128)(2,1)S(1)}, bf16[128,2048]{1,0:T(8,128)(2,1)S(1)}, bf16[128,2048]{1,0:T(8,128)(2,1)S(1)}) custom-call(s32[2]{0:T(128)S(1)} %pad_add_fusion.place_ref, f32[256,768]{1,0:T(8,128)S(1)} %get-tuple-element.84.grad_own_ref, ...), custom_call_target="tpu_custom_call" | custom-call | flops 3221 | bytes 18 | tf_op jit(solution)/shard_map/pallas_call | solution.py:112
  140.4 0.9 collective-permute-done.38
  141.4 1.6 collective-permute-start.40
  143.0 1.0 collective-permute-start.39
  144.0 5.8 %collective-permute-done.40 = bf16[64,2048]{1,0:T(8,128)(2,1)S(1)} collective-permute-done((bf16[64,2048]{1,0:T(8,128)(2,1)S(1)}, bf16[64,2048]{1,0:T(8,128)(2,1)S(1)}, u32[]{:S(2)}, u32[]{:S(2)}) %collective-permute-start.40) | collective-permute-done | bytes 262176 | tf_op jit(solution)/shard_map/ppermute | solution.py:17
  149.8 1.5 collective-permute-start.41
  151.5 1.1 collective-permute-start.44
  152.6 6.6 %shard_map.138.refs_15_ = f32[4,32,768]{2,1,0:T(8,128)} custom-call(s32[2]{0:T(128)S(1)} %pad_add_fusion.place_ref, bf16[96,4096]{1,0:T(8,128)(2,1)S(1)} %shard_map.123.refs_0_, bf16[32,4096]{1,0:T(8,128)(2,1)S(1)} %collective-permute-done.4.refs_1_, bf16[96,4096]{1,0:T(8,128)(2,1)S(1)} %collective-permute-done.6.refs_2_, ...), custom_call_target="tpu_custom_call" | custom-call | flops 3221 | bytes 20 | tf_op jit(solution)/shard_map/pallas_call | solution.py:112
  160.3 1.0 collective-permute-start.45
  161.3 4.2 %shard_map.139.refs_15_ = f32[4,32,768]{2,1,0:T(8,128)} custom-call(s32[2]{0:T(128)S(1)} %pad_add_fusion.place_ref, bf16[96,4096]{1,0:T(8,128)(2,1)S(1)} %shard_map.123.refs_0_, bf16[32,4096]{1,0:T(8,128)(2,1)S(1)} %collective-permute-done.4.refs_1_, bf16[96,4096]{1,0:T(8,128)(2,1)S(1)} %collective-permute-done.6.refs_2_, ...), custom_call_target="tpu_custom_call", output_to_operand_aliasing={{}: (16, {})} | custom-call | flops 1610 | bytes 20 | tf_op jit(solution)/shard_map/pallas_call | solution.py:112
  165.5 0.9 collective-permute-done.46
  166.9 2.6 %collective-permute-start.47 = (bf16[32,2048]{1,0:T(8,128)(2,1)S(1)}, bf16[32,2048]{1,0:T(8,128)(2,1)S(1)}, u32[]{:S(2)}, u32[]{:S(2)}) collective-permute-start(bf16[32,2048]{1,0:T(8,128)(2,1)S(1)} %add_convert_fusion.9), channel_id=1, source_target_pairs={{0,16},{2,18},{4,20},{6,22},{8,24},{10,26},{12,28},{14,30},{16,0},... | collective-permute-start | bytes 393224 | tf_op jit(solution)/shard_map/ppermute | solution.py:17
  169.5 0.8 copy.19
  170.3 3.9 %shard_map.140 = f32[4,32,768]{2,1,0:T(8,128)} custom-call(s32[2]{0:T(128)S(1)} %pad_add_fusion.place_ref, bf16[96,4096]{1,0:T(8,128)(2,1)S(1)} %shard_map.123.refs_0_, bf16[32,4096]{1,0:T(8,128)(2,1)S(1)} %collective-permute-done.4.refs_1_, bf16[96,4096]{1,0:T(8,128)(2,1)S(1)} %collective-permute-done.6.refs_2_, ...), custom_call_target="tpu_custom_call", output_to_operand_aliasing={{}: (16, {})} | custom-call | flops 1610 | bytes 20 | tf_op jit(solution)/shard_map/pallas_call | solution.py:112
  (97 shorter events, 15.2 us)
Async XLA Ops:
  0.6 17.6 %collective-permute-start.1 = (bf16[32,4096]{1,0:T(8,128)(2,1)}, bf16[32,4096]{1,0:T(8,128)(2,1)S(1)}, u32[]{:S(2)}, u32[]{:S(2)}) collective-permute-start(bf16[32,4096]{1,0:T(8,128)(2,1)} %refs_0_.1), channel_id=1, source_target_pairs={{0,4},{2,6},{4,0},{6,2},{8,12},{10,14},{12,8},{14,10},{16,20},{18,... | collective-permute-start | bytes 786440 | tf_op jit(solution)/shard_map/ppermute | solution.py:17
  3.6 14.6 %collective-permute-start = (bf16[32,4096]{1,0:T(8,128)(2,1)}, bf16[32,4096]{1,0:T(8,128)(2,1)S(1)}, u32[]{:S(2)}, u32[]{:S(2)}) collective-permute-start(bf16[32,4096]{1,0:T(8,128)(2,1)} %refs_0_.1), channel_id=1, source_target_pairs={{0,16},{2,18},{4,20},{6,22},{8,24},{10,26},{12,28},{14,30},{16,0},... | collective-permute-start | bytes 786440 | tf_op jit(solution)/shard_map/ppermute | solution.py:17
  6.2 12.2 %collective-permute-start.3 = (bf16[32,4096]{1,0:T(8,128)(2,1)}, bf16[32,4096]{1,0:T(8,128)(2,1)S(1)}, u32[]{:S(2)}, u32[]{:S(2)}) collective-permute-start(bf16[32,4096]{1,0:T(8,128)(2,1)} %refs_0_.1), channel_id=1, source_target_pairs={{0,8},{2,10},{4,12},{6,14},{8,0},{10,2},{12,4},{14,6},{16,24},{18,... | collective-permute-start | bytes 786440 | tf_op jit(solution)/shard_map/ppermute | solution.py:17
  10.2 0.9 copy-start.1
  11.1 0.9 copy-start.2
  12.0 13.0 %copy-start = (bf16[32,4096]{1,0:T(8,128)(2,1)S(1)}, bf16[32,4096]{1,0:T(8,128)(2,1)}, u32[]{:S(2)}) copy-start(bf16[32,4096]{1,0:T(8,128)(2,1)} %refs_0_.1) | copy-start | bytes 786436
  12.0 17.2 %copy-start.4 = (f32[1,12,2048]{2,0,1:T(1,128)S(1)}, f32[1,12,2048]{2,0,1:T(1,128)}, u32[]{:S(2)}) copy-start(f32[1,12,2048]{2,0,1:T(1,128)} %param.19) | copy-start | bytes 294916
  18.2 15.1 %copy-start.5 = (f32[1,12,2048]{2,0,1:T(1,128)S(1)}, f32[1,12,2048]{2,0,1:T(1,128)}, u32[]{:S(2)}) copy-start(f32[1,12,2048]{2,0,1:T(1,128)} %param.18) | copy-start | bytes 294916
  18.2 15.2 %slice-start.3 = ((s8[6291456]{0:T(1024)(128)(4,1)}), s8[4194304]{0:T(1024)(128)(4,1)S(1)}, s32[]{:S(2)}) async-start(s8[6291456]{0:T(1024)(128)(4,1)} %bitcast.10), calls=%async_computation.3 | async-start | bytes 8388608
  18.4 7.3 %collective-permute-start.4 = (bf16[32,4096]{1,0:T(8,128)(2,1)S(1)}, bf16[32,4096]{1,0:T(8,128)(2,1)S(1)}, u32[]{:S(2)}, u32[]{:S(2)}) collective-permute-start(bf16[32,4096]{1,0:T(8,128)(2,1)S(1)} %collective-permute-done.refs_1_.refs_0_), channel_id=1, source_target_pairs={{0,8},{2,10},{4,12},{6,14},{8,0},{10,2},{12,4},{14,6},{16,24},{18,... | collective-permute-start | bytes 786440 | tf_op jit(solution)/shard_map/ppermute | solution.py:17
  19.9 7.0 %collective-permute-start.5 = (bf16[32,4096]{1,0:T(8,128)(2,1)S(1)}, bf16[32,4096]{1,0:T(8,128)(2,1)S(1)}, u32[]{:S(2)}, u32[]{:S(2)}) collective-permute-start(bf16[32,4096]{1,0:T(8,128)(2,1)S(1)} %collective-permute-done.3.refs_2_), channel_id=1, source_target_pairs={{0,4},{2,6},{4,0},{6,2},{8,12},{10,14},{12,8},{14,10},{16,20},{18,... | collective-permute-start | bytes 786440 | tf_op jit(solution)/shard_map/ppermute | solution.py:17
  20.4 4.7 %collective-permute-start.2 = (bf16[32,128]{1,0:T(8,128)(2,1)S(1)}, bf16[32,128]{1,0:T(8,128)(2,1)S(1)}, u32[]{:S(2)}, u32[]{:S(2)}) collective-permute-start(bf16[32,128]{1,0:T(8,128)(2,1)S(1)} %shard_map.121), channel_id=1, source_target_pairs={{0,16},{2,18},{4,20},{6,22},{8,24},{10,26},{12,28},{14,30},{16,0},... | collective-permute-start | bytes 24584 | tf_op jit(solution)/shard_map/ppermute | solution.py:17
  25.7 3.6 %collective-permute-start.6 = (bf16[96,4096]{1,0:T(8,128)(2,1)S(1)}, bf16[96,4096]{1,0:T(8,128)(2,1)S(1)}, u32[]{:S(2)}, u32[]{:S(2)}) collective-permute-start(bf16[96,4096]{1,0:T(8,128)(2,1)S(1)} %shard_map.123.refs_0_), channel_id=1, source_target_pairs={{0,2},{2,0},{4,6},{6,4},{8,10},{10,8},{12,14},{14,12},{16,18},{18,... | collective-permute-start | bytes 2359304 | tf_op jit(solution)/shard_map/ppermute | solution.py:17
  26.9 1.5 collective-permute-start.7
  27.4 14.4 %collective-permute-start.10 = (bf16[64,4096]{1,0:T(8,128)(2,1)S(1)}, bf16[64,4096]{1,0:T(8,128)(2,1)S(1)}, u32[]{:S(2)}, u32[]{:S(2)}) collective-permute-start(bf16[64,4096]{1,0:T(8,128)(2,1)S(1)} %shard_map.127), channel_id=1, source_target_pairs={{0,4},{2,6},{4,0},{6,2},{8,12},{10,14},{12,8},{14,10},{16,20},{18,... | collective-permute-start | bytes 1572872 | tf_op jit(solution)/shard_map/ppermute | solution.py:17
  29.0 12.9 %collective-permute-start.11 = (bf16[64,4096]{1,0:T(8,128)(2,1)S(1)}, bf16[64,4096]{1,0:T(8,128)(2,1)S(1)}, u32[]{:S(2)}, u32[]{:S(2)}) collective-permute-start(bf16[64,4096]{1,0:T(8,128)(2,1)S(1)} %shard_map.126.refs_0_.refs_2_.refs_4_.refs_6_), channel_id=1, source_target_pairs={{0,2},{2,0},{4,6},{6,4},{8,10},{10,8},{12,14},{14,12},{16,18},{18,... | collective-permute-start | bytes 1572872 | tf_op jit(solution)/shard_map/ppermute | solution.py:17
  29.2 4.2 %slice-start.4 = ((s8[6291456]{0:T(1024)(128)(4,1)}), s8[2097152]{0:T(1024)(128)(4,1)S(1)}, s32[]{:S(2)}) async-start(s8[6291456]{0:T(1024)(128)(4,1)} %bitcast.10), calls=%async_computation.4 | async-start | bytes 4194304
  35.9 6.0 %collective-permute-start.9 = (bf16[64,128]{1,0:T(8,128)(2,1)S(1)}, bf16[64,128]{1,0:T(8,128)(2,1)S(1)}, u32[]{:S(2)}, u32[]{:S(2)}) collective-permute-start(bf16[64,128]{1,0:T(8,128)(2,1)S(1)} %pad_maximum_fusion.2), channel_id=1, source_target_pairs={{0,8},{2,10},{4,12},{6,14},{8,0},{10,2},{12,4},{14,6},{16,24},{18,... | collective-permute-start | bytes 49160 | tf_op jit(solution)/shard_map/ppermute | solution.py:17
  41.8 1.9 %collective-permute-start.12 = (bf16[64,4096]{1,0:T(8,128)(2,1)S(1)}, bf16[64,4096]{1,0:T(8,128)(2,1)S(1)}, u32[]{:S(2)}, u32[]{:S(2)}) collective-permute-start(bf16[64,4096]{1,0:T(8,128)(2,1)S(1)} %collective-permute-done.10.refs_1_.refs_3_.refs_5_.refs_7_), channel_id=1, source_target_pairs={{0,2},{2,0},{4,6},{6,4},{8,10},{10,8},{12,14},{14,12},{16,18},{18,... | collective-permute-start | bytes 1572872 | tf_op jit(solution)/shard_map/ppermute | solution.py:17
  41.9 12.0 %collective-permute-start.8 = (bf16[256,768]{1,0:T(8,128)(2,1)S(1)}, bf16[256,768]{1,0:T(8,128)(2,1)S(1)}, u32[]{:S(2)}, u32[]{:S(2)}) collective-permute-start(bf16[256,768]{1,0:T(8,128)(2,1)S(1)} %get-tuple-element.62.refs_0_), channel_id=1, source_target_pairs={{0,1},{1,0},{2,3},{3,2},{4,5},{5,4},{6,7},{7,6},{8,9},{9,8},{10,11... | collective-permute-start | bytes 1179656 | tf_op jit(solution)/shard_map/ppermute | solution.py:17
  47.8 43.9 %copy-start.3 = (bf16[32,2048]{1,0:T(8,128)(2,1)S(1)}, bf16[32,2048]{1,0:T(8,128)(2,1)}, u32[]{:S(2)}) copy-start(bf16[32,2048]{1,0:T(8,128)(2,1)} %param.11) | copy-start | bytes 393220
  47.9 14.0 %collective-permute-start.16 = (bf16[256,768]{1,0:T(8,128)(2,1)S(1)}, bf16[256,768]{1,0:T(8,128)(2,1)S(1)}, u32[]{:S(2)}, u32[]{:S(2)}) collective-permute-start(bf16[256,768]{1,0:T(8,128)(2,1)S(1)} %get-tuple-element.67.refs_0_), channel_id=1, source_target_pairs={{0,1},{1,0},{2,3},{3,2},{4,5},{5,4},{6,7},{7,6},{8,9},{9,8},{10,11... | collective-permute-start | bytes 1179656 | tf_op jit(solution)/shard_map/ppermute | solution.py:17
  49.4 3.9 %collective-permute-start.13 = (bf16[128,128]{1,0:T(8,128)(2,1)S(1)}, bf16[128,128]{1,0:T(8,128)(2,1)S(1)}, u32[]{:S(2)}, u32[]{:S(2)}) collective-permute-start(bf16[128,128]{1,0:T(8,128)(2,1)S(1)} %pad_maximum_fusion.1), channel_id=1, source_target_pairs={{0,4},{2,6},{4,0},{6,2},{8,12},{10,14},{12,8},{14,10},{16,20},{18,... | collective-permute-start | bytes 98312 | tf_op jit(solution)/shard_map/ppermute | solution.py:17
  53.4 1.3 collective-permute-start.14
  64.1 2.0 %collective-permute-start.17 = (bf16[128,2048]{1,0:T(8,128)(2,1)S(1)}, bf16[128,2048]{1,0:T(8,128)(2,1)S(1)}, u32[]{:S(2)}, u32[]{:S(2)}) collective-permute-start(bf16[128,2048]{1,0:T(8,128)(2,1)S(1)} %get-tuple-element.73), channel_id=1, source_target_pairs={{0,2},{2,0},{4,6},{6,4},{8,10},{10,8},{12,14},{14,12},{16,18},{18,... | collective-permute-start | bytes 1572872 | tf_op jit(solution)/shard_map/ppermute | solution.py:17
  64.2 10.9 %collective-permute-start.15 = (bf16[128,2048]{1,0:T(8,128)(2,1)S(1)}, bf16[128,2048]{1,0:T(8,128)(2,1)S(1)}, u32[]{:S(2)}, u32[]{:S(2)}) collective-permute-start(bf16[128,2048]{1,0:T(8,128)(2,1)S(1)} %get-tuple-element.70), channel_id=1, source_target_pairs={{0,2},{2,0},{4,6},{6,4},{8,10},{10,8},{12,14},{14,12},{16,18},{18,... | collective-permute-start | bytes 1572872 | tf_op jit(solution)/shard_map/ppermute | solution.py:17
  66.2 6.4 %collective-permute-start.18 = (bf16[64,1024]{1,0:T(8,128)(2,1)S(1)}, bf16[64,1024]{1,0:T(8,128)(2,1)S(1)}, u32[]{:S(2)}, u32[]{:S(2)}) collective-permute-start(bf16[64,1024]{1,0:T(8,128)(2,1)S(1)} %get-tuple-element.125), channel_id=1, source_target_pairs={{0,4},{2,6},{4,0},{6,2},{8,12},{10,14},{12,8},{14,10},{16,20},{18,... | collective-permute-start | bytes 393224 | tf_op jit(solution)/shard_map/ppermute | solution.py:17
  66.8 7.8 %collective-permute-start.19 = (bf16[64,1024]{1,0:T(8,128)(2,1)S(1)}, bf16[64,1024]{1,0:T(8,128)(2,1)S(1)}, u32[]{:S(2)}, u32[]{:S(2)}) collective-permute-start(bf16[64,1024]{1,0:T(8,128)(2,1)S(1)} %get-tuple-element.124), channel_id=1, source_target_pairs={{0,4},{2,6},{4,0},{6,2},{8,12},{10,14},{12,8},{14,10},{16,20},{18,... | collective-permute-start | bytes 393224 | tf_op jit(solution)/shard_map/ppermute | solution.py:17
  74.6 9.0 %collective-permute-start.20 = (bf16[64,2048]{1,0:T(8,128)(2,1)S(1)}, bf16[64,2048]{1,0:T(8,128)(2,1)S(1)}, u32[]{:S(2)}, u32[]{:S(2)}) collective-permute-start(bf16[64,2048]{1,0:T(8,128)(2,1)S(1)} %add_convert_fusion.7), channel_id=1, source_target_pairs={{0,4},{2,6},{4,0},{6,2},{8,12},{10,14},{12,8},{14,10},{16,20},{18,... | collective-permute-start | bytes 786440 | tf_op jit(solution)/shard_map/ppermute | solution.py:17
  75.3 7.0 %collective-permute-start.21 = (bf16[64,1024]{1,0:T(8,128)(2,1)S(1)}, bf16[64,1024]{1,0:T(8,128)(2,1)S(1)}, u32[]{:S(2)}, u32[]{:S(2)}) collective-permute-start(bf16[64,1024]{1,0:T(8,128)(2,1)S(1)} %get-tuple-element.123), channel_id=1, source_target_pairs={{0,8},{2,10},{4,12},{6,14},{8,0},{10,2},{12,4},{14,6},{16,24},{18,... | collective-permute-start | bytes 393224 | tf_op jit(solution)/shard_map/ppermute | solution.py:17
  78.1 5.6 %collective-permute-start.23 = (bf16[64,1024]{1,0:T(8,128)(2,1)S(1)}, bf16[64,1024]{1,0:T(8,128)(2,1)S(1)}, u32[]{:S(2)}, u32[]{:S(2)}) collective-permute-start(bf16[64,1024]{1,0:T(8,128)(2,1)S(1)} %get-tuple-element.122), channel_id=1, source_target_pairs={{0,8},{2,10},{4,12},{6,14},{8,0},{10,2},{12,4},{14,6},{16,24},{18,... | collective-permute-start | bytes 393224 | tf_op jit(solution)/shard_map/ppermute | solution.py:17
  83.7 5.6 %collective-permute-start.22 = (bf16[32,1024]{1,0:T(8,128)(2,1)S(1)}, bf16[32,1024]{1,0:T(8,128)(2,1)S(1)}, u32[]{:S(2)}, u32[]{:S(2)}) collective-permute-start(bf16[32,1024]{1,0:T(8,128)(2,1)S(1)} %get-tuple-element.117), channel_id=1, source_target_pairs={{0,16},{2,18},{4,20},{6,22},{8,24},{10,26},{12,28},{14,30},{16,0},... | collective-permute-start | bytes 196616 | tf_op jit(solution)/shard_map/ppermute | solution.py:17
  86.0 5.8 %collective-permute-start.24 = (bf16[32,1024]{1,0:T(8,128)(2,1)S(1)}, bf16[32,1024]{1,0:T(8,128)(2,1)S(1)}, u32[]{:S(2)}, u32[]{:S(2)}) collective-permute-start(bf16[32,1024]{1,0:T(8,128)(2,1)S(1)} %get-tuple-element.116), channel_id=1, source_target_pairs={{0,16},{2,18},{4,20},{6,22},{8,24},{10,26},{12,28},{14,30},{16,0},... | collective-permute-start | bytes 196616 | tf_op jit(solution)/shard_map/ppermute | solution.py:17
  91.9 5.3 %collective-permute-start.25 = (bf16[32,1024]{1,0:T(8,128)(2,1)S(1)}, bf16[32,1024]{1,0:T(8,128)(2,1)S(1)}, u32[]{:S(2)}, u32[]{:S(2)}) collective-permute-start(bf16[32,1024]{1,0:T(8,128)(2,1)S(1)} %get-tuple-element.115.refs_0_), channel_id=1, source_target_pairs={{0,16},{2,18},{4,20},{6,22},{8,24},{10,26},{12,28},{14,30},{16,0},... | collective-permute-start | bytes 196616 | tf_op jit(solution)/shard_map/ppermute | solution.py:17
  92.1 5.8 %collective-permute-start.26 = (bf16[32,1024]{1,0:T(8,128)(2,1)S(1)}, bf16[32,1024]{1,0:T(8,128)(2,1)S(1)}, u32[]{:S(2)}, u32[]{:S(2)}) collective-permute-start(bf16[32,1024]{1,0:T(8,128)(2,1)S(1)} %get-tuple-element.114.refs_1_), channel_id=1, source_target_pairs={{0,16},{2,18},{4,20},{6,22},{8,24},{10,26},{12,28},{14,30},{16,0},... | collective-permute-start | bytes 196616 | tf_op jit(solution)/shard_map/ppermute | solution.py:17
  98.5 6.4 %collective-permute-start.27 = (bf16[64,2048]{1,0:T(8,128)(2,1)S(1)}, bf16[64,2048]{1,0:T(8,128)(2,1)S(1)}, u32[]{:S(2)}, u32[]{:S(2)}) collective-permute-start(bf16[64,2048]{1,0:T(8,128)(2,1)S(1)} %shard_map.131.refs_0_), channel_id=1, source_target_pairs={{0,8},{2,10},{4,12},{6,14},{8,0},{10,2},{12,4},{14,6},{16,24},{18,... | collective-permute-start | bytes 786440 | tf_op jit(solution)/shard_map/ppermute | solution.py:17
  100.3 6.4 %collective-permute-start.28 = (bf16[64,2048]{1,0:T(8,128)(2,1)S(1)}, bf16[64,2048]{1,0:T(8,128)(2,1)S(1)}, u32[]{:S(2)}, u32[]{:S(2)}) collective-permute-start(bf16[64,2048]{1,0:T(8,128)(2,1)S(1)} %shard_map.131.refs_0_), channel_id=1, source_target_pairs={{0,4},{2,6},{4,0},{6,2},{8,12},{10,14},{12,8},{14,10},{16,20},{18,... | collective-permute-start | bytes 786440 | tf_op jit(solution)/shard_map/ppermute | solution.py:17
  101.9 4.8 %collective-permute-start.29 = (bf16[64,2048]{1,0:T(8,128)(2,1)S(1)}, bf16[64,2048]{1,0:T(8,128)(2,1)S(1)}, u32[]{:S(2)}, u32[]{:S(2)}) collective-permute-start(bf16[64,2048]{1,0:T(8,128)(2,1)S(1)} %shard_map.131.refs_0_), channel_id=1, source_target_pairs={{0,2},{2,0},{4,6},{6,4},{8,10},{10,8},{12,14},{14,12},{16,18},{18,... | collective-permute-start | bytes 786440 | tf_op jit(solution)/shard_map/ppermute | solution.py:17
  106.7 1.8 %collective-permute-start.30 = (bf16[64,2048]{1,0:T(8,128)(2,1)S(1)}, bf16[64,2048]{1,0:T(8,128)(2,1)S(1)}, u32[]{:S(2)}, u32[]{:S(2)}) collective-permute-start(bf16[64,2048]{1,0:T(8,128)(2,1)S(1)} %collective-permute-done.27.refs_1_), channel_id=1, source_target_pairs={{0,2},{2,0},{4,6},{6,4},{8,10},{10,8},{12,14},{14,12},{16,18},{18,... | collective-permute-start | bytes 786440 | tf_op jit(solution)/shard_map/ppermute | solution.py:17
  106.7 8.7 %collective-permute-start.32 = (bf16[64,2048]{1,0:T(8,128)(2,1)S(1)}, bf16[64,2048]{1,0:T(8,128)(2,1)S(1)}, u32[]{:S(2)}, u32[]{:S(2)}) collective-permute-start(bf16[64,2048]{1,0:T(8,128)(2,1)S(1)} %collective-permute-done.27.refs_1_), channel_id=1, source_target_pairs={{0,4},{2,6},{4,0},{6,2},{8,12},{10,14},{12,8},{14,10},{16,20},{18,... | collective-permute-start | bytes 786440 | tf_op jit(solution)/shard_map/ppermute | solution.py:17
  108.3 7.2 %collective-permute-start.33 = (bf16[64,2048]{1,0:T(8,128)(2,1)S(1)}, bf16[64,2048]{1,0:T(8,128)(2,1)S(1)}, u32[]{:S(2)}, u32[]{:S(2)}) collective-permute-start(bf16[64,2048]{1,0:T(8,128)(2,1)S(1)} %collective-permute-done.28.refs_0_), channel_id=1, source_target_pairs={{0,2},{2,0},{4,6},{6,4},{8,10},{10,8},{12,14},{14,12},{16,18},{18,... | collective-permute-start | bytes 786440 | tf_op jit(solution)/shard_map/ppermute | solution.py:17
  110.9 11.4 %collective-permute-start.31 = (bf16[256,768]{1,0:T(8,128)(2,1)S(1)}, bf16[256,768]{1,0:T(8,128)(2,1)S(1)}, u32[]{:S(2)}, u32[]{:S(2)}) collective-permute-start(bf16[256,768]{1,0:T(8,128)(2,1)S(1)} %get-tuple-element.77), channel_id=1, source_target_pairs={{0,1},{1,0},{2,3},{3,2},{4,5},{5,4},{6,7},{7,6},{8,9},{9,8},{10,11... | collective-permute-start | bytes 1179656 | tf_op jit(solution)/shard_map/ppermute | solution.py:17
  115.4 4.1 %collective-permute-start.34 = (bf16[64,2048]{1,0:T(8,128)(2,1)S(1)}, bf16[64,2048]{1,0:T(8,128)(2,1)S(1)}, u32[]{:S(2)}, u32[]{:S(2)}) collective-permute-start(bf16[64,2048]{1,0:T(8,128)(2,1)S(1)} %collective-permute-done.32.refs_1_), channel_id=1, source_target_pairs={{0,2},{2,0},{4,6},{6,4},{8,10},{10,8},{12,14},{14,12},{16,18},{18,... | collective-permute-start | bytes 786440 | tf_op jit(solution)/shard_map/ppermute | solution.py:17
  124.7 10.6 %collective-permute-start.35 = (bf16[256,768]{1,0:T(8,128)(2,1)S(1)}, bf16[256,768]{1,0:T(8,128)(2,1)S(1)}, u32[]{:S(2)}, u32[]{:S(2)}) collective-permute-start(bf16[256,768]{1,0:T(8,128)(2,1)S(1)} %get-tuple-element.85), channel_id=1, source_target_pairs={{0,1},{1,0},{2,3},{3,2},{4,5},{5,4},{6,7},{7,6},{8,9},{9,8},{10,11... | collective-permute-start | bytes 1179656 | tf_op jit(solution)/shard_map/ppermute | solution.py:17
  130.3 22.3 %slice-start = ((s8[12582912]{0:T(1024)(128)(4,1)}), s8[4194304]{0:T(1024)(128)(4,1)S(1)}, s32[]{:S(2)}) async-start(s8[12582912]{0:T(1024)(128)(4,1)} %bitcast.8), calls=%async_computation | async-start | bytes 8388608
  130.3 22.3 %slice-start.1 = ((s8[12582912]{0:T(1024)(128)(4,1)}), s8[4194304]{0:T(1024)(128)(4,1)S(1)}, s32[]{:S(2)}) async-start(s8[12582912]{0:T(1024)(128)(4,1)} %bitcast.8), calls=%async_computation.1 | async-start | bytes 8388608
  135.3 17.3 %slice-start.2 = ((s8[12582912]{0:T(1024)(128)(4,1)}), s8[4194304]{0:T(1024)(128)(4,1)S(1)}, s32[]{:S(2)}) async-start(s8[12582912]{0:T(1024)(128)(4,1)} %bitcast.8), calls=%async_computation.2 | async-start | bytes 8388608
  139.3 2.0 %collective-permute-start.38 = (bf16[128,2048]{1,0:T(8,128)(2,1)S(1)}, bf16[128,2048]{1,0:T(8,128)(2,1)S(1)}, u32[]{:S(2)}, u32[]{:S(2)}) collective-permute-start(bf16[128,2048]{1,0:T(8,128)(2,1)S(1)} %get-tuple-element.100), channel_id=1, source_target_pairs={{0,2},{2,0},{4,6},{6,4},{8,10},{10,8},{12,14},{14,12},{16,18},{18,... | collective-permute-start | bytes 1572872 | tf_op jit(solution)/shard_map/ppermute | solution.py:17
  139.4 4.6 %collective-permute-start.37 = (bf16[128,2048]{1,0:T(8,128)(2,1)S(1)}, bf16[128,2048]{1,0:T(8,128)(2,1)S(1)}, u32[]{:S(2)}, u32[]{:S(2)}) collective-permute-start(bf16[128,2048]{1,0:T(8,128)(2,1)S(1)} %get-tuple-element.98), channel_id=1, source_target_pairs={{0,2},{2,0},{4,6},{6,4},{8,10},{10,8},{12,14},{14,12},{16,18},{18,... | collective-permute-start | bytes 1572872 | tf_op jit(solution)/shard_map/ppermute | solution.py:17
  139.9 19.4 %collective-permute-start.36 = (bf16[128,2048]{1,0:T(8,128)(2,1)S(1)}, bf16[128,2048]{1,0:T(8,128)(2,1)S(1)}, u32[]{:S(2)}, u32[]{:S(2)}) collective-permute-start(bf16[128,2048]{1,0:T(8,128)(2,1)S(1)} %get-tuple-element.94), channel_id=1, source_target_pairs={{0,2},{2,0},{4,6},{6,4},{8,10},{10,8},{12,14},{14,12},{16,18},{18,... | collective-permute-start | bytes 1572872 | tf_op jit(solution)/shard_map/ppermute | solution.py:17
  139.9 11.4 %collective-permute-start.43 = (bf16[128,2048]{1,0:T(8,128)(2,1)S(1)}, bf16[128,2048]{1,0:T(8,128)(2,1)S(1)}, u32[]{:S(2)}, u32[]{:S(2)}) collective-permute-start(bf16[128,2048]{1,0:T(8,128)(2,1)S(1)} %get-tuple-element.104), channel_id=1, source_target_pairs={{0,2},{2,0},{4,6},{6,4},{8,10},{10,8},{12,14},{14,12},{16,18},{18,... | collective-permute-start | bytes 1572872 | tf_op jit(solution)/shard_map/ppermute | solution.py:17
  141.4 8.4 %collective-permute-start.40 = (bf16[64,2048]{1,0:T(8,128)(2,1)S(1)}, bf16[64,2048]{1,0:T(8,128)(2,1)S(1)}, u32[]{:S(2)}, u32[]{:S(2)}) collective-permute-start(bf16[64,2048]{1,0:T(8,128)(2,1)S(1)} %get-tuple-element.119), channel_id=1, source_target_pairs={{0,1},{1,0},{2,3},{3,2},{4,5},{5,4},{6,7},{7,6},{8,9},{9,8},{10,11... | collective-permute-start | bytes 786440 | tf_op jit(solution)/shard_map/ppermute | solution.py:17
  143.0 8.5 %collective-permute-start.39 = (bf16[64,2048]{1,0:T(8,128)(2,1)S(1)}, bf16[64,2048]{1,0:T(8,128)(2,1)S(1)}, u32[]{:S(2)}, u32[]{:S(2)}) collective-permute-start(bf16[64,2048]{1,0:T(8,128)(2,1)S(1)} %get-tuple-element.118), channel_id=1, source_target_pairs={{0,4},{2,6},{4,0},{6,2},{8,12},{10,14},{12,8},{14,10},{16,20},{18,... | collective-permute-start | bytes 786440 | tf_op jit(solution)/shard_map/ppermute | solution.py:17
  149.8 9.4 %collective-permute-start.41 = (bf16[64,2048]{1,0:T(8,128)(2,1)S(1)}, bf16[64,2048]{1,0:T(8,128)(2,1)S(1)}, u32[]{:S(2)}, u32[]{:S(2)}) collective-permute-start(bf16[64,2048]{1,0:T(8,128)(2,1)S(1)} %add_convert_fusion.5), channel_id=1, source_target_pairs={{0,1},{1,0},{2,3},{3,2},{4,5},{5,4},{6,7},{7,6},{8,9},{9,8},{10,11... | collective-permute-start | bytes 786440 | tf_op jit(solution)/shard_map/ppermute | solution.py:17
  151.5 7.7 %collective-permute-start.44 = (bf16[64,2048]{1,0:T(8,128)(2,1)S(1)}, bf16[64,2048]{1,0:T(8,128)(2,1)S(1)}, u32[]{:S(2)}, u32[]{:S(2)}) collective-permute-start(bf16[64,2048]{1,0:T(8,128)(2,1)S(1)} %get-tuple-element.105), channel_id=1, source_target_pairs={{0,4},{2,6},{4,0},{6,2},{8,12},{10,14},{12,8},{14,10},{16,20},{18,... | collective-permute-start | bytes 786440 | tf_op jit(solution)/shard_map/ppermute | solution.py:17
  159.4 7.0 %collective-permute-start.46 = (bf16[64,2048]{1,0:T(8,128)(2,1)S(1)}, bf16[64,2048]{1,0:T(8,128)(2,1)S(1)}, u32[]{:S(2)}, u32[]{:S(2)}) collective-permute-start(bf16[64,2048]{1,0:T(8,128)(2,1)S(1)} %add_convert_fusion), channel_id=1, source_target_pairs={{0,8},{2,10},{4,12},{6,14},{8,0},{10,2},{12,4},{14,6},{16,24},{18,... | collective-permute-start | bytes 786440 | tf_op jit(solution)/shard_map/ppermute | solution.py:17
  159.7 6.9 %collective-permute-start.42 = (bf16[64,2048]{1,0:T(8,128)(2,1)S(1)}, bf16[64,2048]{1,0:T(8,128)(2,1)S(1)}, u32[]{:S(2)}, u32[]{:S(2)}) collective-permute-start(bf16[64,2048]{1,0:T(8,128)(2,1)S(1)} %add_convert_fusion.3), channel_id=1, source_target_pairs={{0,1},{1,0},{2,3},{3,2},{4,5},{5,4},{6,7},{7,6},{8,9},{9,8},{10,11... | collective-permute-start | bytes 786440 | tf_op jit(solution)/shard_map/ppermute | solution.py:17
  160.3 6.5 %collective-permute-start.45 = (bf16[64,2048]{1,0:T(8,128)(2,1)S(1)}, bf16[64,2048]{1,0:T(8,128)(2,1)S(1)}, u32[]{:S(2)}, u32[]{:S(2)}) collective-permute-start(bf16[64,2048]{1,0:T(8,128)(2,1)S(1)} %get-tuple-element.106), channel_id=1, source_target_pairs={{0,4},{2,6},{4,0},{6,2},{8,12},{10,14},{12,8},{14,10},{16,20},{18,... | collective-permute-start | bytes 786440 | tf_op jit(solution)/shard_map/ppermute | solution.py:17
  166.9 7.4 %collective-permute-start.47 = (bf16[32,2048]{1,0:T(8,128)(2,1)S(1)}, bf16[32,2048]{1,0:T(8,128)(2,1)S(1)}, u32[]{:S(2)}, u32[]{:S(2)}) collective-permute-start(bf16[32,2048]{1,0:T(8,128)(2,1)S(1)} %add_convert_fusion.9), channel_id=1, source_target_pairs={{0,16},{2,18},{4,20},{6,22},{8,24},{10,26},{12,28},{14,30},{16,0},... | collective-permute-start | bytes 393224 | tf_op jit(solution)/shard_map/ppermute | solution.py:17

commit v15 on v14

--- a/solution.py
+++ b/solution.py
@@ -628,8 +628,7 @@
             hidden[1][1:] = [tie(part, sums[0][0]) for part in hidden[1][1:]]
         out_own, out_other = forward_down(place, hidden[c], w_down, terms, c)
         sums.append([out_own, swap(out_other, "expert", 1)])
-    middle = quarter // 2
-    cuts = [slice(0, middle), slice(middle, quarter)]
+    cuts = [slice(0, quarter)]
     mixed = scatter_rows(sums[0], sums[1], cuts)
     error = [
         (mixed[f] - target[:, cuts[f]].astype(F32)).astype(BF16) for f in range(len(cuts))

time: 175 us -> 175 us (level)
  waiting for transfers between devices: 56.3 us -> 62.8 us
  starting transfers between devices: 51.2 us -> 44.9 us
    ppermute x48 -> x44, waiting for transfers between devices: 56.3 us -> 62.8 us  [swap(): return lax.ppermute(array, axis, [(i, i ^ distance) for i in range(size)])]
    ppermute x48 -> x44, starting transfers between devices: 51.2 us -> 44.9 us  [swap(): return lax.ppermute(array, axis, [(i, i ^ distance) for i in range(size)])]
  transfers between devices with their start and end apart: 48 -> 44, of which waited for: 29 -> 26; matrix products, arithmetic and copies ran while one was open for 2% -> 2% of each run, Pallas kernels for 29% -> 29%
where the time goes in v15:
time: 175 us
  waiting for transfers between devices  62.8 us (36%)
  Pallas kernels  60.2 us (34%)
  starting transfers between devices  44.9 us (26%)
  local copies, waits for them, and re-layouts  4.32 us (2%)
  other arithmetic  1.94 us (1%)
    ppermute x44, waiting for transfers between devices, swap(): return lax.ppermute(array, axis, [(i, i ^ distance) for i in range(size)])  62.8 us
    pallas_call x20, Pallas kernels, call(): pl.pallas_call(kernel, grid_spec=pltpu.PrefetchScalarGridSpec(num_scalar_...  60.2 us
    ppermute x44, starting transfers between devices, swap(): return lax.ppermute(array, axis, [(i, i ^ distance) for i in range(size)])  44.9 us
    unnamed x26, local copies, waits for them, and re-layouts  4.28 us
  transfers between devices with their start and end apart: 44, of which 26 were waited for; matrix products, arithmetic and copies ran while one was open for 2% of the time, Pallas kernels for 29%

profile of v15, /device:TPU:0, one launch (start us, length us, event | category | flops | bytes accessed | tf_op | source)
XLA Modules:
  0.0 175.2 jit_solution(627121063296574683)
XLA Ops:
  0.6 3.0 %collective-permute-start.1 = (bf16[32,4096]{1,0:T(8,128)(2,1)}, bf16[32,4096]{1,0:T(8,128)(2,1)S(1)}, u32[]{:S(2)}, u32[]{:S(2)}) collective-permute-start(bf16[32,4096]{1,0:T(8,128)(2,1)} %refs_0_.1), channel_id=1, source_target_pairs={{0,4},{2,6},{4,0},{6,2},{8,12},{10,14},{12,8},{14,10},{16,20},{18,... | collective-permute-start | bytes 786440 | tf_op jit(solution)/shard_map/ppermute | solution.py:17
  3.6 2.6 %collective-permute-start = (bf16[32,4096]{1,0:T(8,128)(2,1)}, bf16[32,4096]{1,0:T(8,128)(2,1)S(1)}, u32[]{:S(2)}, u32[]{:S(2)}) collective-permute-start(bf16[32,4096]{1,0:T(8,128)(2,1)} %refs_0_.1), channel_id=1, source_target_pairs={{0,16},{2,18},{4,20},{6,22},{8,24},{10,26},{12,28},{14,30},{16,0},... | collective-permute-start | bytes 786440 | tf_op jit(solution)/shard_map/ppermute | solution.py:17
  6.2 1.6 collective-permute-start.3
  7.8 0.8 copy.15.route_ref
  8.6 0.8 copy.16.score_ref
  10.2 0.9 copy-done.1
  11.1 0.9 copy-done.2
  12.0 6.2 %shard_map.122.refs_4_.refs_8_.refs_3_ = bf16[4096,1536]{1,0:T(8,128)(2,1)S(1)} custom-call(s32[2]{0:T(128)S(1)} %pad_add_fusion.place_ref, bf16[2,4096,768]{2,1,0:T(8,128)(2,1)} %bitcast.7, f32[2,32,768]{2,1,0:T(8,128)S(1)} %bitcast.13, f32[2,32,768]{2,1,0:T(8,128)S(1)} %bitcast.14), custom_call_target="tpu_custom_call" | custom-call | bytes 25 | tf_op jit(solution)/shard_map/pallas_call | solution.py:112
  18.4 1.4 collective-permute-start.4
  20.4 2.3 %collective-permute-start.2 = (bf16[32,128]{1,0:T(8,128)(2,1)S(1)}, bf16[32,128]{1,0:T(8,128)(2,1)S(1)}, u32[]{:S(2)}, u32[]{:S(2)}) collective-permute-start(bf16[32,128]{1,0:T(8,128)(2,1)S(1)} %shard_map.121), channel_id=1, source_target_pairs={{0,16},{2,18},{4,20},{6,22},{8,24},{10,26},{12,28},{14,30},{16,0},... | collective-permute-start | bytes 24584 | tf_op jit(solution)/shard_map/ppermute | solution.py:17
  22.7 2.3 %collective-permute-done.2 = bf16[32,128]{1,0:T(8,128)(2,1)S(1)} collective-permute-done((bf16[32,128]{1,0:T(8,128)(2,1)S(1)}, bf16[32,128]{1,0:T(8,128)(2,1)S(1)}, u32[]{:S(2)}, u32[]{:S(2)}) %collective-permute-start.2) | collective-permute-done | bytes 8224 | tf_op jit(solution)/shard_map/ppermute | solution.py:17
  25.7 1.1 collective-permute-done.5.refs_1_
  27.4 0.8 collective-permute-start.10
  29.2 4.1 %shard_map.124 = (bf16[256,768]{1,0:T(8,128)(2,1)S(1)}, f32[256,768]{1,0:T(8,128)S(1)}, f32[256,768]{1,0:T(8,128)S(1)}) custom-call(s32[2]{0:T(128)S(1)} %pad_add_fusion.place_ref, bf16[96,4096]{1,0:T(8,128)(2,1)S(1)} %shard_map.123.refs_0_, bf16[32,4096]{1,0:T(8,128)(2,1)S(1)} %collective-permute-done.4.refs_1_, ...), custom_call_target="tpu_custom_call" | custom-call | flops 3221 | bytes 16 | tf_op jit(solution)/shard_map/pallas_call | solution.py:112
  33.4 2.4 %shard_map.125.refs_2_.refs_6_ = bf16[1536,2048]{1,0:T(8,128)(2,1)S(1)} custom-call(s32[2]{0:T(128)S(1)} %pad_add_fusion.place_ref, bf16[1,1536,2048]{2,1,0:T(8,128)(2,1)S(1)} %bitcast.11, f32[1,12,2048]{2,1,0:T(8,128)S(1)} %copy.17.low_ref, f32[1,12,2048]{2,1,0:T(8,128)S(1)} %copy.18.high_ref), custom_call_target="tpu_custom_call" | custom-call | bytes 12 | tf_op jit(solution)/shard_map/pallas_call | solution.py:112
  35.9 3.9 %collective-permute-start.9 = (bf16[64,128]{1,0:T(8,128)(2,1)S(1)}, bf16[64,128]{1,0:T(8,128)(2,1)S(1)}, u32[]{:S(2)}, u32[]{:S(2)}) collective-permute-start(bf16[64,128]{1,0:T(8,128)(2,1)S(1)} %pad_maximum_fusion.2), channel_id=1, source_target_pairs={{0,8},{2,10},{4,12},{6,14},{8,0},{10,2},{12,4},{14,6},{16,24},{18,... | collective-permute-start | bytes 49160 | tf_op jit(solution)/shard_map/ppermute | solution.py:17
  39.7 2.1 %collective-permute-done.10.refs_1_.refs_3_.refs_5_.refs_7_ = bf16[64,4096]{1,0:T(8,128)(2,1)S(1)} collective-permute-done((bf16[64,4096]{1,0:T(8,128)(2,1)S(1)}, bf16[64,4096]{1,0:T(8,128)(2,1)S(1)}, u32[]{:S(2)}, u32[]{:S(2)}) %collective-permute-start.10) | collective-permute-done | bytes 524320 | tf_op jit(solution)/shard_map/ppermute | solution.py:17
  41.9 1.6 collective-permute-start.8
  43.8 4.1 %shard_map.128 = (bf16[256,768]{1,0:T(8,128)(2,1)S(1)}, f32[256,768]{1,0:T(8,128)S(1)}, f32[256,768]{1,0:T(8,128)S(1)}) custom-call(s32[2]{0:T(128)S(1)} %pad_add_fusion.place_ref, bf16[64,4096]{1,0:T(8,128)(2,1)S(1)} %shard_map.126.refs_0_.refs_2_.refs_4_.refs_6_, bf16[64,4096]{1,0:T(8,128)(2,1)S(1)} %collective-permute-done.10.refs_1_.refs_3_.refs_5_.refs_7_, ...), custom_call_target="tpu_custom_call" | custom-call | flops 3221 | bytes 18 | tf_op jit(solution)/shard_map/pallas_call | solution.py:112
  47.9 1.6 collective-permute-start.16
  50.0 3.4 %collective-permute-done.13 = bf16[128,128]{1,0:T(8,128)(2,1)S(1)} collective-permute-done((bf16[128,128]{1,0:T(8,128)(2,1)S(1)}, bf16[128,128]{1,0:T(8,128)(2,1)S(1)}, u32[]{:S(2)}, u32[]{:S(2)}) %collective-permute-start.13) | collective-permute-done | bytes 32800 | tf_op jit(solution)/shard_map/ppermute | solution.py:17
  53.8 0.8 collective-permute-done.14.refs_4_.refs_5_
  54.6 2.3 %shard_map.129 = (bf16[128,2048]{1,0:T(8,128)(2,1)S(1)}, bf16[128,2048]{1,0:T(8,128)(2,1)S(1)}) custom-call(s32[2]{0:T(128)S(1)} %pad_add_fusion.place_ref, bf16[256,768]{1,0:T(8,128)(2,1)S(1)} %get-tuple-element.62.refs_0_, bf16[256,768]{1,0:T(8,128)(2,1)S(1)} %collective-permute-done.8.refs_1_, bf16[1536,2048]{1,0:T(8,128)(2,1)S(1)} %shard_map.125.refs_2_.refs_6_, ...), custom_call_target="tpu_custom_call" | custom-call | flops 1610 | bytes 8 | tf_op jit(solution)/shard_map/pallas_call | solution.py:112
  57.0 4.9 %collective-permute-done.16.refs_1_ = bf16[256,768]{1,0:T(8,128)(2,1)S(1)} collective-permute-done((bf16[256,768]{1,0:T(8,128)(2,1)S(1)}, bf16[256,768]{1,0:T(8,128)(2,1)S(1)}, u32[]{:S(2)}, u32[]{:S(2)}) %collective-permute-start.16) | collective-permute-done | bytes 393248 | tf_op jit(solution)/shard_map/ppermute | solution.py:17
  61.8 2.3 %shard_map.130 = (bf16[128,2048]{1,0:T(8,128)(2,1)S(1)}, bf16[128,2048]{1,0:T(8,128)(2,1)S(1)}) custom-call(s32[2]{0:T(128)S(1)} %pad_add_fusion.place_ref, bf16[256,768]{1,0:T(8,128)(2,1)S(1)} %get-tuple-element.67.refs_0_, bf16[256,768]{1,0:T(8,128)(2,1)S(1)} %collective-permute-done.16.refs_1_, bf16[1536,2048]{1,0:T(8,128)(2,1)S(1)} %shard_map.125.refs_2_.refs_6_, ...), custom_call_target="tpu_custom_call" | custom-call | flops 1610 | bytes 8 | tf_op jit(solution)/shard_map/pallas_call | solution.py:112
  64.7 1.4 collective-permute-done.17
  66.9 7.8 %collective-permute-done.18 = bf16[64,2048]{1,0:T(8,128)(2,1)S(1)} collective-permute-done((bf16[64,2048]{1,0:T(8,128)(2,1)S(1)}, bf16[64,2048]{1,0:T(8,128)(2,1)S(1)}, u32[]{:S(2)}, u32[]{:S(2)}) %collective-permute-start.18) | collective-permute-done | bytes 262176 | tf_op jit(solution)/shard_map/ppermute | solution.py:17
  75.3 2.8 %collective-permute-start.20 = (bf16[64,2048]{1,0:T(8,128)(2,1)S(1)}, bf16[64,2048]{1,0:T(8,128)(2,1)S(1)}, u32[]{:S(2)}, u32[]{:S(2)}) collective-permute-start(bf16[64,2048]{1,0:T(8,128)(2,1)S(1)} %add_convert_fusion.7), channel_id=1, source_target_pairs={{0,8},{2,10},{4,12},{6,14},{8,0},{10,2},{12,4},{14,6},{16,24},{18,... | collective-permute-start | bytes 786440 | tf_op jit(solution)/shard_map/ppermute | solution.py:17
  78.1 4.1 %collective-permute-done.19 = bf16[64,2048]{1,0:T(8,128)(2,1)S(1)} collective-permute-done((bf16[64,2048]{1,0:T(8,128)(2,1)S(1)}, bf16[64,2048]{1,0:T(8,128)(2,1)S(1)}, u32[]{:S(2)}, u32[]{:S(2)}) %collective-permute-start.19) | collective-permute-done | bytes 262176 | tf_op jit(solution)/shard_map/ppermute | solution.py:17
  82.2 1.4 collective-permute-done.20
  83.7 2.3 %collective-permute-start.21 = (bf16[32,2048]{1,0:T(8,128)(2,1)S(1)}, bf16[32,2048]{1,0:T(8,128)(2,1)S(1)}, u32[]{:S(2)}, u32[]{:S(2)}) collective-permute-start(bf16[32,2048]{1,0:T(8,128)(2,1)S(1)} %add_convert_fusion.12), channel_id=1, source_target_pairs={{0,16},{2,18},{4,20},{6,22},{8,24},{10,26},{12,28},{14,30},{16,0},... | collective-permute-start | bytes 393224 | tf_op jit(solution)/shard_map/ppermute | solution.py:17
  86.0 5.2 %collective-permute-done.21 = bf16[32,2048]{1,0:T(8,128)(2,1)S(1)} collective-permute-done((bf16[32,2048]{1,0:T(8,128)(2,1)S(1)}, bf16[32,2048]{1,0:T(8,128)(2,1)S(1)}, u32[]{:S(2)}, u32[]{:S(2)}) %collective-permute-start.21) | collective-permute-done | bytes 131104 | tf_op jit(solution)/shard_map/ppermute | solution.py:17
  91.4 0.8 collective-permute-start.22
  92.2 6.3 %collective-permute-done.22.refs_1_ = bf16[32,2048]{1,0:T(8,128)(2,1)S(1)} collective-permute-done((bf16[32,2048]{1,0:T(8,128)(2,1)S(1)}, bf16[32,2048]{1,0:T(8,128)(2,1)S(1)}, u32[]{:S(2)}, u32[]{:S(2)}) %collective-permute-start.22) | collective-permute-done | bytes 131104 | tf_op jit(solution)/shard_map/ppermute | solution.py:17
  99.1 1.6 collective-permute-start.24
  100.7 4.8 %collective-permute-done.23.refs_1_ = bf16[64,2048]{1,0:T(8,128)(2,1)S(1)} collective-permute-done((bf16[64,2048]{1,0:T(8,128)(2,1)S(1)}, bf16[64,2048]{1,0:T(8,128)(2,1)S(1)}, u32[]{:S(2)}, u32[]{:S(2)}) %collective-permute-start.23) | collective-permute-done | bytes 262176 | tf_op jit(solution)/shard_map/ppermute | solution.py:17
  105.6 1.5 collective-permute-start.28
  107.3 2.4 %shard_map.132 = (bf16[256,2048]{1,0:T(8,128)(2,1)S(1)}, f32[256,768]{1,0:T(8,128)S(1)}, bf16[256,768]{1,0:T(8,128)(2,1)S(1)}) custom-call(s32[2]{0:T(128)S(1)} %pad_add_fusion.place_ref, bf16[64,2048]{1,0:T(8,128)(2,1)S(1)} %shard_map.131.refs_0_, bf16[64,2048]{1,0:T(8,128)(2,1)S(1)} %collective-permute-done.23.refs_1_, ...), custom_call_target="tpu_custom_call" | custom-call | flops 1610 | bytes 9 | tf_op jit(solution)/shard_map/pallas_call | solution.py:112
  109.7 1.6 collective-permute-start.27
  111.3 3.0 %collective-permute-done.28.refs_1_ = bf16[64,2048]{1,0:T(8,128)(2,1)S(1)} collective-permute-done((bf16[64,2048]{1,0:T(8,128)(2,1)S(1)}, bf16[64,2048]{1,0:T(8,128)(2,1)S(1)}, u32[]{:S(2)}, u32[]{:S(2)}) %collective-permute-start.28) | collective-permute-done | bytes 262176 | tf_op jit(solution)/shard_map/ppermute | solution.py:17
  114.3 4.1 %shard_map.134.refs_4_ = f32[2,12,2048]{2,1,0:T(8,128)S(1)} custom-call(s32[2]{0:T(128)S(1)} %pad_add_fusion.place_ref, bf16[256,768]{1,0:T(8,128)(2,1)S(1)} %get-tuple-element.62.refs_0_, bf16[256,768]{1,0:T(8,128)(2,1)S(1)} %collective-permute-done.8.refs_1_, bf16[256,2048]{1,0:T(8,128)(2,1)S(1)} %get-tuple-element.81.refs_2_, ...), custom_call_target="tpu_custom_call" | custom-call | flops 1610 | bytes 8 | tf_op jit(solution)/shard_map/pallas_call | solution.py:112
  118.4 2.7 %collective-permute-done.27.refs_0_ = bf16[256,768]{1,0:T(8,128)(2,1)S(1)} collective-permute-done((bf16[256,768]{1,0:T(8,128)(2,1)S(1)}, bf16[256,768]{1,0:T(8,128)(2,1)S(1)}, u32[]{:S(2)}, u32[]{:S(2)}) %collective-permute-start.27) | collective-permute-done | bytes 393248 | tf_op jit(solution)/shard_map/ppermute | solution.py:17
  121.1 2.4 %shard_map.135 = (bf16[256,2048]{1,0:T(8,128)(2,1)S(1)}, f32[256,768]{1,0:T(8,128)S(1)}, bf16[256,768]{1,0:T(8,128)(2,1)S(1)}) custom-call(s32[2]{0:T(128)S(1)} %pad_add_fusion.place_ref, bf16[64,2048]{1,0:T(8,128)(2,1)S(1)} %collective-permute-done.24.refs_0_, bf16[64,2048]{1,0:T(8,128)(2,1)S(1)} %collective-permute-done.28.refs_1_, ...), custom_call_target="tpu_custom_call" | custom-call | flops 1610 | bytes 9 | tf_op jit(solution)/shard_map/pallas_call | solution.py:112
  123.5 1.6 collective-permute-start.31
  125.1 4.0 %shard_map.136 = f32[2,12,2048]{2,1,0:T(8,128)S(1)} custom-call(s32[2]{0:T(128)S(1)} %pad_add_fusion.place_ref, bf16[256,768]{1,0:T(8,128)(2,1)S(1)} %get-tuple-element.67.refs_0_, bf16[256,768]{1,0:T(8,128)(2,1)S(1)} %collective-permute-done.16.refs_1_, bf16[256,2048]{1,0:T(8,128)(2,1)S(1)} %get-tuple-element.87.refs_2_, ...), custom_call_target="tpu_custom_call" | custom-call | flops 1610 | bytes 8 | tf_op jit(solution)/shard_map/pallas_call | solution.py:112
  129.1 4.0 %shard_map.133 = (bf16[256,1536]{1,0:T(8,128)(2,1)S(1)}, bf16[128,2048]{1,0:T(8,128)(2,1)S(1)}, bf16[128,2048]{1,0:T(8,128)(2,1)S(1)}, bf16[128,2048]{1,0:T(8,128)(2,1)S(1)}, bf16[128,2048]{1,0:T(8,128)(2,1)S(1)}) custom-call(s32[2]{0:T(128)S(1)} %pad_add_fusion.place_ref, f32[256,768]{1,0:T(8,128)S(1)} %get-tuple-element.76.grad_own_ref, ...), custom_call_target="tpu_custom_call" | custom-call | flops 3221 | bytes 18 | tf_op jit(solution)/shard_map/pallas_call | solution.py:112
  133.2 1.0 collective-permute-done.31.refs_0_
  134.1 4.0 %shard_map.137 = (bf16[256,1536]{1,0:T(8,128)(2,1)S(1)}, bf16[128,2048]{1,0:T(8,128)(2,1)S(1)}, bf16[128,2048]{1,0:T(8,128)(2,1)S(1)}, bf16[128,2048]{1,0:T(8,128)(2,1)S(1)}, bf16[128,2048]{1,0:T(8,128)(2,1)S(1)}) custom-call(s32[2]{0:T(128)S(1)} %pad_add_fusion.place_ref, f32[256,768]{1,0:T(8,128)S(1)} %get-tuple-element.84.grad_own_ref, ...), custom_call_target="tpu_custom_call" | custom-call | flops 3221 | bytes 18 | tf_op jit(solution)/shard_map/pallas_call | solution.py:112
  139.2 0.9 collective-permute-done.34
  140.2 1.6 collective-permute-start.36
  141.8 0.9 collective-permute-start.35
  142.8 5.8 %collective-permute-done.36 = bf16[64,2048]{1,0:T(8,128)(2,1)S(1)} collective-permute-done((bf16[64,2048]{1,0:T(8,128)(2,1)S(1)}, bf16[64,2048]{1,0:T(8,128)(2,1)S(1)}, u32[]{:S(2)}, u32[]{:S(2)}) %collective-permute-start.36) | collective-permute-done | bytes 262176 | tf_op jit(solution)/shard_map/ppermute | solution.py:17
  148.7 1.5 collective-permute-start.37
  150.4 1.0 collective-permute-start.40
  151.4 6.6 %shard_map.138.refs_15_ = f32[4,32,768]{2,1,0:T(8,128)} custom-call(s32[2]{0:T(128)S(1)} %pad_add_fusion.place_ref, bf16[96,4096]{1,0:T(8,128)(2,1)S(1)} %shard_map.123.refs_0_, bf16[32,4096]{1,0:T(8,128)(2,1)S(1)} %collective-permute-done.4.refs_1_, bf16[96,4096]{1,0:T(8,128)(2,1)S(1)} %collective-permute-done.6.refs_2_, ...), custom_call_target="tpu_custom_call" | custom-call | flops 3221 | bytes 20 | tf_op jit(solution)/shard_map/pallas_call | solution.py:112
  158.2 2.0 %collective-permute-start.42 = (bf16[64,2048]{1,0:T(8,128)(2,1)S(1)}, bf16[64,2048]{1,0:T(8,128)(2,1)S(1)}, u32[]{:S(2)}, u32[]{:S(2)}) collective-permute-start(bf16[64,2048]{1,0:T(8,128)(2,1)S(1)} %add_convert_fusion), channel_id=1, source_target_pairs={{0,8},{2,10},{4,12},{6,14},{8,0},{10,2},{12,4},{14,6},{16,24},{18,... | collective-permute-start | bytes 786440 | tf_op jit(solution)/shard_map/ppermute | solution.py:17
  160.8 1.0 collective-permute-start.41
  161.9 4.2 %shard_map.139.refs_15_ = f32[4,32,768]{2,1,0:T(8,128)} custom-call(s32[2]{0:T(128)S(1)} %pad_add_fusion.place_ref, bf16[96,4096]{1,0:T(8,128)(2,1)S(1)} %shard_map.123.refs_0_, bf16[32,4096]{1,0:T(8,128)(2,1)S(1)} %collective-permute-done.4.refs_1_, bf16[96,4096]{1,0:T(8,128)(2,1)S(1)} %collective-permute-done.6.refs_2_, ...), custom_call_target="tpu_custom_call", output_to_operand_aliasing={{}: (16, {})} | custom-call | flops 1610 | bytes 20 | tf_op jit(solution)/shard_map/pallas_call | solution.py:112
  166.1 0.9 collective-permute-done.38
  167.3 0.9 collective-permute-start.43
  168.2 0.8 copy.19
  169.0 3.9 %shard_map.140 = f32[4,32,768]{2,1,0:T(8,128)} custom-call(s32[2]{0:T(128)S(1)} %pad_add_fusion.place_ref, bf16[96,4096]{1,0:T(8,128)(2,1)S(1)} %shard_map.123.refs_0_, bf16[32,4096]{1,0:T(8,128)(2,1)S(1)} %collective-permute-done.4.refs_1_, bf16[96,4096]{1,0:T(8,128)(2,1)S(1)} %collective-permute-done.6.refs_2_, ...), custom_call_target="tpu_custom_call", output_to_operand_aliasing={{}: (16, {})} | custom-call | flops 1610 | bytes 20 | tf_op jit(solution)/shard_map/pallas_call | solution.py:112
  173.0 1.4 collective-permute-done.43
  174.4 0.8 add_convert_fusion.10
  (88 shorter events, 10.8 us)
Async XLA Ops:
  0.6 17.6 %collective-permute-start.1 = (bf16[32,4096]{1,0:T(8,128)(2,1)}, bf16[32,4096]{1,0:T(8,128)(2,1)S(1)}, u32[]{:S(2)}, u32[]{:S(2)}) collective-permute-start(bf16[32,4096]{1,0:T(8,128)(2,1)} %refs_0_.1), channel_id=1, source_target_pairs={{0,4},{2,6},{4,0},{6,2},{8,12},{10,14},{12,8},{14,10},{16,20},{18,... | collective-permute-start | bytes 786440 | tf_op jit(solution)/shard_map/ppermute | solution.py:17
  3.6 14.6 %collective-permute-start = (bf16[32,4096]{1,0:T(8,128)(2,1)}, bf16[32,4096]{1,0:T(8,128)(2,1)S(1)}, u32[]{:S(2)}, u32[]{:S(2)}) collective-permute-start(bf16[32,4096]{1,0:T(8,128)(2,1)} %refs_0_.1), channel_id=1, source_target_pairs={{0,16},{2,18},{4,20},{6,22},{8,24},{10,26},{12,28},{14,30},{16,0},... | collective-permute-start | bytes 786440 | tf_op jit(solution)/shard_map/ppermute | solution.py:17
  6.2 12.2 %collective-permute-start.3 = (bf16[32,4096]{1,0:T(8,128)(2,1)}, bf16[32,4096]{1,0:T(8,128)(2,1)S(1)}, u32[]{:S(2)}, u32[]{:S(2)}) collective-permute-start(bf16[32,4096]{1,0:T(8,128)(2,1)} %refs_0_.1), channel_id=1, source_target_pairs={{0,8},{2,10},{4,12},{6,14},{8,0},{10,2},{12,4},{14,6},{16,24},{18,... | collective-permute-start | bytes 786440 | tf_op jit(solution)/shard_map/ppermute | solution.py:17
  10.2 0.9 copy-start.1
  11.1 0.9 copy-start.2
  12.0 13.0 %copy-start = (bf16[32,4096]{1,0:T(8,128)(2,1)S(1)}, bf16[32,4096]{1,0:T(8,128)(2,1)}, u32[]{:S(2)}) copy-start(bf16[32,4096]{1,0:T(8,128)(2,1)} %refs_0_.1) | copy-start | bytes 786436
  12.0 17.2 %copy-start.4 = (f32[1,12,2048]{2,0,1:T(1,128)S(1)}, f32[1,12,2048]{2,0,1:T(1,128)}, u32[]{:S(2)}) copy-start(f32[1,12,2048]{2,0,1:T(1,128)} %param.19) | copy-start | bytes 294916
  18.2 15.1 %copy-start.5 = (f32[1,12,2048]{2,0,1:T(1,128)S(1)}, f32[1,12,2048]{2,0,1:T(1,128)}, u32[]{:S(2)}) copy-start(f32[1,12,2048]{2,0,1:T(1,128)} %param.18) | copy-start | bytes 294916
  18.2 15.2 %slice-start.3 = ((s8[6291456]{0:T(1024)(128)(4,1)}), s8[4194304]{0:T(1024)(128)(4,1)S(1)}, s32[]{:S(2)}) async-start(s8[6291456]{0:T(1024)(128)(4,1)} %bitcast.10), calls=%async_computation.3 | async-start | bytes 8388608
  18.4 7.3 %collective-permute-start.4 = (bf16[32,4096]{1,0:T(8,128)(2,1)S(1)}, bf16[32,4096]{1,0:T(8,128)(2,1)S(1)}, u32[]{:S(2)}, u32[]{:S(2)}) collective-permute-start(bf16[32,4096]{1,0:T(8,128)(2,1)S(1)} %collective-permute-done.refs_1_.refs_0_), channel_id=1, source_target_pairs={{0,8},{2,10},{4,12},{6,14},{8,0},{10,2},{12,4},{14,6},{16,24},{18,... | collective-permute-start | bytes 786440 | tf_op jit(solution)/shard_map/ppermute | solution.py:17
  19.9 7.0 %collective-permute-start.5 = (bf16[32,4096]{1,0:T(8,128)(2,1)S(1)}, bf16[32,4096]{1,0:T(8,128)(2,1)S(1)}, u32[]{:S(2)}, u32[]{:S(2)}) collective-permute-start(bf16[32,4096]{1,0:T(8,128)(2,1)S(1)} %collective-permute-done.3.refs_2_), channel_id=1, source_target_pairs={{0,4},{2,6},{4,0},{6,2},{8,12},{10,14},{12,8},{14,10},{16,20},{18,... | collective-permute-start | bytes 786440 | tf_op jit(solution)/shard_map/ppermute | solution.py:17
  20.4 4.7 %collective-permute-start.2 = (bf16[32,128]{1,0:T(8,128)(2,1)S(1)}, bf16[32,128]{1,0:T(8,128)(2,1)S(1)}, u32[]{:S(2)}, u32[]{:S(2)}) collective-permute-start(bf16[32,128]{1,0:T(8,128)(2,1)S(1)} %shard_map.121), channel_id=1, source_target_pairs={{0,16},{2,18},{4,20},{6,22},{8,24},{10,26},{12,28},{14,30},{16,0},... | collective-permute-start | bytes 24584 | tf_op jit(solution)/shard_map/ppermute | solution.py:17
  25.7 3.6 %collective-permute-start.6 = (bf16[96,4096]{1,0:T(8,128)(2,1)S(1)}, bf16[96,4096]{1,0:T(8,128)(2,1)S(1)}, u32[]{:S(2)}, u32[]{:S(2)}) collective-permute-start(bf16[96,4096]{1,0:T(8,128)(2,1)S(1)} %shard_map.123.refs_0_), channel_id=1, source_target_pairs={{0,2},{2,0},{4,6},{6,4},{8,10},{10,8},{12,14},{14,12},{16,18},{18,... | collective-permute-start | bytes 2359304 | tf_op jit(solution)/shard_map/ppermute | solution.py:17
  26.9 1.5 collective-permute-start.7
  27.4 14.4 %collective-permute-start.10 = (bf16[64,4096]{1,0:T(8,128)(2,1)S(1)}, bf16[64,4096]{1,0:T(8,128)(2,1)S(1)}, u32[]{:S(2)}, u32[]{:S(2)}) collective-permute-start(bf16[64,4096]{1,0:T(8,128)(2,1)S(1)} %shard_map.127), channel_id=1, source_target_pairs={{0,4},{2,6},{4,0},{6,2},{8,12},{10,14},{12,8},{14,10},{16,20},{18,... | collective-permute-start | bytes 1572872 | tf_op jit(solution)/shard_map/ppermute | solution.py:17
  29.0 12.9 %collective-permute-start.11 = (bf16[64,4096]{1,0:T(8,128)(2,1)S(1)}, bf16[64,4096]{1,0:T(8,128)(2,1)S(1)}, u32[]{:S(2)}, u32[]{:S(2)}) collective-permute-start(bf16[64,4096]{1,0:T(8,128)(2,1)S(1)} %shard_map.126.refs_0_.refs_2_.refs_4_.refs_6_), channel_id=1, source_target_pairs={{0,2},{2,0},{4,6},{6,4},{8,10},{10,8},{12,14},{14,12},{16,18},{18,... | collective-permute-start | bytes 1572872 | tf_op jit(solution)/shard_map/ppermute | solution.py:17
  29.2 4.2 %slice-start.4 = ((s8[6291456]{0:T(1024)(128)(4,1)}), s8[2097152]{0:T(1024)(128)(4,1)S(1)}, s32[]{:S(2)}) async-start(s8[6291456]{0:T(1024)(128)(4,1)} %bitcast.10), calls=%async_computation.4 | async-start | bytes 4194304
  35.9 6.0 %collective-permute-start.9 = (bf16[64,128]{1,0:T(8,128)(2,1)S(1)}, bf16[64,128]{1,0:T(8,128)(2,1)S(1)}, u32[]{:S(2)}, u32[]{:S(2)}) collective-permute-start(bf16[64,128]{1,0:T(8,128)(2,1)S(1)} %pad_maximum_fusion.2), channel_id=1, source_target_pairs={{0,8},{2,10},{4,12},{6,14},{8,0},{10,2},{12,4},{14,6},{16,24},{18,... | collective-permute-start | bytes 49160 | tf_op jit(solution)/shard_map/ppermute | solution.py:17
  41.8 1.9 %collective-permute-start.12 = (bf16[64,4096]{1,0:T(8,128)(2,1)S(1)}, bf16[64,4096]{1,0:T(8,128)(2,1)S(1)}, u32[]{:S(2)}, u32[]{:S(2)}) collective-permute-start(bf16[64,4096]{1,0:T(8,128)(2,1)S(1)} %collective-permute-done.10.refs_1_.refs_3_.refs_5_.refs_7_), channel_id=1, source_target_pairs={{0,2},{2,0},{4,6},{6,4},{8,10},{10,8},{12,14},{14,12},{16,18},{18,... | collective-permute-start | bytes 1572872 | tf_op jit(solution)/shard_map/ppermute | solution.py:17
  41.9 12.0 %collective-permute-start.8 = (bf16[256,768]{1,0:T(8,128)(2,1)S(1)}, bf16[256,768]{1,0:T(8,128)(2,1)S(1)}, u32[]{:S(2)}, u32[]{:S(2)}) collective-permute-start(bf16[256,768]{1,0:T(8,128)(2,1)S(1)} %get-tuple-element.62.refs_0_), channel_id=1, source_target_pairs={{0,1},{1,0},{2,3},{3,2},{4,5},{5,4},{6,7},{7,6},{8,9},{9,8},{10,11... | collective-permute-start | bytes 1179656 | tf_op jit(solution)/shard_map/ppermute | solution.py:17
  47.8 43.4 %copy-start.3 = (bf16[32,2048]{1,0:T(8,128)(2,1)S(1)}, bf16[32,2048]{1,0:T(8,128)(2,1)}, u32[]{:S(2)}) copy-start(bf16[32,2048]{1,0:T(8,128)(2,1)} %param.11) | copy-start | bytes 393220
  47.9 14.0 %collective-permute-start.16 = (bf16[256,768]{1,0:T(8,128)(2,1)S(1)}, bf16[256,768]{1,0:T(8,128)(2,1)S(1)}, u32[]{:S(2)}, u32[]{:S(2)}) collective-permute-start(bf16[256,768]{1,0:T(8,128)(2,1)S(1)} %get-tuple-element.67.refs_0_), channel_id=1, source_target_pairs={{0,1},{1,0},{2,3},{3,2},{4,5},{5,4},{6,7},{7,6},{8,9},{9,8},{10,11... | collective-permute-start | bytes 1179656 | tf_op jit(solution)/shard_map/ppermute | solution.py:17
  49.4 3.9 %collective-permute-start.13 = (bf16[128,128]{1,0:T(8,128)(2,1)S(1)}, bf16[128,128]{1,0:T(8,128)(2,1)S(1)}, u32[]{:S(2)}, u32[]{:S(2)}) collective-permute-start(bf16[128,128]{1,0:T(8,128)(2,1)S(1)} %pad_maximum_fusion.1), channel_id=1, source_target_pairs={{0,4},{2,6},{4,0},{6,2},{8,12},{10,14},{12,8},{14,10},{16,20},{18,... | collective-permute-start | bytes 98312 | tf_op jit(solution)/shard_map/ppermute | solution.py:17
  53.4 1.3 collective-permute-start.14
  64.1 2.0 %collective-permute-start.17 = (bf16[128,2048]{1,0:T(8,128)(2,1)S(1)}, bf16[128,2048]{1,0:T(8,128)(2,1)S(1)}, u32[]{:S(2)}, u32[]{:S(2)}) collective-permute-start(bf16[128,2048]{1,0:T(8,128)(2,1)S(1)} %get-tuple-element.73), channel_id=1, source_target_pairs={{0,2},{2,0},{4,6},{6,4},{8,10},{10,8},{12,14},{14,12},{16,18},{18,... | collective-permute-start | bytes 1572872 | tf_op jit(solution)/shard_map/ppermute | solution.py:17
  64.2 11.0 %collective-permute-start.15 = (bf16[128,2048]{1,0:T(8,128)(2,1)S(1)}, bf16[128,2048]{1,0:T(8,128)(2,1)S(1)}, u32[]{:S(2)}, u32[]{:S(2)}) collective-permute-start(bf16[128,2048]{1,0:T(8,128)(2,1)S(1)} %get-tuple-element.70), channel_id=1, source_target_pairs={{0,2},{2,0},{4,6},{6,4},{8,10},{10,8},{12,14},{14,12},{16,18},{18,... | collective-permute-start | bytes 1572872 | tf_op jit(solution)/shard_map/ppermute | solution.py:17
  66.3 8.4 %collective-permute-start.18 = (bf16[64,2048]{1,0:T(8,128)(2,1)S(1)}, bf16[64,2048]{1,0:T(8,128)(2,1)S(1)}, u32[]{:S(2)}, u32[]{:S(2)}) collective-permute-start(bf16[64,2048]{1,0:T(8,128)(2,1)S(1)} %get-tuple-element.119), channel_id=1, source_target_pairs={{0,4},{2,6},{4,0},{6,2},{8,12},{10,14},{12,8},{14,10},{16,20},{18,... | collective-permute-start | bytes 786440 | tf_op jit(solution)/shard_map/ppermute | solution.py:17
  74.7 7.5 %collective-permute-start.19 = (bf16[64,2048]{1,0:T(8,128)(2,1)S(1)}, bf16[64,2048]{1,0:T(8,128)(2,1)S(1)}, u32[]{:S(2)}, u32[]{:S(2)}) collective-permute-start(bf16[64,2048]{1,0:T(8,128)(2,1)S(1)} %get-tuple-element.74), channel_id=1, source_target_pairs={{0,4},{2,6},{4,0},{6,2},{8,12},{10,14},{12,8},{14,10},{16,20},{18,... | collective-permute-start | bytes 786440 | tf_op jit(solution)/shard_map/ppermute | solution.py:17
  75.3 8.3 %collective-permute-start.20 = (bf16[64,2048]{1,0:T(8,128)(2,1)S(1)}, bf16[64,2048]{1,0:T(8,128)(2,1)S(1)}, u32[]{:S(2)}, u32[]{:S(2)}) collective-permute-start(bf16[64,2048]{1,0:T(8,128)(2,1)S(1)} %add_convert_fusion.7), channel_id=1, source_target_pairs={{0,8},{2,10},{4,12},{6,14},{8,0},{10,2},{12,4},{14,6},{16,24},{18,... | collective-permute-start | bytes 786440 | tf_op jit(solution)/shard_map/ppermute | solution.py:17
  83.7 7.6 %collective-permute-start.21 = (bf16[32,2048]{1,0:T(8,128)(2,1)S(1)}, bf16[32,2048]{1,0:T(8,128)(2,1)S(1)}, u32[]{:S(2)}, u32[]{:S(2)}) collective-permute-start(bf16[32,2048]{1,0:T(8,128)(2,1)S(1)} %add_convert_fusion.12), channel_id=1, source_target_pairs={{0,16},{2,18},{4,20},{6,22},{8,24},{10,26},{12,28},{14,30},{16,0},... | collective-permute-start | bytes 393224 | tf_op jit(solution)/shard_map/ppermute | solution.py:17
  91.4 7.1 %collective-permute-start.22 = (bf16[32,2048]{1,0:T(8,128)(2,1)S(1)}, bf16[32,2048]{1,0:T(8,128)(2,1)S(1)}, u32[]{:S(2)}, u32[]{:S(2)}) collective-permute-start(bf16[32,2048]{1,0:T(8,128)(2,1)S(1)} %subtract_convert_fusion.refs_0_), channel_id=1, source_target_pairs={{0,16},{2,18},{4,20},{6,22},{8,24},{10,26},{12,28},{14,30},{16,0},... | collective-permute-start | bytes 393224 | tf_op jit(solution)/shard_map/ppermute | solution.py:17
  99.0 6.4 %collective-permute-start.23 = (bf16[64,2048]{1,0:T(8,128)(2,1)S(1)}, bf16[64,2048]{1,0:T(8,128)(2,1)S(1)}, u32[]{:S(2)}, u32[]{:S(2)}) collective-permute-start(bf16[64,2048]{1,0:T(8,128)(2,1)S(1)} %shard_map.131.refs_0_), channel_id=1, source_target_pairs={{0,8},{2,10},{4,12},{6,14},{8,0},{10,2},{12,4},{14,6},{16,24},{18,... | collective-permute-start | bytes 786440 | tf_op jit(solution)/shard_map/ppermute | solution.py:17
  99.1 6.4 %collective-permute-start.24 = (bf16[64,2048]{1,0:T(8,128)(2,1)S(1)}, bf16[64,2048]{1,0:T(8,128)(2,1)S(1)}, u32[]{:S(2)}, u32[]{:S(2)}) collective-permute-start(bf16[64,2048]{1,0:T(8,128)(2,1)S(1)} %shard_map.131.refs_0_), channel_id=1, source_target_pairs={{0,4},{2,6},{4,0},{6,2},{8,12},{10,14},{12,8},{14,10},{16,20},{18,... | collective-permute-start | bytes 786440 | tf_op jit(solution)/shard_map/ppermute | solution.py:17
  100.7 4.9 %collective-permute-start.25 = (bf16[64,2048]{1,0:T(8,128)(2,1)S(1)}, bf16[64,2048]{1,0:T(8,128)(2,1)S(1)}, u32[]{:S(2)}, u32[]{:S(2)}) collective-permute-start(bf16[64,2048]{1,0:T(8,128)(2,1)S(1)} %shard_map.131.refs_0_), channel_id=1, source_target_pairs={{0,2},{2,0},{4,6},{6,4},{8,10},{10,8},{12,14},{14,12},{16,18},{18,... | collective-permute-start | bytes 786440 | tf_op jit(solution)/shard_map/ppermute | solution.py:17
  105.6 1.7 collective-permute-start.26
  105.6 8.7 %collective-permute-start.28 = (bf16[64,2048]{1,0:T(8,128)(2,1)S(1)}, bf16[64,2048]{1,0:T(8,128)(2,1)S(1)}, u32[]{:S(2)}, u32[]{:S(2)}) collective-permute-start(bf16[64,2048]{1,0:T(8,128)(2,1)S(1)} %collective-permute-done.23.refs_1_), channel_id=1, source_target_pairs={{0,4},{2,6},{4,0},{6,2},{8,12},{10,14},{12,8},{14,10},{16,20},{18,... | collective-permute-start | bytes 786440 | tf_op jit(solution)/shard_map/ppermute | solution.py:17
  107.1 7.2 %collective-permute-start.29 = (bf16[64,2048]{1,0:T(8,128)(2,1)S(1)}, bf16[64,2048]{1,0:T(8,128)(2,1)S(1)}, u32[]{:S(2)}, u32[]{:S(2)}) collective-permute-start(bf16[64,2048]{1,0:T(8,128)(2,1)S(1)} %collective-permute-done.24.refs_0_), channel_id=1, source_target_pairs={{0,2},{2,0},{4,6},{6,4},{8,10},{10,8},{12,14},{14,12},{16,18},{18,... | collective-permute-start | bytes 786440 | tf_op jit(solution)/shard_map/ppermute | solution.py:17
  109.7 11.4 %collective-permute-start.27 = (bf16[256,768]{1,0:T(8,128)(2,1)S(1)}, bf16[256,768]{1,0:T(8,128)(2,1)S(1)}, u32[]{:S(2)}, u32[]{:S(2)}) collective-permute-start(bf16[256,768]{1,0:T(8,128)(2,1)S(1)} %get-tuple-element.77), channel_id=1, source_target_pairs={{0,1},{1,0},{2,3},{3,2},{4,5},{5,4},{6,7},{7,6},{8,9},{9,8},{10,11... | collective-permute-start | bytes 1179656 | tf_op jit(solution)/shard_map/ppermute | solution.py:17
  114.3 4.1 %collective-permute-start.30 = (bf16[64,2048]{1,0:T(8,128)(2,1)S(1)}, bf16[64,2048]{1,0:T(8,128)(2,1)S(1)}, u32[]{:S(2)}, u32[]{:S(2)}) collective-permute-start(bf16[64,2048]{1,0:T(8,128)(2,1)S(1)} %collective-permute-done.28.refs_1_), channel_id=1, source_target_pairs={{0,2},{2,0},{4,6},{6,4},{8,10},{10,8},{12,14},{14,12},{16,18},{18,... | collective-permute-start | bytes 786440 | tf_op jit(solution)/shard_map/ppermute | solution.py:17
  123.5 10.6 %collective-permute-start.31 = (bf16[256,768]{1,0:T(8,128)(2,1)S(1)}, bf16[256,768]{1,0:T(8,128)(2,1)S(1)}, u32[]{:S(2)}, u32[]{:S(2)}) collective-permute-start(bf16[256,768]{1,0:T(8,128)(2,1)S(1)} %get-tuple-element.85), channel_id=1, source_target_pairs={{0,1},{1,0},{2,3},{3,2},{4,5},{5,4},{6,7},{7,6},{8,9},{9,8},{10,11... | collective-permute-start | bytes 1179656 | tf_op jit(solution)/shard_map/ppermute | solution.py:17
  129.1 22.3 %slice-start = ((s8[12582912]{0:T(1024)(128)(4,1)}), s8[4194304]{0:T(1024)(128)(4,1)S(1)}, s32[]{:S(2)}) async-start(s8[12582912]{0:T(1024)(128)(4,1)} %bitcast.8), calls=%async_computation | async-start | bytes 8388608
  129.1 22.3 %slice-start.1 = ((s8[12582912]{0:T(1024)(128)(4,1)}), s8[4194304]{0:T(1024)(128)(4,1)S(1)}, s32[]{:S(2)}) async-start(s8[12582912]{0:T(1024)(128)(4,1)} %bitcast.8), calls=%async_computation.1 | async-start | bytes 8388608
  134.1 17.3 %slice-start.2 = ((s8[12582912]{0:T(1024)(128)(4,1)}), s8[4194304]{0:T(1024)(128)(4,1)S(1)}, s32[]{:S(2)}) async-start(s8[12582912]{0:T(1024)(128)(4,1)} %bitcast.8), calls=%async_computation.2 | async-start | bytes 8388608
  138.1 2.0 %collective-permute-start.34 = (bf16[128,2048]{1,0:T(8,128)(2,1)S(1)}, bf16[128,2048]{1,0:T(8,128)(2,1)S(1)}, u32[]{:S(2)}, u32[]{:S(2)}) collective-permute-start(bf16[128,2048]{1,0:T(8,128)(2,1)S(1)} %get-tuple-element.100), channel_id=1, source_target_pairs={{0,2},{2,0},{4,6},{6,4},{8,10},{10,8},{12,14},{14,12},{16,18},{18,... | collective-permute-start | bytes 1572872 | tf_op jit(solution)/shard_map/ppermute | solution.py:17
  138.2 4.6 %collective-permute-start.33 = (bf16[128,2048]{1,0:T(8,128)(2,1)S(1)}, bf16[128,2048]{1,0:T(8,128)(2,1)S(1)}, u32[]{:S(2)}, u32[]{:S(2)}) collective-permute-start(bf16[128,2048]{1,0:T(8,128)(2,1)S(1)} %get-tuple-element.98), channel_id=1, source_target_pairs={{0,2},{2,0},{4,6},{6,4},{8,10},{10,8},{12,14},{14,12},{16,18},{18,... | collective-permute-start | bytes 1572872 | tf_op jit(solution)/shard_map/ppermute | solution.py:17
  138.7 19.3 %collective-permute-start.32 = (bf16[128,2048]{1,0:T(8,128)(2,1)S(1)}, bf16[128,2048]{1,0:T(8,128)(2,1)S(1)}, u32[]{:S(2)}, u32[]{:S(2)}) collective-permute-start(bf16[128,2048]{1,0:T(8,128)(2,1)S(1)} %get-tuple-element.94), channel_id=1, source_target_pairs={{0,2},{2,0},{4,6},{6,4},{8,10},{10,8},{12,14},{14,12},{16,18},{18,... | collective-permute-start | bytes 1572872 | tf_op jit(solution)/shard_map/ppermute | solution.py:17
  138.8 11.4 %collective-permute-start.39 = (bf16[128,2048]{1,0:T(8,128)(2,1)S(1)}, bf16[128,2048]{1,0:T(8,128)(2,1)S(1)}, u32[]{:S(2)}, u32[]{:S(2)}) collective-permute-start(bf16[128,2048]{1,0:T(8,128)(2,1)S(1)} %get-tuple-element.104), channel_id=1, source_target_pairs={{0,2},{2,0},{4,6},{6,4},{8,10},{10,8},{12,14},{14,12},{16,18},{18,... | collective-permute-start | bytes 1572872 | tf_op jit(solution)/shard_map/ppermute | solution.py:17
  140.2 8.4 %collective-permute-start.36 = (bf16[64,2048]{1,0:T(8,128)(2,1)S(1)}, bf16[64,2048]{1,0:T(8,128)(2,1)S(1)}, u32[]{:S(2)}, u32[]{:S(2)}) collective-permute-start(bf16[64,2048]{1,0:T(8,128)(2,1)S(1)} %get-tuple-element.115), channel_id=1, source_target_pairs={{0,1},{1,0},{2,3},{3,2},{4,5},{5,4},{6,7},{7,6},{8,9},{9,8},{10,11... | collective-permute-start | bytes 786440 | tf_op jit(solution)/shard_map/ppermute | solution.py:17
  141.8 8.5 %collective-permute-start.35 = (bf16[64,2048]{1,0:T(8,128)(2,1)S(1)}, bf16[64,2048]{1,0:T(8,128)(2,1)S(1)}, u32[]{:S(2)}, u32[]{:S(2)}) collective-permute-start(bf16[64,2048]{1,0:T(8,128)(2,1)S(1)} %get-tuple-element.114), channel_id=1, source_target_pairs={{0,4},{2,6},{4,0},{6,2},{8,12},{10,14},{12,8},{14,10},{16,20},{18,... | collective-permute-start | bytes 786440 | tf_op jit(solution)/shard_map/ppermute | solution.py:17
  148.7 9.4 %collective-permute-start.37 = (bf16[64,2048]{1,0:T(8,128)(2,1)S(1)}, bf16[64,2048]{1,0:T(8,128)(2,1)S(1)}, u32[]{:S(2)}, u32[]{:S(2)}) collective-permute-start(bf16[64,2048]{1,0:T(8,128)(2,1)S(1)} %add_convert_fusion.5), channel_id=1, source_target_pairs={{0,1},{1,0},{2,3},{3,2},{4,5},{5,4},{6,7},{7,6},{8,9},{9,8},{10,11... | collective-permute-start | bytes 786440 | tf_op jit(solution)/shard_map/ppermute | solution.py:17
  150.4 7.6 %collective-permute-start.40 = (bf16[64,2048]{1,0:T(8,128)(2,1)S(1)}, bf16[64,2048]{1,0:T(8,128)(2,1)S(1)}, u32[]{:S(2)}, u32[]{:S(2)}) collective-permute-start(bf16[64,2048]{1,0:T(8,128)(2,1)S(1)} %get-tuple-element.105), channel_id=1, source_target_pairs={{0,4},{2,6},{4,0},{6,2},{8,12},{10,14},{12,8},{14,10},{16,20},{18,... | collective-permute-start | bytes 786440 | tf_op jit(solution)/shard_map/ppermute | solution.py:17
  158.2 7.9 %collective-permute-start.42 = (bf16[64,2048]{1,0:T(8,128)(2,1)S(1)}, bf16[64,2048]{1,0:T(8,128)(2,1)S(1)}, u32[]{:S(2)}, u32[]{:S(2)}) collective-permute-start(bf16[64,2048]{1,0:T(8,128)(2,1)S(1)} %add_convert_fusion), channel_id=1, source_target_pairs={{0,8},{2,10},{4,12},{6,14},{8,0},{10,2},{12,4},{14,6},{16,24},{18,... | collective-permute-start | bytes 786440 | tf_op jit(solution)/shard_map/ppermute | solution.py:17
  160.3 6.7 %collective-permute-start.38 = (bf16[64,2048]{1,0:T(8,128)(2,1)S(1)}, bf16[64,2048]{1,0:T(8,128)(2,1)S(1)}, u32[]{:S(2)}, u32[]{:S(2)}) collective-permute-start(bf16[64,2048]{1,0:T(8,128)(2,1)S(1)} %add_convert_fusion.3), channel_id=1, source_target_pairs={{0,1},{1,0},{2,3},{3,2},{4,5},{5,4},{6,7},{7,6},{8,9},{9,8},{10,11... | collective-permute-start | bytes 786440 | tf_op jit(solution)/shard_map/ppermute | solution.py:17
  160.8 6.4 %collective-permute-start.41 = (bf16[64,2048]{1,0:T(8,128)(2,1)S(1)}, bf16[64,2048]{1,0:T(8,128)(2,1)S(1)}, u32[]{:S(2)}, u32[]{:S(2)}) collective-permute-start(bf16[64,2048]{1,0:T(8,128)(2,1)S(1)} %get-tuple-element.106), channel_id=1, source_target_pairs={{0,4},{2,6},{4,0},{6,2},{8,12},{10,14},{12,8},{14,10},{16,20},{18,... | collective-permute-start | bytes 786440 | tf_op jit(solution)/shard_map/ppermute | solution.py:17
  167.3 7.1 %collective-permute-start.43 = (bf16[32,2048]{1,0:T(8,128)(2,1)S(1)}, bf16[32,2048]{1,0:T(8,128)(2,1)S(1)}, u32[]{:S(2)}, u32[]{:S(2)}) collective-permute-start(bf16[32,2048]{1,0:T(8,128)(2,1)S(1)} %add_convert_fusion.11), channel_id=1, source_target_pairs={{0,16},{2,18},{4,20},{6,22},{8,24},{10,26},{12,28},{14,30},{16,0},... | collective-permute-start | bytes 393224 | tf_op jit(solution)/shard_map/ppermute | solution.py:17
